TPU v7x, 32 devices: a whole 2x2x4 slice. The times are simulated.
32 devices in a mesh: stick: 8 (over z, y), band: 4 (over x, core).
Axes of the slice: x: 2, y: 2, z: 4, core: 2. Of those that a mesh axis runs over, the one named last changes fastest.
Arguments:
- sticks: float32 [32, 96, 1024], P('band', None, 'stick'), may hold values from -0.078125 to 0.078125
- stick_columns: int32 [1024], P('stick'), may hold values from -1 to 2303, as said below
Outputs:
- exchange_sticks: float32 [32, 96, 1024], P('band', None, 'stick')
Inputs may be any that keep to these rules, and one draw needn't show every extreme that they name: `stick_columns`: each entry is -1 (an empty slot) or a grid column kx * 48 + ky, and no column appears twice. On each index of the stick axis its 128 slots hold the live sticks first and the empty ones after; one index holds 128 live sticks, another 128 / 4, the others from 32 to 128.
All inputs are finite; a program needn't handle non-finite values.
Results may differ from a plain program's by a relative error of at most 0.0003.
Values sent between devices are 32-bit elements; how exact they have to be, the bound alone decides.
No kernel may reach another device: no remote copies, remote signals or barrier semaphores. Data moves between devices by JAX's collectives and lax.ppermute only.
A program may use at most 64 MiB of HBM per device.

v0:
```python
import functools
import math

import jax
import jax.numpy as jnp
import numpy as np
from jax import lax
from jax.experimental import pallas as pl
from jax.experimental.pallas import tpu as pltpu
from jax.sharding import PartitionSpec as P

HALF = 2
BOX_LENGTH = 18.0
LANES = 128
MID = 64
CHUNK = 8

F32 = jnp.float32
BF16 = jnp.bfloat16


def rounded_parts(table):
    high = table.astype(BF16)
    low = (table - high.astype(np.float64)).astype(BF16)
    return high, low


def trig(g):
    angle = 2.0 * np.pi / g * (np.outer(np.arange(g), np.arange(g)) % g)
    return np.cos(angle), np.sin(angle)


def stacked_left(table):
    high, low = rounded_parts(table)
    return np.concatenate(
        [np.concatenate([high, high], 1), np.concatenate([low, np.zeros_like(low)], 1)], 0
    )


def stacked_right(table):
    high, low = rounded_parts(table)
    return np.concatenate(
        [np.concatenate([high, low], 1), np.concatenate([high, np.zeros_like(low)], 1)], 0
    )


def make_tables(g):
    c, s = trig(g)
    forward = stacked_left(np.concatenate([c, -s], 1))
    backward = stacked_left(np.concatenate([c, s], 1))

    def lane_table(sign, scale):
        out = np.zeros((LANES, LANES))
        out[:g, :g] = c
        out[:g, MID : MID + g] = sign * s
        out[MID : MID + g, :g] = -sign * s
        out[MID : MID + g, MID : MID + g] = c
        return out * scale

    z_forward = stacked_right(lane_table(-1.0, 1.0))
    z_backward = stacked_right(lane_table(1.0, 1.0 / g**3))
    spread = np.zeros((LANES, 2 * g))
    spread[:g, :g] = c
    spread[:g, g:] = -s
    spread[MID : MID + g, :g] = s
    spread[MID : MID + g, g:] = c
    stick_in = stacked_left(spread)
    pick = np.zeros((2 * g, LANES))
    pick[:g, :g] = c
    pick[:g, MID : MID + g] = s
    pick[g:, :g] = -s
    pick[g:, MID : MID + g] = c
    stick_out = stacked_left(pick * g**-1.5)
    freq = np.arange(g)
    square = np.minimum(freq, g - freq) ** 2
    total = square[:, None, None] + square[None, :, None] + square[None, None, :]
    unit = (2.0 * math.pi / BOX_LENGTH) ** 2
    kernel = np.where(total > 0, 4.0 * math.pi / (unit * np.maximum(total, 1)), 0.0)
    coulomb = np.zeros((g, g, LANES), np.float32)
    coulomb[:, :, :g] = kernel
    coulomb[:, :, MID : MID + g] = kernel
    return dict(
        forward=forward,
        backward=backward,
        z_forward=z_forward,
        z_backward=z_backward,
        stick_in=stick_in,
        stick_out=stick_out,
        coulomb=coulomb,
    )


def split(x):
    high = x.astype(BF16)
    low = (x - high.astype(F32)).astype(BF16)
    return high, low


def dot(a, b):
    return jnp.dot(a, b, preferred_element_type=F32)


def lower_lanes(shape):
    return lax.broadcasted_iota(jnp.int32, shape, len(shape) - 1) % LANES < MID


def turned(x):
    rolled = pltpu.roll(x, MID, 1)
    return jnp.where(lower_lanes(x.shape), -rolled, rolled)


def left_pair(table, first, second):
    u = jnp.concatenate([first[0], second[0]], 1)
    v = jnp.concatenate([first[1], second[1]], 1)
    u_high, u_low = split(u)
    v_high, v_low = split(v)
    data = jnp.concatenate([u_high, v_high, u_low, v_low], 0)
    both = dot(table, data)
    g = both.shape[0] // 2
    out = both[:g] + both[g:]
    return out[:, :LANES], out[:, LANES:]


def left_all(table, slabs, expand):
    results = []
    for k in range(0, len(slabs), 2):
        results += left_pair(table, expand(slabs[k]), expand(slabs[k + 1]))
    return results


def complex_slab(x):
    return x, turned(x)


def right(x, table):
    high, low = split(x)
    both = dot(jnp.concatenate([high, low], 1), table)
    return both[:, :LANES] + both[:, LANES:]


def chunks(g, body):
    @pl.loop(0, g // CHUNK)
    def _(step):
        body(step * CHUNK)


def strided_slabs(ref, first, g):
    return [ref[pl.ds(first + k, g, stride=g), :] for k in range(CHUNK)]


def slabs_at(ref, first, g):
    rows = pl.ds(pl.multiple_of(first * g, CHUNK * g), CHUNK * g)
    block = ref[rows, :]
    return [block[k * g : (k + 1) * g] for k in range(CHUNK)]


def store_slabs(ref, first, g, slabs):
    rows = pl.ds(pl.multiple_of(first * g, CHUNK * g), CHUNK * g)
    ref[rows, :] = jnp.concatenate(slabs, 0)


def one_hot(columns, first, rows):
    index = lax.broadcasted_iota(jnp.int32, (rows, columns.shape[1]), 0)
    return jnp.where(index == columns - first, 1.0, 0.0).astype(BF16)


def all_columns(received_ref, row):
    count = received_ref.shape[0]
    rows = [received_ref[k, row : row + 1, :] for k in range(count)]
    return jnp.concatenate(rows, 1).astype(jnp.int32)


def field_kernel(g, received_ref, stick_in_ref, backward_ref, phi_ref, packed_ref, work_a, work_b):
    count = received_ref.shape[0]
    columns = all_columns(received_ref, 2 * g)
    stick_in = stick_in_ref[...]
    backward = backward_ref[...]
    pieces = []
    for k in range(0, count, 2):
        block = jnp.concatenate([received_ref[k, : 2 * g, :], received_ref[k + 1, : 2 * g, :]], 1)
        both = dot(stick_in, jnp.concatenate(split(block), 0))
        lined = both[:LANES] + both[LANES:]
        pieces.append(jnp.concatenate(split(lined.T), 1))
    sticks = jnp.concatenate(pieces, 0)

    def scatter(first):
        rows = CHUNK * g
        hot = one_hot(columns, first * g, rows)
        both = dot(hot, sticks)
        placed = both[:, :LANES] + both[:, LANES:]
        slabs = [placed[k * g : (k + 1) * g] for k in range(CHUNK)]
        store_slabs(work_b, first, g, left_all(backward, slabs, complex_slab))

    chunks(g, scatter)

    def real_slab(x):
        rolled = pltpu.roll(x, MID, 1)
        lower = lower_lanes(x.shape)
        return jnp.where(lower, x, rolled), -jnp.where(lower, rolled, x)

    def finish(first):
        slabs = strided_slabs(work_b, first, g)
        store_slabs(phi_ref, first, g, left_all(backward, slabs, real_slab))

    chunks(g, finish)
    half_rows = g * g // 2
    lower = phi_ref[:half_rows, :]
    packed_ref[...] = jnp.where(lower_lanes(lower.shape), lower, phi_ref[half_rows:, :])


def potentials(g, phi_ref, pair_ref, tables, work_a, work_b, emit):
    forward_ref, backward_ref, z_forward_ref, z_backward_ref, coulomb_ref = tables
    forward = forward_ref[...]
    backward = backward_ref[...]

    def first_steps(first):
        rows = pl.ds(pl.multiple_of(first * g, CHUNK * g), CHUNK * g)
        density = phi_ref[rows, :] * pair_ref[rows, :]
        spectrum = right(density, z_forward_ref[...])
        slabs = [spectrum[k * g : (k + 1) * g] for k in range(CHUNK)]
        store_slabs(work_a, first, g, left_all(forward, slabs, complex_slab))

    chunks(g, first_steps)

    def middle(first):
        slabs = left_all(forward, strided_slabs(work_a, first, g), complex_slab)
        slabs = [slab * coulomb_ref[first + k] for k, slab in enumerate(slabs)]
        store_slabs(work_b, first, g, left_all(backward, slabs, complex_slab))

    chunks(g, middle)

    def last_steps(first):
        slabs = left_all(backward, strided_slabs(work_b, first, g), complex_slab)
        emit(first, right(jnp.concatenate(slabs, 0), z_backward_ref[...]))

    chunks(g, last_steps)


def pair_fields(g, first_ref, second_ref, pair_ref):
    half_rows = g * g // 2
    first, second = first_ref[...], second_ref[...]
    lower = lower_lanes(first.shape)
    pair_ref[:half_rows, :] = jnp.where(lower, first, pltpu.roll(second, MID, 1))
    pair_ref[half_rows:, :] = jnp.where(lower, pltpu.roll(first, MID, 1), second)


def near_kernel(g, phi_ref, other_ref, forward_ref, backward_ref, z_forward_ref, z_backward_ref, coulomb_ref, sum_ref, pair_ref, work_a, work_b):
    half_rows = g * g // 2
    other = other_ref[...]
    own = phi_ref[...]
    lower = lower_lanes(other.shape)
    pair_ref[:half_rows, :] = jnp.where(lower, own[:half_rows], pltpu.roll(other, MID, 1))
    pair_ref[half_rows:, :] = jnp.where(lower, own[half_rows:], other)

    def emit(first, potential):
        rows = pl.ds(pl.multiple_of(first * g, CHUNK * g), CHUNK * g)
        sum_ref[rows, :] = potential * pair_ref[rows, :]

    tables = (forward_ref, backward_ref, z_forward_ref, z_backward_ref, coulomb_ref)
    potentials(g, phi_ref, pair_ref, tables, work_a, work_b, emit)


def middle_kernel(g, phi_ref, first_ref, second_ref, before_ref, forward_ref, backward_ref, z_forward_ref, z_backward_ref, coulomb_ref, sum_ref, pair_ref, work_a, work_b):
    pair_fields(g, first_ref, second_ref, pair_ref)

    def emit(first, potential):
        rows = pl.ds(pl.multiple_of(first * g, CHUNK * g), CHUNK * g)
        sum_ref[rows, :] = potential * pair_ref[rows, :] + before_ref[rows, :]

    tables = (forward_ref, backward_ref, z_forward_ref, z_backward_ref, coulomb_ref)
    potentials(g, phi_ref, pair_ref, tables, work_a, work_b, emit)


def far_kernel(g, weights, phi_ref, first_ref, second_ref, sum_ref, received_ref, forward_ref, backward_ref, z_forward_ref, z_backward_ref, stick_out_ref, coulomb_ref, out_ref, pair_ref, work_a, work_b, picked):
    pair_fields(g, first_ref, second_ref, pair_ref)
    forward = forward_ref[...]

    def emit(first, potential):
        rows = pl.ds(pl.multiple_of(first * g, CHUNK * g), CHUNK * g)
        lower = lower_lanes(potential.shape)
        weight = jnp.where(lower, weights[0], weights[1])
        total = potential * pair_ref[rows, :] * weight + sum_ref[rows, :]
        total = total + pltpu.roll(total, MID, 1)
        slabs = [total[k * g : (k + 1) * g] for k in range(CHUNK)]

        def expand(x):
            low = lower_lanes(x.shape)
            return jnp.where(low, x, 0.0), jnp.where(low, 0.0, x)

        store_slabs(work_a, first, g, left_all(forward, slabs, expand))

    tables = (forward_ref, backward_ref, z_forward_ref, z_backward_ref, coulomb_ref)
    potentials(g, phi_ref, pair_ref, tables, work_a, work_b, emit)

    columns = all_columns(received_ref, 2 * g)
    picked[...] = jnp.zeros_like(picked)

    def pick(first):
        slabs = left_all(forward, strided_slabs(work_a, first, g), complex_slab)
        rows = CHUNK * g
        parts = jnp.concatenate(split(jnp.concatenate(slabs, 0)), 1)
        hot = one_hot(columns, first * g, rows)
        both = lax.dot_general(parts, hot, (((0,), (0,)), ((), ())), preferred_element_type=F32)
        picked[...] += both[:LANES] + both[LANES:]

    chunks(g, pick)
    result = dot(stick_out_ref[...], jnp.concatenate(split(picked[...]), 0))
    result = result[: 2 * g] + result[2 * g :]
    for k in range(out_ref.shape[0]):
        out_ref[k] = result[:, k * LANES : (k + 1) * LANES]


def call(kernel, out_shapes, scratch, flops, *operands):
    vmem = pl.BlockSpec(memory_space=pltpu.VMEM)
    moved = sum(x.size * x.dtype.itemsize for x in operands)
    return pl.pallas_call(
        kernel,
        out_shape=out_shapes,
        in_specs=[vmem] * len(operands),
        out_specs=jax.tree.map(lambda _: vmem, out_shapes),
        scratch_shapes=scratch,
        compiler_params=pltpu.CompilerParams(vmem_limit_bytes=40 * 2**20),
        cost_estimate=pl.CostEstimate(flops=flops, bytes_accessed=moved, transcendentals=0),
    )(*operands)


def on_device(sticks, stick_columns):
    g = sticks.shape[1] // 2
    owners = lax.axis_size("stick")
    groups = lax.axis_size("band")
    t = {name: jnp.asarray(value) for name, value in make_tables(g).items()}
    rows = g * g
    field = jax.ShapeDtypeStruct((rows, LANES), F32)
    half_field = jax.ShapeDtypeStruct((rows // 2, LANES), F32)
    scratch = pltpu.VMEM((rows, LANES), F32)
    pot_flops = 6 * 2 * rows * 256 * 256

    column_rows = jnp.broadcast_to(stick_columns.astype(F32)[None, None, :], (owners, 8, stick_columns.shape[0]))
    payload = jnp.concatenate([sticks, column_rows], 1)
    received = lax.all_to_all(payload, "stick", split_axis=0, concat_axis=0, tiled=True)
    phi, packed = call(
        functools.partial(field_kernel, g),
        (field, half_field),
        [scratch, scratch],
        10**9,
        received,
        t["stick_in"],
        t["backward"],
    )
    pot_tables = [t["forward"], t["backward"], t["z_forward"], t["z_backward"]]
    swap = [(i, i ^ 1) for i in range(groups)]

    def fetched(distance):
        return lax.ppermute(packed, "band", [(i, (i - distance) % groups) for i in range(groups)])

    near = lax.ppermute(packed, "band", swap)
    ahead = fetched(HALF)
    total = call(
        functools.partial(near_kernel, g),
        field,
        [scratch] * 3,
        pot_flops,
        phi,
        near,
        *pot_tables,
        t["coulomb"],
    )
    if groups == 2 * HALF:
        weights = (2.0, 1.0)
        first, second = ahead, lax.ppermute(ahead, "band", swap)
    else:
        weights = (1.0, 0.0)
        behind = fetched(-HALF)
        odd = lax.axis_index("band") % 2 == 1
        first = second = lax.ppermute(jnp.where(odd, behind, ahead), "band", swap)
        total = call(
            functools.partial(middle_kernel, g),
            field,
            [scratch] * 3,
            pot_flops,
            phi,
            ahead,
            behind,
            total,
            *pot_tables,
            t["coulomb"],
        )
    result = call(
        functools.partial(far_kernel, g, weights),
        jax.ShapeDtypeStruct(sticks.shape, F32),
        [scratch] * 3 + [pltpu.VMEM((LANES, owners * stick_columns.shape[0]), F32)],
        pot_flops,
        phi,
        first,
        second,
        total,
        received,
        *pot_tables,
        t["stick_out"],
        t["coulomb"],
    )
    return lax.all_to_all(result, "stick", split_axis=0, concat_axis=0, tiled=True)


def solution(mesh):
    return jax.shard_map(
        on_device,
        mesh=mesh,
        in_specs=(P("band", None, "stick"), P("stick")),
        out_specs=P("band", None, "stick"),
        check_vma=False,
    )
```

profile of v0, /device:TPU:0, one launch (start us, length us, event | category | flops | bytes accessed | tf_op | source)
XLA Modules:
  0.0 83.7 jit_solution(16924952198525847308)
XLA Ops:
  0.0 0.7 convert_element_type.3
  0.7 1.0 %pad_maximum_fusion = f32[8,104,128]{2,1,0:T(8,128)S(1)} fusion(f32[8,8,128]{2,1,0:T(8,128)S(1)} %broadcast_in_dim.2, f32[8,96,128]{2,1,0:T(8,128)} %param.9), kind=kLoop, calls=%fused_computation | loop fusion | flops 106496 | bytes 851968 | tf_op jit(solution)/shard_map/concatenate | solution.py:339
  1.7 19.7 %all_to_all.10.received_ref = f32[8,104,128]{2,1,0:T(8,128)S(1)} all-to-all(f32[8,104,128]{2,1,0:T(8,128)S(1)} %pad_maximum_fusion), channel_id=1, replica_groups=mesh['stick'=8,'band'=4] {'stick'}, dimensions={0} | all-to-all | bytes 851968 | tf_op jit(solution)/shard_map/all_to_all | solution.py:340
  21.5 0.0 copy-done.5
  21.5 0.0 copy-done.3
  21.5 0.0 copy-start.2
  21.5 0.0 copy-start.6
  21.5 6.2 %shard_map.91 = (f32[2304,128]{1,0:T(8,128)S(1)}, f32[1152,128]{1,0:T(8,128)S(1)}) custom-call(f32[8,104,128]{2,1,0:T(8,128)S(1)} %all_to_all.10.received_ref, bf16[256,192]{1,0:T(8,128)(2,1)S(1)} %copy-done.3, bf16[96,192]{1,0:T(8,128)(2,1)S(1)} %copy-done.5), custom_call_target="tpu_custom_call" | custom-call | flops 1000000000 | bytes 561152 | tf_op jit(solution)/shard_map/pallas_call | solution.py:316
  27.7 1.6 %collective-permute-start = (f32[1152,128]{1,0:T(8,128)S(1)}, f32[1152,128]{1,0:T(8,128)S(1)}, u32[]{:S(2)}, u32[]{:S(2)}) collective-permute-start(f32[1152,128]{1,0:T(8,128)S(1)} %get-tuple-element.8), channel_id=1, source_target_pairs={{0,2},{1,3},{2,0},{3,1},{4,6},{5,7},{6,4},{7,5},{8,10},{9,11},{10,... | collective-permute-start | bytes 1769480 | tf_op jit(solution)/shard_map/ppermute | solution.py:354
  29.3 0.0 collective-permute-start.2
  29.3 12.2 %collective-permute-done.first_ref = f32[1152,128]{1,0:T(8,128)S(1)} collective-permute-done((f32[1152,128]{1,0:T(8,128)S(1)}, f32[1152,128]{1,0:T(8,128)S(1)}, u32[]{:S(2)}, u32[]{:S(2)}) %collective-permute-start) | collective-permute-done | bytes 589856 | tf_op jit(solution)/shard_map/ppermute | solution.py:354
  41.5 0.0 collective-permute-start.1
  41.5 0.0 collective-permute-done.2.other_ref
  41.5 0.0 copy-done
  41.5 0.0 copy-done.1
  41.5 0.0 copy-done.2
  41.6 0.0 copy-done.6
  41.6 0.0 copy-start.4
  41.6 9.0 %shard_map.92.sum_ref = f32[2304,128]{1,0:T(8,128)S(1)} custom-call(f32[2304,128]{1,0:T(8,128)S(1)} %get-tuple-element.7.phi_ref, f32[1152,128]{1,0:T(8,128)S(1)} %collective-permute-done.2.other_ref, bf16[96,192]{1,0:T(8,128)(2,1)S(1)} %copy-done.6, bf16[96,192]{1,0:T(8,128)(2,1)S(1)} %copy-done.5, bf16[256,256]{1,0:T(8,128)(2,1)S(1)} %copy-done.2, ...), custom_call_target="tpu_custom_call" | custom-call | flops 1811939328 | bytes 3284992 | tf_op jit(solution)/shard_map/pallas_call | solution.py:316
  50.6 0.0 collective-permute-done.1.second_ref
  50.6 0.0 copy-done.4
  50.6 15.3 %shard_map.93 = f32[8,96,128]{2,1,0:T(8,128)S(1)} custom-call(f32[2304,128]{1,0:T(8,128)S(1)} %get-tuple-element.7.phi_ref, f32[1152,128]{1,0:T(8,128)S(1)} %collective-permute-done.first_ref, f32[1152,128]{1,0:T(8,128)S(1)} %collective-permute-done.1.second_ref, f32[2304,128]{1,0:T(8,128)S(1)} %shard_map.92.sum_ref, ...), custom_call_target="tpu_custom_call" | custom-call | flops 1811939328 | bytes 5578752 | tf_op jit(solution)/shard_map/pallas_call | solution.py:316
  65.9 17.0 %all_to_all.11 = f32[8,96,128]{2,1,0:T(8,128)S(1)} all-to-all(f32[8,96,128]{2,1,0:T(8,128)S(1)} %shard_map.93), channel_id=1, replica_groups=mesh['stick'=8,'band'=4] {'stick'}, dimensions={0} | all-to-all | bytes 786432 | tf_op jit(solution)/shard_map/all_to_all | solution.py:402
  82.9 0.7 copy.11
  (5 shorter events, 0.0 us)
Async XLA Ops:
  0.0 21.5 %copy-start.5 = (bf16[96,192]{1,0:T(8,128)(2,1)S(1)}, bf16[96,192]{1,0:T(8,128)(2,1)}, u32[]{:S(2)}) copy-start(bf16[96,192]{1,0:T(8,128)(2,1)} %constant.15.clone.backward_ref) | copy-start | bytes 110596
  0.0 21.5 %copy-start.3 = (bf16[256,192]{1,0:T(8,128)(2,1)S(1)}, bf16[256,192]{1,0:T(8,128)(2,1)}, u32[]{:S(2)}) copy-start(bf16[256,192]{1,0:T(8,128)(2,1)} %constant.18.clone.stick_in_ref) | copy-start | bytes 294916
  21.5 20.0 %copy-start = (f32[48,48,128]{2,1,0:T(8,128)S(1)}, f32[48,48,128]{2,1,0:T(8,128)}, u32[]{:S(2)}) copy-start(f32[48,48,128]{2,1,0:T(8,128)} %constant.20.clone.coulomb_ref) | copy-start | bytes 3538948
  21.5 20.1 %copy-start.1 = (bf16[256,256]{1,0:T(8,128)(2,1)S(1)}, bf16[256,256]{1,0:T(8,128)(2,1)}, u32[]{:S(2)}) copy-start(bf16[256,256]{1,0:T(8,128)(2,1)} %constant.17.clone.z_backward_ref) | copy-start | bytes 393220
  21.5 20.1 %copy-start.2 = (bf16[256,256]{1,0:T(8,128)(2,1)S(1)}, bf16[256,256]{1,0:T(8,128)(2,1)}, u32[]{:S(2)}) copy-start(bf16[256,256]{1,0:T(8,128)(2,1)} %constant.16.clone.z_forward_ref) | copy-start | bytes 393220
  21.5 20.0 %copy-start.6 = (bf16[96,192]{1,0:T(8,128)(2,1)S(1)}, bf16[96,192]{1,0:T(8,128)(2,1)}, u32[]{:S(2)}) copy-start(bf16[96,192]{1,0:T(8,128)(2,1)} %constant.14.clone.forward_ref) | copy-start | bytes 110596
  27.7 13.8 %collective-permute-start = (f32[1152,128]{1,0:T(8,128)S(1)}, f32[1152,128]{1,0:T(8,128)S(1)}, u32[]{:S(2)}, u32[]{:S(2)}) collective-permute-start(f32[1152,128]{1,0:T(8,128)S(1)} %get-tuple-element.8), channel_id=1, source_target_pairs={{0,2},{1,3},{2,0},{3,1},{4,6},{5,7},{6,4},{7,5},{8,10},{9,11},{10,... | collective-permute-start | bytes 1769480 | tf_op jit(solution)/shard_map/ppermute | solution.py:354
  29.3 12.2 %collective-permute-start.2 = (f32[1152,128]{1,0:T(8,128)S(1)}, f32[1152,128]{1,0:T(8,128)S(1)}, u32[]{:S(2)}, u32[]{:S(2)}) collective-permute-start(f32[1152,128]{1,0:T(8,128)S(1)} %get-tuple-element.8), channel_id=1, source_target_pairs={{0,1},{1,0},{2,3},{3,2},{4,5},{5,4},{6,7},{7,6},{8,9},{9,8},{10,11... | collective-permute-start | bytes 1769480 | tf_op jit(solution)/shard_map/ppermute | solution.py:356
  41.5 9.1 %collective-permute-start.1 = (f32[1152,128]{1,0:T(8,128)S(1)}, f32[1152,128]{1,0:T(8,128)S(1)}, u32[]{:S(2)}, u32[]{:S(2)}) collective-permute-start(f32[1152,128]{1,0:T(8,128)S(1)} %collective-permute-done.first_ref), channel_id=1, source_target_pairs={{0,1},{1,0},{2,3},{3,2},{4,5},{5,4},{6,7},{7,6},{8,9},{9,8},{10,11... | collective-permute-start | bytes 1769480 | tf_op jit(solution)/shard_map/ppermute | solution.py:370
  41.6 9.0 %copy-start.4 = (bf16[192,256]{1,0:T(8,128)(2,1)S(1)}, bf16[192,256]{1,0:T(8,128)(2,1)}, u32[]{:S(2)}) copy-start(bf16[192,256]{1,0:T(8,128)(2,1)} %constant.19.clone.stick_out_ref) | copy-start | bytes 294916
where the time goes:
time: 83.9 us; the launch traced here: 83.7 us
  blocking collectives  36.7 us (44%)
  Pallas kernels  30.5 us (36%)
  waiting for transfers between devices  12.2 us (15%)
  other arithmetic  1.72 us (2%)
  starting transfers between devices  1.56 us (2%)
    pallas_call x3, Pallas kernels, call(): pl.pallas_call(kernel, out_shape=out_shapes, in_specs=[vmem] * len(operan...  30.5 us
    all_to_all x1, blocking collectives, on_device(): lax.all_to_all(payload, 'stick', split_axis=0, concat_axis=0, tiled=True)  19.7 us
    all_to_all x1, blocking collectives, on_device(): lax.all_to_all(result, 'stick', split_axis=0, concat_axis=0, tiled=True)  17 us
    ppermute x1, waiting for transfers between devices, fetched(): lax.ppermute(packed, 'band', [(i, (i - distance) % groups) for i in range...  12.2 us
  transfers between devices with their start and end apart: 3, of which 1 were waited for; matrix products, arithmetic and copies ran while one was open for 0% of the time, Pallas kernels for 11%

commit v1 on v0

--- a/solution.py
+++ b/solution.py
@@ -139,8 +139,7 @@
 
 
 def chunks(g, body):
-    @pl.loop(0, g // CHUNK)
-    def _(step):
+    for step in range(g // CHUNK):
         body(step * CHUNK)
 
 
@@ -149,13 +148,13 @@
 
 
 def slabs_at(ref, first, g):
-    rows = pl.ds(pl.multiple_of(first * g, CHUNK * g), CHUNK * g)
+    rows = pl.ds(first * g, CHUNK * g)
     block = ref[rows, :]
     return [block[k * g : (k + 1) * g] for k in range(CHUNK)]
 
 
 def store_slabs(ref, first, g, slabs):
-    rows = pl.ds(pl.multiple_of(first * g, CHUNK * g), CHUNK * g)
+    rows = pl.ds(first * g, CHUNK * g)
     ref[rows, :] = jnp.concatenate(slabs, 0)
 
 
@@ -214,7 +213,7 @@
     backward = backward_ref[...]
 
     def first_steps(first):
-        rows = pl.ds(pl.multiple_of(first * g, CHUNK * g), CHUNK * g)
+        rows = pl.ds(first * g, CHUNK * g)
         density = phi_ref[rows, :] * pair_ref[rows, :]
         spectrum = right(density, z_forward_ref[...])
         slabs = [spectrum[k * g : (k + 1) * g] for k in range(CHUNK)]
@@ -253,7 +252,7 @@
     pair_ref[half_rows:, :] = jnp.where(lower, own[half_rows:], other)
 
     def emit(first, potential):
-        rows = pl.ds(pl.multiple_of(first * g, CHUNK * g), CHUNK * g)
+        rows = pl.ds(first * g, CHUNK * g)
         sum_ref[rows, :] = potential * pair_ref[rows, :]
 
     tables = (forward_ref, backward_ref, z_forward_ref, z_backward_ref, coulomb_ref)
@@ -264,7 +263,7 @@
     pair_fields(g, first_ref, second_ref, pair_ref)
 
     def emit(first, potential):
-        rows = pl.ds(pl.multiple_of(first * g, CHUNK * g), CHUNK * g)
+        rows = pl.ds(first * g, CHUNK * g)
         sum_ref[rows, :] = potential * pair_ref[rows, :] + before_ref[rows, :]
 
     tables = (forward_ref, backward_ref, z_forward_ref, z_backward_ref, coulomb_ref)
@@ -276,7 +275,7 @@
     forward = forward_ref[...]
 
     def emit(first, potential):
-        rows = pl.ds(pl.multiple_of(first * g, CHUNK * g), CHUNK * g)
+        rows = pl.ds(first * g, CHUNK * g)
         lower = lower_lanes(potential.shape)
         weight = jnp.where(lower, weights[0], weights[1])
         total = potential * pair_ref[rows, :] * weight + sum_ref[rows, :]
@@ -365,6 +364,7 @@
         *pot_tables,
         t["coulomb"],
     )
+    ahead, total = lax.optimization_barrier((ahead, total))
     if groups == 2 * HALF:
         weights = (2.0, 1.0)
         first, second = ahead, lax.ppermute(ahead, "band", swap)

time: 83.9 us -> 70.9 us (0.85)
  Pallas kernels: 30.5 us -> 19.3 us
  blocking collectives: 36.7 us -> 35.2 us
    pallas_call x3, Pallas kernels: 30.5 us -> 19.3 us  [call(): pl.pallas_call(kernel, out_shape=out_shapes, in_specs=[vmem] * len(operan...]
    ppermute x1, waiting for transfers between devices: 12.2 us -> 9.46 us  [fetched(): lax.ppermute(packed, 'band', [(i, (i - distance) % groups) for i in range...]
    ppermute x1, waiting for transfers between devices: 0.01 us -> 2 us  [on_device(): first, second = (ahead, lax.ppermute(ahead, 'band', swap))]
    all_to_all x1, blocking collectives: 17 us -> 15.5 us  [on_device(): lax.all_to_all(result, 'stick', split_axis=0, concat_axis=0, tiled=True)]
  transfers between devices with their start and end apart: 3 -> 3, of which waited for: 1 -> 3; matrix products, arithmetic and copies ran while one was open for 0% -> 0% of each run, Pallas kernels for 11% -> 6%
where the time goes in v1:
time: 70.9 us; the launch traced here: 70.6 us
  blocking collectives  35.2 us (50%)
  Pallas kernels  19.3 us (27%)
  waiting for transfers between devices  11.9 us (17%)
  other arithmetic  1.72 us (2%)
  starting transfers between devices  1.63 us (2%)
  local copies, waits for them, and re-layouts  0.79 us (1%)
    all_to_all x1, blocking collectives, on_device(): lax.all_to_all(payload, 'stick', split_axis=0, concat_axis=0, tiled=True)  19.7 us
    pallas_call x3, Pallas kernels, call(): pl.pallas_call(kernel, out_shape=out_shapes, in_specs=[vmem] * len(operan...  19.3 us
    all_to_all x1, blocking collectives, on_device(): lax.all_to_all(result, 'stick', split_axis=0, concat_axis=0, tiled=True)  15.5 us
    ppermute x1, waiting for transfers between devices, fetched(): lax.ppermute(packed, 'band', [(i, (i - distance) % groups) for i in range...  9.46 us
    ppermute x1, waiting for transfers between devices, on_device(): first, second = (ahead, lax.ppermute(ahead, 'band', swap))  2 us
    ppermute x1, starting transfers between devices, fetched(): lax.ppermute(packed, 'band', [(i, (i - distance) % groups) for i in range...  1.56 us
  transfers between devices with their start and end apart: 3, of which 3 were waited for; matrix products, arithmetic and copies ran while one was open for 0% of the time, Pallas kernels for 6%

profile of v1, /device:TPU:0, one launch (start us, length us, event | category | flops | bytes accessed | tf_op | source)
XLA Modules:
  0.0 70.6 jit_solution(10694226640242622777)
XLA Ops:
  0.0 0.7 convert_element_type.3
  0.7 1.0 %pad_maximum_fusion = f32[8,104,128]{2,1,0:T(8,128)S(1)} fusion(f32[8,8,128]{2,1,0:T(8,128)S(1)} %broadcast_in_dim.2, f32[8,96,128]{2,1,0:T(8,128)} %param.9), kind=kLoop, calls=%fused_computation | loop fusion | flops 106496 | bytes 851968 | tf_op jit(solution)/shard_map/concatenate | solution.py:338
  1.7 19.7 %all_to_all.10.received_ref = f32[8,104,128]{2,1,0:T(8,128)S(1)} all-to-all(f32[8,104,128]{2,1,0:T(8,128)S(1)} %pad_maximum_fusion), channel_id=1, replica_groups=mesh['stick'=8,'band'=4] {'stick'}, dimensions={0} | all-to-all | bytes 851968 | tf_op jit(solution)/shard_map/all_to_all | solution.py:339
  21.5 0.0 copy-done.5
  21.5 0.0 copy-done.3
  21.5 0.0 copy-start.2
  21.5 0.0 copy-start.6
  21.5 5.1 %shard_map.91 = (f32[2304,128]{1,0:T(8,128)S(1)}, f32[1152,128]{1,0:T(8,128)S(1)}) custom-call(f32[8,104,128]{2,1,0:T(8,128)S(1)} %all_to_all.10.received_ref, bf16[256,192]{1,0:T(8,128)(2,1)S(1)} %copy-done.3, bf16[96,192]{1,0:T(8,128)(2,1)S(1)} %copy-done.5), custom_call_target="tpu_custom_call" | custom-call | flops 1000000000 | bytes 561152 | tf_op jit(solution)/shard_map/pallas_call | solution.py:315
  26.6 0.1 collective-permute-start.1
  26.7 1.6 %collective-permute-start = (f32[1152,128]{1,0:T(8,128)S(1)}, f32[1152,128]{1,0:T(8,128)S(1)}, u32[]{:S(2)}, u32[]{:S(2)}) collective-permute-start(f32[1152,128]{1,0:T(8,128)S(1)} %get-tuple-element.10), channel_id=1, source_target_pairs={{0,2},{1,3},{2,0},{3,1},{4,6},{5,7},{6,4},{7,5},{8,10},{9,11},{10,... | collective-permute-start | bytes 1769480 | tf_op jit(solution)/shard_map/ppermute | solution.py:353
  28.2 0.4 collective-permute-done.1.other_ref
  28.6 0.0 copy-done
  28.6 0.0 copy-done.1
  28.7 0.0 copy-done.2
  28.7 0.0 copy-done.6
  28.7 0.0 copy-start.4
  28.7 4.3 %shard_map.92.sum_ref = f32[2304,128]{1,0:T(8,128)S(1)} custom-call(f32[2304,128]{1,0:T(8,128)S(1)} %get-tuple-element.9.phi_ref, f32[1152,128]{1,0:T(8,128)S(1)} %collective-permute-done.1.other_ref, bf16[96,192]{1,0:T(8,128)(2,1)S(1)} %copy-done.6, bf16[96,192]{1,0:T(8,128)(2,1)S(1)} %copy-done.5, bf16[256,256]{1,0:T(8,128)(2,1)S(1)} %copy-done.2, ...), custom_call_target="tpu_custom_call" | custom-call | flops 1811939328 | bytes 3284992 | tf_op jit(solution)/shard_map/pallas_call | solution.py:315
  32.9 9.5 %collective-permute-done.first_ref = f32[1152,128]{1,0:T(8,128)S(1)} collective-permute-done((f32[1152,128]{1,0:T(8,128)S(1)}, f32[1152,128]{1,0:T(8,128)S(1)}, u32[]{:S(2)}, u32[]{:S(2)}) %collective-permute-start) | collective-permute-done | bytes 589856 | tf_op jit(solution)/shard_map/ppermute | solution.py:353
  42.4 0.0 collective-permute-start.2
  42.4 2.0 %collective-permute-done.2.second_ref = f32[1152,128]{1,0:T(8,128)S(1)} collective-permute-done((f32[1152,128]{1,0:T(8,128)S(1)}, f32[1152,128]{1,0:T(8,128)S(1)}, u32[]{:S(2)}, u32[]{:S(2)}) %collective-permute-start.2) | collective-permute-done | bytes 589856 | tf_op jit(solution)/shard_map/ppermute | solution.py:370
  44.4 0.0 copy-done.4
  44.4 10.0 %shard_map.93 = f32[8,96,128]{2,1,0:T(8,128)S(1)} custom-call(f32[2304,128]{1,0:T(8,128)S(1)} %get-tuple-element.9.phi_ref, f32[1152,128]{1,0:T(8,128)S(1)} %collective-permute-done.first_ref, f32[1152,128]{1,0:T(8,128)S(1)} %collective-permute-done.2.second_ref, f32[2304,128]{1,0:T(8,128)S(1)} %shard_map.92.sum_ref, ...), custom_call_target="tpu_custom_call" | custom-call | flops 1811939328 | bytes 5578752 | tf_op jit(solution)/shard_map/pallas_call | solution.py:315
  54.4 15.5 %all_to_all.11 = f32[8,96,128]{2,1,0:T(8,128)S(1)} all-to-all(f32[8,96,128]{2,1,0:T(8,128)S(1)} %shard_map.93), channel_id=1, replica_groups=mesh['stick'=8,'band'=4] {'stick'}, dimensions={0} | all-to-all | bytes 786432 | tf_op jit(solution)/shard_map/all_to_all | solution.py:402
  69.9 0.7 %copy.11 = f32[8,96,128]{2,1,0:T(8,128)} copy(f32[8,96,128]{2,1,0:T(8,128)S(1)} %all_to_all.11) | data formatting | bytes 786432
  (5 shorter events, 0.0 us)
Async XLA Ops:
  0.0 21.5 %copy-start.5 = (bf16[96,192]{1,0:T(8,128)(2,1)S(1)}, bf16[96,192]{1,0:T(8,128)(2,1)}, u32[]{:S(2)}) copy-start(bf16[96,192]{1,0:T(8,128)(2,1)} %constant.15.clone.backward_ref) | copy-start | bytes 110596
  0.0 21.5 %copy-start.3 = (bf16[256,192]{1,0:T(8,128)(2,1)S(1)}, bf16[256,192]{1,0:T(8,128)(2,1)}, u32[]{:S(2)}) copy-start(bf16[256,192]{1,0:T(8,128)(2,1)} %constant.18.clone.stick_in_ref) | copy-start | bytes 294916
  21.5 7.2 %copy-start = (f32[48,48,128]{2,1,0:T(8,128)S(1)}, f32[48,48,128]{2,1,0:T(8,128)}, u32[]{:S(2)}) copy-start(f32[48,48,128]{2,1,0:T(8,128)} %constant.20.clone.coulomb_ref) | copy-start | bytes 3538948
  21.5 7.2 %copy-start.1 = (bf16[256,256]{1,0:T(8,128)(2,1)S(1)}, bf16[256,256]{1,0:T(8,128)(2,1)}, u32[]{:S(2)}) copy-start(bf16[256,256]{1,0:T(8,128)(2,1)} %constant.17.clone.z_backward_ref) | copy-start | bytes 393220
  21.5 7.2 %copy-start.2 = (bf16[256,256]{1,0:T(8,128)(2,1)S(1)}, bf16[256,256]{1,0:T(8,128)(2,1)}, u32[]{:S(2)}) copy-start(bf16[256,256]{1,0:T(8,128)(2,1)} %constant.16.clone.z_forward_ref) | copy-start | bytes 393220
  21.5 7.2 %copy-start.6 = (bf16[96,192]{1,0:T(8,128)(2,1)S(1)}, bf16[96,192]{1,0:T(8,128)(2,1)}, u32[]{:S(2)}) copy-start(bf16[96,192]{1,0:T(8,128)(2,1)} %constant.14.clone.forward_ref) | copy-start | bytes 110596
  26.6 2.1 %collective-permute-start.1 = (f32[1152,128]{1,0:T(8,128)S(1)}, f32[1152,128]{1,0:T(8,128)S(1)}, u32[]{:S(2)}, u32[]{:S(2)}) collective-permute-start(f32[1152,128]{1,0:T(8,128)S(1)} %get-tuple-element.10), channel_id=1, source_target_pairs={{0,1},{1,0},{2,3},{3,2},{4,5},{5,4},{6,7},{7,6},{8,9},{9,8},{10,11... | collective-permute-start | bytes 1769480 | tf_op jit(solution)/shard_map/ppermute | solution.py:355
  26.7 15.7 %collective-permute-start = (f32[1152,128]{1,0:T(8,128)S(1)}, f32[1152,128]{1,0:T(8,128)S(1)}, u32[]{:S(2)}, u32[]{:S(2)}) collective-permute-start(f32[1152,128]{1,0:T(8,128)S(1)} %get-tuple-element.10), channel_id=1, source_target_pairs={{0,2},{1,3},{2,0},{3,1},{4,6},{5,7},{6,4},{7,5},{8,10},{9,11},{10,... | collective-permute-start | bytes 1769480 | tf_op jit(solution)/shard_map/ppermute | solution.py:353
  28.7 15.7 %copy-start.4 = (bf16[192,256]{1,0:T(8,128)(2,1)S(1)}, bf16[192,256]{1,0:T(8,128)(2,1)}, u32[]{:S(2)}) copy-start(bf16[192,256]{1,0:T(8,128)(2,1)} %constant.19.clone.stick_out_ref) | copy-start | bytes 294916
  42.4 2.0 %collective-permute-start.2 = (f32[1152,128]{1,0:T(8,128)S(1)}, f32[1152,128]{1,0:T(8,128)S(1)}, u32[]{:S(2)}, u32[]{:S(2)}) collective-permute-start(f32[1152,128]{1,0:T(8,128)S(1)} %collective-permute-done.first_ref), channel_id=1, source_target_pairs={{0,1},{1,0},{2,3},{3,2},{4,5},{5,4},{6,7},{7,6},{8,9},{9,8},{10,11... | collective-permute-start | bytes 1769480 | tf_op jit(solution)/shard_map/ppermute | solution.py:370

commit v2 on v1

--- a/solution.py
+++ b/solution.py
@@ -163,20 +163,30 @@
     return jnp.where(index == columns - first, 1.0, 0.0).astype(BF16)
 
 
-def all_columns(received_ref, row):
-    count = received_ref.shape[0]
-    rows = [received_ref[k, row : row + 1, :] for k in range(count)]
-    return jnp.concatenate(rows, 1).astype(jnp.int32)
-
-
-def field_kernel(g, received_ref, stick_in_ref, backward_ref, phi_ref, packed_ref, work_a, work_b):
-    count = received_ref.shape[0]
-    columns = all_columns(received_ref, 2 * g)
+def send_kernel(g, sticks_ref, columns_ref, *block_refs):
+    own = lax.axis_index("stick")
+    columns = jnp.broadcast_to(columns_ref[...].astype(F32), (8, LANES))
+    for d, block_ref in enumerate(block_refs):
+        block_ref[: 2 * g, :] = sticks_ref[own ^ d]
+        block_ref[2 * g :, :] = columns
+
+
+def place_kernel(*refs):
+    own = lax.axis_index("stick")
+    out_ref = refs[-1]
+    for d, block_ref in enumerate(refs[:-1]):
+        out_ref[own ^ d] = block_ref[...]
+
+
+def field_kernel(g, count, *refs):
+    received, (stick_in_ref, backward_ref, phi_ref, packed_ref, columns_ref, work_a, work_b) = refs[:count], refs[count:]
+    columns = jnp.concatenate([ref[2 * g : 2 * g + 1, :] for ref in received], 1).astype(jnp.int32)
+    columns_ref[...] = jnp.broadcast_to(columns, columns_ref.shape)
     stick_in = stick_in_ref[...]
     backward = backward_ref[...]
     pieces = []
     for k in range(0, count, 2):
-        block = jnp.concatenate([received_ref[k, : 2 * g, :], received_ref[k + 1, : 2 * g, :]], 1)
+        block = jnp.concatenate([received[k][: 2 * g, :], received[k + 1][: 2 * g, :]], 1)
         both = dot(stick_in, jnp.concatenate(split(block), 0))
         lined = both[:LANES] + both[LANES:]
         pieces.append(jnp.concatenate(split(lined.T), 1))
@@ -270,7 +280,8 @@
     potentials(g, phi_ref, pair_ref, tables, work_a, work_b, emit)
 
 
-def far_kernel(g, weights, phi_ref, first_ref, second_ref, sum_ref, received_ref, forward_ref, backward_ref, z_forward_ref, z_backward_ref, stick_out_ref, coulomb_ref, out_ref, pair_ref, work_a, work_b, picked):
+def far_kernel(g, weights, phi_ref, first_ref, second_ref, sum_ref, columns_ref, forward_ref, backward_ref, z_forward_ref, z_backward_ref, stick_out_ref, coulomb_ref, *rest):
+    out_refs, (pair_ref, work_a, work_b, picked) = rest[:-4], rest[-4:]
     pair_fields(g, first_ref, second_ref, pair_ref)
     forward = forward_ref[...]
 
@@ -291,7 +302,7 @@
     tables = (forward_ref, backward_ref, z_forward_ref, z_backward_ref, coulomb_ref)
     potentials(g, phi_ref, pair_ref, tables, work_a, work_b, emit)
 
-    columns = all_columns(received_ref, 2 * g)
+    columns = columns_ref[:1, :]
     picked[...] = jnp.zeros_like(picked)
 
     def pick(first):
@@ -305,8 +316,8 @@
     chunks(g, pick)
     result = dot(stick_out_ref[...], jnp.concatenate(split(picked[...]), 0))
     result = result[: 2 * g] + result[2 * g :]
-    for k in range(out_ref.shape[0]):
-        out_ref[k] = result[:, k * LANES : (k + 1) * LANES]
+    for k, out_ref in enumerate(out_refs):
+        out_ref[...] = result[:, k * LANES : (k + 1) * LANES]
 
 
 def call(kernel, out_shapes, scratch, flops, *operands):
@@ -323,6 +334,14 @@
     )(*operands)
 
 
+def exchanged(blocks):
+    owners = len(blocks)
+    moved = {}
+    for d in range(owners - 1, 0, -1):
+        moved[d] = lax.ppermute(blocks[d], "stick", [(i, i ^ d) for i in range(owners)])
+    return [blocks[0]] + [moved[d] for d in range(1, owners)]
+
+
 def on_device(sticks, stick_columns):
     g = sticks.shape[1] // 2
     owners = lax.axis_size("stick")
@@ -334,15 +353,22 @@
     scratch = pltpu.VMEM((rows, LANES), F32)
     pot_flops = 6 * 2 * rows * 256 * 256
 
-    column_rows = jnp.broadcast_to(stick_columns.astype(F32)[None, None, :], (owners, 8, stick_columns.shape[0]))
-    payload = jnp.concatenate([sticks, column_rows], 1)
-    received = lax.all_to_all(payload, "stick", split_axis=0, concat_axis=0, tiled=True)
-    phi, packed = call(
-        functools.partial(field_kernel, g),
-        (field, half_field),
+    slots = stick_columns.shape[0]
+    sent = call(
+        functools.partial(send_kernel, g),
+        [jax.ShapeDtypeStruct((2 * g + 8, slots), F32)] * owners,
+        [],
+        10**6,
+        sticks,
+        stick_columns[None, :],
+    )
+    received = exchanged(sent)
+    phi, packed, columns = call(
+        functools.partial(field_kernel, g, owners),
+        [field, half_field, jax.ShapeDtypeStruct((8, owners * slots), jnp.int32)],
         [scratch, scratch],
         10**9,
-        received,
+        *received,
         t["stick_in"],
         t["backward"],
     )
@@ -387,19 +413,19 @@
         )
     result = call(
         functools.partial(far_kernel, g, weights),
-        jax.ShapeDtypeStruct(sticks.shape, F32),
-        [scratch] * 3 + [pltpu.VMEM((LANES, owners * stick_columns.shape[0]), F32)],
+        [jax.ShapeDtypeStruct((2 * g, slots), F32)] * owners,
+        [scratch] * 3 + [pltpu.VMEM((LANES, owners * slots), F32)],
         pot_flops,
         phi,
         first,
         second,
         total,
-        received,
+        columns,
         *pot_tables,
         t["stick_out"],
         t["coulomb"],
     )
-    return lax.all_to_all(result, "stick", split_axis=0, concat_axis=0, tiled=True)
+    return call(place_kernel, jax.ShapeDtypeStruct(sticks.shape, F32), [], 10**6, *exchanged(result))
 
 
 def solution(mesh):

time: 70.9 us -> 70.6 us (level)
  blocking collectives: 35.2 us -> 0 us
  starting transfers between devices: 1.63 us -> 25.3 us
  waiting for transfers between devices: 11.9 us -> 21.4 us
  local copies, waits for them, and re-layouts: 0.79 us -> 3.38 us
  other arithmetic: 1.72 us -> 0 us
  Pallas kernels: 19.3 us -> 20.1 us
    all_to_all x2 -> x0, blocking collectives: 35.2 us -> none  [the longest x1 19.7 us: on_device(): lax.all_to_all(payload, 'stick', split_axis=0, concat_axis=0, tiled=True)]
    ppermute x0 -> x14, starting transfers between devices: none -> 23.7 us  [exchanged(): lax.ppermute(blocks[d], 'stick', [(i, i ^ d) for i in range(owners)])]
    ppermute x0 -> x14, waiting for transfers between devices: none -> 9.56 us  [exchanged(): lax.ppermute(blocks[d], 'stick', [(i, i ^ d) for i in range(owners)])]
    unnamed x15 -> x20, local copies, waits for them, and re-layouts: 0.78 us -> 3.38 us
    concatenate x1 -> x0, other arithmetic: 1.02 us -> none  [on_device(): payload = jnp.concatenate([sticks, column_rows], 1)]
    pallas_call x3 -> x5, Pallas kernels: 19.3 us -> 20.1 us  [call(): pl.pallas_call(kernel, out_shape=out_shapes, in_specs=[vmem] * len(operan...]
  transfers between devices with their start and end apart: 3 -> 17, of which waited for: 3 -> 8; matrix products, arithmetic and copies ran while one was open for 0% -> 0% of each run, Pallas kernels for 6% -> 6%
where the time goes in v2:
time: 70.6 us; the launch traced here: 70.4 us
  starting transfers between devices  25.3 us (36%)
  waiting for transfers between devices  21.4 us (30%)
  Pallas kernels  20.1 us (28%)
  local copies, waits for them, and re-layouts  3.38 us (5%)
    ppermute x14, starting transfers between devices, exchanged(): lax.ppermute(blocks[d], 'stick', [(i, i ^ d) for i in range(owners)])  23.7 us
    pallas_call x5, Pallas kernels, call(): pl.pallas_call(kernel, out_shape=out_shapes, in_specs=[vmem] * len(operan...  20.1 us
    ppermute x14, waiting for transfers between devices, exchanged(): lax.ppermute(blocks[d], 'stick', [(i, i ^ d) for i in range(owners)])  9.56 us
    ppermute x1, waiting for transfers between devices, fetched(): lax.ppermute(packed, 'band', [(i, (i - distance) % groups) for i in range...  9.44 us
    unnamed x20, local copies, waits for them, and re-layouts  3.38 us
    ppermute x1, waiting for transfers between devices, on_device(): first, second = (ahead, lax.ppermute(ahead, 'band', swap))  2 us
    ppermute x1, starting transfers between devices, fetched(): lax.ppermute(packed, 'band', [(i, (i - distance) % groups) for i in range...  1.55 us
  transfers between devices with their start and end apart: 17, of which 8 were waited for; matrix products, arithmetic and copies ran while one was open for 0% of the time, Pallas kernels for 6%

profile of v2, /device:TPU:0, one launch (start us, length us, event | category | flops | bytes accessed | tf_op | source)
XLA Modules:
  0.0 70.4 jit_solution(443644804352871290)
XLA Ops:
  0.0 1.0 %copy-done = f32[8,96,128]{2,1,0:T(8,128)S(1)} copy-done((f32[8,96,128]{2,1,0:T(8,128)S(1)}, f32[8,96,128]{2,1,0:T(8,128)}, u32[]{:S(2)}) %copy-start) | copy-done | bytes 393240
  1.7 3.0 %collective-permute-start = (f32[104,128]{1,0:T(8,128)S(1)}, f32[104,128]{1,0:T(8,128)S(1)}, u32[]{:S(2)}, u32[]{:S(2)}) collective-permute-start(f32[104,128]{1,0:T(8,128)S(1)} %get-tuple-element.27), channel_id=1, source_target_pairs={{0,4},{4,0},{8,12},{12,8},{16,20},{20,16},{24,28},{28,24},{1,5},{5... | collective-permute-start | bytes 159752 | tf_op jit(solution)/shard_map/ppermute | solution.py:341
  4.7 1.6 %collective-permute-start.1 = (f32[104,128]{1,0:T(8,128)S(1)}, f32[104,128]{1,0:T(8,128)S(1)}, u32[]{:S(2)}, u32[]{:S(2)}) collective-permute-start(f32[104,128]{1,0:T(8,128)S(1)} %get-tuple-element.28), channel_id=1, source_target_pairs={{0,8},{4,12},{8,0},{12,4},{16,24},{20,28},{24,16},{28,20},{1,9},{5... | collective-permute-start | bytes 159752 | tf_op jit(solution)/shard_map/ppermute | solution.py:341
  6.3 3.0 %collective-permute-start.3 = (f32[104,128]{1,0:T(8,128)S(1)}, f32[104,128]{1,0:T(8,128)S(1)}, u32[]{:S(2)}, u32[]{:S(2)}) collective-permute-start(f32[104,128]{1,0:T(8,128)S(1)} %get-tuple-element.30), channel_id=1, source_target_pairs={{0,16},{4,20},{8,24},{12,28},{16,0},{20,4},{24,8},{28,12},{1,17},{... | collective-permute-start | bytes 159752 | tf_op jit(solution)/shard_map/ppermute | solution.py:341
  9.3 1.3 %collective-permute-start.4 = (f32[104,128]{1,0:T(8,128)S(1)}, f32[104,128]{1,0:T(8,128)S(1)}, u32[]{:S(2)}, u32[]{:S(2)}) collective-permute-start(f32[104,128]{1,0:T(8,128)S(1)} %get-tuple-element.31), channel_id=1, source_target_pairs={{0,20},{4,16},{8,28},{12,24},{16,4},{20,0},{24,12},{28,8},{1,21},{... | collective-permute-start | bytes 159752 | tf_op jit(solution)/shard_map/ppermute | solution.py:341
  10.6 3.6 %collective-permute-start.5 = (f32[104,128]{1,0:T(8,128)S(1)}, f32[104,128]{1,0:T(8,128)S(1)}, u32[]{:S(2)}, u32[]{:S(2)}) collective-permute-start(f32[104,128]{1,0:T(8,128)S(1)} %get-tuple-element.32), channel_id=1, source_target_pairs={{0,24},{4,28},{8,16},{12,20},{16,8},{20,12},{24,0},{28,4},{1,25},{... | collective-permute-start | bytes 159752 | tf_op jit(solution)/shard_map/ppermute | solution.py:341
  14.2 3.3 %collective-permute-done.4.refs_5_ = f32[104,128]{1,0:T(8,128)S(1)} collective-permute-done((f32[104,128]{1,0:T(8,128)S(1)}, f32[104,128]{1,0:T(8,128)S(1)}, u32[]{:S(2)}, u32[]{:S(2)}) %collective-permute-start.4) | collective-permute-done | bytes 53280 | tf_op jit(solution)/shard_map/ppermute | solution.py:341
  17.5 3.5 %collective-permute-done.6.refs_7_ = f32[104,128]{1,0:T(8,128)S(1)} collective-permute-done((f32[104,128]{1,0:T(8,128)S(1)}, f32[104,128]{1,0:T(8,128)S(1)}, u32[]{:S(2)}, u32[]{:S(2)}) %collective-permute-start.6) | collective-permute-done | bytes 53280 | tf_op jit(solution)/shard_map/ppermute | solution.py:341
  21.0 0.9 %copy-done.5 = bf16[256,192]{1,0:T(8,128)(2,1)S(1)} copy-done((bf16[256,192]{1,0:T(8,128)(2,1)S(1)}, bf16[256,192]{1,0:T(8,128)(2,1)}, u32[]{:S(2)}) %copy-start.5) | copy-done | bytes 98328
  21.9 0.8 %copy-done.7 = bf16[96,192]{1,0:T(8,128)(2,1)S(1)} copy-done((bf16[96,192]{1,0:T(8,128)(2,1)S(1)}, bf16[96,192]{1,0:T(8,128)(2,1)}, u32[]{:S(2)}) %copy-start.7) | copy-done | bytes 36888
  22.7 5.1 %shard_map.92 = (f32[2304,128]{1,0:T(8,128)S(1)}, f32[1152,128]{1,0:T(8,128)S(1)}, s32[8,1024]{1,0:T(8,128)S(1)}) custom-call(f32[104,128]{1,0:T(8,128)S(1)} %get-tuple-element.26.refs_0_, f32[104,128]{1,0:T(8,128)S(1)} %collective-permute-done.refs_1_, f32[104,128]{1,0:T(8,128)S(1)} %collective-permute-done.1.refs_2_, ...), custom_call_target="tpu_custom_call" | custom-call | flops 1000000000 | bytes 561152 | tf_op jit(solution)/shard_map/pallas_call | solution.py:326
  27.9 1.6 %collective-permute-start.7 = (f32[1152,128]{1,0:T(8,128)S(1)}, f32[1152,128]{1,0:T(8,128)S(1)}, u32[]{:S(2)}, u32[]{:S(2)}) collective-permute-start(f32[1152,128]{1,0:T(8,128)S(1)} %get-tuple-element.35), channel_id=1, source_target_pairs={{0,2},{1,3},{2,0},{3,1},{4,6},{5,7},{6,4},{7,5},{8,10},{9,11},{10,... | collective-permute-start | bytes 1769480 | tf_op jit(solution)/shard_map/ppermute | solution.py:379
  29.9 4.3 %shard_map.93.sum_ref = f32[2304,128]{1,0:T(8,128)S(1)} custom-call(f32[2304,128]{1,0:T(8,128)S(1)} %get-tuple-element.34.phi_ref, f32[1152,128]{1,0:T(8,128)S(1)} %collective-permute-done.8.other_ref, bf16[96,192]{1,0:T(8,128)(2,1)S(1)} %copy-done.9, bf16[96,192]{1,0:T(8,128)(2,1)S(1)} %copy-done.8, bf16[256,256]{1,0:T(8,128)(2,1)S(1)} %copy-done.4, ...), custom_call_target="tpu_custom_call" | custom-call | flops 1811939328 | bytes 3284992 | tf_op jit(solution)/shard_map/pallas_call | solution.py:326
  34.2 9.4 %collective-permute-done.7.first_ref = f32[1152,128]{1,0:T(8,128)S(1)} collective-permute-done((f32[1152,128]{1,0:T(8,128)S(1)}, f32[1152,128]{1,0:T(8,128)S(1)}, u32[]{:S(2)}, u32[]{:S(2)}) %collective-permute-start.7) | collective-permute-done | bytes 589856 | tf_op jit(solution)/shard_map/ppermute | solution.py:379
  43.6 2.0 %collective-permute-done.9.second_ref = f32[1152,128]{1,0:T(8,128)S(1)} collective-permute-done((f32[1152,128]{1,0:T(8,128)S(1)}, f32[1152,128]{1,0:T(8,128)S(1)}, u32[]{:S(2)}, u32[]{:S(2)}) %collective-permute-start.9) | collective-permute-done | bytes 589856 | tf_op jit(solution)/shard_map/ppermute | solution.py:396
  45.6 10.0 %shard_map.94 = (f32[96,128]{1,0:T(8,128)S(1)}, f32[96,128]{1,0:T(8,128)S(1)}, f32[96,128]{1,0:T(8,128)S(1)}, f32[96,128]{1,0:T(8,128)S(1)}, f32[96,128]{1,0:T(8...) custom-call(f32[2304,128]{1,0:T(8,128)S(1)} %get-tuple-element.34.phi_ref, ...), custom_call_target="tpu_custom_call" | custom-call | flops 1811939328 | bytes 5185536 | tf_op jit(solution)/shard_map/pallas_call | solution.py:326
  56.2 3.0 %collective-permute-start.12 = (f32[96,128]{1,0:T(8,128)S(1)}, f32[96,128]{1,0:T(8,128)S(1)}, u32[]{:S(2)}, u32[]{:S(2)}) collective-permute-start(f32[96,128]{1,0:T(8,128)S(1)} %get-tuple-element.42), channel_id=1, source_target_pairs={{0,12},{4,8},{8,4},{12,0},{16,28},{20,24},{24,20},{28,16},{1,13},{... | collective-permute-start | bytes 147464 | tf_op jit(solution)/shard_map/ppermute | solution.py:341
  59.2 0.8 %collective-permute-start.13 = (f32[96,128]{1,0:T(8,128)S(1)}, f32[96,128]{1,0:T(8,128)S(1)}, u32[]{:S(2)}, u32[]{:S(2)}) collective-permute-start(f32[96,128]{1,0:T(8,128)S(1)} %get-tuple-element.43), channel_id=1, source_target_pairs={{0,16},{4,20},{8,24},{12,28},{16,0},{20,4},{24,8},{28,12},{1,17},{... | collective-permute-start | bytes 147464 | tf_op jit(solution)/shard_map/ppermute | solution.py:341
  60.1 2.0 %collective-permute-start.14 = (f32[96,128]{1,0:T(8,128)S(1)}, f32[96,128]{1,0:T(8,128)S(1)}, u32[]{:S(2)}, u32[]{:S(2)}) collective-permute-start(f32[96,128]{1,0:T(8,128)S(1)} %get-tuple-element.44), channel_id=1, source_target_pairs={{0,20},{4,16},{8,28},{12,24},{16,4},{20,0},{24,12},{28,8},{1,21},{... | collective-permute-start | bytes 147464 | tf_op jit(solution)/shard_map/ppermute | solution.py:341
  62.1 0.7 %collective-permute-start.15 = (f32[96,128]{1,0:T(8,128)S(1)}, f32[96,128]{1,0:T(8,128)S(1)}, u32[]{:S(2)}, u32[]{:S(2)}) collective-permute-start(f32[96,128]{1,0:T(8,128)S(1)} %get-tuple-element.45), channel_id=1, source_target_pairs={{0,24},{4,28},{8,16},{12,20},{16,8},{20,12},{24,0},{28,4},{1,25},{... | collective-permute-start | bytes 147464 | tf_op jit(solution)/shard_map/ppermute | solution.py:341
  62.8 4.1 %collective-permute-start.16 = (f32[96,128]{1,0:T(8,128)S(1)}, f32[96,128]{1,0:T(8,128)S(1)}, u32[]{:S(2)}, u32[]{:S(2)}) collective-permute-start(f32[96,128]{1,0:T(8,128)S(1)} %get-tuple-element.46), channel_id=1, source_target_pairs={{0,28},{4,24},{8,20},{12,16},{16,12},{20,8},{24,4},{28,0},{1,29},{... | collective-permute-start | bytes 147464 | tf_op jit(solution)/shard_map/ppermute | solution.py:341
  66.9 1.0 %collective-permute-done.14.refs_5_ = f32[96,128]{1,0:T(8,128)S(1)} collective-permute-done((f32[96,128]{1,0:T(8,128)S(1)}, f32[96,128]{1,0:T(8,128)S(1)}, u32[]{:S(2)}, u32[]{:S(2)}) %collective-permute-start.14) | collective-permute-done | bytes 49184 | tf_op jit(solution)/shard_map/ppermute | solution.py:341
  68.0 1.6 %collective-permute-done.16.refs_7_ = f32[96,128]{1,0:T(8,128)S(1)} collective-permute-done((f32[96,128]{1,0:T(8,128)S(1)}, f32[96,128]{1,0:T(8,128)S(1)}, u32[]{:S(2)}, u32[]{:S(2)}) %collective-permute-start.16) | collective-permute-done | bytes 49184 | tf_op jit(solution)/shard_map/ppermute | solution.py:341
  69.6 0.8 %shard_map.95 = f32[8,96,128]{2,1,0:T(8,128)} custom-call(f32[96,128]{1,0:T(8,128)S(1)} %get-tuple-element.39.refs_0_, f32[96,128]{1,0:T(8,128)S(1)} %collective-permute-done.10.refs_1_, f32[96,128]{1,0:T(8,128)S(1)} %collective-permute-done.11.refs_2_, f32[96,128]{1,0:T(8,128)S(1)} %collective-permute-done.12.refs_3_, ...), custom_call_target="tpu_custom_call" | custom-call | flops 1000000 | bytes 393216 | tf_op jit(solution)/shard_map/pallas_call | solution.py:326
  (35 shorter events, 2.0 us)
Async XLA Ops:
  0.0 1.0 %copy-start = (f32[8,96,128]{2,1,0:T(8,128)S(1)}, f32[8,96,128]{2,1,0:T(8,128)}, u32[]{:S(2)}) copy-start(f32[8,96,128]{2,1,0:T(8,128)} %sticks_ref.1) | copy-start | bytes 1179652
  1.7 8.9 %collective-permute-start = (f32[104,128]{1,0:T(8,128)S(1)}, f32[104,128]{1,0:T(8,128)S(1)}, u32[]{:S(2)}, u32[]{:S(2)}) collective-permute-start(f32[104,128]{1,0:T(8,128)S(1)} %get-tuple-element.27), channel_id=1, source_target_pairs={{0,4},{4,0},{8,12},{12,8},{16,20},{20,16},{24,28},{28,24},{1,5},{5... | collective-permute-start | bytes 159752 | tf_op jit(solution)/shard_map/ppermute | solution.py:341
  4.7 9.5 %collective-permute-start.1 = (f32[104,128]{1,0:T(8,128)S(1)}, f32[104,128]{1,0:T(8,128)S(1)}, u32[]{:S(2)}, u32[]{:S(2)}) collective-permute-start(f32[104,128]{1,0:T(8,128)S(1)} %get-tuple-element.28), channel_id=1, source_target_pairs={{0,8},{4,12},{8,0},{12,4},{16,24},{20,28},{24,16},{28,20},{1,9},{5... | collective-permute-start | bytes 159752 | tf_op jit(solution)/shard_map/ppermute | solution.py:341
  6.3 7.9 %collective-permute-start.2 = (f32[104,128]{1,0:T(8,128)S(1)}, f32[104,128]{1,0:T(8,128)S(1)}, u32[]{:S(2)}, u32[]{:S(2)}) collective-permute-start(f32[104,128]{1,0:T(8,128)S(1)} %get-tuple-element.29), channel_id=1, source_target_pairs={{0,12},{4,8},{8,4},{12,0},{16,28},{20,24},{24,20},{28,16},{1,13},{... | collective-permute-start | bytes 159752 | tf_op jit(solution)/shard_map/ppermute | solution.py:341
  6.3 7.9 %collective-permute-start.3 = (f32[104,128]{1,0:T(8,128)S(1)}, f32[104,128]{1,0:T(8,128)S(1)}, u32[]{:S(2)}, u32[]{:S(2)}) collective-permute-start(f32[104,128]{1,0:T(8,128)S(1)} %get-tuple-element.30), channel_id=1, source_target_pairs={{0,16},{4,20},{8,24},{12,28},{16,0},{20,4},{24,8},{28,12},{1,17},{... | collective-permute-start | bytes 159752 | tf_op jit(solution)/shard_map/ppermute | solution.py:341
  9.3 8.2 %collective-permute-start.4 = (f32[104,128]{1,0:T(8,128)S(1)}, f32[104,128]{1,0:T(8,128)S(1)}, u32[]{:S(2)}, u32[]{:S(2)}) collective-permute-start(f32[104,128]{1,0:T(8,128)S(1)} %get-tuple-element.31), channel_id=1, source_target_pairs={{0,20},{4,16},{8,28},{12,24},{16,4},{20,0},{24,12},{28,8},{1,21},{... | collective-permute-start | bytes 159752 | tf_op jit(solution)/shard_map/ppermute | solution.py:341
  10.6 6.9 %collective-permute-start.5 = (f32[104,128]{1,0:T(8,128)S(1)}, f32[104,128]{1,0:T(8,128)S(1)}, u32[]{:S(2)}, u32[]{:S(2)}) collective-permute-start(f32[104,128]{1,0:T(8,128)S(1)} %get-tuple-element.32), channel_id=1, source_target_pairs={{0,24},{4,28},{8,16},{12,20},{16,8},{20,12},{24,0},{28,4},{1,25},{... | collective-permute-start | bytes 159752 | tf_op jit(solution)/shard_map/ppermute | solution.py:341
  14.2 6.8 %collective-permute-start.6 = (f32[104,128]{1,0:T(8,128)S(1)}, f32[104,128]{1,0:T(8,128)S(1)}, u32[]{:S(2)}, u32[]{:S(2)}) collective-permute-start(f32[104,128]{1,0:T(8,128)S(1)} %get-tuple-element.33), channel_id=1, source_target_pairs={{0,28},{4,24},{8,20},{12,16},{16,12},{20,8},{24,4},{28,0},{1,29},{... | collective-permute-start | bytes 159752 | tf_op jit(solution)/shard_map/ppermute | solution.py:341
  22.7 7.2 %copy-start.2 = (f32[48,48,128]{2,1,0:T(8,128)S(1)}, f32[48,48,128]{2,1,0:T(8,128)}, u32[]{:S(2)}) copy-start(f32[48,48,128]{2,1,0:T(8,128)} %constant.20.clone.coulomb_ref) | copy-start | bytes 3538948
  22.7 7.2 %copy-start.3 = (bf16[256,256]{1,0:T(8,128)(2,1)S(1)}, bf16[256,256]{1,0:T(8,128)(2,1)}, u32[]{:S(2)}) copy-start(bf16[256,256]{1,0:T(8,128)(2,1)} %constant.17.clone.z_backward_ref) | copy-start | bytes 393220
  22.7 7.2 %copy-start.4 = (bf16[256,256]{1,0:T(8,128)(2,1)S(1)}, bf16[256,256]{1,0:T(8,128)(2,1)}, u32[]{:S(2)}) copy-start(bf16[256,256]{1,0:T(8,128)(2,1)} %constant.16.clone.z_forward_ref) | copy-start | bytes 393220
  22.7 7.2 %copy-start.8 = (bf16[96,192]{1,0:T(8,128)(2,1)S(1)}, bf16[96,192]{1,0:T(8,128)(2,1)}, u32[]{:S(2)}) copy-start(bf16[96,192]{1,0:T(8,128)(2,1)} %constant.15.clone.refs_9_.backward_ref) | copy-start | bytes 110596
  22.7 7.2 %copy-start.9 = (bf16[96,192]{1,0:T(8,128)(2,1)S(1)}, bf16[96,192]{1,0:T(8,128)(2,1)}, u32[]{:S(2)}) copy-start(bf16[96,192]{1,0:T(8,128)(2,1)} %constant.14.clone.forward_ref) | copy-start | bytes 110596
  27.8 2.1 %collective-permute-start.8 = (f32[1152,128]{1,0:T(8,128)S(1)}, f32[1152,128]{1,0:T(8,128)S(1)}, u32[]{:S(2)}, u32[]{:S(2)}) collective-permute-start(f32[1152,128]{1,0:T(8,128)S(1)} %get-tuple-element.35), channel_id=1, source_target_pairs={{0,1},{1,0},{2,3},{3,2},{4,5},{5,4},{6,7},{7,6},{8,9},{9,8},{10,11... | collective-permute-start | bytes 1769480 | tf_op jit(solution)/shard_map/ppermute | solution.py:381
  27.9 15.7 %collective-permute-start.7 = (f32[1152,128]{1,0:T(8,128)S(1)}, f32[1152,128]{1,0:T(8,128)S(1)}, u32[]{:S(2)}, u32[]{:S(2)}) collective-permute-start(f32[1152,128]{1,0:T(8,128)S(1)} %get-tuple-element.35), channel_id=1, source_target_pairs={{0,2},{1,3},{2,0},{3,1},{4,6},{5,7},{6,4},{7,5},{8,10},{9,11},{10,... | collective-permute-start | bytes 1769480 | tf_op jit(solution)/shard_map/ppermute | solution.py:379
  29.9 15.7 %copy-start.6 = (bf16[192,256]{1,0:T(8,128)(2,1)S(1)}, bf16[192,256]{1,0:T(8,128)(2,1)}, u32[]{:S(2)}) copy-start(bf16[192,256]{1,0:T(8,128)(2,1)} %constant.19.clone.stick_out_ref) | copy-start | bytes 294916
  43.6 2.0 %collective-permute-start.9 = (f32[1152,128]{1,0:T(8,128)S(1)}, f32[1152,128]{1,0:T(8,128)S(1)}, u32[]{:S(2)}, u32[]{:S(2)}) collective-permute-start(f32[1152,128]{1,0:T(8,128)S(1)} %collective-permute-done.7.first_ref), channel_id=1, source_target_pairs={{0,1},{1,0},{2,3},{3,2},{4,5},{5,4},{6,7},{7,6},{8,9},{9,8},{10,11... | collective-permute-start | bytes 1769480 | tf_op jit(solution)/shard_map/ppermute | solution.py:396
  55.7 6.4 %collective-permute-start.10 = (f32[96,128]{1,0:T(8,128)S(1)}, f32[96,128]{1,0:T(8,128)S(1)}, u32[]{:S(2)}, u32[]{:S(2)}) collective-permute-start(f32[96,128]{1,0:T(8,128)S(1)} %get-tuple-element.40), channel_id=1, source_target_pairs={{0,4},{4,0},{8,12},{12,8},{16,20},{20,16},{24,28},{28,24},{1,5},{5... | collective-permute-start | bytes 147464 | tf_op jit(solution)/shard_map/ppermute | solution.py:341
  56.2 6.6 %collective-permute-start.11 = (f32[96,128]{1,0:T(8,128)S(1)}, f32[96,128]{1,0:T(8,128)S(1)}, u32[]{:S(2)}, u32[]{:S(2)}) collective-permute-start(f32[96,128]{1,0:T(8,128)S(1)} %get-tuple-element.41), channel_id=1, source_target_pairs={{0,8},{4,12},{8,0},{12,4},{16,24},{20,28},{24,16},{28,20},{1,9},{5... | collective-permute-start | bytes 147464 | tf_op jit(solution)/shard_map/ppermute | solution.py:341
  56.2 10.6 %collective-permute-start.12 = (f32[96,128]{1,0:T(8,128)S(1)}, f32[96,128]{1,0:T(8,128)S(1)}, u32[]{:S(2)}, u32[]{:S(2)}) collective-permute-start(f32[96,128]{1,0:T(8,128)S(1)} %get-tuple-element.42), channel_id=1, source_target_pairs={{0,12},{4,8},{8,4},{12,0},{16,28},{20,24},{24,20},{28,16},{1,13},{... | collective-permute-start | bytes 147464 | tf_op jit(solution)/shard_map/ppermute | solution.py:341
  59.2 7.7 %collective-permute-start.13 = (f32[96,128]{1,0:T(8,128)S(1)}, f32[96,128]{1,0:T(8,128)S(1)}, u32[]{:S(2)}, u32[]{:S(2)}) collective-permute-start(f32[96,128]{1,0:T(8,128)S(1)} %get-tuple-element.43), channel_id=1, source_target_pairs={{0,16},{4,20},{8,24},{12,28},{16,0},{20,4},{24,8},{28,12},{1,17},{... | collective-permute-start | bytes 147464 | tf_op jit(solution)/shard_map/ppermute | solution.py:341
  60.1 7.8 %collective-permute-start.14 = (f32[96,128]{1,0:T(8,128)S(1)}, f32[96,128]{1,0:T(8,128)S(1)}, u32[]{:S(2)}, u32[]{:S(2)}) collective-permute-start(f32[96,128]{1,0:T(8,128)S(1)} %get-tuple-element.44), channel_id=1, source_target_pairs={{0,20},{4,16},{8,28},{12,24},{16,4},{20,0},{24,12},{28,8},{1,21},{... | collective-permute-start | bytes 147464 | tf_op jit(solution)/shard_map/ppermute | solution.py:341
  62.1 5.9 %collective-permute-start.15 = (f32[96,128]{1,0:T(8,128)S(1)}, f32[96,128]{1,0:T(8,128)S(1)}, u32[]{:S(2)}, u32[]{:S(2)}) collective-permute-start(f32[96,128]{1,0:T(8,128)S(1)} %get-tuple-element.45), channel_id=1, source_target_pairs={{0,24},{4,28},{8,16},{12,20},{16,8},{20,12},{24,0},{28,4},{1,25},{... | collective-permute-start | bytes 147464 | tf_op jit(solution)/shard_map/ppermute | solution.py:341
  62.8 6.8 %collective-permute-start.16 = (f32[96,128]{1,0:T(8,128)S(1)}, f32[96,128]{1,0:T(8,128)S(1)}, u32[]{:S(2)}, u32[]{:S(2)}) collective-permute-start(f32[96,128]{1,0:T(8,128)S(1)} %get-tuple-element.46), channel_id=1, source_target_pairs={{0,28},{4,24},{8,20},{12,16},{16,12},{20,8},{24,4},{28,0},{1,29},{... | collective-permute-start | bytes 147464 | tf_op jit(solution)/shard_map/ppermute | solution.py:341
  (3 other events, 2.4 us)

commit v3 on v2

v3 whole, which is shorter than its diff:
```python
import functools
import math

import jax
import jax.numpy as jnp
import numpy as np
from jax import lax
from jax.experimental import pallas as pl
from jax.experimental.pallas import tpu as pltpu
from jax.sharding import PartitionSpec as P

HALF = 2
BOX_LENGTH = 18.0
LANES = 128
MID = 64
PAIRS = 4
FOLD = 3

F32 = jnp.float32
BF16 = jnp.bfloat16


def rounded_parts(table):
    high = table.astype(BF16).astype(np.float64)
    low = (table - high).astype(BF16).astype(np.float64)
    return high, low


def across(table):
    high, low = rounded_parts(table)
    return np.concatenate([high, high, low], 1).astype(np.float32)


def down(table):
    high, low = rounded_parts(table)
    return np.concatenate([high, high, low], 0).astype(np.float32)


def make_tables(g):
    angle = 2.0 * np.pi / g * (np.outer(np.arange(g), np.arange(g)) % g)
    c, s = np.cos(angle), np.sin(angle)
    lower, upper = slice(0, g), slice(MID, MID + g)

    z_forward = np.zeros((2 * LANES, 2 * LANES))
    z_backward = np.zeros((2 * LANES, 2 * LANES))
    for slab, half in enumerate((lower, upper)):
        base = slab * LANES
        real, imag = slice(base, base + g), slice(base + MID, base + MID + g)
        one, two = half, slice(LANES + half.start, LANES + half.stop)
        z_forward[one, real], z_forward[one, imag] = c, -s
        z_forward[two, real], z_forward[two, imag] = s, c
        z_backward[real, one], z_backward[real, two] = c, s
        z_backward[imag, one], z_backward[imag, two] = -s, c

    stick_in = np.zeros((LANES, 2 * g))
    stick_in[lower, :g], stick_in[lower, g:] = c, -s
    stick_in[upper, :g], stick_in[upper, g:] = s, c
    stick_out = np.block([[c, s], [-s, c]]) * g**-1.5

    freq = np.arange(g)
    square = np.minimum(freq, g - freq) ** 2
    total = square[:, None, None] + square[None, :, None] + square[None, None, :]
    unit = (2.0 * math.pi / BOX_LENGTH) ** 2
    kernel = np.where(total > 0, 4.0 * math.pi / (unit * np.maximum(total, 1)), 0.0)
    coulomb = np.zeros((g, g, LANES), np.float32)
    coulomb[:, :, lower] = kernel
    coulomb[:, :, upper] = kernel
    return dict(
        forward=across(np.concatenate([c, -s], 0)),
        backward=across(np.concatenate([c, s], 0)),
        z_forward=down(z_forward),
        z_backward=down(z_backward / g**3),
        stick_in=across(stick_in),
        stick_out=across(stick_out),
        coulomb=coulomb,
    )


def split(x):
    high = x.astype(BF16)
    low = (x - high.astype(F32)).astype(BF16)
    return high, low


def stacked(x):
    high, low = split(x)
    return jnp.concatenate([high, low, high], 0)


def dot(a, b):
    return jnp.dot(a, b, preferred_element_type=F32)


def lane_halves(shape):
    return lax.broadcasted_iota(jnp.int32, shape, 1) % LANES < MID


def turned(x):
    return jnp.concatenate(
        [pltpu.roll(x[:, k : k + LANES], MID, 1) for k in range(0, x.shape[1], LANES)], 1
    )


def left(table, x):
    both = dot(table, stacked(x))
    g = both.shape[0] // 2
    return both[:g], both[g:]


def left_complex(table, x):
    cos, sin = left(table, x)
    sign = jnp.where(lane_halves((1, x.shape[1])), -1.0, 1.0)
    return cos + turned(sin) * sign


def halves(x):
    return x[:, :LANES], x[:, LANES:]


def beside(a, b):
    return jnp.concatenate([a, b], 1)


def right(parts, table):
    high, low = zip(*[split(x) for x in parts])
    return dot(jnp.concatenate(high + low + high, 1), table)


def strided(ref, first, g):
    return ref[pl.ds(first, g, stride=g), :]


def slab_rows(index, g, count=1):
    return pl.ds(index * g, count * g)


def one_hot(columns, first, rows):
    index = lax.broadcasted_iota(jnp.int16, (rows, columns.shape[1]), 0)
    wanted = (columns - first).astype(jnp.int16)
    return jnp.where(index == wanted, jnp.asarray(1, BF16), jnp.asarray(0, BF16))


def send_kernel(g, sticks_ref, columns_ref, *refs):
    block_refs, (row_ref, sems, row_sem) = refs[:-3], refs[-3:]
    own = lax.axis_index("stick")
    copies = [
        pltpu.make_async_copy(sticks_ref.at[own ^ d], ref.at[pl.ds(0, 2 * g)], sems.at[d])
        for d, ref in enumerate(block_refs)
    ]
    row_copy = pltpu.make_async_copy(columns_ref, row_ref, row_sem)
    row_copy.start()
    for copy in copies:
        copy.start()
    row_copy.wait()
    columns = jnp.broadcast_to(row_ref[...].astype(F32), (8, LANES))
    for ref in block_refs:
        ref[2 * g :, :] = columns
    for copy in copies:
        copy.wait()


def table_kernel(*refs):
    count = len(refs) // 2
    for table_ref, out_ref in zip(refs[:count], refs[count:]):
        out_ref[...] = table_ref[...].astype(BF16)


def place_kernel(*refs):
    own = lax.axis_index("stick")
    out_ref = refs[-1]
    for d, block_ref in enumerate(refs[:-1]):
        out_ref[own ^ d] = block_ref[...]


def fold(field_ref, folded_ref, g):
    rows = folded_ref.shape[0] // FOLD
    used = lax.broadcasted_iota(jnp.int32, (rows, LANES), 1) % MID < g
    last = field_ref[FOLD * rows :, :]
    width = g // FOLD
    for k in range(FOLD):
        part = slice(k * rows, (k + 1) * rows)
        folded_ref[part, :] = jnp.where(used, field_ref[part, :], pltpu.roll(last, g - k * width, 1))


def unfold(folded_ref, field_ref, g):
    rows = folded_ref.shape[0] // FOLD
    lane = lax.broadcasted_iota(jnp.int32, (rows, LANES), 1) % MID
    width = g // FOLD
    last = None
    for k in range(FOLD):
        part = folded_ref[k * rows : (k + 1) * rows, :]
        field_ref[k * rows : (k + 1) * rows, :] = part
        piece = pltpu.roll(part, LANES - (g - k * width), 1)
        last = piece if last is None else jnp.where(lane >= k * width, piece, last)
    field_ref[FOLD * rows :, :] = last


def field_kernel(g, count, *refs):
    received = refs[:count]
    stick_in_ref, backward_ref, phi_ref, folded_ref, columns_ref, work_a = refs[count:]
    columns = jnp.concatenate([ref[2 * g : 2 * g + 1, :] for ref in received], 1).astype(jnp.int32)
    columns_ref[...] = jnp.broadcast_to(columns, columns_ref.shape)
    stick_in, backward = stick_in_ref[...], backward_ref[...]
    pieces = []
    for k in range(0, count, 2):
        block = beside(received[k][: 2 * g, :], received[k + 1][: 2 * g, :])
        pieces.append(beside(*split(dot(stick_in, stacked(block)).T)))
    sticks = jnp.concatenate(pieces, 0)

    for first in range(0, g, 2 * PAIRS):
        both = dot(one_hot(columns, first * g, 2 * PAIRS * g), sticks)
        placed = both[:, :LANES] + both[:, LANES:]
        for k in range(0, 2 * PAIRS, 2):
            x = beside(placed[k * g : (k + 1) * g], placed[(k + 1) * g : (k + 2) * g])
            for j, slab in enumerate(halves(left_complex(backward, x))):
                work_a[slab_rows(first + k + j, g), :] = slab

    for pair in range(g // 2):
        x = beside(strided(work_a, pair, g), strided(work_a, pair + g // 2, g))
        (cos, cos_up), (sin, sin_up) = map(halves, left(backward, x))
        lower = cos - pltpu.roll(sin, MID, 1)
        upper = pltpu.roll(cos_up, MID, 1) - sin_up
        phi_ref[slab_rows(pair, g), :] = jnp.where(lane_halves(lower.shape), lower, upper)
    fold(phi_ref, folded_ref, g)


def potentials(g, phi_ref, first_ref, second_ref, tables, work_a, work_b, emit):
    forward, backward, z_forward, z_backward = [ref[...].astype(BF16) for ref in tables[:4]]
    coulomb_ref = tables[4]
    half = g // 2
    for start in range(0, half, PAIRS):
        rows = slab_rows(start, g, PAIRS)
        phi = phi_ref[rows, :]
        spectrum = right([phi * first_ref[rows, :], phi * second_ref[rows, :]], z_forward)
        for k in range(PAIRS):
            slabs = halves(left_complex(forward, spectrum[k * g : (k + 1) * g]))
            work_a[slab_rows(start + k, g), :] = slabs[0]
            work_a[slab_rows(start + k + half, g), :] = slabs[1]

    for kx in range(0, g, 2):
        x = left_complex(forward, beside(strided(work_a, kx, g), strided(work_a, kx + 1, g)))
        x = left_complex(backward, x * beside(coulomb_ref[kx], coulomb_ref[kx + 1]))
        for j, slab in enumerate(halves(x)):
            work_b[slab_rows(kx + j, g), :] = slab

    for start in range(0, half, PAIRS):
        slabs = [
            left_complex(backward, beside(strided(work_b, pair, g), strided(work_b, pair + half, g)))
            for pair in range(start, start + PAIRS)
        ]
        emit(start, *halves(right([jnp.concatenate(slabs, 0)], z_backward)))


def near_kernel(g, phi_ref, near_ref, *refs):
    tables, (sum_ref, other_ref, work_a, work_b) = refs[:5], refs[5:]
    unfold(near_ref, other_ref, g)

    def emit(start, own, other):
        rows = slab_rows(start, g, PAIRS)
        sum_ref[rows, :] = own * phi_ref[rows, :] + other * other_ref[rows, :]

    potentials(g, phi_ref, phi_ref, other_ref, tables, work_a, work_b, emit)


def middle_kernel(g, phi_ref, ahead_ref, behind_ref, before_ref, *refs):
    tables, (sum_ref, first_ref, second_ref, work_a, work_b) = refs[:5], refs[5:]
    unfold(ahead_ref, first_ref, g)
    unfold(behind_ref, second_ref, g)

    def emit(start, first, second):
        rows = slab_rows(start, g, PAIRS)
        sum_ref[rows, :] = before_ref[rows, :] + first * first_ref[rows, :] + second * second_ref[rows, :]

    potentials(g, phi_ref, first_ref, second_ref, tables, work_a, work_b, emit)


def far_kernel(g, weights, phi_ref, ahead_ref, across_ref, before_ref, columns_ref, stick_out_ref, *refs):
    tables, out_refs = refs[:5], refs[5:-5]
    first_ref, second_ref, work_a, work_b, parts_ref = refs[-5:]
    unfold(ahead_ref, first_ref, g)
    unfold(across_ref, second_ref, g)
    forward = tables[0][...].astype(BF16)
    half = g // 2

    def emit(start, first, second):
        rows = slab_rows(start, g, PAIRS)
        total = before_ref[rows, :] + weights[0] * (first * first_ref[rows, :])
        total = total + weights[1] * (second * second_ref[rows, :])
        for k in range(0, PAIRS, 2):
            cos, sin = left(forward, beside(total[k * g : (k + 1) * g], total[(k + 1) * g : (k + 2) * g]))
            low = lane_halves(cos.shape)
            lower, upper = halves(jnp.where(low, cos, turned(sin))), halves(jnp.where(low, turned(cos), sin))
            for j in range(2):
                work_a[slab_rows(start + k + j, g), :] = lower[j]
                work_a[slab_rows(start + k + j + half, g), :] = upper[j]

    potentials(g, phi_ref, first_ref, second_ref, tables, work_a, work_b, emit)

    for first in range(0, g, 2 * PAIRS):
        slabs = []
        for kx in range(first, first + 2 * PAIRS, 2):
            slabs += halves(left_complex(forward, beside(strided(work_a, kx, g), strided(work_a, kx + 1, g))))
        lined = jnp.concatenate(slabs, 0).T
        lined = jnp.concatenate([lined[:g], lined[MID : MID + g]], 0)
        parts_ref[:, first * g : (first + 2 * PAIRS) * g] = jnp.concatenate(split(lined), 0)

    parts = parts_ref[...]
    stick_out = stick_out_ref[...].astype(BF16)
    for k in range(0, len(out_refs), 2):
        hot = one_hot(columns_ref[:1, k * LANES : (k + 2) * LANES], 0, g * g)
        both = dot(parts, hot)
        picked = both[: 2 * g] + both[2 * g :]
        out_refs[k][...], out_refs[k + 1][...] = halves(dot(stick_out, stacked(picked)))


def call(kernel, out_shapes, scratch, flops, *operands, space=pltpu.VMEM):
    vmem = pl.BlockSpec(memory_space=pltpu.VMEM)
    moved = sum(x.size * x.dtype.itemsize for x in operands)
    return pl.pallas_call(
        kernel,
        out_shape=out_shapes,
        in_specs=[pl.BlockSpec(memory_space=space)] * len(operands),
        out_specs=jax.tree.map(lambda _: vmem, out_shapes),
        scratch_shapes=scratch,
        compiler_params=pltpu.CompilerParams(vmem_limit_bytes=40 * 2**20),
        cost_estimate=pl.CostEstimate(flops=flops, bytes_accessed=moved, transcendentals=0),
    )(*operands)


def exchanged(blocks):
    owners = len(blocks)
    moved = {}
    for d in range(owners - 1, 0, -1):
        moved[d] = lax.ppermute(blocks[d], "stick", [(i, i ^ d) for i in range(owners)])
    return [blocks[0]] + [moved[d] for d in range(1, owners)]


def on_device(sticks, stick_columns):
    g = sticks.shape[1] // 2
    slots = stick_columns.shape[0]
    owners = lax.axis_size("stick")
    groups = lax.axis_size("band")
    t = {name: jnp.asarray(value) for name, value in make_tables(g).items()}
    rows = g * g
    field = jax.ShapeDtypeStruct((rows // 2, LANES), F32)
    folded = jax.ShapeDtypeStruct((rows // 2 * FOLD // (FOLD + 1), LANES), F32)
    field_scratch = pltpu.VMEM((rows // 2, LANES), F32)
    work = pltpu.VMEM((rows, LANES), F32)
    pot_flops = 6 * 2 * rows * 256 * 256

    sent = call(
        functools.partial(send_kernel, g),
        [jax.ShapeDtypeStruct((2 * g + 8, slots), F32)] * owners,
        [pltpu.VMEM((1, slots), jnp.int32), pltpu.SemaphoreType.DMA((owners,)), pltpu.SemaphoreType.DMA],
        10**6,
        sticks,
        stick_columns[None, :],
        space=pltpu.HBM,
    )
    received = exchanged(sent)
    first_tables = lax.optimization_barrier((t["stick_in"], t["backward"], sent[0]))[:2]
    first_tables = call(
        table_kernel, [jax.ShapeDtypeStruct(x.shape, BF16) for x in first_tables], [], 10**9, *first_tables
    )
    phi, packed, columns = call(
        functools.partial(field_kernel, g, owners),
        [field, folded, jax.ShapeDtypeStruct((8, owners * slots), jnp.int32)],
        [work],
        10**9,
        *received,
        *first_tables,
    )
    pot_tables = [t["forward"], t["backward"], t["z_forward"], t["z_backward"], t["coulomb"]]
    swap = [(i, i ^ 1) for i in range(groups)]

    def fetched(distance):
        return lax.ppermute(packed, "band", [(i, (i - distance) % groups) for i in range(groups)])

    near = lax.ppermute(packed, "band", swap)
    ahead = fetched(HALF)
    total = call(
        functools.partial(near_kernel, g), field, [field_scratch, work, work], pot_flops, phi, near, *pot_tables
    )
    ahead, total = lax.optimization_barrier((ahead, total))
    if groups == 2 * HALF:
        weights = (2.0, 1.0)
        first, second = ahead, lax.ppermute(ahead, "band", swap)
    else:
        weights = (1.0, 0.0)
        behind = fetched(-HALF)
        odd = lax.axis_index("band") % 2 == 1
        first = second = lax.ppermute(jnp.where(odd, behind, ahead), "band", swap)
        total = call(
            functools.partial(middle_kernel, g),
            field,
            [field_scratch, field_scratch, work, work],
            pot_flops,
            phi,
            ahead,
            behind,
            total,
            *pot_tables,
        )
    result = call(
        functools.partial(far_kernel, g, weights),
        [jax.ShapeDtypeStruct((2 * g, slots), F32)] * owners,
        [field_scratch, field_scratch, work, work, pltpu.VMEM((4 * g, rows), BF16)],
        pot_flops,
        phi,
        first,
        second,
        total,
        columns,
        t["stick_out"],
        *pot_tables,
    )
    return call(place_kernel, jax.ShapeDtypeStruct(sticks.shape, F32), [], 10**6, *exchanged(result))


def solution(mesh):
    return jax.shard_map(
        on_device,
        mesh=mesh,
        in_specs=(P("band", None, "stick"), P("stick")),
        out_specs=P("band", None, "stick"),
        check_vma=False,
    )
```

time: 70.6 us -> 66.3 us (0.939)
  waiting for transfers between devices: 21.4 us -> 15.6 us
  Pallas kernels: 20.1 us -> 21.6 us
    ppermute x1, waiting for transfers between devices: 9.44 us -> 5.85 us  [fetched(): lax.ppermute(packed, 'band', [(i, (i - distance) % groups) for i in range...]
    ppermute x14, waiting for transfers between devices: 9.56 us -> 7.7 us  [exchanged(): lax.ppermute(blocks[d], 'stick', [(i, i ^ d) for i in range(owners)])]
    pallas_call x5 -> x6, Pallas kernels: 20.1 us -> 21.6 us  [call(): pl.pallas_call(kernel, out_shape=out_shapes, in_specs=[pl.BlockSpec(memor...]
  transfers between devices with their start and end apart: 17 -> 17, of which waited for: 8 -> 8; matrix products, arithmetic and copies ran while one was open for 0% -> 0% of each run, Pallas kernels for 6% -> 7%
where the time goes in v3:
time: 66.3 us; the launch traced here: 66.1 us
  starting transfers between devices  25.3 us (38%)
  Pallas kernels  21.6 us (33%)
  waiting for transfers between devices  15.6 us (24%)
  local copies, waits for them, and re-layouts  3.5 us (5%)
    ppermute x14, starting transfers between devices, exchanged(): lax.ppermute(blocks[d], 'stick', [(i, i ^ d) for i in range(owners)])  23.7 us
    pallas_call x6, Pallas kernels, call(): pl.pallas_call(kernel, out_shape=out_shapes, in_specs=[pl.BlockSpec(memor...  21.6 us
    ppermute x14, waiting for transfers between devices, exchanged(): lax.ppermute(blocks[d], 'stick', [(i, i ^ d) for i in range(owners)])  7.7 us
    ppermute x1, waiting for transfers between devices, fetched(): lax.ppermute(packed, 'band', [(i, (i - distance) % groups) for i in range...  5.85 us
    unnamed x20, local copies, waits for them, and re-layouts  3.5 us
    ppermute x1, waiting for transfers between devices, on_device(): first, second = (ahead, lax.ppermute(ahead, 'band', swap))  1.79 us
    ppermute x1, starting transfers between devices, fetched(): lax.ppermute(packed, 'band', [(i, (i - distance) % groups) for i in range...  1.56 us
  transfers between devices with their start and end apart: 17, of which 8 were waited for; matrix products, arithmetic and copies ran while one was open for 0% of the time, Pallas kernels for 7%

profile of v3, /device:TPU:0, one launch (start us, length us, event | category | flops | bytes accessed | tf_op | source)
XLA Modules:
  0.0 66.1 jit_solution(13484351771839904189)
XLA Ops:
  0.0 1.0 %copy-done = f32[8,96,128]{2,1,0:T(8,128)S(1)} copy-done((f32[8,96,128]{2,1,0:T(8,128)S(1)}, f32[8,96,128]{2,1,0:T(8,128)}, u32[]{:S(2)}) %copy-start) | copy-done | bytes 393240
  2.2 3.0 %collective-permute-start = (f32[104,128]{1,0:T(8,128)S(1)}, f32[104,128]{1,0:T(8,128)S(1)}, u32[]{:S(2)}, u32[]{:S(2)}) collective-permute-start(f32[104,128]{1,0:T(8,128)S(1)} %get-tuple-element.31), channel_id=1, source_target_pairs={{0,4},{4,0},{8,12},{12,8},{16,20},{20,16},{24,28},{28,24},{1,5},{5... | collective-permute-start | bytes 159752 | tf_op jit(solution)/shard_map/ppermute | solution.py:334
  5.3 1.6 %collective-permute-start.1 = (f32[104,128]{1,0:T(8,128)S(1)}, f32[104,128]{1,0:T(8,128)S(1)}, u32[]{:S(2)}, u32[]{:S(2)}) collective-permute-start(f32[104,128]{1,0:T(8,128)S(1)} %get-tuple-element.32), channel_id=1, source_target_pairs={{0,8},{4,12},{8,0},{12,4},{16,24},{20,28},{24,16},{28,20},{1,9},{5... | collective-permute-start | bytes 159752 | tf_op jit(solution)/shard_map/ppermute | solution.py:334
  6.9 3.0 %collective-permute-start.3 = (f32[104,128]{1,0:T(8,128)S(1)}, f32[104,128]{1,0:T(8,128)S(1)}, u32[]{:S(2)}, u32[]{:S(2)}) collective-permute-start(f32[104,128]{1,0:T(8,128)S(1)} %get-tuple-element.34), channel_id=1, source_target_pairs={{0,16},{4,20},{8,24},{12,28},{16,0},{20,4},{24,8},{28,12},{1,17},{... | collective-permute-start | bytes 159752 | tf_op jit(solution)/shard_map/ppermute | solution.py:334
  9.8 1.3 %collective-permute-start.4 = (f32[104,128]{1,0:T(8,128)S(1)}, f32[104,128]{1,0:T(8,128)S(1)}, u32[]{:S(2)}, u32[]{:S(2)}) collective-permute-start(f32[104,128]{1,0:T(8,128)S(1)} %get-tuple-element.35), channel_id=1, source_target_pairs={{0,20},{4,16},{8,28},{12,24},{16,4},{20,0},{24,12},{28,8},{1,21},{... | collective-permute-start | bytes 159752 | tf_op jit(solution)/shard_map/ppermute | solution.py:334
  11.1 3.6 %collective-permute-start.5 = (f32[104,128]{1,0:T(8,128)S(1)}, f32[104,128]{1,0:T(8,128)S(1)}, u32[]{:S(2)}, u32[]{:S(2)}) collective-permute-start(f32[104,128]{1,0:T(8,128)S(1)} %get-tuple-element.36), channel_id=1, source_target_pairs={{0,24},{4,28},{8,16},{12,20},{16,8},{20,12},{24,0},{28,4},{1,25},{... | collective-permute-start | bytes 159752 | tf_op jit(solution)/shard_map/ppermute | solution.py:334
  14.8 0.9 %copy-done.5 = f32[128,288]{1,0:T(8,128)S(1)} copy-done((f32[128,288]{1,0:T(8,128)S(1)}, f32[128,288]{1,0:T(8,128)}, u32[]{:S(2)}) %copy-start.5) | copy-done | bytes 147480
  15.7 0.9 %copy-done.7 = f32[96,144]{1,0:T(8,128)S(1)} copy-done((f32[96,144]{1,0:T(8,128)S(1)}, f32[96,144]{1,0:T(8,128)}, u32[]{:S(2)}) %copy-start.7) | copy-done | bytes 55320
  16.6 1.5 %collective-permute-done.4.refs_5_ = f32[104,128]{1,0:T(8,128)S(1)} collective-permute-done((f32[104,128]{1,0:T(8,128)S(1)}, f32[104,128]{1,0:T(8,128)S(1)}, u32[]{:S(2)}, u32[]{:S(2)}) %collective-permute-start.4) | collective-permute-done | bytes 53280 | tf_op jit(solution)/shard_map/ppermute | solution.py:334
  18.1 3.5 %collective-permute-done.6.refs_7_ = f32[104,128]{1,0:T(8,128)S(1)} collective-permute-done((f32[104,128]{1,0:T(8,128)S(1)}, f32[104,128]{1,0:T(8,128)S(1)}, u32[]{:S(2)}, u32[]{:S(2)}) %collective-permute-start.6) | collective-permute-done | bytes 53280 | tf_op jit(solution)/shard_map/ppermute | solution.py:334
  21.6 4.7 %shard_map.93 = (f32[1152,128]{1,0:T(8,128)S(1)}, f32[864,128]{1,0:T(8,128)S(1)}, s32[8,1024]{1,0:T(8,128)S(1)}) custom-call(f32[104,128]{1,0:T(8,128)S(1)} %get-tuple-element.30.refs_0_, f32[104,128]{1,0:T(8,128)S(1)} %collective-permute-done.refs_1_, f32[104,128]{1,0:T(8,128)S(1)} %collective-permute-done.1.refs_2_, ...), custom_call_target="tpu_custom_call" | custom-call | flops 1000000000 | bytes 527360 | tf_op jit(solution)/shard_map/pallas_call | solution.py:319
  26.4 1.6 %collective-permute-start.7 = (f32[864,128]{1,0:T(8,128)S(1)}, f32[864,128]{1,0:T(8,128)S(1)}, u32[]{:S(2)}, u32[]{:S(2)}) collective-permute-start(f32[864,128]{1,0:T(8,128)S(1)} %get-tuple-element.43), channel_id=1, source_target_pairs={{0,2},{1,3},{2,0},{3,1},{4,6},{5,7},{6,4},{7,5},{8,10},{9,11},{10,... | collective-permute-start | bytes 1327112 | tf_op jit(solution)/shard_map/ppermute | solution.py:377
  28.2 4.9 %shard_map.94.before_ref = f32[1152,128]{1,0:T(8,128)S(1)} custom-call(f32[1152,128]{1,0:T(8,128)S(1)} %get-tuple-element.42.phi_ref, f32[864,128]{1,0:T(8,128)S(1)} %collective-permute-done.8.near_ref, f32[96,144]{1,0:T(8,128)S(1)} %copy-done.9, f32[96,144]{1,0:T(8,128)S(1)} %copy-done.8, f32[768,256]{1,0:T(8,128)S(1)} %copy-done.4, ...), custom_call_target="tpu_custom_call" | custom-call | flops 1811939328 | bytes 3895296 | tf_op jit(solution)/shard_map/pallas_call | solution.py:319
  33.1 5.9 %collective-permute-done.7.ahead_ref = f32[864,128]{1,0:T(8,128)S(1)} collective-permute-done((f32[864,128]{1,0:T(8,128)S(1)}, f32[864,128]{1,0:T(8,128)S(1)}, u32[]{:S(2)}, u32[]{:S(2)}) %collective-permute-start.7) | collective-permute-done | bytes 442400 | tf_op jit(solution)/shard_map/ppermute | solution.py:377
  39.0 1.8 %collective-permute-done.9.across_ref = f32[864,128]{1,0:T(8,128)S(1)} collective-permute-done((f32[864,128]{1,0:T(8,128)S(1)}, f32[864,128]{1,0:T(8,128)S(1)}, u32[]{:S(2)}, u32[]{:S(2)}) %collective-permute-start.9) | collective-permute-done | bytes 442400 | tf_op jit(solution)/shard_map/ppermute | solution.py:387
  40.8 10.5 %shard_map.95 = (f32[96,128]{1,0:T(8,128)S(1)}, f32[96,128]{1,0:T(8,128)S(1)}, f32[96,128]{1,0:T(8,128)S(1)}, f32[96,128]{1,0:T(8,128)S(1)}, f32[96,128]{1,0:T(8...) custom-call(f32[1152,128]{1,0:T(8,128)S(1)} %get-tuple-element.42.phi_ref, ...), custom_call_target="tpu_custom_call" | custom-call | flops 1811939328 | bytes 5070848 | tf_op jit(solution)/shard_map/pallas_call | solution.py:319
  51.9 3.0 %collective-permute-start.12 = (f32[96,128]{1,0:T(8,128)S(1)}, f32[96,128]{1,0:T(8,128)S(1)}, u32[]{:S(2)}, u32[]{:S(2)}) collective-permute-start(f32[96,128]{1,0:T(8,128)S(1)} %get-tuple-element.50), channel_id=1, source_target_pairs={{0,12},{4,8},{8,4},{12,0},{16,28},{20,24},{24,20},{28,16},{1,13},{... | collective-permute-start | bytes 147464 | tf_op jit(solution)/shard_map/ppermute | solution.py:334
  54.9 0.8 %collective-permute-start.13 = (f32[96,128]{1,0:T(8,128)S(1)}, f32[96,128]{1,0:T(8,128)S(1)}, u32[]{:S(2)}, u32[]{:S(2)}) collective-permute-start(f32[96,128]{1,0:T(8,128)S(1)} %get-tuple-element.51), channel_id=1, source_target_pairs={{0,16},{4,20},{8,24},{12,28},{16,0},{20,4},{24,8},{28,12},{1,17},{... | collective-permute-start | bytes 147464 | tf_op jit(solution)/shard_map/ppermute | solution.py:334
  55.7 2.0 %collective-permute-start.14 = (f32[96,128]{1,0:T(8,128)S(1)}, f32[96,128]{1,0:T(8,128)S(1)}, u32[]{:S(2)}, u32[]{:S(2)}) collective-permute-start(f32[96,128]{1,0:T(8,128)S(1)} %get-tuple-element.52), channel_id=1, source_target_pairs={{0,20},{4,16},{8,28},{12,24},{16,4},{20,0},{24,12},{28,8},{1,21},{... | collective-permute-start | bytes 147464 | tf_op jit(solution)/shard_map/ppermute | solution.py:334
  57.8 0.7 %collective-permute-start.15 = (f32[96,128]{1,0:T(8,128)S(1)}, f32[96,128]{1,0:T(8,128)S(1)}, u32[]{:S(2)}, u32[]{:S(2)}) collective-permute-start(f32[96,128]{1,0:T(8,128)S(1)} %get-tuple-element.53), channel_id=1, source_target_pairs={{0,24},{4,28},{8,16},{12,20},{16,8},{20,12},{24,0},{28,4},{1,25},{... | collective-permute-start | bytes 147464 | tf_op jit(solution)/shard_map/ppermute | solution.py:334
  58.5 4.1 %collective-permute-start.16 = (f32[96,128]{1,0:T(8,128)S(1)}, f32[96,128]{1,0:T(8,128)S(1)}, u32[]{:S(2)}, u32[]{:S(2)}) collective-permute-start(f32[96,128]{1,0:T(8,128)S(1)} %get-tuple-element.54), channel_id=1, source_target_pairs={{0,28},{4,24},{8,20},{12,16},{16,12},{20,8},{24,4},{28,0},{1,29},{... | collective-permute-start | bytes 147464 | tf_op jit(solution)/shard_map/ppermute | solution.py:334
  62.6 1.0 %collective-permute-done.14.refs_5_ = f32[96,128]{1,0:T(8,128)S(1)} collective-permute-done((f32[96,128]{1,0:T(8,128)S(1)}, f32[96,128]{1,0:T(8,128)S(1)}, u32[]{:S(2)}, u32[]{:S(2)}) %collective-permute-start.14) | collective-permute-done | bytes 49184 | tf_op jit(solution)/shard_map/ppermute | solution.py:334
  63.7 1.6 %collective-permute-done.16.refs_7_ = f32[96,128]{1,0:T(8,128)S(1)} collective-permute-done((f32[96,128]{1,0:T(8,128)S(1)}, f32[96,128]{1,0:T(8,128)S(1)}, u32[]{:S(2)}, u32[]{:S(2)}) %collective-permute-start.16) | collective-permute-done | bytes 49184 | tf_op jit(solution)/shard_map/ppermute | solution.py:334
  65.3 0.8 %shard_map.96 = f32[8,96,128]{2,1,0:T(8,128)} custom-call(f32[96,128]{1,0:T(8,128)S(1)} %get-tuple-element.47.refs_0_, f32[96,128]{1,0:T(8,128)S(1)} %collective-permute-done.10.refs_1_, f32[96,128]{1,0:T(8,128)S(1)} %collective-permute-done.11.refs_2_, f32[96,128]{1,0:T(8,128)S(1)} %collective-permute-done.12.refs_3_, ...), custom_call_target="tpu_custom_call" | custom-call | flops 1000000 | bytes 393216 | tf_op jit(solution)/shard_map/pallas_call | solution.py:319
  (36 shorter events, 2.4 us)
Async XLA Ops:
  0.0 1.0 %copy-start = (f32[8,96,128]{2,1,0:T(8,128)S(1)}, f32[8,96,128]{2,1,0:T(8,128)}, u32[]{:S(2)}) copy-start(f32[8,96,128]{2,1,0:T(8,128)} %sticks_ref.1) | copy-start | bytes 1179652
  2.2 8.9 %collective-permute-start = (f32[104,128]{1,0:T(8,128)S(1)}, f32[104,128]{1,0:T(8,128)S(1)}, u32[]{:S(2)}, u32[]{:S(2)}) collective-permute-start(f32[104,128]{1,0:T(8,128)S(1)} %get-tuple-element.31), channel_id=1, source_target_pairs={{0,4},{4,0},{8,12},{12,8},{16,20},{20,16},{24,28},{28,24},{1,5},{5... | collective-permute-start | bytes 159752 | tf_op jit(solution)/shard_map/ppermute | solution.py:334
  5.3 9.5 %collective-permute-start.1 = (f32[104,128]{1,0:T(8,128)S(1)}, f32[104,128]{1,0:T(8,128)S(1)}, u32[]{:S(2)}, u32[]{:S(2)}) collective-permute-start(f32[104,128]{1,0:T(8,128)S(1)} %get-tuple-element.32), channel_id=1, source_target_pairs={{0,8},{4,12},{8,0},{12,4},{16,24},{20,28},{24,16},{28,20},{1,9},{5... | collective-permute-start | bytes 159752 | tf_op jit(solution)/shard_map/ppermute | solution.py:334
  6.9 9.7 %collective-permute-start.2 = (f32[104,128]{1,0:T(8,128)S(1)}, f32[104,128]{1,0:T(8,128)S(1)}, u32[]{:S(2)}, u32[]{:S(2)}) collective-permute-start(f32[104,128]{1,0:T(8,128)S(1)} %get-tuple-element.33), channel_id=1, source_target_pairs={{0,12},{4,8},{8,4},{12,0},{16,28},{20,24},{24,20},{28,16},{1,13},{... | collective-permute-start | bytes 159752 | tf_op jit(solution)/shard_map/ppermute | solution.py:334
  6.9 9.7 %collective-permute-start.3 = (f32[104,128]{1,0:T(8,128)S(1)}, f32[104,128]{1,0:T(8,128)S(1)}, u32[]{:S(2)}, u32[]{:S(2)}) collective-permute-start(f32[104,128]{1,0:T(8,128)S(1)} %get-tuple-element.34), channel_id=1, source_target_pairs={{0,16},{4,20},{8,24},{12,28},{16,0},{20,4},{24,8},{28,12},{1,17},{... | collective-permute-start | bytes 159752 | tf_op jit(solution)/shard_map/ppermute | solution.py:334
  9.8 8.2 %collective-permute-start.4 = (f32[104,128]{1,0:T(8,128)S(1)}, f32[104,128]{1,0:T(8,128)S(1)}, u32[]{:S(2)}, u32[]{:S(2)}) collective-permute-start(f32[104,128]{1,0:T(8,128)S(1)} %get-tuple-element.35), channel_id=1, source_target_pairs={{0,20},{4,16},{8,28},{12,24},{16,4},{20,0},{24,12},{28,8},{1,21},{... | collective-permute-start | bytes 159752 | tf_op jit(solution)/shard_map/ppermute | solution.py:334
  11.1 6.9 %collective-permute-start.5 = (f32[104,128]{1,0:T(8,128)S(1)}, f32[104,128]{1,0:T(8,128)S(1)}, u32[]{:S(2)}, u32[]{:S(2)}) collective-permute-start(f32[104,128]{1,0:T(8,128)S(1)} %get-tuple-element.36), channel_id=1, source_target_pairs={{0,24},{4,28},{8,16},{12,20},{16,8},{20,12},{24,0},{28,4},{1,25},{... | collective-permute-start | bytes 159752 | tf_op jit(solution)/shard_map/ppermute | solution.py:334
  14.7 6.8 %collective-permute-start.6 = (f32[104,128]{1,0:T(8,128)S(1)}, f32[104,128]{1,0:T(8,128)S(1)}, u32[]{:S(2)}, u32[]{:S(2)}) collective-permute-start(f32[104,128]{1,0:T(8,128)S(1)} %get-tuple-element.37), channel_id=1, source_target_pairs={{0,28},{4,24},{8,20},{12,16},{16,12},{20,8},{24,4},{28,0},{1,29},{... | collective-permute-start | bytes 159752 | tf_op jit(solution)/shard_map/ppermute | solution.py:334
  21.6 6.6 %copy-start.2 = (f32[48,48,128]{2,1,0:T(8,128)S(1)}, f32[48,48,128]{2,1,0:T(8,128)}, u32[]{:S(2)}) copy-start(f32[48,48,128]{2,1,0:T(8,128)} %constant.20.clone.refs_4_) | copy-start | bytes 3538948
  21.6 6.6 %copy-start.3 = (f32[768,256]{1,0:T(8,128)S(1)}, f32[768,256]{1,0:T(8,128)}, u32[]{:S(2)}) copy-start(f32[768,256]{1,0:T(8,128)} %constant.17.clone.refs_3_) | copy-start | bytes 2359300
  21.6 6.6 %copy-start.4 = (f32[768,256]{1,0:T(8,128)S(1)}, f32[768,256]{1,0:T(8,128)}, u32[]{:S(2)}) copy-start(f32[768,256]{1,0:T(8,128)} %constant.16.clone.refs_2_) | copy-start | bytes 2359300
  21.6 6.6 %copy-start.8 = (f32[96,144]{1,0:T(8,128)S(1)}, f32[96,144]{1,0:T(8,128)}, u32[]{:S(2)}) copy-start(f32[96,144]{1,0:T(8,128)} %constant.15.clone.refs_1_) | copy-start | bytes 165892
  21.6 6.6 %copy-start.9 = (f32[96,144]{1,0:T(8,128)S(1)}, f32[96,144]{1,0:T(8,128)}, u32[]{:S(2)}) copy-start(f32[96,144]{1,0:T(8,128)} %constant.14.clone.refs_0_) | copy-start | bytes 165892
  26.3 1.9 %collective-permute-start.8 = (f32[864,128]{1,0:T(8,128)S(1)}, f32[864,128]{1,0:T(8,128)S(1)}, u32[]{:S(2)}, u32[]{:S(2)}) collective-permute-start(f32[864,128]{1,0:T(8,128)S(1)} %get-tuple-element.43), channel_id=1, source_target_pairs={{0,1},{1,0},{2,3},{3,2},{4,5},{5,4},{6,7},{7,6},{8,9},{9,8},{10,11... | collective-permute-start | bytes 1327112 | tf_op jit(solution)/shard_map/ppermute | solution.py:379
  26.4 12.6 %collective-permute-start.7 = (f32[864,128]{1,0:T(8,128)S(1)}, f32[864,128]{1,0:T(8,128)S(1)}, u32[]{:S(2)}, u32[]{:S(2)}) collective-permute-start(f32[864,128]{1,0:T(8,128)S(1)} %get-tuple-element.43), channel_id=1, source_target_pairs={{0,2},{1,3},{2,0},{3,1},{4,6},{5,7},{6,4},{7,5},{8,10},{9,11},{10,... | collective-permute-start | bytes 1327112 | tf_op jit(solution)/shard_map/ppermute | solution.py:377
  28.2 12.6 %copy-start.6 = (f32[96,288]{1,0:T(8,128)S(1)}, f32[96,288]{1,0:T(8,128)}, u32[]{:S(2)}) copy-start(f32[96,288]{1,0:T(8,128)} %constant.19.clone.stick_out_ref) | copy-start | bytes 331780
  39.0 1.8 %collective-permute-start.9 = (f32[864,128]{1,0:T(8,128)S(1)}, f32[864,128]{1,0:T(8,128)S(1)}, u32[]{:S(2)}, u32[]{:S(2)}) collective-permute-start(f32[864,128]{1,0:T(8,128)S(1)} %collective-permute-done.7.ahead_ref), channel_id=1, source_target_pairs={{0,1},{1,0},{2,3},{3,2},{4,5},{5,4},{6,7},{7,6},{8,9},{9,8},{10,11... | collective-permute-start | bytes 1327112 | tf_op jit(solution)/shard_map/ppermute | solution.py:387
  51.3 6.4 %collective-permute-start.10 = (f32[96,128]{1,0:T(8,128)S(1)}, f32[96,128]{1,0:T(8,128)S(1)}, u32[]{:S(2)}, u32[]{:S(2)}) collective-permute-start(f32[96,128]{1,0:T(8,128)S(1)} %get-tuple-element.48), channel_id=1, source_target_pairs={{0,4},{4,0},{8,12},{12,8},{16,20},{20,16},{24,28},{28,24},{1,5},{5... | collective-permute-start | bytes 147464 | tf_op jit(solution)/shard_map/ppermute | solution.py:334
  51.9 6.6 %collective-permute-start.11 = (f32[96,128]{1,0:T(8,128)S(1)}, f32[96,128]{1,0:T(8,128)S(1)}, u32[]{:S(2)}, u32[]{:S(2)}) collective-permute-start(f32[96,128]{1,0:T(8,128)S(1)} %get-tuple-element.49), channel_id=1, source_target_pairs={{0,8},{4,12},{8,0},{12,4},{16,24},{20,28},{24,16},{28,20},{1,9},{5... | collective-permute-start | bytes 147464 | tf_op jit(solution)/shard_map/ppermute | solution.py:334
  51.9 10.6 %collective-permute-start.12 = (f32[96,128]{1,0:T(8,128)S(1)}, f32[96,128]{1,0:T(8,128)S(1)}, u32[]{:S(2)}, u32[]{:S(2)}) collective-permute-start(f32[96,128]{1,0:T(8,128)S(1)} %get-tuple-element.50), channel_id=1, source_target_pairs={{0,12},{4,8},{8,4},{12,0},{16,28},{20,24},{24,20},{28,16},{1,13},{... | collective-permute-start | bytes 147464 | tf_op jit(solution)/shard_map/ppermute | solution.py:334
  54.9 7.7 %collective-permute-start.13 = (f32[96,128]{1,0:T(8,128)S(1)}, f32[96,128]{1,0:T(8,128)S(1)}, u32[]{:S(2)}, u32[]{:S(2)}) collective-permute-start(f32[96,128]{1,0:T(8,128)S(1)} %get-tuple-element.51), channel_id=1, source_target_pairs={{0,16},{4,20},{8,24},{12,28},{16,0},{20,4},{24,8},{28,12},{1,17},{... | collective-permute-start | bytes 147464 | tf_op jit(solution)/shard_map/ppermute | solution.py:334
  55.7 7.8 %collective-permute-start.14 = (f32[96,128]{1,0:T(8,128)S(1)}, f32[96,128]{1,0:T(8,128)S(1)}, u32[]{:S(2)}, u32[]{:S(2)}) collective-permute-start(f32[96,128]{1,0:T(8,128)S(1)} %get-tuple-element.52), channel_id=1, source_target_pairs={{0,20},{4,16},{8,28},{12,24},{16,4},{20,0},{24,12},{28,8},{1,21},{... | collective-permute-start | bytes 147464 | tf_op jit(solution)/shard_map/ppermute | solution.py:334
  57.8 5.9 %collective-permute-start.15 = (f32[96,128]{1,0:T(8,128)S(1)}, f32[96,128]{1,0:T(8,128)S(1)}, u32[]{:S(2)}, u32[]{:S(2)}) collective-permute-start(f32[96,128]{1,0:T(8,128)S(1)} %get-tuple-element.53), channel_id=1, source_target_pairs={{0,24},{4,28},{8,16},{12,20},{16,8},{20,12},{24,0},{28,4},{1,25},{... | collective-permute-start | bytes 147464 | tf_op jit(solution)/shard_map/ppermute | solution.py:334
  58.5 6.8 %collective-permute-start.16 = (f32[96,128]{1,0:T(8,128)S(1)}, f32[96,128]{1,0:T(8,128)S(1)}, u32[]{:S(2)}, u32[]{:S(2)}) collective-permute-start(f32[96,128]{1,0:T(8,128)S(1)} %get-tuple-element.54), channel_id=1, source_target_pairs={{0,28},{4,24},{8,20},{12,16},{16,12},{20,8},{24,4},{28,0},{1,29},{... | collective-permute-start | bytes 147464 | tf_op jit(solution)/shard_map/ppermute | solution.py:334
  (3 other events, 2.5 us)

commit v4 on v3

--- a/solution.py
+++ b/solution.py
@@ -14,7 +14,6 @@
 LANES = 128
 MID = 64
 PAIRS = 4
-FOLD = 3
 
 F32 = jnp.float32
 BF16 = jnp.bfloat16
@@ -140,23 +139,10 @@
     return jnp.where(index == wanted, jnp.asarray(1, BF16), jnp.asarray(0, BF16))
 
 
-def send_kernel(g, sticks_ref, columns_ref, *refs):
-    block_refs, (row_ref, sems, row_sem) = refs[:-3], refs[-3:]
-    own = lax.axis_index("stick")
-    copies = [
-        pltpu.make_async_copy(sticks_ref.at[own ^ d], ref.at[pl.ds(0, 2 * g)], sems.at[d])
-        for d, ref in enumerate(block_refs)
-    ]
-    row_copy = pltpu.make_async_copy(columns_ref, row_ref, row_sem)
-    row_copy.start()
-    for copy in copies:
-        copy.start()
-    row_copy.wait()
-    columns = jnp.broadcast_to(row_ref[...].astype(F32), (8, LANES))
-    for ref in block_refs:
-        ref[2 * g :, :] = columns
-    for copy in copies:
-        copy.wait()
+def send_kernel(g, sticks_ref, columns_ref, first_ref, second_ref):
+    first_ref[:, :g, :] = sticks_ref[:, :g, :]
+    first_ref[:, g:, :] = jnp.broadcast_to(columns_ref[...].astype(F32), (first_ref.shape[0], 8, LANES))
+    second_ref[...] = sticks_ref[:, g:, :]
 
 
 def table_kernel(*refs):
@@ -165,45 +151,15 @@
         out_ref[...] = table_ref[...].astype(BF16)
 
 
-def place_kernel(*refs):
-    own = lax.axis_index("stick")
-    out_ref = refs[-1]
-    for d, block_ref in enumerate(refs[:-1]):
-        out_ref[own ^ d] = block_ref[...]
-
-
-def fold(field_ref, folded_ref, g):
-    rows = folded_ref.shape[0] // FOLD
-    used = lax.broadcasted_iota(jnp.int32, (rows, LANES), 1) % MID < g
-    last = field_ref[FOLD * rows :, :]
-    width = g // FOLD
-    for k in range(FOLD):
-        part = slice(k * rows, (k + 1) * rows)
-        folded_ref[part, :] = jnp.where(used, field_ref[part, :], pltpu.roll(last, g - k * width, 1))
-
-
-def unfold(folded_ref, field_ref, g):
-    rows = folded_ref.shape[0] // FOLD
-    lane = lax.broadcasted_iota(jnp.int32, (rows, LANES), 1) % MID
-    width = g // FOLD
-    last = None
-    for k in range(FOLD):
-        part = folded_ref[k * rows : (k + 1) * rows, :]
-        field_ref[k * rows : (k + 1) * rows, :] = part
-        piece = pltpu.roll(part, LANES - (g - k * width), 1)
-        last = piece if last is None else jnp.where(lane >= k * width, piece, last)
-    field_ref[FOLD * rows :, :] = last
-
-
-def field_kernel(g, count, *refs):
-    received = refs[:count]
-    stick_in_ref, backward_ref, phi_ref, folded_ref, columns_ref, work_a = refs[count:]
-    columns = jnp.concatenate([ref[2 * g : 2 * g + 1, :] for ref in received], 1).astype(jnp.int32)
+def field_kernel(g, first_ref, second_ref, stick_in_ref, backward_ref, phi_ref, columns_ref, work_a):
+    count = first_ref.shape[0]
+    columns = jnp.concatenate([first_ref[k, g : g + 1, :] for k in range(count)], 1).astype(jnp.int32)
     columns_ref[...] = jnp.broadcast_to(columns, columns_ref.shape)
     stick_in, backward = stick_in_ref[...], backward_ref[...]
     pieces = []
     for k in range(0, count, 2):
-        block = beside(received[k][: 2 * g, :], received[k + 1][: 2 * g, :])
+        blocks = [jnp.concatenate([first_ref[k + j, :g, :], second_ref[k + j]], 0) for j in range(2)]
+        block = beside(*blocks)
         pieces.append(beside(*split(dot(stick_in, stacked(block)).T)))
     sticks = jnp.concatenate(pieces, 0)
 
@@ -221,7 +177,6 @@
         lower = cos - pltpu.roll(sin, MID, 1)
         upper = pltpu.roll(cos_up, MID, 1) - sin_up
         phi_ref[slab_rows(pair, g), :] = jnp.where(lane_halves(lower.shape), lower, upper)
-    fold(phi_ref, folded_ref, g)
 
 
 def potentials(g, phi_ref, first_ref, second_ref, tables, work_a, work_b, emit):
@@ -251,9 +206,8 @@
         emit(start, *halves(right([jnp.concatenate(slabs, 0)], z_backward)))
 
 
-def near_kernel(g, phi_ref, near_ref, *refs):
-    tables, (sum_ref, other_ref, work_a, work_b) = refs[:5], refs[5:]
-    unfold(near_ref, other_ref, g)
+def near_kernel(g, phi_ref, other_ref, *refs):
+    tables, (sum_ref, work_a, work_b) = refs[:5], refs[5:]
 
     def emit(start, own, other):
         rows = slab_rows(start, g, PAIRS)
@@ -262,10 +216,8 @@
     potentials(g, phi_ref, phi_ref, other_ref, tables, work_a, work_b, emit)
 
 
-def middle_kernel(g, phi_ref, ahead_ref, behind_ref, before_ref, *refs):
-    tables, (sum_ref, first_ref, second_ref, work_a, work_b) = refs[:5], refs[5:]
-    unfold(ahead_ref, first_ref, g)
-    unfold(behind_ref, second_ref, g)
+def middle_kernel(g, phi_ref, first_ref, second_ref, before_ref, *refs):
+    tables, (sum_ref, work_a, work_b) = refs[:5], refs[5:]
 
     def emit(start, first, second):
         rows = slab_rows(start, g, PAIRS)
@@ -274,11 +226,8 @@
     potentials(g, phi_ref, first_ref, second_ref, tables, work_a, work_b, emit)
 
 
-def far_kernel(g, weights, phi_ref, ahead_ref, across_ref, before_ref, columns_ref, stick_out_ref, *refs):
-    tables, out_refs = refs[:5], refs[5:-5]
-    first_ref, second_ref, work_a, work_b, parts_ref = refs[-5:]
-    unfold(ahead_ref, first_ref, g)
-    unfold(across_ref, second_ref, g)
+def far_kernel(g, weights, phi_ref, first_ref, second_ref, before_ref, columns_ref, stick_out_ref, *refs):
+    tables, (out_ref, work_a, work_b, parts_ref) = refs[:5], refs[5:]
     forward = tables[0][...].astype(BF16)
     half = g // 2
 
@@ -306,20 +255,20 @@
 
     parts = parts_ref[...]
     stick_out = stick_out_ref[...].astype(BF16)
-    for k in range(0, len(out_refs), 2):
+    for k in range(0, out_ref.shape[0], 2):
         hot = one_hot(columns_ref[:1, k * LANES : (k + 2) * LANES], 0, g * g)
         both = dot(parts, hot)
         picked = both[: 2 * g] + both[2 * g :]
-        out_refs[k][...], out_refs[k + 1][...] = halves(dot(stick_out, stacked(picked)))
-
-
-def call(kernel, out_shapes, scratch, flops, *operands, space=pltpu.VMEM):
+        out_ref[k], out_ref[k + 1] = halves(dot(stick_out, stacked(picked)))
+
+
+def call(kernel, out_shapes, scratch, flops, *operands):
     vmem = pl.BlockSpec(memory_space=pltpu.VMEM)
     moved = sum(x.size * x.dtype.itemsize for x in operands)
     return pl.pallas_call(
         kernel,
         out_shape=out_shapes,
-        in_specs=[pl.BlockSpec(memory_space=space)] * len(operands),
+        in_specs=[vmem] * len(operands),
         out_specs=jax.tree.map(lambda _: vmem, out_shapes),
         scratch_shapes=scratch,
         compiler_params=pltpu.CompilerParams(vmem_limit_bytes=40 * 2**20),
@@ -328,11 +277,7 @@
 
 
 def exchanged(blocks):
-    owners = len(blocks)
-    moved = {}
-    for d in range(owners - 1, 0, -1):
-        moved[d] = lax.ppermute(blocks[d], "stick", [(i, i ^ d) for i in range(owners)])
-    return [blocks[0]] + [moved[d] for d in range(1, owners)]
+    return lax.all_to_all(blocks, "stick", split_axis=0, concat_axis=0, tiled=True)
 
 
 def on_device(sticks, stick_columns):
@@ -343,68 +288,67 @@
     t = {name: jnp.asarray(value) for name, value in make_tables(g).items()}
     rows = g * g
     field = jax.ShapeDtypeStruct((rows // 2, LANES), F32)
-    folded = jax.ShapeDtypeStruct((rows // 2 * FOLD // (FOLD + 1), LANES), F32)
-    field_scratch = pltpu.VMEM((rows // 2, LANES), F32)
     work = pltpu.VMEM((rows, LANES), F32)
     pot_flops = 6 * 2 * rows * 256 * 256
 
+    def shifted(x, distance):
+        return lax.ppermute(x, "band", [(i, (i - distance) % groups) for i in range(groups)])
+
+    def swapped(x):
+        return lax.ppermute(x, "band", [(i, i ^ 1) for i in range(groups)])
+
     sent = call(
         functools.partial(send_kernel, g),
-        [jax.ShapeDtypeStruct((2 * g + 8, slots), F32)] * owners,
-        [pltpu.VMEM((1, slots), jnp.int32), pltpu.SemaphoreType.DMA((owners,)), pltpu.SemaphoreType.DMA],
+        [jax.ShapeDtypeStruct((owners, g + 8, slots), F32), jax.ShapeDtypeStruct((owners, g, slots), F32)],
+        [],
         10**6,
         sticks,
         stick_columns[None, :],
-        space=pltpu.HBM,
-    )
-    received = exchanged(sent)
+    )
     first_tables = lax.optimization_barrier((t["stick_in"], t["backward"], sent[0]))[:2]
     first_tables = call(
         table_kernel, [jax.ShapeDtypeStruct(x.shape, BF16) for x in first_tables], [], 10**9, *first_tables
     )
-    phi, packed, columns = call(
-        functools.partial(field_kernel, g, owners),
-        [field, folded, jax.ShapeDtypeStruct((8, owners * slots), jnp.int32)],
-        [work],
-        10**9,
-        *received,
-        *first_tables,
-    )
+    distances = (HALF,) if groups == 2 * HALF else (HALF, -HALF)
+    own, far = [], {distance: [] for distance in distances}
+    for block in sent:
+        own.append(exchanged(block))
+        for distance in distances:
+            far[distance].append(shifted(own[-1], distance))
+
+    def orbital(blocks):
+        return call(
+            functools.partial(field_kernel, g),
+            [field, jax.ShapeDtypeStruct((8, owners * slots), jnp.int32)],
+            [work],
+            10**9,
+            *blocks,
+            *first_tables,
+        )
+
+    phi, columns = orbital(own)
+    near = swapped(phi)
+    fields = [orbital(far[distance])[0] for distance in distances]
     pot_tables = [t["forward"], t["backward"], t["z_forward"], t["z_backward"], t["coulomb"]]
-    swap = [(i, i ^ 1) for i in range(groups)]
-
-    def fetched(distance):
-        return lax.ppermute(packed, "band", [(i, (i - distance) % groups) for i in range(groups)])
-
-    near = lax.ppermute(packed, "band", swap)
-    ahead = fetched(HALF)
-    total = call(
-        functools.partial(near_kernel, g), field, [field_scratch, work, work], pot_flops, phi, near, *pot_tables
-    )
-    ahead, total = lax.optimization_barrier((ahead, total))
+
+    def potential_sum(kernel, *operands):
+        return call(functools.partial(kernel, g), field, [work, work], pot_flops, phi, *operands, *pot_tables)
+
     if groups == 2 * HALF:
         weights = (2.0, 1.0)
-        first, second = ahead, lax.ppermute(ahead, "band", swap)
+        first, second = fields[0], swapped(fields[0])
+        near, first = lax.optimization_barrier((near, first))
+        total = potential_sum(near_kernel, near)
     else:
         weights = (1.0, 0.0)
-        behind = fetched(-HALF)
         odd = lax.axis_index("band") % 2 == 1
-        first = second = lax.ppermute(jnp.where(odd, behind, ahead), "band", swap)
-        total = call(
-            functools.partial(middle_kernel, g),
-            field,
-            [field_scratch, field_scratch, work, work],
-            pot_flops,
-            phi,
-            ahead,
-            behind,
-            total,
-            *pot_tables,
-        )
+        first = second = swapped(jnp.where(odd, fields[1], fields[0]))
+        total = potential_sum(near_kernel, near)
+        total = potential_sum(middle_kernel, *fields, total)
     result = call(
         functools.partial(far_kernel, g, weights),
-        [jax.ShapeDtypeStruct((2 * g, slots), F32)] * owners,
-        [field_scratch, field_scratch, work, work, pltpu.VMEM((4 * g, rows), BF16)],
+        jax.ShapeDtypeStruct(sticks.shape, F32),
+        [work, work, pltpu.VMEM((4 * g, rows), BF16)],
         pot_flops,
         phi,
         first,
@@ -414,7 +358,7 @@
         t["stick_out"],
         *pot_tables,
     )
-    return call(place_kernel, jax.ShapeDtypeStruct(sticks.shape, F32), [], 10**6, *exchanged(result))
+    return exchanged(result)
 
 
 def solution(mesh):

time: 66.3 us -> 73.2 us (1.10)
  blocking collectives: 0 us -> 31 us
  starting transfers between devices: 25.3 us -> 7.01 us
  waiting for transfers between devices: 15.6 us -> 6.4 us
  Pallas kernels: 21.6 us -> 25.9 us
  local copies, waits for them, and re-layouts: 3.5 us -> 2.43 us
    all_to_all x0 -> x2, blocking collectives: none -> 31 us  [exchanged(): lax.all_to_all(blocks, 'stick', split_axis=0, concat_axis=0, tiled=True)]
    ppermute x17 -> x4, starting transfers between devices: 25.3 us -> 3.6 us  [the longest x2 3.05 us: shifted(): lax.ppermute(x, 'band', [(i, (i - distance) % groups) for i in range(grou...]
    ppermute x17 -> x4, waiting for transfers between devices: 15.6 us -> 0.01 us  [the longest x2 0.01 us: shifted(): lax.ppermute(x, 'band', [(i, (i - distance) % groups) for i in range(grou...]
    all_to_all x0 -> x1, waiting for transfers between devices: none -> 6.39 us  [exchanged(): lax.all_to_all(blocks, 'stick', split_axis=0, concat_axis=0, tiled=True)]
    pallas_call x6, Pallas kernels: 21.6 us -> 25.9 us  [call(): pl.pallas_call(kernel, out_shape=out_shapes, in_specs=[vmem] * len(operan...]
    all_to_all x0 -> x1, starting transfers between devices: none -> 3.4 us  [exchanged(): lax.all_to_all(blocks, 'stick', split_axis=0, concat_axis=0, tiled=True)]
    unnamed x20 -> x19, local copies, waits for them, and re-layouts: 3.5 us -> 2.43 us
  transfers between devices with their start and end apart: 17 -> 5, of which waited for: 8 -> 1; matrix products, arithmetic and copies ran while one was open for 0% -> 0% of each run, Pallas kernels for 7% -> 20%
where the time goes in v4:
time: 73.2 us; the launch traced here: 72.9 us
  blocking collectives  31 us (42%)
  Pallas kernels  25.9 us (35%)
  starting transfers between devices  7.01 us (10%)
  waiting for transfers between devices  6.4 us (9%)
  local copies, waits for them, and re-layouts  2.43 us (3%)
    all_to_all x2, blocking collectives, exchanged(): lax.all_to_all(blocks, 'stick', split_axis=0, concat_axis=0, tiled=True)  31 us
    pallas_call x6, Pallas kernels, call(): pl.pallas_call(kernel, out_shape=out_shapes, in_specs=[vmem] * len(operan...  25.9 us
    all_to_all x1, waiting for transfers between devices, exchanged(): lax.all_to_all(blocks, 'stick', split_axis=0, concat_axis=0, tiled=True)  6.39 us
    all_to_all x1, starting transfers between devices, exchanged(): lax.all_to_all(blocks, 'stick', split_axis=0, concat_axis=0, tiled=True)  3.4 us
    ppermute x2, starting transfers between devices, shifted(): lax.ppermute(x, 'band', [(i, (i - distance) % groups) for i in range(grou...  3.05 us
    unnamed x19, local copies, waits for them, and re-layouts  2.43 us
  transfers between devices with their start and end apart: 5, of which 1 were waited for; matrix products, arithmetic and copies ran while one was open for 0% of the time, Pallas kernels for 20%

profile of v4, /device:TPU:0, one launch (start us, length us, event | category | flops | bytes accessed | tf_op | source)
XLA Modules:
  0.0 72.9 jit_solution(16643050216325989752)
XLA Ops:
  0.0 1.0 %copy-done = f32[8,96,128]{2,1,0:T(8,128)S(1)} copy-done((f32[8,96,128]{2,1,0:T(8,128)S(1)}, f32[8,96,128]{2,1,0:T(8,128)}, u32[]{:S(2)}) %copy-start) | copy-done | bytes 393240
  1.0 0.7 copy-done.1
  1.7 0.7 shard_map.91
  2.4 15.0 %all_to_all.15.second_ref = f32[8,48,128]{2,1,0:T(8,128)S(1)} all-to-all(f32[8,48,128]{2,1,0:T(8,128)S(1)} %get-tuple-element.17), channel_id=1, replica_groups=mesh['stick'=8,'band'=4] {'stick'}, dimensions={0} | all-to-all | bytes 393216 | tf_op jit(solution)/shard_map/all_to_all | solution.py:280
  17.4 3.4 %all-to-all-start = ((f32[8,56,128]{2,1,0:T(8,128)}), f32[8,56,128]{2,1,0:T(8,128)S(1)}, u32[]{:S(2)}, u32[]{:S(2)}) async-start(f32[8,56,128]{2,1,0:T(8,128)} %get-tuple-element.16), calls=%async_computation | async-start | bytes 458752 | tf_op jit(solution)/shard_map/all_to_all | solution.py:280
  20.8 1.6 %collective-permute-start.2 = (f32[8,48,128]{2,1,0:T(8,128)S(1)}, f32[8,48,128]{2,1,0:T(8,128)S(1)}, u32[]{:S(2)}, u32[]{:S(2)}) collective-permute-start(f32[8,48,128]{2,1,0:T(8,128)S(1)} %all_to_all.15.second_ref), channel_id=1, source_target_pairs={{0,2},{1,3},{2,0},{3,1},{4,6},{5,7},{6,4},{7,5},{8,10},{9,11},{10,... | collective-permute-start | bytes 589832 | tf_op jit(solution)/shard_map/ppermute | solution.py:295
  22.4 6.4 %all-to-all-done.first_ref = f32[8,56,128]{2,1,0:T(8,128)S(1)} async-done(((f32[8,56,128]{2,1,0:T(8,128)}), f32[8,56,128]{2,1,0:T(8,128)S(1)}, u32[]{:S(2)}, u32[]{:S(2)}) %all-to-all-start) | async-done | bytes 229408 | tf_op jit(solution)/shard_map/all_to_all | solution.py:280
  28.7 1.5 %collective-permute-start.1 = (f32[8,56,128]{2,1,0:T(8,128)S(1)}, f32[8,56,128]{2,1,0:T(8,128)S(1)}, u32[]{:S(2)}, u32[]{:S(2)}) collective-permute-start(f32[8,56,128]{2,1,0:T(8,128)S(1)} %all-to-all-done.first_ref), channel_id=1, source_target_pairs={{0,2},{1,3},{2,0},{3,1},{4,6},{5,7},{6,4},{7,5},{8,10},{9,11},{10,... | collective-permute-start | bytes 688136 | tf_op jit(solution)/shard_map/ppermute | solution.py:295
  30.3 4.6 %shard_map.93 = (f32[1152,128]{1,0:T(8,128)S(1)}, s32[8,1024]{1,0:T(8,128)S(1)}) custom-call(f32[8,56,128]{2,1,0:T(8,128)S(1)} %all-to-all-done.first_ref, f32[8,48,128]{2,1,0:T(8,128)S(1)} %all_to_all.15.second_ref, bf16[128,288]{1,0:T(8,128)(2,1)S(1)} %get-tuple-element.20.stick_in_ref, bf16[96,144]{1,0:T(8,128)(2,1)S(1)} %get-tuple-element.21.backward_ref), custom_call_target="tpu_custom_call" | custom-call | flops 1000000000 | bytes 527360 | tf_op jit(solution)/shard_map/pallas_call | solution.py:268
  34.9 0.0 copy-start.2
  34.9 0.0 copy-start.3
  34.9 0.0 copy-start.4
  34.9 0.0 copy-start.8
  34.9 0.1 collective-permute-start
  35.0 0.0 collective-permute-done.2.second_ref
  35.0 0.0 collective-permute-done.1.first_ref
  35.0 5.1 %shard_map.94 = (f32[1152,128]{1,0:T(8,128)S(1)}, s32[8,1024]{1,0:T(8,128)}) custom-call(f32[8,56,128]{2,1,0:T(8,128)S(1)} %collective-permute-done.1.first_ref, f32[8,48,128]{2,1,0:T(8,128)S(1)} %collective-permute-done.2.second_ref, bf16[128,288]{1,0:T(8,128)(2,1)S(1)} %get-tuple-element.20.stick_in_ref, bf16[96,144]{1,0:T(8,128)(2,1)S(1)} %get-tuple-element.21.backward_ref), custom_call_target="tpu_custom_call" | custom-call | flops 1000000000 | bytes 527360 | tf_op jit(solution)/shard_map/pallas_call | solution.py:268
  40.2 0.5 collective-permute-start.3
  40.7 0.0 collective-permute-done.other_ref
  40.7 4.9 %shard_map.95.before_ref = f32[1152,128]{1,0:T(8,128)S(1)} custom-call(f32[1152,128]{1,0:T(8,128)S(1)} %get-tuple-element.22.phi_ref, f32[1152,128]{1,0:T(8,128)S(1)} %collective-permute-done.other_ref, f32[96,144]{1,0:T(8,128)S(1)} %copy-done.8, f32[96,144]{1,0:T(8,128)S(1)} %copy-done.7, f32[768,256]{1,0:T(8,128)S(1)} %copy-done.4, ...), custom_call_target="tpu_custom_call" | custom-call | flops 1811939328 | bytes 4042752 | tf_op jit(solution)/shard_map/pallas_call | solution.py:268
  45.6 0.0 collective-permute-done.3.second_ref
  45.6 10.6 %shard_map.96 = f32[8,96,128]{2,1,0:T(8,128)S(1)} custom-call(f32[1152,128]{1,0:T(8,128)S(1)} %get-tuple-element.22.phi_ref, f32[1152,128]{1,0:T(8,128)S(1)} %get-tuple-element.24.first_ref, f32[1152,128]{1,0:T(8,128)S(1)} %collective-permute-done.3.second_ref, f32[1152,128]{1,0:T(8,128)S(1)} %shard_map.95.before_ref, ...), custom_call_target="tpu_custom_call" | custom-call | flops 1811939328 | bytes 5365760 | tf_op jit(solution)/shard_map/pallas_call | solution.py:268
  56.2 16.0 %all_to_all.16 = f32[8,96,128]{2,1,0:T(8,128)S(1)} all-to-all(f32[8,96,128]{2,1,0:T(8,128)S(1)} %shard_map.96), channel_id=1, replica_groups=mesh['stick'=8,'band'=4] {'stick'}, dimensions={0} | all-to-all | bytes 786432 | tf_op jit(solution)/shard_map/all_to_all | solution.py:280
  72.1 0.7 %copy.11 = f32[8,96,128]{2,1,0:T(8,128)} copy(f32[8,96,128]{2,1,0:T(8,128)S(1)} %all_to_all.16) | data formatting | bytes 786432
  (13 shorter events, 0.0 us)
Async XLA Ops:
  0.0 1.0 %copy-start = (f32[8,96,128]{2,1,0:T(8,128)S(1)}, f32[8,96,128]{2,1,0:T(8,128)}, u32[]{:S(2)}) copy-start(f32[8,96,128]{2,1,0:T(8,128)} %sticks_ref.1) | copy-start | bytes 1179652
  1.0 0.7 copy-start.1
  1.7 28.6 %copy-start.5 = (f32[128,288]{1,0:T(8,128)S(1)}, f32[128,288]{1,0:T(8,128)}, u32[]{:S(2)}) copy-start(f32[128,288]{1,0:T(8,128)} %constant.18.clone.refs_0_) | copy-start | bytes 442372
  1.7 28.6 %copy-start.7 = (f32[96,144]{1,0:T(8,128)S(1)}, f32[96,144]{1,0:T(8,128)}, u32[]{:S(2)}) copy-start(f32[96,144]{1,0:T(8,128)} %constant.15.clone.refs_1_) | copy-start | bytes 165892
  17.4 11.4 %all-to-all-start = ((f32[8,56,128]{2,1,0:T(8,128)}), f32[8,56,128]{2,1,0:T(8,128)S(1)}, u32[]{:S(2)}, u32[]{:S(2)}) async-start(f32[8,56,128]{2,1,0:T(8,128)} %get-tuple-element.16), calls=%async_computation | async-start | bytes 458752 | tf_op jit(solution)/shard_map/all_to_all | solution.py:280
  20.8 14.2 %collective-permute-start.2 = (f32[8,48,128]{2,1,0:T(8,128)S(1)}, f32[8,48,128]{2,1,0:T(8,128)S(1)}, u32[]{:S(2)}, u32[]{:S(2)}) collective-permute-start(f32[8,48,128]{2,1,0:T(8,128)S(1)} %all_to_all.15.second_ref), channel_id=1, source_target_pairs={{0,2},{1,3},{2,0},{3,1},{4,6},{5,7},{6,4},{7,5},{8,10},{9,11},{10,... | collective-permute-start | bytes 589832 | tf_op jit(solution)/shard_map/ppermute | solution.py:295
  28.7 6.3 %collective-permute-start.1 = (f32[8,56,128]{2,1,0:T(8,128)S(1)}, f32[8,56,128]{2,1,0:T(8,128)S(1)}, u32[]{:S(2)}, u32[]{:S(2)}) collective-permute-start(f32[8,56,128]{2,1,0:T(8,128)S(1)} %all-to-all-done.first_ref), channel_id=1, source_target_pairs={{0,2},{1,3},{2,0},{3,1},{4,6},{5,7},{6,4},{7,5},{8,10},{9,11},{10,... | collective-permute-start | bytes 688136 | tf_op jit(solution)/shard_map/ppermute | solution.py:295
  34.9 5.8 %copy-start.2 = (f32[48,48,128]{2,1,0:T(8,128)S(1)}, f32[48,48,128]{2,1,0:T(8,128)}, u32[]{:S(2)}) copy-start(f32[48,48,128]{2,1,0:T(8,128)} %constant.20.clone.refs_4_) | copy-start | bytes 3538948
  34.9 5.8 %copy-start.3 = (f32[768,256]{1,0:T(8,128)S(1)}, f32[768,256]{1,0:T(8,128)}, u32[]{:S(2)}) copy-start(f32[768,256]{1,0:T(8,128)} %constant.17.clone.refs_3_) | copy-start | bytes 2359300
  34.9 5.8 %copy-start.4 = (f32[768,256]{1,0:T(8,128)S(1)}, f32[768,256]{1,0:T(8,128)}, u32[]{:S(2)}) copy-start(f32[768,256]{1,0:T(8,128)} %constant.16.clone.refs_2_) | copy-start | bytes 2359300
  34.9 5.8 %copy-start.8 = (f32[96,144]{1,0:T(8,128)S(1)}, f32[96,144]{1,0:T(8,128)}, u32[]{:S(2)}) copy-start(f32[96,144]{1,0:T(8,128)} %constant.14.clone.refs_0_) | copy-start | bytes 165892
  34.9 5.7 %collective-permute-start = (f32[1152,128]{1,0:T(8,128)S(1)}, f32[1152,128]{1,0:T(8,128)S(1)}, u32[]{:S(2)}, u32[]{:S(2)}) collective-permute-start(f32[1152,128]{1,0:T(8,128)S(1)} %get-tuple-element.22.phi_ref), channel_id=1, source_target_pairs={{0,1},{1,0},{2,3},{3,2},{4,5},{5,4},{6,7},{7,6},{8,9},{9,8},{10,11... | collective-permute-start | bytes 1769480 | tf_op jit(solution)/shard_map/ppermute | solution.py:298
  40.2 5.4 %copy-start.6 = (f32[96,288]{1,0:T(8,128)S(1)}, f32[96,288]{1,0:T(8,128)}, u32[]{:S(2)}) copy-start(f32[96,288]{1,0:T(8,128)} %constant.19.clone.stick_out_ref) | copy-start | bytes 331780
  40.2 5.4 %collective-permute-start.3 = (f32[1152,128]{1,0:T(8,128)S(1)}, f32[1152,128]{1,0:T(8,128)S(1)}, u32[]{:S(2)}, u32[]{:S(2)}) collective-permute-start(f32[1152,128]{1,0:T(8,128)S(1)} %get-tuple-element.24.first_ref), channel_id=1, source_target_pairs={{0,1},{1,0},{2,3},{3,2},{4,5},{5,4},{6,7},{7,6},{8,9},{9,8},{10,11... | collective-permute-start | bytes 1769480 | tf_op jit(solution)/shard_map/ppermute | solution.py:298

commit v5 on v3

--- a/solution.py
+++ b/solution.py
@@ -33,7 +33,7 @@
 
 def down(table):
     high, low = rounded_parts(table)
-    return np.concatenate([high, high, low], 0).astype(np.float32)
+    return np.block([[high, low], [high, np.zeros_like(low)]]).astype(np.float32)
 
 
 def make_tables(g):
@@ -41,16 +41,16 @@
     c, s = np.cos(angle), np.sin(angle)
     lower, upper = slice(0, g), slice(MID, MID + g)
 
-    z_forward = np.zeros((2 * LANES, 2 * LANES))
-    z_backward = np.zeros((2 * LANES, 2 * LANES))
-    for slab, half in enumerate((lower, upper)):
-        base = slab * LANES
-        real, imag = slice(base, base + g), slice(base + MID, base + MID + g)
-        one, two = half, slice(LANES + half.start, LANES + half.stop)
-        z_forward[one, real], z_forward[one, imag] = c, -s
-        z_forward[two, real], z_forward[two, imag] = s, c
-        z_backward[real, one], z_backward[real, two] = c, s
-        z_backward[imag, one], z_backward[imag, two] = -s, c
+    forward, backward, real_back = np.zeros((3, LANES, LANES))
+    forward[lower, lower], forward[lower, upper] = c, -s
+    forward[upper, lower], forward[upper, upper] = s, c
+    backward[lower, lower], backward[lower, upper] = c, s
+    backward[upper, lower], backward[upper, upper] = -s, c
+    for half in (lower, upper):
+        real_back[:, half] = backward[:, lower]
+    real_forward = np.zeros((LANES, 2 * LANES))
+    real_forward[lower, :LANES] = forward[lower]
+    real_forward[upper, LANES:] = forward[lower]
 
     stick_in = np.zeros((LANES, 2 * g))
     stick_in[lower, :g], stick_in[lower, g:] = c, -s
@@ -66,13 +66,14 @@
     coulomb[:, :, lower] = kernel
     coulomb[:, :, upper] = kernel
     return dict(
-        forward=across(np.concatenate([c, -s], 0)),
-        backward=across(np.concatenate([c, s], 0)),
-        z_forward=down(z_forward),
-        z_backward=down(z_backward / g**3),
+        forward=down(forward),
+        backward=down(backward),
+        last_backward=down(backward / g**3),
+        real_back=down(real_back),
+        real_forward=down(real_forward),
         stick_in=across(stick_in),
         stick_out=across(stick_out),
-        coulomb=coulomb,
+        coulomb=coulomb.reshape(g * g, LANES),
     )
 
 
@@ -96,34 +97,42 @@
 
 
 def turned(x):
-    return jnp.concatenate(
-        [pltpu.roll(x[:, k : k + LANES], MID, 1) for k in range(0, x.shape[1], LANES)], 1
-    )
-
-
-def left(table, x):
-    both = dot(table, stacked(x))
-    g = both.shape[0] // 2
-    return both[:g], both[g:]
-
-
-def left_complex(table, x):
-    cos, sin = left(table, x)
-    sign = jnp.where(lane_halves((1, x.shape[1])), -1.0, 1.0)
-    return cos + turned(sin) * sign
-
-
-def halves(x):
-    return x[:, :LANES], x[:, LANES:]
+    return pltpu.roll(x, MID, 1)
+
+
+def regrouped(a, b):
+    low = lane_halves(a.shape)
+    return jnp.where(low, a, turned(b)), jnp.where(low, turned(a), b)
+
+
+def transposed(a, b):
+    g = a.shape[0]
+    pad = jnp.zeros((MID - g, LANES), F32)
+    both = jnp.concatenate([a, pad, b, pad], 0).T
+    return regrouped(both[:g], both[MID : MID + g])
+
+
+def pairwise(function, slabs):
+    results = []
+    for k in range(0, len(slabs), 2):
+        results += function(slabs[k], slabs[k + 1])
+    return results
 
 
 def beside(a, b):
     return jnp.concatenate([a, b], 1)
 
 
-def right(parts, table):
-    high, low = zip(*[split(x) for x in parts])
-    return dot(jnp.concatenate(high + low + high, 1), table)
+def right(x, table):
+    both = dot(beside(*split(x)), table)
+    width = both.shape[1] // 2
+    return both[:, :width] + both[:, width:]
+
+
+def right_slabs(slabs, table):
+    g = slabs[0].shape[0]
+    out = right(jnp.concatenate(slabs, 0), table)
+    return [out[k : k + g] for k in range(0, out.shape[0], g)]
 
 
 def strided(ref, first, g):
@@ -172,14 +181,29 @@
         out_ref[own ^ d] = block_ref[...]
 
 
+def folded_parts(parts, g):
+    used = lax.broadcasted_iota(jnp.int32, parts[0].shape, 1) % MID < g
+    width = g // FOLD
+    return [jnp.where(used, parts[k], pltpu.roll(parts[FOLD], g - k * width, 1)) for k in range(FOLD)]
+
+
+def folded_position(columns, g):
+    kx = lax.div(columns, g)
+    ky = columns - kx * g
+    group, member = lax.div(kx, 2 * FOLD + 2), lax.rem(kx, 2 * FOLD + 2)
+    pair, half = lax.div(member, 2), lax.rem(member, 2)
+    width = g // FOLD
+    piece = lax.div(ky, width)
+    last = pair == FOLD
+    row = group * FOLD + jnp.where(last, piece, pair)
+    lane = half * MID + jnp.where(last, g + ky - piece * width, ky)
+    return jnp.where(columns < 0, -1, row * LANES + lane)
+
+
 def fold(field_ref, folded_ref, g):
     rows = folded_ref.shape[0] // FOLD
-    used = lax.broadcasted_iota(jnp.int32, (rows, LANES), 1) % MID < g
-    last = field_ref[FOLD * rows :, :]
-    width = g // FOLD
-    for k in range(FOLD):
-        part = slice(k * rows, (k + 1) * rows)
-        folded_ref[part, :] = jnp.where(used, field_ref[part, :], pltpu.roll(last, g - k * width, 1))
+    parts = [field_ref[k * rows : (k + 1) * rows, :] for k in range(FOLD + 1)]
+    folded_ref[...] = jnp.concatenate(folded_parts(parts, g), 0)
 
 
 def unfold(folded_ref, field_ref, g):
@@ -195,64 +219,72 @@
     field_ref[FOLD * rows :, :] = last
 
 
+def store(ref, first, slabs):
+    g = slabs[0].shape[0]
+    for k, slab in enumerate(slabs):
+        ref[slab_rows(first + k, g), :] = slab
+
+
 def field_kernel(g, count, *refs):
     received = refs[:count]
-    stick_in_ref, backward_ref, phi_ref, folded_ref, columns_ref, work_a = refs[count:]
+    stick_in_ref, backward_ref, real_back_ref, phi_ref, folded_ref, positions_ref, work_a = refs[count:]
     columns = jnp.concatenate([ref[2 * g : 2 * g + 1, :] for ref in received], 1).astype(jnp.int32)
-    columns_ref[...] = jnp.broadcast_to(columns, columns_ref.shape)
-    stick_in, backward = stick_in_ref[...], backward_ref[...]
+    positions_ref[...] = jnp.broadcast_to(folded_position(columns, g), positions_ref.shape)
+    stick_in, backward, real_back = stick_in_ref[...], backward_ref[...], real_back_ref[...]
     pieces = []
     for k in range(0, count, 2):
         block = beside(received[k][: 2 * g, :], received[k + 1][: 2 * g, :])
         pieces.append(beside(*split(dot(stick_in, stacked(block)).T)))
     sticks = jnp.concatenate(pieces, 0)
 
-    for first in range(0, g, 2 * PAIRS):
-        both = dot(one_hot(columns, first * g, 2 * PAIRS * g), sticks)
+    step = g // 4
+    for first in range(0, g, step):
+        both = dot(one_hot(columns, first * g, step * g), sticks)
         placed = both[:, :LANES] + both[:, LANES:]
-        for k in range(0, 2 * PAIRS, 2):
-            x = beside(placed[k * g : (k + 1) * g], placed[(k + 1) * g : (k + 2) * g])
-            for j, slab in enumerate(halves(left_complex(backward, x))):
-                work_a[slab_rows(first + k + j, g), :] = slab
-
-    for pair in range(g // 2):
-        x = beside(strided(work_a, pair, g), strided(work_a, pair + g // 2, g))
-        (cos, cos_up), (sin, sin_up) = map(halves, left(backward, x))
-        lower = cos - pltpu.roll(sin, MID, 1)
-        upper = pltpu.roll(cos_up, MID, 1) - sin_up
-        phi_ref[slab_rows(pair, g), :] = jnp.where(lane_halves(lower.shape), lower, upper)
+        slabs = pairwise(transposed, [placed[k * g : (k + 1) * g] for k in range(step)])
+        store(work_a, first, right_slabs(slabs, backward))
+
+    half = g // 2
+    for start in range(0, half, PAIRS):
+        slabs = []
+        for z in range(start, start + PAIRS):
+            slabs += transposed(strided(work_a, z, g), strided(work_a, z + half, g))
+        slabs = right_slabs(slabs, real_back)
+        low = lane_halves(slabs[0].shape)
+        store(phi_ref, start, pairwise(lambda a, b: [jnp.where(low, a, b)], slabs))
     fold(phi_ref, folded_ref, g)
 
 
 def potentials(g, phi_ref, first_ref, second_ref, tables, work_a, work_b, emit):
-    forward, backward, z_forward, z_backward = [ref[...].astype(BF16) for ref in tables[:4]]
-    coulomb_ref = tables[4]
+    forward, backward, last_backward = [ref[...].astype(BF16) for ref in tables[:3]]
+    coulomb_ref = tables[3]
     half = g // 2
     for start in range(0, half, PAIRS):
         rows = slab_rows(start, g, PAIRS)
         phi = phi_ref[rows, :]
-        spectrum = right([phi * first_ref[rows, :], phi * second_ref[rows, :]], z_forward)
-        for k in range(PAIRS):
-            slabs = halves(left_complex(forward, spectrum[k * g : (k + 1) * g]))
-            work_a[slab_rows(start + k, g), :] = slabs[0]
-            work_a[slab_rows(start + k + half, g), :] = slabs[1]
-
-    for kx in range(0, g, 2):
-        x = left_complex(forward, beside(strided(work_a, kx, g), strided(work_a, kx + 1, g)))
-        x = left_complex(backward, x * beside(coulomb_ref[kx], coulomb_ref[kx + 1]))
-        for j, slab in enumerate(halves(x)):
-            work_b[slab_rows(kx + j, g), :] = slab
+        lower, upper = regrouped(phi * first_ref[rows, :], phi * second_ref[rows, :])
+        spectrum = right(jnp.concatenate([lower, upper], 0), forward)
+        slabs = pairwise(transposed, [spectrum[k * g : (k + 1) * g] for k in range(2 * PAIRS)])
+        slabs = right_slabs(slabs, forward)
+        store(work_a, start, slabs[:PAIRS])
+        store(work_a, start + half, slabs[PAIRS:])
+
+    for first in range(0, g, 2 * PAIRS):
+        slabs = pairwise(transposed, [strided(work_a, first + k, g) for k in range(2 * PAIRS)])
+        spectrum = right(jnp.concatenate(slabs, 0), forward) * coulomb_ref[slab_rows(first, g, 2 * PAIRS), :]
+        spectrum = right(spectrum, backward)
+        slabs = pairwise(transposed, [spectrum[k * g : (k + 1) * g] for k in range(2 * PAIRS)])
+        store(work_b, first, right_slabs(slabs, backward))
 
     for start in range(0, half, PAIRS):
-        slabs = [
-            left_complex(backward, beside(strided(work_b, pair, g), strided(work_b, pair + half, g)))
-            for pair in range(start, start + PAIRS)
-        ]
-        emit(start, *halves(right([jnp.concatenate(slabs, 0)], z_backward)))
+        slabs = [strided(work_b, start + k, g) for k in range(PAIRS)]
+        slabs += [strided(work_b, start + k + half, g) for k in range(PAIRS)]
+        out = right(jnp.concatenate(pairwise(transposed, slabs), 0), last_backward)
+        emit(start, *regrouped(out[: PAIRS * g], out[PAIRS * g :]))
 
 
 def near_kernel(g, phi_ref, near_ref, *refs):
-    tables, (sum_ref, other_ref, work_a, work_b) = refs[:5], refs[5:]
+    tables, (sum_ref, other_ref, work_a, work_b) = refs[:4], refs[4:]
     unfold(near_ref, other_ref, g)
 
     def emit(start, own, other):
@@ -263,7 +295,7 @@
 
 
 def middle_kernel(g, phi_ref, ahead_ref, behind_ref, before_ref, *refs):
-    tables, (sum_ref, first_ref, second_ref, work_a, work_b) = refs[:5], refs[5:]
+    tables, (sum_ref, first_ref, second_ref, work_a, work_b) = refs[:4], refs[4:]
     unfold(ahead_ref, first_ref, g)
     unfold(behind_ref, second_ref, g)
 
@@ -274,43 +306,43 @@
     potentials(g, phi_ref, first_ref, second_ref, tables, work_a, work_b, emit)
 
 
-def far_kernel(g, weights, phi_ref, ahead_ref, across_ref, before_ref, columns_ref, stick_out_ref, *refs):
-    tables, out_refs = refs[:5], refs[5:-5]
+def far_kernel(g, weights, phi_ref, ahead_ref, across_ref, before_ref, positions_ref, stick_out_ref, real_forward_ref, *refs):
+    tables, out_refs = refs[:4], refs[4:-5]
     first_ref, second_ref, work_a, work_b, parts_ref = refs[-5:]
     unfold(ahead_ref, first_ref, g)
     unfold(across_ref, second_ref, g)
-    forward = tables[0][...].astype(BF16)
+    forward, real_forward = tables[0][...].astype(BF16), real_forward_ref[...].astype(BF16)
     half = g // 2
 
     def emit(start, first, second):
         rows = slab_rows(start, g, PAIRS)
         total = before_ref[rows, :] + weights[0] * (first * first_ref[rows, :])
         total = total + weights[1] * (second * second_ref[rows, :])
-        for k in range(0, PAIRS, 2):
-            cos, sin = left(forward, beside(total[k * g : (k + 1) * g], total[(k + 1) * g : (k + 2) * g]))
-            low = lane_halves(cos.shape)
-            lower, upper = halves(jnp.where(low, cos, turned(sin))), halves(jnp.where(low, turned(cos), sin))
-            for j in range(2):
-                work_a[slab_rows(start + k + j, g), :] = lower[j]
-                work_a[slab_rows(start + k + j + half, g), :] = upper[j]
+        spectrum = right(total, real_forward)
+        spectrum = jnp.concatenate([spectrum[:, :LANES], spectrum[:, LANES:]], 0)
+        slabs = pairwise(transposed, [spectrum[k * g : (k + 1) * g] for k in range(2 * PAIRS)])
+        slabs = right_slabs(slabs, forward)
+        store(work_a, start, slabs[:PAIRS])
+        store(work_a, start + half, slabs[PAIRS:])
 
     potentials(g, phi_ref, first_ref, second_ref, tables, work_a, work_b, emit)
 
-    for first in range(0, g, 2 * PAIRS):
-        slabs = []
-        for kx in range(first, first + 2 * PAIRS, 2):
-            slabs += halves(left_complex(forward, beside(strided(work_a, kx, g), strided(work_a, kx + 1, g))))
-        lined = jnp.concatenate(slabs, 0).T
-        lined = jnp.concatenate([lined[:g], lined[MID : MID + g]], 0)
-        parts_ref[:, first * g : (first + 2 * PAIRS) * g] = jnp.concatenate(split(lined), 0)
+    many = 2 * FOLD + 2
+    width = FOLD * LANES
+    for group in range(g // many):
+        parts = []
+        for kx in range(group * many, (group + 1) * many, 2):
+            parts.append(jnp.concatenate(regrouped(strided(work_a, kx, g), strided(work_a, kx + 1, g)), 0))
+        line = jnp.concatenate(folded_parts(parts, g), 1)
+        parts_ref[:, group * width : (group + 1) * width] = jnp.concatenate(split(line), 0)
 
     parts = parts_ref[...]
     stick_out = stick_out_ref[...].astype(BF16)
     for k in range(0, len(out_refs), 2):
-        hot = one_hot(columns_ref[:1, k * LANES : (k + 2) * LANES], 0, g * g)
+        hot = one_hot(positions_ref[:1, k * LANES : (k + 2) * LANES], 0, g * g)
         both = dot(parts, hot)
-        picked = both[: 2 * g] + both[2 * g :]
-        out_refs[k][...], out_refs[k + 1][...] = halves(dot(stick_out, stacked(picked)))
+        picked = dot(stick_out, stacked(both[: 2 * g] + both[2 * g :]))
+        out_refs[k][...], out_refs[k + 1][...] = picked[:, :LANES], picked[:, LANES:]
 
 
 def call(kernel, out_shapes, scratch, flops, *operands, space=pltpu.VMEM):
@@ -358,11 +390,11 @@
         space=pltpu.HBM,
     )
     received = exchanged(sent)
-    first_tables = lax.optimization_barrier((t["stick_in"], t["backward"], sent[0]))[:2]
+    first_tables = lax.optimization_barrier((t["stick_in"], t["backward"], t["real_back"], sent[0]))[:3]
     first_tables = call(
         table_kernel, [jax.ShapeDtypeStruct(x.shape, BF16) for x in first_tables], [], 10**9, *first_tables
     )
-    phi, packed, columns = call(
+    phi, packed, positions = call(
         functools.partial(field_kernel, g, owners),
         [field, folded, jax.ShapeDtypeStruct((8, owners * slots), jnp.int32)],
         [work],
@@ -370,7 +402,7 @@
         *received,
         *first_tables,
     )
-    pot_tables = [t["forward"], t["backward"], t["z_forward"], t["z_backward"], t["coulomb"]]
+    pot_tables = [t["forward"], t["backward"], t["last_backward"], t["coulomb"]]
     swap = [(i, i ^ 1) for i in range(groups)]
 
     def fetched(distance):
@@ -410,8 +442,9 @@
         first,
         second,
         total,
-        columns,
+        positions,
         t["stick_out"],
+        t["real_forward"],
         *pot_tables,
     )
     return call(place_kernel, jax.ShapeDtypeStruct(sticks.shape, F32), [], 10**6, *exchanged(result))

time: 66.3 us -> 69.2 us (1.044)
  Pallas kernels: 21.6 us -> 29.7 us
  waiting for transfers between devices: 15.6 us -> 9.24 us
  local copies, waits for them, and re-layouts: 3.5 us -> 4.5 us
    pallas_call x6, Pallas kernels: 21.6 us -> 29.7 us  [call(): pl.pallas_call(kernel, out_shape=out_shapes, in_specs=[pl.BlockSpec(memor...]
    ppermute x1, waiting for transfers between devices: 5.85 us -> 0.37 us  [fetched(): lax.ppermute(packed, 'band', [(i, (i - distance) % groups) for i in range...]
    unnamed x20 -> x22, local copies, waits for them, and re-layouts: 3.5 us -> 4.5 us
    ppermute x14, waiting for transfers between devices: 7.7 us -> 6.86 us  [exchanged(): lax.ppermute(blocks[d], 'stick', [(i, i ^ d) for i in range(owners)])]
  transfers between devices with their start and end apart: 17 -> 17, of which waited for: 8 -> 8; matrix products, arithmetic and copies ran while one was open for 0% -> 0% of each run, Pallas kernels for 7% -> 15%
where the time goes in v5:
time: 69.2 us; the launch traced here: 68.9 us
  Pallas kernels  29.7 us (43%)
  starting transfers between devices  25.3 us (37%)
  waiting for transfers between devices  9.24 us (13%)
  local copies, waits for them, and re-layouts  4.5 us (7%)
    pallas_call x6, Pallas kernels, call(): pl.pallas_call(kernel, out_shape=out_shapes, in_specs=[pl.BlockSpec(memor...  29.7 us
    ppermute x14, starting transfers between devices, exchanged(): lax.ppermute(blocks[d], 'stick', [(i, i ^ d) for i in range(owners)])  23.7 us
    ppermute x14, waiting for transfers between devices, exchanged(): lax.ppermute(blocks[d], 'stick', [(i, i ^ d) for i in range(owners)])  6.86 us
    unnamed x22, local copies, waits for them, and re-layouts  4.5 us
    ppermute x1, waiting for transfers between devices, on_device(): first, second = (ahead, lax.ppermute(ahead, 'band', swap))  1.79 us
    ppermute x1, starting transfers between devices, fetched(): lax.ppermute(packed, 'band', [(i, (i - distance) % groups) for i in range...  1.55 us
  transfers between devices with their start and end apart: 17, of which 8 were waited for; matrix products, arithmetic and copies ran while one was open for 0% of the time, Pallas kernels for 15%

profile of v5, /device:TPU:0, one launch (start us, length us, event | category | flops | bytes accessed | tf_op | source)
XLA Modules:
  0.0 68.9 jit_solution(2863686481426736584)
XLA Ops:
  0.0 1.0 %copy-done = f32[8,96,128]{2,1,0:T(8,128)S(1)} copy-done((f32[8,96,128]{2,1,0:T(8,128)S(1)}, f32[8,96,128]{2,1,0:T(8,128)}, u32[]{:S(2)}) %copy-start) | copy-done | bytes 393240
  1.0 0.7 copy-done.1
  2.2 3.0 %collective-permute-start = (f32[104,128]{1,0:T(8,128)S(1)}, f32[104,128]{1,0:T(8,128)S(1)}, u32[]{:S(2)}, u32[]{:S(2)}) collective-permute-start(f32[104,128]{1,0:T(8,128)S(1)} %get-tuple-element.33), channel_id=1, source_target_pairs={{0,4},{4,0},{8,12},{12,8},{16,20},{20,16},{24,28},{28,24},{1,5},{5... | collective-permute-start | bytes 159752 | tf_op jit(solution)/shard_map/ppermute | solution.py:366
  5.3 1.6 %collective-permute-start.1 = (f32[104,128]{1,0:T(8,128)S(1)}, f32[104,128]{1,0:T(8,128)S(1)}, u32[]{:S(2)}, u32[]{:S(2)}) collective-permute-start(f32[104,128]{1,0:T(8,128)S(1)} %get-tuple-element.34), channel_id=1, source_target_pairs={{0,8},{4,12},{8,0},{12,4},{16,24},{20,28},{24,16},{28,20},{1,9},{5... | collective-permute-start | bytes 159752 | tf_op jit(solution)/shard_map/ppermute | solution.py:366
  6.9 3.0 %collective-permute-start.3 = (f32[104,128]{1,0:T(8,128)S(1)}, f32[104,128]{1,0:T(8,128)S(1)}, u32[]{:S(2)}, u32[]{:S(2)}) collective-permute-start(f32[104,128]{1,0:T(8,128)S(1)} %get-tuple-element.36), channel_id=1, source_target_pairs={{0,16},{4,20},{8,24},{12,28},{16,0},{20,4},{24,8},{28,12},{1,17},{... | collective-permute-start | bytes 159752 | tf_op jit(solution)/shard_map/ppermute | solution.py:366
  9.8 1.3 %collective-permute-start.4 = (f32[104,128]{1,0:T(8,128)S(1)}, f32[104,128]{1,0:T(8,128)S(1)}, u32[]{:S(2)}, u32[]{:S(2)}) collective-permute-start(f32[104,128]{1,0:T(8,128)S(1)} %get-tuple-element.37), channel_id=1, source_target_pairs={{0,20},{4,16},{8,28},{12,24},{16,4},{20,0},{24,12},{28,8},{1,21},{... | collective-permute-start | bytes 159752 | tf_op jit(solution)/shard_map/ppermute | solution.py:366
  11.1 3.6 %collective-permute-start.5 = (f32[104,128]{1,0:T(8,128)S(1)}, f32[104,128]{1,0:T(8,128)S(1)}, u32[]{:S(2)}, u32[]{:S(2)}) collective-permute-start(f32[104,128]{1,0:T(8,128)S(1)} %get-tuple-element.38), channel_id=1, source_target_pairs={{0,24},{4,28},{8,16},{12,20},{16,8},{20,12},{24,0},{28,4},{1,25},{... | collective-permute-start | bytes 159752 | tf_op jit(solution)/shard_map/ppermute | solution.py:366
  14.8 0.9 %copy-done.4 = f32[256,256]{1,0:T(8,128)S(1)} copy-done((f32[256,256]{1,0:T(8,128)S(1)}, f32[256,256]{1,0:T(8,128)}, u32[]{:S(2)}) %copy-start.4) | copy-done | bytes 262168
  15.7 0.9 %copy-done.8 = f32[256,256]{1,0:T(8,128)S(1)} copy-done((f32[256,256]{1,0:T(8,128)S(1)}, f32[256,256]{1,0:T(8,128)}, u32[]{:S(2)}) %copy-start.8) | copy-done | bytes 262168
  16.7 0.9 %copy-done.9 = f32[128,288]{1,0:T(8,128)S(1)} copy-done((f32[128,288]{1,0:T(8,128)S(1)}, f32[128,288]{1,0:T(8,128)}, u32[]{:S(2)}) %copy-start.9) | copy-done | bytes 147480
  18.1 3.5 %collective-permute-done.6.refs_7_ = f32[104,128]{1,0:T(8,128)S(1)} collective-permute-done((f32[104,128]{1,0:T(8,128)S(1)}, f32[104,128]{1,0:T(8,128)S(1)}, u32[]{:S(2)}, u32[]{:S(2)}) %collective-permute-start.6) | collective-permute-done | bytes 53280 | tf_op jit(solution)/shard_map/ppermute | solution.py:366
  21.6 5.6 %shard_map.102 = (f32[1152,128]{1,0:T(8,128)S(1)}, f32[864,128]{1,0:T(8,128)S(1)}, s32[8,1024]{1,0:T(8,128)S(1)}) custom-call(f32[104,128]{1,0:T(8,128)S(1)} %get-tuple-element.32.refs_0_, f32[104,128]{1,0:T(8,128)S(1)} %collective-permute-done.refs_1_, f32[104,128]{1,0:T(8,128)S(1)} %collective-permute-done.1.refs_2_, ...), custom_call_target="tpu_custom_call" | custom-call | flops 1000000000 | bytes 761856 | tf_op jit(solution)/shard_map/pallas_call | solution.py:351
  27.3 1.6 %collective-permute-start.7 = (f32[864,128]{1,0:T(8,128)S(1)}, f32[864,128]{1,0:T(8,128)S(1)}, u32[]{:S(2)}, u32[]{:S(2)}) collective-permute-start(f32[864,128]{1,0:T(8,128)S(1)} %get-tuple-element.47), channel_id=1, source_target_pairs={{0,2},{1,3},{2,0},{3,1},{4,6},{5,7},{6,4},{7,5},{8,10},{9,11},{10,... | collective-permute-start | bytes 1327112 | tf_op jit(solution)/shard_map/ppermute | solution.py:409
  29.1 10.4 %shard_map.103.before_ref = f32[1152,128]{1,0:T(8,128)S(1)} custom-call(f32[1152,128]{1,0:T(8,128)S(1)} %get-tuple-element.46.phi_ref, f32[864,128]{1,0:T(8,128)S(1)} %collective-permute-done.8.near_ref, f32[256,256]{1,0:T(8,128)S(1)} %copy-done.7, f32[256,256]{1,0:T(8,128)S(1)} %copy-done.5, f32[256,256]{1,0:T(8,128)S(1)} %copy-done.6, ...), custom_call_target="tpu_custom_call" | custom-call | flops 1811939328 | bytes 2998272 | tf_op jit(solution)/shard_map/pallas_call | solution.py:351
  39.9 1.8 %collective-permute-done.9.across_ref = f32[864,128]{1,0:T(8,128)S(1)} collective-permute-done((f32[864,128]{1,0:T(8,128)S(1)}, f32[864,128]{1,0:T(8,128)S(1)}, u32[]{:S(2)}, u32[]{:S(2)}) %collective-permute-start.9) | collective-permute-done | bytes 442400 | tf_op jit(solution)/shard_map/ppermute | solution.py:419
  41.7 12.3 %shard_map.104 = (f32[96,128]{1,0:T(8,128)S(1)}, f32[96,128]{1,0:T(8,128)S(1)}, f32[96,128]{1,0:T(8,128)S(1)}, f32[96,128]{1,0:T(8,128)S(1)}, f32[96,128]{1,0:T(...) custom-call(f32[1152,128]{1,0:T(8,128)S(1)} %get-tuple-element.46.phi_ref, ...), custom_call_target="tpu_custom_call" | custom-call | flops 1811939328 | bytes 4698112 | tf_op jit(solution)/shard_map/pallas_call | solution.py:351
  54.6 3.0 %collective-permute-start.12 = (f32[96,128]{1,0:T(8,128)S(1)}, f32[96,128]{1,0:T(8,128)S(1)}, u32[]{:S(2)}, u32[]{:S(2)}) collective-permute-start(f32[96,128]{1,0:T(8,128)S(1)} %get-tuple-element.54), channel_id=1, source_target_pairs={{0,12},{4,8},{8,4},{12,0},{16,28},{20,24},{24,20},{28,16},{1,13},{... | collective-permute-start | bytes 147464 | tf_op jit(solution)/shard_map/ppermute | solution.py:366
  57.6 0.8 %collective-permute-start.13 = (f32[96,128]{1,0:T(8,128)S(1)}, f32[96,128]{1,0:T(8,128)S(1)}, u32[]{:S(2)}, u32[]{:S(2)}) collective-permute-start(f32[96,128]{1,0:T(8,128)S(1)} %get-tuple-element.55), channel_id=1, source_target_pairs={{0,16},{4,20},{8,24},{12,28},{16,0},{20,4},{24,8},{28,12},{1,17},{... | collective-permute-start | bytes 147464 | tf_op jit(solution)/shard_map/ppermute | solution.py:366
  58.4 2.0 %collective-permute-start.14 = (f32[96,128]{1,0:T(8,128)S(1)}, f32[96,128]{1,0:T(8,128)S(1)}, u32[]{:S(2)}, u32[]{:S(2)}) collective-permute-start(f32[96,128]{1,0:T(8,128)S(1)} %get-tuple-element.56), channel_id=1, source_target_pairs={{0,20},{4,16},{8,28},{12,24},{16,4},{20,0},{24,12},{28,8},{1,21},{... | collective-permute-start | bytes 147464 | tf_op jit(solution)/shard_map/ppermute | solution.py:366
  60.4 0.9 %collective-permute-start.15 = (f32[96,128]{1,0:T(8,128)S(1)}, f32[96,128]{1,0:T(8,128)S(1)}, u32[]{:S(2)}, u32[]{:S(2)}) collective-permute-start(f32[96,128]{1,0:T(8,128)S(1)} %get-tuple-element.57), channel_id=1, source_target_pairs={{0,24},{4,28},{8,16},{12,20},{16,8},{20,12},{24,0},{28,4},{1,25},{... | collective-permute-start | bytes 147464 | tf_op jit(solution)/shard_map/ppermute | solution.py:366
  61.4 3.9 %collective-permute-start.16 = (f32[96,128]{1,0:T(8,128)S(1)}, f32[96,128]{1,0:T(8,128)S(1)}, u32[]{:S(2)}, u32[]{:S(2)}) collective-permute-start(f32[96,128]{1,0:T(8,128)S(1)} %get-tuple-element.58), channel_id=1, source_target_pairs={{0,28},{4,24},{8,20},{12,16},{16,12},{20,8},{24,4},{28,0},{1,29},{... | collective-permute-start | bytes 147464 | tf_op jit(solution)/shard_map/ppermute | solution.py:366
  65.2 1.0 %collective-permute-done.14.refs_5_ = f32[96,128]{1,0:T(8,128)S(1)} collective-permute-done((f32[96,128]{1,0:T(8,128)S(1)}, f32[96,128]{1,0:T(8,128)S(1)}, u32[]{:S(2)}, u32[]{:S(2)}) %collective-permute-start.14) | collective-permute-done | bytes 49184 | tf_op jit(solution)/shard_map/ppermute | solution.py:366
  66.4 1.8 %collective-permute-done.16.refs_7_ = f32[96,128]{1,0:T(8,128)S(1)} collective-permute-done((f32[96,128]{1,0:T(8,128)S(1)}, f32[96,128]{1,0:T(8,128)S(1)}, u32[]{:S(2)}, u32[]{:S(2)}) %collective-permute-start.16) | collective-permute-done | bytes 49184 | tf_op jit(solution)/shard_map/ppermute | solution.py:366
  68.1 0.8 %shard_map.105 = f32[8,96,128]{2,1,0:T(8,128)} custom-call(f32[96,128]{1,0:T(8,128)S(1)} %get-tuple-element.51.refs_0_, f32[96,128]{1,0:T(8,128)S(1)} %collective-permute-done.10.refs_1_, f32[96,128]{1,0:T(8,128)S(1)} %collective-permute-done.11.refs_2_, f32[96,128]{1,0:T(8,128)S(1)} %collective-permute-done.12.refs_3_, ...), custom_call_target="tpu_custom_call" | custom-call | flops 1000000 | bytes 393216 | tf_op jit(solution)/shard_map/pallas_call | solution.py:351
  (38 shorter events, 2.5 us)
Async XLA Ops:
  0.0 1.0 %copy-start = (f32[8,96,128]{2,1,0:T(8,128)S(1)}, f32[8,96,128]{2,1,0:T(8,128)}, u32[]{:S(2)}) copy-start(f32[8,96,128]{2,1,0:T(8,128)} %sticks_ref.1) | copy-start | bytes 1179652
  2.2 8.9 %collective-permute-start = (f32[104,128]{1,0:T(8,128)S(1)}, f32[104,128]{1,0:T(8,128)S(1)}, u32[]{:S(2)}, u32[]{:S(2)}) collective-permute-start(f32[104,128]{1,0:T(8,128)S(1)} %get-tuple-element.33), channel_id=1, source_target_pairs={{0,4},{4,0},{8,12},{12,8},{16,20},{20,16},{24,28},{28,24},{1,5},{5... | collective-permute-start | bytes 159752 | tf_op jit(solution)/shard_map/ppermute | solution.py:366
  5.3 9.5 %collective-permute-start.1 = (f32[104,128]{1,0:T(8,128)S(1)}, f32[104,128]{1,0:T(8,128)S(1)}, u32[]{:S(2)}, u32[]{:S(2)}) collective-permute-start(f32[104,128]{1,0:T(8,128)S(1)} %get-tuple-element.34), channel_id=1, source_target_pairs={{0,8},{4,12},{8,0},{12,4},{16,24},{20,28},{24,16},{28,20},{1,9},{5... | collective-permute-start | bytes 159752 | tf_op jit(solution)/shard_map/ppermute | solution.py:366
  6.9 10.8 %collective-permute-start.2 = (f32[104,128]{1,0:T(8,128)S(1)}, f32[104,128]{1,0:T(8,128)S(1)}, u32[]{:S(2)}, u32[]{:S(2)}) collective-permute-start(f32[104,128]{1,0:T(8,128)S(1)} %get-tuple-element.35), channel_id=1, source_target_pairs={{0,12},{4,8},{8,4},{12,0},{16,28},{20,24},{24,20},{28,16},{1,13},{... | collective-permute-start | bytes 159752 | tf_op jit(solution)/shard_map/ppermute | solution.py:366
  6.9 10.8 %collective-permute-start.3 = (f32[104,128]{1,0:T(8,128)S(1)}, f32[104,128]{1,0:T(8,128)S(1)}, u32[]{:S(2)}, u32[]{:S(2)}) collective-permute-start(f32[104,128]{1,0:T(8,128)S(1)} %get-tuple-element.36), channel_id=1, source_target_pairs={{0,16},{4,20},{8,24},{12,28},{16,0},{20,4},{24,8},{28,12},{1,17},{... | collective-permute-start | bytes 159752 | tf_op jit(solution)/shard_map/ppermute | solution.py:366
  9.8 8.2 %collective-permute-start.4 = (f32[104,128]{1,0:T(8,128)S(1)}, f32[104,128]{1,0:T(8,128)S(1)}, u32[]{:S(2)}, u32[]{:S(2)}) collective-permute-start(f32[104,128]{1,0:T(8,128)S(1)} %get-tuple-element.37), channel_id=1, source_target_pairs={{0,20},{4,16},{8,28},{12,24},{16,4},{20,0},{24,12},{28,8},{1,21},{... | collective-permute-start | bytes 159752 | tf_op jit(solution)/shard_map/ppermute | solution.py:366
  11.1 6.9 %collective-permute-start.5 = (f32[104,128]{1,0:T(8,128)S(1)}, f32[104,128]{1,0:T(8,128)S(1)}, u32[]{:S(2)}, u32[]{:S(2)}) collective-permute-start(f32[104,128]{1,0:T(8,128)S(1)} %get-tuple-element.38), channel_id=1, source_target_pairs={{0,24},{4,28},{8,16},{12,20},{16,8},{20,12},{24,0},{28,4},{1,25},{... | collective-permute-start | bytes 159752 | tf_op jit(solution)/shard_map/ppermute | solution.py:366
  14.7 6.8 %collective-permute-start.6 = (f32[104,128]{1,0:T(8,128)S(1)}, f32[104,128]{1,0:T(8,128)S(1)}, u32[]{:S(2)}, u32[]{:S(2)}) collective-permute-start(f32[104,128]{1,0:T(8,128)S(1)} %get-tuple-element.39), channel_id=1, source_target_pairs={{0,28},{4,24},{8,20},{12,16},{16,12},{20,8},{24,4},{28,0},{1,29},{... | collective-permute-start | bytes 159752 | tf_op jit(solution)/shard_map/ppermute | solution.py:366
  21.6 7.5 %copy-start.2 = (f32[2304,128]{1,0:T(8,128)S(1)}, f32[2304,128]{1,0:T(8,128)}, u32[]{:S(2)}) copy-start(f32[2304,128]{1,0:T(8,128)} %constant.23.clone.refs_3_) | copy-start | bytes 3538948
  21.6 7.5 %copy-start.5 = (f32[256,256]{1,0:T(8,128)S(1)}, f32[256,256]{1,0:T(8,128)}, u32[]{:S(2)}) copy-start(f32[256,256]{1,0:T(8,128)} %constant.17.clone.refs_1_) | copy-start | bytes 786436
  21.6 7.5 %copy-start.6 = (f32[256,256]{1,0:T(8,128)S(1)}, f32[256,256]{1,0:T(8,128)}, u32[]{:S(2)}) copy-start(f32[256,256]{1,0:T(8,128)} %constant.18.clone.refs_2_) | copy-start | bytes 786436
  21.6 7.5 %copy-start.7 = (f32[256,256]{1,0:T(8,128)S(1)}, f32[256,256]{1,0:T(8,128)}, u32[]{:S(2)}) copy-start(f32[256,256]{1,0:T(8,128)} %constant.16.clone.refs_0_) | copy-start | bytes 786436
  27.2 1.9 %collective-permute-start.8 = (f32[864,128]{1,0:T(8,128)S(1)}, f32[864,128]{1,0:T(8,128)S(1)}, u32[]{:S(2)}, u32[]{:S(2)}) collective-permute-start(f32[864,128]{1,0:T(8,128)S(1)} %get-tuple-element.47), channel_id=1, source_target_pairs={{0,1},{1,0},{2,3},{3,2},{4,5},{5,4},{6,7},{7,6},{8,9},{9,8},{10,11... | collective-permute-start | bytes 1327112 | tf_op jit(solution)/shard_map/ppermute | solution.py:411
  27.3 12.6 %collective-permute-start.7 = (f32[864,128]{1,0:T(8,128)S(1)}, f32[864,128]{1,0:T(8,128)S(1)}, u32[]{:S(2)}, u32[]{:S(2)}) collective-permute-start(f32[864,128]{1,0:T(8,128)S(1)} %get-tuple-element.47), channel_id=1, source_target_pairs={{0,2},{1,3},{2,0},{3,1},{4,6},{5,7},{6,4},{7,5},{8,10},{9,11},{10,... | collective-permute-start | bytes 1327112 | tf_op jit(solution)/shard_map/ppermute | solution.py:409
  29.1 12.6 %copy-start.3 = (f32[256,512]{1,0:T(8,128)S(1)}, f32[256,512]{1,0:T(8,128)}, u32[]{:S(2)}) copy-start(f32[256,512]{1,0:T(8,128)} %constant.20.clone.real_forward_ref) | copy-start | bytes 1572868
  29.1 12.6 %copy-start.10 = (f32[96,288]{1,0:T(8,128)S(1)}, f32[96,288]{1,0:T(8,128)}, u32[]{:S(2)}) copy-start(f32[96,288]{1,0:T(8,128)} %constant.22.clone.stick_out_ref) | copy-start | bytes 331780
  39.9 1.8 %collective-permute-start.9 = (f32[864,128]{1,0:T(8,128)S(1)}, f32[864,128]{1,0:T(8,128)S(1)}, u32[]{:S(2)}, u32[]{:S(2)}) collective-permute-start(f32[864,128]{1,0:T(8,128)S(1)} %collective-permute-done.7.ahead_ref), channel_id=1, source_target_pairs={{0,1},{1,0},{2,3},{3,2},{4,5},{5,4},{6,7},{7,6},{8,9},{9,8},{10,11... | collective-permute-start | bytes 1327112 | tf_op jit(solution)/shard_map/ppermute | solution.py:419
  54.0 6.4 %collective-permute-start.10 = (f32[96,128]{1,0:T(8,128)S(1)}, f32[96,128]{1,0:T(8,128)S(1)}, u32[]{:S(2)}, u32[]{:S(2)}) collective-permute-start(f32[96,128]{1,0:T(8,128)S(1)} %get-tuple-element.52), channel_id=1, source_target_pairs={{0,4},{4,0},{8,12},{12,8},{16,20},{20,16},{24,28},{28,24},{1,5},{5... | collective-permute-start | bytes 147464 | tf_op jit(solution)/shard_map/ppermute | solution.py:366
  54.6 6.8 %collective-permute-start.11 = (f32[96,128]{1,0:T(8,128)S(1)}, f32[96,128]{1,0:T(8,128)S(1)}, u32[]{:S(2)}, u32[]{:S(2)}) collective-permute-start(f32[96,128]{1,0:T(8,128)S(1)} %get-tuple-element.53), channel_id=1, source_target_pairs={{0,8},{4,12},{8,0},{12,4},{16,24},{20,28},{24,16},{28,20},{1,9},{5... | collective-permute-start | bytes 147464 | tf_op jit(solution)/shard_map/ppermute | solution.py:366
  54.6 10.6 %collective-permute-start.12 = (f32[96,128]{1,0:T(8,128)S(1)}, f32[96,128]{1,0:T(8,128)S(1)}, u32[]{:S(2)}, u32[]{:S(2)}) collective-permute-start(f32[96,128]{1,0:T(8,128)S(1)} %get-tuple-element.54), channel_id=1, source_target_pairs={{0,12},{4,8},{8,4},{12,0},{16,28},{20,24},{24,20},{28,16},{1,13},{... | collective-permute-start | bytes 147464 | tf_op jit(solution)/shard_map/ppermute | solution.py:366
  57.6 7.7 %collective-permute-start.13 = (f32[96,128]{1,0:T(8,128)S(1)}, f32[96,128]{1,0:T(8,128)S(1)}, u32[]{:S(2)}, u32[]{:S(2)}) collective-permute-start(f32[96,128]{1,0:T(8,128)S(1)} %get-tuple-element.55), channel_id=1, source_target_pairs={{0,16},{4,20},{8,24},{12,28},{16,0},{20,4},{24,8},{28,12},{1,17},{... | collective-permute-start | bytes 147464 | tf_op jit(solution)/shard_map/ppermute | solution.py:366
  58.4 7.8 %collective-permute-start.14 = (f32[96,128]{1,0:T(8,128)S(1)}, f32[96,128]{1,0:T(8,128)S(1)}, u32[]{:S(2)}, u32[]{:S(2)}) collective-permute-start(f32[96,128]{1,0:T(8,128)S(1)} %get-tuple-element.56), channel_id=1, source_target_pairs={{0,20},{4,16},{8,28},{12,24},{16,4},{20,0},{24,12},{28,8},{1,21},{... | collective-permute-start | bytes 147464 | tf_op jit(solution)/shard_map/ppermute | solution.py:366
  60.4 5.9 %collective-permute-start.15 = (f32[96,128]{1,0:T(8,128)S(1)}, f32[96,128]{1,0:T(8,128)S(1)}, u32[]{:S(2)}, u32[]{:S(2)}) collective-permute-start(f32[96,128]{1,0:T(8,128)S(1)} %get-tuple-element.57), channel_id=1, source_target_pairs={{0,24},{4,28},{8,16},{12,20},{16,8},{20,12},{24,0},{28,4},{1,25},{... | collective-permute-start | bytes 147464 | tf_op jit(solution)/shard_map/ppermute | solution.py:366
  61.4 6.8 %collective-permute-start.16 = (f32[96,128]{1,0:T(8,128)S(1)}, f32[96,128]{1,0:T(8,128)S(1)}, u32[]{:S(2)}, u32[]{:S(2)}) collective-permute-start(f32[96,128]{1,0:T(8,128)S(1)} %get-tuple-element.58), channel_id=1, source_target_pairs={{0,28},{4,24},{8,20},{12,16},{16,12},{20,8},{24,4},{28,0},{1,29},{... | collective-permute-start | bytes 147464 | tf_op jit(solution)/shard_map/ppermute | solution.py:366
  (4 other events, 3.5 us)

commit v6 on v3

--- a/solution.py
+++ b/solution.py
@@ -126,8 +126,16 @@
     return dot(jnp.concatenate(high + low + high, 1), table)
 
 
+def pitch(g):
+    return g + 1
+
+
 def strided(ref, first, g):
-    return ref[pl.ds(first, g, stride=g), :]
+    return ref[pl.ds(first, g, stride=pitch(g)), :]
+
+
+def work_rows(index, g):
+    return pl.ds(index * pitch(g), g)
 
 
 def slab_rows(index, g, count=1):
@@ -213,7 +221,7 @@
         for k in range(0, 2 * PAIRS, 2):
             x = beside(placed[k * g : (k + 1) * g], placed[(k + 1) * g : (k + 2) * g])
             for j, slab in enumerate(halves(left_complex(backward, x))):
-                work_a[slab_rows(first + k + j, g), :] = slab
+                work_a[work_rows(first + k + j, g), :] = slab
 
     for pair in range(g // 2):
         x = beside(strided(work_a, pair, g), strided(work_a, pair + g // 2, g))
@@ -234,14 +242,14 @@
         spectrum = right([phi * first_ref[rows, :], phi * second_ref[rows, :]], z_forward)
         for k in range(PAIRS):
             slabs = halves(left_complex(forward, spectrum[k * g : (k + 1) * g]))
-            work_a[slab_rows(start + k, g), :] = slabs[0]
-            work_a[slab_rows(start + k + half, g), :] = slabs[1]
+            work_a[work_rows(start + k, g), :] = slabs[0]
+            work_a[work_rows(start + k + half, g), :] = slabs[1]
 
     for kx in range(0, g, 2):
         x = left_complex(forward, beside(strided(work_a, kx, g), strided(work_a, kx + 1, g)))
         x = left_complex(backward, x * beside(coulomb_ref[kx], coulomb_ref[kx + 1]))
         for j, slab in enumerate(halves(x)):
-            work_b[slab_rows(kx + j, g), :] = slab
+            work_b[work_rows(kx + j, g), :] = slab
 
     for start in range(0, half, PAIRS):
         slabs = [
@@ -291,8 +299,8 @@
             low = lane_halves(cos.shape)
             lower, upper = halves(jnp.where(low, cos, turned(sin))), halves(jnp.where(low, turned(cos), sin))
             for j in range(2):
-                work_a[slab_rows(start + k + j, g), :] = lower[j]
-                work_a[slab_rows(start + k + j + half, g), :] = upper[j]
+                work_a[work_rows(start + k + j, g), :] = lower[j]
+                work_a[work_rows(start + k + j + half, g), :] = upper[j]
 
     potentials(g, phi_ref, first_ref, second_ref, tables, work_a, work_b, emit)
 
@@ -345,7 +353,7 @@
     field = jax.ShapeDtypeStruct((rows // 2, LANES), F32)
     folded = jax.ShapeDtypeStruct((rows // 2 * FOLD // (FOLD + 1), LANES), F32)
     field_scratch = pltpu.VMEM((rows // 2, LANES), F32)
-    work = pltpu.VMEM((rows, LANES), F32)
+    work = pltpu.VMEM((g * pitch(g), LANES), F32)
     pot_flops = 6 * 2 * rows * 256 * 256
 
     sent = call(

time: 66.3 us -> 66 us (level)
  no operation moved by 1% of the time
where the time goes in v6:
time: 66 us; the launch traced here: 65.8 us
  starting transfers between devices  25.3 us (38%)
  Pallas kernels  21.2 us (32%)
  waiting for transfers between devices  15.7 us (24%)
  local copies, waits for them, and re-layouts  3.5 us (5%)
    ppermute x14, starting transfers between devices, exchanged(): lax.ppermute(blocks[d], 'stick', [(i, i ^ d) for i in range(owners)])  23.7 us
    pallas_call x6, Pallas kernels, call(): pl.pallas_call(kernel, out_shape=out_shapes, in_specs=[pl.BlockSpec(memor...  21.2 us
    ppermute x14, waiting for transfers between devices, exchanged(): lax.ppermute(blocks[d], 'stick', [(i, i ^ d) for i in range(owners)])  7.71 us
    ppermute x1, waiting for transfers between devices, fetched(): lax.ppermute(packed, 'band', [(i, (i - distance) % groups) for i in range...  5.97 us
    unnamed x20, local copies, waits for them, and re-layouts  3.5 us
    ppermute x1, waiting for transfers between devices, on_device(): first, second = (ahead, lax.ppermute(ahead, 'band', swap))  1.79 us
    ppermute x1, starting transfers between devices, fetched(): lax.ppermute(packed, 'band', [(i, (i - distance) % groups) for i in range...  1.55 us
  transfers between devices with their start and end apart: 17, of which 8 were waited for; matrix products, arithmetic and copies ran while one was open for 0% of the time, Pallas kernels for 7%

profile of v6, /device:TPU:0, one launch (start us, length us, event | category | flops | bytes accessed | tf_op | source)
XLA Modules:
  0.0 65.8 jit_solution(17697144476336680712)
XLA Ops:
  0.0 1.0 %copy-done = f32[8,96,128]{2,1,0:T(8,128)S(1)} copy-done((f32[8,96,128]{2,1,0:T(8,128)S(1)}, f32[8,96,128]{2,1,0:T(8,128)}, u32[]{:S(2)}) %copy-start) | copy-done | bytes 393240
  2.2 3.0 %collective-permute-start = (f32[104,128]{1,0:T(8,128)S(1)}, f32[104,128]{1,0:T(8,128)S(1)}, u32[]{:S(2)}, u32[]{:S(2)}) collective-permute-start(f32[104,128]{1,0:T(8,128)S(1)} %get-tuple-element.31), channel_id=1, source_target_pairs={{0,4},{4,0},{8,12},{12,8},{16,20},{20,16},{24,28},{28,24},{1,5},{5... | collective-permute-start | bytes 159752 | tf_op jit(solution)/shard_map/ppermute | solution.py:342
  5.3 1.6 %collective-permute-start.1 = (f32[104,128]{1,0:T(8,128)S(1)}, f32[104,128]{1,0:T(8,128)S(1)}, u32[]{:S(2)}, u32[]{:S(2)}) collective-permute-start(f32[104,128]{1,0:T(8,128)S(1)} %get-tuple-element.32), channel_id=1, source_target_pairs={{0,8},{4,12},{8,0},{12,4},{16,24},{20,28},{24,16},{28,20},{1,9},{5... | collective-permute-start | bytes 159752 | tf_op jit(solution)/shard_map/ppermute | solution.py:342
  6.9 3.0 %collective-permute-start.3 = (f32[104,128]{1,0:T(8,128)S(1)}, f32[104,128]{1,0:T(8,128)S(1)}, u32[]{:S(2)}, u32[]{:S(2)}) collective-permute-start(f32[104,128]{1,0:T(8,128)S(1)} %get-tuple-element.34), channel_id=1, source_target_pairs={{0,16},{4,20},{8,24},{12,28},{16,0},{20,4},{24,8},{28,12},{1,17},{... | collective-permute-start | bytes 159752 | tf_op jit(solution)/shard_map/ppermute | solution.py:342
  9.8 1.3 %collective-permute-start.4 = (f32[104,128]{1,0:T(8,128)S(1)}, f32[104,128]{1,0:T(8,128)S(1)}, u32[]{:S(2)}, u32[]{:S(2)}) collective-permute-start(f32[104,128]{1,0:T(8,128)S(1)} %get-tuple-element.35), channel_id=1, source_target_pairs={{0,20},{4,16},{8,28},{12,24},{16,4},{20,0},{24,12},{28,8},{1,21},{... | collective-permute-start | bytes 159752 | tf_op jit(solution)/shard_map/ppermute | solution.py:342
  11.1 3.6 %collective-permute-start.5 = (f32[104,128]{1,0:T(8,128)S(1)}, f32[104,128]{1,0:T(8,128)S(1)}, u32[]{:S(2)}, u32[]{:S(2)}) collective-permute-start(f32[104,128]{1,0:T(8,128)S(1)} %get-tuple-element.36), channel_id=1, source_target_pairs={{0,24},{4,28},{8,16},{12,20},{16,8},{20,12},{24,0},{28,4},{1,25},{... | collective-permute-start | bytes 159752 | tf_op jit(solution)/shard_map/ppermute | solution.py:342
  14.8 0.9 %copy-done.5 = f32[128,288]{1,0:T(8,128)S(1)} copy-done((f32[128,288]{1,0:T(8,128)S(1)}, f32[128,288]{1,0:T(8,128)}, u32[]{:S(2)}) %copy-start.5) | copy-done | bytes 147480
  15.7 0.9 %copy-done.7 = f32[96,144]{1,0:T(8,128)S(1)} copy-done((f32[96,144]{1,0:T(8,128)S(1)}, f32[96,144]{1,0:T(8,128)}, u32[]{:S(2)}) %copy-start.7) | copy-done | bytes 55320
  16.6 1.5 %collective-permute-done.4.refs_5_ = f32[104,128]{1,0:T(8,128)S(1)} collective-permute-done((f32[104,128]{1,0:T(8,128)S(1)}, f32[104,128]{1,0:T(8,128)S(1)}, u32[]{:S(2)}, u32[]{:S(2)}) %collective-permute-start.4) | collective-permute-done | bytes 53280 | tf_op jit(solution)/shard_map/ppermute | solution.py:342
  18.1 3.5 %collective-permute-done.6.refs_7_ = f32[104,128]{1,0:T(8,128)S(1)} collective-permute-done((f32[104,128]{1,0:T(8,128)S(1)}, f32[104,128]{1,0:T(8,128)S(1)}, u32[]{:S(2)}, u32[]{:S(2)}) %collective-permute-start.6) | collective-permute-done | bytes 53280 | tf_op jit(solution)/shard_map/ppermute | solution.py:342
  21.6 4.6 %shard_map.93 = (f32[1152,128]{1,0:T(8,128)S(1)}, f32[864,128]{1,0:T(8,128)S(1)}, s32[8,1024]{1,0:T(8,128)S(1)}) custom-call(f32[104,128]{1,0:T(8,128)S(1)} %get-tuple-element.30.refs_0_, f32[104,128]{1,0:T(8,128)S(1)} %collective-permute-done.refs_1_, f32[104,128]{1,0:T(8,128)S(1)} %collective-permute-done.1.refs_2_, ...), custom_call_target="tpu_custom_call" | custom-call | flops 1000000000 | bytes 527360 | tf_op jit(solution)/shard_map/pallas_call | solution.py:327
  26.3 1.6 %collective-permute-start.7 = (f32[864,128]{1,0:T(8,128)S(1)}, f32[864,128]{1,0:T(8,128)S(1)}, u32[]{:S(2)}, u32[]{:S(2)}) collective-permute-start(f32[864,128]{1,0:T(8,128)S(1)} %get-tuple-element.43), channel_id=1, source_target_pairs={{0,2},{1,3},{2,0},{3,1},{4,6},{5,7},{6,4},{7,5},{8,10},{9,11},{10,... | collective-permute-start | bytes 1327112 | tf_op jit(solution)/shard_map/ppermute | solution.py:385
  28.1 4.8 %shard_map.94.before_ref = f32[1152,128]{1,0:T(8,128)S(1)} custom-call(f32[1152,128]{1,0:T(8,128)S(1)} %get-tuple-element.42.phi_ref, f32[864,128]{1,0:T(8,128)S(1)} %collective-permute-done.8.near_ref, f32[96,144]{1,0:T(8,128)S(1)} %copy-done.9, f32[96,144]{1,0:T(8,128)S(1)} %copy-done.8, f32[768,256]{1,0:T(8,128)S(1)} %copy-done.4, ...), custom_call_target="tpu_custom_call" | custom-call | flops 1811939328 | bytes 3895296 | tf_op jit(solution)/shard_map/pallas_call | solution.py:327
  32.9 6.0 %collective-permute-done.7.ahead_ref = f32[864,128]{1,0:T(8,128)S(1)} collective-permute-done((f32[864,128]{1,0:T(8,128)S(1)}, f32[864,128]{1,0:T(8,128)S(1)}, u32[]{:S(2)}, u32[]{:S(2)}) %collective-permute-start.7) | collective-permute-done | bytes 442400 | tf_op jit(solution)/shard_map/ppermute | solution.py:385
  38.9 1.8 %collective-permute-done.9.across_ref = f32[864,128]{1,0:T(8,128)S(1)} collective-permute-done((f32[864,128]{1,0:T(8,128)S(1)}, f32[864,128]{1,0:T(8,128)S(1)}, u32[]{:S(2)}, u32[]{:S(2)}) %collective-permute-start.9) | collective-permute-done | bytes 442400 | tf_op jit(solution)/shard_map/ppermute | solution.py:395
  40.7 10.4 %shard_map.95 = (f32[96,128]{1,0:T(8,128)S(1)}, f32[96,128]{1,0:T(8,128)S(1)}, f32[96,128]{1,0:T(8,128)S(1)}, f32[96,128]{1,0:T(8,128)S(1)}, f32[96,128]{1,0:T(8...) custom-call(f32[1152,128]{1,0:T(8,128)S(1)} %get-tuple-element.42.phi_ref, ...), custom_call_target="tpu_custom_call" | custom-call | flops 1811939328 | bytes 5070848 | tf_op jit(solution)/shard_map/pallas_call | solution.py:327
  51.6 3.0 %collective-permute-start.12 = (f32[96,128]{1,0:T(8,128)S(1)}, f32[96,128]{1,0:T(8,128)S(1)}, u32[]{:S(2)}, u32[]{:S(2)}) collective-permute-start(f32[96,128]{1,0:T(8,128)S(1)} %get-tuple-element.50), channel_id=1, source_target_pairs={{0,12},{4,8},{8,4},{12,0},{16,28},{20,24},{24,20},{28,16},{1,13},{... | collective-permute-start | bytes 147464 | tf_op jit(solution)/shard_map/ppermute | solution.py:342
  54.6 0.8 %collective-permute-start.13 = (f32[96,128]{1,0:T(8,128)S(1)}, f32[96,128]{1,0:T(8,128)S(1)}, u32[]{:S(2)}, u32[]{:S(2)}) collective-permute-start(f32[96,128]{1,0:T(8,128)S(1)} %get-tuple-element.51), channel_id=1, source_target_pairs={{0,16},{4,20},{8,24},{12,28},{16,0},{20,4},{24,8},{28,12},{1,17},{... | collective-permute-start | bytes 147464 | tf_op jit(solution)/shard_map/ppermute | solution.py:342
  55.5 2.0 %collective-permute-start.14 = (f32[96,128]{1,0:T(8,128)S(1)}, f32[96,128]{1,0:T(8,128)S(1)}, u32[]{:S(2)}, u32[]{:S(2)}) collective-permute-start(f32[96,128]{1,0:T(8,128)S(1)} %get-tuple-element.52), channel_id=1, source_target_pairs={{0,20},{4,16},{8,28},{12,24},{16,4},{20,0},{24,12},{28,8},{1,21},{... | collective-permute-start | bytes 147464 | tf_op jit(solution)/shard_map/ppermute | solution.py:342
  57.5 0.7 %collective-permute-start.15 = (f32[96,128]{1,0:T(8,128)S(1)}, f32[96,128]{1,0:T(8,128)S(1)}, u32[]{:S(2)}, u32[]{:S(2)}) collective-permute-start(f32[96,128]{1,0:T(8,128)S(1)} %get-tuple-element.53), channel_id=1, source_target_pairs={{0,24},{4,28},{8,16},{12,20},{16,8},{20,12},{24,0},{28,4},{1,25},{... | collective-permute-start | bytes 147464 | tf_op jit(solution)/shard_map/ppermute | solution.py:342
  58.2 4.0 %collective-permute-start.16 = (f32[96,128]{1,0:T(8,128)S(1)}, f32[96,128]{1,0:T(8,128)S(1)}, u32[]{:S(2)}, u32[]{:S(2)}) collective-permute-start(f32[96,128]{1,0:T(8,128)S(1)} %get-tuple-element.54), channel_id=1, source_target_pairs={{0,28},{4,24},{8,20},{12,16},{16,12},{20,8},{24,4},{28,0},{1,29},{... | collective-permute-start | bytes 147464 | tf_op jit(solution)/shard_map/ppermute | solution.py:342
  62.3 1.0 %collective-permute-done.14.refs_5_ = f32[96,128]{1,0:T(8,128)S(1)} collective-permute-done((f32[96,128]{1,0:T(8,128)S(1)}, f32[96,128]{1,0:T(8,128)S(1)}, u32[]{:S(2)}, u32[]{:S(2)}) %collective-permute-start.14) | collective-permute-done | bytes 49184 | tf_op jit(solution)/shard_map/ppermute | solution.py:342
  63.4 1.6 %collective-permute-done.16.refs_7_ = f32[96,128]{1,0:T(8,128)S(1)} collective-permute-done((f32[96,128]{1,0:T(8,128)S(1)}, f32[96,128]{1,0:T(8,128)S(1)}, u32[]{:S(2)}, u32[]{:S(2)}) %collective-permute-start.16) | collective-permute-done | bytes 49184 | tf_op jit(solution)/shard_map/ppermute | solution.py:342
  65.0 0.8 %shard_map.96 = f32[8,96,128]{2,1,0:T(8,128)} custom-call(f32[96,128]{1,0:T(8,128)S(1)} %get-tuple-element.47.refs_0_, f32[96,128]{1,0:T(8,128)S(1)} %collective-permute-done.10.refs_1_, f32[96,128]{1,0:T(8,128)S(1)} %collective-permute-done.11.refs_2_, f32[96,128]{1,0:T(8,128)S(1)} %collective-permute-done.12.refs_3_, ...), custom_call_target="tpu_custom_call" | custom-call | flops 1000000 | bytes 393216 | tf_op jit(solution)/shard_map/pallas_call | solution.py:327
  (36 shorter events, 2.4 us)
Async XLA Ops:
  0.0 1.0 %copy-start = (f32[8,96,128]{2,1,0:T(8,128)S(1)}, f32[8,96,128]{2,1,0:T(8,128)}, u32[]{:S(2)}) copy-start(f32[8,96,128]{2,1,0:T(8,128)} %sticks_ref.1) | copy-start | bytes 1179652
  2.2 8.9 %collective-permute-start = (f32[104,128]{1,0:T(8,128)S(1)}, f32[104,128]{1,0:T(8,128)S(1)}, u32[]{:S(2)}, u32[]{:S(2)}) collective-permute-start(f32[104,128]{1,0:T(8,128)S(1)} %get-tuple-element.31), channel_id=1, source_target_pairs={{0,4},{4,0},{8,12},{12,8},{16,20},{20,16},{24,28},{28,24},{1,5},{5... | collective-permute-start | bytes 159752 | tf_op jit(solution)/shard_map/ppermute | solution.py:342
  5.3 9.5 %collective-permute-start.1 = (f32[104,128]{1,0:T(8,128)S(1)}, f32[104,128]{1,0:T(8,128)S(1)}, u32[]{:S(2)}, u32[]{:S(2)}) collective-permute-start(f32[104,128]{1,0:T(8,128)S(1)} %get-tuple-element.32), channel_id=1, source_target_pairs={{0,8},{4,12},{8,0},{12,4},{16,24},{20,28},{24,16},{28,20},{1,9},{5... | collective-permute-start | bytes 159752 | tf_op jit(solution)/shard_map/ppermute | solution.py:342
  6.9 9.7 %collective-permute-start.2 = (f32[104,128]{1,0:T(8,128)S(1)}, f32[104,128]{1,0:T(8,128)S(1)}, u32[]{:S(2)}, u32[]{:S(2)}) collective-permute-start(f32[104,128]{1,0:T(8,128)S(1)} %get-tuple-element.33), channel_id=1, source_target_pairs={{0,12},{4,8},{8,4},{12,0},{16,28},{20,24},{24,20},{28,16},{1,13},{... | collective-permute-start | bytes 159752 | tf_op jit(solution)/shard_map/ppermute | solution.py:342
  6.9 9.7 %collective-permute-start.3 = (f32[104,128]{1,0:T(8,128)S(1)}, f32[104,128]{1,0:T(8,128)S(1)}, u32[]{:S(2)}, u32[]{:S(2)}) collective-permute-start(f32[104,128]{1,0:T(8,128)S(1)} %get-tuple-element.34), channel_id=1, source_target_pairs={{0,16},{4,20},{8,24},{12,28},{16,0},{20,4},{24,8},{28,12},{1,17},{... | collective-permute-start | bytes 159752 | tf_op jit(solution)/shard_map/ppermute | solution.py:342
  9.8 8.2 %collective-permute-start.4 = (f32[104,128]{1,0:T(8,128)S(1)}, f32[104,128]{1,0:T(8,128)S(1)}, u32[]{:S(2)}, u32[]{:S(2)}) collective-permute-start(f32[104,128]{1,0:T(8,128)S(1)} %get-tuple-element.35), channel_id=1, source_target_pairs={{0,20},{4,16},{8,28},{12,24},{16,4},{20,0},{24,12},{28,8},{1,21},{... | collective-permute-start | bytes 159752 | tf_op jit(solution)/shard_map/ppermute | solution.py:342
  11.1 6.9 %collective-permute-start.5 = (f32[104,128]{1,0:T(8,128)S(1)}, f32[104,128]{1,0:T(8,128)S(1)}, u32[]{:S(2)}, u32[]{:S(2)}) collective-permute-start(f32[104,128]{1,0:T(8,128)S(1)} %get-tuple-element.36), channel_id=1, source_target_pairs={{0,24},{4,28},{8,16},{12,20},{16,8},{20,12},{24,0},{28,4},{1,25},{... | collective-permute-start | bytes 159752 | tf_op jit(solution)/shard_map/ppermute | solution.py:342
  14.7 6.8 %collective-permute-start.6 = (f32[104,128]{1,0:T(8,128)S(1)}, f32[104,128]{1,0:T(8,128)S(1)}, u32[]{:S(2)}, u32[]{:S(2)}) collective-permute-start(f32[104,128]{1,0:T(8,128)S(1)} %get-tuple-element.37), channel_id=1, source_target_pairs={{0,28},{4,24},{8,20},{12,16},{16,12},{20,8},{24,4},{28,0},{1,29},{... | collective-permute-start | bytes 159752 | tf_op jit(solution)/shard_map/ppermute | solution.py:342
  21.6 6.5 %copy-start.2 = (f32[48,48,128]{2,1,0:T(8,128)S(1)}, f32[48,48,128]{2,1,0:T(8,128)}, u32[]{:S(2)}) copy-start(f32[48,48,128]{2,1,0:T(8,128)} %constant.20.clone.refs_4_) | copy-start | bytes 3538948
  21.6 6.5 %copy-start.3 = (f32[768,256]{1,0:T(8,128)S(1)}, f32[768,256]{1,0:T(8,128)}, u32[]{:S(2)}) copy-start(f32[768,256]{1,0:T(8,128)} %constant.17.clone.refs_3_) | copy-start | bytes 2359300
  21.6 6.5 %copy-start.4 = (f32[768,256]{1,0:T(8,128)S(1)}, f32[768,256]{1,0:T(8,128)}, u32[]{:S(2)}) copy-start(f32[768,256]{1,0:T(8,128)} %constant.16.clone.refs_2_) | copy-start | bytes 2359300
  21.6 6.5 %copy-start.8 = (f32[96,144]{1,0:T(8,128)S(1)}, f32[96,144]{1,0:T(8,128)}, u32[]{:S(2)}) copy-start(f32[96,144]{1,0:T(8,128)} %constant.15.clone.refs_1_) | copy-start | bytes 165892
  21.6 6.5 %copy-start.9 = (f32[96,144]{1,0:T(8,128)S(1)}, f32[96,144]{1,0:T(8,128)}, u32[]{:S(2)}) copy-start(f32[96,144]{1,0:T(8,128)} %constant.14.clone.refs_0_) | copy-start | bytes 165892
  26.2 1.9 %collective-permute-start.8 = (f32[864,128]{1,0:T(8,128)S(1)}, f32[864,128]{1,0:T(8,128)S(1)}, u32[]{:S(2)}, u32[]{:S(2)}) collective-permute-start(f32[864,128]{1,0:T(8,128)S(1)} %get-tuple-element.43), channel_id=1, source_target_pairs={{0,1},{1,0},{2,3},{3,2},{4,5},{5,4},{6,7},{7,6},{8,9},{9,8},{10,11... | collective-permute-start | bytes 1327112 | tf_op jit(solution)/shard_map/ppermute | solution.py:387
  26.3 12.6 %collective-permute-start.7 = (f32[864,128]{1,0:T(8,128)S(1)}, f32[864,128]{1,0:T(8,128)S(1)}, u32[]{:S(2)}, u32[]{:S(2)}) collective-permute-start(f32[864,128]{1,0:T(8,128)S(1)} %get-tuple-element.43), channel_id=1, source_target_pairs={{0,2},{1,3},{2,0},{3,1},{4,6},{5,7},{6,4},{7,5},{8,10},{9,11},{10,... | collective-permute-start | bytes 1327112 | tf_op jit(solution)/shard_map/ppermute | solution.py:385
  28.1 12.6 %copy-start.6 = (f32[96,288]{1,0:T(8,128)S(1)}, f32[96,288]{1,0:T(8,128)}, u32[]{:S(2)}) copy-start(f32[96,288]{1,0:T(8,128)} %constant.19.clone.stick_out_ref) | copy-start | bytes 331780
  38.9 1.8 %collective-permute-start.9 = (f32[864,128]{1,0:T(8,128)S(1)}, f32[864,128]{1,0:T(8,128)S(1)}, u32[]{:S(2)}, u32[]{:S(2)}) collective-permute-start(f32[864,128]{1,0:T(8,128)S(1)} %collective-permute-done.7.ahead_ref), channel_id=1, source_target_pairs={{0,1},{1,0},{2,3},{3,2},{4,5},{5,4},{6,7},{7,6},{8,9},{9,8},{10,11... | collective-permute-start | bytes 1327112 | tf_op jit(solution)/shard_map/ppermute | solution.py:395
  51.1 6.4 %collective-permute-start.10 = (f32[96,128]{1,0:T(8,128)S(1)}, f32[96,128]{1,0:T(8,128)S(1)}, u32[]{:S(2)}, u32[]{:S(2)}) collective-permute-start(f32[96,128]{1,0:T(8,128)S(1)} %get-tuple-element.48), channel_id=1, source_target_pairs={{0,4},{4,0},{8,12},{12,8},{16,20},{20,16},{24,28},{28,24},{1,5},{5... | collective-permute-start | bytes 147464 | tf_op jit(solution)/shard_map/ppermute | solution.py:342
  51.6 6.6 %collective-permute-start.11 = (f32[96,128]{1,0:T(8,128)S(1)}, f32[96,128]{1,0:T(8,128)S(1)}, u32[]{:S(2)}, u32[]{:S(2)}) collective-permute-start(f32[96,128]{1,0:T(8,128)S(1)} %get-tuple-element.49), channel_id=1, source_target_pairs={{0,8},{4,12},{8,0},{12,4},{16,24},{20,28},{24,16},{28,20},{1,9},{5... | collective-permute-start | bytes 147464 | tf_op jit(solution)/shard_map/ppermute | solution.py:342
  51.6 10.6 %collective-permute-start.12 = (f32[96,128]{1,0:T(8,128)S(1)}, f32[96,128]{1,0:T(8,128)S(1)}, u32[]{:S(2)}, u32[]{:S(2)}) collective-permute-start(f32[96,128]{1,0:T(8,128)S(1)} %get-tuple-element.50), channel_id=1, source_target_pairs={{0,12},{4,8},{8,4},{12,0},{16,28},{20,24},{24,20},{28,16},{1,13},{... | collective-permute-start | bytes 147464 | tf_op jit(solution)/shard_map/ppermute | solution.py:342
  54.6 7.7 %collective-permute-start.13 = (f32[96,128]{1,0:T(8,128)S(1)}, f32[96,128]{1,0:T(8,128)S(1)}, u32[]{:S(2)}, u32[]{:S(2)}) collective-permute-start(f32[96,128]{1,0:T(8,128)S(1)} %get-tuple-element.51), channel_id=1, source_target_pairs={{0,16},{4,20},{8,24},{12,28},{16,0},{20,4},{24,8},{28,12},{1,17},{... | collective-permute-start | bytes 147464 | tf_op jit(solution)/shard_map/ppermute | solution.py:342
  55.5 7.8 %collective-permute-start.14 = (f32[96,128]{1,0:T(8,128)S(1)}, f32[96,128]{1,0:T(8,128)S(1)}, u32[]{:S(2)}, u32[]{:S(2)}) collective-permute-start(f32[96,128]{1,0:T(8,128)S(1)} %get-tuple-element.52), channel_id=1, source_target_pairs={{0,20},{4,16},{8,28},{12,24},{16,4},{20,0},{24,12},{28,8},{1,21},{... | collective-permute-start | bytes 147464 | tf_op jit(solution)/shard_map/ppermute | solution.py:342
  57.5 5.9 %collective-permute-start.15 = (f32[96,128]{1,0:T(8,128)S(1)}, f32[96,128]{1,0:T(8,128)S(1)}, u32[]{:S(2)}, u32[]{:S(2)}) collective-permute-start(f32[96,128]{1,0:T(8,128)S(1)} %get-tuple-element.53), channel_id=1, source_target_pairs={{0,24},{4,28},{8,16},{12,20},{16,8},{20,12},{24,0},{28,4},{1,25},{... | collective-permute-start | bytes 147464 | tf_op jit(solution)/shard_map/ppermute | solution.py:342
  58.2 6.8 %collective-permute-start.16 = (f32[96,128]{1,0:T(8,128)S(1)}, f32[96,128]{1,0:T(8,128)S(1)}, u32[]{:S(2)}, u32[]{:S(2)}) collective-permute-start(f32[96,128]{1,0:T(8,128)S(1)} %get-tuple-element.54), channel_id=1, source_target_pairs={{0,28},{4,24},{8,20},{12,16},{16,12},{20,8},{24,4},{28,0},{1,29},{... | collective-permute-start | bytes 147464 | tf_op jit(solution)/shard_map/ppermute | solution.py:342
  (3 other events, 2.5 us)

commit v7 on v5

--- a/solution.py
+++ b/solution.py
@@ -13,7 +13,7 @@
 BOX_LENGTH = 18.0
 LANES = 128
 MID = 64
-PAIRS = 4
+PAIRS = 6
 FOLD = 3
 
 F32 = jnp.float32
@@ -41,20 +41,16 @@
     c, s = np.cos(angle), np.sin(angle)
     lower, upper = slice(0, g), slice(MID, MID + g)
 
-    forward, backward, real_back = np.zeros((3, LANES, LANES))
+    forward, backward = np.zeros((2, LANES, LANES))
     forward[lower, lower], forward[lower, upper] = c, -s
     forward[upper, lower], forward[upper, upper] = s, c
     backward[lower, lower], backward[lower, upper] = c, s
     backward[upper, lower], backward[upper, upper] = -s, c
-    for half in (lower, upper):
-        real_back[:, half] = backward[:, lower]
     real_forward = np.zeros((LANES, 2 * LANES))
     real_forward[lower, :LANES] = forward[lower]
     real_forward[upper, LANES:] = forward[lower]
 
-    stick_in = np.zeros((LANES, 2 * g))
-    stick_in[lower, :g], stick_in[lower, g:] = c, -s
-    stick_in[upper, :g], stick_in[upper, g:] = s, c
+    stick_in = np.block([[c, -s], [s, c]])
     stick_out = np.block([[c, s], [-s, c]]) * g**-1.5
 
     freq = np.arange(g)
@@ -69,7 +65,8 @@
         forward=down(forward),
         backward=down(backward),
         last_backward=down(backward / g**3),
-        real_back=down(real_back),
+        left_forward=across(np.concatenate([c, -s], 0)),
+        left_backward=across(np.concatenate([c, s], 0)),
         real_forward=down(real_forward),
         stick_in=across(stick_in),
         stick_out=across(stick_out),
@@ -121,6 +118,22 @@
 
 def beside(a, b):
     return jnp.concatenate([a, b], 1)
+
+
+def halves(x):
+    return x[:, :LANES], x[:, LANES:]
+
+
+def left(table, x):
+    both = dot(table, stacked(x))
+    g = both.shape[0] // 2
+    return both[:g], both[g:]
+
+
+def left_complex(table, a, b):
+    cos, sin = left(table, beside(a, b))
+    sign = jnp.where(lane_halves((1, LANES)), -1.0, 1.0)
+    return [p + turned(q) * sign for p, q in zip(halves(cos), halves(sin))]
 
 
 def right(x, table):
@@ -190,14 +203,19 @@
 def folded_position(columns, g):
     kx = lax.div(columns, g)
     ky = columns - kx * g
-    group, member = lax.div(kx, 2 * FOLD + 2), lax.rem(kx, 2 * FOLD + 2)
+    group, member = lax.div(ky, 2 * FOLD + 2), lax.rem(ky, 2 * FOLD + 2)
     pair, half = lax.div(member, 2), lax.rem(member, 2)
     width = g // FOLD
-    piece = lax.div(ky, width)
+    piece = lax.div(kx, width)
     last = pair == FOLD
     row = group * FOLD + jnp.where(last, piece, pair)
-    lane = half * MID + jnp.where(last, g + ky - piece * width, ky)
+    lane = half * MID + jnp.where(last, g + kx - piece * width, kx)
     return jnp.where(columns < 0, -1, row * LANES + lane)
+
+
+def paired_position(columns, g):
+    kx = lax.div(columns, g)
+    return jnp.where(columns < 0, -1, lax.div(kx, 2) * LANES + lax.rem(kx, 2) * MID + columns - kx * g)
 
 
 def fold(field_ref, folded_ref, g):
@@ -227,64 +245,74 @@
 
 def field_kernel(g, count, *refs):
     received = refs[:count]
-    stick_in_ref, backward_ref, real_back_ref, phi_ref, folded_ref, positions_ref, work_a = refs[count:]
+    stick_in_ref, backward_ref, left_ref, phi_ref, folded_ref, positions_ref, work_a = refs[count:]
     columns = jnp.concatenate([ref[2 * g : 2 * g + 1, :] for ref in received], 1).astype(jnp.int32)
     positions_ref[...] = jnp.broadcast_to(folded_position(columns, g), positions_ref.shape)
-    stick_in, backward, real_back = stick_in_ref[...], backward_ref[...], real_back_ref[...]
-    pieces = []
+    stick_in, backward, left_backward = stick_in_ref[...], backward_ref[...], left_ref[...]
+    sticks, rows = [], []
     for k in range(0, count, 2):
         block = beside(received[k][: 2 * g, :], received[k + 1][: 2 * g, :])
-        pieces.append(beside(*split(dot(stick_in, stacked(block)).T)))
-    sticks = jnp.concatenate(pieces, 0)
-
-    step = g // 4
+        sticks.append(jnp.concatenate(split(dot(stick_in, stacked(block))), 0))
+        for ref in received[k : k + 2]:
+            ids = paired_position(ref[2 * g : 2 * g + 8, :].astype(jnp.int32), g).astype(F32)
+            ids = jnp.concatenate([ids] * (LANES // 8), 0).T
+            rows.append(jnp.concatenate([ids, ids], 1).astype(jnp.int32).astype(jnp.int16))
+    sticks = jnp.concatenate(sticks, 1)
+    rows = jnp.concatenate(rows, 0)
+
+    lane = lax.broadcasted_iota(jnp.int16, rows.shape, 1)
+    step = 2 * PAIRS
     for first in range(0, g, step):
-        both = dot(one_hot(columns, first * g, step * g), sticks)
-        placed = both[:, :LANES] + both[:, LANES:]
-        slabs = pairwise(transposed, [placed[k * g : (k + 1) * g] for k in range(step)])
+        slabs = []
+        for kx in range(first, first + step, 4):
+            start = jnp.asarray(kx // 2 * LANES, jnp.int16)
+            hot = jnp.where(rows == lane + start, jnp.asarray(1, BF16), jnp.asarray(0, BF16))
+            both = dot(sticks, hot)
+            placed = both[: 2 * g] + both[2 * g :]
+            for part in halves(placed):
+                slabs += regrouped(part[:g], part[g:])
         store(work_a, first, right_slabs(slabs, backward))
 
     half = g // 2
-    for start in range(0, half, PAIRS):
-        slabs = []
-        for z in range(start, start + PAIRS):
-            slabs += transposed(strided(work_a, z, g), strided(work_a, z + half, g))
-        slabs = right_slabs(slabs, real_back)
-        low = lane_halves(slabs[0].shape)
-        store(phi_ref, start, pairwise(lambda a, b: [jnp.where(low, a, b)], slabs))
+    for z in range(half):
+        x = beside(strided(work_a, z, g), strided(work_a, z + half, g))
+        (cos, cos_up), (sin, sin_up) = map(halves, left(left_backward, x))
+        low = lane_halves(cos.shape)
+        store(phi_ref, z, [jnp.where(low, cos - turned(sin), turned(cos_up) - sin_up)])
     fold(phi_ref, folded_ref, g)
 
 
 def potentials(g, phi_ref, first_ref, second_ref, tables, work_a, work_b, emit):
-    forward, backward, last_backward = [ref[...].astype(BF16) for ref in tables[:3]]
-    coulomb_ref = tables[3]
+    forward, last_backward, left_forward, left_backward = [ref[...].astype(BF16) for ref in tables[:4]]
+    coulomb_ref = tables[4]
     half = g // 2
     for start in range(0, half, PAIRS):
         rows = slab_rows(start, g, PAIRS)
         phi = phi_ref[rows, :]
         lower, upper = regrouped(phi * first_ref[rows, :], phi * second_ref[rows, :])
         spectrum = right(jnp.concatenate([lower, upper], 0), forward)
-        slabs = pairwise(transposed, [spectrum[k * g : (k + 1) * g] for k in range(2 * PAIRS)])
-        slabs = right_slabs(slabs, forward)
-        store(work_a, start, slabs[:PAIRS])
-        store(work_a, start + half, slabs[PAIRS:])
-
-    for first in range(0, g, 2 * PAIRS):
-        slabs = pairwise(transposed, [strided(work_a, first + k, g) for k in range(2 * PAIRS)])
-        spectrum = right(jnp.concatenate(slabs, 0), forward) * coulomb_ref[slab_rows(first, g, 2 * PAIRS), :]
-        spectrum = right(spectrum, backward)
-        slabs = pairwise(transposed, [spectrum[k * g : (k + 1) * g] for k in range(2 * PAIRS)])
-        store(work_b, first, right_slabs(slabs, backward))
+        for k in range(PAIRS):
+            a, b = left_complex(left_forward, *(spectrum[j * g : (j + 1) * g] for j in (k, k + PAIRS)))
+            store(work_a, start + k, [a])
+            store(work_a, start + k + half, [b])
+
+    for kx in range(0, g, 2):
+        slabs = left_complex(left_forward, strided(work_a, kx, g), strided(work_a, kx + 1, g))
+        slabs = [slab * coulomb_ref[slab_rows(kx + j, g), :] for j, slab in enumerate(slabs)]
+        store(work_b, kx, left_complex(left_backward, *slabs))
 
     for start in range(0, half, PAIRS):
-        slabs = [strided(work_b, start + k, g) for k in range(PAIRS)]
-        slabs += [strided(work_b, start + k + half, g) for k in range(PAIRS)]
-        out = right(jnp.concatenate(pairwise(transposed, slabs), 0), last_backward)
+        lower, upper = [], []
+        for z in range(start, start + PAIRS):
+            a, b = left_complex(left_backward, strided(work_b, z, g), strided(work_b, z + half, g))
+            lower.append(a)
+            upper.append(b)
+        out = right(jnp.concatenate(lower + upper, 0), last_backward)
         emit(start, *regrouped(out[: PAIRS * g], out[PAIRS * g :]))
 
 
 def near_kernel(g, phi_ref, near_ref, *refs):
-    tables, (sum_ref, other_ref, work_a, work_b) = refs[:4], refs[4:]
+    tables, (sum_ref, other_ref, work_a, work_b) = refs[:5], refs[5:]
     unfold(near_ref, other_ref, g)
 
     def emit(start, own, other):
@@ -295,7 +323,7 @@
 
 
 def middle_kernel(g, phi_ref, ahead_ref, behind_ref, before_ref, *refs):
-    tables, (sum_ref, first_ref, second_ref, work_a, work_b) = refs[:4], refs[4:]
+    tables, (sum_ref, first_ref, second_ref, work_a, work_b) = refs[:5], refs[5:]
     unfold(ahead_ref, first_ref, g)
     unfold(behind_ref, second_ref, g)
 
@@ -307,7 +335,7 @@
 
 
 def far_kernel(g, weights, phi_ref, ahead_ref, across_ref, before_ref, positions_ref, stick_out_ref, real_forward_ref, *refs):
-    tables, out_refs = refs[:4], refs[4:-5]
+    tables, out_refs = refs[:5], refs[5:-5]
     first_ref, second_ref, work_a, work_b, parts_ref = refs[-5:]
     unfold(ahead_ref, first_ref, g)
     unfold(across_ref, second_ref, g)
@@ -331,8 +359,8 @@
     width = FOLD * LANES
     for group in range(g // many):
         parts = []
-        for kx in range(group * many, (group + 1) * many, 2):
-            parts.append(jnp.concatenate(regrouped(strided(work_a, kx, g), strided(work_a, kx + 1, g)), 0))
+        for ky in range(group * many, (group + 1) * many, 2):
+            parts.append(jnp.concatenate(regrouped(strided(work_a, ky, g), strided(work_a, ky + 1, g)), 0))
         line = jnp.concatenate(folded_parts(parts, g), 1)
         parts_ref[:, group * width : (group + 1) * width] = jnp.concatenate(split(line), 0)
 
@@ -390,7 +418,7 @@
         space=pltpu.HBM,
     )
     received = exchanged(sent)
-    first_tables = lax.optimization_barrier((t["stick_in"], t["backward"], t["real_back"], sent[0]))[:3]
+    first_tables = lax.optimization_barrier((t["stick_in"], t["backward"], t["left_backward"], sent[0]))[:3]
     first_tables = call(
         table_kernel, [jax.ShapeDtypeStruct(x.shape, BF16) for x in first_tables], [], 10**9, *first_tables
     )
@@ -402,7 +430,7 @@
         *received,
         *first_tables,
     )
-    pot_tables = [t["forward"], t["backward"], t["last_backward"], t["coulomb"]]
+    pot_tables = [t["forward"], t["last_backward"], t["left_forward"], t["left_backward"], t["coulomb"]]
     swap = [(i, i ^ 1) for i in range(groups)]
 
     def fetched(distance):

time: 69.2 us -> 64.6 us (0.934)
  Pallas kernels: 29.7 us -> 18.4 us
  waiting for transfers between devices: 9.24 us -> 16 us
    pallas_call x6, Pallas kernels: 29.7 us -> 18.4 us  [call(): pl.pallas_call(kernel, out_shape=out_shapes, in_specs=[pl.BlockSpec(memor...]
    ppermute x1, waiting for transfers between devices: 0.37 us -> 7.13 us  [fetched(): lax.ppermute(packed, 'band', [(i, (i - distance) % groups) for i in range...]
    unnamed x22 -> x24, local copies, waits for them, and re-layouts: 4.5 us -> 4.44 us
  transfers between devices with their start and end apart: 17 -> 17, of which waited for: 8 -> 8; matrix products, arithmetic and copies ran while one was open for 0% -> 0% of each run, Pallas kernels for 15% -> 6%
where the time goes in v7:
time: 64.6 us; the launch traced here: 64.3 us
  starting transfers between devices  25.3 us (39%)
  Pallas kernels  18.4 us (28%)
  waiting for transfers between devices  16 us (25%)
  local copies, waits for them, and re-layouts  4.44 us (7%)
    ppermute x14, starting transfers between devices, exchanged(): lax.ppermute(blocks[d], 'stick', [(i, i ^ d) for i in range(owners)])  23.7 us
    pallas_call x6, Pallas kernels, call(): pl.pallas_call(kernel, out_shape=out_shapes, in_specs=[pl.BlockSpec(memor...  18.4 us
    ppermute x1, waiting for transfers between devices, fetched(): lax.ppermute(packed, 'band', [(i, (i - distance) % groups) for i in range...  7.13 us
    ppermute x14, waiting for transfers between devices, exchanged(): lax.ppermute(blocks[d], 'stick', [(i, i ^ d) for i in range(owners)])  6.86 us
    unnamed x24, local copies, waits for them, and re-layouts  4.44 us
    ppermute x1, waiting for transfers between devices, on_device(): first, second = (ahead, lax.ppermute(ahead, 'band', swap))  1.79 us
    ppermute x1, starting transfers between devices, fetched(): lax.ppermute(packed, 'band', [(i, (i - distance) % groups) for i in range...  1.56 us
  transfers between devices with their start and end apart: 17, of which 8 were waited for; matrix products, arithmetic and copies ran while one was open for 0% of the time, Pallas kernels for 6%

profile of v7, /device:TPU:0, one launch (start us, length us, event | category | flops | bytes accessed | tf_op | source)
XLA Modules:
  0.0 64.3 jit_solution(1080411291959162085)
XLA Ops:
  0.0 1.0 %copy-done = f32[8,96,128]{2,1,0:T(8,128)S(1)} copy-done((f32[8,96,128]{2,1,0:T(8,128)S(1)}, f32[8,96,128]{2,1,0:T(8,128)}, u32[]{:S(2)}) %copy-start) | copy-done | bytes 393240
  2.2 3.0 %collective-permute-start = (f32[104,128]{1,0:T(8,128)S(1)}, f32[104,128]{1,0:T(8,128)S(1)}, u32[]{:S(2)}, u32[]{:S(2)}) collective-permute-start(f32[104,128]{1,0:T(8,128)S(1)} %get-tuple-element.33), channel_id=1, source_target_pairs={{0,4},{4,0},{8,12},{12,8},{16,20},{20,16},{24,28},{28,24},{1,5},{5... | collective-permute-start | bytes 159752 | tf_op jit(solution)/shard_map/ppermute | solution.py:394
  5.3 1.6 %collective-permute-start.1 = (f32[104,128]{1,0:T(8,128)S(1)}, f32[104,128]{1,0:T(8,128)S(1)}, u32[]{:S(2)}, u32[]{:S(2)}) collective-permute-start(f32[104,128]{1,0:T(8,128)S(1)} %get-tuple-element.34), channel_id=1, source_target_pairs={{0,8},{4,12},{8,0},{12,4},{16,24},{20,28},{24,16},{28,20},{1,9},{5... | collective-permute-start | bytes 159752 | tf_op jit(solution)/shard_map/ppermute | solution.py:394
  6.9 3.0 %collective-permute-start.3 = (f32[104,128]{1,0:T(8,128)S(1)}, f32[104,128]{1,0:T(8,128)S(1)}, u32[]{:S(2)}, u32[]{:S(2)}) collective-permute-start(f32[104,128]{1,0:T(8,128)S(1)} %get-tuple-element.36), channel_id=1, source_target_pairs={{0,16},{4,20},{8,24},{12,28},{16,0},{20,4},{24,8},{28,12},{1,17},{... | collective-permute-start | bytes 159752 | tf_op jit(solution)/shard_map/ppermute | solution.py:394
  9.8 1.3 %collective-permute-start.4 = (f32[104,128]{1,0:T(8,128)S(1)}, f32[104,128]{1,0:T(8,128)S(1)}, u32[]{:S(2)}, u32[]{:S(2)}) collective-permute-start(f32[104,128]{1,0:T(8,128)S(1)} %get-tuple-element.37), channel_id=1, source_target_pairs={{0,20},{4,16},{8,28},{12,24},{16,4},{20,0},{24,12},{28,8},{1,21},{... | collective-permute-start | bytes 159752 | tf_op jit(solution)/shard_map/ppermute | solution.py:394
  11.1 3.6 %collective-permute-start.5 = (f32[104,128]{1,0:T(8,128)S(1)}, f32[104,128]{1,0:T(8,128)S(1)}, u32[]{:S(2)}, u32[]{:S(2)}) collective-permute-start(f32[104,128]{1,0:T(8,128)S(1)} %get-tuple-element.38), channel_id=1, source_target_pairs={{0,24},{4,28},{8,16},{12,20},{16,8},{20,12},{24,0},{28,4},{1,25},{... | collective-permute-start | bytes 159752 | tf_op jit(solution)/shard_map/ppermute | solution.py:394
  14.8 0.9 %copy-done.6 = f32[256,256]{1,0:T(8,128)S(1)} copy-done((f32[256,256]{1,0:T(8,128)S(1)}, f32[256,256]{1,0:T(8,128)}, u32[]{:S(2)}) %copy-start.6) | copy-done | bytes 262168
  15.7 0.9 %copy-done.8 = f32[96,288]{1,0:T(8,128)S(1)} copy-done((f32[96,288]{1,0:T(8,128)S(1)}, f32[96,288]{1,0:T(8,128)}, u32[]{:S(2)}) %copy-start.8) | copy-done | bytes 110616
  16.6 0.9 %copy-done.9 = f32[96,144]{1,0:T(8,128)S(1)} copy-done((f32[96,144]{1,0:T(8,128)S(1)}, f32[96,144]{1,0:T(8,128)}, u32[]{:S(2)}) %copy-start.9) | copy-done | bytes 55320
  18.1 3.5 %collective-permute-done.6.refs_7_ = f32[104,128]{1,0:T(8,128)S(1)} collective-permute-done((f32[104,128]{1,0:T(8,128)S(1)}, f32[104,128]{1,0:T(8,128)S(1)}, u32[]{:S(2)}, u32[]{:S(2)}) %collective-permute-start.6) | collective-permute-done | bytes 53280 | tf_op jit(solution)/shard_map/ppermute | solution.py:394
  21.6 3.7 %shard_map.111 = (f32[1152,128]{1,0:T(8,128)S(1)}, f32[864,128]{1,0:T(8,128)S(1)}, s32[8,1024]{1,0:T(8,128)S(1)}) custom-call(f32[104,128]{1,0:T(8,128)S(1)} %get-tuple-element.32.refs_0_, f32[104,128]{1,0:T(8,128)S(1)} %collective-permute-done.refs_1_, f32[104,128]{1,0:T(8,128)S(1)} %collective-permute-done.1.refs_2_, ...), custom_call_target="tpu_custom_call" | custom-call | flops 1000000000 | bytes 640000 | tf_op jit(solution)/shard_map/pallas_call | solution.py:379
  25.4 1.6 %collective-permute-start.7 = (f32[864,128]{1,0:T(8,128)S(1)}, f32[864,128]{1,0:T(8,128)S(1)}, u32[]{:S(2)}, u32[]{:S(2)}) collective-permute-start(f32[864,128]{1,0:T(8,128)S(1)} %get-tuple-element.47), channel_id=1, source_target_pairs={{0,2},{1,3},{2,0},{3,1},{4,6},{5,7},{6,4},{7,5},{8,10},{9,11},{10,... | collective-permute-start | bytes 1327112 | tf_op jit(solution)/shard_map/ppermute | solution.py:437
  27.3 3.6 %shard_map.112.before_ref = f32[1152,128]{1,0:T(8,128)S(1)} custom-call(f32[1152,128]{1,0:T(8,128)S(1)} %get-tuple-element.46.phi_ref, f32[864,128]{1,0:T(8,128)S(1)} %collective-permute-done.8.near_ref, f32[256,256]{1,0:T(8,128)S(1)} %copy-done.5, f32[256,256]{1,0:T(8,128)S(1)} %copy-done.4, f32[96,144]{1,0:T(8,128)S(1)} %copy-done.11, ...), custom_call_target="tpu_custom_call" | custom-call | flops 1811939328 | bytes 2846720 | tf_op jit(solution)/shard_map/pallas_call | solution.py:379
  30.9 7.1 %collective-permute-done.7.ahead_ref = f32[864,128]{1,0:T(8,128)S(1)} collective-permute-done((f32[864,128]{1,0:T(8,128)S(1)}, f32[864,128]{1,0:T(8,128)S(1)}, u32[]{:S(2)}, u32[]{:S(2)}) %collective-permute-start.7) | collective-permute-done | bytes 442400 | tf_op jit(solution)/shard_map/ppermute | solution.py:437
  38.0 1.8 %collective-permute-done.9.across_ref = f32[864,128]{1,0:T(8,128)S(1)} collective-permute-done((f32[864,128]{1,0:T(8,128)S(1)}, f32[864,128]{1,0:T(8,128)S(1)}, u32[]{:S(2)}, u32[]{:S(2)}) %collective-permute-start.9) | collective-permute-done | bytes 442400 | tf_op jit(solution)/shard_map/ppermute | solution.py:447
  39.8 9.7 %shard_map.113 = (f32[96,128]{1,0:T(8,128)S(1)}, f32[96,128]{1,0:T(8,128)S(1)}, f32[96,128]{1,0:T(8,128)S(1)}, f32[96,128]{1,0:T(8,128)S(1)}, f32[96,128]{1,0:T(...) custom-call(f32[1152,128]{1,0:T(8,128)S(1)} %get-tuple-element.46.phi_ref, ...), custom_call_target="tpu_custom_call" | custom-call | flops 1811939328 | bytes 4546560 | tf_op jit(solution)/shard_map/pallas_call | solution.py:379
  50.1 3.0 %collective-permute-start.12 = (f32[96,128]{1,0:T(8,128)S(1)}, f32[96,128]{1,0:T(8,128)S(1)}, u32[]{:S(2)}, u32[]{:S(2)}) collective-permute-start(f32[96,128]{1,0:T(8,128)S(1)} %get-tuple-element.54), channel_id=1, source_target_pairs={{0,12},{4,8},{8,4},{12,0},{16,28},{20,24},{24,20},{28,16},{1,13},{... | collective-permute-start | bytes 147464 | tf_op jit(solution)/shard_map/ppermute | solution.py:394
  53.0 0.8 %collective-permute-start.13 = (f32[96,128]{1,0:T(8,128)S(1)}, f32[96,128]{1,0:T(8,128)S(1)}, u32[]{:S(2)}, u32[]{:S(2)}) collective-permute-start(f32[96,128]{1,0:T(8,128)S(1)} %get-tuple-element.55), channel_id=1, source_target_pairs={{0,16},{4,20},{8,24},{12,28},{16,0},{20,4},{24,8},{28,12},{1,17},{... | collective-permute-start | bytes 147464 | tf_op jit(solution)/shard_map/ppermute | solution.py:394
  53.9 2.0 %collective-permute-start.14 = (f32[96,128]{1,0:T(8,128)S(1)}, f32[96,128]{1,0:T(8,128)S(1)}, u32[]{:S(2)}, u32[]{:S(2)}) collective-permute-start(f32[96,128]{1,0:T(8,128)S(1)} %get-tuple-element.56), channel_id=1, source_target_pairs={{0,20},{4,16},{8,28},{12,24},{16,4},{20,0},{24,12},{28,8},{1,21},{... | collective-permute-start | bytes 147464 | tf_op jit(solution)/shard_map/ppermute | solution.py:394
  55.9 0.8 %collective-permute-start.15 = (f32[96,128]{1,0:T(8,128)S(1)}, f32[96,128]{1,0:T(8,128)S(1)}, u32[]{:S(2)}, u32[]{:S(2)}) collective-permute-start(f32[96,128]{1,0:T(8,128)S(1)} %get-tuple-element.57), channel_id=1, source_target_pairs={{0,24},{4,28},{8,16},{12,20},{16,8},{20,12},{24,0},{28,4},{1,25},{... | collective-permute-start | bytes 147464 | tf_op jit(solution)/shard_map/ppermute | solution.py:394
  56.7 4.0 %collective-permute-start.16 = (f32[96,128]{1,0:T(8,128)S(1)}, f32[96,128]{1,0:T(8,128)S(1)}, u32[]{:S(2)}, u32[]{:S(2)}) collective-permute-start(f32[96,128]{1,0:T(8,128)S(1)} %get-tuple-element.58), channel_id=1, source_target_pairs={{0,28},{4,24},{8,20},{12,16},{16,12},{20,8},{24,4},{28,0},{1,29},{... | collective-permute-start | bytes 147464 | tf_op jit(solution)/shard_map/ppermute | solution.py:394
  60.7 1.0 %collective-permute-done.14.refs_5_ = f32[96,128]{1,0:T(8,128)S(1)} collective-permute-done((f32[96,128]{1,0:T(8,128)S(1)}, f32[96,128]{1,0:T(8,128)S(1)}, u32[]{:S(2)}, u32[]{:S(2)}) %collective-permute-start.14) | collective-permute-done | bytes 49184 | tf_op jit(solution)/shard_map/ppermute | solution.py:394
  61.9 1.7 %collective-permute-done.16.refs_7_ = f32[96,128]{1,0:T(8,128)S(1)} collective-permute-done((f32[96,128]{1,0:T(8,128)S(1)}, f32[96,128]{1,0:T(8,128)S(1)}, u32[]{:S(2)}, u32[]{:S(2)}) %collective-permute-start.16) | collective-permute-done | bytes 49184 | tf_op jit(solution)/shard_map/ppermute | solution.py:394
  63.5 0.8 %shard_map.114 = f32[8,96,128]{2,1,0:T(8,128)} custom-call(f32[96,128]{1,0:T(8,128)S(1)} %get-tuple-element.51.refs_0_, f32[96,128]{1,0:T(8,128)S(1)} %collective-permute-done.10.refs_1_, f32[96,128]{1,0:T(8,128)S(1)} %collective-permute-done.11.refs_2_, f32[96,128]{1,0:T(8,128)S(1)} %collective-permute-done.12.refs_3_, ...), custom_call_target="tpu_custom_call" | custom-call | flops 1000000 | bytes 393216 | tf_op jit(solution)/shard_map/pallas_call | solution.py:379
  (40 shorter events, 2.9 us)
Async XLA Ops:
  2.2 8.9 %collective-permute-start = (f32[104,128]{1,0:T(8,128)S(1)}, f32[104,128]{1,0:T(8,128)S(1)}, u32[]{:S(2)}, u32[]{:S(2)}) collective-permute-start(f32[104,128]{1,0:T(8,128)S(1)} %get-tuple-element.33), channel_id=1, source_target_pairs={{0,4},{4,0},{8,12},{12,8},{16,20},{20,16},{24,28},{28,24},{1,5},{5... | collective-permute-start | bytes 159752 | tf_op jit(solution)/shard_map/ppermute | solution.py:394
  5.3 9.5 %collective-permute-start.1 = (f32[104,128]{1,0:T(8,128)S(1)}, f32[104,128]{1,0:T(8,128)S(1)}, u32[]{:S(2)}, u32[]{:S(2)}) collective-permute-start(f32[104,128]{1,0:T(8,128)S(1)} %get-tuple-element.34), channel_id=1, source_target_pairs={{0,8},{4,12},{8,0},{12,4},{16,24},{20,28},{24,16},{28,20},{1,9},{5... | collective-permute-start | bytes 159752 | tf_op jit(solution)/shard_map/ppermute | solution.py:394
  6.9 10.7 %collective-permute-start.2 = (f32[104,128]{1,0:T(8,128)S(1)}, f32[104,128]{1,0:T(8,128)S(1)}, u32[]{:S(2)}, u32[]{:S(2)}) collective-permute-start(f32[104,128]{1,0:T(8,128)S(1)} %get-tuple-element.35), channel_id=1, source_target_pairs={{0,12},{4,8},{8,4},{12,0},{16,28},{20,24},{24,20},{28,16},{1,13},{... | collective-permute-start | bytes 159752 | tf_op jit(solution)/shard_map/ppermute | solution.py:394
  6.9 10.7 %collective-permute-start.3 = (f32[104,128]{1,0:T(8,128)S(1)}, f32[104,128]{1,0:T(8,128)S(1)}, u32[]{:S(2)}, u32[]{:S(2)}) collective-permute-start(f32[104,128]{1,0:T(8,128)S(1)} %get-tuple-element.36), channel_id=1, source_target_pairs={{0,16},{4,20},{8,24},{12,28},{16,0},{20,4},{24,8},{28,12},{1,17},{... | collective-permute-start | bytes 159752 | tf_op jit(solution)/shard_map/ppermute | solution.py:394
  9.8 8.2 %collective-permute-start.4 = (f32[104,128]{1,0:T(8,128)S(1)}, f32[104,128]{1,0:T(8,128)S(1)}, u32[]{:S(2)}, u32[]{:S(2)}) collective-permute-start(f32[104,128]{1,0:T(8,128)S(1)} %get-tuple-element.37), channel_id=1, source_target_pairs={{0,20},{4,16},{8,28},{12,24},{16,4},{20,0},{24,12},{28,8},{1,21},{... | collective-permute-start | bytes 159752 | tf_op jit(solution)/shard_map/ppermute | solution.py:394
  11.1 6.9 %collective-permute-start.5 = (f32[104,128]{1,0:T(8,128)S(1)}, f32[104,128]{1,0:T(8,128)S(1)}, u32[]{:S(2)}, u32[]{:S(2)}) collective-permute-start(f32[104,128]{1,0:T(8,128)S(1)} %get-tuple-element.38), channel_id=1, source_target_pairs={{0,24},{4,28},{8,16},{12,20},{16,8},{20,12},{24,0},{28,4},{1,25},{... | collective-permute-start | bytes 159752 | tf_op jit(solution)/shard_map/ppermute | solution.py:394
  14.7 6.8 %collective-permute-start.6 = (f32[104,128]{1,0:T(8,128)S(1)}, f32[104,128]{1,0:T(8,128)S(1)}, u32[]{:S(2)}, u32[]{:S(2)}) collective-permute-start(f32[104,128]{1,0:T(8,128)S(1)} %get-tuple-element.39), channel_id=1, source_target_pairs={{0,28},{4,24},{8,20},{12,16},{16,12},{20,8},{24,4},{28,0},{1,29},{... | collective-permute-start | bytes 159752 | tf_op jit(solution)/shard_map/ppermute | solution.py:394
  21.6 5.6 %copy-start.2 = (f32[2304,128]{1,0:T(8,128)S(1)}, f32[2304,128]{1,0:T(8,128)}, u32[]{:S(2)}) copy-start(f32[2304,128]{1,0:T(8,128)} %constant.26.clone.refs_4_) | copy-start | bytes 3538948
  21.6 5.6 %copy-start.4 = (f32[256,256]{1,0:T(8,128)S(1)}, f32[256,256]{1,0:T(8,128)}, u32[]{:S(2)}) copy-start(f32[256,256]{1,0:T(8,128)} %constant.20.clone.refs_1_) | copy-start | bytes 786436
  21.6 5.6 %copy-start.5 = (f32[256,256]{1,0:T(8,128)S(1)}, f32[256,256]{1,0:T(8,128)}, u32[]{:S(2)}) copy-start(f32[256,256]{1,0:T(8,128)} %constant.18.clone.refs_0_) | copy-start | bytes 786436
  21.6 5.6 %copy-start.10 = (f32[96,144]{1,0:T(8,128)S(1)}, f32[96,144]{1,0:T(8,128)}, u32[]{:S(2)}) copy-start(f32[96,144]{1,0:T(8,128)} %constant.22.clone.refs_2_.refs_3_) | copy-start | bytes 165892
  21.6 5.6 %copy-start.11 = (f32[96,144]{1,0:T(8,128)S(1)}, f32[96,144]{1,0:T(8,128)}, u32[]{:S(2)}) copy-start(f32[96,144]{1,0:T(8,128)} %constant.21.clone.refs_2_) | copy-start | bytes 165892
  25.3 1.9 %collective-permute-start.8 = (f32[864,128]{1,0:T(8,128)S(1)}, f32[864,128]{1,0:T(8,128)S(1)}, u32[]{:S(2)}, u32[]{:S(2)}) collective-permute-start(f32[864,128]{1,0:T(8,128)S(1)} %get-tuple-element.47), channel_id=1, source_target_pairs={{0,1},{1,0},{2,3},{3,2},{4,5},{5,4},{6,7},{7,6},{8,9},{9,8},{10,11... | collective-permute-start | bytes 1327112 | tf_op jit(solution)/shard_map/ppermute | solution.py:439
  25.4 12.6 %collective-permute-start.7 = (f32[864,128]{1,0:T(8,128)S(1)}, f32[864,128]{1,0:T(8,128)S(1)}, u32[]{:S(2)}, u32[]{:S(2)}) collective-permute-start(f32[864,128]{1,0:T(8,128)S(1)} %get-tuple-element.47), channel_id=1, source_target_pairs={{0,2},{1,3},{2,0},{3,1},{4,6},{5,7},{6,4},{7,5},{8,10},{9,11},{10,... | collective-permute-start | bytes 1327112 | tf_op jit(solution)/shard_map/ppermute | solution.py:437
  27.2 12.6 %copy-start.3 = (f32[256,512]{1,0:T(8,128)S(1)}, f32[256,512]{1,0:T(8,128)}, u32[]{:S(2)}) copy-start(f32[256,512]{1,0:T(8,128)} %constant.23.clone.real_forward_ref) | copy-start | bytes 1572868
  27.2 12.6 %copy-start.7 = (f32[96,288]{1,0:T(8,128)S(1)}, f32[96,288]{1,0:T(8,128)}, u32[]{:S(2)}) copy-start(f32[96,288]{1,0:T(8,128)} %constant.25.clone.stick_out_ref) | copy-start | bytes 331780
  38.0 1.8 %collective-permute-start.9 = (f32[864,128]{1,0:T(8,128)S(1)}, f32[864,128]{1,0:T(8,128)S(1)}, u32[]{:S(2)}, u32[]{:S(2)}) collective-permute-start(f32[864,128]{1,0:T(8,128)S(1)} %collective-permute-done.7.ahead_ref), channel_id=1, source_target_pairs={{0,1},{1,0},{2,3},{3,2},{4,5},{5,4},{6,7},{7,6},{8,9},{9,8},{10,11... | collective-permute-start | bytes 1327112 | tf_op jit(solution)/shard_map/ppermute | solution.py:447
  49.5 6.4 %collective-permute-start.10 = (f32[96,128]{1,0:T(8,128)S(1)}, f32[96,128]{1,0:T(8,128)S(1)}, u32[]{:S(2)}, u32[]{:S(2)}) collective-permute-start(f32[96,128]{1,0:T(8,128)S(1)} %get-tuple-element.52), channel_id=1, source_target_pairs={{0,4},{4,0},{8,12},{12,8},{16,20},{20,16},{24,28},{28,24},{1,5},{5... | collective-permute-start | bytes 147464 | tf_op jit(solution)/shard_map/ppermute | solution.py:394
  50.1 6.7 %collective-permute-start.11 = (f32[96,128]{1,0:T(8,128)S(1)}, f32[96,128]{1,0:T(8,128)S(1)}, u32[]{:S(2)}, u32[]{:S(2)}) collective-permute-start(f32[96,128]{1,0:T(8,128)S(1)} %get-tuple-element.53), channel_id=1, source_target_pairs={{0,8},{4,12},{8,0},{12,4},{16,24},{20,28},{24,16},{28,20},{1,9},{5... | collective-permute-start | bytes 147464 | tf_op jit(solution)/shard_map/ppermute | solution.py:394
  50.1 10.6 %collective-permute-start.12 = (f32[96,128]{1,0:T(8,128)S(1)}, f32[96,128]{1,0:T(8,128)S(1)}, u32[]{:S(2)}, u32[]{:S(2)}) collective-permute-start(f32[96,128]{1,0:T(8,128)S(1)} %get-tuple-element.54), channel_id=1, source_target_pairs={{0,12},{4,8},{8,4},{12,0},{16,28},{20,24},{24,20},{28,16},{1,13},{... | collective-permute-start | bytes 147464 | tf_op jit(solution)/shard_map/ppermute | solution.py:394
  53.0 7.7 %collective-permute-start.13 = (f32[96,128]{1,0:T(8,128)S(1)}, f32[96,128]{1,0:T(8,128)S(1)}, u32[]{:S(2)}, u32[]{:S(2)}) collective-permute-start(f32[96,128]{1,0:T(8,128)S(1)} %get-tuple-element.55), channel_id=1, source_target_pairs={{0,16},{4,20},{8,24},{12,28},{16,0},{20,4},{24,8},{28,12},{1,17},{... | collective-permute-start | bytes 147464 | tf_op jit(solution)/shard_map/ppermute | solution.py:394
  53.9 7.8 %collective-permute-start.14 = (f32[96,128]{1,0:T(8,128)S(1)}, f32[96,128]{1,0:T(8,128)S(1)}, u32[]{:S(2)}, u32[]{:S(2)}) collective-permute-start(f32[96,128]{1,0:T(8,128)S(1)} %get-tuple-element.56), channel_id=1, source_target_pairs={{0,20},{4,16},{8,28},{12,24},{16,4},{20,0},{24,12},{28,8},{1,21},{... | collective-permute-start | bytes 147464 | tf_op jit(solution)/shard_map/ppermute | solution.py:394
  55.9 5.9 %collective-permute-start.15 = (f32[96,128]{1,0:T(8,128)S(1)}, f32[96,128]{1,0:T(8,128)S(1)}, u32[]{:S(2)}, u32[]{:S(2)}) collective-permute-start(f32[96,128]{1,0:T(8,128)S(1)} %get-tuple-element.57), channel_id=1, source_target_pairs={{0,24},{4,28},{8,16},{12,20},{16,8},{20,12},{24,0},{28,4},{1,25},{... | collective-permute-start | bytes 147464 | tf_op jit(solution)/shard_map/ppermute | solution.py:394
  56.7 6.8 %collective-permute-start.16 = (f32[96,128]{1,0:T(8,128)S(1)}, f32[96,128]{1,0:T(8,128)S(1)}, u32[]{:S(2)}, u32[]{:S(2)}) collective-permute-start(f32[96,128]{1,0:T(8,128)S(1)} %get-tuple-element.58), channel_id=1, source_target_pairs={{0,28},{4,24},{8,20},{12,16},{16,12},{20,8},{24,4},{28,0},{1,29},{... | collective-permute-start | bytes 147464 | tf_op jit(solution)/shard_map/ppermute | solution.py:394
  (5 other events, 4.4 us)

commit v8 on v7

--- a/solution.py
+++ b/solution.py
@@ -46,12 +46,12 @@
     forward[upper, lower], forward[upper, upper] = s, c
     backward[lower, lower], backward[lower, upper] = c, s
     backward[upper, lower], backward[upper, upper] = -s, c
-    real_forward = np.zeros((LANES, 2 * LANES))
-    real_forward[lower, :LANES] = forward[lower]
-    real_forward[upper, LANES:] = forward[lower]
-
-    stick_in = np.block([[c, -s], [s, c]])
-    stick_out = np.block([[c, s], [-s, c]]) * g**-1.5
+    stick_in = np.zeros((LANES, 2 * g))
+    stick_in[lower, :g], stick_in[lower, g:] = c, -s
+    stick_in[upper, :g], stick_in[upper, g:] = s, c
+    stick_out = np.zeros((2 * g, LANES))
+    stick_out[:g, lower], stick_out[:g, upper] = c, s
+    stick_out[g:, lower], stick_out[g:, upper] = -s, c
 
     freq = np.arange(g)
     square = np.minimum(freq, g - freq) ** 2
@@ -63,13 +63,11 @@
     coulomb[:, :, upper] = kernel
     return dict(
         forward=down(forward),
-        backward=down(backward),
         last_backward=down(backward / g**3),
         left_forward=across(np.concatenate([c, -s], 0)),
         left_backward=across(np.concatenate([c, s], 0)),
-        real_forward=down(real_forward),
         stick_in=across(stick_in),
-        stick_out=across(stick_out),
+        stick_out=across(stick_out * g**-1.5),
         coulomb=coulomb.reshape(g * g, LANES),
     )
 
@@ -102,20 +100,6 @@
     return jnp.where(low, a, turned(b)), jnp.where(low, turned(a), b)
 
 
-def transposed(a, b):
-    g = a.shape[0]
-    pad = jnp.zeros((MID - g, LANES), F32)
-    both = jnp.concatenate([a, pad, b, pad], 0).T
-    return regrouped(both[:g], both[MID : MID + g])
-
-
-def pairwise(function, slabs):
-    results = []
-    for k in range(0, len(slabs), 2):
-        results += function(slabs[k], slabs[k + 1])
-    return results
-
-
 def beside(a, b):
     return jnp.concatenate([a, b], 1)
 
@@ -142,12 +126,6 @@
     return both[:, :width] + both[:, width:]
 
 
-def right_slabs(slabs, table):
-    g = slabs[0].shape[0]
-    out = right(jnp.concatenate(slabs, 0), table)
-    return [out[k : k + g] for k in range(0, out.shape[0], g)]
-
-
 def strided(ref, first, g):
     return ref[pl.ds(first, g, stride=g), :]
 
@@ -156,9 +134,7 @@
     return pl.ds(index * g, count * g)
 
 
-def one_hot(columns, first, rows):
-    index = lax.broadcasted_iota(jnp.int16, (rows, columns.shape[1]), 0)
-    wanted = (columns - first).astype(jnp.int16)
+def one_hot(index, wanted):
     return jnp.where(index == wanted, jnp.asarray(1, BF16), jnp.asarray(0, BF16))
 
 
@@ -194,34 +170,14 @@
         out_ref[own ^ d] = block_ref[...]
 
 
-def folded_parts(parts, g):
-    used = lax.broadcasted_iota(jnp.int32, parts[0].shape, 1) % MID < g
-    width = g // FOLD
-    return [jnp.where(used, parts[k], pltpu.roll(parts[FOLD], g - k * width, 1)) for k in range(FOLD)]
-
-
-def folded_position(columns, g):
-    kx = lax.div(columns, g)
-    ky = columns - kx * g
-    group, member = lax.div(ky, 2 * FOLD + 2), lax.rem(ky, 2 * FOLD + 2)
-    pair, half = lax.div(member, 2), lax.rem(member, 2)
-    width = g // FOLD
-    piece = lax.div(kx, width)
-    last = pair == FOLD
-    row = group * FOLD + jnp.where(last, piece, pair)
-    lane = half * MID + jnp.where(last, g + kx - piece * width, kx)
-    return jnp.where(columns < 0, -1, row * LANES + lane)
-
-
-def paired_position(columns, g):
-    kx = lax.div(columns, g)
-    return jnp.where(columns < 0, -1, lax.div(kx, 2) * LANES + lax.rem(kx, 2) * MID + columns - kx * g)
-
-
 def fold(field_ref, folded_ref, g):
     rows = folded_ref.shape[0] // FOLD
-    parts = [field_ref[k * rows : (k + 1) * rows, :] for k in range(FOLD + 1)]
-    folded_ref[...] = jnp.concatenate(folded_parts(parts, g), 0)
+    used = lax.broadcasted_iota(jnp.int32, (rows, LANES), 1) % MID < g
+    last = field_ref[FOLD * rows :, :]
+    width = g // FOLD
+    for k in range(FOLD):
+        part = slice(k * rows, (k + 1) * rows)
+        folded_ref[part, :] = jnp.where(used, field_ref[part, :], pltpu.roll(last, g - k * width, 1))
 
 
 def unfold(folded_ref, field_ref, g):
@@ -245,41 +201,41 @@
 
 def field_kernel(g, count, *refs):
     received = refs[:count]
-    stick_in_ref, backward_ref, left_ref, phi_ref, folded_ref, positions_ref, work_a = refs[count:]
-    columns = jnp.concatenate([ref[2 * g : 2 * g + 1, :] for ref in received], 1).astype(jnp.int32)
-    positions_ref[...] = jnp.broadcast_to(folded_position(columns, g), positions_ref.shape)
-    stick_in, backward, left_backward = stick_in_ref[...], backward_ref[...], left_ref[...]
-    sticks, rows = [], []
+    stick_in_ref, left_ref, phi_ref, folded_ref, columns_ref, work_a = refs[count:]
+    columns = jnp.concatenate([ref[2 * g : 2 * g + 1, :] for ref in received], 1)
+    columns_ref[...] = jnp.broadcast_to(columns, columns_ref.shape)
+    columns = columns.astype(jnp.int32)
+    stick_in, backward = stick_in_ref[...], left_ref[...]
+    sticks = []
     for k in range(0, count, 2):
         block = beside(received[k][: 2 * g, :], received[k + 1][: 2 * g, :])
-        sticks.append(jnp.concatenate(split(dot(stick_in, stacked(block))), 0))
-        for ref in received[k : k + 2]:
-            ids = paired_position(ref[2 * g : 2 * g + 8, :].astype(jnp.int32), g).astype(F32)
-            ids = jnp.concatenate([ids] * (LANES // 8), 0).T
-            rows.append(jnp.concatenate([ids, ids], 1).astype(jnp.int32).astype(jnp.int16))
-    sticks = jnp.concatenate(sticks, 1)
-    rows = jnp.concatenate(rows, 0)
-
-    lane = lax.broadcasted_iota(jnp.int16, rows.shape, 1)
-    step = 2 * PAIRS
-    for first in range(0, g, step):
-        slabs = []
-        for kx in range(first, first + step, 4):
-            start = jnp.asarray(kx // 2 * LANES, jnp.int16)
-            hot = jnp.where(rows == lane + start, jnp.asarray(1, BF16), jnp.asarray(0, BF16))
-            both = dot(sticks, hot)
-            placed = both[: 2 * g] + both[2 * g :]
-            for part in halves(placed):
-                slabs += regrouped(part[:g], part[g:])
-        store(work_a, first, right_slabs(slabs, backward))
+        sticks.append(beside(*split(dot(stick_in, stacked(block)).T)))
+    sticks = jnp.concatenate(sticks, 0)
 
     half = g // 2
-    for z in range(half):
-        x = beside(strided(work_a, z, g), strided(work_a, z + half, g))
-        (cos, cos_up), (sin, sin_up) = map(halves, left(left_backward, x))
+    index = lax.broadcasted_iota(jnp.int16, (half * g, columns.shape[1]), 0)
+    for first in (0, half):
+        both = dot(one_hot(index, (columns - first * g).astype(jnp.int16)), sticks)
+        placed = both[:, :LANES] + both[:, LANES:]
+        for k in range(0, half, 2):
+            slabs = left_complex(backward, placed[k * g : (k + 1) * g], placed[(k + 1) * g : (k + 2) * g])
+            store(work_a, first + k, slabs)
+
+    for y in range(half):
+        x = beside(strided(work_a, y, g), strided(work_a, y + half, g))
+        (cos, cos_up), (sin, sin_up) = map(halves, left(backward, x))
         low = lane_halves(cos.shape)
-        store(phi_ref, z, [jnp.where(low, cos - turned(sin), turned(cos_up) - sin_up)])
+        store(phi_ref, y, [jnp.where(low, cos - turned(sin), turned(cos_up) - sin_up)])
     fold(phi_ref, folded_ref, g)
+
+
+def pick_kernel(g, columns_ref, hot_ref):
+    for k in range(0, columns_ref.shape[1], LANES):
+        block = columns_ref[:, k : k + LANES]
+        wanted = jnp.concatenate([block] * (LANES // block.shape[0]), 0).T.astype(jnp.int32)
+        for c in range(0, hot_ref.shape[1], LANES):
+            index = lax.broadcasted_iota(jnp.int16, (LANES, LANES), 1)
+            hot_ref[k : k + LANES, c : c + LANES] = one_hot(index, (wanted - c).astype(jnp.int16))
 
 
 def potentials(g, phi_ref, first_ref, second_ref, tables, work_a, work_b, emit):
@@ -334,43 +290,43 @@
     potentials(g, phi_ref, first_ref, second_ref, tables, work_a, work_b, emit)
 
 
-def far_kernel(g, weights, phi_ref, ahead_ref, across_ref, before_ref, positions_ref, stick_out_ref, real_forward_ref, *refs):
+def far_kernel(g, weights, phi_ref, ahead_ref, across_ref, before_ref, hot_ref, stick_out_ref, *refs):
     tables, out_refs = refs[:5], refs[5:-5]
-    first_ref, second_ref, work_a, work_b, parts_ref = refs[-5:]
+    first_ref, second_ref, work_a, work_b, picked_ref = refs[-5:]
     unfold(ahead_ref, first_ref, g)
     unfold(across_ref, second_ref, g)
-    forward, real_forward = tables[0][...].astype(BF16), real_forward_ref[...].astype(BF16)
+    forward = tables[2][...].astype(BF16)
     half = g // 2
 
     def emit(start, first, second):
         rows = slab_rows(start, g, PAIRS)
         total = before_ref[rows, :] + weights[0] * (first * first_ref[rows, :])
         total = total + weights[1] * (second * second_ref[rows, :])
-        spectrum = right(total, real_forward)
-        spectrum = jnp.concatenate([spectrum[:, :LANES], spectrum[:, LANES:]], 0)
-        slabs = pairwise(transposed, [spectrum[k * g : (k + 1) * g] for k in range(2 * PAIRS)])
-        slabs = right_slabs(slabs, forward)
-        store(work_a, start, slabs[:PAIRS])
-        store(work_a, start + half, slabs[PAIRS:])
+        for k in range(0, PAIRS, 2):
+            cos, sin = left(forward, beside(total[k * g : (k + 1) * g], total[(k + 1) * g : (k + 2) * g]))
+            for j, (real, imag) in enumerate(zip(halves(cos), halves(sin))):
+                lower, upper = regrouped(real, imag)
+                store(work_a, start + k + j, [lower])
+                store(work_a, start + k + j + half, [upper])
 
     potentials(g, phi_ref, first_ref, second_ref, tables, work_a, work_b, emit)
 
-    many = 2 * FOLD + 2
-    width = FOLD * LANES
-    for group in range(g // many):
-        parts = []
-        for ky in range(group * many, (group + 1) * many, 2):
-            parts.append(jnp.concatenate(regrouped(strided(work_a, ky, g), strided(work_a, ky + 1, g)), 0))
-        line = jnp.concatenate(folded_parts(parts, g), 1)
-        parts_ref[:, group * width : (group + 1) * width] = jnp.concatenate(split(line), 0)
-
-    parts = parts_ref[...]
+    step = g // 3
+    for first in range(0, g, step):
+        slabs = []
+        for kx in range(first, first + step, 2):
+            slabs += left_complex(forward, strided(work_a, kx, g), strided(work_a, kx + 1, g))
+        spectrum = beside(*split(jnp.concatenate(slabs, 0)))
+        both = dot(hot_ref[:, first * g : (first + step) * g], spectrum)
+        both = both[:, :LANES] + both[:, LANES:]
+        picked_ref[...] = both if first == 0 else picked_ref[...] + both
+
     stick_out = stick_out_ref[...].astype(BF16)
     for k in range(0, len(out_refs), 2):
-        hot = one_hot(positions_ref[:1, k * LANES : (k + 2) * LANES], 0, g * g)
-        both = dot(parts, hot)
-        picked = dot(stick_out, stacked(both[: 2 * g] + both[2 * g :]))
-        out_refs[k][...], out_refs[k + 1][...] = picked[:, :LANES], picked[:, LANES:]
+        high, low = split(picked_ref[k * LANES : (k + 2) * LANES, :])
+        lined = jnp.concatenate([high, low, high], 1)
+        out = lax.dot_general(stick_out, lined, (((1,), (1,)), ((), ())), preferred_element_type=F32)
+        out_refs[k][...], out_refs[k + 1][...] = halves(out)
 
 
 def call(kernel, out_shapes, scratch, flops, *operands, space=pltpu.VMEM):
@@ -418,13 +374,13 @@
         space=pltpu.HBM,
     )
     received = exchanged(sent)
-    first_tables = lax.optimization_barrier((t["stick_in"], t["backward"], t["left_backward"], sent[0]))[:3]
+    first_tables = lax.optimization_barrier((t["stick_in"], t["left_backward"], sent[0]))[:2]
     first_tables = call(
         table_kernel, [jax.ShapeDtypeStruct(x.shape, BF16) for x in first_tables], [], 10**9, *first_tables
     )
-    phi, packed, positions = call(
+    phi, packed, columns = call(
         functools.partial(field_kernel, g, owners),
-        [field, folded, jax.ShapeDtypeStruct((8, owners * slots), jnp.int32)],
+        [field, folded, jax.ShapeDtypeStruct((8, owners * slots), F32)],
         [work],
         10**9,
         *received,
@@ -441,7 +397,10 @@
     total = call(
         functools.partial(near_kernel, g), field, [field_scratch, work, work], pot_flops, phi, near, *pot_tables
     )
-    ahead, total = lax.optimization_barrier((ahead, total))
+    hot = call(
+        functools.partial(pick_kernel, g), jax.ShapeDtypeStruct((owners * slots, rows), BF16), [], pot_flops, columns
+    )
+    ahead, total, hot = lax.optimization_barrier((ahead, total, hot))
     if groups == 2 * HALF:
         weights = (2.0, 1.0)
         first, second = ahead, lax.ppermute(ahead, "band", swap)
@@ -464,15 +423,14 @@
     result = call(
         functools.partial(far_kernel, g, weights),
         [jax.ShapeDtypeStruct((2 * g, slots), F32)] * owners,
-        [field_scratch, field_scratch, work, work, pltpu.VMEM((4 * g, rows), BF16)],
+        [field_scratch, field_scratch, work, work, pltpu.VMEM((owners * slots, LANES), F32)],
         pot_flops,
         phi,
         first,
         second,
         total,
-        positions,
+        hot,
         t["stick_out"],
-        t["real_forward"],
         *pot_tables,
     )
     return call(place_kernel, jax.ShapeDtypeStruct(sticks.shape, F32), [], 10**6, *exchanged(result))

time: 64.6 us -> 62.9 us (0.974)
  local copies, waits for them, and re-layouts: 4.44 us -> 3.5 us
    ppermute x1, waiting for transfers between devices: 7.13 us -> 6.12 us  [fetched(): lax.ppermute(packed, 'band', [(i, (i - distance) % groups) for i in range...]
    unnamed x24 -> x20, local copies, waits for them, and re-layouts: 4.44 us -> 3.5 us
    ppermute x14, waiting for transfers between devices: 6.86 us -> 7.71 us  [exchanged(): lax.ppermute(blocks[d], 'stick', [(i, i ^ d) for i in range(owners)])]
    pallas_call x6 -> x7, Pallas kernels: 18.4 us -> 18.1 us  [call(): pl.pallas_call(kernel, out_shape=out_shapes, in_specs=[pl.BlockSpec(memor...]
  transfers between devices with their start and end apart: 17 -> 17, of which waited for: 8 -> 7; matrix products, arithmetic and copies ran while one was open for 0% -> 0% of each run, Pallas kernels for 6% -> 8%
where the time goes in v8:
time: 62.9 us; the launch traced here: 62.7 us
  starting transfers between devices  25.3 us (40%)
  Pallas kernels  18.1 us (29%)
  waiting for transfers between devices  15.6 us (25%)
  local copies, waits for them, and re-layouts  3.5 us (6%)
    ppermute x14, starting transfers between devices, exchanged(): lax.ppermute(blocks[d], 'stick', [(i, i ^ d) for i in range(owners)])  23.7 us
    pallas_call x7, Pallas kernels, call(): pl.pallas_call(kernel, out_shape=out_shapes, in_specs=[pl.BlockSpec(memor...  18.1 us
    ppermute x14, waiting for transfers between devices, exchanged(): lax.ppermute(blocks[d], 'stick', [(i, i ^ d) for i in range(owners)])  7.71 us
    ppermute x1, waiting for transfers between devices, fetched(): lax.ppermute(packed, 'band', [(i, (i - distance) % groups) for i in range...  6.12 us
    unnamed x20, local copies, waits for them, and re-layouts  3.5 us
    ppermute x1, waiting for transfers between devices, on_device(): first, second = (ahead, lax.ppermute(ahead, 'band', swap))  1.79 us
    ppermute x1, starting transfers between devices, fetched(): lax.ppermute(packed, 'band', [(i, (i - distance) % groups) for i in range...  1.55 us
  transfers between devices with their start and end apart: 17, of which 7 were waited for; matrix products, arithmetic and copies ran while one was open for 0% of the time, Pallas kernels for 8%

profile of v8, /device:TPU:0, one launch (start us, length us, event | category | flops | bytes accessed | tf_op | source)
XLA Modules:
  0.0 62.7 jit_solution(3199893717287554023)
XLA Ops:
  0.0 1.0 %copy-done.1 = f32[8,96,128]{2,1,0:T(8,128)S(1)} copy-done((f32[8,96,128]{2,1,0:T(8,128)S(1)}, f32[8,96,128]{2,1,0:T(8,128)}, u32[]{:S(2)}) %copy-start.1) | copy-done | bytes 393240
  2.2 3.0 %collective-permute-start = (f32[104,128]{1,0:T(8,128)S(1)}, f32[104,128]{1,0:T(8,128)S(1)}, u32[]{:S(2)}, u32[]{:S(2)}) collective-permute-start(f32[104,128]{1,0:T(8,128)S(1)} %get-tuple-element.32), channel_id=1, source_target_pairs={{0,4},{4,0},{8,12},{12,8},{16,20},{20,16},{24,28},{28,24},{1,5},{5... | collective-permute-start | bytes 159752 | tf_op jit(solution)/shard_map/ppermute | solution.py:350
  5.3 1.6 %collective-permute-start.1 = (f32[104,128]{1,0:T(8,128)S(1)}, f32[104,128]{1,0:T(8,128)S(1)}, u32[]{:S(2)}, u32[]{:S(2)}) collective-permute-start(f32[104,128]{1,0:T(8,128)S(1)} %get-tuple-element.33), channel_id=1, source_target_pairs={{0,8},{4,12},{8,0},{12,4},{16,24},{20,28},{24,16},{28,20},{1,9},{5... | collective-permute-start | bytes 159752 | tf_op jit(solution)/shard_map/ppermute | solution.py:350
  6.9 3.0 %collective-permute-start.3 = (f32[104,128]{1,0:T(8,128)S(1)}, f32[104,128]{1,0:T(8,128)S(1)}, u32[]{:S(2)}, u32[]{:S(2)}) collective-permute-start(f32[104,128]{1,0:T(8,128)S(1)} %get-tuple-element.35), channel_id=1, source_target_pairs={{0,16},{4,20},{8,24},{12,28},{16,0},{20,4},{24,8},{28,12},{1,17},{... | collective-permute-start | bytes 159752 | tf_op jit(solution)/shard_map/ppermute | solution.py:350
  9.8 1.3 %collective-permute-start.4 = (f32[104,128]{1,0:T(8,128)S(1)}, f32[104,128]{1,0:T(8,128)S(1)}, u32[]{:S(2)}, u32[]{:S(2)}) collective-permute-start(f32[104,128]{1,0:T(8,128)S(1)} %get-tuple-element.36), channel_id=1, source_target_pairs={{0,20},{4,16},{8,28},{12,24},{16,4},{20,0},{24,12},{28,8},{1,21},{... | collective-permute-start | bytes 159752 | tf_op jit(solution)/shard_map/ppermute | solution.py:350
  11.1 3.6 %collective-permute-start.5 = (f32[104,128]{1,0:T(8,128)S(1)}, f32[104,128]{1,0:T(8,128)S(1)}, u32[]{:S(2)}, u32[]{:S(2)}) collective-permute-start(f32[104,128]{1,0:T(8,128)S(1)} %get-tuple-element.37), channel_id=1, source_target_pairs={{0,24},{4,28},{8,16},{12,20},{16,8},{20,12},{24,0},{28,4},{1,25},{... | collective-permute-start | bytes 159752 | tf_op jit(solution)/shard_map/ppermute | solution.py:350
  14.8 0.9 %copy-done.5 = f32[96,144]{1,0:T(8,128)S(1)} copy-done((f32[96,144]{1,0:T(8,128)S(1)}, f32[96,144]{1,0:T(8,128)}, u32[]{:S(2)}) %copy-start.5) | copy-done | bytes 55320
  15.6 0.9 %copy-done.9 = f32[128,288]{1,0:T(8,128)S(1)} copy-done((f32[128,288]{1,0:T(8,128)S(1)}, f32[128,288]{1,0:T(8,128)}, u32[]{:S(2)}) %copy-start.9) | copy-done | bytes 147480
  16.6 1.5 %collective-permute-done.4.refs_5_ = f32[104,128]{1,0:T(8,128)S(1)} collective-permute-done((f32[104,128]{1,0:T(8,128)S(1)}, f32[104,128]{1,0:T(8,128)S(1)}, u32[]{:S(2)}, u32[]{:S(2)}) %collective-permute-start.4) | collective-permute-done | bytes 53280 | tf_op jit(solution)/shard_map/ppermute | solution.py:350
  18.1 3.5 %collective-permute-done.6.refs_7_ = f32[104,128]{1,0:T(8,128)S(1)} collective-permute-done((f32[104,128]{1,0:T(8,128)S(1)}, f32[104,128]{1,0:T(8,128)S(1)}, u32[]{:S(2)}, u32[]{:S(2)}) %collective-permute-start.6) | collective-permute-done | bytes 53280 | tf_op jit(solution)/shard_map/ppermute | solution.py:350
  21.6 4.0 %shard_map.93 = (f32[1152,128]{1,0:T(8,128)S(1)}, f32[864,128]{1,0:T(8,128)S(1)}, f32[8,1024]{1,0:T(8,128)S(1)}) custom-call(f32[104,128]{1,0:T(8,128)S(1)} %get-tuple-element.31.refs_0_, f32[104,128]{1,0:T(8,128)S(1)} %collective-permute-done.refs_1_, f32[104,128]{1,0:T(8,128)S(1)} %collective-permute-done.1.refs_2_, ...), custom_call_target="tpu_custom_call" | custom-call | flops 1000000000 | bytes 527360 | tf_op jit(solution)/shard_map/pallas_call | solution.py:335
  25.7 1.6 %collective-permute-start.7 = (f32[864,128]{1,0:T(8,128)S(1)}, f32[864,128]{1,0:T(8,128)S(1)}, u32[]{:S(2)}, u32[]{:S(2)}) collective-permute-start(f32[864,128]{1,0:T(8,128)S(1)} %get-tuple-element.44), channel_id=1, source_target_pairs={{0,2},{1,3},{2,0},{3,1},{4,6},{5,7},{6,4},{7,5},{8,10},{9,11},{10,... | collective-permute-start | bytes 1327112 | tf_op jit(solution)/shard_map/ppermute | solution.py:393
  27.3 1.2 %shard_map.95.hot_ref = bf16[1024,2304]{1,0:T(8,128)(2,1)S(1)} custom-call(f32[8,1024]{1,0:T(8,128)S(1)} %get-tuple-element.45.columns_ref), custom_call_target="tpu_custom_call" | custom-call | flops 1811939328 | bytes 32768 | tf_op jit(solution)/shard_map/pallas_call | solution.py:335
  28.6 3.6 %shard_map.94.before_ref = f32[1152,128]{1,0:T(8,128)S(1)} custom-call(f32[1152,128]{1,0:T(8,128)S(1)} %get-tuple-element.43.phi_ref, f32[864,128]{1,0:T(8,128)S(1)} %collective-permute-done.8.near_ref, f32[256,256]{1,0:T(8,128)S(1)} %copy-done.3, f32[256,256]{1,0:T(8,128)S(1)} %copy-done.2, f32[96,144]{1,0:T(8,128)S(1)} %copy-done.7, ...), custom_call_target="tpu_custom_call" | custom-call | flops 1811939328 | bytes 2846720 | tf_op jit(solution)/shard_map/pallas_call | solution.py:335
  32.2 6.1 %collective-permute-done.7.ahead_ref = f32[864,128]{1,0:T(8,128)S(1)} collective-permute-done((f32[864,128]{1,0:T(8,128)S(1)}, f32[864,128]{1,0:T(8,128)S(1)}, u32[]{:S(2)}, u32[]{:S(2)}) %collective-permute-start.7) | collective-permute-done | bytes 442400 | tf_op jit(solution)/shard_map/ppermute | solution.py:393
  38.3 1.8 %collective-permute-done.9.across_ref = f32[864,128]{1,0:T(8,128)S(1)} collective-permute-done((f32[864,128]{1,0:T(8,128)S(1)}, f32[864,128]{1,0:T(8,128)S(1)}, u32[]{:S(2)}, u32[]{:S(2)}) %collective-permute-start.9) | collective-permute-done | bytes 442400 | tf_op jit(solution)/shard_map/ppermute | solution.py:406
  40.1 7.9 %shard_map.96 = (f32[96,128]{1,0:T(8,128)S(1)}, f32[96,128]{1,0:T(8,128)S(1)}, f32[96,128]{1,0:T(8,128)S(1)}, f32[96,128]{1,0:T(8,128)S(1)}, f32[96,128]{1,0:T(8...) custom-call(f32[1152,128]{1,0:T(8,128)S(1)} %get-tuple-element.43.phi_ref, ...), custom_call_target="tpu_custom_call" | custom-call | flops 1811939328 | bytes 8744960 | tf_op jit(solution)/shard_map/pallas_call | solution.py:335
  48.6 3.0 %collective-permute-start.12 = (f32[96,128]{1,0:T(8,128)S(1)}, f32[96,128]{1,0:T(8,128)S(1)}, u32[]{:S(2)}, u32[]{:S(2)}) collective-permute-start(f32[96,128]{1,0:T(8,128)S(1)} %get-tuple-element.52), channel_id=1, source_target_pairs={{0,12},{4,8},{8,4},{12,0},{16,28},{20,24},{24,20},{28,16},{1,13},{... | collective-permute-start | bytes 147464 | tf_op jit(solution)/shard_map/ppermute | solution.py:350
  51.5 0.8 %collective-permute-start.13 = (f32[96,128]{1,0:T(8,128)S(1)}, f32[96,128]{1,0:T(8,128)S(1)}, u32[]{:S(2)}, u32[]{:S(2)}) collective-permute-start(f32[96,128]{1,0:T(8,128)S(1)} %get-tuple-element.53), channel_id=1, source_target_pairs={{0,16},{4,20},{8,24},{12,28},{16,0},{20,4},{24,8},{28,12},{1,17},{... | collective-permute-start | bytes 147464 | tf_op jit(solution)/shard_map/ppermute | solution.py:350
  52.4 2.0 %collective-permute-start.14 = (f32[96,128]{1,0:T(8,128)S(1)}, f32[96,128]{1,0:T(8,128)S(1)}, u32[]{:S(2)}, u32[]{:S(2)}) collective-permute-start(f32[96,128]{1,0:T(8,128)S(1)} %get-tuple-element.54), channel_id=1, source_target_pairs={{0,20},{4,16},{8,28},{12,24},{16,4},{20,0},{24,12},{28,8},{1,21},{... | collective-permute-start | bytes 147464 | tf_op jit(solution)/shard_map/ppermute | solution.py:350
  55.1 4.0 %collective-permute-start.16 = (f32[96,128]{1,0:T(8,128)S(1)}, f32[96,128]{1,0:T(8,128)S(1)}, u32[]{:S(2)}, u32[]{:S(2)}) collective-permute-start(f32[96,128]{1,0:T(8,128)S(1)} %get-tuple-element.56), channel_id=1, source_target_pairs={{0,28},{4,24},{8,20},{12,16},{16,12},{20,8},{24,4},{28,0},{1,29},{... | collective-permute-start | bytes 147464 | tf_op jit(solution)/shard_map/ppermute | solution.py:350
  59.2 1.0 %collective-permute-done.14.refs_5_ = f32[96,128]{1,0:T(8,128)S(1)} collective-permute-done((f32[96,128]{1,0:T(8,128)S(1)}, f32[96,128]{1,0:T(8,128)S(1)}, u32[]{:S(2)}, u32[]{:S(2)}) %collective-permute-start.14) | collective-permute-done | bytes 49184 | tf_op jit(solution)/shard_map/ppermute | solution.py:350
  60.4 1.6 %collective-permute-done.16.refs_7_ = f32[96,128]{1,0:T(8,128)S(1)} collective-permute-done((f32[96,128]{1,0:T(8,128)S(1)}, f32[96,128]{1,0:T(8,128)S(1)}, u32[]{:S(2)}, u32[]{:S(2)}) %collective-permute-start.16) | collective-permute-done | bytes 49184 | tf_op jit(solution)/shard_map/ppermute | solution.py:350
  61.9 0.8 %shard_map.97 = f32[8,96,128]{2,1,0:T(8,128)} custom-call(f32[96,128]{1,0:T(8,128)S(1)} %get-tuple-element.49.refs_0_, f32[96,128]{1,0:T(8,128)S(1)} %collective-permute-done.10.refs_1_, f32[96,128]{1,0:T(8,128)S(1)} %collective-permute-done.11.refs_2_, f32[96,128]{1,0:T(8,128)S(1)} %collective-permute-done.12.refs_3_, ...), custom_call_target="tpu_custom_call" | custom-call | flops 1000000 | bytes 393216 | tf_op jit(solution)/shard_map/pallas_call | solution.py:335
  (37 shorter events, 2.9 us)
Async XLA Ops:
  0.0 1.0 %copy-start.1 = (f32[8,96,128]{2,1,0:T(8,128)S(1)}, f32[8,96,128]{2,1,0:T(8,128)}, u32[]{:S(2)}) copy-start(f32[8,96,128]{2,1,0:T(8,128)} %sticks_ref.1) | copy-start | bytes 1179652
  2.2 8.9 %collective-permute-start = (f32[104,128]{1,0:T(8,128)S(1)}, f32[104,128]{1,0:T(8,128)S(1)}, u32[]{:S(2)}, u32[]{:S(2)}) collective-permute-start(f32[104,128]{1,0:T(8,128)S(1)} %get-tuple-element.32), channel_id=1, source_target_pairs={{0,4},{4,0},{8,12},{12,8},{16,20},{20,16},{24,28},{28,24},{1,5},{5... | collective-permute-start | bytes 159752 | tf_op jit(solution)/shard_map/ppermute | solution.py:350
  5.3 9.5 %collective-permute-start.1 = (f32[104,128]{1,0:T(8,128)S(1)}, f32[104,128]{1,0:T(8,128)S(1)}, u32[]{:S(2)}, u32[]{:S(2)}) collective-permute-start(f32[104,128]{1,0:T(8,128)S(1)} %get-tuple-element.33), channel_id=1, source_target_pairs={{0,8},{4,12},{8,0},{12,4},{16,24},{20,28},{24,16},{28,20},{1,9},{5... | collective-permute-start | bytes 159752 | tf_op jit(solution)/shard_map/ppermute | solution.py:350
  6.9 9.7 %collective-permute-start.2 = (f32[104,128]{1,0:T(8,128)S(1)}, f32[104,128]{1,0:T(8,128)S(1)}, u32[]{:S(2)}, u32[]{:S(2)}) collective-permute-start(f32[104,128]{1,0:T(8,128)S(1)} %get-tuple-element.34), channel_id=1, source_target_pairs={{0,12},{4,8},{8,4},{12,0},{16,28},{20,24},{24,20},{28,16},{1,13},{... | collective-permute-start | bytes 159752 | tf_op jit(solution)/shard_map/ppermute | solution.py:350
  6.9 9.7 %collective-permute-start.3 = (f32[104,128]{1,0:T(8,128)S(1)}, f32[104,128]{1,0:T(8,128)S(1)}, u32[]{:S(2)}, u32[]{:S(2)}) collective-permute-start(f32[104,128]{1,0:T(8,128)S(1)} %get-tuple-element.35), channel_id=1, source_target_pairs={{0,16},{4,20},{8,24},{12,28},{16,0},{20,4},{24,8},{28,12},{1,17},{... | collective-permute-start | bytes 159752 | tf_op jit(solution)/shard_map/ppermute | solution.py:350
  9.8 8.2 %collective-permute-start.4 = (f32[104,128]{1,0:T(8,128)S(1)}, f32[104,128]{1,0:T(8,128)S(1)}, u32[]{:S(2)}, u32[]{:S(2)}) collective-permute-start(f32[104,128]{1,0:T(8,128)S(1)} %get-tuple-element.36), channel_id=1, source_target_pairs={{0,20},{4,16},{8,28},{12,24},{16,4},{20,0},{24,12},{28,8},{1,21},{... | collective-permute-start | bytes 159752 | tf_op jit(solution)/shard_map/ppermute | solution.py:350
  11.1 6.9 %collective-permute-start.5 = (f32[104,128]{1,0:T(8,128)S(1)}, f32[104,128]{1,0:T(8,128)S(1)}, u32[]{:S(2)}, u32[]{:S(2)}) collective-permute-start(f32[104,128]{1,0:T(8,128)S(1)} %get-tuple-element.37), channel_id=1, source_target_pairs={{0,24},{4,28},{8,16},{12,20},{16,8},{20,12},{24,0},{28,4},{1,25},{... | collective-permute-start | bytes 159752 | tf_op jit(solution)/shard_map/ppermute | solution.py:350
  14.7 6.8 %collective-permute-start.6 = (f32[104,128]{1,0:T(8,128)S(1)}, f32[104,128]{1,0:T(8,128)S(1)}, u32[]{:S(2)}, u32[]{:S(2)}) collective-permute-start(f32[104,128]{1,0:T(8,128)S(1)} %get-tuple-element.38), channel_id=1, source_target_pairs={{0,28},{4,24},{8,20},{12,16},{16,12},{20,8},{24,4},{28,0},{1,29},{... | collective-permute-start | bytes 159752 | tf_op jit(solution)/shard_map/ppermute | solution.py:350
  21.6 7.0 %copy-start = (f32[2304,128]{1,0:T(8,128)S(1)}, f32[2304,128]{1,0:T(8,128)}, u32[]{:S(2)}) copy-start(f32[2304,128]{1,0:T(8,128)} %constant.20.clone.refs_4_) | copy-start | bytes 3538948
  21.6 7.0 %copy-start.2 = (f32[256,256]{1,0:T(8,128)S(1)}, f32[256,256]{1,0:T(8,128)}, u32[]{:S(2)}) copy-start(f32[256,256]{1,0:T(8,128)} %constant.15.clone.refs_1_) | copy-start | bytes 786436
  21.6 7.0 %copy-start.3 = (f32[256,256]{1,0:T(8,128)S(1)}, f32[256,256]{1,0:T(8,128)}, u32[]{:S(2)}) copy-start(f32[256,256]{1,0:T(8,128)} %constant.14.clone.refs_0_) | copy-start | bytes 786436
  21.6 7.0 %copy-start.6 = (f32[96,144]{1,0:T(8,128)S(1)}, f32[96,144]{1,0:T(8,128)}, u32[]{:S(2)}) copy-start(f32[96,144]{1,0:T(8,128)} %constant.17.clone.refs_1_.refs_3_) | copy-start | bytes 165892
  21.6 7.0 %copy-start.7 = (f32[96,144]{1,0:T(8,128)S(1)}, f32[96,144]{1,0:T(8,128)}, u32[]{:S(2)}) copy-start(f32[96,144]{1,0:T(8,128)} %constant.16.clone.refs_2_) | copy-start | bytes 165892
  25.7 2.9 %collective-permute-start.8 = (f32[864,128]{1,0:T(8,128)S(1)}, f32[864,128]{1,0:T(8,128)S(1)}, u32[]{:S(2)}, u32[]{:S(2)}) collective-permute-start(f32[864,128]{1,0:T(8,128)S(1)} %get-tuple-element.44), channel_id=1, source_target_pairs={{0,1},{1,0},{2,3},{3,2},{4,5},{5,4},{6,7},{7,6},{8,9},{9,8},{10,11... | collective-permute-start | bytes 1327112 | tf_op jit(solution)/shard_map/ppermute | solution.py:395
  25.7 12.6 %collective-permute-start.7 = (f32[864,128]{1,0:T(8,128)S(1)}, f32[864,128]{1,0:T(8,128)S(1)}, u32[]{:S(2)}, u32[]{:S(2)}) collective-permute-start(f32[864,128]{1,0:T(8,128)S(1)} %get-tuple-element.44), channel_id=1, source_target_pairs={{0,2},{1,3},{2,0},{3,1},{4,6},{5,7},{6,4},{7,5},{8,10},{9,11},{10,... | collective-permute-start | bytes 1327112 | tf_op jit(solution)/shard_map/ppermute | solution.py:393
  28.5 11.6 %copy-start.4 = (f32[96,384]{1,0:T(8,128)S(1)}, f32[96,384]{1,0:T(8,128)}, u32[]{:S(2)}) copy-start(f32[96,384]{1,0:T(8,128)} %constant.19.clone.stick_out_ref) | copy-start | bytes 442372
  38.3 1.8 %collective-permute-start.9 = (f32[864,128]{1,0:T(8,128)S(1)}, f32[864,128]{1,0:T(8,128)S(1)}, u32[]{:S(2)}, u32[]{:S(2)}) collective-permute-start(f32[864,128]{1,0:T(8,128)S(1)} %collective-permute-done.7.ahead_ref), channel_id=1, source_target_pairs={{0,1},{1,0},{2,3},{3,2},{4,5},{5,4},{6,7},{7,6},{8,9},{9,8},{10,11... | collective-permute-start | bytes 1327112 | tf_op jit(solution)/shard_map/ppermute | solution.py:406
  48.0 6.4 %collective-permute-start.10 = (f32[96,128]{1,0:T(8,128)S(1)}, f32[96,128]{1,0:T(8,128)S(1)}, u32[]{:S(2)}, u32[]{:S(2)}) collective-permute-start(f32[96,128]{1,0:T(8,128)S(1)} %get-tuple-element.50), channel_id=1, source_target_pairs={{0,4},{4,0},{8,12},{12,8},{16,20},{20,16},{24,28},{28,24},{1,5},{5... | collective-permute-start | bytes 147464 | tf_op jit(solution)/shard_map/ppermute | solution.py:350
  48.6 6.6 %collective-permute-start.11 = (f32[96,128]{1,0:T(8,128)S(1)}, f32[96,128]{1,0:T(8,128)S(1)}, u32[]{:S(2)}, u32[]{:S(2)}) collective-permute-start(f32[96,128]{1,0:T(8,128)S(1)} %get-tuple-element.51), channel_id=1, source_target_pairs={{0,8},{4,12},{8,0},{12,4},{16,24},{20,28},{24,16},{28,20},{1,9},{5... | collective-permute-start | bytes 147464 | tf_op jit(solution)/shard_map/ppermute | solution.py:350
  48.6 10.6 %collective-permute-start.12 = (f32[96,128]{1,0:T(8,128)S(1)}, f32[96,128]{1,0:T(8,128)S(1)}, u32[]{:S(2)}, u32[]{:S(2)}) collective-permute-start(f32[96,128]{1,0:T(8,128)S(1)} %get-tuple-element.52), channel_id=1, source_target_pairs={{0,12},{4,8},{8,4},{12,0},{16,28},{20,24},{24,20},{28,16},{1,13},{... | collective-permute-start | bytes 147464 | tf_op jit(solution)/shard_map/ppermute | solution.py:350
  51.5 7.7 %collective-permute-start.13 = (f32[96,128]{1,0:T(8,128)S(1)}, f32[96,128]{1,0:T(8,128)S(1)}, u32[]{:S(2)}, u32[]{:S(2)}) collective-permute-start(f32[96,128]{1,0:T(8,128)S(1)} %get-tuple-element.53), channel_id=1, source_target_pairs={{0,16},{4,20},{8,24},{12,28},{16,0},{20,4},{24,8},{28,12},{1,17},{... | collective-permute-start | bytes 147464 | tf_op jit(solution)/shard_map/ppermute | solution.py:350
  52.4 7.8 %collective-permute-start.14 = (f32[96,128]{1,0:T(8,128)S(1)}, f32[96,128]{1,0:T(8,128)S(1)}, u32[]{:S(2)}, u32[]{:S(2)}) collective-permute-start(f32[96,128]{1,0:T(8,128)S(1)} %get-tuple-element.54), channel_id=1, source_target_pairs={{0,20},{4,16},{8,28},{12,24},{16,4},{20,0},{24,12},{28,8},{1,21},{... | collective-permute-start | bytes 147464 | tf_op jit(solution)/shard_map/ppermute | solution.py:350
  54.4 5.9 %collective-permute-start.15 = (f32[96,128]{1,0:T(8,128)S(1)}, f32[96,128]{1,0:T(8,128)S(1)}, u32[]{:S(2)}, u32[]{:S(2)}) collective-permute-start(f32[96,128]{1,0:T(8,128)S(1)} %get-tuple-element.55), channel_id=1, source_target_pairs={{0,24},{4,28},{8,16},{12,20},{16,8},{20,12},{24,0},{28,4},{1,25},{... | collective-permute-start | bytes 147464 | tf_op jit(solution)/shard_map/ppermute | solution.py:350
  55.1 6.8 %collective-permute-start.16 = (f32[96,128]{1,0:T(8,128)S(1)}, f32[96,128]{1,0:T(8,128)S(1)}, u32[]{:S(2)}, u32[]{:S(2)}) collective-permute-start(f32[96,128]{1,0:T(8,128)S(1)} %get-tuple-element.56), channel_id=1, source_target_pairs={{0,28},{4,24},{8,20},{12,16},{16,12},{20,8},{24,4},{28,0},{1,29},{... | collective-permute-start | bytes 147464 | tf_op jit(solution)/shard_map/ppermute | solution.py:350
  (3 other events, 2.5 us)

commit v9 on v8

--- a/solution.py
+++ b/solution.py
@@ -13,8 +13,8 @@
 BOX_LENGTH = 18.0
 LANES = 128
 MID = 64
+SEND_GRANT = 60
 PAIRS = 6
-FOLD = 3
 
 F32 = jnp.float32
 BF16 = jnp.bfloat16
@@ -139,21 +139,26 @@
 
 
 def send_kernel(g, sticks_ref, columns_ref, *refs):
-    block_refs, (row_ref, sems, row_sem) = refs[:-3], refs[-3:]
+    block_refs, (row_ref, rows_ref, sems, row_sem) = refs[:-4], refs[-4:]
     own = lax.axis_index("stick")
+    count = len(block_refs)
+    row_copy = pltpu.make_async_copy(columns_ref, row_ref, row_sem)
+    row_copy.start()
     copies = [
         pltpu.make_async_copy(sticks_ref.at[own ^ d], ref.at[pl.ds(0, 2 * g)], sems.at[d])
         for d, ref in enumerate(block_refs)
     ]
-    row_copy = pltpu.make_async_copy(columns_ref, row_ref, row_sem)
-    row_copy.start()
     for copy in copies:
         copy.start()
     row_copy.wait()
-    columns = jnp.broadcast_to(row_ref[...].astype(F32), (8, LANES))
-    for ref in block_refs:
-        ref[2 * g :, :] = columns
-    for copy in copies:
+    rows_ref[...] = jnp.broadcast_to(row_ref[...].astype(F32), rows_ref.shape)
+    row_copies = [
+        pltpu.make_async_copy(rows_ref, ref.at[pl.ds(2 * g, 8)], sems.at[count + d])
+        for d, ref in enumerate(block_refs)
+    ]
+    for copy in row_copies:
+        copy.start()
+    for copy in copies + row_copies:
         copy.wait()
 
 
@@ -170,46 +175,28 @@
         out_ref[own ^ d] = block_ref[...]
 
 
-def fold(field_ref, folded_ref, g):
-    rows = folded_ref.shape[0] // FOLD
-    used = lax.broadcasted_iota(jnp.int32, (rows, LANES), 1) % MID < g
-    last = field_ref[FOLD * rows :, :]
-    width = g // FOLD
-    for k in range(FOLD):
-        part = slice(k * rows, (k + 1) * rows)
-        folded_ref[part, :] = jnp.where(used, field_ref[part, :], pltpu.roll(last, g - k * width, 1))
-
-
-def unfold(folded_ref, field_ref, g):
-    rows = folded_ref.shape[0] // FOLD
-    lane = lax.broadcasted_iota(jnp.int32, (rows, LANES), 1) % MID
-    width = g // FOLD
-    last = None
-    for k in range(FOLD):
-        part = folded_ref[k * rows : (k + 1) * rows, :]
-        field_ref[k * rows : (k + 1) * rows, :] = part
-        piece = pltpu.roll(part, LANES - (g - k * width), 1)
-        last = piece if last is None else jnp.where(lane >= k * width, piece, last)
-    field_ref[FOLD * rows :, :] = last
-
-
 def store(ref, first, slabs):
     g = slabs[0].shape[0]
     for k, slab in enumerate(slabs):
         ref[slab_rows(first + k, g), :] = slab
 
 
-def field_kernel(g, count, *refs):
-    received = refs[:count]
-    stick_in_ref, left_ref, phi_ref, folded_ref, columns_ref, work_a = refs[count:]
-    columns = jnp.concatenate([ref[2 * g : 2 * g + 1, :] for ref in received], 1)
-    columns_ref[...] = jnp.broadcast_to(columns, columns_ref.shape)
-    columns = columns.astype(jnp.int32)
+def relay_kernel(g, *refs):
+    blocks, (coefficients_ref, columns_ref) = refs[:-2], refs[-2:]
+    for k, ref in enumerate(blocks):
+        coefficients_ref[k * 2 * g : (k + 1) * 2 * g, :] = ref[: 2 * g, :]
+        columns_ref[:, k * LANES : (k + 1) * LANES] = ref[2 * g :, :]
+
+
+def field_kernel(g, first_ref, second_ref, first_columns_ref, second_columns_ref, stick_in_ref, left_ref, phi_ref, work_a):
+    columns = beside(first_columns_ref[:1, :], second_columns_ref[:1, :]).astype(jnp.int32)
     stick_in, backward = stick_in_ref[...], left_ref[...]
+    blocks = []
+    for ref in (first_ref, second_ref):
+        blocks += [ref[k : k + 2 * g, :] for k in range(0, ref.shape[0], 2 * g)]
     sticks = []
-    for k in range(0, count, 2):
-        block = beside(received[k][: 2 * g, :], received[k + 1][: 2 * g, :])
-        sticks.append(beside(*split(dot(stick_in, stacked(block)).T)))
+    for k in range(0, len(blocks), 2):
+        sticks.append(beside(*split(dot(stick_in, stacked(beside(blocks[k], blocks[k + 1]))).T)))
     sticks = jnp.concatenate(sticks, 0)
 
     half = g // 2
@@ -226,12 +213,12 @@
         (cos, cos_up), (sin, sin_up) = map(halves, left(backward, x))
         low = lane_halves(cos.shape)
         store(phi_ref, y, [jnp.where(low, cos - turned(sin), turned(cos_up) - sin_up)])
-    fold(phi_ref, folded_ref, g)
-
-
-def pick_kernel(g, columns_ref, hot_ref):
-    for k in range(0, columns_ref.shape[1], LANES):
-        block = columns_ref[:, k : k + LANES]
+
+
+def pick_kernel(g, first_columns_ref, second_columns_ref, hot_ref):
+    columns = beside(first_columns_ref[...], second_columns_ref[...])
+    for k in range(0, columns.shape[1], LANES):
+        block = columns[:, k : k + LANES]
         wanted = jnp.concatenate([block] * (LANES // block.shape[0]), 0).T.astype(jnp.int32)
         for c in range(0, hot_ref.shape[1], LANES):
             index = lax.broadcasted_iota(jnp.int16, (LANES, LANES), 1)
@@ -267,9 +254,8 @@
         emit(start, *regrouped(out[: PAIRS * g], out[PAIRS * g :]))
 
 
-def near_kernel(g, phi_ref, near_ref, *refs):
-    tables, (sum_ref, other_ref, work_a, work_b) = refs[:5], refs[5:]
-    unfold(near_ref, other_ref, g)
+def near_kernel(g, phi_ref, other_ref, *refs):
+    tables, (sum_ref, work_a, work_b) = refs[:5], refs[5:]
 
     def emit(start, own, other):
         rows = slab_rows(start, g, PAIRS)
@@ -278,10 +264,8 @@
     potentials(g, phi_ref, phi_ref, other_ref, tables, work_a, work_b, emit)
 
 
-def middle_kernel(g, phi_ref, ahead_ref, behind_ref, before_ref, *refs):
-    tables, (sum_ref, first_ref, second_ref, work_a, work_b) = refs[:5], refs[5:]
-    unfold(ahead_ref, first_ref, g)
-    unfold(behind_ref, second_ref, g)
+def middle_kernel(g, phi_ref, first_ref, second_ref, before_ref, *refs):
+    tables, (sum_ref, work_a, work_b) = refs[:5], refs[5:]
 
     def emit(start, first, second):
         rows = slab_rows(start, g, PAIRS)
@@ -290,11 +274,9 @@
     potentials(g, phi_ref, first_ref, second_ref, tables, work_a, work_b, emit)
 
 
-def far_kernel(g, weights, phi_ref, ahead_ref, across_ref, before_ref, hot_ref, stick_out_ref, *refs):
-    tables, out_refs = refs[:5], refs[5:-5]
-    first_ref, second_ref, work_a, work_b, picked_ref = refs[-5:]
-    unfold(ahead_ref, first_ref, g)
-    unfold(across_ref, second_ref, g)
+def far_kernel(g, weights, phi_ref, first_ref, second_ref, before_ref, hot_ref, stick_out_ref, *refs):
+    tables, out_refs = refs[:5], refs[5:-3]
+    work_a, work_b, picked_ref = refs[-3:]
     forward = tables[2][...].astype(BF16)
     half = g // 2
 
@@ -329,16 +311,16 @@
         out_refs[k][...], out_refs[k + 1][...] = halves(out)
 
 
-def call(kernel, out_shapes, scratch, flops, *operands, space=pltpu.VMEM):
-    vmem = pl.BlockSpec(memory_space=pltpu.VMEM)
+def call(kernel, out_shapes, scratch, flops, *operands, space=pltpu.VMEM, out_space=pltpu.VMEM, grant=40):
     moved = sum(x.size * x.dtype.itemsize for x in operands)
+    out_spec = pl.BlockSpec(memory_space=out_space)
     return pl.pallas_call(
         kernel,
         out_shape=out_shapes,
         in_specs=[pl.BlockSpec(memory_space=space)] * len(operands),
-        out_specs=jax.tree.map(lambda _: vmem, out_shapes),
+        out_specs=jax.tree.map(lambda _: out_spec, out_shapes),
         scratch_shapes=scratch,
-        compiler_params=pltpu.CompilerParams(vmem_limit_bytes=40 * 2**20),
+        compiler_params=pltpu.CompilerParams(vmem_limit_bytes=grant * 2**20),
         cost_estimate=pl.CostEstimate(flops=flops, bytes_accessed=moved, transcendentals=0),
     )(*operands)
 
@@ -359,71 +341,78 @@
     t = {name: jnp.asarray(value) for name, value in make_tables(g).items()}
     rows = g * g
     field = jax.ShapeDtypeStruct((rows // 2, LANES), F32)
-    folded = jax.ShapeDtypeStruct((rows // 2 * FOLD // (FOLD + 1), LANES), F32)
-    field_scratch = pltpu.VMEM((rows // 2, LANES), F32)
     work = pltpu.VMEM((rows, LANES), F32)
     pot_flops = 6 * 2 * rows * 256 * 256
+
+    def shifted(x, distance):
+        return lax.ppermute(x, "band", [(i, (i - distance) % groups) for i in range(groups)])
+
+    def swapped(x):
+        return lax.ppermute(x, "band", [(i, i ^ 1) for i in range(groups)])
 
     sent = call(
         functools.partial(send_kernel, g),
         [jax.ShapeDtypeStruct((2 * g + 8, slots), F32)] * owners,
-        [pltpu.VMEM((1, slots), jnp.int32), pltpu.SemaphoreType.DMA((owners,)), pltpu.SemaphoreType.DMA],
+        [
+            pltpu.VMEM((1, slots), jnp.int32),
+            pltpu.VMEM((8, slots), F32),
+            pltpu.SemaphoreType.DMA((2 * owners,)),
+            pltpu.SemaphoreType.DMA,
+        ],
         10**6,
         sticks,
         stick_columns[None, :],
         space=pltpu.HBM,
+        out_space=pltpu.HBM,
+        grant=SEND_GRANT,
     )
     received = exchanged(sent)
     first_tables = lax.optimization_barrier((t["stick_in"], t["left_backward"], sent[0]))[:2]
     first_tables = call(
         table_kernel, [jax.ShapeDtypeStruct(x.shape, BF16) for x in first_tables], [], 10**9, *first_tables
     )
-    phi, packed, columns = call(
-        functools.partial(field_kernel, g, owners),
-        [field, folded, jax.ShapeDtypeStruct((8, owners * slots), F32)],
-        [work],
-        10**9,
-        *received,
-        *first_tables,
-    )
+
+    half = owners // 2
+    order = [0] + list(range(half, owners)) + list(range(1, half))
+    relays, columns = [], []
+    for part in (order[: half + 1], order[half + 1 :]):
+        shapes = [(len(part) * 2 * g, slots), (8, len(part) * slots)]
+        shapes = [jax.ShapeDtypeStruct(shape, F32) for shape in shapes]
+        relay, column = call(functools.partial(relay_kernel, g), shapes, [], 10**6, *[received[d] for d in part])
+        relays.append(relay)
+        columns.append(column)
+
+    def orbital(blocks):
+        return call(functools.partial(field_kernel, g), field, [work], 10**9, *blocks, *columns, *first_tables)
+
+    phi = orbital(relays)
+    near = swapped(phi)
+    hot = call(
+        functools.partial(pick_kernel, g), jax.ShapeDtypeStruct((owners * slots, rows), BF16), [], pot_flops, *columns
+    )
+    distances = (HALF,) if groups == 2 * HALF else (HALF, -HALF)
+    fields = [orbital([shifted(x, distance) for x in relays]) for distance in distances]
     pot_tables = [t["forward"], t["last_backward"], t["left_forward"], t["left_backward"], t["coulomb"]]
-    swap = [(i, i ^ 1) for i in range(groups)]
-
-    def fetched(distance):
-        return lax.ppermute(packed, "band", [(i, (i - distance) % groups) for i in range(groups)])
-
-    near = lax.ppermute(packed, "band", swap)
-    ahead = fetched(HALF)
-    total = call(
-        functools.partial(near_kernel, g), field, [field_scratch, work, work], pot_flops, phi, near, *pot_tables
-    )
-    hot = call(
-        functools.partial(pick_kernel, g), jax.ShapeDtypeStruct((owners * slots, rows), BF16), [], pot_flops, columns
-    )
-    ahead, total, hot = lax.optimization_barrier((ahead, total, hot))
+
+    def potential_sum(kernel, *operands):
+        return call(functools.partial(kernel, g), field, [work, work], pot_flops, phi, *operands, *pot_tables)
+
     if groups == 2 * HALF:
         weights = (2.0, 1.0)
-        first, second = ahead, lax.ppermute(ahead, "band", swap)
+        first, second = fields[0], swapped(fields[0])
+        near, first = lax.optimization_barrier((near, first))
+        total = potential_sum(near_kernel, near)
     else:
         weights = (1.0, 0.0)
-        behind = fetched(-HALF)
         odd = lax.axis_index("band") % 2 == 1
-        first = second = lax.ppermute(jnp.where(odd, behind, ahead), "band", swap)
-        total = call(
-            functools.partial(middle_kernel, g),
-            field,
-            [field_scratch, field_scratch, work, work],
-            pot_flops,
-            phi,
-            ahead,
-            behind,
-            total,
-            *pot_tables,
-        )
+        first = second = swapped(jnp.where(odd, fields[1], fields[0]))
+        total = potential_sum(near_kernel, near)
+        total = potential_sum(middle_kernel, *fields, total)
+    order_back = {d: k for k, d in enumerate(order)}
     result = call(
         functools.partial(far_kernel, g, weights),
         [jax.ShapeDtypeStruct((2 * g, slots), F32)] * owners,
-        [field_scratch, field_scratch, work, work, pltpu.VMEM((owners * slots, LANES), F32)],
+        [work, work, pltpu.VMEM((owners * slots, LANES), F32)],
         pot_flops,
         phi,
         first,
@@ -433,6 +422,7 @@
         t["stick_out"],
         *pot_tables,
     )
+    result = [result[order_back[d]] for d in range(owners)]
     return call(place_kernel, jax.ShapeDtypeStruct(sticks.shape, F32), [], 10**6, *exchanged(result))
 
 

time: 62.9 us -> 73.8 us (1.17)
  Pallas kernels: 18.1 us -> 34.8 us
  waiting for transfers between devices: 15.6 us -> 10.9 us
  local copies, waits for them, and re-layouts: 3.5 us -> 2.67 us
    pallas_call x7 -> x10, Pallas kernels: 18.1 us -> 34.8 us  [call(): pl.pallas_call(kernel, out_shape=out_shapes, in_specs=[pl.BlockSpec(memor...]
    ppermute x3 -> x4, waiting for transfers between devices: 7.91 us -> 1.21 us  [the longest x2 1.21 us: shifted(): lax.ppermute(x, 'band', [(i, (i - distance) % groups) for i in range(grou...]
    ppermute x14, waiting for transfers between devices: 7.71 us -> 9.65 us  [exchanged(): lax.ppermute(blocks[d], 'stick', [(i, i ^ d) for i in range(owners)])]
    ppermute x14, starting transfers between devices: 23.7 us -> 22.8 us  [exchanged(): lax.ppermute(blocks[d], 'stick', [(i, i ^ d) for i in range(owners)])]
    unnamed x20 -> x18, local copies, waits for them, and re-layouts: 3.5 us -> 2.67 us
    ppermute x3 -> x4, starting transfers between devices: 1.63 us -> 2.3 us  [the longest x2 2.16 us: shifted(): lax.ppermute(x, 'band', [(i, (i - distance) % groups) for i in range(grou...]
  transfers between devices with their start and end apart: 17 -> 18, of which waited for: 7 -> 5; matrix products, arithmetic and copies ran while one was open for 0% -> 0% of each run, Pallas kernels for 8% -> 18%
where the time goes in v9:
time: 73.8 us; the launch traced here: 73.6 us
  Pallas kernels  34.8 us (47%)
  starting transfers between devices  25.1 us (34%)
  waiting for transfers between devices  10.9 us (15%)
  local copies, waits for them, and re-layouts  2.67 us (4%)
    pallas_call x10, Pallas kernels, call(): pl.pallas_call(kernel, out_shape=out_shapes, in_specs=[pl.BlockSpec(memor...  34.8 us
    ppermute x14, starting transfers between devices, exchanged(): lax.ppermute(blocks[d], 'stick', [(i, i ^ d) for i in range(owners)])  22.8 us
    ppermute x14, waiting for transfers between devices, exchanged(): lax.ppermute(blocks[d], 'stick', [(i, i ^ d) for i in range(owners)])  9.65 us
    unnamed x18, local copies, waits for them, and re-layouts  2.67 us
    ppermute x2, starting transfers between devices, shifted(): lax.ppermute(x, 'band', [(i, (i - distance) % groups) for i in range(grou...  2.16 us
  transfers between devices with their start and end apart: 18, of which 5 were waited for; matrix products, arithmetic and copies ran while one was open for 0% of the time, Pallas kernels for 18%

profile of v9, /device:TPU:0, one launch (start us, length us, event | category | flops | bytes accessed | tf_op | source)
XLA Modules:
  0.0 73.6 jit_solution(6138050472584672037)
XLA Ops:
  0.0 13.2 %shard_map.91 = (f32[104,128]{1,0:T(8,128)}, f32[104,128]{1,0:T(8,128)}, f32[104,128]{1,0:T(8,128)}, f32[104,128]{1,0:T(8,128)}, f32[104,128]{1,0:T(8,128)}, /*i...) custom-call(f32[8,96,128]{2,1,0:T(8,128)} %sticks_ref.1, s32[1,128]{1,0:T(1,128)} %bitcast.1), custom_call_target="tpu_custom_call" | custom-call | flops 1000000 | bytes 393728 | tf_op jit(solution)/shard_map/pallas_call | solution.py:317
  13.2 4.1 %collective-permute-start = (f32[104,128]{1,0:T(8,128)}, f32[104,128]{1,0:T(8,128)S(1)}, u32[]{:S(2)}, u32[]{:S(2)}) collective-permute-start(f32[104,128]{1,0:T(8,128)} %get-tuple-element.32), channel_id=1, source_target_pairs={{0,16},{4,20},{8,24},{12,28},{16,0},{20,4},{24,8},{28,12},{1,17},{... | collective-permute-start | bytes 159752 | tf_op jit(solution)/shard_map/ppermute | solution.py:332
  17.3 1.3 %collective-permute-start.1 = (f32[104,128]{1,0:T(8,128)}, f32[104,128]{1,0:T(8,128)S(1)}, u32[]{:S(2)}, u32[]{:S(2)}) collective-permute-start(f32[104,128]{1,0:T(8,128)} %get-tuple-element.33), channel_id=1, source_target_pairs={{0,20},{4,16},{8,28},{12,24},{16,4},{20,0},{24,12},{28,8},{1,21},{... | collective-permute-start | bytes 159752 | tf_op jit(solution)/shard_map/ppermute | solution.py:332
  18.6 3.6 %collective-permute-start.2 = (f32[104,128]{1,0:T(8,128)}, f32[104,128]{1,0:T(8,128)S(1)}, u32[]{:S(2)}, u32[]{:S(2)}) collective-permute-start(f32[104,128]{1,0:T(8,128)} %get-tuple-element.34), channel_id=1, source_target_pairs={{0,24},{4,28},{8,16},{12,20},{16,8},{20,12},{24,0},{28,4},{1,25},{... | collective-permute-start | bytes 159752 | tf_op jit(solution)/shard_map/ppermute | solution.py:332
  22.2 1.7 %collective-permute-start.4 = (f32[104,128]{1,0:T(8,128)}, f32[104,128]{1,0:T(8,128)S(1)}, u32[]{:S(2)}, u32[]{:S(2)}) collective-permute-start(f32[104,128]{1,0:T(8,128)} %get-tuple-element.37), channel_id=1, source_target_pairs={{0,4},{4,0},{8,12},{12,8},{16,20},{20,16},{24,28},{28,24},{1,5},{5... | collective-permute-start | bytes 159752 | tf_op jit(solution)/shard_map/ppermute | solution.py:332
  23.9 2.2 %collective-permute-done.1.refs_2_ = f32[104,128]{1,0:T(8,128)S(1)} collective-permute-done((f32[104,128]{1,0:T(8,128)}, f32[104,128]{1,0:T(8,128)S(1)}, u32[]{:S(2)}, u32[]{:S(2)}) %collective-permute-start.1) | collective-permute-done | bytes 53280 | tf_op jit(solution)/shard_map/ppermute | solution.py:332
  26.3 2.9 %collective-permute-done.3.refs_4_ = f32[104,128]{1,0:T(8,128)S(1)} collective-permute-done((f32[104,128]{1,0:T(8,128)}, f32[104,128]{1,0:T(8,128)S(1)}, u32[]{:S(2)}, u32[]{:S(2)}) %collective-permute-start.3) | collective-permute-done | bytes 53280 | tf_op jit(solution)/shard_map/ppermute | solution.py:332
  29.2 0.8 %copy-done.7 = f32[104,128]{1,0:T(8,128)S(1)} copy-done((f32[104,128]{1,0:T(8,128)S(1)}, f32[104,128]{1,0:T(8,128)}, u32[]{:S(2)}) %copy-start.7) | copy-done | bytes 53272
  30.1 1.6 %collective-permute-start.8 = (f32[480,128]{1,0:T(8,128)S(1)}, f32[480,128]{1,0:T(8,128)S(1)}, u32[]{:S(2)}, u32[]{:S(2)}) collective-permute-start(f32[480,128]{1,0:T(8,128)S(1)} %get-tuple-element.36.first_ref), channel_id=1, source_target_pairs={{0,2},{1,3},{2,0},{3,1},{4,6},{5,7},{6,4},{7,5},{8,10},{9,11},{10,... | collective-permute-start | bytes 737288 | tf_op jit(solution)/shard_map/ppermute | solution.py:348
  31.6 0.9 %copy-done.4 = f32[96,144]{1,0:T(8,128)S(1)} copy-done((f32[96,144]{1,0:T(8,128)S(1)}, f32[96,144]{1,0:T(8,128)}, u32[]{:S(2)}) %copy-start.4) | copy-done | bytes 55320
  32.5 0.9 %copy-done.8 = f32[128,288]{1,0:T(8,128)S(1)} copy-done((f32[128,288]{1,0:T(8,128)S(1)}, f32[128,288]{1,0:T(8,128)}, u32[]{:S(2)}) %copy-start.8) | copy-done | bytes 147480
  34.1 4.0 %shard_map.95.phi_ref = f32[1152,128]{1,0:T(8,128)S(1)} custom-call(f32[480,128]{1,0:T(8,128)S(1)} %get-tuple-element.36.first_ref, f32[288,128]{1,0:T(8,128)S(1)} %get-tuple-element.40.second_ref, f32[8,640]{1,0:T(8,128)S(1)} %get-tuple-element.41.first_columns_ref, f32[8,384]{1,0:T(8,128)S(1)} %get-tuple-element.42.second_columns_ref, ...), custom_call_target="tpu_custom_call" | custom-call | flops 1000000000 | bytes 527360 | tf_op jit(solution)/shard_map/pallas_call | solution.py:317
  38.3 1.2 %collective-permute-done.9.second_ref = f32[288,128]{1,0:T(8,128)S(1)} collective-permute-done((f32[288,128]{1,0:T(8,128)S(1)}, f32[288,128]{1,0:T(8,128)S(1)}, u32[]{:S(2)}, u32[]{:S(2)}) %collective-permute-start.9) | collective-permute-done | bytes 147488 | tf_op jit(solution)/shard_map/ppermute | solution.py:348
  39.5 4.0 %shard_map.96.first_ref = f32[1152,128]{1,0:T(8,128)S(1)} custom-call(f32[480,128]{1,0:T(8,128)S(1)} %collective-permute-done.8.first_ref, f32[288,128]{1,0:T(8,128)S(1)} %collective-permute-done.9.second_ref, f32[8,640]{1,0:T(8,128)S(1)} %get-tuple-element.41.first_columns_ref, f32[8,384]{1,0:T(8,128)S(1)} %get-tuple-element.42.second_columns_ref, ...), custom_call_target="tpu_custom_call" | custom-call | flops 1000000000 | bytes 527360 | tf_op jit(solution)/shard_map/pallas_call | solution.py:317
  43.6 1.2 %shard_map.98.hot_ref = bf16[1024,2304]{1,0:T(8,128)(2,1)S(1)} custom-call(f32[8,640]{1,0:T(8,128)S(1)} %get-tuple-element.41.first_columns_ref, f32[8,384]{1,0:T(8,128)S(1)} %get-tuple-element.42.second_columns_ref), custom_call_target="tpu_custom_call" | custom-call | flops 1811939328 | bytes 32768 | tf_op jit(solution)/shard_map/pallas_call | solution.py:317
  44.9 3.6 %shard_map.97.before_ref = f32[1152,128]{1,0:T(8,128)S(1)} custom-call(f32[1152,128]{1,0:T(8,128)S(1)} %shard_map.95.phi_ref, f32[1152,128]{1,0:T(8,128)S(1)} %collective-permute-done.7.other_ref, f32[256,256]{1,0:T(8,128)S(1)} %copy-done.2, f32[256,256]{1,0:T(8,128)S(1)} %copy-done.1, f32[96,144]{1,0:T(8,128)S(1)} %copy-done.6, f32[96,144]{1,0:T(8,128)S(1)} %copy-done.5, ...), custom_call_target="tpu_custom_call" | custom-call | flops 1811939328 | bytes 2994176 | tf_op jit(solution)/shard_map/pallas_call | solution.py:317
  48.5 7.9 %shard_map.99 = (f32[96,128]{1,0:T(8,128)S(1)}, f32[96,128]{1,0:T(8,128)S(1)}, f32[96,128]{1,0:T(8,128)S(1)}, f32[96,128]{1,0:T(8,128)S(1)}, f32[96,128]{1,0:T(8...) custom-call(f32[1152,128]{1,0:T(8,128)S(1)} %shard_map.95.phi_ref, ...), custom_call_target="tpu_custom_call" | custom-call | flops 1811939328 | bytes 9039872 | tf_op jit(solution)/shard_map/pallas_call | solution.py:317
  57.1 1.5 %collective-permute-start.12 = (f32[96,128]{1,0:T(8,128)S(1)}, f32[96,128]{1,0:T(8,128)S(1)}, u32[]{:S(2)}, u32[]{:S(2)}) collective-permute-start(f32[96,128]{1,0:T(8,128)S(1)} %get-tuple-element.51), channel_id=1, source_target_pairs={{0,8},{4,12},{8,0},{12,4},{16,24},{20,28},{24,16},{28,20},{1,9},{5... | collective-permute-start | bytes 147464 | tf_op jit(solution)/shard_map/ppermute | solution.py:332
  58.6 1.4 %collective-permute-start.13 = (f32[96,128]{1,0:T(8,128)S(1)}, f32[96,128]{1,0:T(8,128)S(1)}, u32[]{:S(2)}, u32[]{:S(2)}) collective-permute-start(f32[96,128]{1,0:T(8,128)S(1)} %get-tuple-element.52), channel_id=1, source_target_pairs={{0,12},{4,8},{8,4},{12,0},{16,28},{20,24},{24,20},{28,16},{1,13},{... | collective-permute-start | bytes 147464 | tf_op jit(solution)/shard_map/ppermute | solution.py:332
  60.0 3.6 %collective-permute-start.14 = (f32[96,128]{1,0:T(8,128)S(1)}, f32[96,128]{1,0:T(8,128)S(1)}, u32[]{:S(2)}, u32[]{:S(2)}) collective-permute-start(f32[96,128]{1,0:T(8,128)S(1)} %get-tuple-element.53), channel_id=1, source_target_pairs={{0,16},{4,20},{8,24},{12,28},{16,0},{20,4},{24,8},{28,12},{1,17},{... | collective-permute-start | bytes 147464 | tf_op jit(solution)/shard_map/ppermute | solution.py:332
  63.5 2.4 %collective-permute-start.16 = (f32[96,128]{1,0:T(8,128)S(1)}, f32[96,128]{1,0:T(8,128)S(1)}, u32[]{:S(2)}, u32[]{:S(2)}) collective-permute-start(f32[96,128]{1,0:T(8,128)S(1)} %get-tuple-element.55), channel_id=1, source_target_pairs={{0,24},{4,28},{8,16},{12,20},{16,8},{20,12},{24,0},{28,4},{1,25},{... | collective-permute-start | bytes 147464 | tf_op jit(solution)/shard_map/ppermute | solution.py:332
  65.9 2.4 %collective-permute-start.17 = (f32[96,128]{1,0:T(8,128)S(1)}, f32[96,128]{1,0:T(8,128)S(1)}, u32[]{:S(2)}, u32[]{:S(2)}) collective-permute-start(f32[96,128]{1,0:T(8,128)S(1)} %get-tuple-element.56), channel_id=1, source_target_pairs={{0,28},{4,24},{8,20},{12,16},{16,12},{20,8},{24,4},{28,0},{1,29},{... | collective-permute-start | bytes 147464 | tf_op jit(solution)/shard_map/ppermute | solution.py:332
  68.3 3.3 %collective-permute-done.15.refs_5_ = f32[96,128]{1,0:T(8,128)S(1)} collective-permute-done((f32[96,128]{1,0:T(8,128)S(1)}, f32[96,128]{1,0:T(8,128)S(1)}, u32[]{:S(2)}, u32[]{:S(2)}) %collective-permute-start.15) | collective-permute-done | bytes 49184 | tf_op jit(solution)/shard_map/ppermute | solution.py:332
  71.5 1.3 %collective-permute-done.17.refs_7_ = f32[96,128]{1,0:T(8,128)S(1)} collective-permute-done((f32[96,128]{1,0:T(8,128)S(1)}, f32[96,128]{1,0:T(8,128)S(1)}, u32[]{:S(2)}, u32[]{:S(2)}) %collective-permute-start.17) | collective-permute-done | bytes 49184 | tf_op jit(solution)/shard_map/ppermute | solution.py:332
  (40 shorter events, 2.6 us)
Async XLA Ops:
  13.2 10.7 %collective-permute-start = (f32[104,128]{1,0:T(8,128)}, f32[104,128]{1,0:T(8,128)S(1)}, u32[]{:S(2)}, u32[]{:S(2)}) collective-permute-start(f32[104,128]{1,0:T(8,128)} %get-tuple-element.32), channel_id=1, source_target_pairs={{0,16},{4,20},{8,24},{12,28},{16,0},{20,4},{24,8},{28,12},{1,17},{... | collective-permute-start | bytes 159752 | tf_op jit(solution)/shard_map/ppermute | solution.py:332
  17.3 8.7 %collective-permute-start.1 = (f32[104,128]{1,0:T(8,128)}, f32[104,128]{1,0:T(8,128)S(1)}, u32[]{:S(2)}, u32[]{:S(2)}) collective-permute-start(f32[104,128]{1,0:T(8,128)} %get-tuple-element.33), channel_id=1, source_target_pairs={{0,20},{4,16},{8,28},{12,24},{16,4},{20,0},{24,12},{28,8},{1,21},{... | collective-permute-start | bytes 159752 | tf_op jit(solution)/shard_map/ppermute | solution.py:332
  18.6 7.7 %collective-permute-start.2 = (f32[104,128]{1,0:T(8,128)}, f32[104,128]{1,0:T(8,128)S(1)}, u32[]{:S(2)}, u32[]{:S(2)}) collective-permute-start(f32[104,128]{1,0:T(8,128)} %get-tuple-element.34), channel_id=1, source_target_pairs={{0,24},{4,28},{8,16},{12,20},{16,8},{20,12},{24,0},{28,4},{1,25},{... | collective-permute-start | bytes 159752 | tf_op jit(solution)/shard_map/ppermute | solution.py:332
  22.2 7.0 %collective-permute-start.3 = (f32[104,128]{1,0:T(8,128)}, f32[104,128]{1,0:T(8,128)S(1)}, u32[]{:S(2)}, u32[]{:S(2)}) collective-permute-start(f32[104,128]{1,0:T(8,128)} %get-tuple-element.35), channel_id=1, source_target_pairs={{0,28},{4,24},{8,20},{12,16},{16,12},{20,8},{24,4},{28,0},{1,29},{... | collective-permute-start | bytes 159752 | tf_op jit(solution)/shard_map/ppermute | solution.py:332
  22.2 11.3 %collective-permute-start.4 = (f32[104,128]{1,0:T(8,128)}, f32[104,128]{1,0:T(8,128)S(1)}, u32[]{:S(2)}, u32[]{:S(2)}) collective-permute-start(f32[104,128]{1,0:T(8,128)} %get-tuple-element.37), channel_id=1, source_target_pairs={{0,4},{4,0},{8,12},{12,8},{16,20},{20,16},{24,28},{28,24},{1,5},{5... | collective-permute-start | bytes 159752 | tf_op jit(solution)/shard_map/ppermute | solution.py:332
  23.9 9.6 %collective-permute-start.5 = (f32[104,128]{1,0:T(8,128)}, f32[104,128]{1,0:T(8,128)S(1)}, u32[]{:S(2)}, u32[]{:S(2)}) collective-permute-start(f32[104,128]{1,0:T(8,128)} %get-tuple-element.38), channel_id=1, source_target_pairs={{0,8},{4,12},{8,0},{12,4},{16,24},{20,28},{24,16},{28,20},{1,9},{5... | collective-permute-start | bytes 159752 | tf_op jit(solution)/shard_map/ppermute | solution.py:332
  26.0 7.4 %collective-permute-start.6 = (f32[104,128]{1,0:T(8,128)}, f32[104,128]{1,0:T(8,128)S(1)}, u32[]{:S(2)}, u32[]{:S(2)}) collective-permute-start(f32[104,128]{1,0:T(8,128)} %get-tuple-element.39), channel_id=1, source_target_pairs={{0,12},{4,8},{8,4},{12,0},{16,28},{20,24},{24,20},{28,16},{1,13},{... | collective-permute-start | bytes 159752 | tf_op jit(solution)/shard_map/ppermute | solution.py:332
  30.1 9.4 %collective-permute-start.8 = (f32[480,128]{1,0:T(8,128)S(1)}, f32[480,128]{1,0:T(8,128)S(1)}, u32[]{:S(2)}, u32[]{:S(2)}) collective-permute-start(f32[480,128]{1,0:T(8,128)S(1)} %get-tuple-element.36.first_ref), channel_id=1, source_target_pairs={{0,2},{1,3},{2,0},{3,1},{4,6},{5,7},{6,4},{7,5},{8,10},{9,11},{10,... | collective-permute-start | bytes 737288 | tf_op jit(solution)/shard_map/ppermute | solution.py:348
  33.5 6.0 %collective-permute-start.9 = (f32[288,128]{1,0:T(8,128)S(1)}, f32[288,128]{1,0:T(8,128)S(1)}, u32[]{:S(2)}, u32[]{:S(2)}) collective-permute-start(f32[288,128]{1,0:T(8,128)S(1)} %get-tuple-element.40.second_ref), channel_id=1, source_target_pairs={{0,2},{1,3},{2,0},{3,1},{4,6},{5,7},{6,4},{7,5},{8,10},{9,11},{10,... | collective-permute-start | bytes 442376 | tf_op jit(solution)/shard_map/ppermute | solution.py:348
  38.1 6.7 %copy-start = (f32[2304,128]{1,0:T(8,128)S(1)}, f32[2304,128]{1,0:T(8,128)}, u32[]{:S(2)}) copy-start(f32[2304,128]{1,0:T(8,128)} %constant.20.clone.refs_4_) | copy-start | bytes 3538948
  38.1 6.7 %copy-start.1 = (f32[256,256]{1,0:T(8,128)S(1)}, f32[256,256]{1,0:T(8,128)}, u32[]{:S(2)}) copy-start(f32[256,256]{1,0:T(8,128)} %constant.15.clone.refs_1_) | copy-start | bytes 786436
  38.2 6.7 %copy-start.2 = (f32[256,256]{1,0:T(8,128)S(1)}, f32[256,256]{1,0:T(8,128)}, u32[]{:S(2)}) copy-start(f32[256,256]{1,0:T(8,128)} %constant.14.clone.refs_0_) | copy-start | bytes 786436
  38.2 6.7 %copy-start.5 = (f32[96,144]{1,0:T(8,128)S(1)}, f32[96,144]{1,0:T(8,128)}, u32[]{:S(2)}) copy-start(f32[96,144]{1,0:T(8,128)} %constant.17.clone.refs_1_.refs_3_) | copy-start | bytes 165892
  38.2 6.7 %copy-start.6 = (f32[96,144]{1,0:T(8,128)S(1)}, f32[96,144]{1,0:T(8,128)}, u32[]{:S(2)}) copy-start(f32[96,144]{1,0:T(8,128)} %constant.16.clone.refs_2_) | copy-start | bytes 165892
  38.2 6.6 %collective-permute-start.7 = (f32[1152,128]{1,0:T(8,128)S(1)}, f32[1152,128]{1,0:T(8,128)S(1)}, u32[]{:S(2)}, u32[]{:S(2)}) collective-permute-start(f32[1152,128]{1,0:T(8,128)S(1)} %shard_map.95.phi_ref), channel_id=1, source_target_pairs={{0,1},{1,0},{2,3},{3,2},{4,5},{5,4},{6,7},{7,6},{8,9},{9,8},{10,11... | collective-permute-start | bytes 1769480 | tf_op jit(solution)/shard_map/ppermute | solution.py:351
  43.5 5.0 %collective-permute-start.10 = (f32[1152,128]{1,0:T(8,128)S(1)}, f32[1152,128]{1,0:T(8,128)S(1)}, u32[]{:S(2)}, u32[]{:S(2)}) collective-permute-start(f32[1152,128]{1,0:T(8,128)S(1)} %shard_map.96.first_ref), channel_id=1, source_target_pairs={{0,1},{1,0},{2,3},{3,2},{4,5},{5,4},{6,7},{7,6},{8,9},{9,8},{10,11... | collective-permute-start | bytes 1769480 | tf_op jit(solution)/shard_map/ppermute | solution.py:351
  44.8 3.7 %copy-start.3 = (f32[96,384]{1,0:T(8,128)S(1)}, f32[96,384]{1,0:T(8,128)}, u32[]{:S(2)}) copy-start(f32[96,384]{1,0:T(8,128)} %constant.19.clone.stick_out_ref) | copy-start | bytes 442372
  56.4 7.1 %collective-permute-start.11 = (f32[96,128]{1,0:T(8,128)S(1)}, f32[96,128]{1,0:T(8,128)S(1)}, u32[]{:S(2)}, u32[]{:S(2)}) collective-permute-start(f32[96,128]{1,0:T(8,128)S(1)} %get-tuple-element.50), channel_id=1, source_target_pairs={{0,4},{4,0},{8,12},{12,8},{16,20},{20,16},{24,28},{28,24},{1,5},{5... | collective-permute-start | bytes 147464 | tf_op jit(solution)/shard_map/ppermute | solution.py:332
  57.1 8.8 %collective-permute-start.12 = (f32[96,128]{1,0:T(8,128)S(1)}, f32[96,128]{1,0:T(8,128)S(1)}, u32[]{:S(2)}, u32[]{:S(2)}) collective-permute-start(f32[96,128]{1,0:T(8,128)S(1)} %get-tuple-element.51), channel_id=1, source_target_pairs={{0,8},{4,12},{8,0},{12,4},{16,24},{20,28},{24,16},{28,20},{1,9},{5... | collective-permute-start | bytes 147464 | tf_op jit(solution)/shard_map/ppermute | solution.py:332
  58.6 9.7 %collective-permute-start.13 = (f32[96,128]{1,0:T(8,128)S(1)}, f32[96,128]{1,0:T(8,128)S(1)}, u32[]{:S(2)}, u32[]{:S(2)}) collective-permute-start(f32[96,128]{1,0:T(8,128)S(1)} %get-tuple-element.52), channel_id=1, source_target_pairs={{0,12},{4,8},{8,4},{12,0},{16,28},{20,24},{24,20},{28,16},{1,13},{... | collective-permute-start | bytes 147464 | tf_op jit(solution)/shard_map/ppermute | solution.py:332
  60.0 8.3 %collective-permute-start.14 = (f32[96,128]{1,0:T(8,128)S(1)}, f32[96,128]{1,0:T(8,128)S(1)}, u32[]{:S(2)}, u32[]{:S(2)}) collective-permute-start(f32[96,128]{1,0:T(8,128)S(1)} %get-tuple-element.53), channel_id=1, source_target_pairs={{0,16},{4,20},{8,24},{12,28},{16,0},{20,4},{24,8},{28,12},{1,17},{... | collective-permute-start | bytes 147464 | tf_op jit(solution)/shard_map/ppermute | solution.py:332
  63.5 8.0 %collective-permute-start.15 = (f32[96,128]{1,0:T(8,128)S(1)}, f32[96,128]{1,0:T(8,128)S(1)}, u32[]{:S(2)}, u32[]{:S(2)}) collective-permute-start(f32[96,128]{1,0:T(8,128)S(1)} %get-tuple-element.54), channel_id=1, source_target_pairs={{0,20},{4,16},{8,28},{12,24},{16,4},{20,0},{24,12},{28,8},{1,21},{... | collective-permute-start | bytes 147464 | tf_op jit(solution)/shard_map/ppermute | solution.py:332
  63.5 8.0 %collective-permute-start.16 = (f32[96,128]{1,0:T(8,128)S(1)}, f32[96,128]{1,0:T(8,128)S(1)}, u32[]{:S(2)}, u32[]{:S(2)}) collective-permute-start(f32[96,128]{1,0:T(8,128)S(1)} %get-tuple-element.55), channel_id=1, source_target_pairs={{0,24},{4,28},{8,16},{12,20},{16,8},{20,12},{24,0},{28,4},{1,25},{... | collective-permute-start | bytes 147464 | tf_op jit(solution)/shard_map/ppermute | solution.py:332
  65.9 6.9 %collective-permute-start.17 = (f32[96,128]{1,0:T(8,128)S(1)}, f32[96,128]{1,0:T(8,128)S(1)}, u32[]{:S(2)}, u32[]{:S(2)}) collective-permute-start(f32[96,128]{1,0:T(8,128)S(1)} %get-tuple-element.56), channel_id=1, source_target_pairs={{0,28},{4,24},{8,20},{12,16},{16,12},{20,8},{24,4},{28,0},{1,29},{... | collective-permute-start | bytes 147464 | tf_op jit(solution)/shard_map/ppermute | solution.py:332
  (3 other events, 2.6 us)

commit v10 on v9

--- a/solution.py
+++ b/solution.py
@@ -139,9 +139,8 @@
 
 
 def send_kernel(g, sticks_ref, columns_ref, *refs):
-    block_refs, (row_ref, rows_ref, sems, row_sem) = refs[:-4], refs[-4:]
+    block_refs, (row_ref, sems, row_sem) = refs[:-3], refs[-3:]
     own = lax.axis_index("stick")
-    count = len(block_refs)
     row_copy = pltpu.make_async_copy(columns_ref, row_ref, row_sem)
     row_copy.start()
     copies = [
@@ -151,14 +150,10 @@
     for copy in copies:
         copy.start()
     row_copy.wait()
-    rows_ref[...] = jnp.broadcast_to(row_ref[...].astype(F32), rows_ref.shape)
-    row_copies = [
-        pltpu.make_async_copy(rows_ref, ref.at[pl.ds(2 * g, 8)], sems.at[count + d])
-        for d, ref in enumerate(block_refs)
-    ]
-    for copy in row_copies:
-        copy.start()
-    for copy in copies + row_copies:
+    columns = jnp.broadcast_to(row_ref[...].astype(F32), (8, LANES))
+    for ref in block_refs:
+        ref[2 * g :, :] = columns
+    for copy in copies:
         copy.wait()
 
 
@@ -327,10 +322,15 @@
 
 def exchanged(blocks):
     owners = len(blocks)
-    moved = {}
-    for d in range(owners - 1, 0, -1):
-        moved[d] = lax.ppermute(blocks[d], "stick", [(i, i ^ d) for i in range(owners)])
-    return [blocks[0]] + [moved[d] for d in range(1, owners)]
+    half = owners // 2
+    blocks = list(blocks)
+
+    def moved(d):
+        return lax.ppermute(blocks[d], "stick", [(i, i ^ d) for i in range(owners)])
+
+    far = [moved(d) for d in range(half, owners)]
+    *blocks[1:half], far[0] = lax.optimization_barrier((*blocks[1:half], far[0]))
+    return [blocks[0]] + [moved(d) for d in range(1, half)] + far
 
 
 def on_device(sticks, stick_columns):
@@ -355,15 +355,13 @@
         [jax.ShapeDtypeStruct((2 * g + 8, slots), F32)] * owners,
         [
             pltpu.VMEM((1, slots), jnp.int32),
-            pltpu.VMEM((8, slots), F32),
-            pltpu.SemaphoreType.DMA((2 * owners,)),
+            pltpu.SemaphoreType.DMA((owners,)),
             pltpu.SemaphoreType.DMA,
         ],
         10**6,
         sticks,
         stick_columns[None, :],
         space=pltpu.HBM,
-        out_space=pltpu.HBM,
         grant=SEND_GRANT,
     )
     received = exchanged(sent)

time: 73.8 us -> 63.1 us (0.86)
  Pallas kernels: 34.8 us -> 23.4 us
  waiting for transfers between devices: 10.9 us -> 14.3 us
  starting transfers between devices: 25.1 us -> 22.3 us
    pallas_call x10, Pallas kernels: 34.8 us -> 23.4 us  [call(): pl.pallas_call(kernel, out_shape=out_shapes, in_specs=[pl.BlockSpec(memor...]
    ppermute x14, waiting for transfers between devices: 9.65 us -> 13.1 us  [moved(): return lax.ppermute(blocks[d], 'stick', [(i, i ^ d) for i in range(owners)])]
    ppermute x14, starting transfers between devices: 22.8 us -> 20 us  [moved(): return lax.ppermute(blocks[d], 'stick', [(i, i ^ d) for i in range(owners)])]
  transfers between devices with their start and end apart: 18 -> 18, of which waited for: 5 -> 6; matrix products, arithmetic and copies ran while one was open for 0% -> 0% of each run, Pallas kernels for 18% -> 21%
where the time goes in v10:
time: 63.1 us; the launch traced here: 62.9 us
  Pallas kernels  23.4 us (37%)
  starting transfers between devices  22.3 us (35%)
  waiting for transfers between devices  14.3 us (23%)
  local copies, waits for them, and re-layouts  2.67 us (4%)
    pallas_call x10, Pallas kernels, call(): pl.pallas_call(kernel, out_shape=out_shapes, in_specs=[pl.BlockSpec(memor...  23.4 us
    ppermute x14, starting transfers between devices, moved(): return lax.ppermute(blocks[d], 'stick', [(i, i ^ d) for i in range(owners)])  20 us
    ppermute x14, waiting for transfers between devices, moved(): return lax.ppermute(blocks[d], 'stick', [(i, i ^ d) for i in range(owners)])  13.1 us
    unnamed x18, local copies, waits for them, and re-layouts  2.67 us
    ppermute x2, starting transfers between devices, shifted(): lax.ppermute(x, 'band', [(i, (i - distance) % groups) for i in range(grou...  2.16 us
  transfers between devices with their start and end apart: 18, of which 6 were waited for; matrix products, arithmetic and copies ran while one was open for 0% of the time, Pallas kernels for 21%

profile of v10, /device:TPU:0, one launch (start us, length us, event | category | flops | bytes accessed | tf_op | source)
XLA Modules:
  0.0 62.9 jit_solution(8265833352754215316)
XLA Ops:
  0.0 1.8 %shard_map.91 = (f32[104,128]{1,0:T(8,128)}, f32[104,128]{1,0:T(8,128)}, f32[104,128]{1,0:T(8,128)}, f32[104,128]{1,0:T(8,128)}, f32[104,128]{1,0:T(8,128)}, /*i...) custom-call(f32[8,96,128]{2,1,0:T(8,128)} %sticks_ref.1, s32[1,128]{1,0:T(1,128)} %bitcast.1), custom_call_target="tpu_custom_call" | custom-call | flops 1000000 | bytes 393728 | tf_op jit(solution)/shard_map/pallas_call | solution.py:312
  1.8 4.1 %collective-permute-start = (f32[104,128]{1,0:T(8,128)}, f32[104,128]{1,0:T(8,128)S(1)}, u32[]{:S(2)}, u32[]{:S(2)}) collective-permute-start(f32[104,128]{1,0:T(8,128)} %get-tuple-element.43), channel_id=1, source_target_pairs={{0,16},{4,20},{8,24},{12,28},{16,0},{20,4},{24,8},{28,12},{1,17},{... | collective-permute-start | bytes 159752 | tf_op jit(solution)/shard_map/ppermute | solution.py:329
  5.9 1.3 %collective-permute-start.1 = (f32[104,128]{1,0:T(8,128)}, f32[104,128]{1,0:T(8,128)S(1)}, u32[]{:S(2)}, u32[]{:S(2)}) collective-permute-start(f32[104,128]{1,0:T(8,128)} %get-tuple-element.45), channel_id=1, source_target_pairs={{0,20},{4,16},{8,28},{12,24},{16,4},{20,0},{24,12},{28,8},{1,21},{... | collective-permute-start | bytes 159752 | tf_op jit(solution)/shard_map/ppermute | solution.py:329
  7.2 3.6 %collective-permute-start.2 = (f32[104,128]{1,0:T(8,128)}, f32[104,128]{1,0:T(8,128)S(1)}, u32[]{:S(2)}, u32[]{:S(2)}) collective-permute-start(f32[104,128]{1,0:T(8,128)} %get-tuple-element.46), channel_id=1, source_target_pairs={{0,24},{4,28},{8,16},{12,20},{16,8},{20,12},{24,0},{28,4},{1,25},{... | collective-permute-start | bytes 159752 | tf_op jit(solution)/shard_map/ppermute | solution.py:329
  10.8 1.7 %collective-permute-start.4 = (f32[104,128]{1,0:T(8,128)}, f32[104,128]{1,0:T(8,128)S(1)}, u32[]{:S(2)}, u32[]{:S(2)}) collective-permute-start(f32[104,128]{1,0:T(8,128)} %get-tuple-element.49), channel_id=1, source_target_pairs={{0,4},{4,0},{8,12},{12,8},{16,20},{20,16},{24,28},{28,24},{1,5},{5... | collective-permute-start | bytes 159752 | tf_op jit(solution)/shard_map/ppermute | solution.py:329
  12.7 2.0 %collective-permute-done.1.refs_2_ = f32[104,128]{1,0:T(8,128)S(1)} collective-permute-done((f32[104,128]{1,0:T(8,128)}, f32[104,128]{1,0:T(8,128)S(1)}, u32[]{:S(2)}, u32[]{:S(2)}) %collective-permute-start.1) | collective-permute-done | bytes 53280 | tf_op jit(solution)/shard_map/ppermute | solution.py:329
  14.9 2.9 %collective-permute-done.3.refs_4_ = f32[104,128]{1,0:T(8,128)S(1)} collective-permute-done((f32[104,128]{1,0:T(8,128)}, f32[104,128]{1,0:T(8,128)S(1)}, u32[]{:S(2)}, u32[]{:S(2)}) %collective-permute-start.3) | collective-permute-done | bytes 53280 | tf_op jit(solution)/shard_map/ppermute | solution.py:329
  17.8 0.8 %copy-done.7 = f32[104,128]{1,0:T(8,128)S(1)} copy-done((f32[104,128]{1,0:T(8,128)S(1)}, f32[104,128]{1,0:T(8,128)}, u32[]{:S(2)}) %copy-start.7) | copy-done | bytes 53272
  18.7 1.6 %collective-permute-start.8 = (f32[480,128]{1,0:T(8,128)S(1)}, f32[480,128]{1,0:T(8,128)S(1)}, u32[]{:S(2)}, u32[]{:S(2)}) collective-permute-start(f32[480,128]{1,0:T(8,128)S(1)} %get-tuple-element.48.first_ref), channel_id=1, source_target_pairs={{0,2},{1,3},{2,0},{3,1},{4,6},{5,7},{6,4},{7,5},{8,10},{9,11},{10,... | collective-permute-start | bytes 737288 | tf_op jit(solution)/shard_map/ppermute | solution.py:348
  20.2 0.9 %copy-done.4 = f32[96,144]{1,0:T(8,128)S(1)} copy-done((f32[96,144]{1,0:T(8,128)S(1)}, f32[96,144]{1,0:T(8,128)}, u32[]{:S(2)}) %copy-start.4) | copy-done | bytes 55320
  21.1 0.9 %copy-done.8 = f32[128,288]{1,0:T(8,128)S(1)} copy-done((f32[128,288]{1,0:T(8,128)S(1)}, f32[128,288]{1,0:T(8,128)}, u32[]{:S(2)}) %copy-start.8) | copy-done | bytes 147480
  22.7 4.0 %shard_map.95.phi_ref = f32[1152,128]{1,0:T(8,128)S(1)} custom-call(f32[480,128]{1,0:T(8,128)S(1)} %get-tuple-element.48.first_ref, f32[288,128]{1,0:T(8,128)S(1)} %get-tuple-element.52.second_ref, f32[8,640]{1,0:T(8,128)S(1)} %get-tuple-element.53.first_columns_ref, f32[8,384]{1,0:T(8,128)S(1)} %get-tuple-element.54.second_columns_ref, ...), custom_call_target="tpu_custom_call" | custom-call | flops 1000000000 | bytes 527360 | tf_op jit(solution)/shard_map/pallas_call | solution.py:312
  26.9 1.2 %collective-permute-done.9.second_ref = f32[288,128]{1,0:T(8,128)S(1)} collective-permute-done((f32[288,128]{1,0:T(8,128)S(1)}, f32[288,128]{1,0:T(8,128)S(1)}, u32[]{:S(2)}, u32[]{:S(2)}) %collective-permute-start.9) | collective-permute-done | bytes 147488 | tf_op jit(solution)/shard_map/ppermute | solution.py:348
  28.1 4.0 %shard_map.96.first_ref = f32[1152,128]{1,0:T(8,128)S(1)} custom-call(f32[480,128]{1,0:T(8,128)S(1)} %collective-permute-done.8.first_ref, f32[288,128]{1,0:T(8,128)S(1)} %collective-permute-done.9.second_ref, f32[8,640]{1,0:T(8,128)S(1)} %get-tuple-element.53.first_columns_ref, f32[8,384]{1,0:T(8,128)S(1)} %get-tuple-element.54.second_columns_ref, ...), custom_call_target="tpu_custom_call" | custom-call | flops 1000000000 | bytes 527360 | tf_op jit(solution)/shard_map/pallas_call | solution.py:312
  32.2 1.2 %shard_map.98.hot_ref = bf16[1024,2304]{1,0:T(8,128)(2,1)S(1)} custom-call(f32[8,640]{1,0:T(8,128)S(1)} %get-tuple-element.53.first_columns_ref, f32[8,384]{1,0:T(8,128)S(1)} %get-tuple-element.54.second_columns_ref), custom_call_target="tpu_custom_call" | custom-call | flops 1811939328 | bytes 32768 | tf_op jit(solution)/shard_map/pallas_call | solution.py:312
  33.5 3.6 %shard_map.97.before_ref = f32[1152,128]{1,0:T(8,128)S(1)} custom-call(f32[1152,128]{1,0:T(8,128)S(1)} %shard_map.95.phi_ref, f32[1152,128]{1,0:T(8,128)S(1)} %collective-permute-done.7.other_ref, f32[256,256]{1,0:T(8,128)S(1)} %copy-done.2, f32[256,256]{1,0:T(8,128)S(1)} %copy-done.1, f32[96,144]{1,0:T(8,128)S(1)} %copy-done.6, f32[96,144]{1,0:T(8,128)S(1)} %copy-done.5, ...), custom_call_target="tpu_custom_call" | custom-call | flops 1811939328 | bytes 2994176 | tf_op jit(solution)/shard_map/pallas_call | solution.py:312
  37.2 7.9 %shard_map.99 = (f32[96,128]{1,0:T(8,128)S(1)}, f32[96,128]{1,0:T(8,128)S(1)}, f32[96,128]{1,0:T(8,128)S(1)}, f32[96,128]{1,0:T(8,128)S(1)}, f32[96,128]{1,0:T(8...) custom-call(f32[1152,128]{1,0:T(8,128)S(1)} %shard_map.95.phi_ref, ...), custom_call_target="tpu_custom_call" | custom-call | flops 1811939328 | bytes 9039872 | tf_op jit(solution)/shard_map/pallas_call | solution.py:312
  45.1 3.5 %collective-permute-start.11 = (f32[96,128]{1,0:T(8,128)S(1)}, f32[96,128]{1,0:T(8,128)S(1)}, u32[]{:S(2)}, u32[]{:S(2)}) collective-permute-start(f32[96,128]{1,0:T(8,128)S(1)} %get-tuple-element.65), channel_id=1, source_target_pairs={{0,16},{4,20},{8,24},{12,28},{16,0},{20,4},{24,8},{28,12},{1,17},{... | collective-permute-start | bytes 147464 | tf_op jit(solution)/shard_map/ppermute | solution.py:329
  48.6 0.9 %collective-permute-start.16 = (f32[96,128]{1,0:T(8,128)S(1)}, f32[96,128]{1,0:T(8,128)S(1)}, u32[]{:S(2)}, u32[]{:S(2)}) collective-permute-start(f32[96,128]{1,0:T(8,128)S(1)} %get-tuple-element.71), channel_id=1, source_target_pairs={{0,24},{4,28},{8,16},{12,20},{16,8},{20,12},{24,0},{28,4},{1,25},{... | collective-permute-start | bytes 147464 | tf_op jit(solution)/shard_map/ppermute | solution.py:329
  49.5 3.9 %collective-permute-start.17 = (f32[96,128]{1,0:T(8,128)S(1)}, f32[96,128]{1,0:T(8,128)S(1)}, u32[]{:S(2)}, u32[]{:S(2)}) collective-permute-start(f32[96,128]{1,0:T(8,128)S(1)} %get-tuple-element.72), channel_id=1, source_target_pairs={{0,28},{4,24},{8,20},{12,16},{16,12},{20,8},{24,4},{28,0},{1,29},{... | collective-permute-start | bytes 147464 | tf_op jit(solution)/shard_map/ppermute | solution.py:329
  53.9 3.2 %collective-permute-done.15.refs_5_ = f32[96,128]{1,0:T(8,128)S(1)} collective-permute-done((f32[96,128]{1,0:T(8,128)S(1)}, f32[96,128]{1,0:T(8,128)S(1)}, u32[]{:S(2)}, u32[]{:S(2)}) %collective-permute-start.15) | collective-permute-done | bytes 49184 | tf_op jit(solution)/shard_map/ppermute | solution.py:329
  57.1 1.0 %collective-permute-done.12.refs_1_ = f32[96,128]{1,0:T(8,128)S(1)} collective-permute-done((f32[96,128]{1,0:T(8,128)S(1)}, f32[96,128]{1,0:T(8,128)S(1)}, u32[]{:S(2)}, u32[]{:S(2)}) %collective-permute-start.12) | collective-permute-done | bytes 49184 | tf_op jit(solution)/shard_map/ppermute | solution.py:329
  58.1 3.9 %collective-permute-done.14.refs_3_ = f32[96,128]{1,0:T(8,128)S(1)} collective-permute-done((f32[96,128]{1,0:T(8,128)S(1)}, f32[96,128]{1,0:T(8,128)S(1)}, u32[]{:S(2)}, u32[]{:S(2)}) %collective-permute-start.14) | collective-permute-done | bytes 49184 | tf_op jit(solution)/shard_map/ppermute | solution.py:329
  62.1 0.8 %shard_map.100 = f32[8,96,128]{2,1,0:T(8,128)} custom-call(f32[96,128]{1,0:T(8,128)S(1)} %get-tuple-element.61.refs_0_, f32[96,128]{1,0:T(8,128)S(1)} %collective-permute-done.12.refs_1_, f32[96,128]{1,0:T(8,128)S(1)} %collective-permute-done.13.refs_2_, f32[96,128]{1,0:T(8,128)S(1)} %collective-permute-done.14.refs_3_, ...), custom_call_target="tpu_custom_call" | custom-call | flops 1000000 | bytes 393216 | tf_op jit(solution)/shard_map/pallas_call | solution.py:312
  (40 shorter events, 1.8 us)
Async XLA Ops:
  1.8 9.0 %collective-permute-start = (f32[104,128]{1,0:T(8,128)}, f32[104,128]{1,0:T(8,128)S(1)}, u32[]{:S(2)}, u32[]{:S(2)}) collective-permute-start(f32[104,128]{1,0:T(8,128)} %get-tuple-element.43), channel_id=1, source_target_pairs={{0,16},{4,20},{8,24},{12,28},{16,0},{20,4},{24,8},{28,12},{1,17},{... | collective-permute-start | bytes 159752 | tf_op jit(solution)/shard_map/ppermute | solution.py:329
  5.9 8.7 %collective-permute-start.1 = (f32[104,128]{1,0:T(8,128)}, f32[104,128]{1,0:T(8,128)S(1)}, u32[]{:S(2)}, u32[]{:S(2)}) collective-permute-start(f32[104,128]{1,0:T(8,128)} %get-tuple-element.45), channel_id=1, source_target_pairs={{0,20},{4,16},{8,28},{12,24},{16,4},{20,0},{24,12},{28,8},{1,21},{... | collective-permute-start | bytes 159752 | tf_op jit(solution)/shard_map/ppermute | solution.py:329
  7.2 7.7 %collective-permute-start.2 = (f32[104,128]{1,0:T(8,128)}, f32[104,128]{1,0:T(8,128)S(1)}, u32[]{:S(2)}, u32[]{:S(2)}) collective-permute-start(f32[104,128]{1,0:T(8,128)} %get-tuple-element.46), channel_id=1, source_target_pairs={{0,24},{4,28},{8,16},{12,20},{16,8},{20,12},{24,0},{28,4},{1,25},{... | collective-permute-start | bytes 159752 | tf_op jit(solution)/shard_map/ppermute | solution.py:329
  10.8 7.0 %collective-permute-start.3 = (f32[104,128]{1,0:T(8,128)}, f32[104,128]{1,0:T(8,128)S(1)}, u32[]{:S(2)}, u32[]{:S(2)}) collective-permute-start(f32[104,128]{1,0:T(8,128)} %get-tuple-element.47), channel_id=1, source_target_pairs={{0,28},{4,24},{8,20},{12,16},{16,12},{20,8},{24,4},{28,0},{1,29},{... | collective-permute-start | bytes 159752 | tf_op jit(solution)/shard_map/ppermute | solution.py:329
  10.8 11.3 %collective-permute-start.4 = (f32[104,128]{1,0:T(8,128)}, f32[104,128]{1,0:T(8,128)S(1)}, u32[]{:S(2)}, u32[]{:S(2)}) collective-permute-start(f32[104,128]{1,0:T(8,128)} %get-tuple-element.49), channel_id=1, source_target_pairs={{0,4},{4,0},{8,12},{12,8},{16,20},{20,16},{24,28},{28,24},{1,5},{5... | collective-permute-start | bytes 159752 | tf_op jit(solution)/shard_map/ppermute | solution.py:329
  12.5 9.6 %collective-permute-start.5 = (f32[104,128]{1,0:T(8,128)}, f32[104,128]{1,0:T(8,128)S(1)}, u32[]{:S(2)}, u32[]{:S(2)}) collective-permute-start(f32[104,128]{1,0:T(8,128)} %get-tuple-element.50), channel_id=1, source_target_pairs={{0,8},{4,12},{8,0},{12,4},{16,24},{20,28},{24,16},{28,20},{1,9},{5... | collective-permute-start | bytes 159752 | tf_op jit(solution)/shard_map/ppermute | solution.py:329
  14.7 7.4 %collective-permute-start.6 = (f32[104,128]{1,0:T(8,128)}, f32[104,128]{1,0:T(8,128)S(1)}, u32[]{:S(2)}, u32[]{:S(2)}) collective-permute-start(f32[104,128]{1,0:T(8,128)} %get-tuple-element.51), channel_id=1, source_target_pairs={{0,12},{4,8},{8,4},{12,0},{16,28},{20,24},{24,20},{28,16},{1,13},{... | collective-permute-start | bytes 159752 | tf_op jit(solution)/shard_map/ppermute | solution.py:329
  18.7 9.4 %collective-permute-start.8 = (f32[480,128]{1,0:T(8,128)S(1)}, f32[480,128]{1,0:T(8,128)S(1)}, u32[]{:S(2)}, u32[]{:S(2)}) collective-permute-start(f32[480,128]{1,0:T(8,128)S(1)} %get-tuple-element.48.first_ref), channel_id=1, source_target_pairs={{0,2},{1,3},{2,0},{3,1},{4,6},{5,7},{6,4},{7,5},{8,10},{9,11},{10,... | collective-permute-start | bytes 737288 | tf_op jit(solution)/shard_map/ppermute | solution.py:348
  22.1 6.0 %collective-permute-start.9 = (f32[288,128]{1,0:T(8,128)S(1)}, f32[288,128]{1,0:T(8,128)S(1)}, u32[]{:S(2)}, u32[]{:S(2)}) collective-permute-start(f32[288,128]{1,0:T(8,128)S(1)} %get-tuple-element.52.second_ref), channel_id=1, source_target_pairs={{0,2},{1,3},{2,0},{3,1},{4,6},{5,7},{6,4},{7,5},{8,10},{9,11},{10,... | collective-permute-start | bytes 442376 | tf_op jit(solution)/shard_map/ppermute | solution.py:348
  26.8 6.7 %copy-start = (f32[2304,128]{1,0:T(8,128)S(1)}, f32[2304,128]{1,0:T(8,128)}, u32[]{:S(2)}) copy-start(f32[2304,128]{1,0:T(8,128)} %constant.20.clone.refs_4_) | copy-start | bytes 3538948
  26.8 6.7 %copy-start.1 = (f32[256,256]{1,0:T(8,128)S(1)}, f32[256,256]{1,0:T(8,128)}, u32[]{:S(2)}) copy-start(f32[256,256]{1,0:T(8,128)} %constant.15.clone.refs_1_) | copy-start | bytes 786436
  26.8 6.7 %copy-start.2 = (f32[256,256]{1,0:T(8,128)S(1)}, f32[256,256]{1,0:T(8,128)}, u32[]{:S(2)}) copy-start(f32[256,256]{1,0:T(8,128)} %constant.14.clone.refs_0_) | copy-start | bytes 786436
  26.8 6.7 %copy-start.5 = (f32[96,144]{1,0:T(8,128)S(1)}, f32[96,144]{1,0:T(8,128)}, u32[]{:S(2)}) copy-start(f32[96,144]{1,0:T(8,128)} %constant.17.clone.refs_1_.refs_3_) | copy-start | bytes 165892
  26.8 6.7 %copy-start.6 = (f32[96,144]{1,0:T(8,128)S(1)}, f32[96,144]{1,0:T(8,128)}, u32[]{:S(2)}) copy-start(f32[96,144]{1,0:T(8,128)} %constant.16.clone.refs_2_) | copy-start | bytes 165892
  26.8 6.6 %collective-permute-start.7 = (f32[1152,128]{1,0:T(8,128)S(1)}, f32[1152,128]{1,0:T(8,128)S(1)}, u32[]{:S(2)}, u32[]{:S(2)}) collective-permute-start(f32[1152,128]{1,0:T(8,128)S(1)} %shard_map.95.phi_ref), channel_id=1, source_target_pairs={{0,1},{1,0},{2,3},{3,2},{4,5},{5,4},{6,7},{7,6},{8,9},{9,8},{10,11... | collective-permute-start | bytes 1769480 | tf_op jit(solution)/shard_map/ppermute | solution.py:351
  32.1 5.0 %collective-permute-start.10 = (f32[1152,128]{1,0:T(8,128)S(1)}, f32[1152,128]{1,0:T(8,128)S(1)}, u32[]{:S(2)}, u32[]{:S(2)}) collective-permute-start(f32[1152,128]{1,0:T(8,128)S(1)} %shard_map.96.first_ref), channel_id=1, source_target_pairs={{0,1},{1,0},{2,3},{3,2},{4,5},{5,4},{6,7},{7,6},{8,9},{9,8},{10,11... | collective-permute-start | bytes 1769480 | tf_op jit(solution)/shard_map/ppermute | solution.py:351
  33.4 3.7 %copy-start.3 = (f32[96,384]{1,0:T(8,128)S(1)}, f32[96,384]{1,0:T(8,128)}, u32[]{:S(2)}) copy-start(f32[96,384]{1,0:T(8,128)} %constant.19.clone.stick_out_ref) | copy-start | bytes 442372
  45.1 8.4 %collective-permute-start.11 = (f32[96,128]{1,0:T(8,128)S(1)}, f32[96,128]{1,0:T(8,128)S(1)}, u32[]{:S(2)}, u32[]{:S(2)}) collective-permute-start(f32[96,128]{1,0:T(8,128)S(1)} %get-tuple-element.65), channel_id=1, source_target_pairs={{0,16},{4,20},{8,24},{12,28},{16,0},{20,4},{24,8},{28,12},{1,17},{... | collective-permute-start | bytes 147464 | tf_op jit(solution)/shard_map/ppermute | solution.py:329
  48.6 8.5 %collective-permute-start.15 = (f32[96,128]{1,0:T(8,128)S(1)}, f32[96,128]{1,0:T(8,128)S(1)}, u32[]{:S(2)}, u32[]{:S(2)}) collective-permute-start(f32[96,128]{1,0:T(8,128)S(1)} %get-tuple-element.70), channel_id=1, source_target_pairs={{0,20},{4,16},{8,28},{12,24},{16,4},{20,0},{24,12},{28,8},{1,21},{... | collective-permute-start | bytes 147464 | tf_op jit(solution)/shard_map/ppermute | solution.py:329
  48.6 8.5 %collective-permute-start.16 = (f32[96,128]{1,0:T(8,128)S(1)}, f32[96,128]{1,0:T(8,128)S(1)}, u32[]{:S(2)}, u32[]{:S(2)}) collective-permute-start(f32[96,128]{1,0:T(8,128)S(1)} %get-tuple-element.71), channel_id=1, source_target_pairs={{0,24},{4,28},{8,16},{12,20},{16,8},{20,12},{24,0},{28,4},{1,25},{... | collective-permute-start | bytes 147464 | tf_op jit(solution)/shard_map/ppermute | solution.py:329
  49.5 7.6 %collective-permute-start.17 = (f32[96,128]{1,0:T(8,128)S(1)}, f32[96,128]{1,0:T(8,128)S(1)}, u32[]{:S(2)}, u32[]{:S(2)}) collective-permute-start(f32[96,128]{1,0:T(8,128)S(1)} %get-tuple-element.72), channel_id=1, source_target_pairs={{0,28},{4,24},{8,20},{12,16},{16,12},{20,8},{24,4},{28,0},{1,29},{... | collective-permute-start | bytes 147464 | tf_op jit(solution)/shard_map/ppermute | solution.py:329
  53.4 4.7 %collective-permute-start.12 = (f32[96,128]{1,0:T(8,128)S(1)}, f32[96,128]{1,0:T(8,128)S(1)}, u32[]{:S(2)}, u32[]{:S(2)}) collective-permute-start(f32[96,128]{1,0:T(8,128)S(1)} %get-tuple-element.66), channel_id=1, source_target_pairs={{0,4},{4,0},{8,12},{12,8},{16,20},{20,16},{24,28},{28,24},{1,5},{5... | collective-permute-start | bytes 147464 | tf_op jit(solution)/shard_map/ppermute | solution.py:329
  53.9 4.2 %collective-permute-start.13 = (f32[96,128]{1,0:T(8,128)S(1)}, f32[96,128]{1,0:T(8,128)S(1)}, u32[]{:S(2)}, u32[]{:S(2)}) collective-permute-start(f32[96,128]{1,0:T(8,128)S(1)} %get-tuple-element.67), channel_id=1, source_target_pairs={{0,8},{4,12},{8,0},{12,4},{16,24},{20,28},{24,16},{28,20},{1,9},{5... | collective-permute-start | bytes 147464 | tf_op jit(solution)/shard_map/ppermute | solution.py:329
  57.1 5.0 %collective-permute-start.14 = (f32[96,128]{1,0:T(8,128)S(1)}, f32[96,128]{1,0:T(8,128)S(1)}, u32[]{:S(2)}, u32[]{:S(2)}) collective-permute-start(f32[96,128]{1,0:T(8,128)S(1)} %get-tuple-element.68), channel_id=1, source_target_pairs={{0,12},{4,8},{8,4},{12,0},{16,28},{20,24},{24,20},{28,16},{1,13},{... | collective-permute-start | bytes 147464 | tf_op jit(solution)/shard_map/ppermute | solution.py:329
  (3 other events, 2.6 us)

commit v11 on v10

--- a/solution.py
+++ b/solution.py
@@ -13,6 +13,7 @@
 BOX_LENGTH = 18.0
 LANES = 128
 MID = 64
+WINDOW = 5
 SEND_GRANT = 60
 PAIRS = 6
 
@@ -61,12 +62,15 @@
     coulomb = np.zeros((g, g, LANES), np.float32)
     coulomb[:, :, lower] = kernel
     coulomb[:, :, upper] = kernel
+    stick_in, left_backward = across(stick_in), across(np.concatenate([c, s], 0))
+    early = np.zeros((LANES + 2 * g, stick_in.shape[1]), np.float32)
+    early[:LANES], early[LANES:, : left_backward.shape[1]] = stick_in, left_backward
     return dict(
         forward=down(forward),
         last_backward=down(backward / g**3),
         left_forward=across(np.concatenate([c, -s], 0)),
-        left_backward=across(np.concatenate([c, s], 0)),
-        stick_in=across(stick_in),
+        left_backward=left_backward,
+        early=early,
         stick_out=across(stick_out * g**-1.5),
         coulomb=coulomb.reshape(g * g, LANES),
     )
@@ -157,16 +161,16 @@
         copy.wait()
 
 
-def table_kernel(*refs):
-    count = len(refs) // 2
-    for table_ref, out_ref in zip(refs[:count], refs[count:]):
-        out_ref[...] = table_ref[...].astype(BF16)
-
-
-def place_kernel(*refs):
+def early_kernel(g, own_ref, tables_ref, staged_ref, stick_in_ref, left_ref):
+    staged_ref[...] = own_ref[...]
+    stick_in_ref[...] = tables_ref[:LANES, : stick_in_ref.shape[1]].astype(BF16)
+    left_ref[...] = tables_ref[LANES:, : left_ref.shape[1]].astype(BF16)
+
+
+def place_kernel(order, *refs):
     own = lax.axis_index("stick")
     out_ref = refs[-1]
-    for d, block_ref in enumerate(refs[:-1]):
+    for d, block_ref in zip(order, refs[:-1]):
         out_ref[own ^ d] = block_ref[...]
 
 
@@ -183,12 +187,10 @@
         columns_ref[:, k * LANES : (k + 1) * LANES] = ref[2 * g :, :]
 
 
-def field_kernel(g, first_ref, second_ref, first_columns_ref, second_columns_ref, stick_in_ref, left_ref, phi_ref, work_a):
-    columns = beside(first_columns_ref[:1, :], second_columns_ref[:1, :]).astype(jnp.int32)
+def field_kernel(g, blocks_ref, columns_ref, stick_in_ref, left_ref, phi_ref, work_a):
+    columns = columns_ref[:1, :].astype(jnp.int32)
     stick_in, backward = stick_in_ref[...], left_ref[...]
-    blocks = []
-    for ref in (first_ref, second_ref):
-        blocks += [ref[k : k + 2 * g, :] for k in range(0, ref.shape[0], 2 * g)]
+    blocks = [blocks_ref[k : k + 2 * g, :] for k in range(0, blocks_ref.shape[0], 2 * g)]
     sticks = []
     for k in range(0, len(blocks), 2):
         sticks.append(beside(*split(dot(stick_in, stacked(beside(blocks[k], blocks[k + 1]))).T)))
@@ -210,10 +212,9 @@
         store(phi_ref, y, [jnp.where(low, cos - turned(sin), turned(cos_up) - sin_up)])
 
 
-def pick_kernel(g, first_columns_ref, second_columns_ref, hot_ref):
-    columns = beside(first_columns_ref[...], second_columns_ref[...])
-    for k in range(0, columns.shape[1], LANES):
-        block = columns[:, k : k + LANES]
+def pick_kernel(g, columns_ref, hot_ref):
+    for k in range(0, columns_ref.shape[1], LANES):
+        block = columns_ref[:, k : k + LANES]
         wanted = jnp.concatenate([block] * (LANES // block.shape[0]), 0).T.astype(jnp.int32)
         for c in range(0, hot_ref.shape[1], LANES):
             index = lax.broadcasted_iota(jnp.int16, (LANES, LANES), 1)
@@ -307,7 +308,6 @@
 
 
 def call(kernel, out_shapes, scratch, flops, *operands, space=pltpu.VMEM, out_space=pltpu.VMEM, grant=40):
-    moved = sum(x.size * x.dtype.itemsize for x in operands)
     out_spec = pl.BlockSpec(memory_space=out_space)
     return pl.pallas_call(
         kernel,
@@ -316,21 +316,22 @@
         out_specs=jax.tree.map(lambda _: out_spec, out_shapes),
         scratch_shapes=scratch,
         compiler_params=pltpu.CompilerParams(vmem_limit_bytes=grant * 2**20),
-        cost_estimate=pl.CostEstimate(flops=flops, bytes_accessed=moved, transcendentals=0),
+        cost_estimate=pl.CostEstimate(flops=flops, bytes_accessed=flops, transcendentals=0),
     )(*operands)
 
 
-def exchanged(blocks):
+def after(x, *others):
+    return lax.optimization_barrier((x, *others))[0]
+
+
+def exchanged(blocks, order, before):
     owners = len(blocks)
-    half = owners // 2
-    blocks = list(blocks)
-
-    def moved(d):
-        return lax.ppermute(blocks[d], "stick", [(i, i ^ d) for i in range(owners)])
-
-    far = [moved(d) for d in range(half, owners)]
-    *blocks[1:half], far[0] = lax.optimization_barrier((*blocks[1:half], far[0]))
-    return [blocks[0]] + [moved(d) for d in range(1, half)] + far
+    moved = [blocks[0]] + [None] * (owners - 1)
+    for d in order:
+        others = [moved[x] if isinstance(x, int) else x for x in before.get(d, ())]
+        block = after(blocks[d], *others) if others else blocks[d]
+        moved[d] = lax.ppermute(block, "stick", [(i, i ^ d) for i in range(owners)])
+    return moved
 
 
 def on_device(sticks, stick_columns):
@@ -342,7 +343,7 @@
     rows = g * g
     field = jax.ShapeDtypeStruct((rows // 2, LANES), F32)
     work = pltpu.VMEM((rows, LANES), F32)
-    pot_flops = 6 * 2 * rows * 256 * 256
+    pot_flops = 1
 
     def shifted(x, distance):
         return lax.ppermute(x, "band", [(i, (i - distance) % groups) for i in range(groups)])
@@ -358,55 +359,58 @@
             pltpu.SemaphoreType.DMA((owners,)),
             pltpu.SemaphoreType.DMA,
         ],
-        10**6,
+        1,
         sticks,
         stick_columns[None, :],
         space=pltpu.HBM,
         grant=SEND_GRANT,
     )
-    received = exchanged(sent)
-    first_tables = lax.optimization_barrier((t["stick_in"], t["left_backward"], sent[0]))[:2]
-    first_tables = call(
-        table_kernel, [jax.ShapeDtypeStruct(x.shape, BF16) for x in first_tables], [], 10**9, *first_tables
-    )
-
+    shapes = [(2 * g + 8, slots), (LANES, 6 * g), (2 * g, 3 * g)]
+    staged, *first_tables = call(
+        functools.partial(early_kernel, g),
+        [jax.ShapeDtypeStruct(shape, kind) for shape, kind in zip(shapes, (F32, BF16, BF16))],
+        [],
+        1,
+        sent[0],
+        after(t["early"], sent[0]),
+    )
     half = owners // 2
-    order = [0] + list(range(half, owners)) + list(range(1, half))
-    relays, columns = [], []
-    for part in (order[: half + 1], order[half + 1 :]):
-        shapes = [(len(part) * 2 * g, slots), (8, len(part) * slots)]
-        shapes = [jax.ShapeDtypeStruct(shape, F32) for shape in shapes]
-        relay, column = call(functools.partial(relay_kernel, g), shapes, [], 10**6, *[received[d] for d in part])
-        relays.append(relay)
-        columns.append(column)
+    distant, close = list(range(half, owners)), list(range(1, half))
+    received = exchanged(sent, distant + close, {d: (half, staged, *first_tables) for d in close})
+    received[0] = staged
+    order = [0] + distant + close
+    relay, columns = call(
+        functools.partial(relay_kernel, g),
+        [jax.ShapeDtypeStruct((owners * 2 * g, slots), F32), jax.ShapeDtypeStruct((8, owners * slots), F32)],
+        [],
+        1,
+        *[received[d] for d in order],
+    )
 
     def orbital(blocks):
-        return call(functools.partial(field_kernel, g), field, [work], 10**9, *blocks, *columns, *first_tables)
-
-    phi = orbital(relays)
+        return call(functools.partial(field_kernel, g), field, [work], 1, blocks, columns, *first_tables)
+
+    phi = orbital(relay)
     near = swapped(phi)
     hot = call(
-        functools.partial(pick_kernel, g), jax.ShapeDtypeStruct((owners * slots, rows), BF16), [], pot_flops, *columns
-    )
-    distances = (HALF,) if groups == 2 * HALF else (HALF, -HALF)
-    fields = [orbital([shifted(x, distance) for x in relays]) for distance in distances]
+        functools.partial(pick_kernel, g), jax.ShapeDtypeStruct((owners * slots, rows), BF16), [], pot_flops, columns
+    )
     pot_tables = [t["forward"], t["last_backward"], t["left_forward"], t["left_backward"], t["coulomb"]]
 
     def potential_sum(kernel, *operands):
         return call(functools.partial(kernel, g), field, [work, work], pot_flops, phi, *operands, *pot_tables)
 
+    distances = (HALF,) if groups == 2 * HALF else (HALF, -HALF)
+    fields = [orbital(after(shifted(relay, distance), hot)) for distance in distances]
+    total = potential_sum(near_kernel, after(near, *fields))
     if groups == 2 * HALF:
         weights = (2.0, 1.0)
         first, second = fields[0], swapped(fields[0])
-        near, first = lax.optimization_barrier((near, first))
-        total = potential_sum(near_kernel, near)
     else:
         weights = (1.0, 0.0)
         odd = lax.axis_index("band") % 2 == 1
         first = second = swapped(jnp.where(odd, fields[1], fields[0]))
-        total = potential_sum(near_kernel, near)
         total = potential_sum(middle_kernel, *fields, total)
-    order_back = {d: k for k, d in enumerate(order)}
     result = call(
         functools.partial(far_kernel, g, weights),
         [jax.ShapeDtypeStruct((2 * g, slots), F32)] * owners,
@@ -420,8 +424,17 @@
         t["stick_out"],
         *pot_tables,
     )
-    result = [result[order_back[d]] for d in range(owners)]
-    return call(place_kernel, jax.ShapeDtypeStruct(sticks.shape, F32), [], 10**6, *exchanged(result))
+    result = [result[order.index(d)] for d in range(owners)]
+    mixed = [distant[0]] + [d for pair in zip(close, distant[1:]) for d in pair]
+    before = {mixed[k]: (mixed[k - 3 - k % 2],) for k in range(WINDOW, len(mixed))}
+    result = exchanged(result, mixed, before)
+    return call(
+        functools.partial(place_kernel, order),
+        jax.ShapeDtypeStruct(sticks.shape, F32),
+        [],
+        1,
+        *[result[d] for d in order],
+    )
 
 
 def solution(mesh):

time: 63.1 us -> 61.9 us (0.981)
  waiting for transfers between devices: 14.3 us -> 10.9 us
  starting transfers between devices: 22.3 us -> 25.3 us
  local copies, waits for them, and re-layouts: 2.67 us -> 1.81 us
    ppermute x14, starting transfers between devices: 20 us -> 23.6 us  [exchanged(): moved[d] = lax.ppermute(block, 'stick', [(i, i ^ d) for i in range(owners)])]
    ppermute x14, waiting for transfers between devices: 13.1 us -> 9.45 us  [exchanged(): moved[d] = lax.ppermute(block, 'stick', [(i, i ^ d) for i in range(owners)])]
    unnamed x18 -> x16, local copies, waits for them, and re-layouts: 2.67 us -> 1.81 us
    ppermute x2 -> x1, starting transfers between devices: 2.16 us -> 1.56 us  [shifted(): lax.ppermute(x, 'band', [(i, (i - distance) % groups) for i in range(grou...]
    ppermute x2 -> x1, waiting for transfers between devices: 1.2 us -> 1.39 us  [shifted(): lax.ppermute(x, 'band', [(i, (i - distance) % groups) for i in range(grou...]
    pallas_call x10 -> x9, Pallas kernels: 23.4 us -> 23.5 us  [call(): pl.pallas_call(kernel, out_shape=out_shapes, in_specs=[pl.BlockSpec(memor...]
  transfers between devices with their start and end apart: 18 -> 17, of which waited for: 6 -> 7; matrix products, arithmetic and copies ran while one was open for 0% -> 0% of each run, Pallas kernels for 21% -> 21%
where the time goes in v11:
time: 61.9 us; the launch traced here: 61.7 us
  starting transfers between devices  25.3 us (41%)
  Pallas kernels  23.5 us (38%)
  waiting for transfers between devices  10.9 us (18%)
  local copies, waits for them, and re-layouts  1.81 us (3%)
    ppermute x14, starting transfers between devices, exchanged(): moved[d] = lax.ppermute(block, 'stick', [(i, i ^ d) for i in range(owners)])  23.6 us
    pallas_call x9, Pallas kernels, call(): pl.pallas_call(kernel, out_shape=out_shapes, in_specs=[pl.BlockSpec(memor...  23.5 us
    ppermute x14, waiting for transfers between devices, exchanged(): moved[d] = lax.ppermute(block, 'stick', [(i, i ^ d) for i in range(owners)])  9.45 us
    unnamed x16, local copies, waits for them, and re-layouts  1.81 us
    ppermute x1, starting transfers between devices, shifted(): lax.ppermute(x, 'band', [(i, (i - distance) % groups) for i in range(grou...  1.56 us
    ppermute x1, waiting for transfers between devices, shifted(): lax.ppermute(x, 'band', [(i, (i - distance) % groups) for i in range(grou...  1.39 us
  transfers between devices with their start and end apart: 17, of which 7 were waited for; matrix products, arithmetic and copies ran while one was open for 0% of the time, Pallas kernels for 21%

profile of v11, /device:TPU:0, one launch (start us, length us, event | category | flops | bytes accessed | tf_op | source)
XLA Modules:
  0.0 61.7 jit_solution(1150249420778001146)
XLA Ops:
  0.0 1.9 %shard_map.91 = (f32[104,128]{1,0:T(8,128)}, f32[104,128]{1,0:T(8,128)}, f32[104,128]{1,0:T(8,128)}, f32[104,128]{1,0:T(8,128)}, f32[104,128]{1,0:T(8,128)}, /*i...) custom-call(f32[8,96,128]{2,1,0:T(8,128)} %sticks_ref.1, s32[1,128]{1,0:T(1,128)} %bitcast.1), custom_call_target="tpu_custom_call" | custom-call | flops 1 | bytes 1 | tf_op jit(solution)/shard_map/pallas_call | solution.py:312
  2.0 4.1 %collective-permute-start = (f32[104,128]{1,0:T(8,128)}, f32[104,128]{1,0:T(8,128)S(1)}, u32[]{:S(2)}, u32[]{:S(2)}) collective-permute-start(f32[104,128]{1,0:T(8,128)} %get-tuple-element.37), channel_id=1, source_target_pairs={{0,16},{4,20},{8,24},{12,28},{16,0},{20,4},{24,8},{28,12},{1,17},{... | collective-permute-start | bytes 159752 | tf_op jit(solution)/shard_map/ppermute | solution.py:333
  6.1 1.3 %collective-permute-start.1 = (f32[104,128]{1,0:T(8,128)}, f32[104,128]{1,0:T(8,128)S(1)}, u32[]{:S(2)}, u32[]{:S(2)}) collective-permute-start(f32[104,128]{1,0:T(8,128)} %get-tuple-element.38), channel_id=1, source_target_pairs={{0,20},{4,16},{8,28},{12,24},{16,4},{20,0},{24,12},{28,8},{1,21},{... | collective-permute-start | bytes 159752 | tf_op jit(solution)/shard_map/ppermute | solution.py:333
  7.4 3.6 %collective-permute-start.2 = (f32[104,128]{1,0:T(8,128)}, f32[104,128]{1,0:T(8,128)S(1)}, u32[]{:S(2)}, u32[]{:S(2)}) collective-permute-start(f32[104,128]{1,0:T(8,128)} %get-tuple-element.39), channel_id=1, source_target_pairs={{0,24},{4,28},{8,16},{12,20},{16,8},{20,12},{24,0},{28,4},{1,25},{... | collective-permute-start | bytes 159752 | tf_op jit(solution)/shard_map/ppermute | solution.py:333
  11.0 1.0 %copy-done.5 = f32[224,288]{1,0:T(8,128)S(1)} copy-done((f32[224,288]{1,0:T(8,128)S(1)}, f32[224,288]{1,0:T(8,128)}, u32[]{:S(2)}) %copy-start.5) | copy-done | bytes 258072
  11.9 0.8 %copy-done.7 = f32[104,128]{1,0:T(8,128)S(1)} copy-done((f32[104,128]{1,0:T(8,128)S(1)}, f32[104,128]{1,0:T(8,128)}, u32[]{:S(2)}) %copy-start.7) | copy-done | bytes 53272
  12.8 1.7 %collective-permute-start.4 = (f32[104,128]{1,0:T(8,128)}, f32[104,128]{1,0:T(8,128)S(1)}, u32[]{:S(2)}, u32[]{:S(2)}) collective-permute-start(f32[104,128]{1,0:T(8,128)} %get-tuple-element.44), channel_id=1, source_target_pairs={{0,4},{4,0},{8,12},{12,8},{16,20},{20,16},{24,28},{28,24},{1,5},{5... | collective-permute-start | bytes 159752 | tf_op jit(solution)/shard_map/ppermute | solution.py:333
  14.8 1.5 %collective-permute-start.6 = (f32[104,128]{1,0:T(8,128)}, f32[104,128]{1,0:T(8,128)S(1)}, u32[]{:S(2)}, u32[]{:S(2)}) collective-permute-start(f32[104,128]{1,0:T(8,128)} %get-tuple-element.48), channel_id=1, source_target_pairs={{0,12},{4,8},{8,4},{12,0},{16,28},{20,24},{24,20},{28,16},{1,13},{... | collective-permute-start | bytes 159752 | tf_op jit(solution)/shard_map/ppermute | solution.py:333
  16.4 2.1 %collective-permute-done.3.refs_4_ = f32[104,128]{1,0:T(8,128)S(1)} collective-permute-done((f32[104,128]{1,0:T(8,128)}, f32[104,128]{1,0:T(8,128)S(1)}, u32[]{:S(2)}, u32[]{:S(2)}) %collective-permute-start.3) | collective-permute-done | bytes 53280 | tf_op jit(solution)/shard_map/ppermute | solution.py:333
  18.9 1.2 %collective-permute-done.6.refs_7_ = f32[104,128]{1,0:T(8,128)S(1)} collective-permute-done((f32[104,128]{1,0:T(8,128)}, f32[104,128]{1,0:T(8,128)S(1)}, u32[]{:S(2)}, u32[]{:S(2)}) %collective-permute-start.6) | collective-permute-done | bytes 53280 | tf_op jit(solution)/shard_map/ppermute | solution.py:333
  20.1 1.6 %collective-permute-start.7 = (f32[768,128]{1,0:T(8,128)S(1)}, f32[768,128]{1,0:T(8,128)S(1)}, u32[]{:S(2)}, u32[]{:S(2)}) collective-permute-start(f32[768,128]{1,0:T(8,128)S(1)} %get-tuple-element.49.blocks_ref), channel_id=1, source_target_pairs={{0,2},{1,3},{2,0},{3,1},{4,6},{5,7},{6,4},{7,5},{8,10},{9,11},{10,... | collective-permute-start | bytes 1179656 | tf_op jit(solution)/shard_map/ppermute | solution.py:349
  21.6 4.0 %shard_map.94.phi_ref = f32[1152,128]{1,0:T(8,128)S(1)} custom-call(f32[768,128]{1,0:T(8,128)S(1)} %get-tuple-element.49.blocks_ref, f32[8,1024]{1,0:T(8,128)S(1)} %get-tuple-element.50.columns_ref, bf16[128,288]{1,0:T(8,128)(2,1)S(1)} %get-tuple-element.42.stick_in_ref, bf16[96,144]{1,0:T(8,128)(2,1)S(1)} %get-tuple-element.43.left_ref), custom_call_target="tpu_custom_call" | custom-call | flops 1 | bytes 1 | tf_op jit(solution)/shard_map/pallas_call | solution.py:312
  25.7 1.2 %shard_map.95.hot_ref = bf16[1024,2304]{1,0:T(8,128)(2,1)S(1)} custom-call(f32[8,1024]{1,0:T(8,128)S(1)} %get-tuple-element.50.columns_ref), custom_call_target="tpu_custom_call" | custom-call | flops 1 | bytes 1 | tf_op jit(solution)/shard_map/pallas_call | solution.py:312
  27.0 1.4 %collective-permute-done.7.blocks_ref = f32[768,128]{1,0:T(8,128)S(1)} collective-permute-done((f32[768,128]{1,0:T(8,128)S(1)}, f32[768,128]{1,0:T(8,128)S(1)}, u32[]{:S(2)}, u32[]{:S(2)}) %collective-permute-start.7) | collective-permute-done | bytes 393248 | tf_op jit(solution)/shard_map/ppermute | solution.py:349
  28.4 4.0 %shard_map.96.first_ref = f32[1152,128]{1,0:T(8,128)S(1)} custom-call(f32[768,128]{1,0:T(8,128)S(1)} %collective-permute-done.7.blocks_ref, f32[8,1024]{1,0:T(8,128)S(1)} %get-tuple-element.50.columns_ref, bf16[128,288]{1,0:T(8,128)(2,1)S(1)} %get-tuple-element.42.stick_in_ref, bf16[96,144]{1,0:T(8,128)(2,1)S(1)} %get-tuple-element.43.left_ref), custom_call_target="tpu_custom_call" | custom-call | flops 1 | bytes 1 | tf_op jit(solution)/shard_map/pallas_call | solution.py:312
  32.5 3.6 %shard_map.97.before_ref = f32[1152,128]{1,0:T(8,128)S(1)} custom-call(f32[1152,128]{1,0:T(8,128)S(1)} %shard_map.94.phi_ref, f32[1152,128]{1,0:T(8,128)S(1)} %collective-permute-done.9.other_ref, f32[256,256]{1,0:T(8,128)S(1)} %copy-done.2, f32[256,256]{1,0:T(8,128)S(1)} %copy-done.1, f32[96,144]{1,0:T(8,128)S(1)} %copy-done.4, f32[96,144]{1,0:T(8,128)S(1)} %copy-done.3, ...), custom_call_target="tpu_custom_call" | custom-call | flops 1 | bytes 1 | tf_op jit(solution)/shard_map/pallas_call | solution.py:312
  36.2 7.9 %shard_map.98 = (f32[96,128]{1,0:T(8,128)S(1)}, f32[96,128]{1,0:T(8,128)S(1)}, f32[96,128]{1,0:T(8,128)S(1)}, f32[96,128]{1,0:T(8,128)S(1)}, f32[96,128]{1,0:T(8...) custom-call(f32[1152,128]{1,0:T(8,128)S(1)} %shard_map.94.phi_ref, ...), custom_call_target="tpu_custom_call" | custom-call | flops 1 | bytes 1 | tf_op jit(solution)/shard_map/pallas_call | solution.py:312
  44.1 1.9 %collective-permute-start.13 = (f32[96,128]{1,0:T(8,128)S(1)}, f32[96,128]{1,0:T(8,128)S(1)}, u32[]{:S(2)}, u32[]{:S(2)}) collective-permute-start(f32[96,128]{1,0:T(8,128)S(1)} %get-tuple-element.58), channel_id=1, source_target_pairs={{0,8},{4,12},{8,0},{12,4},{16,24},{20,28},{24,16},{28,20},{1,9},{5... | collective-permute-start | bytes 147464 | tf_op jit(solution)/shard_map/ppermute | solution.py:333
  46.5 3.1 %collective-permute-start.10 = (f32[96,128]{1,0:T(8,128)S(1)}, f32[96,128]{1,0:T(8,128)S(1)}, u32[]{:S(2)}, u32[]{:S(2)}) collective-permute-start(f32[96,128]{1,0:T(8,128)S(1)} %get-tuple-element.54), channel_id=1, source_target_pairs={{0,16},{4,20},{8,24},{12,28},{16,0},{20,4},{24,8},{28,12},{1,17},{... | collective-permute-start | bytes 147464 | tf_op jit(solution)/shard_map/ppermute | solution.py:333
  49.6 1.5 %collective-permute-start.11 = (f32[96,128]{1,0:T(8,128)S(1)}, f32[96,128]{1,0:T(8,128)S(1)}, u32[]{:S(2)}, u32[]{:S(2)}) collective-permute-start(f32[96,128]{1,0:T(8,128)S(1)} %get-tuple-element.55), channel_id=1, source_target_pairs={{0,20},{4,16},{8,28},{12,24},{16,4},{20,0},{24,12},{28,8},{1,21},{... | collective-permute-start | bytes 147464 | tf_op jit(solution)/shard_map/ppermute | solution.py:333
  51.0 3.1 %collective-permute-start.12 = (f32[96,128]{1,0:T(8,128)S(1)}, f32[96,128]{1,0:T(8,128)S(1)}, u32[]{:S(2)}, u32[]{:S(2)}) collective-permute-start(f32[96,128]{1,0:T(8,128)S(1)} %get-tuple-element.56), channel_id=1, source_target_pairs={{0,24},{4,28},{8,16},{12,20},{16,8},{20,12},{24,0},{28,4},{1,25},{... | collective-permute-start | bytes 147464 | tf_op jit(solution)/shard_map/ppermute | solution.py:333
  55.4 2.1 %collective-permute-done.11.refs_2_ = f32[96,128]{1,0:T(8,128)S(1)} collective-permute-done((f32[96,128]{1,0:T(8,128)S(1)}, f32[96,128]{1,0:T(8,128)S(1)}, u32[]{:S(2)}, u32[]{:S(2)}) %collective-permute-start.11) | collective-permute-done | bytes 49184 | tf_op jit(solution)/shard_map/ppermute | solution.py:333
  57.6 3.3 %collective-permute-done.14.refs_4_ = f32[96,128]{1,0:T(8,128)S(1)} collective-permute-done((f32[96,128]{1,0:T(8,128)S(1)}, f32[96,128]{1,0:T(8,128)S(1)}, u32[]{:S(2)}, u32[]{:S(2)}) %collective-permute-start.14) | collective-permute-done | bytes 49184 | tf_op jit(solution)/shard_map/ppermute | solution.py:333
  60.9 0.8 %shard_map.99 = f32[8,96,128]{2,1,0:T(8,128)} custom-call(f32[96,128]{1,0:T(8,128)S(1)} %get-tuple-element.53.refs_0_, f32[96,128]{1,0:T(8,128)S(1)} %collective-permute-done.10.refs_1_, f32[96,128]{1,0:T(8,128)S(1)} %collective-permute-done.11.refs_2_, f32[96,128]{1,0:T(8,128)S(1)} %collective-permute-done.12.refs_3_, ...), custom_call_target="tpu_custom_call" | custom-call | flops 1 | bytes 1 | tf_op jit(solution)/shard_map/pallas_call | solution.py:312
  (35 shorter events, 2.8 us)
Async XLA Ops:
  0.0 32.5 %copy-start = (f32[2304,128]{1,0:T(8,128)S(1)}, f32[2304,128]{1,0:T(8,128)}, u32[]{:S(2)}) copy-start(f32[2304,128]{1,0:T(8,128)} %constant.20.clone.refs_4_) | copy-start | bytes 3538948
  0.0 32.5 %copy-start.3 = (f32[96,144]{1,0:T(8,128)S(1)}, f32[96,144]{1,0:T(8,128)}, u32[]{:S(2)}) copy-start(f32[96,144]{1,0:T(8,128)} %constant.17.clone.refs_3_) | copy-start | bytes 165892
  0.0 32.5 %copy-start.4 = (f32[96,144]{1,0:T(8,128)S(1)}, f32[96,144]{1,0:T(8,128)}, u32[]{:S(2)}) copy-start(f32[96,144]{1,0:T(8,128)} %constant.16.clone.refs_2_) | copy-start | bytes 165892
  0.0 32.5 %copy-start.1 = (f32[256,256]{1,0:T(8,128)S(1)}, f32[256,256]{1,0:T(8,128)}, u32[]{:S(2)}) copy-start(f32[256,256]{1,0:T(8,128)} %constant.15.clone.refs_1_) | copy-start | bytes 786436
  0.0 32.5 %copy-start.2 = (f32[256,256]{1,0:T(8,128)S(1)}, f32[256,256]{1,0:T(8,128)}, u32[]{:S(2)}) copy-start(f32[256,256]{1,0:T(8,128)} %constant.14.clone.refs_0_) | copy-start | bytes 786436
  2.0 10.8 %collective-permute-start = (f32[104,128]{1,0:T(8,128)}, f32[104,128]{1,0:T(8,128)S(1)}, u32[]{:S(2)}, u32[]{:S(2)}) collective-permute-start(f32[104,128]{1,0:T(8,128)} %get-tuple-element.37), channel_id=1, source_target_pairs={{0,16},{4,20},{8,24},{12,28},{16,0},{20,4},{24,8},{28,12},{1,17},{... | collective-permute-start | bytes 159752 | tf_op jit(solution)/shard_map/ppermute | solution.py:333
  6.1 8.7 %collective-permute-start.1 = (f32[104,128]{1,0:T(8,128)}, f32[104,128]{1,0:T(8,128)S(1)}, u32[]{:S(2)}, u32[]{:S(2)}) collective-permute-start(f32[104,128]{1,0:T(8,128)} %get-tuple-element.38), channel_id=1, source_target_pairs={{0,20},{4,16},{8,28},{12,24},{16,4},{20,0},{24,12},{28,8},{1,21},{... | collective-permute-start | bytes 159752 | tf_op jit(solution)/shard_map/ppermute | solution.py:333
  7.4 9.0 %collective-permute-start.2 = (f32[104,128]{1,0:T(8,128)}, f32[104,128]{1,0:T(8,128)S(1)}, u32[]{:S(2)}, u32[]{:S(2)}) collective-permute-start(f32[104,128]{1,0:T(8,128)} %get-tuple-element.39), channel_id=1, source_target_pairs={{0,24},{4,28},{8,16},{12,20},{16,8},{20,12},{24,0},{28,4},{1,25},{... | collective-permute-start | bytes 159752 | tf_op jit(solution)/shard_map/ppermute | solution.py:333
  11.0 7.5 %collective-permute-start.3 = (f32[104,128]{1,0:T(8,128)}, f32[104,128]{1,0:T(8,128)S(1)}, u32[]{:S(2)}, u32[]{:S(2)}) collective-permute-start(f32[104,128]{1,0:T(8,128)} %get-tuple-element.40), channel_id=1, source_target_pairs={{0,28},{4,24},{8,20},{12,16},{16,12},{20,8},{24,4},{28,0},{1,29},{... | collective-permute-start | bytes 159752 | tf_op jit(solution)/shard_map/ppermute | solution.py:333
  11.0 1.0 %copy-start.5 = (f32[224,288]{1,0:T(8,128)S(1)}, f32[224,288]{1,0:T(8,128)}, u32[]{:S(2)}) copy-start(f32[224,288]{1,0:T(8,128)} %constant.18.clone.tables_ref) | copy-start | bytes 774148
  12.8 5.6 %collective-permute-start.4 = (f32[104,128]{1,0:T(8,128)}, f32[104,128]{1,0:T(8,128)S(1)}, u32[]{:S(2)}, u32[]{:S(2)}) collective-permute-start(f32[104,128]{1,0:T(8,128)} %get-tuple-element.44), channel_id=1, source_target_pairs={{0,4},{4,0},{8,12},{12,8},{16,20},{20,16},{24,28},{28,24},{1,5},{5... | collective-permute-start | bytes 159752 | tf_op jit(solution)/shard_map/ppermute | solution.py:333
  14.5 4.3 %collective-permute-start.5 = (f32[104,128]{1,0:T(8,128)}, f32[104,128]{1,0:T(8,128)S(1)}, u32[]{:S(2)}, u32[]{:S(2)}) collective-permute-start(f32[104,128]{1,0:T(8,128)} %get-tuple-element.46), channel_id=1, source_target_pairs={{0,8},{4,12},{8,0},{12,4},{16,24},{20,28},{24,16},{28,20},{1,9},{5... | collective-permute-start | bytes 159752 | tf_op jit(solution)/shard_map/ppermute | solution.py:333
  14.8 5.2 %collective-permute-start.6 = (f32[104,128]{1,0:T(8,128)}, f32[104,128]{1,0:T(8,128)S(1)}, u32[]{:S(2)}, u32[]{:S(2)}) collective-permute-start(f32[104,128]{1,0:T(8,128)} %get-tuple-element.48), channel_id=1, source_target_pairs={{0,12},{4,8},{8,4},{12,0},{16,28},{20,24},{24,20},{28,16},{1,13},{... | collective-permute-start | bytes 159752 | tf_op jit(solution)/shard_map/ppermute | solution.py:333
  20.1 8.3 %collective-permute-start.7 = (f32[768,128]{1,0:T(8,128)S(1)}, f32[768,128]{1,0:T(8,128)S(1)}, u32[]{:S(2)}, u32[]{:S(2)}) collective-permute-start(f32[768,128]{1,0:T(8,128)S(1)} %get-tuple-element.49.blocks_ref), channel_id=1, source_target_pairs={{0,2},{1,3},{2,0},{3,1},{4,6},{5,7},{6,4},{7,5},{8,10},{9,11},{10,... | collective-permute-start | bytes 1179656 | tf_op jit(solution)/shard_map/ppermute | solution.py:349
  25.7 10.5 %copy-start.6 = (f32[96,384]{1,0:T(8,128)S(1)}, f32[96,384]{1,0:T(8,128)}, u32[]{:S(2)}) copy-start(f32[96,384]{1,0:T(8,128)} %constant.19.clone.stick_out_ref) | copy-start | bytes 442372
  25.7 6.8 %collective-permute-start.9 = (f32[1152,128]{1,0:T(8,128)S(1)}, f32[1152,128]{1,0:T(8,128)S(1)}, u32[]{:S(2)}, u32[]{:S(2)}) collective-permute-start(f32[1152,128]{1,0:T(8,128)S(1)} %shard_map.94.phi_ref), channel_id=1, source_target_pairs={{0,1},{1,0},{2,3},{3,2},{4,5},{5,4},{6,7},{7,6},{8,9},{9,8},{10,11... | collective-permute-start | bytes 1769480 | tf_op jit(solution)/shard_map/ppermute | solution.py:352
  32.4 3.8 %collective-permute-start.8 = (f32[1152,128]{1,0:T(8,128)S(1)}, f32[1152,128]{1,0:T(8,128)S(1)}, u32[]{:S(2)}, u32[]{:S(2)}) collective-permute-start(f32[1152,128]{1,0:T(8,128)S(1)} %shard_map.96.first_ref), channel_id=1, source_target_pairs={{0,1},{1,0},{2,3},{3,2},{4,5},{5,4},{6,7},{7,6},{8,9},{9,8},{10,11... | collective-permute-start | bytes 1769480 | tf_op jit(solution)/shard_map/ppermute | solution.py:352
  44.1 10.0 %collective-permute-start.13 = (f32[96,128]{1,0:T(8,128)S(1)}, f32[96,128]{1,0:T(8,128)S(1)}, u32[]{:S(2)}, u32[]{:S(2)}) collective-permute-start(f32[96,128]{1,0:T(8,128)S(1)} %get-tuple-element.58), channel_id=1, source_target_pairs={{0,8},{4,12},{8,0},{12,4},{16,24},{20,28},{24,16},{28,20},{1,9},{5... | collective-permute-start | bytes 147464 | tf_op jit(solution)/shard_map/ppermute | solution.py:333
  46.0 8.9 %collective-permute-start.15 = (f32[96,128]{1,0:T(8,128)S(1)}, f32[96,128]{1,0:T(8,128)S(1)}, u32[]{:S(2)}, u32[]{:S(2)}) collective-permute-start(f32[96,128]{1,0:T(8,128)S(1)} %get-tuple-element.60), channel_id=1, source_target_pairs={{0,4},{4,0},{8,12},{12,8},{16,20},{20,16},{24,28},{28,24},{1,5},{5... | collective-permute-start | bytes 147464 | tf_op jit(solution)/shard_map/ppermute | solution.py:333
  46.5 9.0 %collective-permute-start.10 = (f32[96,128]{1,0:T(8,128)S(1)}, f32[96,128]{1,0:T(8,128)S(1)}, u32[]{:S(2)}, u32[]{:S(2)}) collective-permute-start(f32[96,128]{1,0:T(8,128)S(1)} %get-tuple-element.54), channel_id=1, source_target_pairs={{0,16},{4,20},{8,24},{12,28},{16,0},{20,4},{24,8},{28,12},{1,17},{... | collective-permute-start | bytes 147464 | tf_op jit(solution)/shard_map/ppermute | solution.py:333
  49.6 8.0 %collective-permute-start.11 = (f32[96,128]{1,0:T(8,128)S(1)}, f32[96,128]{1,0:T(8,128)S(1)}, u32[]{:S(2)}, u32[]{:S(2)}) collective-permute-start(f32[96,128]{1,0:T(8,128)S(1)} %get-tuple-element.55), channel_id=1, source_target_pairs={{0,20},{4,16},{8,28},{12,24},{16,4},{20,0},{24,12},{28,8},{1,21},{... | collective-permute-start | bytes 147464 | tf_op jit(solution)/shard_map/ppermute | solution.py:333
  51.0 6.5 %collective-permute-start.12 = (f32[96,128]{1,0:T(8,128)S(1)}, f32[96,128]{1,0:T(8,128)S(1)}, u32[]{:S(2)}, u32[]{:S(2)}) collective-permute-start(f32[96,128]{1,0:T(8,128)S(1)} %get-tuple-element.56), channel_id=1, source_target_pairs={{0,24},{4,28},{8,16},{12,20},{16,8},{20,12},{24,0},{28,4},{1,25},{... | collective-permute-start | bytes 147464 | tf_op jit(solution)/shard_map/ppermute | solution.py:333
  54.1 6.8 %collective-permute-start.14 = (f32[96,128]{1,0:T(8,128)S(1)}, f32[96,128]{1,0:T(8,128)S(1)}, u32[]{:S(2)}, u32[]{:S(2)}) collective-permute-start(f32[96,128]{1,0:T(8,128)S(1)} %get-tuple-element.59), channel_id=1, source_target_pairs={{0,28},{4,24},{8,20},{12,16},{16,12},{20,8},{24,4},{28,0},{1,29},{... | collective-permute-start | bytes 147464 | tf_op jit(solution)/shard_map/ppermute | solution.py:333
  54.9 6.0 %collective-permute-start.16 = (f32[96,128]{1,0:T(8,128)S(1)}, f32[96,128]{1,0:T(8,128)S(1)}, u32[]{:S(2)}, u32[]{:S(2)}) collective-permute-start(f32[96,128]{1,0:T(8,128)S(1)} %get-tuple-element.62), channel_id=1, source_target_pairs={{0,12},{4,8},{8,4},{12,0},{16,28},{20,24},{24,20},{28,16},{1,13},{... | collective-permute-start | bytes 147464 | tf_op jit(solution)/shard_map/ppermute | solution.py:333
  (1 other events, 0.8 us)

commit v12 on v11

--- a/solution.py
+++ b/solution.py
@@ -13,7 +13,6 @@
 BOX_LENGTH = 18.0
 LANES = 128
 MID = 64
-WINDOW = 5
 SEND_GRANT = 60
 PAIRS = 6
 
@@ -212,13 +211,16 @@
         store(phi_ref, y, [jnp.where(low, cos - turned(sin), turned(cos_up) - sin_up)])
 
 
-def pick_kernel(g, columns_ref, hot_ref):
-    for k in range(0, columns_ref.shape[1], LANES):
-        block = columns_ref[:, k : k + LANES]
-        wanted = jnp.concatenate([block] * (LANES // block.shape[0]), 0).T.astype(jnp.int32)
-        for c in range(0, hot_ref.shape[1], LANES):
-            index = lax.broadcasted_iota(jnp.int16, (LANES, LANES), 1)
-            hot_ref[k : k + LANES, c : c + LANES] = one_hot(index, (wanted - c).astype(jnp.int16))
+def hot_kernel(g, columns_ref, *hot_refs):
+    first = 0
+    for hot_ref in hot_refs:
+        for k in range(0, hot_ref.shape[0], LANES):
+            block = columns_ref[:, first + k : first + k + LANES]
+            wanted = jnp.concatenate([block] * (LANES // block.shape[0]), 0).T.astype(jnp.int32)
+            for c in range(0, hot_ref.shape[1], LANES):
+                index = lax.broadcasted_iota(jnp.int16, (LANES, LANES), 1)
+                hot_ref[k : k + LANES, c : c + LANES] = one_hot(index, (wanted - c).astype(jnp.int16))
+        first += hot_ref.shape[0]
 
 
 def potentials(g, phi_ref, first_ref, second_ref, tables, work_a, work_b, emit):
@@ -270,9 +272,8 @@
     potentials(g, phi_ref, first_ref, second_ref, tables, work_a, work_b, emit)
 
 
-def far_kernel(g, weights, phi_ref, first_ref, second_ref, before_ref, hot_ref, stick_out_ref, *refs):
-    tables, out_refs = refs[:5], refs[5:-3]
-    work_a, work_b, picked_ref = refs[-3:]
+def far_kernel(g, weights, phi_ref, first_ref, second_ref, before_ref, *refs):
+    tables, (spectrum_ref, work_a, work_b) = refs[:5], refs[5:]
     forward = tables[2][...].astype(BF16)
     half = g // 2
 
@@ -289,22 +290,18 @@
 
     potentials(g, phi_ref, first_ref, second_ref, tables, work_a, work_b, emit)
 
-    step = g // 3
-    for first in range(0, g, step):
-        slabs = []
-        for kx in range(first, first + step, 2):
-            slabs += left_complex(forward, strided(work_a, kx, g), strided(work_a, kx + 1, g))
-        spectrum = beside(*split(jnp.concatenate(slabs, 0)))
-        both = dot(hot_ref[:, first * g : (first + step) * g], spectrum)
-        both = both[:, :LANES] + both[:, LANES:]
-        picked_ref[...] = both if first == 0 else picked_ref[...] + both
-
+    for kx in range(0, g, 2):
+        slabs = left_complex(forward, strided(work_a, kx, g), strided(work_a, kx + 1, g))
+        spectrum_ref[slab_rows(kx, g, 2), :] = beside(*split(jnp.concatenate(slabs, 0)))
+
+
+def pick_kernel(g, spectrum_ref, hot_ref, stick_out_ref, *out_refs):
+    both = dot(hot_ref[...], spectrum_ref[...])
+    picked = both[:, :LANES] + both[:, LANES:]
     stick_out = stick_out_ref[...].astype(BF16)
     for k in range(0, len(out_refs), 2):
-        high, low = split(picked_ref[k * LANES : (k + 2) * LANES, :])
-        lined = jnp.concatenate([high, low, high], 1)
-        out = lax.dot_general(stick_out, lined, (((1,), (1,)), ((), ())), preferred_element_type=F32)
-        out_refs[k][...], out_refs[k + 1][...] = halves(out)
+        lined = beside(*[picked[j * LANES : (j + 1) * LANES].T for j in (k, k + 1)])
+        out_refs[k][...], out_refs[k + 1][...] = halves(dot(stick_out, stacked(lined)))
 
 
 def call(kernel, out_shapes, scratch, flops, *operands, space=pltpu.VMEM, out_space=pltpu.VMEM, grant=40):
@@ -324,14 +321,8 @@
     return lax.optimization_barrier((x, *others))[0]
 
 
-def exchanged(blocks, order, before):
-    owners = len(blocks)
-    moved = [blocks[0]] + [None] * (owners - 1)
-    for d in order:
-        others = [moved[x] if isinstance(x, int) else x for x in before.get(d, ())]
-        block = after(blocks[d], *others) if others else blocks[d]
-        moved[d] = lax.ppermute(block, "stick", [(i, i ^ d) for i in range(owners)])
-    return moved
+def moved(block, d, owners):
+    return lax.ppermute(block, "stick", [(i, i ^ d) for i in range(owners)])
 
 
 def on_device(sticks, stick_columns):
@@ -376,9 +367,12 @@
     )
     half = owners // 2
     distant, close = list(range(half, owners)), list(range(1, half))
-    received = exchanged(sent, distant + close, {d: (half, staged, *first_tables) for d in close})
-    received[0] = staged
-    order = [0] + distant + close
+    received = {0: staged}
+    for d in distant:
+        received[d] = moved(sent[d], d, owners)
+    for d in close:
+        received[d] = moved(after(sent[d], received[half], staged, *first_tables), d, owners)
+    order = distant + close + [0]
     relay, columns = call(
         functools.partial(relay_kernel, g),
         [jax.ShapeDtypeStruct((owners * 2 * g, slots), F32), jax.ShapeDtypeStruct((8, owners * slots), F32)],
@@ -393,7 +387,11 @@
     phi = orbital(relay)
     near = swapped(phi)
     hot = call(
-        functools.partial(pick_kernel, g), jax.ShapeDtypeStruct((owners * slots, rows), BF16), [], pot_flops, columns
+        functools.partial(hot_kernel, g),
+        [jax.ShapeDtypeStruct((half * slots, rows), BF16)] * 2,
+        [],
+        pot_flops,
+        columns,
     )
     pot_tables = [t["forward"], t["last_backward"], t["left_forward"], t["left_backward"], t["coulomb"]]
 
@@ -401,7 +399,7 @@
         return call(functools.partial(kernel, g), field, [work, work], pot_flops, phi, *operands, *pot_tables)
 
     distances = (HALF,) if groups == 2 * HALF else (HALF, -HALF)
-    fields = [orbital(after(shifted(relay, distance), hot)) for distance in distances]
+    fields = [orbital(after(shifted(relay, distance), *hot)) for distance in distances]
     total = potential_sum(near_kernel, after(near, *fields))
     if groups == 2 * HALF:
         weights = (2.0, 1.0)
@@ -411,23 +409,28 @@
         odd = lax.axis_index("band") % 2 == 1
         first = second = swapped(jnp.where(odd, fields[1], fields[0]))
         total = potential_sum(middle_kernel, *fields, total)
-    result = call(
+    spectrum = call(
         functools.partial(far_kernel, g, weights),
-        [jax.ShapeDtypeStruct((2 * g, slots), F32)] * owners,
-        [work, work, pltpu.VMEM((owners * slots, LANES), F32)],
+        jax.ShapeDtypeStruct((rows, 2 * LANES), BF16),
+        [work, work],
         pot_flops,
         phi,
         first,
         second,
         total,
-        hot,
-        t["stick_out"],
         *pot_tables,
     )
-    result = [result[order.index(d)] for d in range(owners)]
-    mixed = [distant[0]] + [d for pair in zip(close, distant[1:]) for d in pair]
-    before = {mixed[k]: (mixed[k - 3 - k % 2],) for k in range(WINDOW, len(mixed))}
-    result = exchanged(result, mixed, before)
+
+    def picked(spectrum, hot):
+        shapes = [jax.ShapeDtypeStruct((2 * g, slots), F32)] * half
+        return call(functools.partial(pick_kernel, g), shapes, [], 1, spectrum, hot, t["stick_out"])
+
+    result = {}
+    for d, block in zip(distant, picked(spectrum, hot[0])):
+        result[d] = moved(block, d, owners)
+    *blocks, result[0] = picked(after(spectrum, result[half]), hot[1])
+    for k, block in enumerate(blocks):
+        result[close[k]] = moved(block, close[k], owners)
     return call(
         functools.partial(place_kernel, order),
         jax.ShapeDtypeStruct(sticks.shape, F32),

time: 61.9 us -> 62.8 us (1.015)
    pallas_call x9 -> x11, Pallas kernels: 23.5 us -> 24.1 us  [call(): pl.pallas_call(kernel, out_shape=out_shapes, in_specs=[pl.BlockSpec(memor...]
  transfers between devices with their start and end apart: 17 -> 17, of which waited for: 7 -> 10; matrix products, arithmetic and copies ran while one was open for 0% -> 0% of each run, Pallas kernels for 21% -> 22%
where the time goes in v12:
time: 62.8 us; the launch traced here: 62.6 us
  starting transfers between devices  25 us (40%)
  Pallas kernels  24.1 us (38%)
  waiting for transfers between devices  11.5 us (18%)
  local copies, waits for them, and re-layouts  1.81 us (3%)
    pallas_call x11, Pallas kernels, call(): pl.pallas_call(kernel, out_shape=out_shapes, in_specs=[pl.BlockSpec(memor...  24.1 us
    ppermute x14, starting transfers between devices, moved(): return lax.ppermute(block, 'stick', [(i, i ^ d) for i in range(owners)])  23.3 us
    ppermute x14, waiting for transfers between devices, moved(): return lax.ppermute(block, 'stick', [(i, i ^ d) for i in range(owners)])  10 us
    unnamed x16, local copies, waits for them, and re-layouts  1.81 us
    ppermute x1, starting transfers between devices, shifted(): lax.ppermute(x, 'band', [(i, (i - distance) % groups) for i in range(grou...  1.56 us
    ppermute x1, waiting for transfers between devices, shifted(): lax.ppermute(x, 'band', [(i, (i - distance) % groups) for i in range(grou...  1.4 us
  transfers between devices with their start and end apart: 17, of which 10 were waited for; matrix products, arithmetic and copies ran while one was open for 0% of the time, Pallas kernels for 22%

profile of v12, /device:TPU:0, one launch (start us, length us, event | category | flops | bytes accessed | tf_op | source)
XLA Modules:
  0.0 62.6 jit_solution(14279268417964519398)
XLA Ops:
  0.0 1.9 %shard_map.91 = (f32[104,128]{1,0:T(8,128)}, f32[104,128]{1,0:T(8,128)}, f32[104,128]{1,0:T(8,128)}, f32[104,128]{1,0:T(8,128)}, f32[104,128]{1,0:T(8,128)}, /*i...) custom-call(f32[8,96,128]{2,1,0:T(8,128)} %sticks_ref.1, s32[1,128]{1,0:T(1,128)} %bitcast.1), custom_call_target="tpu_custom_call" | custom-call | flops 1 | bytes 1 | tf_op jit(solution)/shard_map/pallas_call | solution.py:309
  2.0 4.1 %collective-permute-start = (f32[104,128]{1,0:T(8,128)}, f32[104,128]{1,0:T(8,128)S(1)}, u32[]{:S(2)}, u32[]{:S(2)}) collective-permute-start(f32[104,128]{1,0:T(8,128)} %get-tuple-element.35), channel_id=1, source_target_pairs={{0,16},{4,20},{8,24},{12,28},{16,0},{20,4},{24,8},{28,12},{1,17},{... | collective-permute-start | bytes 159752 | tf_op jit(solution)/shard_map/ppermute | solution.py:325
  6.1 1.3 %collective-permute-start.1 = (f32[104,128]{1,0:T(8,128)}, f32[104,128]{1,0:T(8,128)S(1)}, u32[]{:S(2)}, u32[]{:S(2)}) collective-permute-start(f32[104,128]{1,0:T(8,128)} %get-tuple-element.36), channel_id=1, source_target_pairs={{0,20},{4,16},{8,28},{12,24},{16,4},{20,0},{24,12},{28,8},{1,21},{... | collective-permute-start | bytes 159752 | tf_op jit(solution)/shard_map/ppermute | solution.py:325
  7.4 3.6 %collective-permute-start.2 = (f32[104,128]{1,0:T(8,128)}, f32[104,128]{1,0:T(8,128)S(1)}, u32[]{:S(2)}, u32[]{:S(2)}) collective-permute-start(f32[104,128]{1,0:T(8,128)} %get-tuple-element.37), channel_id=1, source_target_pairs={{0,24},{4,28},{8,16},{12,20},{16,8},{20,12},{24,0},{28,4},{1,25},{... | collective-permute-start | bytes 159752 | tf_op jit(solution)/shard_map/ppermute | solution.py:325
  12.8 1.7 %collective-permute-start.4 = (f32[104,128]{1,0:T(8,128)}, f32[104,128]{1,0:T(8,128)S(1)}, u32[]{:S(2)}, u32[]{:S(2)}) collective-permute-start(f32[104,128]{1,0:T(8,128)} %get-tuple-element.45), channel_id=1, source_target_pairs={{0,4},{4,0},{8,12},{12,8},{16,20},{20,16},{24,28},{28,24},{1,5},{5... | collective-permute-start | bytes 159752 | tf_op jit(solution)/shard_map/ppermute | solution.py:325
  14.8 1.5 %collective-permute-start.6 = (f32[104,128]{1,0:T(8,128)}, f32[104,128]{1,0:T(8,128)S(1)}, u32[]{:S(2)}, u32[]{:S(2)}) collective-permute-start(f32[104,128]{1,0:T(8,128)} %get-tuple-element.49), channel_id=1, source_target_pairs={{0,12},{4,8},{8,4},{12,0},{16,28},{20,24},{24,20},{28,16},{1,13},{... | collective-permute-start | bytes 159752 | tf_op jit(solution)/shard_map/ppermute | solution.py:325
  16.4 2.1 %collective-permute-done.3.refs_3_ = f32[104,128]{1,0:T(8,128)S(1)} collective-permute-done((f32[104,128]{1,0:T(8,128)}, f32[104,128]{1,0:T(8,128)S(1)}, u32[]{:S(2)}, u32[]{:S(2)}) %collective-permute-start.3) | collective-permute-done | bytes 53280 | tf_op jit(solution)/shard_map/ppermute | solution.py:325
  18.9 1.2 %collective-permute-done.6.refs_6_ = f32[104,128]{1,0:T(8,128)S(1)} collective-permute-done((f32[104,128]{1,0:T(8,128)}, f32[104,128]{1,0:T(8,128)S(1)}, u32[]{:S(2)}, u32[]{:S(2)}) %collective-permute-start.6) | collective-permute-done | bytes 53280 | tf_op jit(solution)/shard_map/ppermute | solution.py:325
  20.1 1.6 %collective-permute-start.7 = (f32[768,128]{1,0:T(8,128)S(1)}, f32[768,128]{1,0:T(8,128)S(1)}, u32[]{:S(2)}, u32[]{:S(2)}) collective-permute-start(f32[768,128]{1,0:T(8,128)S(1)} %get-tuple-element.50.blocks_ref), channel_id=1, source_target_pairs={{0,2},{1,3},{2,0},{3,1},{4,6},{5,7},{6,4},{7,5},{8,10},{9,11},{10,... | collective-permute-start | bytes 1179656 | tf_op jit(solution)/shard_map/ppermute | solution.py:340
  21.6 4.0 %shard_map.94.phi_ref = f32[1152,128]{1,0:T(8,128)S(1)} custom-call(f32[768,128]{1,0:T(8,128)S(1)} %get-tuple-element.50.blocks_ref, f32[8,1024]{1,0:T(8,128)S(1)} %get-tuple-element.51.columns_ref, bf16[128,288]{1,0:T(8,128)(2,1)S(1)} %get-tuple-element.43.stick_in_ref, bf16[96,144]{1,0:T(8,128)(2,1)S(1)} %get-tuple-element.44.left_ref), custom_call_target="tpu_custom_call" | custom-call | flops 1 | bytes 1 | tf_op jit(solution)/shard_map/pallas_call | solution.py:309
  25.7 1.2 %shard_map.95 = (bf16[512,2304]{1,0:T(8,128)(2,1)S(1)}, bf16[512,2304]{1,0:T(8,128)(2,1)S(1)}) custom-call(f32[8,1024]{1,0:T(8,128)S(1)} %get-tuple-element.51.columns_ref), custom_call_target="tpu_custom_call" | custom-call | flops 1 | bytes 1 | tf_op jit(solution)/shard_map/pallas_call | solution.py:309
  27.0 1.4 %collective-permute-done.7.blocks_ref = f32[768,128]{1,0:T(8,128)S(1)} collective-permute-done((f32[768,128]{1,0:T(8,128)S(1)}, f32[768,128]{1,0:T(8,128)S(1)}, u32[]{:S(2)}, u32[]{:S(2)}) %collective-permute-start.7) | collective-permute-done | bytes 393248 | tf_op jit(solution)/shard_map/ppermute | solution.py:340
  28.4 4.0 %shard_map.96.first_ref = f32[1152,128]{1,0:T(8,128)S(1)} custom-call(f32[768,128]{1,0:T(8,128)S(1)} %collective-permute-done.7.blocks_ref, f32[8,1024]{1,0:T(8,128)S(1)} %get-tuple-element.51.columns_ref, bf16[128,288]{1,0:T(8,128)(2,1)S(1)} %get-tuple-element.43.stick_in_ref, bf16[96,144]{1,0:T(8,128)(2,1)S(1)} %get-tuple-element.44.left_ref), custom_call_target="tpu_custom_call" | custom-call | flops 1 | bytes 1 | tf_op jit(solution)/shard_map/pallas_call | solution.py:309
  32.5 3.6 %shard_map.97.before_ref = f32[1152,128]{1,0:T(8,128)S(1)} custom-call(f32[1152,128]{1,0:T(8,128)S(1)} %shard_map.94.phi_ref, f32[1152,128]{1,0:T(8,128)S(1)} %collective-permute-done.9.other_ref, f32[256,256]{1,0:T(8,128)S(1)} %copy-done.2, f32[256,256]{1,0:T(8,128)S(1)} %copy-done.1, f32[96,144]{1,0:T(8,128)S(1)} %copy-done.5, f32[96,144]{1,0:T(8,128)S(1)} %copy-done.4, ...), custom_call_target="tpu_custom_call" | custom-call | flops 1 | bytes 1 | tf_op jit(solution)/shard_map/pallas_call | solution.py:309
  36.2 6.3 %shard_map.98.spectrum_ref = bf16[2304,256]{1,0:T(8,128)(2,1)S(1)} custom-call(f32[1152,128]{1,0:T(8,128)S(1)} %shard_map.94.phi_ref, f32[1152,128]{1,0:T(8,128)S(1)} %shard_map.96.first_ref, f32[1152,128]{1,0:T(8,128)S(1)} %collective-permute-done.8.second_ref, f32[1152,128]{1,0:T(8,128)S(1)} %shard_map.97.before_ref, f32[256,256]{1,0:T(8,128)S(1)} %copy-done.2, ...), custom_call_target="tpu_custom_call" | custom-call | flops 1 | bytes 1 | tf_op jit(solution)/shard_map/pallas_call | solution.py:309
  42.5 1.1 %shard_map.99 = (f32[96,128]{1,0:T(8,128)S(1)}, f32[96,128]{1,0:T(8,128)S(1)}, f32[96,128]{1,0:T(8,128)S(1)}, f32[96,128]{1,0:T(8,128)S(1)}) custom-call(bf16[2304,256]{1,0:T(8,128)(2,1)S(1)} %shard_map.98.spectrum_ref, bf16[512,2304]{1,0:T(8,128)(2,1)S(1)} %get-tuple-element.52.hot_ref, f32[96,384]{1,0:T(8,128)S(1)} %copy-done.3), custom_call_target="tpu_custom_call" | custom-call | flops 1 | bytes 1 | tf_op jit(solution)/shard_map/pallas_call | solution.py:309
  43.6 4.2 %collective-permute-start.10 = (f32[96,128]{1,0:T(8,128)S(1)}, f32[96,128]{1,0:T(8,128)S(1)}, u32[]{:S(2)}, u32[]{:S(2)}) collective-permute-start(f32[96,128]{1,0:T(8,128)S(1)} %get-tuple-element.56), channel_id=1, source_target_pairs={{0,16},{4,20},{8,24},{12,28},{16,0},{20,4},{24,8},{28,12},{1,17},{... | collective-permute-start | bytes 147464 | tf_op jit(solution)/shard_map/ppermute | solution.py:325
  47.8 2.8 %collective-permute-start.12 = (f32[96,128]{1,0:T(8,128)S(1)}, f32[96,128]{1,0:T(8,128)S(1)}, u32[]{:S(2)}, u32[]{:S(2)}) collective-permute-start(f32[96,128]{1,0:T(8,128)S(1)} %get-tuple-element.58), channel_id=1, source_target_pairs={{0,24},{4,28},{8,16},{12,20},{16,8},{20,12},{24,0},{28,4},{1,25},{... | collective-permute-start | bytes 147464 | tf_op jit(solution)/shard_map/ppermute | solution.py:325
  50.6 2.0 %collective-permute-start.13 = (f32[96,128]{1,0:T(8,128)S(1)}, f32[96,128]{1,0:T(8,128)S(1)}, u32[]{:S(2)}, u32[]{:S(2)}) collective-permute-start(f32[96,128]{1,0:T(8,128)S(1)} %get-tuple-element.59), channel_id=1, source_target_pairs={{0,28},{4,24},{8,20},{12,16},{16,12},{20,8},{24,4},{28,0},{1,29},{... | collective-permute-start | bytes 147464 | tf_op jit(solution)/shard_map/ppermute | solution.py:325
  52.6 1.1 %shard_map.100 = (f32[96,128]{1,0:T(8,128)S(1)}, f32[96,128]{1,0:T(8,128)S(1)}, f32[96,128]{1,0:T(8,128)S(1)}, f32[96,128]{1,0:T(8,128)S(1)}) custom-call(bf16[2304,256]{1,0:T(8,128)(2,1)S(1)} %shard_map.98.spectrum_ref, bf16[512,2304]{1,0:T(8,128)(2,1)S(1)} %get-tuple-element.53.hot_ref, f32[96,384]{1,0:T(8,128)S(1)} %copy-done.3), custom_call_target="tpu_custom_call" | custom-call | flops 1 | bytes 1 | tf_op jit(solution)/shard_map/pallas_call | solution.py:309
  54.2 1.0 %collective-permute-start.15 = (f32[96,128]{1,0:T(8,128)S(1)}, f32[96,128]{1,0:T(8,128)S(1)}, u32[]{:S(2)}, u32[]{:S(2)}) collective-permute-start(f32[96,128]{1,0:T(8,128)S(1)} %get-tuple-element.62), channel_id=1, source_target_pairs={{0,8},{4,12},{8,0},{12,4},{16,24},{20,28},{24,16},{28,20},{1,9},{5... | collective-permute-start | bytes 147464 | tf_op jit(solution)/shard_map/ppermute | solution.py:325
  55.2 1.5 %collective-permute-done.11.refs_1_ = f32[96,128]{1,0:T(8,128)S(1)} collective-permute-done((f32[96,128]{1,0:T(8,128)S(1)}, f32[96,128]{1,0:T(8,128)S(1)}, u32[]{:S(2)}, u32[]{:S(2)}) %collective-permute-start.11) | collective-permute-done | bytes 49184 | tf_op jit(solution)/shard_map/ppermute | solution.py:325
  58.0 1.3 %collective-permute-done.15.refs_5_ = f32[96,128]{1,0:T(8,128)S(1)} collective-permute-done((f32[96,128]{1,0:T(8,128)S(1)}, f32[96,128]{1,0:T(8,128)S(1)}, u32[]{:S(2)}, u32[]{:S(2)}) %collective-permute-start.15) | collective-permute-done | bytes 49184 | tf_op jit(solution)/shard_map/ppermute | solution.py:325
  59.3 2.5 %collective-permute-done.16.refs_6_ = f32[96,128]{1,0:T(8,128)S(1)} collective-permute-done((f32[96,128]{1,0:T(8,128)S(1)}, f32[96,128]{1,0:T(8,128)S(1)}, u32[]{:S(2)}, u32[]{:S(2)}) %collective-permute-start.16) | collective-permute-done | bytes 49184 | tf_op jit(solution)/shard_map/ppermute | solution.py:325
  (37 shorter events, 5.3 us)
Async XLA Ops:
  0.0 32.5 %copy-start = (f32[2304,128]{1,0:T(8,128)S(1)}, f32[2304,128]{1,0:T(8,128)}, u32[]{:S(2)}) copy-start(f32[2304,128]{1,0:T(8,128)} %constant.20.clone.refs_4_) | copy-start | bytes 3538948
  0.0 32.5 %copy-start.4 = (f32[96,144]{1,0:T(8,128)S(1)}, f32[96,144]{1,0:T(8,128)}, u32[]{:S(2)}) copy-start(f32[96,144]{1,0:T(8,128)} %constant.17.clone.refs_3_) | copy-start | bytes 165892
  0.0 32.5 %copy-start.5 = (f32[96,144]{1,0:T(8,128)S(1)}, f32[96,144]{1,0:T(8,128)}, u32[]{:S(2)}) copy-start(f32[96,144]{1,0:T(8,128)} %constant.16.clone.refs_2_) | copy-start | bytes 165892
  0.0 32.5 %copy-start.1 = (f32[256,256]{1,0:T(8,128)S(1)}, f32[256,256]{1,0:T(8,128)}, u32[]{:S(2)}) copy-start(f32[256,256]{1,0:T(8,128)} %constant.15.clone.refs_1_) | copy-start | bytes 786436
  0.0 32.5 %copy-start.2 = (f32[256,256]{1,0:T(8,128)S(1)}, f32[256,256]{1,0:T(8,128)}, u32[]{:S(2)}) copy-start(f32[256,256]{1,0:T(8,128)} %constant.14.clone.refs_0_) | copy-start | bytes 786436
  2.0 10.8 %collective-permute-start = (f32[104,128]{1,0:T(8,128)}, f32[104,128]{1,0:T(8,128)S(1)}, u32[]{:S(2)}, u32[]{:S(2)}) collective-permute-start(f32[104,128]{1,0:T(8,128)} %get-tuple-element.35), channel_id=1, source_target_pairs={{0,16},{4,20},{8,24},{12,28},{16,0},{20,4},{24,8},{28,12},{1,17},{... | collective-permute-start | bytes 159752 | tf_op jit(solution)/shard_map/ppermute | solution.py:325
  6.1 8.7 %collective-permute-start.1 = (f32[104,128]{1,0:T(8,128)}, f32[104,128]{1,0:T(8,128)S(1)}, u32[]{:S(2)}, u32[]{:S(2)}) collective-permute-start(f32[104,128]{1,0:T(8,128)} %get-tuple-element.36), channel_id=1, source_target_pairs={{0,20},{4,16},{8,28},{12,24},{16,4},{20,0},{24,12},{28,8},{1,21},{... | collective-permute-start | bytes 159752 | tf_op jit(solution)/shard_map/ppermute | solution.py:325
  7.4 9.0 %collective-permute-start.2 = (f32[104,128]{1,0:T(8,128)}, f32[104,128]{1,0:T(8,128)S(1)}, u32[]{:S(2)}, u32[]{:S(2)}) collective-permute-start(f32[104,128]{1,0:T(8,128)} %get-tuple-element.37), channel_id=1, source_target_pairs={{0,24},{4,28},{8,16},{12,20},{16,8},{20,12},{24,0},{28,4},{1,25},{... | collective-permute-start | bytes 159752 | tf_op jit(solution)/shard_map/ppermute | solution.py:325
  11.0 7.5 %collective-permute-start.3 = (f32[104,128]{1,0:T(8,128)}, f32[104,128]{1,0:T(8,128)S(1)}, u32[]{:S(2)}, u32[]{:S(2)}) collective-permute-start(f32[104,128]{1,0:T(8,128)} %get-tuple-element.38), channel_id=1, source_target_pairs={{0,28},{4,24},{8,20},{12,16},{16,12},{20,8},{24,4},{28,0},{1,29},{... | collective-permute-start | bytes 159752 | tf_op jit(solution)/shard_map/ppermute | solution.py:325
  11.0 1.0 %copy-start.6 = (f32[224,288]{1,0:T(8,128)S(1)}, f32[224,288]{1,0:T(8,128)}, u32[]{:S(2)}) copy-start(f32[224,288]{1,0:T(8,128)} %constant.18.clone.tables_ref) | copy-start | bytes 774148
  12.8 5.6 %collective-permute-start.4 = (f32[104,128]{1,0:T(8,128)}, f32[104,128]{1,0:T(8,128)S(1)}, u32[]{:S(2)}, u32[]{:S(2)}) collective-permute-start(f32[104,128]{1,0:T(8,128)} %get-tuple-element.45), channel_id=1, source_target_pairs={{0,4},{4,0},{8,12},{12,8},{16,20},{20,16},{24,28},{28,24},{1,5},{5... | collective-permute-start | bytes 159752 | tf_op jit(solution)/shard_map/ppermute | solution.py:325
  14.5 4.3 %collective-permute-start.5 = (f32[104,128]{1,0:T(8,128)}, f32[104,128]{1,0:T(8,128)S(1)}, u32[]{:S(2)}, u32[]{:S(2)}) collective-permute-start(f32[104,128]{1,0:T(8,128)} %get-tuple-element.47), channel_id=1, source_target_pairs={{0,8},{4,12},{8,0},{12,4},{16,24},{20,28},{24,16},{28,20},{1,9},{5... | collective-permute-start | bytes 159752 | tf_op jit(solution)/shard_map/ppermute | solution.py:325
  14.8 5.2 %collective-permute-start.6 = (f32[104,128]{1,0:T(8,128)}, f32[104,128]{1,0:T(8,128)S(1)}, u32[]{:S(2)}, u32[]{:S(2)}) collective-permute-start(f32[104,128]{1,0:T(8,128)} %get-tuple-element.49), channel_id=1, source_target_pairs={{0,12},{4,8},{8,4},{12,0},{16,28},{20,24},{24,20},{28,16},{1,13},{... | collective-permute-start | bytes 159752 | tf_op jit(solution)/shard_map/ppermute | solution.py:325
  20.1 8.3 %collective-permute-start.7 = (f32[768,128]{1,0:T(8,128)S(1)}, f32[768,128]{1,0:T(8,128)S(1)}, u32[]{:S(2)}, u32[]{:S(2)}) collective-permute-start(f32[768,128]{1,0:T(8,128)S(1)} %get-tuple-element.50.blocks_ref), channel_id=1, source_target_pairs={{0,2},{1,3},{2,0},{3,1},{4,6},{5,7},{6,4},{7,5},{8,10},{9,11},{10,... | collective-permute-start | bytes 1179656 | tf_op jit(solution)/shard_map/ppermute | solution.py:340
  25.7 6.8 %collective-permute-start.9 = (f32[1152,128]{1,0:T(8,128)S(1)}, f32[1152,128]{1,0:T(8,128)S(1)}, u32[]{:S(2)}, u32[]{:S(2)}) collective-permute-start(f32[1152,128]{1,0:T(8,128)S(1)} %shard_map.94.phi_ref), channel_id=1, source_target_pairs={{0,1},{1,0},{2,3},{3,2},{4,5},{5,4},{6,7},{7,6},{8,9},{9,8},{10,11... | collective-permute-start | bytes 1769480 | tf_op jit(solution)/shard_map/ppermute | solution.py:343
  32.4 3.8 %collective-permute-start.8 = (f32[1152,128]{1,0:T(8,128)S(1)}, f32[1152,128]{1,0:T(8,128)S(1)}, u32[]{:S(2)}, u32[]{:S(2)}) collective-permute-start(f32[1152,128]{1,0:T(8,128)S(1)} %shard_map.96.first_ref), channel_id=1, source_target_pairs={{0,1},{1,0},{2,3},{3,2},{4,5},{5,4},{6,7},{7,6},{8,9},{9,8},{10,11... | collective-permute-start | bytes 1769480 | tf_op jit(solution)/shard_map/ppermute | solution.py:343
  36.1 6.3 %copy-start.3 = (f32[96,384]{1,0:T(8,128)S(1)}, f32[96,384]{1,0:T(8,128)}, u32[]{:S(2)}) copy-start(f32[96,384]{1,0:T(8,128)} %constant.19.clone.stick_out_ref) | copy-start | bytes 442372
  43.6 9.0 %collective-permute-start.10 = (f32[96,128]{1,0:T(8,128)S(1)}, f32[96,128]{1,0:T(8,128)S(1)}, u32[]{:S(2)}, u32[]{:S(2)}) collective-permute-start(f32[96,128]{1,0:T(8,128)S(1)} %get-tuple-element.56), channel_id=1, source_target_pairs={{0,16},{4,20},{8,24},{12,28},{16,0},{20,4},{24,8},{28,12},{1,17},{... | collective-permute-start | bytes 147464 | tf_op jit(solution)/shard_map/ppermute | solution.py:325
  47.8 9.0 %collective-permute-start.11 = (f32[96,128]{1,0:T(8,128)S(1)}, f32[96,128]{1,0:T(8,128)S(1)}, u32[]{:S(2)}, u32[]{:S(2)}) collective-permute-start(f32[96,128]{1,0:T(8,128)S(1)} %get-tuple-element.57), channel_id=1, source_target_pairs={{0,20},{4,16},{8,28},{12,24},{16,4},{20,0},{24,12},{28,8},{1,21},{... | collective-permute-start | bytes 147464 | tf_op jit(solution)/shard_map/ppermute | solution.py:325
  47.8 9.5 %collective-permute-start.12 = (f32[96,128]{1,0:T(8,128)S(1)}, f32[96,128]{1,0:T(8,128)S(1)}, u32[]{:S(2)}, u32[]{:S(2)}) collective-permute-start(f32[96,128]{1,0:T(8,128)S(1)} %get-tuple-element.58), channel_id=1, source_target_pairs={{0,24},{4,28},{8,16},{12,20},{16,8},{20,12},{24,0},{28,4},{1,25},{... | collective-permute-start | bytes 147464 | tf_op jit(solution)/shard_map/ppermute | solution.py:325
  50.6 6.9 %collective-permute-start.13 = (f32[96,128]{1,0:T(8,128)S(1)}, f32[96,128]{1,0:T(8,128)S(1)}, u32[]{:S(2)}, u32[]{:S(2)}) collective-permute-start(f32[96,128]{1,0:T(8,128)S(1)} %get-tuple-element.59), channel_id=1, source_target_pairs={{0,28},{4,24},{8,20},{12,16},{16,12},{20,8},{24,4},{28,0},{1,29},{... | collective-permute-start | bytes 147464 | tf_op jit(solution)/shard_map/ppermute | solution.py:325
  53.7 4.3 %collective-permute-start.14 = (f32[96,128]{1,0:T(8,128)S(1)}, f32[96,128]{1,0:T(8,128)S(1)}, u32[]{:S(2)}, u32[]{:S(2)}) collective-permute-start(f32[96,128]{1,0:T(8,128)S(1)} %get-tuple-element.61), channel_id=1, source_target_pairs={{0,4},{4,0},{8,12},{12,8},{16,20},{20,16},{24,28},{28,24},{1,5},{5... | collective-permute-start | bytes 147464 | tf_op jit(solution)/shard_map/ppermute | solution.py:325
  54.2 5.0 %collective-permute-start.15 = (f32[96,128]{1,0:T(8,128)S(1)}, f32[96,128]{1,0:T(8,128)S(1)}, u32[]{:S(2)}, u32[]{:S(2)}) collective-permute-start(f32[96,128]{1,0:T(8,128)S(1)} %get-tuple-element.62), channel_id=1, source_target_pairs={{0,8},{4,12},{8,0},{12,4},{16,24},{20,28},{24,16},{28,20},{1,9},{5... | collective-permute-start | bytes 147464 | tf_op jit(solution)/shard_map/ppermute | solution.py:325
  56.8 5.0 %collective-permute-start.16 = (f32[96,128]{1,0:T(8,128)S(1)}, f32[96,128]{1,0:T(8,128)S(1)}, u32[]{:S(2)}, u32[]{:S(2)}) collective-permute-start(f32[96,128]{1,0:T(8,128)S(1)} %get-tuple-element.63), channel_id=1, source_target_pairs={{0,12},{4,8},{8,4},{12,0},{16,28},{20,24},{24,20},{28,16},{1,13},{... | collective-permute-start | bytes 147464 | tf_op jit(solution)/shard_map/ppermute | solution.py:325
  (1 other events, 0.8 us)

commit v13 on v11

--- a/solution.py
+++ b/solution.py
@@ -15,7 +15,8 @@
 MID = 64
 WINDOW = 5
 SEND_GRANT = 60
-PAIRS = 6
+PAIRS = 4
+WIDE = 8
 
 F32 = jnp.float32
 BF16 = jnp.bfloat16
@@ -108,20 +109,19 @@
     return jnp.concatenate([a, b], 1)
 
 
-def halves(x):
-    return x[:, :LANES], x[:, LANES:]
-
-
-def left(table, x):
-    both = dot(table, stacked(x))
+def pieces(x):
+    return [x[:, k : k + LANES] for k in range(0, x.shape[1], LANES)]
+
+
+def left(table, slabs):
+    both = dot(table, stacked(jnp.concatenate(slabs, 1)))
     g = both.shape[0] // 2
-    return both[:g], both[g:]
-
-
-def left_complex(table, a, b):
-    cos, sin = left(table, beside(a, b))
+    return pieces(both[:g]), pieces(both[g:])
+
+
+def left_complex(table, slabs):
     sign = jnp.where(lane_halves((1, LANES)), -1.0, 1.0)
-    return [p + turned(q) * sign for p, q in zip(halves(cos), halves(sin))]
+    return [cos + turned(sin) * sign for cos, sin in zip(*left(table, slabs))]
 
 
 def right(x, table):
@@ -201,15 +201,19 @@
     for first in (0, half):
         both = dot(one_hot(index, (columns - first * g).astype(jnp.int16)), sticks)
         placed = both[:, :LANES] + both[:, LANES:]
-        for k in range(0, half, 2):
-            slabs = left_complex(backward, placed[k * g : (k + 1) * g], placed[(k + 1) * g : (k + 2) * g])
+        for k in range(0, half, WIDE):
+            slabs = left_complex(backward, [placed[j * g : (j + 1) * g] for j in range(k, k + WIDE)])
             store(work_a, first + k, slabs)
 
-    for y in range(half):
-        x = beside(strided(work_a, y, g), strided(work_a, y + half, g))
-        (cos, cos_up), (sin, sin_up) = map(halves, left(backward, x))
-        low = lane_halves(cos.shape)
-        store(phi_ref, y, [jnp.where(low, cos - turned(sin), turned(cos_up) - sin_up)])
+    low = lane_halves((g, LANES))
+    for first in range(0, half, WIDE // 2):
+        lower = [strided(work_a, y, g) for y in range(first, first + WIDE // 2)]
+        upper = [strided(work_a, y + half, g) for y in range(first, first + WIDE // 2)]
+        cos, sin = left(backward, lower + upper)
+        for k in range(WIDE // 2):
+            j = k + WIDE // 2
+            field = jnp.where(low, cos[k] - turned(sin[k]), turned(cos[j]) - sin[j])
+            store(phi_ref, first + k, [field])
 
 
 def pick_kernel(g, columns_ref, hot_ref):
@@ -230,22 +234,24 @@
         phi = phi_ref[rows, :]
         lower, upper = regrouped(phi * first_ref[rows, :], phi * second_ref[rows, :])
         spectrum = right(jnp.concatenate([lower, upper], 0), forward)
-        for k in range(PAIRS):
-            a, b = left_complex(left_forward, *(spectrum[j * g : (j + 1) * g] for j in (k, k + PAIRS)))
-            store(work_a, start + k, [a])
-            store(work_a, start + k + half, [b])
-
-    for kx in range(0, g, 2):
-        slabs = left_complex(left_forward, strided(work_a, kx, g), strided(work_a, kx + 1, g))
+        for k in range(0, PAIRS, WIDE // 2):
+            chosen = list(range(k, k + WIDE // 2)) + list(range(k + PAIRS, k + PAIRS + WIDE // 2))
+            slabs = left_complex(left_forward, [spectrum[j * g : (j + 1) * g] for j in chosen])
+            store(work_a, start + k, slabs[: WIDE // 2])
+            store(work_a, start + k + half, slabs[WIDE // 2 :])
+
+    for kx in range(0, g, WIDE):
+        slabs = left_complex(left_forward, [strided(work_a, kx + j, g) for j in range(WIDE)])
         slabs = [slab * coulomb_ref[slab_rows(kx + j, g), :] for j, slab in enumerate(slabs)]
-        store(work_b, kx, left_complex(left_backward, *slabs))
+        store(work_b, kx, left_complex(left_backward, slabs))
 
     for start in range(0, half, PAIRS):
         lower, upper = [], []
-        for z in range(start, start + PAIRS):
-            a, b = left_complex(left_backward, strided(work_b, z, g), strided(work_b, z + half, g))
-            lower.append(a)
-            upper.append(b)
+        for y in range(start, start + PAIRS, WIDE // 2):
+            chosen = list(range(y, y + WIDE // 2))
+            slabs = left_complex(left_backward, [strided(work_b, j, g) for j in chosen + [j + half for j in chosen]])
+            lower += slabs[: WIDE // 2]
+            upper += slabs[WIDE // 2 :]
         out = right(jnp.concatenate(lower + upper, 0), last_backward)
         emit(start, *regrouped(out[: PAIRS * g], out[PAIRS * g :]))
 
@@ -280,20 +286,19 @@
         rows = slab_rows(start, g, PAIRS)
         total = before_ref[rows, :] + weights[0] * (first * first_ref[rows, :])
         total = total + weights[1] * (second * second_ref[rows, :])
-        for k in range(0, PAIRS, 2):
-            cos, sin = left(forward, beside(total[k * g : (k + 1) * g], total[(k + 1) * g : (k + 2) * g]))
-            for j, (real, imag) in enumerate(zip(halves(cos), halves(sin))):
-                lower, upper = regrouped(real, imag)
-                store(work_a, start + k + j, [lower])
-                store(work_a, start + k + j + half, [upper])
+        cos, sin = left(forward, [total[k * g : (k + 1) * g] for k in range(PAIRS)])
+        for k, (real, imag) in enumerate(zip(cos, sin)):
+            lower, upper = regrouped(real, imag)
+            store(work_a, start + k, [lower])
+            store(work_a, start + k + half, [upper])
 
     potentials(g, phi_ref, first_ref, second_ref, tables, work_a, work_b, emit)
 
     step = g // 3
     for first in range(0, g, step):
         slabs = []
-        for kx in range(first, first + step, 2):
-            slabs += left_complex(forward, strided(work_a, kx, g), strided(work_a, kx + 1, g))
+        for kx in range(first, first + step, WIDE):
+            slabs += left_complex(forward, [strided(work_a, kx + j, g) for j in range(WIDE)])
         spectrum = beside(*split(jnp.concatenate(slabs, 0)))
         both = dot(hot_ref[:, first * g : (first + step) * g], spectrum)
         both = both[:, :LANES] + both[:, LANES:]
@@ -301,10 +306,8 @@
 
     stick_out = stick_out_ref[...].astype(BF16)
     for k in range(0, len(out_refs), 2):
-        high, low = split(picked_ref[k * LANES : (k + 2) * LANES, :])
-        lined = jnp.concatenate([high, low, high], 1)
-        out = lax.dot_general(stick_out, lined, (((1,), (1,)), ((), ())), preferred_element_type=F32)
-        out_refs[k][...], out_refs[k + 1][...] = halves(out)
+        lined = beside(*[picked_ref[j * LANES : (j + 1) * LANES, :].T for j in (k, k + 1)])
+        out_refs[k][...], out_refs[k + 1][...] = pieces(dot(stick_out, stacked(lined)))
 
 
 def call(kernel, out_shapes, scratch, flops, *operands, space=pltpu.VMEM, out_space=pltpu.VMEM, grant=40):
@@ -376,7 +379,10 @@
     )
     half = owners // 2
     distant, close = list(range(half, owners)), list(range(1, half))
-    received = exchanged(sent, distant + close, {d: (half, staged, *first_tables) for d in close})
+    mixed = [distant[0]] + [d for pair in zip(close, distant[1:]) for d in pair]
+    before = {mixed[k]: (mixed[k - 3 - k % 2],) for k in range(WINDOW, len(mixed))}
+    last = mixed[WINDOW]
+    received = exchanged(sent, mixed, {**before, last: (*before[last], staged, *first_tables)})
     received[0] = staged
     order = [0] + distant + close
     relay, columns = call(
@@ -425,8 +431,6 @@
         *pot_tables,
     )
     result = [result[order.index(d)] for d in range(owners)]
-    mixed = [distant[0]] + [d for pair in zip(close, distant[1:]) for d in pair]
-    before = {mixed[k]: (mixed[k - 3 - k % 2],) for k in range(WINDOW, len(mixed))}
     result = exchanged(result, mixed, before)
     return call(
         functools.partial(place_kernel, order),

time: 61.9 us -> 63.8 us (1.031)
  Pallas kernels: 23.5 us -> 26.7 us
  starting transfers between devices: 25.3 us -> 23.4 us
    pallas_call x9, Pallas kernels: 23.5 us -> 26.7 us  [call(): pl.pallas_call(kernel, out_shape=out_shapes, in_specs=[pl.BlockSpec(memor...]
    ppermute x14, starting transfers between devices: 23.6 us -> 21.7 us  [exchanged(): moved[d] = lax.ppermute(block, 'stick', [(i, i ^ d) for i in range(owners)])]
  transfers between devices with their start and end apart: 17 -> 17, of which waited for: 7 -> 6; matrix products, arithmetic and copies ran while one was open for 0% -> 0% of each run, Pallas kernels for 21% -> 22%
where the time goes in v13:
time: 63.8 us; the launch traced here: 63.6 us
  Pallas kernels  26.7 us (42%)
  starting transfers between devices  23.4 us (37%)
  waiting for transfers between devices  11.5 us (18%)
  local copies, waits for them, and re-layouts  1.81 us (3%)
    pallas_call x9, Pallas kernels, call(): pl.pallas_call(kernel, out_shape=out_shapes, in_specs=[pl.BlockSpec(memor...  26.7 us
    ppermute x14, starting transfers between devices, exchanged(): moved[d] = lax.ppermute(block, 'stick', [(i, i ^ d) for i in range(owners)])  21.7 us
    ppermute x14, waiting for transfers between devices, exchanged(): moved[d] = lax.ppermute(block, 'stick', [(i, i ^ d) for i in range(owners)])  10 us
    unnamed x16, local copies, waits for them, and re-layouts  1.81 us
    ppermute x1, starting transfers between devices, shifted(): lax.ppermute(x, 'band', [(i, (i - distance) % groups) for i in range(grou...  1.56 us
    ppermute x1, waiting for transfers between devices, shifted(): lax.ppermute(x, 'band', [(i, (i - distance) % groups) for i in range(grou...  1.47 us
  transfers between devices with their start and end apart: 17, of which 6 were waited for; matrix products, arithmetic and copies ran while one was open for 0% of the time, Pallas kernels for 22%

profile of v13, /device:TPU:0, one launch (start us, length us, event | category | flops | bytes accessed | tf_op | source)
XLA Modules:
  0.0 63.6 jit_solution(657874466414572380)
XLA Ops:
  0.0 1.9 %shard_map.91 = (f32[104,128]{1,0:T(8,128)}, f32[104,128]{1,0:T(8,128)}, f32[104,128]{1,0:T(8,128)}, f32[104,128]{1,0:T(8,128)}, f32[104,128]{1,0:T(8,128)}, /*i...) custom-call(f32[8,96,128]{2,1,0:T(8,128)} %sticks_ref.1, s32[1,128]{1,0:T(1,128)} %bitcast.1), custom_call_target="tpu_custom_call" | custom-call | flops 1 | bytes 1 | tf_op jit(solution)/shard_map/pallas_call | solution.py:315
  2.0 3.1 %collective-permute-start.3 = (f32[104,128]{1,0:T(8,128)}, f32[104,128]{1,0:T(8,128)S(1)}, u32[]{:S(2)}, u32[]{:S(2)}) collective-permute-start(f32[104,128]{1,0:T(8,128)} %get-tuple-element.40), channel_id=1, source_target_pairs={{0,8},{4,12},{8,0},{12,4},{16,24},{20,28},{24,16},{28,20},{1,9},{5... | collective-permute-start | bytes 159752 | tf_op jit(solution)/shard_map/ppermute | solution.py:336
  5.1 1.5 %collective-permute-start.5 = (f32[104,128]{1,0:T(8,128)}, f32[104,128]{1,0:T(8,128)S(1)}, u32[]{:S(2)}, u32[]{:S(2)}) collective-permute-start(f32[104,128]{1,0:T(8,128)} %get-tuple-element.42), channel_id=1, source_target_pairs={{0,4},{4,0},{8,12},{12,8},{16,20},{20,16},{24,28},{28,24},{1,5},{5... | collective-permute-start | bytes 159752 | tf_op jit(solution)/shard_map/ppermute | solution.py:336
  6.6 2.6 %collective-permute-start = (f32[104,128]{1,0:T(8,128)}, f32[104,128]{1,0:T(8,128)S(1)}, u32[]{:S(2)}, u32[]{:S(2)}) collective-permute-start(f32[104,128]{1,0:T(8,128)} %get-tuple-element.36), channel_id=1, source_target_pairs={{0,16},{4,20},{8,24},{12,28},{16,0},{20,4},{24,8},{28,12},{1,17},{... | collective-permute-start | bytes 159752 | tf_op jit(solution)/shard_map/ppermute | solution.py:336
  9.4 2.5 %collective-permute-start.2 = (f32[104,128]{1,0:T(8,128)}, f32[104,128]{1,0:T(8,128)S(1)}, u32[]{:S(2)}, u32[]{:S(2)}) collective-permute-start(f32[104,128]{1,0:T(8,128)} %get-tuple-element.38), channel_id=1, source_target_pairs={{0,24},{4,28},{8,16},{12,20},{16,8},{20,12},{24,0},{28,4},{1,25},{... | collective-permute-start | bytes 159752 | tf_op jit(solution)/shard_map/ppermute | solution.py:336
  11.9 1.0 %copy-done.5 = f32[224,288]{1,0:T(8,128)S(1)} copy-done((f32[224,288]{1,0:T(8,128)S(1)}, f32[224,288]{1,0:T(8,128)}, u32[]{:S(2)}) %copy-start.5) | copy-done | bytes 258072
  12.9 0.8 %copy-done.7 = f32[104,128]{1,0:T(8,128)S(1)} copy-done((f32[104,128]{1,0:T(8,128)S(1)}, f32[104,128]{1,0:T(8,128)}, u32[]{:S(2)}) %copy-start.7) | copy-done | bytes 53272
  13.7 2.4 %collective-permute-start.4 = (f32[104,128]{1,0:T(8,128)}, f32[104,128]{1,0:T(8,128)S(1)}, u32[]{:S(2)}, u32[]{:S(2)}) collective-permute-start(f32[104,128]{1,0:T(8,128)} %get-tuple-element.41), channel_id=1, source_target_pairs={{0,28},{4,24},{8,20},{12,16},{16,12},{20,8},{24,4},{28,0},{1,29},{... | collective-permute-start | bytes 159752 | tf_op jit(solution)/shard_map/ppermute | solution.py:336
  16.1 4.7 %collective-permute-done.4.refs_4_ = f32[104,128]{1,0:T(8,128)S(1)} collective-permute-done((f32[104,128]{1,0:T(8,128)}, f32[104,128]{1,0:T(8,128)S(1)}, u32[]{:S(2)}, u32[]{:S(2)}) %collective-permute-start.4) | collective-permute-done | bytes 53280 | tf_op jit(solution)/shard_map/ppermute | solution.py:336
  21.5 1.6 %collective-permute-start.7 = (f32[768,128]{1,0:T(8,128)S(1)}, f32[768,128]{1,0:T(8,128)S(1)}, u32[]{:S(2)}, u32[]{:S(2)}) collective-permute-start(f32[768,128]{1,0:T(8,128)S(1)} %get-tuple-element.47.blocks_ref), channel_id=1, source_target_pairs={{0,2},{1,3},{2,0},{3,1},{4,6},{5,7},{6,4},{7,5},{8,10},{9,11},{10,... | collective-permute-start | bytes 1179656 | tf_op jit(solution)/shard_map/ppermute | solution.py:352
  23.0 4.1 %shard_map.94.phi_ref = f32[1152,128]{1,0:T(8,128)S(1)} custom-call(f32[768,128]{1,0:T(8,128)S(1)} %get-tuple-element.47.blocks_ref, f32[8,1024]{1,0:T(8,128)S(1)} %get-tuple-element.48.columns_ref, bf16[128,288]{1,0:T(8,128)(2,1)S(1)} %get-tuple-element.44.stick_in_ref, bf16[96,144]{1,0:T(8,128)(2,1)S(1)} %get-tuple-element.45.left_ref), custom_call_target="tpu_custom_call" | custom-call | flops 1 | bytes 1 | tf_op jit(solution)/shard_map/pallas_call | solution.py:315
  27.2 1.2 %shard_map.95.hot_ref = bf16[1024,2304]{1,0:T(8,128)(2,1)S(1)} custom-call(f32[8,1024]{1,0:T(8,128)S(1)} %get-tuple-element.48.columns_ref), custom_call_target="tpu_custom_call" | custom-call | flops 1 | bytes 1 | tf_op jit(solution)/shard_map/pallas_call | solution.py:315
  28.4 1.5 %collective-permute-done.7.blocks_ref = f32[768,128]{1,0:T(8,128)S(1)} collective-permute-done((f32[768,128]{1,0:T(8,128)S(1)}, f32[768,128]{1,0:T(8,128)S(1)}, u32[]{:S(2)}, u32[]{:S(2)}) %collective-permute-start.7) | collective-permute-done | bytes 393248 | tf_op jit(solution)/shard_map/ppermute | solution.py:352
  29.9 4.1 %shard_map.96.first_ref = f32[1152,128]{1,0:T(8,128)S(1)} custom-call(f32[768,128]{1,0:T(8,128)S(1)} %collective-permute-done.7.blocks_ref, f32[8,1024]{1,0:T(8,128)S(1)} %get-tuple-element.48.columns_ref, bf16[128,288]{1,0:T(8,128)(2,1)S(1)} %get-tuple-element.44.stick_in_ref, bf16[96,144]{1,0:T(8,128)(2,1)S(1)} %get-tuple-element.45.left_ref), custom_call_target="tpu_custom_call" | custom-call | flops 1 | bytes 1 | tf_op jit(solution)/shard_map/pallas_call | solution.py:315
  34.1 4.6 %shard_map.97.before_ref = f32[1152,128]{1,0:T(8,128)S(1)} custom-call(f32[1152,128]{1,0:T(8,128)S(1)} %shard_map.94.phi_ref, f32[1152,128]{1,0:T(8,128)S(1)} %collective-permute-done.9.other_ref, f32[256,256]{1,0:T(8,128)S(1)} %copy-done.2, f32[256,256]{1,0:T(8,128)S(1)} %copy-done.1, f32[96,144]{1,0:T(8,128)S(1)} %copy-done.4, f32[96,144]{1,0:T(8,128)S(1)} %copy-done.3, ...), custom_call_target="tpu_custom_call" | custom-call | flops 1 | bytes 1 | tf_op jit(solution)/shard_map/pallas_call | solution.py:315
  38.6 10.0 %shard_map.98 = (f32[96,128]{1,0:T(8,128)S(1)}, f32[96,128]{1,0:T(8,128)S(1)}, f32[96,128]{1,0:T(8,128)S(1)}, f32[96,128]{1,0:T(8,128)S(1)}, f32[96,128]{1,0:T(8...) custom-call(f32[1152,128]{1,0:T(8,128)S(1)} %shard_map.94.phi_ref, ...), custom_call_target="tpu_custom_call" | custom-call | flops 1 | bytes 1 | tf_op jit(solution)/shard_map/pallas_call | solution.py:315
  48.7 1.1 %collective-permute-start.15 = (f32[96,128]{1,0:T(8,128)S(1)}, f32[96,128]{1,0:T(8,128)S(1)}, u32[]{:S(2)}, u32[]{:S(2)}) collective-permute-start(f32[96,128]{1,0:T(8,128)S(1)} %get-tuple-element.58), channel_id=1, source_target_pairs={{0,4},{4,0},{8,12},{12,8},{16,20},{20,16},{24,28},{28,24},{1,5},{5... | collective-permute-start | bytes 147464 | tf_op jit(solution)/shard_map/ppermute | solution.py:336
  49.8 2.4 %collective-permute-start.10 = (f32[96,128]{1,0:T(8,128)S(1)}, f32[96,128]{1,0:T(8,128)S(1)}, u32[]{:S(2)}, u32[]{:S(2)}) collective-permute-start(f32[96,128]{1,0:T(8,128)S(1)} %get-tuple-element.52), channel_id=1, source_target_pairs={{0,16},{4,20},{8,24},{12,28},{16,0},{20,4},{24,8},{28,12},{1,17},{... | collective-permute-start | bytes 147464 | tf_op jit(solution)/shard_map/ppermute | solution.py:336
  52.2 1.0 %collective-permute-start.11 = (f32[96,128]{1,0:T(8,128)S(1)}, f32[96,128]{1,0:T(8,128)S(1)}, u32[]{:S(2)}, u32[]{:S(2)}) collective-permute-start(f32[96,128]{1,0:T(8,128)S(1)} %get-tuple-element.53), channel_id=1, source_target_pairs={{0,20},{4,16},{8,28},{12,24},{16,4},{20,0},{24,12},{28,8},{1,21},{... | collective-permute-start | bytes 147464 | tf_op jit(solution)/shard_map/ppermute | solution.py:336
  53.2 2.2 %collective-permute-start.12 = (f32[96,128]{1,0:T(8,128)S(1)}, f32[96,128]{1,0:T(8,128)S(1)}, u32[]{:S(2)}, u32[]{:S(2)}) collective-permute-start(f32[96,128]{1,0:T(8,128)S(1)} %get-tuple-element.54), channel_id=1, source_target_pairs={{0,24},{4,28},{8,16},{12,20},{16,8},{20,12},{24,0},{28,4},{1,25},{... | collective-permute-start | bytes 147464 | tf_op jit(solution)/shard_map/ppermute | solution.py:336
  55.4 2.1 %collective-permute-start.14 = (f32[96,128]{1,0:T(8,128)S(1)}, f32[96,128]{1,0:T(8,128)S(1)}, u32[]{:S(2)}, u32[]{:S(2)}) collective-permute-start(f32[96,128]{1,0:T(8,128)S(1)} %get-tuple-element.57), channel_id=1, source_target_pairs={{0,28},{4,24},{8,20},{12,16},{16,12},{20,8},{24,4},{28,0},{1,29},{... | collective-permute-start | bytes 147464 | tf_op jit(solution)/shard_map/ppermute | solution.py:336
  58.1 2.7 %collective-permute-done.11.refs_2_ = f32[96,128]{1,0:T(8,128)S(1)} collective-permute-done((f32[96,128]{1,0:T(8,128)S(1)}, f32[96,128]{1,0:T(8,128)S(1)}, u32[]{:S(2)}, u32[]{:S(2)}) %collective-permute-start.11) | collective-permute-done | bytes 49184 | tf_op jit(solution)/shard_map/ppermute | solution.py:336
  60.8 1.5 %collective-permute-done.14.refs_4_ = f32[96,128]{1,0:T(8,128)S(1)} collective-permute-done((f32[96,128]{1,0:T(8,128)S(1)}, f32[96,128]{1,0:T(8,128)S(1)}, u32[]{:S(2)}, u32[]{:S(2)}) %collective-permute-start.14) | collective-permute-done | bytes 49184 | tf_op jit(solution)/shard_map/ppermute | solution.py:336
  62.8 0.8 %shard_map.99 = f32[8,96,128]{2,1,0:T(8,128)} custom-call(f32[96,128]{1,0:T(8,128)S(1)} %get-tuple-element.51.refs_0_, f32[96,128]{1,0:T(8,128)S(1)} %collective-permute-done.10.refs_1_, f32[96,128]{1,0:T(8,128)S(1)} %collective-permute-done.11.refs_2_, f32[96,128]{1,0:T(8,128)S(1)} %collective-permute-done.12.refs_3_, ...), custom_call_target="tpu_custom_call" | custom-call | flops 1 | bytes 1 | tf_op jit(solution)/shard_map/pallas_call | solution.py:315
  (35 shorter events, 2.3 us)
Async XLA Ops:
  0.0 34.0 %copy-start = (f32[2304,128]{1,0:T(8,128)S(1)}, f32[2304,128]{1,0:T(8,128)}, u32[]{:S(2)}) copy-start(f32[2304,128]{1,0:T(8,128)} %constant.20.clone.refs_4_) | copy-start | bytes 3538948
  0.0 34.0 %copy-start.3 = (f32[96,144]{1,0:T(8,128)S(1)}, f32[96,144]{1,0:T(8,128)}, u32[]{:S(2)}) copy-start(f32[96,144]{1,0:T(8,128)} %constant.17.clone.refs_3_) | copy-start | bytes 165892
  0.0 34.0 %copy-start.4 = (f32[96,144]{1,0:T(8,128)S(1)}, f32[96,144]{1,0:T(8,128)}, u32[]{:S(2)}) copy-start(f32[96,144]{1,0:T(8,128)} %constant.16.clone.refs_2_) | copy-start | bytes 165892
  0.0 34.0 %copy-start.1 = (f32[256,256]{1,0:T(8,128)S(1)}, f32[256,256]{1,0:T(8,128)}, u32[]{:S(2)}) copy-start(f32[256,256]{1,0:T(8,128)} %constant.15.clone.refs_1_) | copy-start | bytes 786436
  0.0 34.0 %copy-start.2 = (f32[256,256]{1,0:T(8,128)S(1)}, f32[256,256]{1,0:T(8,128)}, u32[]{:S(2)}) copy-start(f32[256,256]{1,0:T(8,128)} %constant.14.clone.refs_0_) | copy-start | bytes 786436
  2.0 11.8 %collective-permute-start.3 = (f32[104,128]{1,0:T(8,128)}, f32[104,128]{1,0:T(8,128)S(1)}, u32[]{:S(2)}, u32[]{:S(2)}) collective-permute-start(f32[104,128]{1,0:T(8,128)} %get-tuple-element.40), channel_id=1, source_target_pairs={{0,8},{4,12},{8,0},{12,4},{16,24},{20,28},{24,16},{28,20},{1,9},{5... | collective-permute-start | bytes 159752 | tf_op jit(solution)/shard_map/ppermute | solution.py:336
  5.1 11.1 %collective-permute-start.5 = (f32[104,128]{1,0:T(8,128)}, f32[104,128]{1,0:T(8,128)S(1)}, u32[]{:S(2)}, u32[]{:S(2)}) collective-permute-start(f32[104,128]{1,0:T(8,128)} %get-tuple-element.42), channel_id=1, source_target_pairs={{0,4},{4,0},{8,12},{12,8},{16,20},{20,16},{24,28},{28,24},{1,5},{5... | collective-permute-start | bytes 159752 | tf_op jit(solution)/shard_map/ppermute | solution.py:336
  6.6 9.5 %collective-permute-start = (f32[104,128]{1,0:T(8,128)}, f32[104,128]{1,0:T(8,128)S(1)}, u32[]{:S(2)}, u32[]{:S(2)}) collective-permute-start(f32[104,128]{1,0:T(8,128)} %get-tuple-element.36), channel_id=1, source_target_pairs={{0,16},{4,20},{8,24},{12,28},{16,0},{20,4},{24,8},{28,12},{1,17},{... | collective-permute-start | bytes 159752 | tf_op jit(solution)/shard_map/ppermute | solution.py:336
  9.2 7.0 %collective-permute-start.1 = (f32[104,128]{1,0:T(8,128)}, f32[104,128]{1,0:T(8,128)S(1)}, u32[]{:S(2)}, u32[]{:S(2)}) collective-permute-start(f32[104,128]{1,0:T(8,128)} %get-tuple-element.37), channel_id=1, source_target_pairs={{0,20},{4,16},{8,28},{12,24},{16,4},{20,0},{24,12},{28,8},{1,21},{... | collective-permute-start | bytes 159752 | tf_op jit(solution)/shard_map/ppermute | solution.py:336
  9.4 6.7 %collective-permute-start.2 = (f32[104,128]{1,0:T(8,128)}, f32[104,128]{1,0:T(8,128)S(1)}, u32[]{:S(2)}, u32[]{:S(2)}) collective-permute-start(f32[104,128]{1,0:T(8,128)} %get-tuple-element.38), channel_id=1, source_target_pairs={{0,24},{4,28},{8,16},{12,20},{16,8},{20,12},{24,0},{28,4},{1,25},{... | collective-permute-start | bytes 159752 | tf_op jit(solution)/shard_map/ppermute | solution.py:336
  11.9 1.0 %copy-start.5 = (f32[224,288]{1,0:T(8,128)S(1)}, f32[224,288]{1,0:T(8,128)}, u32[]{:S(2)}) copy-start(f32[224,288]{1,0:T(8,128)} %constant.18.clone.tables_ref) | copy-start | bytes 774148
  13.7 7.1 %collective-permute-start.4 = (f32[104,128]{1,0:T(8,128)}, f32[104,128]{1,0:T(8,128)S(1)}, u32[]{:S(2)}, u32[]{:S(2)}) collective-permute-start(f32[104,128]{1,0:T(8,128)} %get-tuple-element.41), channel_id=1, source_target_pairs={{0,28},{4,24},{8,20},{12,16},{16,12},{20,8},{24,4},{28,0},{1,29},{... | collective-permute-start | bytes 159752 | tf_op jit(solution)/shard_map/ppermute | solution.py:336
  16.1 5.3 %collective-permute-start.6 = (f32[104,128]{1,0:T(8,128)}, f32[104,128]{1,0:T(8,128)S(1)}, u32[]{:S(2)}, u32[]{:S(2)}) collective-permute-start(f32[104,128]{1,0:T(8,128)} %get-tuple-element.46), channel_id=1, source_target_pairs={{0,12},{4,8},{8,4},{12,0},{16,28},{20,24},{24,20},{28,16},{1,13},{... | collective-permute-start | bytes 159752 | tf_op jit(solution)/shard_map/ppermute | solution.py:336
  21.5 8.4 %collective-permute-start.7 = (f32[768,128]{1,0:T(8,128)S(1)}, f32[768,128]{1,0:T(8,128)S(1)}, u32[]{:S(2)}, u32[]{:S(2)}) collective-permute-start(f32[768,128]{1,0:T(8,128)S(1)} %get-tuple-element.47.blocks_ref), channel_id=1, source_target_pairs={{0,2},{1,3},{2,0},{3,1},{4,6},{5,7},{6,4},{7,5},{8,10},{9,11},{10,... | collective-permute-start | bytes 1179656 | tf_op jit(solution)/shard_map/ppermute | solution.py:352
  27.1 11.6 %copy-start.6 = (f32[96,384]{1,0:T(8,128)S(1)}, f32[96,384]{1,0:T(8,128)}, u32[]{:S(2)}) copy-start(f32[96,384]{1,0:T(8,128)} %constant.19.clone.stick_out_ref) | copy-start | bytes 442372
  27.1 6.9 %collective-permute-start.9 = (f32[1152,128]{1,0:T(8,128)S(1)}, f32[1152,128]{1,0:T(8,128)S(1)}, u32[]{:S(2)}, u32[]{:S(2)}) collective-permute-start(f32[1152,128]{1,0:T(8,128)S(1)} %shard_map.94.phi_ref), channel_id=1, source_target_pairs={{0,1},{1,0},{2,3},{3,2},{4,5},{5,4},{6,7},{7,6},{8,9},{9,8},{10,11... | collective-permute-start | bytes 1769480 | tf_op jit(solution)/shard_map/ppermute | solution.py:355
  33.9 4.7 %collective-permute-start.8 = (f32[1152,128]{1,0:T(8,128)S(1)}, f32[1152,128]{1,0:T(8,128)S(1)}, u32[]{:S(2)}, u32[]{:S(2)}) collective-permute-start(f32[1152,128]{1,0:T(8,128)S(1)} %shard_map.96.first_ref), channel_id=1, source_target_pairs={{0,1},{1,0},{2,3},{3,2},{4,5},{5,4},{6,7},{7,6},{8,9},{9,8},{10,11... | collective-permute-start | bytes 1769480 | tf_op jit(solution)/shard_map/ppermute | solution.py:355
  48.7 6.7 %collective-permute-start.13 = (f32[96,128]{1,0:T(8,128)S(1)}, f32[96,128]{1,0:T(8,128)S(1)}, u32[]{:S(2)}, u32[]{:S(2)}) collective-permute-start(f32[96,128]{1,0:T(8,128)S(1)} %get-tuple-element.56), channel_id=1, source_target_pairs={{0,8},{4,12},{8,0},{12,4},{16,24},{20,28},{24,16},{28,20},{1,9},{5... | collective-permute-start | bytes 147464 | tf_op jit(solution)/shard_map/ppermute | solution.py:336
  48.7 8.7 %collective-permute-start.15 = (f32[96,128]{1,0:T(8,128)S(1)}, f32[96,128]{1,0:T(8,128)S(1)}, u32[]{:S(2)}, u32[]{:S(2)}) collective-permute-start(f32[96,128]{1,0:T(8,128)S(1)} %get-tuple-element.58), channel_id=1, source_target_pairs={{0,4},{4,0},{8,12},{12,8},{16,20},{20,16},{24,28},{28,24},{1,5},{5... | collective-permute-start | bytes 147464 | tf_op jit(solution)/shard_map/ppermute | solution.py:336
  49.8 8.3 %collective-permute-start.10 = (f32[96,128]{1,0:T(8,128)S(1)}, f32[96,128]{1,0:T(8,128)S(1)}, u32[]{:S(2)}, u32[]{:S(2)}) collective-permute-start(f32[96,128]{1,0:T(8,128)S(1)} %get-tuple-element.52), channel_id=1, source_target_pairs={{0,16},{4,20},{8,24},{12,28},{16,0},{20,4},{24,8},{28,12},{1,17},{... | collective-permute-start | bytes 147464 | tf_op jit(solution)/shard_map/ppermute | solution.py:336
  52.2 8.6 %collective-permute-start.11 = (f32[96,128]{1,0:T(8,128)S(1)}, f32[96,128]{1,0:T(8,128)S(1)}, u32[]{:S(2)}, u32[]{:S(2)}) collective-permute-start(f32[96,128]{1,0:T(8,128)S(1)} %get-tuple-element.53), channel_id=1, source_target_pairs={{0,20},{4,16},{8,28},{12,24},{16,4},{20,0},{24,12},{28,8},{1,21},{... | collective-permute-start | bytes 147464 | tf_op jit(solution)/shard_map/ppermute | solution.py:336
  53.2 7.6 %collective-permute-start.12 = (f32[96,128]{1,0:T(8,128)S(1)}, f32[96,128]{1,0:T(8,128)S(1)}, u32[]{:S(2)}, u32[]{:S(2)}) collective-permute-start(f32[96,128]{1,0:T(8,128)S(1)} %get-tuple-element.54), channel_id=1, source_target_pairs={{0,24},{4,28},{8,16},{12,20},{16,8},{20,12},{24,0},{28,4},{1,25},{... | collective-permute-start | bytes 147464 | tf_op jit(solution)/shard_map/ppermute | solution.py:336
  55.4 6.9 %collective-permute-start.14 = (f32[96,128]{1,0:T(8,128)S(1)}, f32[96,128]{1,0:T(8,128)S(1)}, u32[]{:S(2)}, u32[]{:S(2)}) collective-permute-start(f32[96,128]{1,0:T(8,128)S(1)} %get-tuple-element.57), channel_id=1, source_target_pairs={{0,28},{4,24},{8,20},{12,16},{16,12},{20,8},{24,4},{28,0},{1,29},{... | collective-permute-start | bytes 147464 | tf_op jit(solution)/shard_map/ppermute | solution.py:336
  57.5 5.3 %collective-permute-start.16 = (f32[96,128]{1,0:T(8,128)S(1)}, f32[96,128]{1,0:T(8,128)S(1)}, u32[]{:S(2)}, u32[]{:S(2)}) collective-permute-start(f32[96,128]{1,0:T(8,128)S(1)} %get-tuple-element.60), channel_id=1, source_target_pairs={{0,12},{4,8},{8,4},{12,0},{16,28},{20,24},{24,20},{28,16},{1,13},{... | collective-permute-start | bytes 147464 | tf_op jit(solution)/shard_map/ppermute | solution.py:336
  (1 other events, 0.8 us)

commit v14 on v11

--- a/solution.py
+++ b/solution.py
@@ -15,7 +15,7 @@
 MID = 64
 WINDOW = 5
 SEND_GRANT = 60
-PAIRS = 6
+PAIRS = 4
 
 F32 = jnp.float32
 BF16 = jnp.bfloat16
@@ -376,9 +376,12 @@
     )
     half = owners // 2
     distant, close = list(range(half, owners)), list(range(1, half))
-    received = exchanged(sent, distant + close, {d: (half, staged, *first_tables) for d in close})
+    mixed = [distant[0]] + [d for pair in zip(close, distant[1:]) for d in pair]
+    before = {mixed[k]: (half,) for k in range(WINDOW, len(mixed))}
+    last = mixed[WINDOW]
+    received = exchanged(sent, mixed, {**before, last: (*before[last], staged, *first_tables)})
     received[0] = staged
-    order = [0] + distant + close
+    order = [0] + mixed
     relay, columns = call(
         functools.partial(relay_kernel, g),
         [jax.ShapeDtypeStruct((owners * 2 * g, slots), F32), jax.ShapeDtypeStruct((8, owners * slots), F32)],
@@ -425,8 +428,6 @@
         *pot_tables,
     )
     result = [result[order.index(d)] for d in range(owners)]
-    mixed = [distant[0]] + [d for pair in zip(close, distant[1:]) for d in pair]
-    before = {mixed[k]: (mixed[k - 3 - k % 2],) for k in range(WINDOW, len(mixed))}
     result = exchanged(result, mixed, before)
     return call(
         functools.partial(place_kernel, order),

time: 61.9 us -> 62.2 us (level)
  starting transfers between devices: 25.3 us -> 24.3 us
  Pallas kernels: 23.5 us -> 24.3 us
    ppermute x14, starting transfers between devices: 23.6 us -> 22.6 us  [exchanged(): moved[d] = lax.ppermute(block, 'stick', [(i, i ^ d) for i in range(owners)])]
    pallas_call x9, Pallas kernels: 23.5 us -> 24.3 us  [call(): pl.pallas_call(kernel, out_shape=out_shapes, in_specs=[pl.BlockSpec(memor...]
  transfers between devices with their start and end apart: 17 -> 17, of which waited for: 7 -> 6; matrix products, arithmetic and copies ran while one was open for 0% -> 0% of each run, Pallas kernels for 21% -> 21%
where the time goes in v14:
time: 62.2 us; the launch traced here: 62 us
  Pallas kernels  24.3 us (39%)
  starting transfers between devices  24.3 us (39%)
  waiting for transfers between devices  11.3 us (18%)
  local copies, waits for them, and re-layouts  1.81 us (3%)
    pallas_call x9, Pallas kernels, call(): pl.pallas_call(kernel, out_shape=out_shapes, in_specs=[pl.BlockSpec(memor...  24.3 us
    ppermute x14, starting transfers between devices, exchanged(): moved[d] = lax.ppermute(block, 'stick', [(i, i ^ d) for i in range(owners)])  22.6 us
    ppermute x14, waiting for transfers between devices, exchanged(): moved[d] = lax.ppermute(block, 'stick', [(i, i ^ d) for i in range(owners)])  9.79 us
    unnamed x16, local copies, waits for them, and re-layouts  1.81 us
    ppermute x1, starting transfers between devices, shifted(): lax.ppermute(x, 'band', [(i, (i - distance) % groups) for i in range(grou...  1.56 us
    ppermute x1, waiting for transfers between devices, shifted(): lax.ppermute(x, 'band', [(i, (i - distance) % groups) for i in range(grou...  1.49 us
  transfers between devices with their start and end apart: 17, of which 6 were waited for; matrix products, arithmetic and copies ran while one was open for 0% of the time, Pallas kernels for 21%

profile of v14, /device:TPU:0, one launch (start us, length us, event | category | flops | bytes accessed | tf_op | source)
XLA Modules:
  0.0 62.0 jit_solution(16305936836800621177)
XLA Ops:
  0.0 1.9 %shard_map.91 = (f32[104,128]{1,0:T(8,128)}, f32[104,128]{1,0:T(8,128)}, f32[104,128]{1,0:T(8,128)}, f32[104,128]{1,0:T(8,128)}, f32[104,128]{1,0:T(8,128)}, /*i...) custom-call(f32[8,96,128]{2,1,0:T(8,128)} %sticks_ref.1, s32[1,128]{1,0:T(1,128)} %bitcast.1), custom_call_target="tpu_custom_call" | custom-call | flops 1 | bytes 1 | tf_op jit(solution)/shard_map/pallas_call | solution.py:312
  2.0 4.1 %collective-permute-start = (f32[104,128]{1,0:T(8,128)}, f32[104,128]{1,0:T(8,128)S(1)}, u32[]{:S(2)}, u32[]{:S(2)}) collective-permute-start(f32[104,128]{1,0:T(8,128)} %get-tuple-element.36), channel_id=1, source_target_pairs={{0,16},{4,20},{8,24},{12,28},{16,0},{20,4},{24,8},{28,12},{1,17},{... | collective-permute-start | bytes 159752 | tf_op jit(solution)/shard_map/ppermute | solution.py:333
  6.1 1.5 %collective-permute-start.1 = (f32[104,128]{1,0:T(8,128)}, f32[104,128]{1,0:T(8,128)S(1)}, u32[]{:S(2)}, u32[]{:S(2)}) collective-permute-start(f32[104,128]{1,0:T(8,128)} %get-tuple-element.37), channel_id=1, source_target_pairs={{0,4},{4,0},{8,12},{12,8},{16,20},{20,16},{24,28},{28,24},{1,5},{5... | collective-permute-start | bytes 159752 | tf_op jit(solution)/shard_map/ppermute | solution.py:333
  7.6 1.8 %collective-permute-start.3 = (f32[104,128]{1,0:T(8,128)}, f32[104,128]{1,0:T(8,128)S(1)}, u32[]{:S(2)}, u32[]{:S(2)}) collective-permute-start(f32[104,128]{1,0:T(8,128)} %get-tuple-element.39), channel_id=1, source_target_pairs={{0,8},{4,12},{8,0},{12,4},{16,24},{20,28},{24,16},{28,20},{1,9},{5... | collective-permute-start | bytes 159752 | tf_op jit(solution)/shard_map/ppermute | solution.py:333
  9.4 2.5 %collective-permute-start.4 = (f32[104,128]{1,0:T(8,128)}, f32[104,128]{1,0:T(8,128)S(1)}, u32[]{:S(2)}, u32[]{:S(2)}) collective-permute-start(f32[104,128]{1,0:T(8,128)} %get-tuple-element.40), channel_id=1, source_target_pairs={{0,24},{4,28},{8,16},{12,20},{16,8},{20,12},{24,0},{28,4},{1,25},{... | collective-permute-start | bytes 159752 | tf_op jit(solution)/shard_map/ppermute | solution.py:333
  11.9 1.0 %copy-done.5 = f32[224,288]{1,0:T(8,128)S(1)} copy-done((f32[224,288]{1,0:T(8,128)S(1)}, f32[224,288]{1,0:T(8,128)}, u32[]{:S(2)}) %copy-start.5) | copy-done | bytes 258072
  12.9 0.8 %copy-done.7 = f32[104,128]{1,0:T(8,128)S(1)} copy-done((f32[104,128]{1,0:T(8,128)S(1)}, f32[104,128]{1,0:T(8,128)}, u32[]{:S(2)}) %copy-start.7) | copy-done | bytes 53272
  13.7 2.4 %collective-permute-start.6 = (f32[104,128]{1,0:T(8,128)}, f32[104,128]{1,0:T(8,128)S(1)}, u32[]{:S(2)}, u32[]{:S(2)}) collective-permute-start(f32[104,128]{1,0:T(8,128)} %get-tuple-element.46), channel_id=1, source_target_pairs={{0,28},{4,24},{8,20},{12,16},{16,12},{20,8},{24,4},{28,0},{1,29},{... | collective-permute-start | bytes 159752 | tf_op jit(solution)/shard_map/ppermute | solution.py:333
  16.1 4.7 %collective-permute-done.6.refs_7_ = f32[104,128]{1,0:T(8,128)S(1)} collective-permute-done((f32[104,128]{1,0:T(8,128)}, f32[104,128]{1,0:T(8,128)S(1)}, u32[]{:S(2)}, u32[]{:S(2)}) %collective-permute-start.6) | collective-permute-done | bytes 53280 | tf_op jit(solution)/shard_map/ppermute | solution.py:333
  21.5 1.6 %collective-permute-start.7 = (f32[768,128]{1,0:T(8,128)S(1)}, f32[768,128]{1,0:T(8,128)S(1)}, u32[]{:S(2)}, u32[]{:S(2)}) collective-permute-start(f32[768,128]{1,0:T(8,128)S(1)} %get-tuple-element.47.blocks_ref), channel_id=1, source_target_pairs={{0,2},{1,3},{2,0},{3,1},{4,6},{5,7},{6,4},{7,5},{8,10},{9,11},{10,... | collective-permute-start | bytes 1179656 | tf_op jit(solution)/shard_map/ppermute | solution.py:349
  23.0 4.0 %shard_map.94.phi_ref = f32[1152,128]{1,0:T(8,128)S(1)} custom-call(f32[768,128]{1,0:T(8,128)S(1)} %get-tuple-element.47.blocks_ref, f32[8,1024]{1,0:T(8,128)S(1)} %get-tuple-element.48.columns_ref, bf16[128,288]{1,0:T(8,128)(2,1)S(1)} %get-tuple-element.42.stick_in_ref, bf16[96,144]{1,0:T(8,128)(2,1)S(1)} %get-tuple-element.43.left_ref), custom_call_target="tpu_custom_call" | custom-call | flops 1 | bytes 1 | tf_op jit(solution)/shard_map/pallas_call | solution.py:312
  27.1 1.2 %shard_map.95.hot_ref = bf16[1024,2304]{1,0:T(8,128)(2,1)S(1)} custom-call(f32[8,1024]{1,0:T(8,128)S(1)} %get-tuple-element.48.columns_ref), custom_call_target="tpu_custom_call" | custom-call | flops 1 | bytes 1 | tf_op jit(solution)/shard_map/pallas_call | solution.py:312
  28.3 1.5 %collective-permute-done.7.blocks_ref = f32[768,128]{1,0:T(8,128)S(1)} collective-permute-done((f32[768,128]{1,0:T(8,128)S(1)}, f32[768,128]{1,0:T(8,128)S(1)}, u32[]{:S(2)}, u32[]{:S(2)}) %collective-permute-start.7) | collective-permute-done | bytes 393248 | tf_op jit(solution)/shard_map/ppermute | solution.py:349
  29.8 4.0 %shard_map.96.first_ref = f32[1152,128]{1,0:T(8,128)S(1)} custom-call(f32[768,128]{1,0:T(8,128)S(1)} %collective-permute-done.7.blocks_ref, f32[8,1024]{1,0:T(8,128)S(1)} %get-tuple-element.48.columns_ref, bf16[128,288]{1,0:T(8,128)(2,1)S(1)} %get-tuple-element.42.stick_in_ref, bf16[96,144]{1,0:T(8,128)(2,1)S(1)} %get-tuple-element.43.left_ref), custom_call_target="tpu_custom_call" | custom-call | flops 1 | bytes 1 | tf_op jit(solution)/shard_map/pallas_call | solution.py:312
  34.0 3.6 %shard_map.97.before_ref = f32[1152,128]{1,0:T(8,128)S(1)} custom-call(f32[1152,128]{1,0:T(8,128)S(1)} %shard_map.94.phi_ref, f32[1152,128]{1,0:T(8,128)S(1)} %collective-permute-done.9.other_ref, f32[256,256]{1,0:T(8,128)S(1)} %copy-done.2, f32[256,256]{1,0:T(8,128)S(1)} %copy-done.1, f32[96,144]{1,0:T(8,128)S(1)} %copy-done.4, f32[96,144]{1,0:T(8,128)S(1)} %copy-done.3, ...), custom_call_target="tpu_custom_call" | custom-call | flops 1 | bytes 1 | tf_op jit(solution)/shard_map/pallas_call | solution.py:312
  37.6 8.8 %shard_map.98 = (f32[96,128]{1,0:T(8,128)S(1)}, f32[96,128]{1,0:T(8,128)S(1)}, f32[96,128]{1,0:T(8,128)S(1)}, f32[96,128]{1,0:T(8,128)S(1)}, f32[96,128]{1,0:T(8...) custom-call(f32[1152,128]{1,0:T(8,128)S(1)} %shard_map.94.phi_ref, ...), custom_call_target="tpu_custom_call" | custom-call | flops 1 | bytes 1 | tf_op jit(solution)/shard_map/pallas_call | solution.py:312
  46.4 1.1 %collective-permute-start.10 = (f32[96,128]{1,0:T(8,128)S(1)}, f32[96,128]{1,0:T(8,128)S(1)}, u32[]{:S(2)}, u32[]{:S(2)}) collective-permute-start(f32[96,128]{1,0:T(8,128)S(1)} %get-tuple-element.52), channel_id=1, source_target_pairs={{0,16},{4,20},{8,24},{12,28},{16,0},{20,4},{24,8},{28,12},{1,17},{... | collective-permute-start | bytes 147464 | tf_op jit(solution)/shard_map/ppermute | solution.py:333
  47.5 1.5 %collective-permute-start.11 = (f32[96,128]{1,0:T(8,128)S(1)}, f32[96,128]{1,0:T(8,128)S(1)}, u32[]{:S(2)}, u32[]{:S(2)}) collective-permute-start(f32[96,128]{1,0:T(8,128)S(1)} %get-tuple-element.53), channel_id=1, source_target_pairs={{0,4},{4,0},{8,12},{12,8},{16,20},{20,16},{24,28},{28,24},{1,5},{5... | collective-permute-start | bytes 147464 | tf_op jit(solution)/shard_map/ppermute | solution.py:333
  49.0 1.8 %collective-permute-start.12 = (f32[96,128]{1,0:T(8,128)S(1)}, f32[96,128]{1,0:T(8,128)S(1)}, u32[]{:S(2)}, u32[]{:S(2)}) collective-permute-start(f32[96,128]{1,0:T(8,128)S(1)} %get-tuple-element.54), channel_id=1, source_target_pairs={{0,20},{4,16},{8,28},{12,24},{16,4},{20,0},{24,12},{28,8},{1,21},{... | collective-permute-start | bytes 147464 | tf_op jit(solution)/shard_map/ppermute | solution.py:333
  50.8 2.5 %collective-permute-start.14 = (f32[96,128]{1,0:T(8,128)S(1)}, f32[96,128]{1,0:T(8,128)S(1)}, u32[]{:S(2)}, u32[]{:S(2)}) collective-permute-start(f32[96,128]{1,0:T(8,128)S(1)} %get-tuple-element.56), channel_id=1, source_target_pairs={{0,24},{4,28},{8,16},{12,20},{16,8},{20,12},{24,0},{28,4},{1,25},{... | collective-permute-start | bytes 147464 | tf_op jit(solution)/shard_map/ppermute | solution.py:333
  53.3 1.0 %collective-permute-start.15 = (f32[96,128]{1,0:T(8,128)S(1)}, f32[96,128]{1,0:T(8,128)S(1)}, u32[]{:S(2)}, u32[]{:S(2)}) collective-permute-start(f32[96,128]{1,0:T(8,128)S(1)} %get-tuple-element.58), channel_id=1, source_target_pairs={{0,12},{4,8},{8,4},{12,0},{16,28},{20,24},{24,20},{28,16},{1,13},{... | collective-permute-start | bytes 147464 | tf_op jit(solution)/shard_map/ppermute | solution.py:333
  54.3 2.4 %collective-permute-start.16 = (f32[96,128]{1,0:T(8,128)S(1)}, f32[96,128]{1,0:T(8,128)S(1)}, u32[]{:S(2)}, u32[]{:S(2)}) collective-permute-start(f32[96,128]{1,0:T(8,128)S(1)} %get-tuple-element.60), channel_id=1, source_target_pairs={{0,28},{4,24},{8,20},{12,16},{16,12},{20,8},{24,4},{28,0},{1,29},{... | collective-permute-start | bytes 147464 | tf_op jit(solution)/shard_map/ppermute | solution.py:333
  57.1 1.2 %collective-permute-done.15.refs_6_ = f32[96,128]{1,0:T(8,128)S(1)} collective-permute-done((f32[96,128]{1,0:T(8,128)S(1)}, f32[96,128]{1,0:T(8,128)S(1)}, u32[]{:S(2)}, u32[]{:S(2)}) %collective-permute-start.15) | collective-permute-done | bytes 49184 | tf_op jit(solution)/shard_map/ppermute | solution.py:333
  58.3 2.9 %collective-permute-done.16.refs_7_ = f32[96,128]{1,0:T(8,128)S(1)} collective-permute-done((f32[96,128]{1,0:T(8,128)S(1)}, f32[96,128]{1,0:T(8,128)S(1)}, u32[]{:S(2)}, u32[]{:S(2)}) %collective-permute-start.16) | collective-permute-done | bytes 49184 | tf_op jit(solution)/shard_map/ppermute | solution.py:333
  (35 shorter events, 2.1 us)
Async XLA Ops:
  0.0 33.9 %copy-start = (f32[2304,128]{1,0:T(8,128)S(1)}, f32[2304,128]{1,0:T(8,128)}, u32[]{:S(2)}) copy-start(f32[2304,128]{1,0:T(8,128)} %constant.20.clone.refs_4_) | copy-start | bytes 3538948
  0.0 33.9 %copy-start.3 = (f32[96,144]{1,0:T(8,128)S(1)}, f32[96,144]{1,0:T(8,128)}, u32[]{:S(2)}) copy-start(f32[96,144]{1,0:T(8,128)} %constant.17.clone.refs_3_) | copy-start | bytes 165892
  0.0 33.9 %copy-start.4 = (f32[96,144]{1,0:T(8,128)S(1)}, f32[96,144]{1,0:T(8,128)}, u32[]{:S(2)}) copy-start(f32[96,144]{1,0:T(8,128)} %constant.16.clone.refs_2_) | copy-start | bytes 165892
  0.0 33.9 %copy-start.1 = (f32[256,256]{1,0:T(8,128)S(1)}, f32[256,256]{1,0:T(8,128)}, u32[]{:S(2)}) copy-start(f32[256,256]{1,0:T(8,128)} %constant.15.clone.refs_1_) | copy-start | bytes 786436
  0.0 34.0 %copy-start.2 = (f32[256,256]{1,0:T(8,128)S(1)}, f32[256,256]{1,0:T(8,128)}, u32[]{:S(2)}) copy-start(f32[256,256]{1,0:T(8,128)} %constant.14.clone.refs_0_) | copy-start | bytes 786436
  2.0 11.8 %collective-permute-start = (f32[104,128]{1,0:T(8,128)}, f32[104,128]{1,0:T(8,128)S(1)}, u32[]{:S(2)}, u32[]{:S(2)}) collective-permute-start(f32[104,128]{1,0:T(8,128)} %get-tuple-element.36), channel_id=1, source_target_pairs={{0,16},{4,20},{8,24},{12,28},{16,0},{20,4},{24,8},{28,12},{1,17},{... | collective-permute-start | bytes 159752 | tf_op jit(solution)/shard_map/ppermute | solution.py:333
  6.1 10.0 %collective-permute-start.1 = (f32[104,128]{1,0:T(8,128)}, f32[104,128]{1,0:T(8,128)S(1)}, u32[]{:S(2)}, u32[]{:S(2)}) collective-permute-start(f32[104,128]{1,0:T(8,128)} %get-tuple-element.37), channel_id=1, source_target_pairs={{0,4},{4,0},{8,12},{12,8},{16,20},{20,16},{24,28},{28,24},{1,5},{5... | collective-permute-start | bytes 159752 | tf_op jit(solution)/shard_map/ppermute | solution.py:333
  7.6 8.5 %collective-permute-start.2 = (f32[104,128]{1,0:T(8,128)}, f32[104,128]{1,0:T(8,128)S(1)}, u32[]{:S(2)}, u32[]{:S(2)}) collective-permute-start(f32[104,128]{1,0:T(8,128)} %get-tuple-element.38), channel_id=1, source_target_pairs={{0,20},{4,16},{8,28},{12,24},{16,4},{20,0},{24,12},{28,8},{1,21},{... | collective-permute-start | bytes 159752 | tf_op jit(solution)/shard_map/ppermute | solution.py:333
  7.6 8.5 %collective-permute-start.3 = (f32[104,128]{1,0:T(8,128)}, f32[104,128]{1,0:T(8,128)S(1)}, u32[]{:S(2)}, u32[]{:S(2)}) collective-permute-start(f32[104,128]{1,0:T(8,128)} %get-tuple-element.39), channel_id=1, source_target_pairs={{0,8},{4,12},{8,0},{12,4},{16,24},{20,28},{24,16},{28,20},{1,9},{5... | collective-permute-start | bytes 159752 | tf_op jit(solution)/shard_map/ppermute | solution.py:333
  9.4 6.7 %collective-permute-start.4 = (f32[104,128]{1,0:T(8,128)}, f32[104,128]{1,0:T(8,128)S(1)}, u32[]{:S(2)}, u32[]{:S(2)}) collective-permute-start(f32[104,128]{1,0:T(8,128)} %get-tuple-element.40), channel_id=1, source_target_pairs={{0,24},{4,28},{8,16},{12,20},{16,8},{20,12},{24,0},{28,4},{1,25},{... | collective-permute-start | bytes 159752 | tf_op jit(solution)/shard_map/ppermute | solution.py:333
  11.9 1.0 %copy-start.5 = (f32[224,288]{1,0:T(8,128)S(1)}, f32[224,288]{1,0:T(8,128)}, u32[]{:S(2)}) copy-start(f32[224,288]{1,0:T(8,128)} %constant.18.clone.tables_ref) | copy-start | bytes 774148
  13.7 7.1 %collective-permute-start.6 = (f32[104,128]{1,0:T(8,128)}, f32[104,128]{1,0:T(8,128)S(1)}, u32[]{:S(2)}, u32[]{:S(2)}) collective-permute-start(f32[104,128]{1,0:T(8,128)} %get-tuple-element.46), channel_id=1, source_target_pairs={{0,28},{4,24},{8,20},{12,16},{16,12},{20,8},{24,4},{28,0},{1,29},{... | collective-permute-start | bytes 159752 | tf_op jit(solution)/shard_map/ppermute | solution.py:333
  16.1 5.3 %collective-permute-start.5 = (f32[104,128]{1,0:T(8,128)}, f32[104,128]{1,0:T(8,128)S(1)}, u32[]{:S(2)}, u32[]{:S(2)}) collective-permute-start(f32[104,128]{1,0:T(8,128)} %get-tuple-element.44), channel_id=1, source_target_pairs={{0,12},{4,8},{8,4},{12,0},{16,28},{20,24},{24,20},{28,16},{1,13},{... | collective-permute-start | bytes 159752 | tf_op jit(solution)/shard_map/ppermute | solution.py:333
  21.5 8.4 %collective-permute-start.7 = (f32[768,128]{1,0:T(8,128)S(1)}, f32[768,128]{1,0:T(8,128)S(1)}, u32[]{:S(2)}, u32[]{:S(2)}) collective-permute-start(f32[768,128]{1,0:T(8,128)S(1)} %get-tuple-element.47.blocks_ref), channel_id=1, source_target_pairs={{0,2},{1,3},{2,0},{3,1},{4,6},{5,7},{6,4},{7,5},{8,10},{9,11},{10,... | collective-permute-start | bytes 1179656 | tf_op jit(solution)/shard_map/ppermute | solution.py:349
  27.0 10.6 %copy-start.6 = (f32[96,384]{1,0:T(8,128)S(1)}, f32[96,384]{1,0:T(8,128)}, u32[]{:S(2)}) copy-start(f32[96,384]{1,0:T(8,128)} %constant.19.clone.stick_out_ref) | copy-start | bytes 442372
  27.0 6.9 %collective-permute-start.9 = (f32[1152,128]{1,0:T(8,128)S(1)}, f32[1152,128]{1,0:T(8,128)S(1)}, u32[]{:S(2)}, u32[]{:S(2)}) collective-permute-start(f32[1152,128]{1,0:T(8,128)S(1)} %shard_map.94.phi_ref), channel_id=1, source_target_pairs={{0,1},{1,0},{2,3},{3,2},{4,5},{5,4},{6,7},{7,6},{8,9},{9,8},{10,11... | collective-permute-start | bytes 1769480 | tf_op jit(solution)/shard_map/ppermute | solution.py:352
  33.8 3.7 %collective-permute-start.8 = (f32[1152,128]{1,0:T(8,128)S(1)}, f32[1152,128]{1,0:T(8,128)S(1)}, u32[]{:S(2)}, u32[]{:S(2)}) collective-permute-start(f32[1152,128]{1,0:T(8,128)S(1)} %shard_map.96.first_ref), channel_id=1, source_target_pairs={{0,1},{1,0},{2,3},{3,2},{4,5},{5,4},{6,7},{7,6},{8,9},{9,8},{10,11... | collective-permute-start | bytes 1769480 | tf_op jit(solution)/shard_map/ppermute | solution.py:352
  46.4 7.0 %collective-permute-start.10 = (f32[96,128]{1,0:T(8,128)S(1)}, f32[96,128]{1,0:T(8,128)S(1)}, u32[]{:S(2)}, u32[]{:S(2)}) collective-permute-start(f32[96,128]{1,0:T(8,128)S(1)} %get-tuple-element.52), channel_id=1, source_target_pairs={{0,16},{4,20},{8,24},{12,28},{16,0},{20,4},{24,8},{28,12},{1,17},{... | collective-permute-start | bytes 147464 | tf_op jit(solution)/shard_map/ppermute | solution.py:333
  47.5 6.8 %collective-permute-start.11 = (f32[96,128]{1,0:T(8,128)S(1)}, f32[96,128]{1,0:T(8,128)S(1)}, u32[]{:S(2)}, u32[]{:S(2)}) collective-permute-start(f32[96,128]{1,0:T(8,128)S(1)} %get-tuple-element.53), channel_id=1, source_target_pairs={{0,4},{4,0},{8,12},{12,8},{16,20},{20,16},{24,28},{28,24},{1,5},{5... | collective-permute-start | bytes 147464 | tf_op jit(solution)/shard_map/ppermute | solution.py:333
  49.0 7.7 %collective-permute-start.12 = (f32[96,128]{1,0:T(8,128)S(1)}, f32[96,128]{1,0:T(8,128)S(1)}, u32[]{:S(2)}, u32[]{:S(2)}) collective-permute-start(f32[96,128]{1,0:T(8,128)S(1)} %get-tuple-element.54), channel_id=1, source_target_pairs={{0,20},{4,16},{8,28},{12,24},{16,4},{20,0},{24,12},{28,8},{1,21},{... | collective-permute-start | bytes 147464 | tf_op jit(solution)/shard_map/ppermute | solution.py:333
  50.8 5.9 %collective-permute-start.13 = (f32[96,128]{1,0:T(8,128)S(1)}, f32[96,128]{1,0:T(8,128)S(1)}, u32[]{:S(2)}, u32[]{:S(2)}) collective-permute-start(f32[96,128]{1,0:T(8,128)S(1)} %get-tuple-element.55), channel_id=1, source_target_pairs={{0,8},{4,12},{8,0},{12,4},{16,24},{20,28},{24,16},{28,20},{1,9},{5... | collective-permute-start | bytes 147464 | tf_op jit(solution)/shard_map/ppermute | solution.py:333
  50.8 6.3 %collective-permute-start.14 = (f32[96,128]{1,0:T(8,128)S(1)}, f32[96,128]{1,0:T(8,128)S(1)}, u32[]{:S(2)}, u32[]{:S(2)}) collective-permute-start(f32[96,128]{1,0:T(8,128)S(1)} %get-tuple-element.56), channel_id=1, source_target_pairs={{0,24},{4,28},{8,16},{12,20},{16,8},{20,12},{24,0},{28,4},{1,25},{... | collective-permute-start | bytes 147464 | tf_op jit(solution)/shard_map/ppermute | solution.py:333
  53.3 5.0 %collective-permute-start.15 = (f32[96,128]{1,0:T(8,128)S(1)}, f32[96,128]{1,0:T(8,128)S(1)}, u32[]{:S(2)}, u32[]{:S(2)}) collective-permute-start(f32[96,128]{1,0:T(8,128)S(1)} %get-tuple-element.58), channel_id=1, source_target_pairs={{0,12},{4,8},{8,4},{12,0},{16,28},{20,24},{24,20},{28,16},{1,13},{... | collective-permute-start | bytes 147464 | tf_op jit(solution)/shard_map/ppermute | solution.py:333
  54.3 6.9 %collective-permute-start.16 = (f32[96,128]{1,0:T(8,128)S(1)}, f32[96,128]{1,0:T(8,128)S(1)}, u32[]{:S(2)}, u32[]{:S(2)}) collective-permute-start(f32[96,128]{1,0:T(8,128)S(1)} %get-tuple-element.60), channel_id=1, source_target_pairs={{0,28},{4,24},{8,20},{12,16},{16,12},{20,8},{24,4},{28,0},{1,29},{... | collective-permute-start | bytes 147464 | tf_op jit(solution)/shard_map/ppermute | solution.py:333
  (1 other events, 0.8 us)

commit v15 on v14

--- a/solution.py
+++ b/solution.py
@@ -15,7 +15,7 @@
 MID = 64
 WINDOW = 5
 SEND_GRANT = 60
-PAIRS = 4
+PAIRS = 12
 
 F32 = jnp.float32
 BF16 = jnp.bfloat16
@@ -377,11 +377,11 @@
     half = owners // 2
     distant, close = list(range(half, owners)), list(range(1, half))
     mixed = [distant[0]] + [d for pair in zip(close, distant[1:]) for d in pair]
-    before = {mixed[k]: (half,) for k in range(WINDOW, len(mixed))}
+    before = {mixed[k]: (mixed[k - 3 - k % 2],) for k in range(WINDOW, len(mixed))}
     last = mixed[WINDOW]
     received = exchanged(sent, mixed, {**before, last: (*before[last], staged, *first_tables)})
     received[0] = staged
-    order = [0] + mixed
+    order = [0] + distant + close
     relay, columns = call(
         functools.partial(relay_kernel, g),
         [jax.ShapeDtypeStruct((owners * 2 * g, slots), F32), jax.ShapeDtypeStruct((8, owners * slots), F32)],

time: 62.2 us -> 60.2 us (0.968)
  Pallas kernels: 24.3 us -> 22.9 us
  starting transfers between devices: 24.3 us -> 23.4 us
    pallas_call x9, Pallas kernels: 24.3 us -> 22.9 us  [call(): pl.pallas_call(kernel, out_shape=out_shapes, in_specs=[pl.BlockSpec(memor...]
    ppermute x14, starting transfers between devices: 22.6 us -> 21.7 us  [exchanged(): moved[d] = lax.ppermute(block, 'stick', [(i, i ^ d) for i in range(owners)])]
  transfers between devices with their start and end apart: 17 -> 17, of which waited for: 6 -> 6; matrix products, arithmetic and copies ran while one was open for 0% -> 0% of each run, Pallas kernels for 21% -> 22%
where the time goes in v15:
time: 60.2 us; the launch traced here: 59.9 us
  starting transfers between devices  23.4 us (39%)
  Pallas kernels  22.9 us (38%)
  waiting for transfers between devices  11.6 us (19%)
  local copies, waits for them, and re-layouts  1.81 us (3%)
    pallas_call x9, Pallas kernels, call(): pl.pallas_call(kernel, out_shape=out_shapes, in_specs=[pl.BlockSpec(memor...  22.9 us
    ppermute x14, starting transfers between devices, exchanged(): moved[d] = lax.ppermute(block, 'stick', [(i, i ^ d) for i in range(owners)])  21.7 us
    ppermute x14, waiting for transfers between devices, exchanged(): moved[d] = lax.ppermute(block, 'stick', [(i, i ^ d) for i in range(owners)])  10 us
    unnamed x16, local copies, waits for them, and re-layouts  1.81 us
    ppermute x1, starting transfers between devices, shifted(): lax.ppermute(x, 'band', [(i, (i - distance) % groups) for i in range(grou...  1.56 us
    ppermute x1, waiting for transfers between devices, shifted(): lax.ppermute(x, 'band', [(i, (i - distance) % groups) for i in range(grou...  1.53 us
  transfers between devices with their start and end apart: 17, of which 6 were waited for; matrix products, arithmetic and copies ran while one was open for 0% of the time, Pallas kernels for 22%

profile of v15, /device:TPU:0, one launch (start us, length us, event | category | flops | bytes accessed | tf_op | source)
XLA Modules:
  0.0 59.9 jit_solution(2588760436313059981)
XLA Ops:
  0.0 1.9 %shard_map.91 = (f32[104,128]{1,0:T(8,128)}, f32[104,128]{1,0:T(8,128)}, f32[104,128]{1,0:T(8,128)}, f32[104,128]{1,0:T(8,128)}, f32[104,128]{1,0:T(8,128)}, /*i...) custom-call(f32[8,96,128]{2,1,0:T(8,128)} %sticks_ref.1, s32[1,128]{1,0:T(1,128)} %bitcast.1), custom_call_target="tpu_custom_call" | custom-call | flops 1 | bytes 1 | tf_op jit(solution)/shard_map/pallas_call | solution.py:312
  2.0 3.1 %collective-permute-start.3 = (f32[104,128]{1,0:T(8,128)}, f32[104,128]{1,0:T(8,128)S(1)}, u32[]{:S(2)}, u32[]{:S(2)}) collective-permute-start(f32[104,128]{1,0:T(8,128)} %get-tuple-element.40), channel_id=1, source_target_pairs={{0,8},{4,12},{8,0},{12,4},{16,24},{20,28},{24,16},{28,20},{1,9},{5... | collective-permute-start | bytes 159752 | tf_op jit(solution)/shard_map/ppermute | solution.py:333
  5.1 1.5 %collective-permute-start.5 = (f32[104,128]{1,0:T(8,128)}, f32[104,128]{1,0:T(8,128)S(1)}, u32[]{:S(2)}, u32[]{:S(2)}) collective-permute-start(f32[104,128]{1,0:T(8,128)} %get-tuple-element.42), channel_id=1, source_target_pairs={{0,4},{4,0},{8,12},{12,8},{16,20},{20,16},{24,28},{28,24},{1,5},{5... | collective-permute-start | bytes 159752 | tf_op jit(solution)/shard_map/ppermute | solution.py:333
  6.6 2.6 %collective-permute-start = (f32[104,128]{1,0:T(8,128)}, f32[104,128]{1,0:T(8,128)S(1)}, u32[]{:S(2)}, u32[]{:S(2)}) collective-permute-start(f32[104,128]{1,0:T(8,128)} %get-tuple-element.36), channel_id=1, source_target_pairs={{0,16},{4,20},{8,24},{12,28},{16,0},{20,4},{24,8},{28,12},{1,17},{... | collective-permute-start | bytes 159752 | tf_op jit(solution)/shard_map/ppermute | solution.py:333
  9.4 2.5 %collective-permute-start.2 = (f32[104,128]{1,0:T(8,128)}, f32[104,128]{1,0:T(8,128)S(1)}, u32[]{:S(2)}, u32[]{:S(2)}) collective-permute-start(f32[104,128]{1,0:T(8,128)} %get-tuple-element.38), channel_id=1, source_target_pairs={{0,24},{4,28},{8,16},{12,20},{16,8},{20,12},{24,0},{28,4},{1,25},{... | collective-permute-start | bytes 159752 | tf_op jit(solution)/shard_map/ppermute | solution.py:333
  11.9 1.0 %copy-done.5 = f32[224,288]{1,0:T(8,128)S(1)} copy-done((f32[224,288]{1,0:T(8,128)S(1)}, f32[224,288]{1,0:T(8,128)}, u32[]{:S(2)}) %copy-start.5) | copy-done | bytes 258072
  12.9 0.8 %copy-done.7 = f32[104,128]{1,0:T(8,128)S(1)} copy-done((f32[104,128]{1,0:T(8,128)S(1)}, f32[104,128]{1,0:T(8,128)}, u32[]{:S(2)}) %copy-start.7) | copy-done | bytes 53272
  13.7 2.4 %collective-permute-start.4 = (f32[104,128]{1,0:T(8,128)}, f32[104,128]{1,0:T(8,128)S(1)}, u32[]{:S(2)}, u32[]{:S(2)}) collective-permute-start(f32[104,128]{1,0:T(8,128)} %get-tuple-element.41), channel_id=1, source_target_pairs={{0,28},{4,24},{8,20},{12,16},{16,12},{20,8},{24,4},{28,0},{1,29},{... | collective-permute-start | bytes 159752 | tf_op jit(solution)/shard_map/ppermute | solution.py:333
  16.1 4.7 %collective-permute-done.4.refs_4_ = f32[104,128]{1,0:T(8,128)S(1)} collective-permute-done((f32[104,128]{1,0:T(8,128)}, f32[104,128]{1,0:T(8,128)S(1)}, u32[]{:S(2)}, u32[]{:S(2)}) %collective-permute-start.4) | collective-permute-done | bytes 53280 | tf_op jit(solution)/shard_map/ppermute | solution.py:333
  21.5 1.6 %collective-permute-start.7 = (f32[768,128]{1,0:T(8,128)S(1)}, f32[768,128]{1,0:T(8,128)S(1)}, u32[]{:S(2)}, u32[]{:S(2)}) collective-permute-start(f32[768,128]{1,0:T(8,128)S(1)} %get-tuple-element.47.blocks_ref), channel_id=1, source_target_pairs={{0,2},{1,3},{2,0},{3,1},{4,6},{5,7},{6,4},{7,5},{8,10},{9,11},{10,... | collective-permute-start | bytes 1179656 | tf_op jit(solution)/shard_map/ppermute | solution.py:349
  23.0 4.0 %shard_map.94.phi_ref = f32[1152,128]{1,0:T(8,128)S(1)} custom-call(f32[768,128]{1,0:T(8,128)S(1)} %get-tuple-element.47.blocks_ref, f32[8,1024]{1,0:T(8,128)S(1)} %get-tuple-element.48.columns_ref, bf16[128,288]{1,0:T(8,128)(2,1)S(1)} %get-tuple-element.44.stick_in_ref, bf16[96,144]{1,0:T(8,128)(2,1)S(1)} %get-tuple-element.45.left_ref), custom_call_target="tpu_custom_call" | custom-call | flops 1 | bytes 1 | tf_op jit(solution)/shard_map/pallas_call | solution.py:312
  27.1 1.2 %shard_map.95.hot_ref = bf16[1024,2304]{1,0:T(8,128)(2,1)S(1)} custom-call(f32[8,1024]{1,0:T(8,128)S(1)} %get-tuple-element.48.columns_ref), custom_call_target="tpu_custom_call" | custom-call | flops 1 | bytes 1 | tf_op jit(solution)/shard_map/pallas_call | solution.py:312
  28.3 1.5 %collective-permute-done.7.blocks_ref = f32[768,128]{1,0:T(8,128)S(1)} collective-permute-done((f32[768,128]{1,0:T(8,128)S(1)}, f32[768,128]{1,0:T(8,128)S(1)}, u32[]{:S(2)}, u32[]{:S(2)}) %collective-permute-start.7) | collective-permute-done | bytes 393248 | tf_op jit(solution)/shard_map/ppermute | solution.py:349
  29.9 4.0 %shard_map.96.first_ref = f32[1152,128]{1,0:T(8,128)S(1)} custom-call(f32[768,128]{1,0:T(8,128)S(1)} %collective-permute-done.7.blocks_ref, f32[8,1024]{1,0:T(8,128)S(1)} %get-tuple-element.48.columns_ref, bf16[128,288]{1,0:T(8,128)(2,1)S(1)} %get-tuple-element.44.stick_in_ref, bf16[96,144]{1,0:T(8,128)(2,1)S(1)} %get-tuple-element.45.left_ref), custom_call_target="tpu_custom_call" | custom-call | flops 1 | bytes 1 | tf_op jit(solution)/shard_map/pallas_call | solution.py:312
  34.0 3.7 %shard_map.97.before_ref = f32[1152,128]{1,0:T(8,128)S(1)} custom-call(f32[1152,128]{1,0:T(8,128)S(1)} %shard_map.94.phi_ref, f32[1152,128]{1,0:T(8,128)S(1)} %collective-permute-done.9.other_ref, f32[256,256]{1,0:T(8,128)S(1)} %copy-done.2, f32[256,256]{1,0:T(8,128)S(1)} %copy-done.1, f32[96,144]{1,0:T(8,128)S(1)} %copy-done.4, f32[96,144]{1,0:T(8,128)S(1)} %copy-done.3, ...), custom_call_target="tpu_custom_call" | custom-call | flops 1 | bytes 1 | tf_op jit(solution)/shard_map/pallas_call | solution.py:312
  37.8 7.2 %shard_map.98 = (f32[96,128]{1,0:T(8,128)S(1)}, f32[96,128]{1,0:T(8,128)S(1)}, f32[96,128]{1,0:T(8,128)S(1)}, f32[96,128]{1,0:T(8,128)S(1)}, f32[96,128]{1,0:T(8...) custom-call(f32[1152,128]{1,0:T(8,128)S(1)} %shard_map.94.phi_ref, ...), custom_call_target="tpu_custom_call" | custom-call | flops 1 | bytes 1 | tf_op jit(solution)/shard_map/pallas_call | solution.py:312
  45.1 1.1 %collective-permute-start.15 = (f32[96,128]{1,0:T(8,128)S(1)}, f32[96,128]{1,0:T(8,128)S(1)}, u32[]{:S(2)}, u32[]{:S(2)}) collective-permute-start(f32[96,128]{1,0:T(8,128)S(1)} %get-tuple-element.58), channel_id=1, source_target_pairs={{0,4},{4,0},{8,12},{12,8},{16,20},{20,16},{24,28},{28,24},{1,5},{5... | collective-permute-start | bytes 147464 | tf_op jit(solution)/shard_map/ppermute | solution.py:333
  46.2 2.4 %collective-permute-start.10 = (f32[96,128]{1,0:T(8,128)S(1)}, f32[96,128]{1,0:T(8,128)S(1)}, u32[]{:S(2)}, u32[]{:S(2)}) collective-permute-start(f32[96,128]{1,0:T(8,128)S(1)} %get-tuple-element.52), channel_id=1, source_target_pairs={{0,16},{4,20},{8,24},{12,28},{16,0},{20,4},{24,8},{28,12},{1,17},{... | collective-permute-start | bytes 147464 | tf_op jit(solution)/shard_map/ppermute | solution.py:333
  48.6 1.0 %collective-permute-start.11 = (f32[96,128]{1,0:T(8,128)S(1)}, f32[96,128]{1,0:T(8,128)S(1)}, u32[]{:S(2)}, u32[]{:S(2)}) collective-permute-start(f32[96,128]{1,0:T(8,128)S(1)} %get-tuple-element.53), channel_id=1, source_target_pairs={{0,20},{4,16},{8,28},{12,24},{16,4},{20,0},{24,12},{28,8},{1,21},{... | collective-permute-start | bytes 147464 | tf_op jit(solution)/shard_map/ppermute | solution.py:333
  49.5 2.2 %collective-permute-start.12 = (f32[96,128]{1,0:T(8,128)S(1)}, f32[96,128]{1,0:T(8,128)S(1)}, u32[]{:S(2)}, u32[]{:S(2)}) collective-permute-start(f32[96,128]{1,0:T(8,128)S(1)} %get-tuple-element.54), channel_id=1, source_target_pairs={{0,24},{4,28},{8,16},{12,20},{16,8},{20,12},{24,0},{28,4},{1,25},{... | collective-permute-start | bytes 147464 | tf_op jit(solution)/shard_map/ppermute | solution.py:333
  51.7 2.1 %collective-permute-start.14 = (f32[96,128]{1,0:T(8,128)S(1)}, f32[96,128]{1,0:T(8,128)S(1)}, u32[]{:S(2)}, u32[]{:S(2)}) collective-permute-start(f32[96,128]{1,0:T(8,128)S(1)} %get-tuple-element.57), channel_id=1, source_target_pairs={{0,28},{4,24},{8,20},{12,16},{16,12},{20,8},{24,4},{28,0},{1,29},{... | collective-permute-start | bytes 147464 | tf_op jit(solution)/shard_map/ppermute | solution.py:333
  54.4 2.7 %collective-permute-done.11.refs_2_ = f32[96,128]{1,0:T(8,128)S(1)} collective-permute-done((f32[96,128]{1,0:T(8,128)S(1)}, f32[96,128]{1,0:T(8,128)S(1)}, u32[]{:S(2)}, u32[]{:S(2)}) %collective-permute-start.11) | collective-permute-done | bytes 49184 | tf_op jit(solution)/shard_map/ppermute | solution.py:333
  57.1 1.5 %collective-permute-done.14.refs_4_ = f32[96,128]{1,0:T(8,128)S(1)} collective-permute-done((f32[96,128]{1,0:T(8,128)S(1)}, f32[96,128]{1,0:T(8,128)S(1)}, u32[]{:S(2)}, u32[]{:S(2)}) %collective-permute-start.14) | collective-permute-done | bytes 49184 | tf_op jit(solution)/shard_map/ppermute | solution.py:333
  59.2 0.8 %shard_map.99 = f32[8,96,128]{2,1,0:T(8,128)} custom-call(f32[96,128]{1,0:T(8,128)S(1)} %get-tuple-element.51.refs_0_, f32[96,128]{1,0:T(8,128)S(1)} %collective-permute-done.10.refs_1_, f32[96,128]{1,0:T(8,128)S(1)} %collective-permute-done.11.refs_2_, f32[96,128]{1,0:T(8,128)S(1)} %collective-permute-done.12.refs_3_, ...), custom_call_target="tpu_custom_call" | custom-call | flops 1 | bytes 1 | tf_op jit(solution)/shard_map/pallas_call | solution.py:312
  (35 shorter events, 2.2 us)
Async XLA Ops:
  0.0 34.0 %copy-start = (f32[2304,128]{1,0:T(8,128)S(1)}, f32[2304,128]{1,0:T(8,128)}, u32[]{:S(2)}) copy-start(f32[2304,128]{1,0:T(8,128)} %constant.20.clone.refs_4_) | copy-start | bytes 3538948
  0.0 34.0 %copy-start.3 = (f32[96,144]{1,0:T(8,128)S(1)}, f32[96,144]{1,0:T(8,128)}, u32[]{:S(2)}) copy-start(f32[96,144]{1,0:T(8,128)} %constant.17.clone.refs_3_) | copy-start | bytes 165892
  0.0 34.0 %copy-start.4 = (f32[96,144]{1,0:T(8,128)S(1)}, f32[96,144]{1,0:T(8,128)}, u32[]{:S(2)}) copy-start(f32[96,144]{1,0:T(8,128)} %constant.16.clone.refs_2_) | copy-start | bytes 165892
  0.0 34.0 %copy-start.1 = (f32[256,256]{1,0:T(8,128)S(1)}, f32[256,256]{1,0:T(8,128)}, u32[]{:S(2)}) copy-start(f32[256,256]{1,0:T(8,128)} %constant.15.clone.refs_1_) | copy-start | bytes 786436
  0.0 34.0 %copy-start.2 = (f32[256,256]{1,0:T(8,128)S(1)}, f32[256,256]{1,0:T(8,128)}, u32[]{:S(2)}) copy-start(f32[256,256]{1,0:T(8,128)} %constant.14.clone.refs_0_) | copy-start | bytes 786436
  2.0 11.8 %collective-permute-start.3 = (f32[104,128]{1,0:T(8,128)}, f32[104,128]{1,0:T(8,128)S(1)}, u32[]{:S(2)}, u32[]{:S(2)}) collective-permute-start(f32[104,128]{1,0:T(8,128)} %get-tuple-element.40), channel_id=1, source_target_pairs={{0,8},{4,12},{8,0},{12,4},{16,24},{20,28},{24,16},{28,20},{1,9},{5... | collective-permute-start | bytes 159752 | tf_op jit(solution)/shard_map/ppermute | solution.py:333
  5.1 11.1 %collective-permute-start.5 = (f32[104,128]{1,0:T(8,128)}, f32[104,128]{1,0:T(8,128)S(1)}, u32[]{:S(2)}, u32[]{:S(2)}) collective-permute-start(f32[104,128]{1,0:T(8,128)} %get-tuple-element.42), channel_id=1, source_target_pairs={{0,4},{4,0},{8,12},{12,8},{16,20},{20,16},{24,28},{28,24},{1,5},{5... | collective-permute-start | bytes 159752 | tf_op jit(solution)/shard_map/ppermute | solution.py:333
  6.6 9.5 %collective-permute-start = (f32[104,128]{1,0:T(8,128)}, f32[104,128]{1,0:T(8,128)S(1)}, u32[]{:S(2)}, u32[]{:S(2)}) collective-permute-start(f32[104,128]{1,0:T(8,128)} %get-tuple-element.36), channel_id=1, source_target_pairs={{0,16},{4,20},{8,24},{12,28},{16,0},{20,4},{24,8},{28,12},{1,17},{... | collective-permute-start | bytes 159752 | tf_op jit(solution)/shard_map/ppermute | solution.py:333
  9.2 7.0 %collective-permute-start.1 = (f32[104,128]{1,0:T(8,128)}, f32[104,128]{1,0:T(8,128)S(1)}, u32[]{:S(2)}, u32[]{:S(2)}) collective-permute-start(f32[104,128]{1,0:T(8,128)} %get-tuple-element.37), channel_id=1, source_target_pairs={{0,20},{4,16},{8,28},{12,24},{16,4},{20,0},{24,12},{28,8},{1,21},{... | collective-permute-start | bytes 159752 | tf_op jit(solution)/shard_map/ppermute | solution.py:333
  9.4 6.7 %collective-permute-start.2 = (f32[104,128]{1,0:T(8,128)}, f32[104,128]{1,0:T(8,128)S(1)}, u32[]{:S(2)}, u32[]{:S(2)}) collective-permute-start(f32[104,128]{1,0:T(8,128)} %get-tuple-element.38), channel_id=1, source_target_pairs={{0,24},{4,28},{8,16},{12,20},{16,8},{20,12},{24,0},{28,4},{1,25},{... | collective-permute-start | bytes 159752 | tf_op jit(solution)/shard_map/ppermute | solution.py:333
  11.9 1.0 %copy-start.5 = (f32[224,288]{1,0:T(8,128)S(1)}, f32[224,288]{1,0:T(8,128)}, u32[]{:S(2)}) copy-start(f32[224,288]{1,0:T(8,128)} %constant.18.clone.tables_ref) | copy-start | bytes 774148
  13.7 7.1 %collective-permute-start.4 = (f32[104,128]{1,0:T(8,128)}, f32[104,128]{1,0:T(8,128)S(1)}, u32[]{:S(2)}, u32[]{:S(2)}) collective-permute-start(f32[104,128]{1,0:T(8,128)} %get-tuple-element.41), channel_id=1, source_target_pairs={{0,28},{4,24},{8,20},{12,16},{16,12},{20,8},{24,4},{28,0},{1,29},{... | collective-permute-start | bytes 159752 | tf_op jit(solution)/shard_map/ppermute | solution.py:333
  16.1 5.3 %collective-permute-start.6 = (f32[104,128]{1,0:T(8,128)}, f32[104,128]{1,0:T(8,128)S(1)}, u32[]{:S(2)}, u32[]{:S(2)}) collective-permute-start(f32[104,128]{1,0:T(8,128)} %get-tuple-element.46), channel_id=1, source_target_pairs={{0,12},{4,8},{8,4},{12,0},{16,28},{20,24},{24,20},{28,16},{1,13},{... | collective-permute-start | bytes 159752 | tf_op jit(solution)/shard_map/ppermute | solution.py:333
  21.5 8.4 %collective-permute-start.7 = (f32[768,128]{1,0:T(8,128)S(1)}, f32[768,128]{1,0:T(8,128)S(1)}, u32[]{:S(2)}, u32[]{:S(2)}) collective-permute-start(f32[768,128]{1,0:T(8,128)S(1)} %get-tuple-element.47.blocks_ref), channel_id=1, source_target_pairs={{0,2},{1,3},{2,0},{3,1},{4,6},{5,7},{6,4},{7,5},{8,10},{9,11},{10,... | collective-permute-start | bytes 1179656 | tf_op jit(solution)/shard_map/ppermute | solution.py:349
  27.0 10.7 %copy-start.6 = (f32[96,384]{1,0:T(8,128)S(1)}, f32[96,384]{1,0:T(8,128)}, u32[]{:S(2)}) copy-start(f32[96,384]{1,0:T(8,128)} %constant.19.clone.stick_out_ref) | copy-start | bytes 442372
  27.0 6.9 %collective-permute-start.9 = (f32[1152,128]{1,0:T(8,128)S(1)}, f32[1152,128]{1,0:T(8,128)S(1)}, u32[]{:S(2)}, u32[]{:S(2)}) collective-permute-start(f32[1152,128]{1,0:T(8,128)S(1)} %shard_map.94.phi_ref), channel_id=1, source_target_pairs={{0,1},{1,0},{2,3},{3,2},{4,5},{5,4},{6,7},{7,6},{8,9},{9,8},{10,11... | collective-permute-start | bytes 1769480 | tf_op jit(solution)/shard_map/ppermute | solution.py:352
  33.9 3.9 %collective-permute-start.8 = (f32[1152,128]{1,0:T(8,128)S(1)}, f32[1152,128]{1,0:T(8,128)S(1)}, u32[]{:S(2)}, u32[]{:S(2)}) collective-permute-start(f32[1152,128]{1,0:T(8,128)S(1)} %shard_map.96.first_ref), channel_id=1, source_target_pairs={{0,1},{1,0},{2,3},{3,2},{4,5},{5,4},{6,7},{7,6},{8,9},{9,8},{10,11... | collective-permute-start | bytes 1769480 | tf_op jit(solution)/shard_map/ppermute | solution.py:352
  45.0 6.7 %collective-permute-start.13 = (f32[96,128]{1,0:T(8,128)S(1)}, f32[96,128]{1,0:T(8,128)S(1)}, u32[]{:S(2)}, u32[]{:S(2)}) collective-permute-start(f32[96,128]{1,0:T(8,128)S(1)} %get-tuple-element.56), channel_id=1, source_target_pairs={{0,8},{4,12},{8,0},{12,4},{16,24},{20,28},{24,16},{28,20},{1,9},{5... | collective-permute-start | bytes 147464 | tf_op jit(solution)/shard_map/ppermute | solution.py:333
  45.1 8.8 %collective-permute-start.15 = (f32[96,128]{1,0:T(8,128)S(1)}, f32[96,128]{1,0:T(8,128)S(1)}, u32[]{:S(2)}, u32[]{:S(2)}) collective-permute-start(f32[96,128]{1,0:T(8,128)S(1)} %get-tuple-element.58), channel_id=1, source_target_pairs={{0,4},{4,0},{8,12},{12,8},{16,20},{20,16},{24,28},{28,24},{1,5},{5... | collective-permute-start | bytes 147464 | tf_op jit(solution)/shard_map/ppermute | solution.py:333
  46.2 8.2 %collective-permute-start.10 = (f32[96,128]{1,0:T(8,128)S(1)}, f32[96,128]{1,0:T(8,128)S(1)}, u32[]{:S(2)}, u32[]{:S(2)}) collective-permute-start(f32[96,128]{1,0:T(8,128)S(1)} %get-tuple-element.52), channel_id=1, source_target_pairs={{0,16},{4,20},{8,24},{12,28},{16,0},{20,4},{24,8},{28,12},{1,17},{... | collective-permute-start | bytes 147464 | tf_op jit(solution)/shard_map/ppermute | solution.py:333
  48.6 8.6 %collective-permute-start.11 = (f32[96,128]{1,0:T(8,128)S(1)}, f32[96,128]{1,0:T(8,128)S(1)}, u32[]{:S(2)}, u32[]{:S(2)}) collective-permute-start(f32[96,128]{1,0:T(8,128)S(1)} %get-tuple-element.53), channel_id=1, source_target_pairs={{0,20},{4,16},{8,28},{12,24},{16,4},{20,0},{24,12},{28,8},{1,21},{... | collective-permute-start | bytes 147464 | tf_op jit(solution)/shard_map/ppermute | solution.py:333
  49.5 7.6 %collective-permute-start.12 = (f32[96,128]{1,0:T(8,128)S(1)}, f32[96,128]{1,0:T(8,128)S(1)}, u32[]{:S(2)}, u32[]{:S(2)}) collective-permute-start(f32[96,128]{1,0:T(8,128)S(1)} %get-tuple-element.54), channel_id=1, source_target_pairs={{0,24},{4,28},{8,16},{12,20},{16,8},{20,12},{24,0},{28,4},{1,25},{... | collective-permute-start | bytes 147464 | tf_op jit(solution)/shard_map/ppermute | solution.py:333
  51.7 6.9 %collective-permute-start.14 = (f32[96,128]{1,0:T(8,128)S(1)}, f32[96,128]{1,0:T(8,128)S(1)}, u32[]{:S(2)}, u32[]{:S(2)}) collective-permute-start(f32[96,128]{1,0:T(8,128)S(1)} %get-tuple-element.57), channel_id=1, source_target_pairs={{0,28},{4,24},{8,20},{12,16},{16,12},{20,8},{24,4},{28,0},{1,29},{... | collective-permute-start | bytes 147464 | tf_op jit(solution)/shard_map/ppermute | solution.py:333
  53.8 5.3 %collective-permute-start.16 = (f32[96,128]{1,0:T(8,128)S(1)}, f32[96,128]{1,0:T(8,128)S(1)}, u32[]{:S(2)}, u32[]{:S(2)}) collective-permute-start(f32[96,128]{1,0:T(8,128)S(1)} %get-tuple-element.60), channel_id=1, source_target_pairs={{0,12},{4,8},{8,4},{12,0},{16,28},{20,24},{24,20},{28,16},{1,13},{... | collective-permute-start | bytes 147464 | tf_op jit(solution)/shard_map/ppermute | solution.py:333
  (1 other events, 0.8 us)

commit v16 on v15

--- a/solution.py
+++ b/solution.py
@@ -15,7 +15,7 @@
 MID = 64
 WINDOW = 5
 SEND_GRANT = 60
-PAIRS = 12
+PAIRS = 6
 
 F32 = jnp.float32
 BF16 = jnp.bfloat16
@@ -187,23 +187,34 @@
         columns_ref[:, k * LANES : (k + 1) * LANES] = ref[2 * g :, :]
 
 
-def field_kernel(g, blocks_ref, columns_ref, stick_in_ref, left_ref, phi_ref, work_a):
+def placed(g, blocks_ref, columns_ref, stick_in_ref):
     columns = columns_ref[:1, :].astype(jnp.int32)
-    stick_in, backward = stick_in_ref[...], left_ref[...]
+    stick_in = stick_in_ref[...]
     blocks = [blocks_ref[k : k + 2 * g, :] for k in range(0, blocks_ref.shape[0], 2 * g)]
     sticks = []
     for k in range(0, len(blocks), 2):
         sticks.append(beside(*split(dot(stick_in, stacked(beside(blocks[k], blocks[k + 1]))).T)))
     sticks = jnp.concatenate(sticks, 0)
-
+    rows = g * g // 2
+    index = lax.broadcasted_iota(jnp.int16, (rows, columns.shape[1]), 0)
+    for first in (0, rows):
+        both = dot(one_hot(index, (columns - first).astype(jnp.int16)), sticks)
+        yield first, both[:, :LANES] + both[:, LANES:]
+
+
+def place_sticks_kernel(g, blocks_ref, columns_ref, stick_in_ref, grid_ref):
+    for first, part in placed(g, blocks_ref, columns_ref, stick_in_ref):
+        grid_ref[first : first + part.shape[0], :] = part
+
+
+def field_kernel(g, grid_ref, blocks_ref, columns_ref, stick_in_ref, left_ref, phi_ref, work_a):
+    backward = left_ref[...]
     half = g // 2
-    index = lax.broadcasted_iota(jnp.int16, (half * g, columns.shape[1]), 0)
-    for first in (0, half):
-        both = dot(one_hot(index, (columns - first * g).astype(jnp.int16)), sticks)
-        placed = both[:, :LANES] + both[:, LANES:]
+    for first, part in placed(g, blocks_ref, columns_ref, stick_in_ref):
+        part = part + grid_ref[first : first + part.shape[0], :]
         for k in range(0, half, 2):
-            slabs = left_complex(backward, placed[k * g : (k + 1) * g], placed[(k + 1) * g : (k + 2) * g])
-            store(work_a, first + k, slabs)
+            slabs = left_complex(backward, part[k * g : (k + 1) * g], part[(k + 1) * g : (k + 2) * g])
+            store(work_a, first // g + k, slabs)
 
     for y in range(half):
         x = beside(strided(work_a, y, g), strided(work_a, y + half, g))
@@ -212,16 +223,17 @@
         store(phi_ref, y, [jnp.where(low, cos - turned(sin), turned(cos_up) - sin_up)])
 
 
-def pick_kernel(g, columns_ref, hot_ref):
-    for k in range(0, columns_ref.shape[1], LANES):
-        block = columns_ref[:, k : k + LANES]
+def pick_kernel(g, first_columns_ref, second_columns_ref, hot_ref):
+    columns = beside(first_columns_ref[...], second_columns_ref[...])
+    for k in range(0, columns.shape[1], LANES):
+        block = columns[:, k : k + LANES]
         wanted = jnp.concatenate([block] * (LANES // block.shape[0]), 0).T.astype(jnp.int32)
         for c in range(0, hot_ref.shape[1], LANES):
             index = lax.broadcasted_iota(jnp.int16, (LANES, LANES), 1)
             hot_ref[k : k + LANES, c : c + LANES] = one_hot(index, (wanted - c).astype(jnp.int16))
 
 
-def potentials(g, phi_ref, first_ref, second_ref, tables, work_a, work_b, emit):
+def potentials(g, phi_ref, first_ref, second_ref, tables, work_a, work_b, emit, last=PAIRS):
     forward, last_backward, left_forward, left_backward = [ref[...].astype(BF16) for ref in tables[:4]]
     coulomb_ref = tables[4]
     half = g // 2
@@ -240,14 +252,14 @@
         slabs = [slab * coulomb_ref[slab_rows(kx + j, g), :] for j, slab in enumerate(slabs)]
         store(work_b, kx, left_complex(left_backward, *slabs))
 
-    for start in range(0, half, PAIRS):
+    for start in range(0, half, last):
         lower, upper = [], []
-        for z in range(start, start + PAIRS):
+        for z in range(start, start + last):
             a, b = left_complex(left_backward, strided(work_b, z, g), strided(work_b, z + half, g))
             lower.append(a)
             upper.append(b)
         out = right(jnp.concatenate(lower + upper, 0), last_backward)
-        emit(start, *regrouped(out[: PAIRS * g], out[PAIRS * g :]))
+        emit(start, *regrouped(out[: last * g], out[last * g :]))
 
 
 def near_kernel(g, phi_ref, other_ref, *refs):
@@ -277,17 +289,17 @@
     half = g // 2
 
     def emit(start, first, second):
-        rows = slab_rows(start, g, PAIRS)
+        rows = slab_rows(start, g, half)
         total = before_ref[rows, :] + weights[0] * (first * first_ref[rows, :])
         total = total + weights[1] * (second * second_ref[rows, :])
-        for k in range(0, PAIRS, 2):
+        for k in range(0, half, 2):
             cos, sin = left(forward, beside(total[k * g : (k + 1) * g], total[(k + 1) * g : (k + 2) * g]))
             for j, (real, imag) in enumerate(zip(halves(cos), halves(sin))):
                 lower, upper = regrouped(real, imag)
                 store(work_a, start + k + j, [lower])
                 store(work_a, start + k + j + half, [upper])
 
-    potentials(g, phi_ref, first_ref, second_ref, tables, work_a, work_b, emit)
+    potentials(g, phi_ref, first_ref, second_ref, tables, work_a, work_b, emit, half)
 
     step = g // 3
     for first in range(0, g, step):
@@ -381,22 +393,34 @@
     last = mixed[WINDOW]
     received = exchanged(sent, mixed, {**before, last: (*before[last], staged, *first_tables)})
     received[0] = staged
-    order = [0] + distant + close
-    relay, columns = call(
-        functools.partial(relay_kernel, g),
-        [jax.ShapeDtypeStruct((owners * 2 * g, slots), F32), jax.ShapeDtypeStruct((8, owners * slots), F32)],
-        [],
-        1,
-        *[received[d] for d in order],
-    )
-
-    def orbital(blocks):
-        return call(functools.partial(field_kernel, g), field, [work], 1, blocks, columns, *first_tables)
-
-    phi = orbital(relay)
+    cut = owners * 3 // 4
+    order = [0] + mixed
+    order = order[:cut] + order[:cut - 1:-1]
+    stick_in, left_table = first_tables
+
+    def relayed(part):
+        shapes = [(len(part) * 2 * g, slots), (8, len(part) * slots)]
+        shapes = [jax.ShapeDtypeStruct(shape, F32) for shape in shapes]
+        return call(functools.partial(relay_kernel, g), shapes, [], 1, *[received[d] for d in part])
+
+    def on_grid(blocks):
+        grid = jax.ShapeDtypeStruct((rows, LANES), F32)
+        return call(functools.partial(place_sticks_kernel, g), grid, [], 1, blocks, columns[0], stick_in)
+
+    def orbital(grid, rest):
+        operands = (grid, rest, columns[1], stick_in, left_table)
+        return call(functools.partial(field_kernel, g), field, [work], 1, *operands)
+
+    first_blocks, first_columns = relayed(order[:cut])
+    columns = [first_columns]
+    own_grid = on_grid(first_blocks)
+    received[order[cut]] = after(received[order[cut]], own_grid)
+    last_blocks, last_columns = relayed(order[cut:])
+    columns.append(last_columns)
+    phi = orbital(own_grid, last_blocks)
     near = swapped(phi)
     hot = call(
-        functools.partial(pick_kernel, g), jax.ShapeDtypeStruct((owners * slots, rows), BF16), [], pot_flops, columns
+        functools.partial(pick_kernel, g), jax.ShapeDtypeStruct((owners * slots, rows), BF16), [], pot_flops, *columns
     )
     pot_tables = [t["forward"], t["last_backward"], t["left_forward"], t["left_backward"], t["coulomb"]]
 
@@ -404,7 +428,7 @@
         return call(functools.partial(kernel, g), field, [work, work], pot_flops, phi, *operands, *pot_tables)
 
     distances = (HALF,) if groups == 2 * HALF else (HALF, -HALF)
-    fields = [orbital(after(shifted(relay, distance), hot)) for distance in distances]
+    fields = [orbital(on_grid(shifted(first_blocks, d)), shifted(last_blocks, d)) for d in distances]
     total = potential_sum(near_kernel, after(near, *fields))
     if groups == 2 * HALF:
         weights = (2.0, 1.0)
@@ -429,12 +453,13 @@
     )
     result = [result[order.index(d)] for d in range(owners)]
     result = exchanged(result, mixed, before)
+    out_order = [0] + distant + close
     return call(
-        functools.partial(place_kernel, order),
+        functools.partial(place_kernel, out_order),
         jax.ShapeDtypeStruct(sticks.shape, F32),
         [],
         1,
-        *[result[d] for d in order],
+        *[result[d] for d in out_order],
     )
 
 

time: 60.2 us -> 59.3 us (0.985)
  starting transfers between devices: 23.4 us -> 25.1 us
  Pallas kernels: 22.9 us -> 21.2 us
  waiting for transfers between devices: 11.6 us -> 10.7 us
    pallas_call x9 -> x12, Pallas kernels: 22.9 us -> 21.2 us  [call(): pl.pallas_call(kernel, out_shape=out_shapes, in_specs=[pl.BlockSpec(memor...]
    ppermute x14, starting transfers between devices: 21.7 us -> 22.8 us  [exchanged(): moved[d] = lax.ppermute(block, 'stick', [(i, i ^ d) for i in range(owners)])]
    ppermute x1 -> x2, waiting for transfers between devices: 1.53 us -> 0.51 us  [shifted(): lax.ppermute(x, 'band', [(i, (i - distance) % groups) for i in range(grou...]
    ppermute x1 -> x2, starting transfers between devices: 1.56 us -> 2.16 us  [shifted(): lax.ppermute(x, 'band', [(i, (i - distance) % groups) for i in range(grou...]
  transfers between devices with their start and end apart: 17 -> 18, of which waited for: 6 -> 9; matrix products, arithmetic and copies ran while one was open for 0% -> 0% of each run, Pallas kernels for 22% -> 20%
where the time goes in v16:
time: 59.3 us; the launch traced here: 59 us
  starting transfers between devices  25.1 us (42%)
  Pallas kernels  21.2 us (36%)
  waiting for transfers between devices  10.7 us (18%)
  local copies, waits for them, and re-layouts  1.83 us (3%)
    ppermute x14, starting transfers between devices, exchanged(): moved[d] = lax.ppermute(block, 'stick', [(i, i ^ d) for i in range(owners)])  22.8 us
    pallas_call x12, Pallas kernels, call(): pl.pallas_call(kernel, out_shape=out_shapes, in_specs=[pl.BlockSpec(memor...  21.2 us
    ppermute x14, waiting for transfers between devices, exchanged(): moved[d] = lax.ppermute(block, 'stick', [(i, i ^ d) for i in range(owners)])  10.2 us
    ppermute x2, starting transfers between devices, shifted(): lax.ppermute(x, 'band', [(i, (i - distance) % groups) for i in range(grou...  2.16 us
    unnamed x16, local copies, waits for them, and re-layouts  1.83 us
  transfers between devices with their start and end apart: 18, of which 9 were waited for; matrix products, arithmetic and copies ran while one was open for 0% of the time, Pallas kernels for 20%

profile of v16, /device:TPU:0, one launch (start us, length us, event | category | flops | bytes accessed | tf_op | source)
XLA Modules:
  0.0 59.0 jit_solution(12489756724751582655)
XLA Ops:
  0.0 1.8 %shard_map.91 = (f32[104,128]{1,0:T(8,128)}, f32[104,128]{1,0:T(8,128)}, f32[104,128]{1,0:T(8,128)}, f32[104,128]{1,0:T(8,128)}, f32[104,128]{1,0:T(8,128)}, /*i...) custom-call(f32[8,96,128]{2,1,0:T(8,128)} %sticks_ref.1, s32[1,128]{1,0:T(1,128)} %bitcast.1), custom_call_target="tpu_custom_call" | custom-call | flops 1 | bytes 1 | tf_op jit(solution)/shard_map/pallas_call | solution.py:324
  1.8 4.1 %collective-permute-start = (f32[104,128]{1,0:T(8,128)}, f32[104,128]{1,0:T(8,128)S(1)}, u32[]{:S(2)}, u32[]{:S(2)}) collective-permute-start(f32[104,128]{1,0:T(8,128)} %get-tuple-element.38), channel_id=1, source_target_pairs={{0,16},{4,20},{8,24},{12,28},{16,0},{20,4},{24,8},{28,12},{1,17},{... | collective-permute-start | bytes 159752 | tf_op jit(solution)/shard_map/ppermute | solution.py:345
  5.9 1.5 %collective-permute-start.1 = (f32[104,128]{1,0:T(8,128)}, f32[104,128]{1,0:T(8,128)S(1)}, u32[]{:S(2)}, u32[]{:S(2)}) collective-permute-start(f32[104,128]{1,0:T(8,128)} %get-tuple-element.39), channel_id=1, source_target_pairs={{0,4},{4,0},{8,12},{12,8},{16,20},{20,16},{24,28},{28,24},{1,5},{5... | collective-permute-start | bytes 159752 | tf_op jit(solution)/shard_map/ppermute | solution.py:345
  7.5 1.8 %collective-permute-start.3 = (f32[104,128]{1,0:T(8,128)}, f32[104,128]{1,0:T(8,128)S(1)}, u32[]{:S(2)}, u32[]{:S(2)}) collective-permute-start(f32[104,128]{1,0:T(8,128)} %get-tuple-element.41), channel_id=1, source_target_pairs={{0,8},{4,12},{8,0},{12,4},{16,24},{20,28},{24,16},{28,20},{1,9},{5... | collective-permute-start | bytes 159752 | tf_op jit(solution)/shard_map/ppermute | solution.py:345
  9.3 2.5 %collective-permute-start.4 = (f32[104,128]{1,0:T(8,128)}, f32[104,128]{1,0:T(8,128)S(1)}, u32[]{:S(2)}, u32[]{:S(2)}) collective-permute-start(f32[104,128]{1,0:T(8,128)} %get-tuple-element.42), channel_id=1, source_target_pairs={{0,24},{4,28},{8,16},{12,20},{16,8},{20,12},{24,0},{28,4},{1,25},{... | collective-permute-start | bytes 159752 | tf_op jit(solution)/shard_map/ppermute | solution.py:345
  13.6 1.6 %collective-permute-done.2.refs_3_ = f32[104,128]{1,0:T(8,128)S(1)} collective-permute-done((f32[104,128]{1,0:T(8,128)}, f32[104,128]{1,0:T(8,128)S(1)}, u32[]{:S(2)}, u32[]{:S(2)}) %collective-permute-start.2) | collective-permute-done | bytes 53280 | tf_op jit(solution)/shard_map/ppermute | solution.py:345
  15.5 1.6 %collective-permute-start.7 = (f32[576,128]{1,0:T(8,128)S(1)}, f32[576,128]{1,0:T(8,128)S(1)}, u32[]{:S(2)}, u32[]{:S(2)}) collective-permute-start(f32[576,128]{1,0:T(8,128)S(1)} %get-tuple-element.43.blocks_ref), channel_id=1, source_target_pairs={{0,2},{1,3},{2,0},{3,1},{4,6},{5,7},{6,4},{7,5},{8,10},{9,11},{10,... | collective-permute-start | bytes 884744 | tf_op jit(solution)/shard_map/ppermute | solution.py:361
  17.0 3.4 %collective-permute-start.5 = (f32[104,128]{1,0:T(8,128)}, f32[104,128]{1,0:T(8,128)S(1)}, u32[]{:S(2)}, u32[]{:S(2)}) collective-permute-start(f32[104,128]{1,0:T(8,128)} %get-tuple-element.47), channel_id=1, source_target_pairs={{0,28},{4,24},{8,20},{12,16},{16,12},{20,8},{24,4},{28,0},{1,29},{... | collective-permute-start | bytes 159752 | tf_op jit(solution)/shard_map/ppermute | solution.py:345
  20.4 1.3 %shard_map.94.grid_ref = f32[2304,128]{1,0:T(8,128)S(1)} custom-call(f32[576,128]{1,0:T(8,128)S(1)} %get-tuple-element.43.blocks_ref, f32[8,768]{1,0:T(8,128)S(1)} %get-tuple-element.44.columns_ref.first_columns_ref, bf16[128,288]{1,0:T(8,128)(2,1)S(1)} %get-tuple-element.45.stick_in_ref), custom_call_target="tpu_custom_call" | custom-call | flops 1 | bytes 1 | tf_op jit(solution)/shard_map/pallas_call | solution.py:324
  21.8 2.3 %collective-permute-done.5.refs_0_ = f32[104,128]{1,0:T(8,128)S(1)} collective-permute-done((f32[104,128]{1,0:T(8,128)}, f32[104,128]{1,0:T(8,128)S(1)}, u32[]{:S(2)}, u32[]{:S(2)}) %collective-permute-start.5) | collective-permute-done | bytes 53280 | tf_op jit(solution)/shard_map/ppermute | solution.py:345
  24.1 1.6 %collective-permute-done.6.refs_1_ = f32[104,128]{1,0:T(8,128)S(1)} collective-permute-done((f32[104,128]{1,0:T(8,128)}, f32[104,128]{1,0:T(8,128)S(1)}, u32[]{:S(2)}, u32[]{:S(2)}) %collective-permute-start.6) | collective-permute-done | bytes 53280 | tf_op jit(solution)/shard_map/ppermute | solution.py:345
  26.3 2.1 %shard_map.96.phi_ref = f32[1152,128]{1,0:T(8,128)S(1)} custom-call(f32[2304,128]{1,0:T(8,128)S(1)} %shard_map.94.grid_ref, f32[192,128]{1,0:T(8,128)S(1)} %get-tuple-element.52.blocks_ref, f32[8,256]{1,0:T(8,128)S(1)} %get-tuple-element.53.columns_ref.second_columns_ref, bf16[128,288]{1,0:T(8,128)(2,1)S(1)} %get-tuple-element.45.stick_in_ref, ...), custom_call_target="tpu_custom_call" | custom-call | flops 1 | bytes 1 | tf_op jit(solution)/shard_map/pallas_call | solution.py:324
  28.5 1.3 %shard_map.97.grid_ref = f32[2304,128]{1,0:T(8,128)S(1)} custom-call(f32[576,128]{1,0:T(8,128)S(1)} %collective-permute-done.7.blocks_ref, f32[8,768]{1,0:T(8,128)S(1)} %get-tuple-element.44.columns_ref.first_columns_ref, bf16[128,288]{1,0:T(8,128)(2,1)S(1)} %get-tuple-element.45.stick_in_ref), custom_call_target="tpu_custom_call" | custom-call | flops 1 | bytes 1 | tf_op jit(solution)/shard_map/pallas_call | solution.py:324
  30.4 2.1 %shard_map.98.first_ref = f32[1152,128]{1,0:T(8,128)S(1)} custom-call(f32[2304,128]{1,0:T(8,128)S(1)} %shard_map.97.grid_ref, f32[192,128]{1,0:T(8,128)S(1)} %collective-permute-done.8.blocks_ref, f32[8,256]{1,0:T(8,128)S(1)} %get-tuple-element.53.columns_ref.second_columns_ref, bf16[128,288]{1,0:T(8,128)(2,1)S(1)} %get-tuple-element.45.stick_in_ref, ...), custom_call_target="tpu_custom_call" | custom-call | flops 1 | bytes 1 | tf_op jit(solution)/shard_map/pallas_call | solution.py:324
  32.7 1.2 %shard_map.100.hot_ref = bf16[1024,2304]{1,0:T(8,128)(2,1)S(1)} custom-call(f32[8,768]{1,0:T(8,128)S(1)} %get-tuple-element.44.columns_ref.first_columns_ref, f32[8,256]{1,0:T(8,128)S(1)} %get-tuple-element.53.columns_ref.second_columns_ref), custom_call_target="tpu_custom_call" | custom-call | flops 1 | bytes 1 | tf_op jit(solution)/shard_map/pallas_call | solution.py:324
  34.0 3.6 %shard_map.99.before_ref = f32[1152,128]{1,0:T(8,128)S(1)} custom-call(f32[1152,128]{1,0:T(8,128)S(1)} %shard_map.96.phi_ref, f32[1152,128]{1,0:T(8,128)S(1)} %collective-permute-done.10.other_ref, f32[256,256]{1,0:T(8,128)S(1)} %copy-done.2, f32[256,256]{1,0:T(8,128)S(1)} %copy-done.1, f32[96,144]{1,0:T(8,128)S(1)} %copy-done.4, f32[96,144]{1,0:T(8,128)S(1)} %copy-done.3, ...), custom_call_target="tpu_custom_call" | custom-call | flops 1 | bytes 1 | tf_op jit(solution)/shard_map/pallas_call | solution.py:324
  37.6 6.8 %shard_map.101 = (f32[96,128]{1,0:T(8,128)S(1)}, f32[96,128]{1,0:T(8,128)S(1)}, f32[96,128]{1,0:T(8,128)S(1)}, f32[96,128]{1,0:T(8,128)S(1)}, f32[96,128]{1,0:T(...) custom-call(f32[1152,128]{1,0:T(8,128)S(1)} %shard_map.96.phi_ref, ...), custom_call_target="tpu_custom_call" | custom-call | flops 1 | bytes 1 | tf_op jit(solution)/shard_map/pallas_call | solution.py:324
  44.5 1.1 %collective-permute-start.16 = (f32[96,128]{1,0:T(8,128)S(1)}, f32[96,128]{1,0:T(8,128)S(1)}, u32[]{:S(2)}, u32[]{:S(2)}) collective-permute-start(f32[96,128]{1,0:T(8,128)S(1)} %get-tuple-element.62), channel_id=1, source_target_pairs={{0,4},{4,0},{8,12},{12,8},{16,20},{20,16},{24,28},{28,24},{1,5},{5... | collective-permute-start | bytes 147464 | tf_op jit(solution)/shard_map/ppermute | solution.py:345
  45.6 1.9 %collective-permute-start.11 = (f32[96,128]{1,0:T(8,128)S(1)}, f32[96,128]{1,0:T(8,128)S(1)}, u32[]{:S(2)}, u32[]{:S(2)}) collective-permute-start(f32[96,128]{1,0:T(8,128)S(1)} %get-tuple-element.56), channel_id=1, source_target_pairs={{0,16},{4,20},{8,24},{12,28},{16,0},{20,4},{24,8},{28,12},{1,17},{... | collective-permute-start | bytes 147464 | tf_op jit(solution)/shard_map/ppermute | solution.py:345
  47.5 1.5 %collective-permute-start.12 = (f32[96,128]{1,0:T(8,128)S(1)}, f32[96,128]{1,0:T(8,128)S(1)}, u32[]{:S(2)}, u32[]{:S(2)}) collective-permute-start(f32[96,128]{1,0:T(8,128)S(1)} %get-tuple-element.57), channel_id=1, source_target_pairs={{0,20},{4,16},{8,28},{12,24},{16,4},{20,0},{24,12},{28,8},{1,21},{... | collective-permute-start | bytes 147464 | tf_op jit(solution)/shard_map/ppermute | solution.py:345
  48.9 1.4 %collective-permute-start.13 = (f32[96,128]{1,0:T(8,128)S(1)}, f32[96,128]{1,0:T(8,128)S(1)}, u32[]{:S(2)}, u32[]{:S(2)}) collective-permute-start(f32[96,128]{1,0:T(8,128)S(1)} %get-tuple-element.58), channel_id=1, source_target_pairs={{0,24},{4,28},{8,16},{12,20},{16,8},{20,12},{24,0},{28,4},{1,25},{... | collective-permute-start | bytes 147464 | tf_op jit(solution)/shard_map/ppermute | solution.py:345
  50.4 2.9 %collective-permute-start.15 = (f32[96,128]{1,0:T(8,128)S(1)}, f32[96,128]{1,0:T(8,128)S(1)}, u32[]{:S(2)}, u32[]{:S(2)}) collective-permute-start(f32[96,128]{1,0:T(8,128)S(1)} %get-tuple-element.61), channel_id=1, source_target_pairs={{0,28},{4,24},{8,20},{12,16},{16,12},{20,8},{24,4},{28,0},{1,29},{... | collective-permute-start | bytes 147464 | tf_op jit(solution)/shard_map/ppermute | solution.py:345
  55.2 2.1 %collective-permute-done.15.refs_4_ = f32[96,128]{1,0:T(8,128)S(1)} collective-permute-done((f32[96,128]{1,0:T(8,128)S(1)}, f32[96,128]{1,0:T(8,128)S(1)}, u32[]{:S(2)}, u32[]{:S(2)}) %collective-permute-start.15) | collective-permute-done | bytes 49184 | tf_op jit(solution)/shard_map/ppermute | solution.py:345
  57.2 1.0 %collective-permute-done.17.refs_7_ = f32[96,128]{1,0:T(8,128)S(1)} collective-permute-done((f32[96,128]{1,0:T(8,128)S(1)}, f32[96,128]{1,0:T(8,128)S(1)}, u32[]{:S(2)}, u32[]{:S(2)}) %collective-permute-start.17) | collective-permute-done | bytes 49184 | tf_op jit(solution)/shard_map/ppermute | solution.py:345
  (40 shorter events, 6.2 us)
Async XLA Ops:
  1.8 11.8 %collective-permute-start = (f32[104,128]{1,0:T(8,128)}, f32[104,128]{1,0:T(8,128)S(1)}, u32[]{:S(2)}, u32[]{:S(2)}) collective-permute-start(f32[104,128]{1,0:T(8,128)} %get-tuple-element.38), channel_id=1, source_target_pairs={{0,16},{4,20},{8,24},{12,28},{16,0},{20,4},{24,8},{28,12},{1,17},{... | collective-permute-start | bytes 159752 | tf_op jit(solution)/shard_map/ppermute | solution.py:345
  5.9 7.7 %collective-permute-start.1 = (f32[104,128]{1,0:T(8,128)}, f32[104,128]{1,0:T(8,128)S(1)}, u32[]{:S(2)}, u32[]{:S(2)}) collective-permute-start(f32[104,128]{1,0:T(8,128)} %get-tuple-element.39), channel_id=1, source_target_pairs={{0,4},{4,0},{8,12},{12,8},{16,20},{20,16},{24,28},{28,24},{1,5},{5... | collective-permute-start | bytes 159752 | tf_op jit(solution)/shard_map/ppermute | solution.py:345
  7.4 7.7 %collective-permute-start.2 = (f32[104,128]{1,0:T(8,128)}, f32[104,128]{1,0:T(8,128)S(1)}, u32[]{:S(2)}, u32[]{:S(2)}) collective-permute-start(f32[104,128]{1,0:T(8,128)} %get-tuple-element.40), channel_id=1, source_target_pairs={{0,20},{4,16},{8,28},{12,24},{16,4},{20,0},{24,12},{28,8},{1,21},{... | collective-permute-start | bytes 159752 | tf_op jit(solution)/shard_map/ppermute | solution.py:345
  7.5 7.7 %collective-permute-start.3 = (f32[104,128]{1,0:T(8,128)}, f32[104,128]{1,0:T(8,128)S(1)}, u32[]{:S(2)}, u32[]{:S(2)}) collective-permute-start(f32[104,128]{1,0:T(8,128)} %get-tuple-element.41), channel_id=1, source_target_pairs={{0,8},{4,12},{8,0},{12,4},{16,24},{20,28},{24,16},{28,20},{1,9},{5... | collective-permute-start | bytes 159752 | tf_op jit(solution)/shard_map/ppermute | solution.py:345
  9.3 6.1 %collective-permute-start.4 = (f32[104,128]{1,0:T(8,128)}, f32[104,128]{1,0:T(8,128)S(1)}, u32[]{:S(2)}, u32[]{:S(2)}) collective-permute-start(f32[104,128]{1,0:T(8,128)} %get-tuple-element.42), channel_id=1, source_target_pairs={{0,24},{4,28},{8,16},{12,20},{16,8},{20,12},{24,0},{28,4},{1,25},{... | collective-permute-start | bytes 159752 | tf_op jit(solution)/shard_map/ppermute | solution.py:345
  15.5 13.1 %collective-permute-start.7 = (f32[576,128]{1,0:T(8,128)S(1)}, f32[576,128]{1,0:T(8,128)S(1)}, u32[]{:S(2)}, u32[]{:S(2)}) collective-permute-start(f32[576,128]{1,0:T(8,128)S(1)} %get-tuple-element.43.blocks_ref), channel_id=1, source_target_pairs={{0,2},{1,3},{2,0},{3,1},{4,6},{5,7},{6,4},{7,5},{8,10},{9,11},{10,... | collective-permute-start | bytes 884744 | tf_op jit(solution)/shard_map/ppermute | solution.py:361
  17.0 7.0 %collective-permute-start.5 = (f32[104,128]{1,0:T(8,128)}, f32[104,128]{1,0:T(8,128)S(1)}, u32[]{:S(2)}, u32[]{:S(2)}) collective-permute-start(f32[104,128]{1,0:T(8,128)} %get-tuple-element.47), channel_id=1, source_target_pairs={{0,28},{4,24},{8,20},{12,16},{16,12},{20,8},{24,4},{28,0},{1,29},{... | collective-permute-start | bytes 159752 | tf_op jit(solution)/shard_map/ppermute | solution.py:345
  20.4 5.2 %collective-permute-start.6 = (f32[104,128]{1,0:T(8,128)}, f32[104,128]{1,0:T(8,128)S(1)}, u32[]{:S(2)}, u32[]{:S(2)}) collective-permute-start(f32[104,128]{1,0:T(8,128)} %get-tuple-element.51), channel_id=1, source_target_pairs={{0,12},{4,8},{8,4},{12,0},{16,28},{20,24},{24,20},{28,16},{1,13},{... | collective-permute-start | bytes 159752 | tf_op jit(solution)/shard_map/ppermute | solution.py:345
  25.7 4.7 %collective-permute-start.8 = (f32[192,128]{1,0:T(8,128)S(1)}, f32[192,128]{1,0:T(8,128)S(1)}, u32[]{:S(2)}, u32[]{:S(2)}) collective-permute-start(f32[192,128]{1,0:T(8,128)S(1)} %get-tuple-element.52.blocks_ref), channel_id=1, source_target_pairs={{0,2},{1,3},{2,0},{3,1},{4,6},{5,7},{6,4},{7,5},{8,10},{9,11},{10,... | collective-permute-start | bytes 294920 | tf_op jit(solution)/shard_map/ppermute | solution.py:361
  28.4 5.5 %collective-permute-start.10 = (f32[1152,128]{1,0:T(8,128)S(1)}, f32[1152,128]{1,0:T(8,128)S(1)}, u32[]{:S(2)}, u32[]{:S(2)}) collective-permute-start(f32[1152,128]{1,0:T(8,128)S(1)} %shard_map.96.phi_ref), channel_id=1, source_target_pairs={{0,1},{1,0},{2,3},{3,2},{4,5},{5,4},{6,7},{7,6},{8,9},{9,8},{10,11... | collective-permute-start | bytes 1769480 | tf_op jit(solution)/shard_map/ppermute | solution.py:364
  32.5 1.4 %copy-start = (f32[2304,128]{1,0:T(8,128)S(1)}, f32[2304,128]{1,0:T(8,128)}, u32[]{:S(2)}) copy-start(f32[2304,128]{1,0:T(8,128)} %constant.20.clone.refs_4_) | copy-start | bytes 3538948
  32.5 1.4 %copy-start.1 = (f32[256,256]{1,0:T(8,128)S(1)}, f32[256,256]{1,0:T(8,128)}, u32[]{:S(2)}) copy-start(f32[256,256]{1,0:T(8,128)} %constant.15.clone.refs_1_) | copy-start | bytes 786436
  32.5 1.4 %copy-start.2 = (f32[256,256]{1,0:T(8,128)S(1)}, f32[256,256]{1,0:T(8,128)}, u32[]{:S(2)}) copy-start(f32[256,256]{1,0:T(8,128)} %constant.14.clone.refs_0_) | copy-start | bytes 786436
  32.6 1.4 %copy-start.3 = (f32[96,144]{1,0:T(8,128)S(1)}, f32[96,144]{1,0:T(8,128)}, u32[]{:S(2)}) copy-start(f32[96,144]{1,0:T(8,128)} %constant.17.clone.refs_3_) | copy-start | bytes 165892
  32.6 1.4 %copy-start.4 = (f32[96,144]{1,0:T(8,128)S(1)}, f32[96,144]{1,0:T(8,128)}, u32[]{:S(2)}) copy-start(f32[96,144]{1,0:T(8,128)} %constant.16.clone.refs_2_) | copy-start | bytes 165892
  32.6 5.0 %collective-permute-start.9 = (f32[1152,128]{1,0:T(8,128)S(1)}, f32[1152,128]{1,0:T(8,128)S(1)}, u32[]{:S(2)}, u32[]{:S(2)}) collective-permute-start(f32[1152,128]{1,0:T(8,128)S(1)} %shard_map.98.first_ref), channel_id=1, source_target_pairs={{0,1},{1,0},{2,3},{3,2},{4,5},{5,4},{6,7},{7,6},{8,9},{9,8},{10,11... | collective-permute-start | bytes 1769480 | tf_op jit(solution)/shard_map/ppermute | solution.py:364
  33.9 3.7 %copy-start.6 = (f32[96,384]{1,0:T(8,128)S(1)}, f32[96,384]{1,0:T(8,128)}, u32[]{:S(2)}) copy-start(f32[96,384]{1,0:T(8,128)} %constant.19.clone.stick_out_ref) | copy-start | bytes 442372
  44.4 6.0 %collective-permute-start.14 = (f32[96,128]{1,0:T(8,128)S(1)}, f32[96,128]{1,0:T(8,128)S(1)}, u32[]{:S(2)}, u32[]{:S(2)}) collective-permute-start(f32[96,128]{1,0:T(8,128)S(1)} %get-tuple-element.60), channel_id=1, source_target_pairs={{0,8},{4,12},{8,0},{12,4},{16,24},{20,28},{24,16},{28,20},{1,9},{5... | collective-permute-start | bytes 147464 | tf_op jit(solution)/shard_map/ppermute | solution.py:345
  44.5 8.8 %collective-permute-start.16 = (f32[96,128]{1,0:T(8,128)S(1)}, f32[96,128]{1,0:T(8,128)S(1)}, u32[]{:S(2)}, u32[]{:S(2)}) collective-permute-start(f32[96,128]{1,0:T(8,128)S(1)} %get-tuple-element.62), channel_id=1, source_target_pairs={{0,4},{4,0},{8,12},{12,8},{16,20},{20,16},{24,28},{28,24},{1,5},{5... | collective-permute-start | bytes 147464 | tf_op jit(solution)/shard_map/ppermute | solution.py:345
  45.6 8.2 %collective-permute-start.11 = (f32[96,128]{1,0:T(8,128)S(1)}, f32[96,128]{1,0:T(8,128)S(1)}, u32[]{:S(2)}, u32[]{:S(2)}) collective-permute-start(f32[96,128]{1,0:T(8,128)S(1)} %get-tuple-element.56), channel_id=1, source_target_pairs={{0,16},{4,20},{8,24},{12,28},{16,0},{20,4},{24,8},{28,12},{1,17},{... | collective-permute-start | bytes 147464 | tf_op jit(solution)/shard_map/ppermute | solution.py:345
  47.5 7.3 %collective-permute-start.12 = (f32[96,128]{1,0:T(8,128)S(1)}, f32[96,128]{1,0:T(8,128)S(1)}, u32[]{:S(2)}, u32[]{:S(2)}) collective-permute-start(f32[96,128]{1,0:T(8,128)S(1)} %get-tuple-element.57), channel_id=1, source_target_pairs={{0,20},{4,16},{8,28},{12,24},{16,4},{20,0},{24,12},{28,8},{1,21},{... | collective-permute-start | bytes 147464 | tf_op jit(solution)/shard_map/ppermute | solution.py:345
  48.9 6.2 %collective-permute-start.13 = (f32[96,128]{1,0:T(8,128)S(1)}, f32[96,128]{1,0:T(8,128)S(1)}, u32[]{:S(2)}, u32[]{:S(2)}) collective-permute-start(f32[96,128]{1,0:T(8,128)S(1)} %get-tuple-element.58), channel_id=1, source_target_pairs={{0,24},{4,28},{8,16},{12,20},{16,8},{20,12},{24,0},{28,4},{1,25},{... | collective-permute-start | bytes 147464 | tf_op jit(solution)/shard_map/ppermute | solution.py:345
  50.4 6.9 %collective-permute-start.15 = (f32[96,128]{1,0:T(8,128)S(1)}, f32[96,128]{1,0:T(8,128)S(1)}, u32[]{:S(2)}, u32[]{:S(2)}) collective-permute-start(f32[96,128]{1,0:T(8,128)S(1)} %get-tuple-element.61), channel_id=1, source_target_pairs={{0,28},{4,24},{8,20},{12,16},{16,12},{20,8},{24,4},{28,0},{1,29},{... | collective-permute-start | bytes 147464 | tf_op jit(solution)/shard_map/ppermute | solution.py:345
  53.3 5.0 %collective-permute-start.17 = (f32[96,128]{1,0:T(8,128)S(1)}, f32[96,128]{1,0:T(8,128)S(1)}, u32[]{:S(2)}, u32[]{:S(2)}) collective-permute-start(f32[96,128]{1,0:T(8,128)S(1)} %get-tuple-element.64), channel_id=1, source_target_pairs={{0,12},{4,8},{8,4},{12,0},{16,28},{20,24},{24,20},{28,16},{1,13},{... | collective-permute-start | bytes 147464 | tf_op jit(solution)/shard_map/ppermute | solution.py:345
  (2 other events, 1.8 us)

commit v17 on v16

--- a/solution.py
+++ b/solution.py
@@ -403,9 +403,9 @@
         shapes = [jax.ShapeDtypeStruct(shape, F32) for shape in shapes]
         return call(functools.partial(relay_kernel, g), shapes, [], 1, *[received[d] for d in part])
 
-    def on_grid(blocks):
+    def on_grid(blocks, flops=1):
         grid = jax.ShapeDtypeStruct((rows, LANES), F32)
-        return call(functools.partial(place_sticks_kernel, g), grid, [], 1, blocks, columns[0], stick_in)
+        return call(functools.partial(place_sticks_kernel, g), grid, [], flops, blocks, columns[0], stick_in)
 
     def orbital(grid, rest):
         operands = (grid, rest, columns[1], stick_in, left_table)
@@ -413,7 +413,7 @@
 
     first_blocks, first_columns = relayed(order[:cut])
     columns = [first_columns]
-    own_grid = on_grid(first_blocks)
+    own_grid = on_grid(first_blocks, 5 * 10**9)
     received[order[cut]] = after(received[order[cut]], own_grid)
     last_blocks, last_columns = relayed(order[cut:])
     columns.append(last_columns)

time: 59.3 us -> 56.7 us (0.956)
  waiting for transfers between devices: 10.7 us -> 7.48 us
    ppermute x14, waiting for transfers between devices: 10.2 us -> 7.47 us  [exchanged(): moved[d] = lax.ppermute(block, 'stick', [(i, i ^ d) for i in range(owners)])]
    ppermute x2, starting transfers between devices: 2.16 us -> 3.11 us  [shifted(): lax.ppermute(x, 'band', [(i, (i - distance) % groups) for i in range(grou...]
    ppermute x14, starting transfers between devices: 22.8 us -> 21.9 us  [exchanged(): moved[d] = lax.ppermute(block, 'stick', [(i, i ^ d) for i in range(owners)])]
  transfers between devices with their start and end apart: 18 -> 18, of which waited for: 9 -> 5; matrix products, arithmetic and copies ran while one was open for 0% -> 0% of each run, Pallas kernels for 20% -> 21%
where the time goes in v17:
time: 56.7 us; the launch traced here: 56.4 us
  starting transfers between devices  25.6 us (45%)
  Pallas kernels  21.2 us (37%)
  waiting for transfers between devices  7.48 us (13%)
  local copies, waits for them, and re-layouts  1.83 us (3%)
    ppermute x14, starting transfers between devices, exchanged(): moved[d] = lax.ppermute(block, 'stick', [(i, i ^ d) for i in range(owners)])  21.9 us
    pallas_call x12, Pallas kernels, call(): pl.pallas_call(kernel, out_shape=out_shapes, in_specs=[pl.BlockSpec(memor...  21.2 us
    ppermute x14, waiting for transfers between devices, exchanged(): moved[d] = lax.ppermute(block, 'stick', [(i, i ^ d) for i in range(owners)])  7.47 us
    ppermute x2, starting transfers between devices, shifted(): lax.ppermute(x, 'band', [(i, (i - distance) % groups) for i in range(grou...  3.11 us
    unnamed x16, local copies, waits for them, and re-layouts  1.83 us
  transfers between devices with their start and end apart: 18, of which 5 were waited for; matrix products, arithmetic and copies ran while one was open for 0% of the time, Pallas kernels for 21%

profile of v17, /device:TPU:0, one launch (start us, length us, event | category | flops | bytes accessed | tf_op | source)
XLA Modules:
  0.0 56.4 jit_solution(11466815507080490962)
XLA Ops:
  0.0 1.8 %shard_map.91 = (f32[104,128]{1,0:T(8,128)}, f32[104,128]{1,0:T(8,128)}, f32[104,128]{1,0:T(8,128)}, f32[104,128]{1,0:T(8,128)}, f32[104,128]{1,0:T(8,128)}, /*i...) custom-call(f32[8,96,128]{2,1,0:T(8,128)} %sticks_ref.1, s32[1,128]{1,0:T(1,128)} %bitcast.1), custom_call_target="tpu_custom_call" | custom-call | flops 1 | bytes 1 | tf_op jit(solution)/shard_map/pallas_call | solution.py:324
  1.8 3.1 %collective-permute-start.3 = (f32[104,128]{1,0:T(8,128)}, f32[104,128]{1,0:T(8,128)S(1)}, u32[]{:S(2)}, u32[]{:S(2)}) collective-permute-start(f32[104,128]{1,0:T(8,128)} %get-tuple-element.41), channel_id=1, source_target_pairs={{0,8},{4,12},{8,0},{12,4},{16,24},{20,28},{24,16},{28,20},{1,9},{5... | collective-permute-start | bytes 159752 | tf_op jit(solution)/shard_map/ppermute | solution.py:345
  4.9 1.5 %collective-permute-start.1 = (f32[104,128]{1,0:T(8,128)}, f32[104,128]{1,0:T(8,128)S(1)}, u32[]{:S(2)}, u32[]{:S(2)}) collective-permute-start(f32[104,128]{1,0:T(8,128)} %get-tuple-element.39), channel_id=1, source_target_pairs={{0,4},{4,0},{8,12},{12,8},{16,20},{20,16},{24,28},{28,24},{1,5},{5... | collective-permute-start | bytes 159752 | tf_op jit(solution)/shard_map/ppermute | solution.py:345
  6.4 2.6 %collective-permute-start = (f32[104,128]{1,0:T(8,128)}, f32[104,128]{1,0:T(8,128)S(1)}, u32[]{:S(2)}, u32[]{:S(2)}) collective-permute-start(f32[104,128]{1,0:T(8,128)} %get-tuple-element.38), channel_id=1, source_target_pairs={{0,16},{4,20},{8,24},{12,28},{16,0},{20,4},{24,8},{28,12},{1,17},{... | collective-permute-start | bytes 159752 | tf_op jit(solution)/shard_map/ppermute | solution.py:345
  9.3 2.5 %collective-permute-start.4 = (f32[104,128]{1,0:T(8,128)}, f32[104,128]{1,0:T(8,128)S(1)}, u32[]{:S(2)}, u32[]{:S(2)}) collective-permute-start(f32[104,128]{1,0:T(8,128)} %get-tuple-element.42), channel_id=1, source_target_pairs={{0,24},{4,28},{8,16},{12,20},{16,8},{20,12},{24,0},{28,4},{1,25},{... | collective-permute-start | bytes 159752 | tf_op jit(solution)/shard_map/ppermute | solution.py:345
  11.8 1.0 %copy-done.5 = f32[224,288]{1,0:T(8,128)S(1)} copy-done((f32[224,288]{1,0:T(8,128)S(1)}, f32[224,288]{1,0:T(8,128)}, u32[]{:S(2)}) %copy-start.5) | copy-done | bytes 258072
  13.6 2.4 %collective-permute-start.5 = (f32[104,128]{1,0:T(8,128)}, f32[104,128]{1,0:T(8,128)S(1)}, u32[]{:S(2)}, u32[]{:S(2)}) collective-permute-start(f32[104,128]{1,0:T(8,128)} %get-tuple-element.47), channel_id=1, source_target_pairs={{0,28},{4,24},{8,20},{12,16},{16,12},{20,8},{24,4},{28,0},{1,29},{... | collective-permute-start | bytes 159752 | tf_op jit(solution)/shard_map/ppermute | solution.py:345
  16.0 1.6 %collective-permute-start.7 = (f32[576,128]{1,0:T(8,128)S(1)}, f32[576,128]{1,0:T(8,128)S(1)}, u32[]{:S(2)}, u32[]{:S(2)}) collective-permute-start(f32[576,128]{1,0:T(8,128)S(1)} %get-tuple-element.43.blocks_ref), channel_id=1, source_target_pairs={{0,2},{1,3},{2,0},{3,1},{4,6},{5,7},{6,4},{7,5},{8,10},{9,11},{10,... | collective-permute-start | bytes 884744 | tf_op jit(solution)/shard_map/ppermute | solution.py:361
  17.6 1.3 %shard_map.94.grid_ref = f32[2304,128]{1,0:T(8,128)S(1)} custom-call(f32[576,128]{1,0:T(8,128)S(1)} %get-tuple-element.43.blocks_ref, f32[8,768]{1,0:T(8,128)S(1)} %get-tuple-element.44.columns_ref.first_columns_ref, bf16[128,288]{1,0:T(8,128)(2,1)S(1)} %get-tuple-element.45.stick_in_ref), custom_call_target="tpu_custom_call" | custom-call | flops 5000000000 | bytes 5000000000 | tf_op jit(solution)/shard_map/pallas_call | solution.py:324
  18.9 1.8 %collective-permute-done.5.refs_0_ = f32[104,128]{1,0:T(8,128)S(1)} collective-permute-done((f32[104,128]{1,0:T(8,128)}, f32[104,128]{1,0:T(8,128)S(1)}, u32[]{:S(2)}, u32[]{:S(2)}) %collective-permute-start.5) | collective-permute-done | bytes 53280 | tf_op jit(solution)/shard_map/ppermute | solution.py:345
  21.3 1.6 %collective-permute-start.8 = (f32[192,128]{1,0:T(8,128)S(1)}, f32[192,128]{1,0:T(8,128)S(1)}, u32[]{:S(2)}, u32[]{:S(2)}) collective-permute-start(f32[192,128]{1,0:T(8,128)S(1)} %get-tuple-element.52.blocks_ref), channel_id=1, source_target_pairs={{0,2},{1,3},{2,0},{3,1},{4,6},{5,7},{6,4},{7,5},{8,10},{9,11},{10,... | collective-permute-start | bytes 294920 | tf_op jit(solution)/shard_map/ppermute | solution.py:361
  22.8 2.1 %shard_map.96.phi_ref = f32[1152,128]{1,0:T(8,128)S(1)} custom-call(f32[2304,128]{1,0:T(8,128)S(1)} %shard_map.94.grid_ref, f32[192,128]{1,0:T(8,128)S(1)} %get-tuple-element.52.blocks_ref, f32[8,256]{1,0:T(8,128)S(1)} %get-tuple-element.53.columns_ref.second_columns_ref, bf16[128,288]{1,0:T(8,128)(2,1)S(1)} %get-tuple-element.45.stick_in_ref, ...), custom_call_target="tpu_custom_call" | custom-call | flops 1 | bytes 1 | tf_op jit(solution)/shard_map/pallas_call | solution.py:324
  25.1 1.3 %shard_map.97.grid_ref = f32[2304,128]{1,0:T(8,128)S(1)} custom-call(f32[576,128]{1,0:T(8,128)S(1)} %collective-permute-done.7.blocks_ref, f32[8,768]{1,0:T(8,128)S(1)} %get-tuple-element.44.columns_ref.first_columns_ref, bf16[128,288]{1,0:T(8,128)(2,1)S(1)} %get-tuple-element.45.stick_in_ref), custom_call_target="tpu_custom_call" | custom-call | flops 1 | bytes 1 | tf_op jit(solution)/shard_map/pallas_call | solution.py:324
  26.4 2.1 %shard_map.98.first_ref = f32[1152,128]{1,0:T(8,128)S(1)} custom-call(f32[2304,128]{1,0:T(8,128)S(1)} %shard_map.97.grid_ref, f32[192,128]{1,0:T(8,128)S(1)} %collective-permute-done.8.blocks_ref, f32[8,256]{1,0:T(8,128)S(1)} %get-tuple-element.53.columns_ref.second_columns_ref, bf16[128,288]{1,0:T(8,128)(2,1)S(1)} %get-tuple-element.45.stick_in_ref, ...), custom_call_target="tpu_custom_call" | custom-call | flops 1 | bytes 1 | tf_op jit(solution)/shard_map/pallas_call | solution.py:324
  29.2 1.2 %shard_map.100.hot_ref = bf16[1024,2304]{1,0:T(8,128)(2,1)S(1)} custom-call(f32[8,768]{1,0:T(8,128)S(1)} %get-tuple-element.44.columns_ref.first_columns_ref, f32[8,256]{1,0:T(8,128)S(1)} %get-tuple-element.53.columns_ref.second_columns_ref), custom_call_target="tpu_custom_call" | custom-call | flops 1 | bytes 1 | tf_op jit(solution)/shard_map/pallas_call | solution.py:324
  30.5 3.6 %shard_map.99.before_ref = f32[1152,128]{1,0:T(8,128)S(1)} custom-call(f32[1152,128]{1,0:T(8,128)S(1)} %shard_map.96.phi_ref, f32[1152,128]{1,0:T(8,128)S(1)} %collective-permute-done.10.other_ref, f32[256,256]{1,0:T(8,128)S(1)} %copy-done.2, f32[256,256]{1,0:T(8,128)S(1)} %copy-done.1, f32[96,144]{1,0:T(8,128)S(1)} %copy-done.4, f32[96,144]{1,0:T(8,128)S(1)} %copy-done.3, ...), custom_call_target="tpu_custom_call" | custom-call | flops 1 | bytes 1 | tf_op jit(solution)/shard_map/pallas_call | solution.py:324
  34.1 6.8 %shard_map.101 = (f32[96,128]{1,0:T(8,128)S(1)}, f32[96,128]{1,0:T(8,128)S(1)}, f32[96,128]{1,0:T(8,128)S(1)}, f32[96,128]{1,0:T(8,128)S(1)}, f32[96,128]{1,0:T(...) custom-call(f32[1152,128]{1,0:T(8,128)S(1)} %shard_map.96.phi_ref, ...), custom_call_target="tpu_custom_call" | custom-call | flops 1 | bytes 1 | tf_op jit(solution)/shard_map/pallas_call | solution.py:324
  40.9 1.4 %collective-permute-start.14 = (f32[96,128]{1,0:T(8,128)S(1)}, f32[96,128]{1,0:T(8,128)S(1)}, u32[]{:S(2)}, u32[]{:S(2)}) collective-permute-start(f32[96,128]{1,0:T(8,128)S(1)} %get-tuple-element.60), channel_id=1, source_target_pairs={{0,8},{4,12},{8,0},{12,4},{16,24},{20,28},{24,16},{28,20},{1,9},{5... | collective-permute-start | bytes 147464 | tf_op jit(solution)/shard_map/ppermute | solution.py:345
  42.8 1.6 %collective-permute-start.11 = (f32[96,128]{1,0:T(8,128)S(1)}, f32[96,128]{1,0:T(8,128)S(1)}, u32[]{:S(2)}, u32[]{:S(2)}) collective-permute-start(f32[96,128]{1,0:T(8,128)S(1)} %get-tuple-element.56), channel_id=1, source_target_pairs={{0,16},{4,20},{8,24},{12,28},{16,0},{20,4},{24,8},{28,12},{1,17},{... | collective-permute-start | bytes 147464 | tf_op jit(solution)/shard_map/ppermute | solution.py:345
  44.5 2.3 %collective-permute-start.12 = (f32[96,128]{1,0:T(8,128)S(1)}, f32[96,128]{1,0:T(8,128)S(1)}, u32[]{:S(2)}, u32[]{:S(2)}) collective-permute-start(f32[96,128]{1,0:T(8,128)S(1)} %get-tuple-element.57), channel_id=1, source_target_pairs={{0,20},{4,16},{8,28},{12,24},{16,4},{20,0},{24,12},{28,8},{1,21},{... | collective-permute-start | bytes 147464 | tf_op jit(solution)/shard_map/ppermute | solution.py:345
  46.7 1.5 %collective-permute-start.13 = (f32[96,128]{1,0:T(8,128)S(1)}, f32[96,128]{1,0:T(8,128)S(1)}, u32[]{:S(2)}, u32[]{:S(2)}) collective-permute-start(f32[96,128]{1,0:T(8,128)S(1)} %get-tuple-element.58), channel_id=1, source_target_pairs={{0,24},{4,28},{8,16},{12,20},{16,8},{20,12},{24,0},{28,4},{1,25},{... | collective-permute-start | bytes 147464 | tf_op jit(solution)/shard_map/ppermute | solution.py:345
  48.2 2.3 %collective-permute-start.15 = (f32[96,128]{1,0:T(8,128)S(1)}, f32[96,128]{1,0:T(8,128)S(1)}, u32[]{:S(2)}, u32[]{:S(2)}) collective-permute-start(f32[96,128]{1,0:T(8,128)S(1)} %get-tuple-element.61), channel_id=1, source_target_pairs={{0,28},{4,24},{8,20},{12,16},{16,12},{20,8},{24,4},{28,0},{1,29},{... | collective-permute-start | bytes 147464 | tf_op jit(solution)/shard_map/ppermute | solution.py:345
  50.5 3.0 %collective-permute-done.12.refs_2_ = f32[96,128]{1,0:T(8,128)S(1)} collective-permute-done((f32[96,128]{1,0:T(8,128)S(1)}, f32[96,128]{1,0:T(8,128)S(1)}, u32[]{:S(2)}, u32[]{:S(2)}) %collective-permute-start.12) | collective-permute-done | bytes 49184 | tf_op jit(solution)/shard_map/ppermute | solution.py:345
  53.5 1.6 %collective-permute-done.15.refs_4_ = f32[96,128]{1,0:T(8,128)S(1)} collective-permute-done((f32[96,128]{1,0:T(8,128)S(1)}, f32[96,128]{1,0:T(8,128)S(1)}, u32[]{:S(2)}, u32[]{:S(2)}) %collective-permute-start.15) | collective-permute-done | bytes 49184 | tf_op jit(solution)/shard_map/ppermute | solution.py:345
  (40 shorter events, 4.2 us)
Async XLA Ops:
  1.8 11.8 %collective-permute-start.3 = (f32[104,128]{1,0:T(8,128)}, f32[104,128]{1,0:T(8,128)S(1)}, u32[]{:S(2)}, u32[]{:S(2)}) collective-permute-start(f32[104,128]{1,0:T(8,128)} %get-tuple-element.41), channel_id=1, source_target_pairs={{0,8},{4,12},{8,0},{12,4},{16,24},{20,28},{24,16},{28,20},{1,9},{5... | collective-permute-start | bytes 159752 | tf_op jit(solution)/shard_map/ppermute | solution.py:345
  4.9 11.1 %collective-permute-start.1 = (f32[104,128]{1,0:T(8,128)}, f32[104,128]{1,0:T(8,128)S(1)}, u32[]{:S(2)}, u32[]{:S(2)}) collective-permute-start(f32[104,128]{1,0:T(8,128)} %get-tuple-element.39), channel_id=1, source_target_pairs={{0,4},{4,0},{8,12},{12,8},{16,20},{20,16},{24,28},{28,24},{1,5},{5... | collective-permute-start | bytes 159752 | tf_op jit(solution)/shard_map/ppermute | solution.py:345
  6.4 9.5 %collective-permute-start = (f32[104,128]{1,0:T(8,128)}, f32[104,128]{1,0:T(8,128)S(1)}, u32[]{:S(2)}, u32[]{:S(2)}) collective-permute-start(f32[104,128]{1,0:T(8,128)} %get-tuple-element.38), channel_id=1, source_target_pairs={{0,16},{4,20},{8,24},{12,28},{16,0},{20,4},{24,8},{28,12},{1,17},{... | collective-permute-start | bytes 159752 | tf_op jit(solution)/shard_map/ppermute | solution.py:345
  9.0 7.0 %collective-permute-start.2 = (f32[104,128]{1,0:T(8,128)}, f32[104,128]{1,0:T(8,128)S(1)}, u32[]{:S(2)}, u32[]{:S(2)}) collective-permute-start(f32[104,128]{1,0:T(8,128)} %get-tuple-element.40), channel_id=1, source_target_pairs={{0,20},{4,16},{8,28},{12,24},{16,4},{20,0},{24,12},{28,8},{1,21},{... | collective-permute-start | bytes 159752 | tf_op jit(solution)/shard_map/ppermute | solution.py:345
  9.3 6.7 %collective-permute-start.4 = (f32[104,128]{1,0:T(8,128)}, f32[104,128]{1,0:T(8,128)S(1)}, u32[]{:S(2)}, u32[]{:S(2)}) collective-permute-start(f32[104,128]{1,0:T(8,128)} %get-tuple-element.42), channel_id=1, source_target_pairs={{0,24},{4,28},{8,16},{12,20},{16,8},{20,12},{24,0},{28,4},{1,25},{... | collective-permute-start | bytes 159752 | tf_op jit(solution)/shard_map/ppermute | solution.py:345
  13.6 7.1 %collective-permute-start.5 = (f32[104,128]{1,0:T(8,128)}, f32[104,128]{1,0:T(8,128)S(1)}, u32[]{:S(2)}, u32[]{:S(2)}) collective-permute-start(f32[104,128]{1,0:T(8,128)} %get-tuple-element.47), channel_id=1, source_target_pairs={{0,28},{4,24},{8,20},{12,16},{16,12},{20,8},{24,4},{28,0},{1,29},{... | collective-permute-start | bytes 159752 | tf_op jit(solution)/shard_map/ppermute | solution.py:345
  16.0 5.3 %collective-permute-start.6 = (f32[104,128]{1,0:T(8,128)}, f32[104,128]{1,0:T(8,128)S(1)}, u32[]{:S(2)}, u32[]{:S(2)}) collective-permute-start(f32[104,128]{1,0:T(8,128)} %get-tuple-element.51), channel_id=1, source_target_pairs={{0,12},{4,8},{8,4},{12,0},{16,28},{20,24},{24,20},{28,16},{1,13},{... | collective-permute-start | bytes 159752 | tf_op jit(solution)/shard_map/ppermute | solution.py:345
  16.0 9.0 %collective-permute-start.7 = (f32[576,128]{1,0:T(8,128)S(1)}, f32[576,128]{1,0:T(8,128)S(1)}, u32[]{:S(2)}, u32[]{:S(2)}) collective-permute-start(f32[576,128]{1,0:T(8,128)S(1)} %get-tuple-element.43.blocks_ref), channel_id=1, source_target_pairs={{0,2},{1,3},{2,0},{3,1},{4,6},{5,7},{6,4},{7,5},{8,10},{9,11},{10,... | collective-permute-start | bytes 884744 | tf_op jit(solution)/shard_map/ppermute | solution.py:361
  21.3 5.1 %collective-permute-start.8 = (f32[192,128]{1,0:T(8,128)S(1)}, f32[192,128]{1,0:T(8,128)S(1)}, u32[]{:S(2)}, u32[]{:S(2)}) collective-permute-start(f32[192,128]{1,0:T(8,128)S(1)} %get-tuple-element.52.blocks_ref), channel_id=1, source_target_pairs={{0,2},{1,3},{2,0},{3,1},{4,6},{5,7},{6,4},{7,5},{8,10},{9,11},{10,... | collective-permute-start | bytes 294920 | tf_op jit(solution)/shard_map/ppermute | solution.py:361
  25.0 5.4 %collective-permute-start.10 = (f32[1152,128]{1,0:T(8,128)S(1)}, f32[1152,128]{1,0:T(8,128)S(1)}, u32[]{:S(2)}, u32[]{:S(2)}) collective-permute-start(f32[1152,128]{1,0:T(8,128)S(1)} %shard_map.96.phi_ref), channel_id=1, source_target_pairs={{0,1},{1,0},{2,3},{3,2},{4,5},{5,4},{6,7},{7,6},{8,9},{9,8},{10,11... | collective-permute-start | bytes 1769480 | tf_op jit(solution)/shard_map/ppermute | solution.py:364
  28.5 1.9 %copy-start = (f32[2304,128]{1,0:T(8,128)S(1)}, f32[2304,128]{1,0:T(8,128)}, u32[]{:S(2)}) copy-start(f32[2304,128]{1,0:T(8,128)} %constant.20.clone.refs_4_) | copy-start | bytes 3538948
  28.6 1.9 %copy-start.1 = (f32[256,256]{1,0:T(8,128)S(1)}, f32[256,256]{1,0:T(8,128)}, u32[]{:S(2)}) copy-start(f32[256,256]{1,0:T(8,128)} %constant.15.clone.refs_1_) | copy-start | bytes 786436
  28.6 1.9 %copy-start.2 = (f32[256,256]{1,0:T(8,128)S(1)}, f32[256,256]{1,0:T(8,128)}, u32[]{:S(2)}) copy-start(f32[256,256]{1,0:T(8,128)} %constant.14.clone.refs_0_) | copy-start | bytes 786436
  28.6 1.9 %copy-start.3 = (f32[96,144]{1,0:T(8,128)S(1)}, f32[96,144]{1,0:T(8,128)}, u32[]{:S(2)}) copy-start(f32[96,144]{1,0:T(8,128)} %constant.17.clone.refs_3_) | copy-start | bytes 165892
  28.6 1.9 %copy-start.4 = (f32[96,144]{1,0:T(8,128)S(1)}, f32[96,144]{1,0:T(8,128)}, u32[]{:S(2)}) copy-start(f32[96,144]{1,0:T(8,128)} %constant.16.clone.refs_2_) | copy-start | bytes 165892
  28.6 5.5 %collective-permute-start.9 = (f32[1152,128]{1,0:T(8,128)S(1)}, f32[1152,128]{1,0:T(8,128)S(1)}, u32[]{:S(2)}, u32[]{:S(2)}) collective-permute-start(f32[1152,128]{1,0:T(8,128)S(1)} %shard_map.98.first_ref), channel_id=1, source_target_pairs={{0,1},{1,0},{2,3},{3,2},{4,5},{5,4},{6,7},{7,6},{8,9},{9,8},{10,11... | collective-permute-start | bytes 1769480 | tf_op jit(solution)/shard_map/ppermute | solution.py:364
  30.4 3.7 %copy-start.6 = (f32[96,384]{1,0:T(8,128)S(1)}, f32[96,384]{1,0:T(8,128)}, u32[]{:S(2)}) copy-start(f32[96,384]{1,0:T(8,128)} %constant.19.clone.stick_out_ref) | copy-start | bytes 442372
  40.9 7.3 %collective-permute-start.14 = (f32[96,128]{1,0:T(8,128)S(1)}, f32[96,128]{1,0:T(8,128)S(1)}, u32[]{:S(2)}, u32[]{:S(2)}) collective-permute-start(f32[96,128]{1,0:T(8,128)S(1)} %get-tuple-element.60), channel_id=1, source_target_pairs={{0,8},{4,12},{8,0},{12,4},{16,24},{20,28},{24,16},{28,20},{1,9},{5... | collective-permute-start | bytes 147464 | tf_op jit(solution)/shard_map/ppermute | solution.py:345
  42.3 8.2 %collective-permute-start.16 = (f32[96,128]{1,0:T(8,128)S(1)}, f32[96,128]{1,0:T(8,128)S(1)}, u32[]{:S(2)}, u32[]{:S(2)}) collective-permute-start(f32[96,128]{1,0:T(8,128)S(1)} %get-tuple-element.62), channel_id=1, source_target_pairs={{0,4},{4,0},{8,12},{12,8},{16,20},{20,16},{24,28},{28,24},{1,5},{5... | collective-permute-start | bytes 147464 | tf_op jit(solution)/shard_map/ppermute | solution.py:345
  42.8 7.7 %collective-permute-start.11 = (f32[96,128]{1,0:T(8,128)S(1)}, f32[96,128]{1,0:T(8,128)S(1)}, u32[]{:S(2)}, u32[]{:S(2)}) collective-permute-start(f32[96,128]{1,0:T(8,128)S(1)} %get-tuple-element.56), channel_id=1, source_target_pairs={{0,16},{4,20},{8,24},{12,28},{16,0},{20,4},{24,8},{28,12},{1,17},{... | collective-permute-start | bytes 147464 | tf_op jit(solution)/shard_map/ppermute | solution.py:345
  44.5 9.1 %collective-permute-start.12 = (f32[96,128]{1,0:T(8,128)S(1)}, f32[96,128]{1,0:T(8,128)S(1)}, u32[]{:S(2)}, u32[]{:S(2)}) collective-permute-start(f32[96,128]{1,0:T(8,128)S(1)} %get-tuple-element.57), channel_id=1, source_target_pairs={{0,20},{4,16},{8,28},{12,24},{16,4},{20,0},{24,12},{28,8},{1,21},{... | collective-permute-start | bytes 147464 | tf_op jit(solution)/shard_map/ppermute | solution.py:345
  46.7 6.8 %collective-permute-start.13 = (f32[96,128]{1,0:T(8,128)S(1)}, f32[96,128]{1,0:T(8,128)S(1)}, u32[]{:S(2)}, u32[]{:S(2)}) collective-permute-start(f32[96,128]{1,0:T(8,128)S(1)} %get-tuple-element.58), channel_id=1, source_target_pairs={{0,24},{4,28},{8,16},{12,20},{16,8},{20,12},{24,0},{28,4},{1,25},{... | collective-permute-start | bytes 147464 | tf_op jit(solution)/shard_map/ppermute | solution.py:345
  48.2 6.9 %collective-permute-start.15 = (f32[96,128]{1,0:T(8,128)S(1)}, f32[96,128]{1,0:T(8,128)S(1)}, u32[]{:S(2)}, u32[]{:S(2)}) collective-permute-start(f32[96,128]{1,0:T(8,128)S(1)} %get-tuple-element.61), channel_id=1, source_target_pairs={{0,28},{4,24},{8,20},{12,16},{16,12},{20,8},{24,4},{28,0},{1,29},{... | collective-permute-start | bytes 147464 | tf_op jit(solution)/shard_map/ppermute | solution.py:345
  50.5 5.1 %collective-permute-start.17 = (f32[96,128]{1,0:T(8,128)S(1)}, f32[96,128]{1,0:T(8,128)S(1)}, u32[]{:S(2)}, u32[]{:S(2)}) collective-permute-start(f32[96,128]{1,0:T(8,128)S(1)} %get-tuple-element.64), channel_id=1, source_target_pairs={{0,12},{4,8},{8,4},{12,0},{16,28},{20,24},{24,20},{28,16},{1,13},{... | collective-permute-start | bytes 147464 | tf_op jit(solution)/shard_map/ppermute | solution.py:345
  (2 other events, 1.8 us)

commit v18 on v17

--- a/solution.py
+++ b/solution.py
@@ -161,8 +161,7 @@
         copy.wait()
 
 
-def early_kernel(g, own_ref, tables_ref, staged_ref, stick_in_ref, left_ref):
-    staged_ref[...] = own_ref[...]
+def early_kernel(g, tables_ref, stick_in_ref, left_ref):
     stick_in_ref[...] = tables_ref[:LANES, : stick_in_ref.shape[1]].astype(BF16)
     left_ref[...] = tables_ref[LANES:, : left_ref.shape[1]].astype(BF16)
 
@@ -223,10 +222,9 @@
         store(phi_ref, y, [jnp.where(low, cos - turned(sin), turned(cos_up) - sin_up)])
 
 
-def pick_kernel(g, first_columns_ref, second_columns_ref, hot_ref):
-    columns = beside(first_columns_ref[...], second_columns_ref[...])
-    for k in range(0, columns.shape[1], LANES):
-        block = columns[:, k : k + LANES]
+def pick_kernel(g, columns_ref, hot_ref):
+    for k in range(0, columns_ref.shape[1], LANES):
+        block = columns_ref[:, k : k + LANES]
         wanted = jnp.concatenate([block] * (LANES // block.shape[0]), 0).T.astype(jnp.int32)
         for c in range(0, hot_ref.shape[1], LANES):
             index = lax.broadcasted_iota(jnp.int16, (LANES, LANES), 1)
@@ -282,7 +280,7 @@
     potentials(g, phi_ref, first_ref, second_ref, tables, work_a, work_b, emit)
 
 
-def far_kernel(g, weights, phi_ref, first_ref, second_ref, before_ref, hot_ref, stick_out_ref, *refs):
+def far_kernel(g, weights, phi_ref, first_ref, second_ref, before_ref, hot_ref, last_hot_ref, stick_out_ref, *refs):
     tables, out_refs = refs[:5], refs[5:-3]
     work_a, work_b, picked_ref = refs[-3:]
     forward = tables[2][...].astype(BF16)
@@ -307,9 +305,13 @@
         for kx in range(first, first + step, 2):
             slabs += left_complex(forward, strided(work_a, kx, g), strided(work_a, kx + 1, g))
         spectrum = beside(*split(jnp.concatenate(slabs, 0)))
-        both = dot(hot_ref[:, first * g : (first + step) * g], spectrum)
-        both = both[:, :LANES] + both[:, LANES:]
-        picked_ref[...] = both if first == 0 else picked_ref[...] + both
+        start = 0
+        for ref in (hot_ref, last_hot_ref):
+            both = dot(ref[:, first * g : (first + step) * g], spectrum)
+            both = both[:, :LANES] + both[:, LANES:]
+            rows = slice(start, start + ref.shape[0])
+            picked_ref[rows, :] = both if first == 0 else picked_ref[rows, :] + both
+            start += ref.shape[0]
 
     stick_out = stick_out_ref[...].astype(BF16)
     for k in range(0, len(out_refs), 2):
@@ -377,25 +379,21 @@
         space=pltpu.HBM,
         grant=SEND_GRANT,
     )
-    shapes = [(2 * g + 8, slots), (LANES, 6 * g), (2 * g, 3 * g)]
-    staged, *first_tables = call(
-        functools.partial(early_kernel, g),
-        [jax.ShapeDtypeStruct(shape, kind) for shape, kind in zip(shapes, (F32, BF16, BF16))],
-        [],
-        1,
-        sent[0],
-        after(t["early"], sent[0]),
-    )
     half = owners // 2
     distant, close = list(range(half, owners)), list(range(1, half))
     mixed = [distant[0]] + [d for pair in zip(close, distant[1:]) for d in pair]
-    before = {mixed[k]: (mixed[k - 3 - k % 2],) for k in range(WINDOW, len(mixed))}
-    last = mixed[WINDOW]
-    received = exchanged(sent, mixed, {**before, last: (*before[last], staged, *first_tables)})
-    received[0] = staged
+    before = {mixed[k]: (mixed[k - 2 if k % 2 else k - 5],) for k in range(WINDOW, len(mixed))}
+    received = exchanged(sent, mixed, before)
     cut = owners * 3 // 4
     order = [0] + mixed
     order = order[:cut] + order[:cut - 1:-1]
+    first_tables = call(
+        functools.partial(early_kernel, g),
+        [jax.ShapeDtypeStruct(shape, BF16) for shape in ((LANES, 6 * g), (2 * g, 3 * g))],
+        [],
+        1,
+        after(t["early"], received[distant[-2]]),
+    )
     stick_in, left_table = first_tables
 
     def relayed(part):
@@ -414,14 +412,18 @@
     first_blocks, first_columns = relayed(order[:cut])
     columns = [first_columns]
     own_grid = on_grid(first_blocks, 5 * 10**9)
-    received[order[cut]] = after(received[order[cut]], own_grid)
+
+    def hot_rows(columns):
+        shape = jax.ShapeDtypeStruct((columns.shape[1], rows), BF16)
+        return call(functools.partial(pick_kernel, g), shape, [], 1, columns)
+
+    hot = [hot_rows(first_columns)]
+    received[order[cut]] = after(received[order[cut]], own_grid, *hot)
     last_blocks, last_columns = relayed(order[cut:])
     columns.append(last_columns)
+    hot.append(hot_rows(last_columns))
     phi = orbital(own_grid, last_blocks)
     near = swapped(phi)
-    hot = call(
-        functools.partial(pick_kernel, g), jax.ShapeDtypeStruct((owners * slots, rows), BF16), [], pot_flops, *columns
-    )
     pot_tables = [t["forward"], t["last_backward"], t["left_forward"], t["left_backward"], t["coulomb"]]
 
     def potential_sum(kernel, *operands):
@@ -447,7 +449,7 @@
         first,
         second,
         total,
-        hot,
+        *hot,
         t["stick_out"],
         *pot_tables,
     )

time: 56.7 us -> 57.8 us (1.019)
  waiting for transfers between devices: 7.48 us -> 8.7 us
    ppermute x14, starting transfers between devices: 21.9 us -> 23.1 us  [exchanged(): moved[d] = lax.ppermute(block, 'stick', [(i, i ^ d) for i in range(owners)])]
    ppermute x2, waiting for transfers between devices: 0.01 us -> 0.97 us  [shifted(): lax.ppermute(x, 'band', [(i, (i - distance) % groups) for i in range(grou...]
    ppermute x2, starting transfers between devices: 3.11 us -> 2.16 us  [shifted(): lax.ppermute(x, 'band', [(i, (i - distance) % groups) for i in range(grou...]
    pallas_call x12 -> x13, Pallas kernels: 21.2 us -> 21.3 us  [call(): pl.pallas_call(kernel, out_shape=out_shapes, in_specs=[pl.BlockSpec(memor...]
  transfers between devices with their start and end apart: 18 -> 18, of which waited for: 5 -> 6; matrix products, arithmetic and copies ran while one was open for 0% -> 0% of each run, Pallas kernels for 21% -> 21%
where the time goes in v18:
time: 57.8 us; the launch traced here: 57.5 us
  starting transfers between devices  25.4 us (44%)
  Pallas kernels  21.3 us (37%)
  waiting for transfers between devices  8.7 us (15%)
  local copies, waits for them, and re-layouts  1.82 us (3%)
    ppermute x14, starting transfers between devices, exchanged(): moved[d] = lax.ppermute(block, 'stick', [(i, i ^ d) for i in range(owners)])  23.1 us
    pallas_call x13, Pallas kernels, call(): pl.pallas_call(kernel, out_shape=out_shapes, in_specs=[pl.BlockSpec(memor...  21.3 us
    ppermute x14, waiting for transfers between devices, exchanged(): moved[d] = lax.ppermute(block, 'stick', [(i, i ^ d) for i in range(owners)])  7.72 us
    ppermute x2, starting transfers between devices, shifted(): lax.ppermute(x, 'band', [(i, (i - distance) % groups) for i in range(grou...  2.16 us
    unnamed x16, local copies, waits for them, and re-layouts  1.82 us
  transfers between devices with their start and end apart: 18, of which 6 were waited for; matrix products, arithmetic and copies ran while one was open for 0% of the time, Pallas kernels for 21%

profile of v18, /device:TPU:0, one launch (start us, length us, event | category | flops | bytes accessed | tf_op | source)
XLA Modules:
  0.0 57.5 jit_solution(16840345032668963209)
XLA Ops:
  0.0 1.8 %shard_map.91 = (f32[104,128]{1,0:T(8,128)}, f32[104,128]{1,0:T(8,128)}, f32[104,128]{1,0:T(8,128)}, f32[104,128]{1,0:T(8,128)}, f32[104,128]{1,0:T(8,128)}, /*i...) custom-call(f32[8,96,128]{2,1,0:T(8,128)} %sticks_ref.1, s32[1,128]{1,0:T(1,128)} %bitcast.1), custom_call_target="tpu_custom_call" | custom-call | flops 1 | bytes 1 | tf_op jit(solution)/shard_map/pallas_call | solution.py:326
  1.8 3.0 %collective-permute-start.1 = (f32[104,128]{1,0:T(8,128)}, f32[104,128]{1,0:T(8,128)S(1)}, u32[]{:S(2)}, u32[]{:S(2)}) collective-permute-start(f32[104,128]{1,0:T(8,128)} %get-tuple-element.36), channel_id=1, source_target_pairs={{0,4},{4,0},{8,12},{12,8},{16,20},{20,16},{24,28},{28,24},{1,5},{5... | collective-permute-start | bytes 159752 | tf_op jit(solution)/shard_map/ppermute | solution.py:347
  4.8 1.6 %collective-permute-start.3 = (f32[104,128]{1,0:T(8,128)}, f32[104,128]{1,0:T(8,128)S(1)}, u32[]{:S(2)}, u32[]{:S(2)}) collective-permute-start(f32[104,128]{1,0:T(8,128)} %get-tuple-element.38), channel_id=1, source_target_pairs={{0,8},{4,12},{8,0},{12,4},{16,24},{20,28},{24,16},{28,20},{1,9},{5... | collective-permute-start | bytes 159752 | tf_op jit(solution)/shard_map/ppermute | solution.py:347
  6.4 2.5 %collective-permute-start.4 = (f32[104,128]{1,0:T(8,128)}, f32[104,128]{1,0:T(8,128)S(1)}, u32[]{:S(2)}, u32[]{:S(2)}) collective-permute-start(f32[104,128]{1,0:T(8,128)} %get-tuple-element.39), channel_id=1, source_target_pairs={{0,24},{4,28},{8,16},{12,20},{16,8},{20,12},{24,0},{28,4},{1,25},{... | collective-permute-start | bytes 159752 | tf_op jit(solution)/shard_map/ppermute | solution.py:347
  9.0 2.8 %collective-permute-start.2 = (f32[104,128]{1,0:T(8,128)}, f32[104,128]{1,0:T(8,128)S(1)}, u32[]{:S(2)}, u32[]{:S(2)}) collective-permute-start(f32[104,128]{1,0:T(8,128)} %get-tuple-element.37), channel_id=1, source_target_pairs={{0,20},{4,16},{8,28},{12,24},{16,4},{20,0},{24,12},{28,8},{1,21},{... | collective-permute-start | bytes 159752 | tf_op jit(solution)/shard_map/ppermute | solution.py:347
  11.8 2.3 %collective-permute-start.5 = (f32[104,128]{1,0:T(8,128)}, f32[104,128]{1,0:T(8,128)S(1)}, u32[]{:S(2)}, u32[]{:S(2)}) collective-permute-start(f32[104,128]{1,0:T(8,128)} %get-tuple-element.45), channel_id=1, source_target_pairs={{0,28},{4,24},{8,20},{12,16},{16,12},{20,8},{24,4},{28,0},{1,29},{... | collective-permute-start | bytes 159752 | tf_op jit(solution)/shard_map/ppermute | solution.py:347
  14.1 1.0 %copy-done.5 = f32[224,288]{1,0:T(8,128)S(1)} copy-done((f32[224,288]{1,0:T(8,128)S(1)}, f32[224,288]{1,0:T(8,128)}, u32[]{:S(2)}) %copy-start.5) | copy-done | bytes 258072
  15.1 1.3 %collective-permute-done.refs_1_ = f32[104,128]{1,0:T(8,128)S(1)} collective-permute-done((f32[104,128]{1,0:T(8,128)}, f32[104,128]{1,0:T(8,128)S(1)}, u32[]{:S(2)}, u32[]{:S(2)}) %collective-permute-start) | collective-permute-done | bytes 53280 | tf_op jit(solution)/shard_map/ppermute | solution.py:347
  16.4 1.4 %collective-permute-done.2.refs_3_ = f32[104,128]{1,0:T(8,128)S(1)} collective-permute-done((f32[104,128]{1,0:T(8,128)}, f32[104,128]{1,0:T(8,128)S(1)}, u32[]{:S(2)}, u32[]{:S(2)}) %collective-permute-start.2) | collective-permute-done | bytes 53280 | tf_op jit(solution)/shard_map/ppermute | solution.py:347
  18.6 1.6 %collective-permute-start.7 = (f32[576,128]{1,0:T(8,128)S(1)}, f32[576,128]{1,0:T(8,128)S(1)}, u32[]{:S(2)}, u32[]{:S(2)}) collective-permute-start(f32[576,128]{1,0:T(8,128)S(1)} %get-tuple-element.40.blocks_ref), channel_id=1, source_target_pairs={{0,2},{1,3},{2,0},{3,1},{4,6},{5,7},{6,4},{7,5},{8,10},{9,11},{10,... | collective-permute-start | bytes 884744 | tf_op jit(solution)/shard_map/ppermute | solution.py:363
  20.2 1.3 %shard_map.94.grid_ref = f32[2304,128]{1,0:T(8,128)S(1)} custom-call(f32[576,128]{1,0:T(8,128)S(1)} %get-tuple-element.40.blocks_ref, f32[8,768]{1,0:T(8,128)S(1)} %get-tuple-element.41.columns_ref, bf16[128,288]{1,0:T(8,128)(2,1)S(1)} %get-tuple-element.43.stick_in_ref), custom_call_target="tpu_custom_call" | custom-call | flops 5000000000 | bytes 5000000000 | tf_op jit(solution)/shard_map/pallas_call | solution.py:326
  23.1 2.1 %shard_map.97.phi_ref = f32[1152,128]{1,0:T(8,128)S(1)} custom-call(f32[2304,128]{1,0:T(8,128)S(1)} %shard_map.94.grid_ref, f32[192,128]{1,0:T(8,128)S(1)} %get-tuple-element.49.blocks_ref, f32[8,256]{1,0:T(8,128)S(1)} %get-tuple-element.50.columns_ref, bf16[128,288]{1,0:T(8,128)(2,1)S(1)} %get-tuple-element.43.stick_in_ref, ...), custom_call_target="tpu_custom_call" | custom-call | flops 1 | bytes 1 | tf_op jit(solution)/shard_map/pallas_call | solution.py:326
  25.3 1.0 %collective-permute-done.7.blocks_ref = f32[576,128]{1,0:T(8,128)S(1)} collective-permute-done((f32[576,128]{1,0:T(8,128)S(1)}, f32[576,128]{1,0:T(8,128)S(1)}, u32[]{:S(2)}, u32[]{:S(2)}) %collective-permute-start.7) | collective-permute-done | bytes 294944 | tf_op jit(solution)/shard_map/ppermute | solution.py:363
  26.3 1.3 %shard_map.98.grid_ref = f32[2304,128]{1,0:T(8,128)S(1)} custom-call(f32[576,128]{1,0:T(8,128)S(1)} %collective-permute-done.7.blocks_ref, f32[8,768]{1,0:T(8,128)S(1)} %get-tuple-element.41.columns_ref, bf16[128,288]{1,0:T(8,128)(2,1)S(1)} %get-tuple-element.43.stick_in_ref), custom_call_target="tpu_custom_call" | custom-call | flops 1 | bytes 1 | tf_op jit(solution)/shard_map/pallas_call | solution.py:326
  27.7 2.1 %shard_map.99.first_ref = f32[1152,128]{1,0:T(8,128)S(1)} custom-call(f32[2304,128]{1,0:T(8,128)S(1)} %shard_map.98.grid_ref, f32[192,128]{1,0:T(8,128)S(1)} %collective-permute-done.8.blocks_ref, f32[8,256]{1,0:T(8,128)S(1)} %get-tuple-element.50.columns_ref, bf16[128,288]{1,0:T(8,128)(2,1)S(1)} %get-tuple-element.43.stick_in_ref, ...), custom_call_target="tpu_custom_call" | custom-call | flops 1 | bytes 1 | tf_op jit(solution)/shard_map/pallas_call | solution.py:326
  30.4 3.6 %shard_map.100.before_ref = f32[1152,128]{1,0:T(8,128)S(1)} custom-call(f32[1152,128]{1,0:T(8,128)S(1)} %shard_map.97.phi_ref, f32[1152,128]{1,0:T(8,128)S(1)} %collective-permute-done.10.other_ref, f32[256,256]{1,0:T(8,128)S(1)} %copy-done.2, f32[256,256]{1,0:T(8,128)S(1)} %copy-done.1, f32[96,144]{1,0:T(8,128)S(1)} %copy-done.4, f32[96,144]{1,0:T(8,128)S(1)} %copy-done.3, ...), custom_call_target="tpu_custom_call" | custom-call | flops 1 | bytes 1 | tf_op jit(solution)/shard_map/pallas_call | solution.py:326
  34.1 6.8 %shard_map.102 = (f32[96,128]{1,0:T(8,128)S(1)}, f32[96,128]{1,0:T(8,128)S(1)}, f32[96,128]{1,0:T(8,128)S(1)}, f32[96,128]{1,0:T(8,128)S(1)}, f32[96,128]{1,0:T(...) custom-call(f32[1152,128]{1,0:T(8,128)S(1)} %shard_map.97.phi_ref, ...), custom_call_target="tpu_custom_call" | custom-call | flops 1 | bytes 1 | tf_op jit(solution)/shard_map/pallas_call | solution.py:326
  40.9 3.2 %collective-permute-start.14 = (f32[96,128]{1,0:T(8,128)S(1)}, f32[96,128]{1,0:T(8,128)S(1)}, u32[]{:S(2)}, u32[]{:S(2)}) collective-permute-start(f32[96,128]{1,0:T(8,128)S(1)} %get-tuple-element.58), channel_id=1, source_target_pairs={{0,4},{4,0},{8,12},{12,8},{16,20},{20,16},{24,28},{28,24},{1,5},{5... | collective-permute-start | bytes 147464 | tf_op jit(solution)/shard_map/ppermute | solution.py:347
  44.1 2.2 %collective-permute-start.11 = (f32[96,128]{1,0:T(8,128)S(1)}, f32[96,128]{1,0:T(8,128)S(1)}, u32[]{:S(2)}, u32[]{:S(2)}) collective-permute-start(f32[96,128]{1,0:T(8,128)S(1)} %get-tuple-element.54), channel_id=1, source_target_pairs={{0,16},{4,20},{8,24},{12,28},{16,0},{20,4},{24,8},{28,12},{1,17},{... | collective-permute-start | bytes 147464 | tf_op jit(solution)/shard_map/ppermute | solution.py:347
  46.6 1.9 %collective-permute-start.13 = (f32[96,128]{1,0:T(8,128)S(1)}, f32[96,128]{1,0:T(8,128)S(1)}, u32[]{:S(2)}, u32[]{:S(2)}) collective-permute-start(f32[96,128]{1,0:T(8,128)S(1)} %get-tuple-element.56), channel_id=1, source_target_pairs={{0,24},{4,28},{8,16},{12,20},{16,8},{20,12},{24,0},{28,4},{1,25},{... | collective-permute-start | bytes 147464 | tf_op jit(solution)/shard_map/ppermute | solution.py:347
  48.5 3.3 %collective-permute-start.15 = (f32[96,128]{1,0:T(8,128)S(1)}, f32[96,128]{1,0:T(8,128)S(1)}, u32[]{:S(2)}, u32[]{:S(2)}) collective-permute-start(f32[96,128]{1,0:T(8,128)S(1)} %get-tuple-element.59), channel_id=1, source_target_pairs={{0,28},{4,24},{8,20},{12,16},{16,12},{20,8},{24,4},{28,0},{1,29},{... | collective-permute-start | bytes 147464 | tf_op jit(solution)/shard_map/ppermute | solution.py:347
  51.7 1.5 %collective-permute-done.12.refs_2_ = f32[96,128]{1,0:T(8,128)S(1)} collective-permute-done((f32[96,128]{1,0:T(8,128)S(1)}, f32[96,128]{1,0:T(8,128)S(1)}, u32[]{:S(2)}, u32[]{:S(2)}) %collective-permute-start.12) | collective-permute-done | bytes 49184 | tf_op jit(solution)/shard_map/ppermute | solution.py:347
  53.3 2.1 %collective-permute-done.15.refs_4_ = f32[96,128]{1,0:T(8,128)S(1)} collective-permute-done((f32[96,128]{1,0:T(8,128)S(1)}, f32[96,128]{1,0:T(8,128)S(1)}, u32[]{:S(2)}, u32[]{:S(2)}) %collective-permute-start.15) | collective-permute-done | bytes 49184 | tf_op jit(solution)/shard_map/ppermute | solution.py:347
  55.3 1.4 %collective-permute-done.17.refs_7_ = f32[96,128]{1,0:T(8,128)S(1)} collective-permute-done((f32[96,128]{1,0:T(8,128)S(1)}, f32[96,128]{1,0:T(8,128)S(1)}, u32[]{:S(2)}, u32[]{:S(2)}) %collective-permute-start.17) | collective-permute-done | bytes 49184 | tf_op jit(solution)/shard_map/ppermute | solution.py:347
  (41 shorter events, 4.2 us)
Async XLA Ops:
  1.8 10.0 %collective-permute-start.1 = (f32[104,128]{1,0:T(8,128)}, f32[104,128]{1,0:T(8,128)S(1)}, u32[]{:S(2)}, u32[]{:S(2)}) collective-permute-start(f32[104,128]{1,0:T(8,128)} %get-tuple-element.36), channel_id=1, source_target_pairs={{0,4},{4,0},{8,12},{12,8},{16,20},{20,16},{24,28},{28,24},{1,5},{5... | collective-permute-start | bytes 159752 | tf_op jit(solution)/shard_map/ppermute | solution.py:347
  4.8 9.2 %collective-permute-start.3 = (f32[104,128]{1,0:T(8,128)}, f32[104,128]{1,0:T(8,128)S(1)}, u32[]{:S(2)}, u32[]{:S(2)}) collective-permute-start(f32[104,128]{1,0:T(8,128)} %get-tuple-element.38), channel_id=1, source_target_pairs={{0,8},{4,12},{8,0},{12,4},{16,24},{20,28},{24,16},{28,20},{1,9},{5... | collective-permute-start | bytes 159752 | tf_op jit(solution)/shard_map/ppermute | solution.py:347
  6.4 7.7 %collective-permute-start.4 = (f32[104,128]{1,0:T(8,128)}, f32[104,128]{1,0:T(8,128)S(1)}, u32[]{:S(2)}, u32[]{:S(2)}) collective-permute-start(f32[104,128]{1,0:T(8,128)} %get-tuple-element.39), channel_id=1, source_target_pairs={{0,24},{4,28},{8,16},{12,20},{16,8},{20,12},{24,0},{28,4},{1,25},{... | collective-permute-start | bytes 159752 | tf_op jit(solution)/shard_map/ppermute | solution.py:347
  8.9 7.5 %collective-permute-start = (f32[104,128]{1,0:T(8,128)}, f32[104,128]{1,0:T(8,128)S(1)}, u32[]{:S(2)}, u32[]{:S(2)}) collective-permute-start(f32[104,128]{1,0:T(8,128)} %get-tuple-element.35), channel_id=1, source_target_pairs={{0,16},{4,20},{8,24},{12,28},{16,0},{20,4},{24,8},{28,12},{1,17},{... | collective-permute-start | bytes 159752 | tf_op jit(solution)/shard_map/ppermute | solution.py:347
  9.0 8.8 %collective-permute-start.2 = (f32[104,128]{1,0:T(8,128)}, f32[104,128]{1,0:T(8,128)S(1)}, u32[]{:S(2)}, u32[]{:S(2)}) collective-permute-start(f32[104,128]{1,0:T(8,128)} %get-tuple-element.37), channel_id=1, source_target_pairs={{0,20},{4,16},{8,28},{12,24},{16,4},{20,0},{24,12},{28,8},{1,21},{... | collective-permute-start | bytes 159752 | tf_op jit(solution)/shard_map/ppermute | solution.py:347
  11.8 10.7 %collective-permute-start.5 = (f32[104,128]{1,0:T(8,128)}, f32[104,128]{1,0:T(8,128)S(1)}, u32[]{:S(2)}, u32[]{:S(2)}) collective-permute-start(f32[104,128]{1,0:T(8,128)} %get-tuple-element.45), channel_id=1, source_target_pairs={{0,28},{4,24},{8,20},{12,16},{16,12},{20,8},{24,4},{28,0},{1,29},{... | collective-permute-start | bytes 159752 | tf_op jit(solution)/shard_map/ppermute | solution.py:347
  14.1 8.4 %collective-permute-start.6 = (f32[104,128]{1,0:T(8,128)}, f32[104,128]{1,0:T(8,128)S(1)}, u32[]{:S(2)}, u32[]{:S(2)}) collective-permute-start(f32[104,128]{1,0:T(8,128)} %get-tuple-element.48), channel_id=1, source_target_pairs={{0,12},{4,8},{8,4},{12,0},{16,28},{20,24},{24,20},{28,16},{1,13},{... | collective-permute-start | bytes 159752 | tf_op jit(solution)/shard_map/ppermute | solution.py:347
  18.6 7.7 %collective-permute-start.7 = (f32[576,128]{1,0:T(8,128)S(1)}, f32[576,128]{1,0:T(8,128)S(1)}, u32[]{:S(2)}, u32[]{:S(2)}) collective-permute-start(f32[576,128]{1,0:T(8,128)S(1)} %get-tuple-element.40.blocks_ref), channel_id=1, source_target_pairs={{0,2},{1,3},{2,0},{3,1},{4,6},{5,7},{6,4},{7,5},{8,10},{9,11},{10,... | collective-permute-start | bytes 884744 | tf_op jit(solution)/shard_map/ppermute | solution.py:363
  22.5 5.2 %collective-permute-start.8 = (f32[192,128]{1,0:T(8,128)S(1)}, f32[192,128]{1,0:T(8,128)S(1)}, u32[]{:S(2)}, u32[]{:S(2)}) collective-permute-start(f32[192,128]{1,0:T(8,128)S(1)} %get-tuple-element.49.blocks_ref), channel_id=1, source_target_pairs={{0,2},{1,3},{2,0},{3,1},{4,6},{5,7},{6,4},{7,5},{8,10},{9,11},{10,... | collective-permute-start | bytes 294920 | tf_op jit(solution)/shard_map/ppermute | solution.py:363
  25.3 5.1 %collective-permute-start.10 = (f32[1152,128]{1,0:T(8,128)S(1)}, f32[1152,128]{1,0:T(8,128)S(1)}, u32[]{:S(2)}, u32[]{:S(2)}) collective-permute-start(f32[1152,128]{1,0:T(8,128)S(1)} %shard_map.97.phi_ref), channel_id=1, source_target_pairs={{0,1},{1,0},{2,3},{3,2},{4,5},{5,4},{6,7},{7,6},{8,9},{9,8},{10,11... | collective-permute-start | bytes 1769480 | tf_op jit(solution)/shard_map/ppermute | solution.py:366
  27.7 2.7 %copy-start = (f32[2304,128]{1,0:T(8,128)S(1)}, f32[2304,128]{1,0:T(8,128)}, u32[]{:S(2)}) copy-start(f32[2304,128]{1,0:T(8,128)} %constant.20.clone.refs_4_) | copy-start | bytes 3538948
  27.7 2.7 %copy-start.1 = (f32[256,256]{1,0:T(8,128)S(1)}, f32[256,256]{1,0:T(8,128)}, u32[]{:S(2)}) copy-start(f32[256,256]{1,0:T(8,128)} %constant.15.clone.refs_1_) | copy-start | bytes 786436
  27.7 2.7 %copy-start.2 = (f32[256,256]{1,0:T(8,128)S(1)}, f32[256,256]{1,0:T(8,128)}, u32[]{:S(2)}) copy-start(f32[256,256]{1,0:T(8,128)} %constant.14.clone.refs_0_) | copy-start | bytes 786436
  27.7 2.7 %copy-start.3 = (f32[96,144]{1,0:T(8,128)S(1)}, f32[96,144]{1,0:T(8,128)}, u32[]{:S(2)}) copy-start(f32[96,144]{1,0:T(8,128)} %constant.17.clone.refs_3_) | copy-start | bytes 165892
  27.7 2.7 %copy-start.4 = (f32[96,144]{1,0:T(8,128)S(1)}, f32[96,144]{1,0:T(8,128)}, u32[]{:S(2)}) copy-start(f32[96,144]{1,0:T(8,128)} %constant.16.clone.refs_2_) | copy-start | bytes 165892
  29.9 4.2 %collective-permute-start.9 = (f32[1152,128]{1,0:T(8,128)S(1)}, f32[1152,128]{1,0:T(8,128)S(1)}, u32[]{:S(2)}, u32[]{:S(2)}) collective-permute-start(f32[1152,128]{1,0:T(8,128)S(1)} %shard_map.99.first_ref), channel_id=1, source_target_pairs={{0,1},{1,0},{2,3},{3,2},{4,5},{5,4},{6,7},{7,6},{8,9},{9,8},{10,11... | collective-permute-start | bytes 1769480 | tf_op jit(solution)/shard_map/ppermute | solution.py:366
  30.3 3.7 %copy-start.6 = (f32[96,384]{1,0:T(8,128)S(1)}, f32[96,384]{1,0:T(8,128)}, u32[]{:S(2)}) copy-start(f32[96,384]{1,0:T(8,128)} %constant.19.clone.stick_out_ref) | copy-start | bytes 442372
  40.9 7.6 %collective-permute-start.14 = (f32[96,128]{1,0:T(8,128)S(1)}, f32[96,128]{1,0:T(8,128)S(1)}, u32[]{:S(2)}, u32[]{:S(2)}) collective-permute-start(f32[96,128]{1,0:T(8,128)S(1)} %get-tuple-element.58), channel_id=1, source_target_pairs={{0,4},{4,0},{8,12},{12,8},{16,20},{20,16},{24,28},{28,24},{1,5},{5... | collective-permute-start | bytes 147464 | tf_op jit(solution)/shard_map/ppermute | solution.py:347
  44.1 7.7 %collective-permute-start.16 = (f32[96,128]{1,0:T(8,128)S(1)}, f32[96,128]{1,0:T(8,128)S(1)}, u32[]{:S(2)}, u32[]{:S(2)}) collective-permute-start(f32[96,128]{1,0:T(8,128)S(1)} %get-tuple-element.60), channel_id=1, source_target_pairs={{0,8},{4,12},{8,0},{12,4},{16,24},{20,28},{24,16},{28,20},{1,9},{5... | collective-permute-start | bytes 147464 | tf_op jit(solution)/shard_map/ppermute | solution.py:347
  44.1 7.7 %collective-permute-start.11 = (f32[96,128]{1,0:T(8,128)S(1)}, f32[96,128]{1,0:T(8,128)S(1)}, u32[]{:S(2)}, u32[]{:S(2)}) collective-permute-start(f32[96,128]{1,0:T(8,128)S(1)} %get-tuple-element.54), channel_id=1, source_target_pairs={{0,16},{4,20},{8,24},{12,28},{16,0},{20,4},{24,8},{28,12},{1,17},{... | collective-permute-start | bytes 147464 | tf_op jit(solution)/shard_map/ppermute | solution.py:347
  46.3 7.0 %collective-permute-start.12 = (f32[96,128]{1,0:T(8,128)S(1)}, f32[96,128]{1,0:T(8,128)S(1)}, u32[]{:S(2)}, u32[]{:S(2)}) collective-permute-start(f32[96,128]{1,0:T(8,128)S(1)} %get-tuple-element.55), channel_id=1, source_target_pairs={{0,20},{4,16},{8,28},{12,24},{16,4},{20,0},{24,12},{28,8},{1,21},{... | collective-permute-start | bytes 147464 | tf_op jit(solution)/shard_map/ppermute | solution.py:347
  46.6 6.7 %collective-permute-start.13 = (f32[96,128]{1,0:T(8,128)S(1)}, f32[96,128]{1,0:T(8,128)S(1)}, u32[]{:S(2)}, u32[]{:S(2)}) collective-permute-start(f32[96,128]{1,0:T(8,128)S(1)} %get-tuple-element.56), channel_id=1, source_target_pairs={{0,24},{4,28},{8,16},{12,20},{16,8},{20,12},{24,0},{28,4},{1,25},{... | collective-permute-start | bytes 147464 | tf_op jit(solution)/shard_map/ppermute | solution.py:347
  48.5 6.9 %collective-permute-start.15 = (f32[96,128]{1,0:T(8,128)S(1)}, f32[96,128]{1,0:T(8,128)S(1)}, u32[]{:S(2)}, u32[]{:S(2)}) collective-permute-start(f32[96,128]{1,0:T(8,128)S(1)} %get-tuple-element.59), channel_id=1, source_target_pairs={{0,28},{4,24},{8,20},{12,16},{16,12},{20,8},{24,4},{28,0},{1,29},{... | collective-permute-start | bytes 147464 | tf_op jit(solution)/shard_map/ppermute | solution.py:347
  51.7 5.0 %collective-permute-start.17 = (f32[96,128]{1,0:T(8,128)S(1)}, f32[96,128]{1,0:T(8,128)S(1)}, u32[]{:S(2)}, u32[]{:S(2)}) collective-permute-start(f32[96,128]{1,0:T(8,128)S(1)} %get-tuple-element.62), channel_id=1, source_target_pairs={{0,12},{4,8},{8,4},{12,0},{16,28},{20,24},{24,20},{28,16},{1,13},{... | collective-permute-start | bytes 147464 | tf_op jit(solution)/shard_map/ppermute | solution.py:347
  (2 other events, 1.8 us)

commit v19 on v18

--- a/solution.py
+++ b/solution.py
@@ -161,7 +161,8 @@
         copy.wait()
 
 
-def early_kernel(g, tables_ref, stick_in_ref, left_ref):
+def early_kernel(g, own_ref, tables_ref, staged_ref, stick_in_ref, left_ref):
+    staged_ref[...] = own_ref[...]
     stick_in_ref[...] = tables_ref[:LANES, : stick_in_ref.shape[1]].astype(BF16)
     left_ref[...] = tables_ref[LANES:, : left_ref.shape[1]].astype(BF16)
 
@@ -379,21 +380,25 @@
         space=pltpu.HBM,
         grant=SEND_GRANT,
     )
+    shapes = [(2 * g + 8, slots), (LANES, 6 * g), (2 * g, 3 * g)]
+    staged, *first_tables = call(
+        functools.partial(early_kernel, g),
+        [jax.ShapeDtypeStruct(shape, kind) for shape, kind in zip(shapes, (F32, BF16, BF16))],
+        [],
+        1,
+        sent[0],
+        after(t["early"], sent[0]),
+    )
     half = owners // 2
     distant, close = list(range(half, owners)), list(range(1, half))
     mixed = [distant[0]] + [d for pair in zip(close, distant[1:]) for d in pair]
-    before = {mixed[k]: (mixed[k - 2 if k % 2 else k - 5],) for k in range(WINDOW, len(mixed))}
-    received = exchanged(sent, mixed, before)
+    before = {mixed[k]: (mixed[k - 3 - k % 2],) for k in range(WINDOW, len(mixed))}
+    last = mixed[WINDOW]
+    received = exchanged(sent, mixed, {**before, last: (*before[last], staged, *first_tables)})
+    received[0] = staged
     cut = owners * 3 // 4
     order = [0] + mixed
     order = order[:cut] + order[:cut - 1:-1]
-    first_tables = call(
-        functools.partial(early_kernel, g),
-        [jax.ShapeDtypeStruct(shape, BF16) for shape in ((LANES, 6 * g), (2 * g, 3 * g))],
-        [],
-        1,
-        after(t["early"], received[distant[-2]]),
-    )
     stick_in, left_table = first_tables
 
     def relayed(part):

time: 57.8 us -> 55.8 us (0.965)
  waiting for transfers between devices: 8.7 us -> 6.53 us
    ppermute x14, starting transfers between devices: 23.1 us -> 21.9 us  [exchanged(): moved[d] = lax.ppermute(block, 'stick', [(i, i ^ d) for i in range(owners)])]
    ppermute x14, waiting for transfers between devices: 7.72 us -> 6.52 us  [exchanged(): moved[d] = lax.ppermute(block, 'stick', [(i, i ^ d) for i in range(owners)])]
    ppermute x2, waiting for transfers between devices: 0.97 us -> 0.01 us  [shifted(): lax.ppermute(x, 'band', [(i, (i - distance) % groups) for i in range(grou...]
    ppermute x2, starting transfers between devices: 2.16 us -> 3.11 us  [shifted(): lax.ppermute(x, 'band', [(i, (i - distance) % groups) for i in range(grou...]
  transfers between devices with their start and end apart: 18 -> 18, of which waited for: 6 -> 5; matrix products, arithmetic and copies ran while one was open for 0% -> 0% of each run, Pallas kernels for 21% -> 21%
where the time goes in v19:
time: 55.8 us; the launch traced here: 55.5 us
  starting transfers between devices  25.6 us (46%)
  Pallas kernels  21.3 us (38%)
  waiting for transfers between devices  6.53 us (12%)
  local copies, waits for them, and re-layouts  1.83 us (3%)
    ppermute x14, starting transfers between devices, exchanged(): moved[d] = lax.ppermute(block, 'stick', [(i, i ^ d) for i in range(owners)])  21.9 us
    pallas_call x13, Pallas kernels, call(): pl.pallas_call(kernel, out_shape=out_shapes, in_specs=[pl.BlockSpec(memor...  21.3 us
    ppermute x14, waiting for transfers between devices, exchanged(): moved[d] = lax.ppermute(block, 'stick', [(i, i ^ d) for i in range(owners)])  6.52 us
    ppermute x2, starting transfers between devices, shifted(): lax.ppermute(x, 'band', [(i, (i - distance) % groups) for i in range(grou...  3.11 us
    unnamed x16, local copies, waits for them, and re-layouts  1.83 us
  transfers between devices with their start and end apart: 18, of which 5 were waited for; matrix products, arithmetic and copies ran while one was open for 0% of the time, Pallas kernels for 21%

profile of v19, /device:TPU:0, one launch (start us, length us, event | category | flops | bytes accessed | tf_op | source)
XLA Modules:
  0.0 55.5 jit_solution(14343455627420890830)
XLA Ops:
  0.0 1.8 %shard_map.91 = (f32[104,128]{1,0:T(8,128)}, f32[104,128]{1,0:T(8,128)}, f32[104,128]{1,0:T(8,128)}, f32[104,128]{1,0:T(8,128)}, f32[104,128]{1,0:T(8,128)}, /*i...) custom-call(f32[8,96,128]{2,1,0:T(8,128)} %sticks_ref.1, s32[1,128]{1,0:T(1,128)} %bitcast.1), custom_call_target="tpu_custom_call" | custom-call | flops 1 | bytes 1 | tf_op jit(solution)/shard_map/pallas_call | solution.py:327
  1.8 3.1 %collective-permute-start.3 = (f32[104,128]{1,0:T(8,128)}, f32[104,128]{1,0:T(8,128)S(1)}, u32[]{:S(2)}, u32[]{:S(2)}) collective-permute-start(f32[104,128]{1,0:T(8,128)} %get-tuple-element.41), channel_id=1, source_target_pairs={{0,8},{4,12},{8,0},{12,4},{16,24},{20,28},{24,16},{28,20},{1,9},{5... | collective-permute-start | bytes 159752 | tf_op jit(solution)/shard_map/ppermute | solution.py:348
  4.9 1.5 %collective-permute-start.1 = (f32[104,128]{1,0:T(8,128)}, f32[104,128]{1,0:T(8,128)S(1)}, u32[]{:S(2)}, u32[]{:S(2)}) collective-permute-start(f32[104,128]{1,0:T(8,128)} %get-tuple-element.39), channel_id=1, source_target_pairs={{0,4},{4,0},{8,12},{12,8},{16,20},{20,16},{24,28},{28,24},{1,5},{5... | collective-permute-start | bytes 159752 | tf_op jit(solution)/shard_map/ppermute | solution.py:348
  6.4 2.6 %collective-permute-start = (f32[104,128]{1,0:T(8,128)}, f32[104,128]{1,0:T(8,128)S(1)}, u32[]{:S(2)}, u32[]{:S(2)}) collective-permute-start(f32[104,128]{1,0:T(8,128)} %get-tuple-element.38), channel_id=1, source_target_pairs={{0,16},{4,20},{8,24},{12,28},{16,0},{20,4},{24,8},{28,12},{1,17},{... | collective-permute-start | bytes 159752 | tf_op jit(solution)/shard_map/ppermute | solution.py:348
  9.3 2.5 %collective-permute-start.4 = (f32[104,128]{1,0:T(8,128)}, f32[104,128]{1,0:T(8,128)S(1)}, u32[]{:S(2)}, u32[]{:S(2)}) collective-permute-start(f32[104,128]{1,0:T(8,128)} %get-tuple-element.42), channel_id=1, source_target_pairs={{0,24},{4,28},{8,16},{12,20},{16,8},{20,12},{24,0},{28,4},{1,25},{... | collective-permute-start | bytes 159752 | tf_op jit(solution)/shard_map/ppermute | solution.py:348
  11.8 1.0 %copy-done.5 = f32[224,288]{1,0:T(8,128)S(1)} copy-done((f32[224,288]{1,0:T(8,128)S(1)}, f32[224,288]{1,0:T(8,128)}, u32[]{:S(2)}) %copy-start.5) | copy-done | bytes 258072
  13.6 2.4 %collective-permute-start.5 = (f32[104,128]{1,0:T(8,128)}, f32[104,128]{1,0:T(8,128)S(1)}, u32[]{:S(2)}, u32[]{:S(2)}) collective-permute-start(f32[104,128]{1,0:T(8,128)} %get-tuple-element.47), channel_id=1, source_target_pairs={{0,28},{4,24},{8,20},{12,16},{16,12},{20,8},{24,4},{28,0},{1,29},{... | collective-permute-start | bytes 159752 | tf_op jit(solution)/shard_map/ppermute | solution.py:348
  16.0 1.6 %collective-permute-start.7 = (f32[576,128]{1,0:T(8,128)S(1)}, f32[576,128]{1,0:T(8,128)S(1)}, u32[]{:S(2)}, u32[]{:S(2)}) collective-permute-start(f32[576,128]{1,0:T(8,128)S(1)} %get-tuple-element.43.blocks_ref), channel_id=1, source_target_pairs={{0,2},{1,3},{2,0},{3,1},{4,6},{5,7},{6,4},{7,5},{8,10},{9,11},{10,... | collective-permute-start | bytes 884744 | tf_op jit(solution)/shard_map/ppermute | solution.py:364
  17.6 1.3 %shard_map.94.grid_ref = f32[2304,128]{1,0:T(8,128)S(1)} custom-call(f32[576,128]{1,0:T(8,128)S(1)} %get-tuple-element.43.blocks_ref, f32[8,768]{1,0:T(8,128)S(1)} %get-tuple-element.44.columns_ref, bf16[128,288]{1,0:T(8,128)(2,1)S(1)} %get-tuple-element.45.stick_in_ref), custom_call_target="tpu_custom_call" | custom-call | flops 5000000000 | bytes 5000000000 | tf_op jit(solution)/shard_map/pallas_call | solution.py:327
  18.9 0.9 %shard_map.95.hot_ref = bf16[768,2304]{1,0:T(8,128)(2,1)S(1)} custom-call(f32[8,768]{1,0:T(8,128)S(1)} %get-tuple-element.44.columns_ref), custom_call_target="tpu_custom_call" | custom-call | flops 1 | bytes 1 | tf_op jit(solution)/shard_map/pallas_call | solution.py:327
  19.9 0.8 %collective-permute-done.5.refs_0_ = f32[104,128]{1,0:T(8,128)S(1)} collective-permute-done((f32[104,128]{1,0:T(8,128)}, f32[104,128]{1,0:T(8,128)S(1)}, u32[]{:S(2)}, u32[]{:S(2)}) %collective-permute-start.5) | collective-permute-done | bytes 53280 | tf_op jit(solution)/shard_map/ppermute | solution.py:348
  21.3 1.6 %collective-permute-start.8 = (f32[192,128]{1,0:T(8,128)S(1)}, f32[192,128]{1,0:T(8,128)S(1)}, u32[]{:S(2)}, u32[]{:S(2)}) collective-permute-start(f32[192,128]{1,0:T(8,128)S(1)} %get-tuple-element.52.blocks_ref), channel_id=1, source_target_pairs={{0,2},{1,3},{2,0},{3,1},{4,6},{5,7},{6,4},{7,5},{8,10},{9,11},{10,... | collective-permute-start | bytes 294920 | tf_op jit(solution)/shard_map/ppermute | solution.py:364
  22.8 2.1 %shard_map.97.phi_ref = f32[1152,128]{1,0:T(8,128)S(1)} custom-call(f32[2304,128]{1,0:T(8,128)S(1)} %shard_map.94.grid_ref, f32[192,128]{1,0:T(8,128)S(1)} %get-tuple-element.52.blocks_ref, f32[8,256]{1,0:T(8,128)S(1)} %get-tuple-element.53.columns_ref, bf16[128,288]{1,0:T(8,128)(2,1)S(1)} %get-tuple-element.45.stick_in_ref, ...), custom_call_target="tpu_custom_call" | custom-call | flops 1 | bytes 1 | tf_op jit(solution)/shard_map/pallas_call | solution.py:327
  25.1 1.3 %shard_map.98.grid_ref = f32[2304,128]{1,0:T(8,128)S(1)} custom-call(f32[576,128]{1,0:T(8,128)S(1)} %collective-permute-done.7.blocks_ref, f32[8,768]{1,0:T(8,128)S(1)} %get-tuple-element.44.columns_ref, bf16[128,288]{1,0:T(8,128)(2,1)S(1)} %get-tuple-element.45.stick_in_ref), custom_call_target="tpu_custom_call" | custom-call | flops 1 | bytes 1 | tf_op jit(solution)/shard_map/pallas_call | solution.py:327
  26.5 2.1 %shard_map.99.first_ref = f32[1152,128]{1,0:T(8,128)S(1)} custom-call(f32[2304,128]{1,0:T(8,128)S(1)} %shard_map.98.grid_ref, f32[192,128]{1,0:T(8,128)S(1)} %collective-permute-done.8.blocks_ref, f32[8,256]{1,0:T(8,128)S(1)} %get-tuple-element.53.columns_ref, bf16[128,288]{1,0:T(8,128)(2,1)S(1)} %get-tuple-element.45.stick_in_ref, ...), custom_call_target="tpu_custom_call" | custom-call | flops 1 | bytes 1 | tf_op jit(solution)/shard_map/pallas_call | solution.py:327
  29.6 3.6 %shard_map.100.before_ref = f32[1152,128]{1,0:T(8,128)S(1)} custom-call(f32[1152,128]{1,0:T(8,128)S(1)} %shard_map.97.phi_ref, f32[1152,128]{1,0:T(8,128)S(1)} %collective-permute-done.10.other_ref, f32[256,256]{1,0:T(8,128)S(1)} %copy-done.2, f32[256,256]{1,0:T(8,128)S(1)} %copy-done.1, f32[96,144]{1,0:T(8,128)S(1)} %copy-done.4, f32[96,144]{1,0:T(8,128)S(1)} %copy-done.3, ...), custom_call_target="tpu_custom_call" | custom-call | flops 1 | bytes 1 | tf_op jit(solution)/shard_map/pallas_call | solution.py:327
  33.3 6.8 %shard_map.102 = (f32[96,128]{1,0:T(8,128)S(1)}, f32[96,128]{1,0:T(8,128)S(1)}, f32[96,128]{1,0:T(8,128)S(1)}, f32[96,128]{1,0:T(8,128)S(1)}, f32[96,128]{1,0:T(...) custom-call(f32[1152,128]{1,0:T(8,128)S(1)} %shard_map.97.phi_ref, ...), custom_call_target="tpu_custom_call" | custom-call | flops 1 | bytes 1 | tf_op jit(solution)/shard_map/pallas_call | solution.py:327
  40.1 1.4 %collective-permute-start.14 = (f32[96,128]{1,0:T(8,128)S(1)}, f32[96,128]{1,0:T(8,128)S(1)}, u32[]{:S(2)}, u32[]{:S(2)}) collective-permute-start(f32[96,128]{1,0:T(8,128)S(1)} %get-tuple-element.60), channel_id=1, source_target_pairs={{0,8},{4,12},{8,0},{12,4},{16,24},{20,28},{24,16},{28,20},{1,9},{5... | collective-permute-start | bytes 147464 | tf_op jit(solution)/shard_map/ppermute | solution.py:348
  42.0 1.6 %collective-permute-start.11 = (f32[96,128]{1,0:T(8,128)S(1)}, f32[96,128]{1,0:T(8,128)S(1)}, u32[]{:S(2)}, u32[]{:S(2)}) collective-permute-start(f32[96,128]{1,0:T(8,128)S(1)} %get-tuple-element.56), channel_id=1, source_target_pairs={{0,16},{4,20},{8,24},{12,28},{16,0},{20,4},{24,8},{28,12},{1,17},{... | collective-permute-start | bytes 147464 | tf_op jit(solution)/shard_map/ppermute | solution.py:348
  43.6 2.3 %collective-permute-start.12 = (f32[96,128]{1,0:T(8,128)S(1)}, f32[96,128]{1,0:T(8,128)S(1)}, u32[]{:S(2)}, u32[]{:S(2)}) collective-permute-start(f32[96,128]{1,0:T(8,128)S(1)} %get-tuple-element.57), channel_id=1, source_target_pairs={{0,20},{4,16},{8,28},{12,24},{16,4},{20,0},{24,12},{28,8},{1,21},{... | collective-permute-start | bytes 147464 | tf_op jit(solution)/shard_map/ppermute | solution.py:348
  45.9 1.5 %collective-permute-start.13 = (f32[96,128]{1,0:T(8,128)S(1)}, f32[96,128]{1,0:T(8,128)S(1)}, u32[]{:S(2)}, u32[]{:S(2)}) collective-permute-start(f32[96,128]{1,0:T(8,128)S(1)} %get-tuple-element.58), channel_id=1, source_target_pairs={{0,24},{4,28},{8,16},{12,20},{16,8},{20,12},{24,0},{28,4},{1,25},{... | collective-permute-start | bytes 147464 | tf_op jit(solution)/shard_map/ppermute | solution.py:348
  47.3 2.3 %collective-permute-start.15 = (f32[96,128]{1,0:T(8,128)S(1)}, f32[96,128]{1,0:T(8,128)S(1)}, u32[]{:S(2)}, u32[]{:S(2)}) collective-permute-start(f32[96,128]{1,0:T(8,128)S(1)} %get-tuple-element.61), channel_id=1, source_target_pairs={{0,28},{4,24},{8,20},{12,16},{16,12},{20,8},{24,4},{28,0},{1,29},{... | collective-permute-start | bytes 147464 | tf_op jit(solution)/shard_map/ppermute | solution.py:348
  49.7 3.0 %collective-permute-done.12.refs_2_ = f32[96,128]{1,0:T(8,128)S(1)} collective-permute-done((f32[96,128]{1,0:T(8,128)S(1)}, f32[96,128]{1,0:T(8,128)S(1)}, u32[]{:S(2)}, u32[]{:S(2)}) %collective-permute-start.12) | collective-permute-done | bytes 49184 | tf_op jit(solution)/shard_map/ppermute | solution.py:348
  52.7 1.6 %collective-permute-done.15.refs_4_ = f32[96,128]{1,0:T(8,128)S(1)} collective-permute-done((f32[96,128]{1,0:T(8,128)S(1)}, f32[96,128]{1,0:T(8,128)S(1)}, u32[]{:S(2)}, u32[]{:S(2)}) %collective-permute-start.15) | collective-permute-done | bytes 49184 | tf_op jit(solution)/shard_map/ppermute | solution.py:348
  (41 shorter events, 4.6 us)
Async XLA Ops:
  1.8 11.8 %collective-permute-start.3 = (f32[104,128]{1,0:T(8,128)}, f32[104,128]{1,0:T(8,128)S(1)}, u32[]{:S(2)}, u32[]{:S(2)}) collective-permute-start(f32[104,128]{1,0:T(8,128)} %get-tuple-element.41), channel_id=1, source_target_pairs={{0,8},{4,12},{8,0},{12,4},{16,24},{20,28},{24,16},{28,20},{1,9},{5... | collective-permute-start | bytes 159752 | tf_op jit(solution)/shard_map/ppermute | solution.py:348
  4.9 11.1 %collective-permute-start.1 = (f32[104,128]{1,0:T(8,128)}, f32[104,128]{1,0:T(8,128)S(1)}, u32[]{:S(2)}, u32[]{:S(2)}) collective-permute-start(f32[104,128]{1,0:T(8,128)} %get-tuple-element.39), channel_id=1, source_target_pairs={{0,4},{4,0},{8,12},{12,8},{16,20},{20,16},{24,28},{28,24},{1,5},{5... | collective-permute-start | bytes 159752 | tf_op jit(solution)/shard_map/ppermute | solution.py:348
  6.4 9.5 %collective-permute-start = (f32[104,128]{1,0:T(8,128)}, f32[104,128]{1,0:T(8,128)S(1)}, u32[]{:S(2)}, u32[]{:S(2)}) collective-permute-start(f32[104,128]{1,0:T(8,128)} %get-tuple-element.38), channel_id=1, source_target_pairs={{0,16},{4,20},{8,24},{12,28},{16,0},{20,4},{24,8},{28,12},{1,17},{... | collective-permute-start | bytes 159752 | tf_op jit(solution)/shard_map/ppermute | solution.py:348
  9.0 7.0 %collective-permute-start.2 = (f32[104,128]{1,0:T(8,128)}, f32[104,128]{1,0:T(8,128)S(1)}, u32[]{:S(2)}, u32[]{:S(2)}) collective-permute-start(f32[104,128]{1,0:T(8,128)} %get-tuple-element.40), channel_id=1, source_target_pairs={{0,20},{4,16},{8,28},{12,24},{16,4},{20,0},{24,12},{28,8},{1,21},{... | collective-permute-start | bytes 159752 | tf_op jit(solution)/shard_map/ppermute | solution.py:348
  9.3 6.7 %collective-permute-start.4 = (f32[104,128]{1,0:T(8,128)}, f32[104,128]{1,0:T(8,128)S(1)}, u32[]{:S(2)}, u32[]{:S(2)}) collective-permute-start(f32[104,128]{1,0:T(8,128)} %get-tuple-element.42), channel_id=1, source_target_pairs={{0,24},{4,28},{8,16},{12,20},{16,8},{20,12},{24,0},{28,4},{1,25},{... | collective-permute-start | bytes 159752 | tf_op jit(solution)/shard_map/ppermute | solution.py:348
  13.6 7.1 %collective-permute-start.5 = (f32[104,128]{1,0:T(8,128)}, f32[104,128]{1,0:T(8,128)S(1)}, u32[]{:S(2)}, u32[]{:S(2)}) collective-permute-start(f32[104,128]{1,0:T(8,128)} %get-tuple-element.47), channel_id=1, source_target_pairs={{0,28},{4,24},{8,20},{12,16},{16,12},{20,8},{24,4},{28,0},{1,29},{... | collective-permute-start | bytes 159752 | tf_op jit(solution)/shard_map/ppermute | solution.py:348
  16.0 5.3 %collective-permute-start.6 = (f32[104,128]{1,0:T(8,128)}, f32[104,128]{1,0:T(8,128)S(1)}, u32[]{:S(2)}, u32[]{:S(2)}) collective-permute-start(f32[104,128]{1,0:T(8,128)} %get-tuple-element.51), channel_id=1, source_target_pairs={{0,12},{4,8},{8,4},{12,0},{16,28},{20,24},{24,20},{28,16},{1,13},{... | collective-permute-start | bytes 159752 | tf_op jit(solution)/shard_map/ppermute | solution.py:348
  16.0 9.0 %collective-permute-start.7 = (f32[576,128]{1,0:T(8,128)S(1)}, f32[576,128]{1,0:T(8,128)S(1)}, u32[]{:S(2)}, u32[]{:S(2)}) collective-permute-start(f32[576,128]{1,0:T(8,128)S(1)} %get-tuple-element.43.blocks_ref), channel_id=1, source_target_pairs={{0,2},{1,3},{2,0},{3,1},{4,6},{5,7},{6,4},{7,5},{8,10},{9,11},{10,... | collective-permute-start | bytes 884744 | tf_op jit(solution)/shard_map/ppermute | solution.py:364
  21.3 5.2 %collective-permute-start.8 = (f32[192,128]{1,0:T(8,128)S(1)}, f32[192,128]{1,0:T(8,128)S(1)}, u32[]{:S(2)}, u32[]{:S(2)}) collective-permute-start(f32[192,128]{1,0:T(8,128)S(1)} %get-tuple-element.52.blocks_ref), channel_id=1, source_target_pairs={{0,2},{1,3},{2,0},{3,1},{4,6},{5,7},{6,4},{7,5},{8,10},{9,11},{10,... | collective-permute-start | bytes 294920 | tf_op jit(solution)/shard_map/ppermute | solution.py:364
  25.0 4.6 %collective-permute-start.10 = (f32[1152,128]{1,0:T(8,128)S(1)}, f32[1152,128]{1,0:T(8,128)S(1)}, u32[]{:S(2)}, u32[]{:S(2)}) collective-permute-start(f32[1152,128]{1,0:T(8,128)S(1)} %shard_map.97.phi_ref), channel_id=1, source_target_pairs={{0,1},{1,0},{2,3},{3,2},{4,5},{5,4},{6,7},{7,6},{8,9},{9,8},{10,11... | collective-permute-start | bytes 1769480 | tf_op jit(solution)/shard_map/ppermute | solution.py:367
  26.4 3.2 %copy-start = (f32[2304,128]{1,0:T(8,128)S(1)}, f32[2304,128]{1,0:T(8,128)}, u32[]{:S(2)}) copy-start(f32[2304,128]{1,0:T(8,128)} %constant.20.clone.refs_4_) | copy-start | bytes 3538948
  26.4 3.1 %copy-start.1 = (f32[256,256]{1,0:T(8,128)S(1)}, f32[256,256]{1,0:T(8,128)}, u32[]{:S(2)}) copy-start(f32[256,256]{1,0:T(8,128)} %constant.15.clone.refs_1_) | copy-start | bytes 786436
  26.4 3.1 %copy-start.2 = (f32[256,256]{1,0:T(8,128)S(1)}, f32[256,256]{1,0:T(8,128)}, u32[]{:S(2)}) copy-start(f32[256,256]{1,0:T(8,128)} %constant.14.clone.refs_0_) | copy-start | bytes 786436
  26.5 3.1 %copy-start.3 = (f32[96,144]{1,0:T(8,128)S(1)}, f32[96,144]{1,0:T(8,128)}, u32[]{:S(2)}) copy-start(f32[96,144]{1,0:T(8,128)} %constant.17.clone.refs_3_) | copy-start | bytes 165892
  26.5 3.1 %copy-start.4 = (f32[96,144]{1,0:T(8,128)S(1)}, f32[96,144]{1,0:T(8,128)}, u32[]{:S(2)}) copy-start(f32[96,144]{1,0:T(8,128)} %constant.16.clone.refs_2_) | copy-start | bytes 165892
  28.6 4.6 %collective-permute-start.9 = (f32[1152,128]{1,0:T(8,128)S(1)}, f32[1152,128]{1,0:T(8,128)S(1)}, u32[]{:S(2)}, u32[]{:S(2)}) collective-permute-start(f32[1152,128]{1,0:T(8,128)S(1)} %shard_map.99.first_ref), channel_id=1, source_target_pairs={{0,1},{1,0},{2,3},{3,2},{4,5},{5,4},{6,7},{7,6},{8,9},{9,8},{10,11... | collective-permute-start | bytes 1769480 | tf_op jit(solution)/shard_map/ppermute | solution.py:367
  29.5 3.7 %copy-start.6 = (f32[96,384]{1,0:T(8,128)S(1)}, f32[96,384]{1,0:T(8,128)}, u32[]{:S(2)}) copy-start(f32[96,384]{1,0:T(8,128)} %constant.19.clone.stick_out_ref) | copy-start | bytes 442372
  40.1 7.3 %collective-permute-start.14 = (f32[96,128]{1,0:T(8,128)S(1)}, f32[96,128]{1,0:T(8,128)S(1)}, u32[]{:S(2)}, u32[]{:S(2)}) collective-permute-start(f32[96,128]{1,0:T(8,128)S(1)} %get-tuple-element.60), channel_id=1, source_target_pairs={{0,8},{4,12},{8,0},{12,4},{16,24},{20,28},{24,16},{28,20},{1,9},{5... | collective-permute-start | bytes 147464 | tf_op jit(solution)/shard_map/ppermute | solution.py:348
  41.5 8.2 %collective-permute-start.16 = (f32[96,128]{1,0:T(8,128)S(1)}, f32[96,128]{1,0:T(8,128)S(1)}, u32[]{:S(2)}, u32[]{:S(2)}) collective-permute-start(f32[96,128]{1,0:T(8,128)S(1)} %get-tuple-element.62), channel_id=1, source_target_pairs={{0,4},{4,0},{8,12},{12,8},{16,20},{20,16},{24,28},{28,24},{1,5},{5... | collective-permute-start | bytes 147464 | tf_op jit(solution)/shard_map/ppermute | solution.py:348
  42.0 7.7 %collective-permute-start.11 = (f32[96,128]{1,0:T(8,128)S(1)}, f32[96,128]{1,0:T(8,128)S(1)}, u32[]{:S(2)}, u32[]{:S(2)}) collective-permute-start(f32[96,128]{1,0:T(8,128)S(1)} %get-tuple-element.56), channel_id=1, source_target_pairs={{0,16},{4,20},{8,24},{12,28},{16,0},{20,4},{24,8},{28,12},{1,17},{... | collective-permute-start | bytes 147464 | tf_op jit(solution)/shard_map/ppermute | solution.py:348
  43.6 9.1 %collective-permute-start.12 = (f32[96,128]{1,0:T(8,128)S(1)}, f32[96,128]{1,0:T(8,128)S(1)}, u32[]{:S(2)}, u32[]{:S(2)}) collective-permute-start(f32[96,128]{1,0:T(8,128)S(1)} %get-tuple-element.57), channel_id=1, source_target_pairs={{0,20},{4,16},{8,28},{12,24},{16,4},{20,0},{24,12},{28,8},{1,21},{... | collective-permute-start | bytes 147464 | tf_op jit(solution)/shard_map/ppermute | solution.py:348
  45.9 6.8 %collective-permute-start.13 = (f32[96,128]{1,0:T(8,128)S(1)}, f32[96,128]{1,0:T(8,128)S(1)}, u32[]{:S(2)}, u32[]{:S(2)}) collective-permute-start(f32[96,128]{1,0:T(8,128)S(1)} %get-tuple-element.58), channel_id=1, source_target_pairs={{0,24},{4,28},{8,16},{12,20},{16,8},{20,12},{24,0},{28,4},{1,25},{... | collective-permute-start | bytes 147464 | tf_op jit(solution)/shard_map/ppermute | solution.py:348
  47.3 6.9 %collective-permute-start.15 = (f32[96,128]{1,0:T(8,128)S(1)}, f32[96,128]{1,0:T(8,128)S(1)}, u32[]{:S(2)}, u32[]{:S(2)}) collective-permute-start(f32[96,128]{1,0:T(8,128)S(1)} %get-tuple-element.61), channel_id=1, source_target_pairs={{0,28},{4,24},{8,20},{12,16},{16,12},{20,8},{24,4},{28,0},{1,29},{... | collective-permute-start | bytes 147464 | tf_op jit(solution)/shard_map/ppermute | solution.py:348
  49.6 5.1 %collective-permute-start.17 = (f32[96,128]{1,0:T(8,128)S(1)}, f32[96,128]{1,0:T(8,128)S(1)}, u32[]{:S(2)}, u32[]{:S(2)}) collective-permute-start(f32[96,128]{1,0:T(8,128)S(1)} %get-tuple-element.64), channel_id=1, source_target_pairs={{0,12},{4,8},{8,4},{12,0},{16,28},{20,24},{24,20},{28,16},{1,13},{... | collective-permute-start | bytes 147464 | tf_op jit(solution)/shard_map/ppermute | solution.py:348
  (2 other events, 1.8 us)

commit v20 on v19

--- a/solution.py
+++ b/solution.py
@@ -394,7 +394,7 @@
     mixed = [distant[0]] + [d for pair in zip(close, distant[1:]) for d in pair]
     before = {mixed[k]: (mixed[k - 3 - k % 2],) for k in range(WINDOW, len(mixed))}
     last = mixed[WINDOW]
-    received = exchanged(sent, mixed, {**before, last: (*before[last], staged, *first_tables)})
+    received = exchanged(sent, mixed, {d: (half, staged, *first_tables) if d == last else (half,) for d in before})
     received[0] = staged
     cut = owners * 3 // 4
     order = [0] + mixed
@@ -459,8 +459,8 @@
         *pot_tables,
     )
     result = [result[order.index(d)] for d in range(owners)]
-    result = exchanged(result, mixed, before)
-    out_order = [0] + distant + close
+    result = exchanged(result, mixed, {d: (half,) for d in before})
+    out_order = [0] + mixed
     return call(
         functools.partial(place_kernel, out_order),
         jax.ShapeDtypeStruct(sticks.shape, F32),

time: 55.8 us -> 55.9 us (level)
  starting transfers between devices: 25.6 us -> 26.4 us
  waiting for transfers between devices: 6.53 us -> 5.95 us
    ppermute x14, starting transfers between devices: 21.9 us -> 22.6 us  [exchanged(): moved[d] = lax.ppermute(block, 'stick', [(i, i ^ d) for i in range(owners)])]
    ppermute x14, waiting for transfers between devices: 6.52 us -> 5.94 us  [exchanged(): moved[d] = lax.ppermute(block, 'stick', [(i, i ^ d) for i in range(owners)])]
where the time goes in v20:
time: 55.9 us; the launch traced here: 55.7 us
  starting transfers between devices  26.4 us (47%)
  Pallas kernels  21.3 us (38%)
  waiting for transfers between devices  5.95 us (11%)
  local copies, waits for them, and re-layouts  1.83 us (3%)
    ppermute x14, starting transfers between devices, exchanged(): moved[d] = lax.ppermute(block, 'stick', [(i, i ^ d) for i in range(owners)])  22.6 us
    pallas_call x13, Pallas kernels, call(): pl.pallas_call(kernel, out_shape=out_shapes, in_specs=[pl.BlockSpec(memor...  21.3 us
    ppermute x14, waiting for transfers between devices, exchanged(): moved[d] = lax.ppermute(block, 'stick', [(i, i ^ d) for i in range(owners)])  5.94 us
    ppermute x2, starting transfers between devices, shifted(): lax.ppermute(x, 'band', [(i, (i - distance) % groups) for i in range(grou...  3.11 us
    unnamed x16, local copies, waits for them, and re-layouts  1.83 us
  transfers between devices with their start and end apart: 18, of which 5 were waited for; matrix products, arithmetic and copies ran while one was open for 0% of the time, Pallas kernels for 21%

profile of v20, /device:TPU:0, one launch (start us, length us, event | category | flops | bytes accessed | tf_op | source)
XLA Modules:
  0.0 55.7 jit_solution(14831280032694161102)
XLA Ops:
  0.0 1.8 %shard_map.91 = (f32[104,128]{1,0:T(8,128)}, f32[104,128]{1,0:T(8,128)}, f32[104,128]{1,0:T(8,128)}, f32[104,128]{1,0:T(8,128)}, f32[104,128]{1,0:T(8,128)}, /*i...) custom-call(f32[8,96,128]{2,1,0:T(8,128)} %sticks_ref.1, s32[1,128]{1,0:T(1,128)} %bitcast.1), custom_call_target="tpu_custom_call" | custom-call | flops 1 | bytes 1 | tf_op jit(solution)/shard_map/pallas_call | solution.py:327
  1.8 4.1 %collective-permute-start = (f32[104,128]{1,0:T(8,128)}, f32[104,128]{1,0:T(8,128)S(1)}, u32[]{:S(2)}, u32[]{:S(2)}) collective-permute-start(f32[104,128]{1,0:T(8,128)} %get-tuple-element.38), channel_id=1, source_target_pairs={{0,16},{4,20},{8,24},{12,28},{16,0},{20,4},{24,8},{28,12},{1,17},{... | collective-permute-start | bytes 159752 | tf_op jit(solution)/shard_map/ppermute | solution.py:348
  5.9 1.5 %collective-permute-start.1 = (f32[104,128]{1,0:T(8,128)}, f32[104,128]{1,0:T(8,128)S(1)}, u32[]{:S(2)}, u32[]{:S(2)}) collective-permute-start(f32[104,128]{1,0:T(8,128)} %get-tuple-element.39), channel_id=1, source_target_pairs={{0,4},{4,0},{8,12},{12,8},{16,20},{20,16},{24,28},{28,24},{1,5},{5... | collective-permute-start | bytes 159752 | tf_op jit(solution)/shard_map/ppermute | solution.py:348
  7.5 1.8 %collective-permute-start.3 = (f32[104,128]{1,0:T(8,128)}, f32[104,128]{1,0:T(8,128)S(1)}, u32[]{:S(2)}, u32[]{:S(2)}) collective-permute-start(f32[104,128]{1,0:T(8,128)} %get-tuple-element.41), channel_id=1, source_target_pairs={{0,8},{4,12},{8,0},{12,4},{16,24},{20,28},{24,16},{28,20},{1,9},{5... | collective-permute-start | bytes 159752 | tf_op jit(solution)/shard_map/ppermute | solution.py:348
  9.3 2.5 %collective-permute-start.4 = (f32[104,128]{1,0:T(8,128)}, f32[104,128]{1,0:T(8,128)S(1)}, u32[]{:S(2)}, u32[]{:S(2)}) collective-permute-start(f32[104,128]{1,0:T(8,128)} %get-tuple-element.42), channel_id=1, source_target_pairs={{0,24},{4,28},{8,16},{12,20},{16,8},{20,12},{24,0},{28,4},{1,25},{... | collective-permute-start | bytes 159752 | tf_op jit(solution)/shard_map/ppermute | solution.py:348
  11.8 1.0 %copy-done.5 = f32[224,288]{1,0:T(8,128)S(1)} copy-done((f32[224,288]{1,0:T(8,128)S(1)}, f32[224,288]{1,0:T(8,128)}, u32[]{:S(2)}) %copy-start.5) | copy-done | bytes 258072
  13.6 2.4 %collective-permute-start.5 = (f32[104,128]{1,0:T(8,128)}, f32[104,128]{1,0:T(8,128)S(1)}, u32[]{:S(2)}, u32[]{:S(2)}) collective-permute-start(f32[104,128]{1,0:T(8,128)} %get-tuple-element.47), channel_id=1, source_target_pairs={{0,28},{4,24},{8,20},{12,16},{16,12},{20,8},{24,4},{28,0},{1,29},{... | collective-permute-start | bytes 159752 | tf_op jit(solution)/shard_map/ppermute | solution.py:348
  16.0 1.6 %collective-permute-start.7 = (f32[576,128]{1,0:T(8,128)S(1)}, f32[576,128]{1,0:T(8,128)S(1)}, u32[]{:S(2)}, u32[]{:S(2)}) collective-permute-start(f32[576,128]{1,0:T(8,128)S(1)} %get-tuple-element.43.blocks_ref), channel_id=1, source_target_pairs={{0,2},{1,3},{2,0},{3,1},{4,6},{5,7},{6,4},{7,5},{8,10},{9,11},{10,... | collective-permute-start | bytes 884744 | tf_op jit(solution)/shard_map/ppermute | solution.py:364
  17.6 1.3 %shard_map.94.grid_ref = f32[2304,128]{1,0:T(8,128)S(1)} custom-call(f32[576,128]{1,0:T(8,128)S(1)} %get-tuple-element.43.blocks_ref, f32[8,768]{1,0:T(8,128)S(1)} %get-tuple-element.44.columns_ref, bf16[128,288]{1,0:T(8,128)(2,1)S(1)} %get-tuple-element.45.stick_in_ref), custom_call_target="tpu_custom_call" | custom-call | flops 5000000000 | bytes 5000000000 | tf_op jit(solution)/shard_map/pallas_call | solution.py:327
  18.9 0.9 %shard_map.95.hot_ref = bf16[768,2304]{1,0:T(8,128)(2,1)S(1)} custom-call(f32[8,768]{1,0:T(8,128)S(1)} %get-tuple-element.44.columns_ref), custom_call_target="tpu_custom_call" | custom-call | flops 1 | bytes 1 | tf_op jit(solution)/shard_map/pallas_call | solution.py:327
  19.9 0.8 %collective-permute-done.5.refs_0_ = f32[104,128]{1,0:T(8,128)S(1)} collective-permute-done((f32[104,128]{1,0:T(8,128)}, f32[104,128]{1,0:T(8,128)S(1)}, u32[]{:S(2)}, u32[]{:S(2)}) %collective-permute-start.5) | collective-permute-done | bytes 53280 | tf_op jit(solution)/shard_map/ppermute | solution.py:348
  21.3 1.6 %collective-permute-start.8 = (f32[192,128]{1,0:T(8,128)S(1)}, f32[192,128]{1,0:T(8,128)S(1)}, u32[]{:S(2)}, u32[]{:S(2)}) collective-permute-start(f32[192,128]{1,0:T(8,128)S(1)} %get-tuple-element.52.blocks_ref), channel_id=1, source_target_pairs={{0,2},{1,3},{2,0},{3,1},{4,6},{5,7},{6,4},{7,5},{8,10},{9,11},{10,... | collective-permute-start | bytes 294920 | tf_op jit(solution)/shard_map/ppermute | solution.py:364
  22.8 2.1 %shard_map.97.phi_ref = f32[1152,128]{1,0:T(8,128)S(1)} custom-call(f32[2304,128]{1,0:T(8,128)S(1)} %shard_map.94.grid_ref, f32[192,128]{1,0:T(8,128)S(1)} %get-tuple-element.52.blocks_ref, f32[8,256]{1,0:T(8,128)S(1)} %get-tuple-element.53.columns_ref, bf16[128,288]{1,0:T(8,128)(2,1)S(1)} %get-tuple-element.45.stick_in_ref, ...), custom_call_target="tpu_custom_call" | custom-call | flops 1 | bytes 1 | tf_op jit(solution)/shard_map/pallas_call | solution.py:327
  25.1 1.3 %shard_map.98.grid_ref = f32[2304,128]{1,0:T(8,128)S(1)} custom-call(f32[576,128]{1,0:T(8,128)S(1)} %collective-permute-done.7.blocks_ref, f32[8,768]{1,0:T(8,128)S(1)} %get-tuple-element.44.columns_ref, bf16[128,288]{1,0:T(8,128)(2,1)S(1)} %get-tuple-element.45.stick_in_ref), custom_call_target="tpu_custom_call" | custom-call | flops 1 | bytes 1 | tf_op jit(solution)/shard_map/pallas_call | solution.py:327
  26.5 2.1 %shard_map.99.first_ref = f32[1152,128]{1,0:T(8,128)S(1)} custom-call(f32[2304,128]{1,0:T(8,128)S(1)} %shard_map.98.grid_ref, f32[192,128]{1,0:T(8,128)S(1)} %collective-permute-done.8.blocks_ref, f32[8,256]{1,0:T(8,128)S(1)} %get-tuple-element.53.columns_ref, bf16[128,288]{1,0:T(8,128)(2,1)S(1)} %get-tuple-element.45.stick_in_ref, ...), custom_call_target="tpu_custom_call" | custom-call | flops 1 | bytes 1 | tf_op jit(solution)/shard_map/pallas_call | solution.py:327
  29.6 3.6 %shard_map.100.before_ref = f32[1152,128]{1,0:T(8,128)S(1)} custom-call(f32[1152,128]{1,0:T(8,128)S(1)} %shard_map.97.phi_ref, f32[1152,128]{1,0:T(8,128)S(1)} %collective-permute-done.10.other_ref, f32[256,256]{1,0:T(8,128)S(1)} %copy-done.2, f32[256,256]{1,0:T(8,128)S(1)} %copy-done.1, f32[96,144]{1,0:T(8,128)S(1)} %copy-done.4, f32[96,144]{1,0:T(8,128)S(1)} %copy-done.3, ...), custom_call_target="tpu_custom_call" | custom-call | flops 1 | bytes 1 | tf_op jit(solution)/shard_map/pallas_call | solution.py:327
  33.3 6.8 %shard_map.102 = (f32[96,128]{1,0:T(8,128)S(1)}, f32[96,128]{1,0:T(8,128)S(1)}, f32[96,128]{1,0:T(8,128)S(1)}, f32[96,128]{1,0:T(8,128)S(1)}, f32[96,128]{1,0:T(...) custom-call(f32[1152,128]{1,0:T(8,128)S(1)} %shard_map.97.phi_ref, ...), custom_call_target="tpu_custom_call" | custom-call | flops 1 | bytes 1 | tf_op jit(solution)/shard_map/pallas_call | solution.py:327
  40.1 1.4 %collective-permute-start.11 = (f32[96,128]{1,0:T(8,128)S(1)}, f32[96,128]{1,0:T(8,128)S(1)}, u32[]{:S(2)}, u32[]{:S(2)}) collective-permute-start(f32[96,128]{1,0:T(8,128)S(1)} %get-tuple-element.56), channel_id=1, source_target_pairs={{0,16},{4,20},{8,24},{12,28},{16,0},{20,4},{24,8},{28,12},{1,17},{... | collective-permute-start | bytes 147464 | tf_op jit(solution)/shard_map/ppermute | solution.py:348
  41.5 1.5 %collective-permute-start.12 = (f32[96,128]{1,0:T(8,128)S(1)}, f32[96,128]{1,0:T(8,128)S(1)}, u32[]{:S(2)}, u32[]{:S(2)}) collective-permute-start(f32[96,128]{1,0:T(8,128)S(1)} %get-tuple-element.57), channel_id=1, source_target_pairs={{0,4},{4,0},{8,12},{12,8},{16,20},{20,16},{24,28},{28,24},{1,5},{5... | collective-permute-start | bytes 147464 | tf_op jit(solution)/shard_map/ppermute | solution.py:348
  43.0 1.5 %collective-permute-start.13 = (f32[96,128]{1,0:T(8,128)S(1)}, f32[96,128]{1,0:T(8,128)S(1)}, u32[]{:S(2)}, u32[]{:S(2)}) collective-permute-start(f32[96,128]{1,0:T(8,128)S(1)} %get-tuple-element.58), channel_id=1, source_target_pairs={{0,20},{4,16},{8,28},{12,24},{16,4},{20,0},{24,12},{28,8},{1,21},{... | collective-permute-start | bytes 147464 | tf_op jit(solution)/shard_map/ppermute | solution.py:348
  44.9 2.5 %collective-permute-start.15 = (f32[96,128]{1,0:T(8,128)S(1)}, f32[96,128]{1,0:T(8,128)S(1)}, u32[]{:S(2)}, u32[]{:S(2)}) collective-permute-start(f32[96,128]{1,0:T(8,128)S(1)} %get-tuple-element.60), channel_id=1, source_target_pairs={{0,24},{4,28},{8,16},{12,20},{16,8},{20,12},{24,0},{28,4},{1,25},{... | collective-permute-start | bytes 147464 | tf_op jit(solution)/shard_map/ppermute | solution.py:348
  48.0 2.4 %collective-permute-start.17 = (f32[96,128]{1,0:T(8,128)S(1)}, f32[96,128]{1,0:T(8,128)S(1)}, u32[]{:S(2)}, u32[]{:S(2)}) collective-permute-start(f32[96,128]{1,0:T(8,128)S(1)} %get-tuple-element.64), channel_id=1, source_target_pairs={{0,28},{4,24},{8,20},{12,16},{16,12},{20,8},{24,4},{28,0},{1,29},{... | collective-permute-start | bytes 147464 | tf_op jit(solution)/shard_map/ppermute | solution.py:348
  51.1 1.7 %collective-permute-done.16.refs_6_ = f32[96,128]{1,0:T(8,128)S(1)} collective-permute-done((f32[96,128]{1,0:T(8,128)S(1)}, f32[96,128]{1,0:T(8,128)S(1)}, u32[]{:S(2)}, u32[]{:S(2)}) %collective-permute-start.16) | collective-permute-done | bytes 49184 | tf_op jit(solution)/shard_map/ppermute | solution.py:348
  52.9 2.0 %collective-permute-done.17.refs_7_ = f32[96,128]{1,0:T(8,128)S(1)} collective-permute-done((f32[96,128]{1,0:T(8,128)S(1)}, f32[96,128]{1,0:T(8,128)S(1)}, u32[]{:S(2)}, u32[]{:S(2)}) %collective-permute-start.17) | collective-permute-done | bytes 49184 | tf_op jit(solution)/shard_map/ppermute | solution.py:348
  (41 shorter events, 5.0 us)
Async XLA Ops:
  1.8 11.8 %collective-permute-start = (f32[104,128]{1,0:T(8,128)}, f32[104,128]{1,0:T(8,128)S(1)}, u32[]{:S(2)}, u32[]{:S(2)}) collective-permute-start(f32[104,128]{1,0:T(8,128)} %get-tuple-element.38), channel_id=1, source_target_pairs={{0,16},{4,20},{8,24},{12,28},{16,0},{20,4},{24,8},{28,12},{1,17},{... | collective-permute-start | bytes 159752 | tf_op jit(solution)/shard_map/ppermute | solution.py:348
  5.9 10.0 %collective-permute-start.1 = (f32[104,128]{1,0:T(8,128)}, f32[104,128]{1,0:T(8,128)S(1)}, u32[]{:S(2)}, u32[]{:S(2)}) collective-permute-start(f32[104,128]{1,0:T(8,128)} %get-tuple-element.39), channel_id=1, source_target_pairs={{0,4},{4,0},{8,12},{12,8},{16,20},{20,16},{24,28},{28,24},{1,5},{5... | collective-permute-start | bytes 159752 | tf_op jit(solution)/shard_map/ppermute | solution.py:348
  7.4 8.5 %collective-permute-start.2 = (f32[104,128]{1,0:T(8,128)}, f32[104,128]{1,0:T(8,128)S(1)}, u32[]{:S(2)}, u32[]{:S(2)}) collective-permute-start(f32[104,128]{1,0:T(8,128)} %get-tuple-element.40), channel_id=1, source_target_pairs={{0,20},{4,16},{8,28},{12,24},{16,4},{20,0},{24,12},{28,8},{1,21},{... | collective-permute-start | bytes 159752 | tf_op jit(solution)/shard_map/ppermute | solution.py:348
  7.5 8.5 %collective-permute-start.3 = (f32[104,128]{1,0:T(8,128)}, f32[104,128]{1,0:T(8,128)S(1)}, u32[]{:S(2)}, u32[]{:S(2)}) collective-permute-start(f32[104,128]{1,0:T(8,128)} %get-tuple-element.41), channel_id=1, source_target_pairs={{0,8},{4,12},{8,0},{12,4},{16,24},{20,28},{24,16},{28,20},{1,9},{5... | collective-permute-start | bytes 159752 | tf_op jit(solution)/shard_map/ppermute | solution.py:348
  9.3 6.7 %collective-permute-start.4 = (f32[104,128]{1,0:T(8,128)}, f32[104,128]{1,0:T(8,128)S(1)}, u32[]{:S(2)}, u32[]{:S(2)}) collective-permute-start(f32[104,128]{1,0:T(8,128)} %get-tuple-element.42), channel_id=1, source_target_pairs={{0,24},{4,28},{8,16},{12,20},{16,8},{20,12},{24,0},{28,4},{1,25},{... | collective-permute-start | bytes 159752 | tf_op jit(solution)/shard_map/ppermute | solution.py:348
  13.6 7.1 %collective-permute-start.5 = (f32[104,128]{1,0:T(8,128)}, f32[104,128]{1,0:T(8,128)S(1)}, u32[]{:S(2)}, u32[]{:S(2)}) collective-permute-start(f32[104,128]{1,0:T(8,128)} %get-tuple-element.47), channel_id=1, source_target_pairs={{0,28},{4,24},{8,20},{12,16},{16,12},{20,8},{24,4},{28,0},{1,29},{... | collective-permute-start | bytes 159752 | tf_op jit(solution)/shard_map/ppermute | solution.py:348
  16.0 5.3 %collective-permute-start.6 = (f32[104,128]{1,0:T(8,128)}, f32[104,128]{1,0:T(8,128)S(1)}, u32[]{:S(2)}, u32[]{:S(2)}) collective-permute-start(f32[104,128]{1,0:T(8,128)} %get-tuple-element.51), channel_id=1, source_target_pairs={{0,12},{4,8},{8,4},{12,0},{16,28},{20,24},{24,20},{28,16},{1,13},{... | collective-permute-start | bytes 159752 | tf_op jit(solution)/shard_map/ppermute | solution.py:348
  16.0 9.0 %collective-permute-start.7 = (f32[576,128]{1,0:T(8,128)S(1)}, f32[576,128]{1,0:T(8,128)S(1)}, u32[]{:S(2)}, u32[]{:S(2)}) collective-permute-start(f32[576,128]{1,0:T(8,128)S(1)} %get-tuple-element.43.blocks_ref), channel_id=1, source_target_pairs={{0,2},{1,3},{2,0},{3,1},{4,6},{5,7},{6,4},{7,5},{8,10},{9,11},{10,... | collective-permute-start | bytes 884744 | tf_op jit(solution)/shard_map/ppermute | solution.py:364
  21.3 5.2 %collective-permute-start.8 = (f32[192,128]{1,0:T(8,128)S(1)}, f32[192,128]{1,0:T(8,128)S(1)}, u32[]{:S(2)}, u32[]{:S(2)}) collective-permute-start(f32[192,128]{1,0:T(8,128)S(1)} %get-tuple-element.52.blocks_ref), channel_id=1, source_target_pairs={{0,2},{1,3},{2,0},{3,1},{4,6},{5,7},{6,4},{7,5},{8,10},{9,11},{10,... | collective-permute-start | bytes 294920 | tf_op jit(solution)/shard_map/ppermute | solution.py:364
  25.0 4.6 %collective-permute-start.10 = (f32[1152,128]{1,0:T(8,128)S(1)}, f32[1152,128]{1,0:T(8,128)S(1)}, u32[]{:S(2)}, u32[]{:S(2)}) collective-permute-start(f32[1152,128]{1,0:T(8,128)S(1)} %shard_map.97.phi_ref), channel_id=1, source_target_pairs={{0,1},{1,0},{2,3},{3,2},{4,5},{5,4},{6,7},{7,6},{8,9},{9,8},{10,11... | collective-permute-start | bytes 1769480 | tf_op jit(solution)/shard_map/ppermute | solution.py:367
  26.4 3.2 %copy-start = (f32[2304,128]{1,0:T(8,128)S(1)}, f32[2304,128]{1,0:T(8,128)}, u32[]{:S(2)}) copy-start(f32[2304,128]{1,0:T(8,128)} %constant.20.clone.refs_4_) | copy-start | bytes 3538948
  26.4 3.1 %copy-start.1 = (f32[256,256]{1,0:T(8,128)S(1)}, f32[256,256]{1,0:T(8,128)}, u32[]{:S(2)}) copy-start(f32[256,256]{1,0:T(8,128)} %constant.15.clone.refs_1_) | copy-start | bytes 786436
  26.4 3.1 %copy-start.2 = (f32[256,256]{1,0:T(8,128)S(1)}, f32[256,256]{1,0:T(8,128)}, u32[]{:S(2)}) copy-start(f32[256,256]{1,0:T(8,128)} %constant.14.clone.refs_0_) | copy-start | bytes 786436
  26.5 3.1 %copy-start.3 = (f32[96,144]{1,0:T(8,128)S(1)}, f32[96,144]{1,0:T(8,128)}, u32[]{:S(2)}) copy-start(f32[96,144]{1,0:T(8,128)} %constant.17.clone.refs_3_) | copy-start | bytes 165892
  26.5 3.1 %copy-start.4 = (f32[96,144]{1,0:T(8,128)S(1)}, f32[96,144]{1,0:T(8,128)}, u32[]{:S(2)}) copy-start(f32[96,144]{1,0:T(8,128)} %constant.16.clone.refs_2_) | copy-start | bytes 165892
  28.6 4.6 %collective-permute-start.9 = (f32[1152,128]{1,0:T(8,128)S(1)}, f32[1152,128]{1,0:T(8,128)S(1)}, u32[]{:S(2)}, u32[]{:S(2)}) collective-permute-start(f32[1152,128]{1,0:T(8,128)S(1)} %shard_map.99.first_ref), channel_id=1, source_target_pairs={{0,1},{1,0},{2,3},{3,2},{4,5},{5,4},{6,7},{7,6},{8,9},{9,8},{10,11... | collective-permute-start | bytes 1769480 | tf_op jit(solution)/shard_map/ppermute | solution.py:367
  29.5 3.7 %copy-start.6 = (f32[96,384]{1,0:T(8,128)S(1)}, f32[96,384]{1,0:T(8,128)}, u32[]{:S(2)}) copy-start(f32[96,384]{1,0:T(8,128)} %constant.19.clone.stick_out_ref) | copy-start | bytes 442372
  40.1 7.3 %collective-permute-start.11 = (f32[96,128]{1,0:T(8,128)S(1)}, f32[96,128]{1,0:T(8,128)S(1)}, u32[]{:S(2)}, u32[]{:S(2)}) collective-permute-start(f32[96,128]{1,0:T(8,128)S(1)} %get-tuple-element.56), channel_id=1, source_target_pairs={{0,16},{4,20},{8,24},{12,28},{16,0},{20,4},{24,8},{28,12},{1,17},{... | collective-permute-start | bytes 147464 | tf_op jit(solution)/shard_map/ppermute | solution.py:348
  41.5 6.5 %collective-permute-start.12 = (f32[96,128]{1,0:T(8,128)S(1)}, f32[96,128]{1,0:T(8,128)S(1)}, u32[]{:S(2)}, u32[]{:S(2)}) collective-permute-start(f32[96,128]{1,0:T(8,128)S(1)} %get-tuple-element.57), channel_id=1, source_target_pairs={{0,4},{4,0},{8,12},{12,8},{16,20},{20,16},{24,28},{28,24},{1,5},{5... | collective-permute-start | bytes 147464 | tf_op jit(solution)/shard_map/ppermute | solution.py:348
  43.0 7.4 %collective-permute-start.13 = (f32[96,128]{1,0:T(8,128)S(1)}, f32[96,128]{1,0:T(8,128)S(1)}, u32[]{:S(2)}, u32[]{:S(2)}) collective-permute-start(f32[96,128]{1,0:T(8,128)S(1)} %get-tuple-element.58), channel_id=1, source_target_pairs={{0,20},{4,16},{8,28},{12,24},{16,4},{20,0},{24,12},{28,8},{1,21},{... | collective-permute-start | bytes 147464 | tf_op jit(solution)/shard_map/ppermute | solution.py:348
  44.5 5.9 %collective-permute-start.14 = (f32[96,128]{1,0:T(8,128)S(1)}, f32[96,128]{1,0:T(8,128)S(1)}, u32[]{:S(2)}, u32[]{:S(2)}) collective-permute-start(f32[96,128]{1,0:T(8,128)S(1)} %get-tuple-element.59), channel_id=1, source_target_pairs={{0,8},{4,12},{8,0},{12,4},{16,24},{20,28},{24,16},{28,20},{1,9},{5... | collective-permute-start | bytes 147464 | tf_op jit(solution)/shard_map/ppermute | solution.py:348
  44.9 6.2 %collective-permute-start.15 = (f32[96,128]{1,0:T(8,128)S(1)}, f32[96,128]{1,0:T(8,128)S(1)}, u32[]{:S(2)}, u32[]{:S(2)}) collective-permute-start(f32[96,128]{1,0:T(8,128)S(1)} %get-tuple-element.60), channel_id=1, source_target_pairs={{0,24},{4,28},{8,16},{12,20},{16,8},{20,12},{24,0},{28,4},{1,25},{... | collective-permute-start | bytes 147464 | tf_op jit(solution)/shard_map/ppermute | solution.py:348
  47.3 5.5 %collective-permute-start.16 = (f32[96,128]{1,0:T(8,128)S(1)}, f32[96,128]{1,0:T(8,128)S(1)}, u32[]{:S(2)}, u32[]{:S(2)}) collective-permute-start(f32[96,128]{1,0:T(8,128)S(1)} %get-tuple-element.62), channel_id=1, source_target_pairs={{0,12},{4,8},{8,4},{12,0},{16,28},{20,24},{24,20},{28,16},{1,13},{... | collective-permute-start | bytes 147464 | tf_op jit(solution)/shard_map/ppermute | solution.py:348
  48.0 6.9 %collective-permute-start.17 = (f32[96,128]{1,0:T(8,128)S(1)}, f32[96,128]{1,0:T(8,128)S(1)}, u32[]{:S(2)}, u32[]{:S(2)}) collective-permute-start(f32[96,128]{1,0:T(8,128)S(1)} %get-tuple-element.64), channel_id=1, source_target_pairs={{0,28},{4,24},{8,20},{12,16},{16,12},{20,8},{24,4},{28,0},{1,29},{... | collective-permute-start | bytes 147464 | tf_op jit(solution)/shard_map/ppermute | solution.py:348
  (2 other events, 1.8 us)

commit v21 on v20

--- a/solution.py
+++ b/solution.py
@@ -169,9 +169,14 @@
 
 def place_kernel(order, *refs):
     own = lax.axis_index("stick")
-    out_ref = refs[-1]
-    for d, block_ref in zip(order, refs[:-1]):
-        out_ref[own ^ d] = block_ref[...]
+    block_refs, (out_ref, sems) = refs[:-2], refs[-2:]
+    copies = [
+        pltpu.make_async_copy(ref, out_ref.at[own ^ d], sems.at[k]) for k, (d, ref) in enumerate(zip(order, block_refs))
+    ]
+    for copy in copies:
+        copy.start()
+    for copy in copies:
+        copy.wait()
 
 
 def store(ref, first, slabs):
@@ -459,14 +464,19 @@
         *pot_tables,
     )
     result = [result[order.index(d)] for d in range(owners)]
-    result = exchanged(result, mixed, {d: (half,) for d in before})
-    out_order = [0] + mixed
+    out_order = []
+    for k in range(0, half, 2):
+        out_order += distant[k : k + 2] + close[k // 2 : k // 2 + 1]
+    out_order = [d for d in out_order if d not in close[half // 4 :]] + close[half // 4 :]
+    result = exchanged(result, out_order, {d: (half,) for d in out_order[WINDOW:]})
+    out_order = [0] + out_order
     return call(
         functools.partial(place_kernel, out_order),
         jax.ShapeDtypeStruct(sticks.shape, F32),
-        [],
+        [pltpu.SemaphoreType.DMA((owners,))],
         1,
         *[result[d] for d in out_order],
+        out_space=pltpu.HBM,
     )
 
 

time: 55.9 us -> 55.7 us (level)
  waiting for transfers between devices: 5.95 us -> 5.2 us
    ppermute x14, waiting for transfers between devices: 5.94 us -> 5.19 us  [exchanged(): moved[d] = lax.ppermute(block, 'stick', [(i, i ^ d) for i in range(owners)])]
  transfers between devices with their start and end apart: 18 -> 18, of which waited for: 5 -> 5; matrix products, arithmetic and copies ran while one was open for 0% -> 0% of each run, Pallas kernels for 21% -> 22%
where the time goes in v21:
time: 55.7 us; the launch traced here: 55.4 us
  starting transfers between devices  26.6 us (48%)
  Pallas kernels  21.3 us (38%)
  waiting for transfers between devices  5.2 us (9%)
  local copies, waits for them, and re-layouts  1.83 us (3%)
    ppermute x14, starting transfers between devices, exchanged(): moved[d] = lax.ppermute(block, 'stick', [(i, i ^ d) for i in range(owners)])  22.9 us
    pallas_call x13, Pallas kernels, call(): pl.pallas_call(kernel, out_shape=out_shapes, in_specs=[pl.BlockSpec(memor...  21.3 us
    ppermute x14, waiting for transfers between devices, exchanged(): moved[d] = lax.ppermute(block, 'stick', [(i, i ^ d) for i in range(owners)])  5.19 us
    ppermute x2, starting transfers between devices, shifted(): lax.ppermute(x, 'band', [(i, (i - distance) % groups) for i in range(grou...  3.11 us
    unnamed x16, local copies, waits for them, and re-layouts  1.83 us
  transfers between devices with their start and end apart: 18, of which 5 were waited for; matrix products, arithmetic and copies ran while one was open for 0% of the time, Pallas kernels for 22%

profile of v21, /device:TPU:0, one launch (start us, length us, event | category | flops | bytes accessed | tf_op | source)
XLA Modules:
  0.0 55.4 jit_solution(3229080399532423404)
XLA Ops:
  0.0 1.8 %shard_map.91 = (f32[104,128]{1,0:T(8,128)}, f32[104,128]{1,0:T(8,128)}, f32[104,128]{1,0:T(8,128)}, f32[104,128]{1,0:T(8,128)}, f32[104,128]{1,0:T(8,128)}, /*i...) custom-call(f32[8,96,128]{2,1,0:T(8,128)} %sticks_ref.1, s32[1,128]{1,0:T(1,128)} %bitcast.1), custom_call_target="tpu_custom_call" | custom-call | flops 1 | bytes 1 | tf_op jit(solution)/shard_map/pallas_call | solution.py:332
  1.8 4.1 %collective-permute-start = (f32[104,128]{1,0:T(8,128)}, f32[104,128]{1,0:T(8,128)S(1)}, u32[]{:S(2)}, u32[]{:S(2)}) collective-permute-start(f32[104,128]{1,0:T(8,128)} %get-tuple-element.38), channel_id=1, source_target_pairs={{0,16},{4,20},{8,24},{12,28},{16,0},{20,4},{24,8},{28,12},{1,17},{... | collective-permute-start | bytes 159752 | tf_op jit(solution)/shard_map/ppermute | solution.py:353
  5.9 1.5 %collective-permute-start.1 = (f32[104,128]{1,0:T(8,128)}, f32[104,128]{1,0:T(8,128)S(1)}, u32[]{:S(2)}, u32[]{:S(2)}) collective-permute-start(f32[104,128]{1,0:T(8,128)} %get-tuple-element.39), channel_id=1, source_target_pairs={{0,4},{4,0},{8,12},{12,8},{16,20},{20,16},{24,28},{28,24},{1,5},{5... | collective-permute-start | bytes 159752 | tf_op jit(solution)/shard_map/ppermute | solution.py:353
  7.5 1.8 %collective-permute-start.3 = (f32[104,128]{1,0:T(8,128)}, f32[104,128]{1,0:T(8,128)S(1)}, u32[]{:S(2)}, u32[]{:S(2)}) collective-permute-start(f32[104,128]{1,0:T(8,128)} %get-tuple-element.41), channel_id=1, source_target_pairs={{0,8},{4,12},{8,0},{12,4},{16,24},{20,28},{24,16},{28,20},{1,9},{5... | collective-permute-start | bytes 159752 | tf_op jit(solution)/shard_map/ppermute | solution.py:353
  9.3 2.5 %collective-permute-start.4 = (f32[104,128]{1,0:T(8,128)}, f32[104,128]{1,0:T(8,128)S(1)}, u32[]{:S(2)}, u32[]{:S(2)}) collective-permute-start(f32[104,128]{1,0:T(8,128)} %get-tuple-element.42), channel_id=1, source_target_pairs={{0,24},{4,28},{8,16},{12,20},{16,8},{20,12},{24,0},{28,4},{1,25},{... | collective-permute-start | bytes 159752 | tf_op jit(solution)/shard_map/ppermute | solution.py:353
  11.8 1.0 %copy-done.5 = f32[224,288]{1,0:T(8,128)S(1)} copy-done((f32[224,288]{1,0:T(8,128)S(1)}, f32[224,288]{1,0:T(8,128)}, u32[]{:S(2)}) %copy-start.5) | copy-done | bytes 258072
  13.6 2.4 %collective-permute-start.5 = (f32[104,128]{1,0:T(8,128)}, f32[104,128]{1,0:T(8,128)S(1)}, u32[]{:S(2)}, u32[]{:S(2)}) collective-permute-start(f32[104,128]{1,0:T(8,128)} %get-tuple-element.47), channel_id=1, source_target_pairs={{0,28},{4,24},{8,20},{12,16},{16,12},{20,8},{24,4},{28,0},{1,29},{... | collective-permute-start | bytes 159752 | tf_op jit(solution)/shard_map/ppermute | solution.py:353
  16.0 1.6 %collective-permute-start.7 = (f32[576,128]{1,0:T(8,128)S(1)}, f32[576,128]{1,0:T(8,128)S(1)}, u32[]{:S(2)}, u32[]{:S(2)}) collective-permute-start(f32[576,128]{1,0:T(8,128)S(1)} %get-tuple-element.43.blocks_ref), channel_id=1, source_target_pairs={{0,2},{1,3},{2,0},{3,1},{4,6},{5,7},{6,4},{7,5},{8,10},{9,11},{10,... | collective-permute-start | bytes 884744 | tf_op jit(solution)/shard_map/ppermute | solution.py:369
  17.6 1.3 %shard_map.94.grid_ref = f32[2304,128]{1,0:T(8,128)S(1)} custom-call(f32[576,128]{1,0:T(8,128)S(1)} %get-tuple-element.43.blocks_ref, f32[8,768]{1,0:T(8,128)S(1)} %get-tuple-element.44.columns_ref, bf16[128,288]{1,0:T(8,128)(2,1)S(1)} %get-tuple-element.45.stick_in_ref), custom_call_target="tpu_custom_call" | custom-call | flops 5000000000 | bytes 5000000000 | tf_op jit(solution)/shard_map/pallas_call | solution.py:332
  18.9 0.9 %shard_map.95.hot_ref = bf16[768,2304]{1,0:T(8,128)(2,1)S(1)} custom-call(f32[8,768]{1,0:T(8,128)S(1)} %get-tuple-element.44.columns_ref), custom_call_target="tpu_custom_call" | custom-call | flops 1 | bytes 1 | tf_op jit(solution)/shard_map/pallas_call | solution.py:332
  19.9 0.8 %collective-permute-done.5.refs_0_ = f32[104,128]{1,0:T(8,128)S(1)} collective-permute-done((f32[104,128]{1,0:T(8,128)}, f32[104,128]{1,0:T(8,128)S(1)}, u32[]{:S(2)}, u32[]{:S(2)}) %collective-permute-start.5) | collective-permute-done | bytes 53280 | tf_op jit(solution)/shard_map/ppermute | solution.py:353
  21.3 1.6 %collective-permute-start.8 = (f32[192,128]{1,0:T(8,128)S(1)}, f32[192,128]{1,0:T(8,128)S(1)}, u32[]{:S(2)}, u32[]{:S(2)}) collective-permute-start(f32[192,128]{1,0:T(8,128)S(1)} %get-tuple-element.52.blocks_ref), channel_id=1, source_target_pairs={{0,2},{1,3},{2,0},{3,1},{4,6},{5,7},{6,4},{7,5},{8,10},{9,11},{10,... | collective-permute-start | bytes 294920 | tf_op jit(solution)/shard_map/ppermute | solution.py:369
  22.8 2.1 %shard_map.97.phi_ref = f32[1152,128]{1,0:T(8,128)S(1)} custom-call(f32[2304,128]{1,0:T(8,128)S(1)} %shard_map.94.grid_ref, f32[192,128]{1,0:T(8,128)S(1)} %get-tuple-element.52.blocks_ref, f32[8,256]{1,0:T(8,128)S(1)} %get-tuple-element.53.columns_ref, bf16[128,288]{1,0:T(8,128)(2,1)S(1)} %get-tuple-element.45.stick_in_ref, ...), custom_call_target="tpu_custom_call" | custom-call | flops 1 | bytes 1 | tf_op jit(solution)/shard_map/pallas_call | solution.py:332
  25.1 1.3 %shard_map.98.grid_ref = f32[2304,128]{1,0:T(8,128)S(1)} custom-call(f32[576,128]{1,0:T(8,128)S(1)} %collective-permute-done.7.blocks_ref, f32[8,768]{1,0:T(8,128)S(1)} %get-tuple-element.44.columns_ref, bf16[128,288]{1,0:T(8,128)(2,1)S(1)} %get-tuple-element.45.stick_in_ref), custom_call_target="tpu_custom_call" | custom-call | flops 1 | bytes 1 | tf_op jit(solution)/shard_map/pallas_call | solution.py:332
  26.5 2.1 %shard_map.99.first_ref = f32[1152,128]{1,0:T(8,128)S(1)} custom-call(f32[2304,128]{1,0:T(8,128)S(1)} %shard_map.98.grid_ref, f32[192,128]{1,0:T(8,128)S(1)} %collective-permute-done.8.blocks_ref, f32[8,256]{1,0:T(8,128)S(1)} %get-tuple-element.53.columns_ref, bf16[128,288]{1,0:T(8,128)(2,1)S(1)} %get-tuple-element.45.stick_in_ref, ...), custom_call_target="tpu_custom_call" | custom-call | flops 1 | bytes 1 | tf_op jit(solution)/shard_map/pallas_call | solution.py:332
  29.6 3.6 %shard_map.100.before_ref = f32[1152,128]{1,0:T(8,128)S(1)} custom-call(f32[1152,128]{1,0:T(8,128)S(1)} %shard_map.97.phi_ref, f32[1152,128]{1,0:T(8,128)S(1)} %collective-permute-done.10.other_ref, f32[256,256]{1,0:T(8,128)S(1)} %copy-done.2, f32[256,256]{1,0:T(8,128)S(1)} %copy-done.1, f32[96,144]{1,0:T(8,128)S(1)} %copy-done.4, f32[96,144]{1,0:T(8,128)S(1)} %copy-done.3, ...), custom_call_target="tpu_custom_call" | custom-call | flops 1 | bytes 1 | tf_op jit(solution)/shard_map/pallas_call | solution.py:332
  33.3 6.8 %shard_map.102 = (f32[96,128]{1,0:T(8,128)S(1)}, f32[96,128]{1,0:T(8,128)S(1)}, f32[96,128]{1,0:T(8,128)S(1)}, f32[96,128]{1,0:T(8,128)S(1)}, f32[96,128]{1,0:T(...) custom-call(f32[1152,128]{1,0:T(8,128)S(1)} %shard_map.97.phi_ref, ...), custom_call_target="tpu_custom_call" | custom-call | flops 1 | bytes 1 | tf_op jit(solution)/shard_map/pallas_call | solution.py:332
  40.1 1.4 %collective-permute-start.11 = (f32[96,128]{1,0:T(8,128)S(1)}, f32[96,128]{1,0:T(8,128)S(1)}, u32[]{:S(2)}, u32[]{:S(2)}) collective-permute-start(f32[96,128]{1,0:T(8,128)S(1)} %get-tuple-element.56), channel_id=1, source_target_pairs={{0,16},{4,20},{8,24},{12,28},{16,0},{20,4},{24,8},{28,12},{1,17},{... | collective-permute-start | bytes 147464 | tf_op jit(solution)/shard_map/ppermute | solution.py:353
  41.5 2.0 %collective-permute-start.12 = (f32[96,128]{1,0:T(8,128)S(1)}, f32[96,128]{1,0:T(8,128)S(1)}, u32[]{:S(2)}, u32[]{:S(2)}) collective-permute-start(f32[96,128]{1,0:T(8,128)S(1)} %get-tuple-element.57), channel_id=1, source_target_pairs={{0,20},{4,16},{8,28},{12,24},{16,4},{20,0},{24,12},{28,8},{1,21},{... | collective-permute-start | bytes 147464 | tf_op jit(solution)/shard_map/ppermute | solution.py:353
  43.5 1.0 %collective-permute-start.13 = (f32[96,128]{1,0:T(8,128)S(1)}, f32[96,128]{1,0:T(8,128)S(1)}, u32[]{:S(2)}, u32[]{:S(2)}) collective-permute-start(f32[96,128]{1,0:T(8,128)S(1)} %get-tuple-element.58), channel_id=1, source_target_pairs={{0,4},{4,0},{8,12},{12,8},{16,20},{20,16},{24,28},{28,24},{1,5},{5... | collective-permute-start | bytes 147464 | tf_op jit(solution)/shard_map/ppermute | solution.py:353
  44.5 2.4 %collective-permute-start.14 = (f32[96,128]{1,0:T(8,128)S(1)}, f32[96,128]{1,0:T(8,128)S(1)}, u32[]{:S(2)}, u32[]{:S(2)}) collective-permute-start(f32[96,128]{1,0:T(8,128)S(1)} %get-tuple-element.59), channel_id=1, source_target_pairs={{0,24},{4,28},{8,16},{12,20},{16,8},{20,12},{24,0},{28,4},{1,25},{... | collective-permute-start | bytes 147464 | tf_op jit(solution)/shard_map/ppermute | solution.py:353
  46.9 1.9 %collective-permute-start.15 = (f32[96,128]{1,0:T(8,128)S(1)}, f32[96,128]{1,0:T(8,128)S(1)}, u32[]{:S(2)}, u32[]{:S(2)}) collective-permute-start(f32[96,128]{1,0:T(8,128)S(1)} %get-tuple-element.60), channel_id=1, source_target_pairs={{0,28},{4,24},{8,20},{12,16},{16,12},{20,8},{24,4},{28,0},{1,29},{... | collective-permute-start | bytes 147464 | tf_op jit(solution)/shard_map/ppermute | solution.py:353
  49.4 1.8 %collective-permute-start.17 = (f32[96,128]{1,0:T(8,128)S(1)}, f32[96,128]{1,0:T(8,128)S(1)}, u32[]{:S(2)}, u32[]{:S(2)}) collective-permute-start(f32[96,128]{1,0:T(8,128)S(1)} %get-tuple-element.64), channel_id=1, source_target_pairs={{0,12},{4,8},{8,4},{12,0},{16,28},{20,24},{24,20},{28,16},{1,13},{... | collective-permute-start | bytes 147464 | tf_op jit(solution)/shard_map/ppermute | solution.py:353
  51.3 2.5 %collective-permute-done.15.refs_5_ = f32[96,128]{1,0:T(8,128)S(1)} collective-permute-done((f32[96,128]{1,0:T(8,128)S(1)}, f32[96,128]{1,0:T(8,128)S(1)}, u32[]{:S(2)}, u32[]{:S(2)}) %collective-permute-start.15) | collective-permute-done | bytes 49184 | tf_op jit(solution)/shard_map/ppermute | solution.py:353
  (41 shorter events, 4.5 us)
Async XLA Ops:
  1.8 11.8 %collective-permute-start = (f32[104,128]{1,0:T(8,128)}, f32[104,128]{1,0:T(8,128)S(1)}, u32[]{:S(2)}, u32[]{:S(2)}) collective-permute-start(f32[104,128]{1,0:T(8,128)} %get-tuple-element.38), channel_id=1, source_target_pairs={{0,16},{4,20},{8,24},{12,28},{16,0},{20,4},{24,8},{28,12},{1,17},{... | collective-permute-start | bytes 159752 | tf_op jit(solution)/shard_map/ppermute | solution.py:353
  5.9 10.0 %collective-permute-start.1 = (f32[104,128]{1,0:T(8,128)}, f32[104,128]{1,0:T(8,128)S(1)}, u32[]{:S(2)}, u32[]{:S(2)}) collective-permute-start(f32[104,128]{1,0:T(8,128)} %get-tuple-element.39), channel_id=1, source_target_pairs={{0,4},{4,0},{8,12},{12,8},{16,20},{20,16},{24,28},{28,24},{1,5},{5... | collective-permute-start | bytes 159752 | tf_op jit(solution)/shard_map/ppermute | solution.py:353
  7.4 8.5 %collective-permute-start.2 = (f32[104,128]{1,0:T(8,128)}, f32[104,128]{1,0:T(8,128)S(1)}, u32[]{:S(2)}, u32[]{:S(2)}) collective-permute-start(f32[104,128]{1,0:T(8,128)} %get-tuple-element.40), channel_id=1, source_target_pairs={{0,20},{4,16},{8,28},{12,24},{16,4},{20,0},{24,12},{28,8},{1,21},{... | collective-permute-start | bytes 159752 | tf_op jit(solution)/shard_map/ppermute | solution.py:353
  7.5 8.5 %collective-permute-start.3 = (f32[104,128]{1,0:T(8,128)}, f32[104,128]{1,0:T(8,128)S(1)}, u32[]{:S(2)}, u32[]{:S(2)}) collective-permute-start(f32[104,128]{1,0:T(8,128)} %get-tuple-element.41), channel_id=1, source_target_pairs={{0,8},{4,12},{8,0},{12,4},{16,24},{20,28},{24,16},{28,20},{1,9},{5... | collective-permute-start | bytes 159752 | tf_op jit(solution)/shard_map/ppermute | solution.py:353
  9.3 6.7 %collective-permute-start.4 = (f32[104,128]{1,0:T(8,128)}, f32[104,128]{1,0:T(8,128)S(1)}, u32[]{:S(2)}, u32[]{:S(2)}) collective-permute-start(f32[104,128]{1,0:T(8,128)} %get-tuple-element.42), channel_id=1, source_target_pairs={{0,24},{4,28},{8,16},{12,20},{16,8},{20,12},{24,0},{28,4},{1,25},{... | collective-permute-start | bytes 159752 | tf_op jit(solution)/shard_map/ppermute | solution.py:353
  13.6 7.1 %collective-permute-start.5 = (f32[104,128]{1,0:T(8,128)}, f32[104,128]{1,0:T(8,128)S(1)}, u32[]{:S(2)}, u32[]{:S(2)}) collective-permute-start(f32[104,128]{1,0:T(8,128)} %get-tuple-element.47), channel_id=1, source_target_pairs={{0,28},{4,24},{8,20},{12,16},{16,12},{20,8},{24,4},{28,0},{1,29},{... | collective-permute-start | bytes 159752 | tf_op jit(solution)/shard_map/ppermute | solution.py:353
  16.0 5.3 %collective-permute-start.6 = (f32[104,128]{1,0:T(8,128)}, f32[104,128]{1,0:T(8,128)S(1)}, u32[]{:S(2)}, u32[]{:S(2)}) collective-permute-start(f32[104,128]{1,0:T(8,128)} %get-tuple-element.51), channel_id=1, source_target_pairs={{0,12},{4,8},{8,4},{12,0},{16,28},{20,24},{24,20},{28,16},{1,13},{... | collective-permute-start | bytes 159752 | tf_op jit(solution)/shard_map/ppermute | solution.py:353
  16.0 9.0 %collective-permute-start.7 = (f32[576,128]{1,0:T(8,128)S(1)}, f32[576,128]{1,0:T(8,128)S(1)}, u32[]{:S(2)}, u32[]{:S(2)}) collective-permute-start(f32[576,128]{1,0:T(8,128)S(1)} %get-tuple-element.43.blocks_ref), channel_id=1, source_target_pairs={{0,2},{1,3},{2,0},{3,1},{4,6},{5,7},{6,4},{7,5},{8,10},{9,11},{10,... | collective-permute-start | bytes 884744 | tf_op jit(solution)/shard_map/ppermute | solution.py:369
  21.3 5.2 %collective-permute-start.8 = (f32[192,128]{1,0:T(8,128)S(1)}, f32[192,128]{1,0:T(8,128)S(1)}, u32[]{:S(2)}, u32[]{:S(2)}) collective-permute-start(f32[192,128]{1,0:T(8,128)S(1)} %get-tuple-element.52.blocks_ref), channel_id=1, source_target_pairs={{0,2},{1,3},{2,0},{3,1},{4,6},{5,7},{6,4},{7,5},{8,10},{9,11},{10,... | collective-permute-start | bytes 294920 | tf_op jit(solution)/shard_map/ppermute | solution.py:369
  25.0 4.6 %collective-permute-start.10 = (f32[1152,128]{1,0:T(8,128)S(1)}, f32[1152,128]{1,0:T(8,128)S(1)}, u32[]{:S(2)}, u32[]{:S(2)}) collective-permute-start(f32[1152,128]{1,0:T(8,128)S(1)} %shard_map.97.phi_ref), channel_id=1, source_target_pairs={{0,1},{1,0},{2,3},{3,2},{4,5},{5,4},{6,7},{7,6},{8,9},{9,8},{10,11... | collective-permute-start | bytes 1769480 | tf_op jit(solution)/shard_map/ppermute | solution.py:372
  26.4 3.2 %copy-start = (f32[2304,128]{1,0:T(8,128)S(1)}, f32[2304,128]{1,0:T(8,128)}, u32[]{:S(2)}) copy-start(f32[2304,128]{1,0:T(8,128)} %constant.20.clone.refs_4_) | copy-start | bytes 3538948
  26.4 3.1 %copy-start.1 = (f32[256,256]{1,0:T(8,128)S(1)}, f32[256,256]{1,0:T(8,128)}, u32[]{:S(2)}) copy-start(f32[256,256]{1,0:T(8,128)} %constant.15.clone.refs_1_) | copy-start | bytes 786436
  26.4 3.1 %copy-start.2 = (f32[256,256]{1,0:T(8,128)S(1)}, f32[256,256]{1,0:T(8,128)}, u32[]{:S(2)}) copy-start(f32[256,256]{1,0:T(8,128)} %constant.14.clone.refs_0_) | copy-start | bytes 786436
  26.5 3.1 %copy-start.3 = (f32[96,144]{1,0:T(8,128)S(1)}, f32[96,144]{1,0:T(8,128)}, u32[]{:S(2)}) copy-start(f32[96,144]{1,0:T(8,128)} %constant.17.clone.refs_3_) | copy-start | bytes 165892
  26.5 3.1 %copy-start.4 = (f32[96,144]{1,0:T(8,128)S(1)}, f32[96,144]{1,0:T(8,128)}, u32[]{:S(2)}) copy-start(f32[96,144]{1,0:T(8,128)} %constant.16.clone.refs_2_) | copy-start | bytes 165892
  28.6 4.6 %collective-permute-start.9 = (f32[1152,128]{1,0:T(8,128)S(1)}, f32[1152,128]{1,0:T(8,128)S(1)}, u32[]{:S(2)}, u32[]{:S(2)}) collective-permute-start(f32[1152,128]{1,0:T(8,128)S(1)} %shard_map.99.first_ref), channel_id=1, source_target_pairs={{0,1},{1,0},{2,3},{3,2},{4,5},{5,4},{6,7},{7,6},{8,9},{9,8},{10,11... | collective-permute-start | bytes 1769480 | tf_op jit(solution)/shard_map/ppermute | solution.py:372
  29.5 3.7 %copy-start.6 = (f32[96,384]{1,0:T(8,128)S(1)}, f32[96,384]{1,0:T(8,128)}, u32[]{:S(2)}) copy-start(f32[96,384]{1,0:T(8,128)} %constant.19.clone.stick_out_ref) | copy-start | bytes 442372
  40.1 8.7 %collective-permute-start.11 = (f32[96,128]{1,0:T(8,128)S(1)}, f32[96,128]{1,0:T(8,128)S(1)}, u32[]{:S(2)}, u32[]{:S(2)}) collective-permute-start(f32[96,128]{1,0:T(8,128)S(1)} %get-tuple-element.56), channel_id=1, source_target_pairs={{0,16},{4,20},{8,24},{12,28},{16,0},{20,4},{24,8},{28,12},{1,17},{... | collective-permute-start | bytes 147464 | tf_op jit(solution)/shard_map/ppermute | solution.py:353
  41.5 8.0 %collective-permute-start.12 = (f32[96,128]{1,0:T(8,128)S(1)}, f32[96,128]{1,0:T(8,128)S(1)}, u32[]{:S(2)}, u32[]{:S(2)}) collective-permute-start(f32[96,128]{1,0:T(8,128)S(1)} %get-tuple-element.57), channel_id=1, source_target_pairs={{0,20},{4,16},{8,28},{12,24},{16,4},{20,0},{24,12},{28,8},{1,21},{... | collective-permute-start | bytes 147464 | tf_op jit(solution)/shard_map/ppermute | solution.py:353
  43.5 7.8 %collective-permute-start.13 = (f32[96,128]{1,0:T(8,128)S(1)}, f32[96,128]{1,0:T(8,128)S(1)}, u32[]{:S(2)}, u32[]{:S(2)}) collective-permute-start(f32[96,128]{1,0:T(8,128)S(1)} %get-tuple-element.58), channel_id=1, source_target_pairs={{0,4},{4,0},{8,12},{12,8},{16,20},{20,16},{24,28},{28,24},{1,5},{5... | collective-permute-start | bytes 147464 | tf_op jit(solution)/shard_map/ppermute | solution.py:353
  44.5 6.8 %collective-permute-start.14 = (f32[96,128]{1,0:T(8,128)S(1)}, f32[96,128]{1,0:T(8,128)S(1)}, u32[]{:S(2)}, u32[]{:S(2)}) collective-permute-start(f32[96,128]{1,0:T(8,128)S(1)} %get-tuple-element.59), channel_id=1, source_target_pairs={{0,24},{4,28},{8,16},{12,20},{16,8},{20,12},{24,0},{28,4},{1,25},{... | collective-permute-start | bytes 147464 | tf_op jit(solution)/shard_map/ppermute | solution.py:353
  46.9 6.9 %collective-permute-start.15 = (f32[96,128]{1,0:T(8,128)S(1)}, f32[96,128]{1,0:T(8,128)S(1)}, u32[]{:S(2)}, u32[]{:S(2)}) collective-permute-start(f32[96,128]{1,0:T(8,128)S(1)} %get-tuple-element.60), channel_id=1, source_target_pairs={{0,28},{4,24},{8,20},{12,16},{16,12},{20,8},{24,4},{28,0},{1,29},{... | collective-permute-start | bytes 147464 | tf_op jit(solution)/shard_map/ppermute | solution.py:353
  48.8 5.0 %collective-permute-start.16 = (f32[96,128]{1,0:T(8,128)S(1)}, f32[96,128]{1,0:T(8,128)S(1)}, u32[]{:S(2)}, u32[]{:S(2)}) collective-permute-start(f32[96,128]{1,0:T(8,128)S(1)} %get-tuple-element.62), channel_id=1, source_target_pairs={{0,8},{4,12},{8,0},{12,4},{16,24},{20,28},{24,16},{28,20},{1,9},{5... | collective-permute-start | bytes 147464 | tf_op jit(solution)/shard_map/ppermute | solution.py:353
  49.4 5.0 %collective-permute-start.17 = (f32[96,128]{1,0:T(8,128)S(1)}, f32[96,128]{1,0:T(8,128)S(1)}, u32[]{:S(2)}, u32[]{:S(2)}) collective-permute-start(f32[96,128]{1,0:T(8,128)S(1)} %get-tuple-element.64), channel_id=1, source_target_pairs={{0,12},{4,8},{8,4},{12,0},{16,28},{20,24},{24,20},{28,16},{1,13},{... | collective-permute-start | bytes 147464 | tf_op jit(solution)/shard_map/ppermute | solution.py:353
  (2 other events, 1.8 us)

commit v22 on v20

--- a/solution.py
+++ b/solution.py
@@ -63,8 +63,10 @@
     coulomb[:, :, lower] = kernel
     coulomb[:, :, upper] = kernel
     stick_in, left_backward = across(stick_in), across(np.concatenate([c, s], 0))
-    early = np.zeros((LANES + 2 * g, stick_in.shape[1]), np.float32)
-    early[:LANES], early[LANES:, : left_backward.shape[1]] = stick_in, left_backward
+    high, low = rounded_parts(np.concatenate([c, -s], 1))
+    real_backward = np.block([[high, high], [low, np.zeros_like(low)]])
+    early_parts = (stick_in, left_backward, real_backward)
+    early = np.concatenate([np.pad(x, ((0, 0), (0, 6 * g - x.shape[1]))) for x in early_parts], 0).astype(np.float32)
     return dict(
         forward=down(forward),
         last_backward=down(backward / g**3),
@@ -161,10 +163,12 @@
         copy.wait()
 
 
-def early_kernel(g, own_ref, tables_ref, staged_ref, stick_in_ref, left_ref):
+def early_kernel(g, own_ref, tables_ref, staged_ref, stick_in_ref, left_ref, real_ref):
     staged_ref[...] = own_ref[...]
-    stick_in_ref[...] = tables_ref[:LANES, : stick_in_ref.shape[1]].astype(BF16)
-    left_ref[...] = tables_ref[LANES:, : left_ref.shape[1]].astype(BF16)
+    first = 0
+    for ref in (stick_in_ref, left_ref, real_ref):
+        ref[...] = tables_ref[first : first + ref.shape[0], : ref.shape[1]].astype(BF16)
+        first += ref.shape[0]
 
 
 def place_kernel(order, *refs):
@@ -207,7 +211,7 @@
         grid_ref[first : first + part.shape[0], :] = part
 
 
-def field_kernel(g, grid_ref, blocks_ref, columns_ref, stick_in_ref, left_ref, phi_ref, work_a):
+def field_kernel(g, grid_ref, blocks_ref, columns_ref, stick_in_ref, left_ref, real_ref, phi_ref, work_a):
     backward = left_ref[...]
     half = g // 2
     for first, part in placed(g, blocks_ref, columns_ref, stick_in_ref):
@@ -216,11 +220,11 @@
             slabs = left_complex(backward, part[k * g : (k + 1) * g], part[(k + 1) * g : (k + 2) * g])
             store(work_a, first // g + k, slabs)
 
-    for y in range(half):
-        x = beside(strided(work_a, y, g), strided(work_a, y + half, g))
-        (cos, cos_up), (sin, sin_up) = map(halves, left(backward, x))
-        low = lane_halves(cos.shape)
-        store(phi_ref, y, [jnp.where(low, cos - turned(sin), turned(cos_up) - sin_up)])
+    for y in range(0, half, 2):
+        real, imag = zip(*[regrouped(strided(work_a, j, g), strided(work_a, j + half, g)) for j in (y, y + 1)])
+        parts = [split(beside(*real)), split(beside(*imag))]
+        both = dot(real_ref[...], jnp.concatenate([x[k] for k in range(2) for x in parts], 0))
+        store(phi_ref, y, halves(both[:g] + both[g:]))
 
 
 def pick_kernel(g, columns_ref, hot_ref):
@@ -380,10 +384,10 @@
         space=pltpu.HBM,
         grant=SEND_GRANT,
     )
-    shapes = [(2 * g + 8, slots), (LANES, 6 * g), (2 * g, 3 * g)]
+    shapes = [(2 * g + 8, slots), (LANES, 6 * g), (2 * g, 3 * g), (2 * g, 4 * g)]
     staged, *first_tables = call(
         functools.partial(early_kernel, g),
-        [jax.ShapeDtypeStruct(shape, kind) for shape, kind in zip(shapes, (F32, BF16, BF16))],
+        [jax.ShapeDtypeStruct(shape, kind) for shape, kind in zip(shapes, (F32, BF16, BF16, BF16))],
         [],
         1,
         sent[0],
@@ -399,7 +403,7 @@
     cut = owners * 3 // 4
     order = [0] + mixed
     order = order[:cut] + order[:cut - 1:-1]
-    stick_in, left_table = first_tables
+    stick_in, *field_tables = first_tables
 
     def relayed(part):
         shapes = [(len(part) * 2 * g, slots), (8, len(part) * slots)]
@@ -411,7 +415,7 @@
         return call(functools.partial(place_sticks_kernel, g), grid, [], flops, blocks, columns[0], stick_in)
 
     def orbital(grid, rest):
-        operands = (grid, rest, columns[1], stick_in, left_table)
+        operands = (grid, rest, columns[1], stick_in, *field_tables)
         return call(functools.partial(field_kernel, g), field, [work], 1, *operands)
 
     first_blocks, first_columns = relayed(order[:cut])

time: 55.9 us -> 55.3 us (0.989)
  Pallas kernels: 21.3 us -> 20.7 us
    pallas_call x13, Pallas kernels: 21.3 us -> 20.7 us  [call(): pl.pallas_call(kernel, out_shape=out_shapes, in_specs=[pl.BlockSpec(memor...]
where the time goes in v22:
time: 55.3 us; the launch traced here: 55 us
  starting transfers between devices  26.4 us (48%)
  Pallas kernels  20.7 us (37%)
  waiting for transfers between devices  5.89 us (11%)
  local copies, waits for them, and re-layouts  1.88 us (3%)
    ppermute x14, starting transfers between devices, exchanged(): moved[d] = lax.ppermute(block, 'stick', [(i, i ^ d) for i in range(owners)])  22.6 us
    pallas_call x13, Pallas kernels, call(): pl.pallas_call(kernel, out_shape=out_shapes, in_specs=[pl.BlockSpec(memor...  20.7 us
    ppermute x14, waiting for transfers between devices, exchanged(): moved[d] = lax.ppermute(block, 'stick', [(i, i ^ d) for i in range(owners)])  5.88 us
    ppermute x2, starting transfers between devices, shifted(): lax.ppermute(x, 'band', [(i, (i - distance) % groups) for i in range(grou...  3.11 us
    unnamed x16, local copies, waits for them, and re-layouts  1.88 us
  transfers between devices with their start and end apart: 18, of which 5 were waited for; matrix products, arithmetic and copies ran while one was open for 0% of the time, Pallas kernels for 21%

profile of v22, /device:TPU:0, one launch (start us, length us, event | category | flops | bytes accessed | tf_op | source)
XLA Modules:
  0.0 55.0 jit_solution(3765238828621483375)
XLA Ops:
  0.0 1.8 %shard_map.91 = (f32[104,128]{1,0:T(8,128)}, f32[104,128]{1,0:T(8,128)}, f32[104,128]{1,0:T(8,128)}, f32[104,128]{1,0:T(8,128)}, f32[104,128]{1,0:T(8,128)}, /*i...) custom-call(f32[8,96,128]{2,1,0:T(8,128)} %sticks_ref.1, s32[1,128]{1,0:T(1,128)} %bitcast.1), custom_call_target="tpu_custom_call" | custom-call | flops 1 | bytes 1 | tf_op jit(solution)/shard_map/pallas_call | solution.py:331
  1.8 4.1 %collective-permute-start = (f32[104,128]{1,0:T(8,128)}, f32[104,128]{1,0:T(8,128)S(1)}, u32[]{:S(2)}, u32[]{:S(2)}) collective-permute-start(f32[104,128]{1,0:T(8,128)} %get-tuple-element.39), channel_id=1, source_target_pairs={{0,16},{4,20},{8,24},{12,28},{16,0},{20,4},{24,8},{28,12},{1,17},{... | collective-permute-start | bytes 159752 | tf_op jit(solution)/shard_map/ppermute | solution.py:352
  5.9 1.5 %collective-permute-start.1 = (f32[104,128]{1,0:T(8,128)}, f32[104,128]{1,0:T(8,128)S(1)}, u32[]{:S(2)}, u32[]{:S(2)}) collective-permute-start(f32[104,128]{1,0:T(8,128)} %get-tuple-element.40), channel_id=1, source_target_pairs={{0,4},{4,0},{8,12},{12,8},{16,20},{20,16},{24,28},{28,24},{1,5},{5... | collective-permute-start | bytes 159752 | tf_op jit(solution)/shard_map/ppermute | solution.py:352
  7.5 1.8 %collective-permute-start.3 = (f32[104,128]{1,0:T(8,128)}, f32[104,128]{1,0:T(8,128)S(1)}, u32[]{:S(2)}, u32[]{:S(2)}) collective-permute-start(f32[104,128]{1,0:T(8,128)} %get-tuple-element.42), channel_id=1, source_target_pairs={{0,8},{4,12},{8,0},{12,4},{16,24},{20,28},{24,16},{28,20},{1,9},{5... | collective-permute-start | bytes 159752 | tf_op jit(solution)/shard_map/ppermute | solution.py:352
  9.3 2.5 %collective-permute-start.4 = (f32[104,128]{1,0:T(8,128)}, f32[104,128]{1,0:T(8,128)S(1)}, u32[]{:S(2)}, u32[]{:S(2)}) collective-permute-start(f32[104,128]{1,0:T(8,128)} %get-tuple-element.43), channel_id=1, source_target_pairs={{0,24},{4,28},{8,16},{12,20},{16,8},{20,12},{24,0},{28,4},{1,25},{... | collective-permute-start | bytes 159752 | tf_op jit(solution)/shard_map/ppermute | solution.py:352
  11.8 1.0 %copy-done.3 = f32[320,288]{1,0:T(8,128)S(1)} copy-done((f32[320,288]{1,0:T(8,128)S(1)}, f32[320,288]{1,0:T(8,128)}, u32[]{:S(2)}) %copy-start.3) | copy-done | bytes 368664
  13.6 2.4 %collective-permute-start.5 = (f32[104,128]{1,0:T(8,128)}, f32[104,128]{1,0:T(8,128)S(1)}, u32[]{:S(2)}, u32[]{:S(2)}) collective-permute-start(f32[104,128]{1,0:T(8,128)} %get-tuple-element.48), channel_id=1, source_target_pairs={{0,28},{4,24},{8,20},{12,16},{16,12},{20,8},{24,4},{28,0},{1,29},{... | collective-permute-start | bytes 159752 | tf_op jit(solution)/shard_map/ppermute | solution.py:352
  16.1 1.6 %collective-permute-start.7 = (f32[576,128]{1,0:T(8,128)S(1)}, f32[576,128]{1,0:T(8,128)S(1)}, u32[]{:S(2)}, u32[]{:S(2)}) collective-permute-start(f32[576,128]{1,0:T(8,128)S(1)} %get-tuple-element.44.blocks_ref), channel_id=1, source_target_pairs={{0,2},{1,3},{2,0},{3,1},{4,6},{5,7},{6,4},{7,5},{8,10},{9,11},{10,... | collective-permute-start | bytes 884744 | tf_op jit(solution)/shard_map/ppermute | solution.py:368
  17.6 1.3 %shard_map.94.grid_ref = f32[2304,128]{1,0:T(8,128)S(1)} custom-call(f32[576,128]{1,0:T(8,128)S(1)} %get-tuple-element.44.blocks_ref, f32[8,768]{1,0:T(8,128)S(1)} %get-tuple-element.45.columns_ref, bf16[128,288]{1,0:T(8,128)(2,1)S(1)} %get-tuple-element.46.stick_in_ref), custom_call_target="tpu_custom_call" | custom-call | flops 5000000000 | bytes 5000000000 | tf_op jit(solution)/shard_map/pallas_call | solution.py:331
  19.0 0.9 %shard_map.95.hot_ref = bf16[768,2304]{1,0:T(8,128)(2,1)S(1)} custom-call(f32[8,768]{1,0:T(8,128)S(1)} %get-tuple-element.45.columns_ref), custom_call_target="tpu_custom_call" | custom-call | flops 1 | bytes 1 | tf_op jit(solution)/shard_map/pallas_call | solution.py:331
  19.9 0.8 %collective-permute-done.5.refs_0_ = f32[104,128]{1,0:T(8,128)S(1)} collective-permute-done((f32[104,128]{1,0:T(8,128)}, f32[104,128]{1,0:T(8,128)S(1)}, u32[]{:S(2)}, u32[]{:S(2)}) %collective-permute-start.5) | collective-permute-done | bytes 53280 | tf_op jit(solution)/shard_map/ppermute | solution.py:352
  21.3 1.6 %collective-permute-start.8 = (f32[192,128]{1,0:T(8,128)S(1)}, f32[192,128]{1,0:T(8,128)S(1)}, u32[]{:S(2)}, u32[]{:S(2)}) collective-permute-start(f32[192,128]{1,0:T(8,128)S(1)} %get-tuple-element.54.blocks_ref), channel_id=1, source_target_pairs={{0,2},{1,3},{2,0},{3,1},{4,6},{5,7},{6,4},{7,5},{8,10},{9,11},{10,... | collective-permute-start | bytes 294920 | tf_op jit(solution)/shard_map/ppermute | solution.py:368
  22.9 1.8 %shard_map.97.phi_ref = f32[1152,128]{1,0:T(8,128)S(1)} custom-call(f32[2304,128]{1,0:T(8,128)S(1)} %shard_map.94.grid_ref, f32[192,128]{1,0:T(8,128)S(1)} %get-tuple-element.54.blocks_ref, f32[8,256]{1,0:T(8,128)S(1)} %get-tuple-element.55.columns_ref, bf16[128,288]{1,0:T(8,128)(2,1)S(1)} %get-tuple-element.46.stick_in_ref, ...), custom_call_target="tpu_custom_call" | custom-call | flops 1 | bytes 1 | tf_op jit(solution)/shard_map/pallas_call | solution.py:331
  24.8 1.3 %shard_map.98.grid_ref = f32[2304,128]{1,0:T(8,128)S(1)} custom-call(f32[576,128]{1,0:T(8,128)S(1)} %collective-permute-done.7.blocks_ref, f32[8,768]{1,0:T(8,128)S(1)} %get-tuple-element.45.columns_ref, bf16[128,288]{1,0:T(8,128)(2,1)S(1)} %get-tuple-element.46.stick_in_ref), custom_call_target="tpu_custom_call" | custom-call | flops 1 | bytes 1 | tf_op jit(solution)/shard_map/pallas_call | solution.py:331
  26.2 1.8 %shard_map.99.first_ref = f32[1152,128]{1,0:T(8,128)S(1)} custom-call(f32[2304,128]{1,0:T(8,128)S(1)} %shard_map.98.grid_ref, f32[192,128]{1,0:T(8,128)S(1)} %collective-permute-done.8.blocks_ref, f32[8,256]{1,0:T(8,128)S(1)} %get-tuple-element.55.columns_ref, bf16[128,288]{1,0:T(8,128)(2,1)S(1)} %get-tuple-element.46.stick_in_ref, ...), custom_call_target="tpu_custom_call" | custom-call | flops 1 | bytes 1 | tf_op jit(solution)/shard_map/pallas_call | solution.py:331
  29.1 3.6 %shard_map.100.before_ref = f32[1152,128]{1,0:T(8,128)S(1)} custom-call(f32[1152,128]{1,0:T(8,128)S(1)} %shard_map.97.phi_ref, f32[1152,128]{1,0:T(8,128)S(1)} %collective-permute-done.10.other_ref, f32[256,256]{1,0:T(8,128)S(1)} %copy-done.2, f32[256,256]{1,0:T(8,128)S(1)} %copy-done.1, f32[96,144]{1,0:T(8,128)S(1)} %copy-done.5, f32[96,144]{1,0:T(8,128)S(1)} %copy-done.4, ...), custom_call_target="tpu_custom_call" | custom-call | flops 1 | bytes 1 | tf_op jit(solution)/shard_map/pallas_call | solution.py:331
  32.7 6.8 %shard_map.102 = (f32[96,128]{1,0:T(8,128)S(1)}, f32[96,128]{1,0:T(8,128)S(1)}, f32[96,128]{1,0:T(8,128)S(1)}, f32[96,128]{1,0:T(8,128)S(1)}, f32[96,128]{1,0:T(...) custom-call(f32[1152,128]{1,0:T(8,128)S(1)} %shard_map.97.phi_ref, ...), custom_call_target="tpu_custom_call" | custom-call | flops 1 | bytes 1 | tf_op jit(solution)/shard_map/pallas_call | solution.py:331
  39.5 1.7 %collective-permute-start.11 = (f32[96,128]{1,0:T(8,128)S(1)}, f32[96,128]{1,0:T(8,128)S(1)}, u32[]{:S(2)}, u32[]{:S(2)}) collective-permute-start(f32[96,128]{1,0:T(8,128)S(1)} %get-tuple-element.58), channel_id=1, source_target_pairs={{0,16},{4,20},{8,24},{12,28},{16,0},{20,4},{24,8},{28,12},{1,17},{... | collective-permute-start | bytes 147464 | tf_op jit(solution)/shard_map/ppermute | solution.py:352
  41.2 1.5 %collective-permute-start.12 = (f32[96,128]{1,0:T(8,128)S(1)}, f32[96,128]{1,0:T(8,128)S(1)}, u32[]{:S(2)}, u32[]{:S(2)}) collective-permute-start(f32[96,128]{1,0:T(8,128)S(1)} %get-tuple-element.59), channel_id=1, source_target_pairs={{0,4},{4,0},{8,12},{12,8},{16,20},{20,16},{24,28},{28,24},{1,5},{5... | collective-permute-start | bytes 147464 | tf_op jit(solution)/shard_map/ppermute | solution.py:352
  42.8 1.2 %collective-permute-start.13 = (f32[96,128]{1,0:T(8,128)S(1)}, f32[96,128]{1,0:T(8,128)S(1)}, u32[]{:S(2)}, u32[]{:S(2)}) collective-permute-start(f32[96,128]{1,0:T(8,128)S(1)} %get-tuple-element.60), channel_id=1, source_target_pairs={{0,20},{4,16},{8,28},{12,24},{16,4},{20,0},{24,12},{28,8},{1,21},{... | collective-permute-start | bytes 147464 | tf_op jit(solution)/shard_map/ppermute | solution.py:352
  44.6 2.5 %collective-permute-start.15 = (f32[96,128]{1,0:T(8,128)S(1)}, f32[96,128]{1,0:T(8,128)S(1)}, u32[]{:S(2)}, u32[]{:S(2)}) collective-permute-start(f32[96,128]{1,0:T(8,128)S(1)} %get-tuple-element.62), channel_id=1, source_target_pairs={{0,24},{4,28},{8,16},{12,20},{16,8},{20,12},{24,0},{28,4},{1,25},{... | collective-permute-start | bytes 147464 | tf_op jit(solution)/shard_map/ppermute | solution.py:352
  47.4 2.4 %collective-permute-start.17 = (f32[96,128]{1,0:T(8,128)S(1)}, f32[96,128]{1,0:T(8,128)S(1)}, u32[]{:S(2)}, u32[]{:S(2)}) collective-permute-start(f32[96,128]{1,0:T(8,128)S(1)} %get-tuple-element.66), channel_id=1, source_target_pairs={{0,28},{4,24},{8,20},{12,16},{16,12},{20,8},{24,4},{28,0},{1,29},{... | collective-permute-start | bytes 147464 | tf_op jit(solution)/shard_map/ppermute | solution.py:352
  50.6 2.0 %collective-permute-done.16.refs_6_ = f32[96,128]{1,0:T(8,128)S(1)} collective-permute-done((f32[96,128]{1,0:T(8,128)S(1)}, f32[96,128]{1,0:T(8,128)S(1)}, u32[]{:S(2)}, u32[]{:S(2)}) %collective-permute-start.16) | collective-permute-done | bytes 49184 | tf_op jit(solution)/shard_map/ppermute | solution.py:352
  52.6 1.7 %collective-permute-done.17.refs_7_ = f32[96,128]{1,0:T(8,128)S(1)} collective-permute-done((f32[96,128]{1,0:T(8,128)S(1)}, f32[96,128]{1,0:T(8,128)S(1)}, u32[]{:S(2)}, u32[]{:S(2)}) %collective-permute-start.17) | collective-permute-done | bytes 49184 | tf_op jit(solution)/shard_map/ppermute | solution.py:352
  (41 shorter events, 5.1 us)
Async XLA Ops:
  1.8 11.8 %collective-permute-start = (f32[104,128]{1,0:T(8,128)}, f32[104,128]{1,0:T(8,128)S(1)}, u32[]{:S(2)}, u32[]{:S(2)}) collective-permute-start(f32[104,128]{1,0:T(8,128)} %get-tuple-element.39), channel_id=1, source_target_pairs={{0,16},{4,20},{8,24},{12,28},{16,0},{20,4},{24,8},{28,12},{1,17},{... | collective-permute-start | bytes 159752 | tf_op jit(solution)/shard_map/ppermute | solution.py:352
  5.9 10.1 %collective-permute-start.1 = (f32[104,128]{1,0:T(8,128)}, f32[104,128]{1,0:T(8,128)S(1)}, u32[]{:S(2)}, u32[]{:S(2)}) collective-permute-start(f32[104,128]{1,0:T(8,128)} %get-tuple-element.40), channel_id=1, source_target_pairs={{0,4},{4,0},{8,12},{12,8},{16,20},{20,16},{24,28},{28,24},{1,5},{5... | collective-permute-start | bytes 159752 | tf_op jit(solution)/shard_map/ppermute | solution.py:352
  7.4 8.6 %collective-permute-start.2 = (f32[104,128]{1,0:T(8,128)}, f32[104,128]{1,0:T(8,128)S(1)}, u32[]{:S(2)}, u32[]{:S(2)}) collective-permute-start(f32[104,128]{1,0:T(8,128)} %get-tuple-element.41), channel_id=1, source_target_pairs={{0,20},{4,16},{8,28},{12,24},{16,4},{20,0},{24,12},{28,8},{1,21},{... | collective-permute-start | bytes 159752 | tf_op jit(solution)/shard_map/ppermute | solution.py:352
  7.5 8.6 %collective-permute-start.3 = (f32[104,128]{1,0:T(8,128)}, f32[104,128]{1,0:T(8,128)S(1)}, u32[]{:S(2)}, u32[]{:S(2)}) collective-permute-start(f32[104,128]{1,0:T(8,128)} %get-tuple-element.42), channel_id=1, source_target_pairs={{0,8},{4,12},{8,0},{12,4},{16,24},{20,28},{24,16},{28,20},{1,9},{5... | collective-permute-start | bytes 159752 | tf_op jit(solution)/shard_map/ppermute | solution.py:352
  9.3 6.8 %collective-permute-start.4 = (f32[104,128]{1,0:T(8,128)}, f32[104,128]{1,0:T(8,128)S(1)}, u32[]{:S(2)}, u32[]{:S(2)}) collective-permute-start(f32[104,128]{1,0:T(8,128)} %get-tuple-element.43), channel_id=1, source_target_pairs={{0,24},{4,28},{8,16},{12,20},{16,8},{20,12},{24,0},{28,4},{1,25},{... | collective-permute-start | bytes 159752 | tf_op jit(solution)/shard_map/ppermute | solution.py:352
  13.6 7.1 %collective-permute-start.5 = (f32[104,128]{1,0:T(8,128)}, f32[104,128]{1,0:T(8,128)S(1)}, u32[]{:S(2)}, u32[]{:S(2)}) collective-permute-start(f32[104,128]{1,0:T(8,128)} %get-tuple-element.48), channel_id=1, source_target_pairs={{0,28},{4,24},{8,20},{12,16},{16,12},{20,8},{24,4},{28,0},{1,29},{... | collective-permute-start | bytes 159752 | tf_op jit(solution)/shard_map/ppermute | solution.py:352
  16.0 5.3 %collective-permute-start.6 = (f32[104,128]{1,0:T(8,128)}, f32[104,128]{1,0:T(8,128)S(1)}, u32[]{:S(2)}, u32[]{:S(2)}) collective-permute-start(f32[104,128]{1,0:T(8,128)} %get-tuple-element.53), channel_id=1, source_target_pairs={{0,12},{4,8},{8,4},{12,0},{16,28},{20,24},{24,20},{28,16},{1,13},{... | collective-permute-start | bytes 159752 | tf_op jit(solution)/shard_map/ppermute | solution.py:352
  16.1 8.7 %collective-permute-start.7 = (f32[576,128]{1,0:T(8,128)S(1)}, f32[576,128]{1,0:T(8,128)S(1)}, u32[]{:S(2)}, u32[]{:S(2)}) collective-permute-start(f32[576,128]{1,0:T(8,128)S(1)} %get-tuple-element.44.blocks_ref), channel_id=1, source_target_pairs={{0,2},{1,3},{2,0},{3,1},{4,6},{5,7},{6,4},{7,5},{8,10},{9,11},{10,... | collective-permute-start | bytes 884744 | tf_op jit(solution)/shard_map/ppermute | solution.py:368
  21.3 4.9 %collective-permute-start.8 = (f32[192,128]{1,0:T(8,128)S(1)}, f32[192,128]{1,0:T(8,128)S(1)}, u32[]{:S(2)}, u32[]{:S(2)}) collective-permute-start(f32[192,128]{1,0:T(8,128)S(1)} %get-tuple-element.54.blocks_ref), channel_id=1, source_target_pairs={{0,2},{1,3},{2,0},{3,1},{4,6},{5,7},{6,4},{7,5},{8,10},{9,11},{10,... | collective-permute-start | bytes 294920 | tf_op jit(solution)/shard_map/ppermute | solution.py:368
  24.7 4.3 %collective-permute-start.10 = (f32[1152,128]{1,0:T(8,128)S(1)}, f32[1152,128]{1,0:T(8,128)S(1)}, u32[]{:S(2)}, u32[]{:S(2)}) collective-permute-start(f32[1152,128]{1,0:T(8,128)S(1)} %shard_map.97.phi_ref), channel_id=1, source_target_pairs={{0,1},{1,0},{2,3},{3,2},{4,5},{5,4},{6,7},{7,6},{8,9},{9,8},{10,11... | collective-permute-start | bytes 1769480 | tf_op jit(solution)/shard_map/ppermute | solution.py:371
  26.2 2.9 %copy-start = (f32[2304,128]{1,0:T(8,128)S(1)}, f32[2304,128]{1,0:T(8,128)}, u32[]{:S(2)}) copy-start(f32[2304,128]{1,0:T(8,128)} %constant.20.clone.refs_4_) | copy-start | bytes 3538948
  26.2 2.9 %copy-start.1 = (f32[256,256]{1,0:T(8,128)S(1)}, f32[256,256]{1,0:T(8,128)}, u32[]{:S(2)}) copy-start(f32[256,256]{1,0:T(8,128)} %constant.15.clone.refs_1_) | copy-start | bytes 786436
  26.2 2.8 %copy-start.2 = (f32[256,256]{1,0:T(8,128)S(1)}, f32[256,256]{1,0:T(8,128)}, u32[]{:S(2)}) copy-start(f32[256,256]{1,0:T(8,128)} %constant.14.clone.refs_0_) | copy-start | bytes 786436
  26.2 2.8 %copy-start.4 = (f32[96,144]{1,0:T(8,128)S(1)}, f32[96,144]{1,0:T(8,128)}, u32[]{:S(2)}) copy-start(f32[96,144]{1,0:T(8,128)} %constant.17.clone.refs_3_) | copy-start | bytes 165892
  26.2 2.8 %copy-start.5 = (f32[96,144]{1,0:T(8,128)S(1)}, f32[96,144]{1,0:T(8,128)}, u32[]{:S(2)}) copy-start(f32[96,144]{1,0:T(8,128)} %constant.16.clone.refs_2_) | copy-start | bytes 165892
  28.1 4.6 %collective-permute-start.9 = (f32[1152,128]{1,0:T(8,128)S(1)}, f32[1152,128]{1,0:T(8,128)S(1)}, u32[]{:S(2)}, u32[]{:S(2)}) collective-permute-start(f32[1152,128]{1,0:T(8,128)S(1)} %shard_map.99.first_ref), channel_id=1, source_target_pairs={{0,1},{1,0},{2,3},{3,2},{4,5},{5,4},{6,7},{7,6},{8,9},{9,8},{10,11... | collective-permute-start | bytes 1769480 | tf_op jit(solution)/shard_map/ppermute | solution.py:371
  29.0 3.7 %copy-start.6 = (f32[96,384]{1,0:T(8,128)S(1)}, f32[96,384]{1,0:T(8,128)}, u32[]{:S(2)}) copy-start(f32[96,384]{1,0:T(8,128)} %constant.19.clone.stick_out_ref) | copy-start | bytes 442372
  39.5 7.6 %collective-permute-start.11 = (f32[96,128]{1,0:T(8,128)S(1)}, f32[96,128]{1,0:T(8,128)S(1)}, u32[]{:S(2)}, u32[]{:S(2)}) collective-permute-start(f32[96,128]{1,0:T(8,128)S(1)} %get-tuple-element.58), channel_id=1, source_target_pairs={{0,16},{4,20},{8,24},{12,28},{16,0},{20,4},{24,8},{28,12},{1,17},{... | collective-permute-start | bytes 147464 | tf_op jit(solution)/shard_map/ppermute | solution.py:352
  41.2 6.2 %collective-permute-start.12 = (f32[96,128]{1,0:T(8,128)S(1)}, f32[96,128]{1,0:T(8,128)S(1)}, u32[]{:S(2)}, u32[]{:S(2)}) collective-permute-start(f32[96,128]{1,0:T(8,128)S(1)} %get-tuple-element.59), channel_id=1, source_target_pairs={{0,4},{4,0},{8,12},{12,8},{16,20},{20,16},{24,28},{28,24},{1,5},{5... | collective-permute-start | bytes 147464 | tf_op jit(solution)/shard_map/ppermute | solution.py:352
  42.8 7.1 %collective-permute-start.13 = (f32[96,128]{1,0:T(8,128)S(1)}, f32[96,128]{1,0:T(8,128)S(1)}, u32[]{:S(2)}, u32[]{:S(2)}) collective-permute-start(f32[96,128]{1,0:T(8,128)S(1)} %get-tuple-element.60), channel_id=1, source_target_pairs={{0,20},{4,16},{8,28},{12,24},{16,4},{20,0},{24,12},{28,8},{1,21},{... | collective-permute-start | bytes 147464 | tf_op jit(solution)/shard_map/ppermute | solution.py:352
  43.9 5.9 %collective-permute-start.14 = (f32[96,128]{1,0:T(8,128)S(1)}, f32[96,128]{1,0:T(8,128)S(1)}, u32[]{:S(2)}, u32[]{:S(2)}) collective-permute-start(f32[96,128]{1,0:T(8,128)S(1)} %get-tuple-element.61), channel_id=1, source_target_pairs={{0,8},{4,12},{8,0},{12,4},{16,24},{20,28},{24,16},{28,20},{1,9},{5... | collective-permute-start | bytes 147464 | tf_op jit(solution)/shard_map/ppermute | solution.py:352
  44.6 6.0 %collective-permute-start.15 = (f32[96,128]{1,0:T(8,128)S(1)}, f32[96,128]{1,0:T(8,128)S(1)}, u32[]{:S(2)}, u32[]{:S(2)}) collective-permute-start(f32[96,128]{1,0:T(8,128)S(1)} %get-tuple-element.62), channel_id=1, source_target_pairs={{0,24},{4,28},{8,16},{12,20},{16,8},{20,12},{24,0},{28,4},{1,25},{... | collective-permute-start | bytes 147464 | tf_op jit(solution)/shard_map/ppermute | solution.py:352
  47.1 5.5 %collective-permute-start.16 = (f32[96,128]{1,0:T(8,128)S(1)}, f32[96,128]{1,0:T(8,128)S(1)}, u32[]{:S(2)}, u32[]{:S(2)}) collective-permute-start(f32[96,128]{1,0:T(8,128)S(1)} %get-tuple-element.64), channel_id=1, source_target_pairs={{0,12},{4,8},{8,4},{12,0},{16,28},{20,24},{24,20},{28,16},{1,13},{... | collective-permute-start | bytes 147464 | tf_op jit(solution)/shard_map/ppermute | solution.py:352
  47.4 6.8 %collective-permute-start.17 = (f32[96,128]{1,0:T(8,128)S(1)}, f32[96,128]{1,0:T(8,128)S(1)}, u32[]{:S(2)}, u32[]{:S(2)}) collective-permute-start(f32[96,128]{1,0:T(8,128)S(1)} %get-tuple-element.66), channel_id=1, source_target_pairs={{0,28},{4,24},{8,20},{12,16},{16,12},{20,8},{24,4},{28,0},{1,29},{... | collective-permute-start | bytes 147464 | tf_op jit(solution)/shard_map/ppermute | solution.py:352
  (2 other events, 1.8 us)

commit v23 on v22

--- a/solution.py
+++ b/solution.py
@@ -35,6 +35,11 @@
 def down(table):
     high, low = rounded_parts(table)
     return np.block([[high, low], [high, np.zeros_like(low)]]).astype(np.float32)
+
+
+def over_rows(table):
+    high, low = rounded_parts(table)
+    return np.block([[high, high], [low, np.zeros_like(low)]]).astype(np.float32)
 
 
 def make_tables(g):
@@ -62,15 +67,16 @@
     coulomb = np.zeros((g, g, LANES), np.float32)
     coulomb[:, :, lower] = kernel
     coulomb[:, :, upper] = kernel
-    stick_in, left_backward = across(stick_in), across(np.concatenate([c, s], 0))
-    high, low = rounded_parts(np.concatenate([c, -s], 1))
-    real_backward = np.block([[high, high], [low, np.zeros_like(low)]])
+    stick_in = across(stick_in)
+    real_backward = over_rows(np.concatenate([c, -s], 1))
+    left_forward, left_backward = over_rows(np.block([[c, s], [-s, c]])), over_rows(np.block([[c, -s], [s, c]]))
     early_parts = (stick_in, left_backward, real_backward)
     early = np.concatenate([np.pad(x, ((0, 0), (0, 6 * g - x.shape[1]))) for x in early_parts], 0).astype(np.float32)
     return dict(
         forward=down(forward),
         last_backward=down(backward / g**3),
-        left_forward=across(np.concatenate([c, -s], 0)),
+        real_forward=across(np.concatenate([c, -s], 0)),
+        left_forward=left_forward,
         left_backward=left_backward,
         early=early,
         stick_out=across(stick_out * g**-1.5),
@@ -120,10 +126,27 @@
     return both[:g], both[g:]
 
 
-def left_complex(table, a, b):
-    cos, sin = left(table, beside(a, b))
-    sign = jnp.where(lane_halves((1, LANES)), -1.0, 1.0)
-    return [p + turned(q) * sign for p, q in zip(halves(cos), halves(sin))]
+def packed(slabs):
+    real, imag = zip(*[regrouped(slabs[k], slabs[k + 1]) for k in (0, 2)])
+    return beside(*real), beside(*imag)
+
+
+def unpacked(real, imag):
+    slabs = []
+    for pair in zip(halves(real), halves(imag)):
+        slabs += regrouped(*pair)
+    return slabs
+
+
+def left_packed(table, real, imag):
+    parts = [split(real), split(imag)]
+    both = dot(table, jnp.concatenate([x[k] for k in range(2) for x in parts], 0))
+    out = both[: both.shape[0] // 2] + both[both.shape[0] // 2 :]
+    return out[: real.shape[0]], out[real.shape[0] :]
+
+
+def left_complex(table, slabs):
+    return unpacked(*left_packed(table, *packed(slabs)))
 
 
 def right(x, table):
@@ -216,13 +239,13 @@
     half = g // 2
     for first, part in placed(g, blocks_ref, columns_ref, stick_in_ref):
         part = part + grid_ref[first : first + part.shape[0], :]
-        for k in range(0, half, 2):
-            slabs = left_complex(backward, part[k * g : (k + 1) * g], part[(k + 1) * g : (k + 2) * g])
+        for k in range(0, half, 4):
+            slabs = left_complex(backward, [part[j * g : (j + 1) * g] for j in range(k, k + 4)])
             store(work_a, first // g + k, slabs)
 
     for y in range(0, half, 2):
-        real, imag = zip(*[regrouped(strided(work_a, j, g), strided(work_a, j + half, g)) for j in (y, y + 1)])
-        parts = [split(beside(*real)), split(beside(*imag))]
+        real, imag = packed([strided(work_a, j, g) for j in (y, y + half, y + 1, y + 1 + half)])
+        parts = [split(real), split(imag)]
         both = dot(real_ref[...], jnp.concatenate([x[k] for k in range(2) for x in parts], 0))
         store(phi_ref, y, halves(both[:g] + both[g:]))
 
@@ -245,22 +268,25 @@
         phi = phi_ref[rows, :]
         lower, upper = regrouped(phi * first_ref[rows, :], phi * second_ref[rows, :])
         spectrum = right(jnp.concatenate([lower, upper], 0), forward)
-        for k in range(PAIRS):
-            a, b = left_complex(left_forward, *(spectrum[j * g : (j + 1) * g] for j in (k, k + PAIRS)))
-            store(work_a, start + k, [a])
-            store(work_a, start + k + half, [b])
-
-    for kx in range(0, g, 2):
-        slabs = left_complex(left_forward, strided(work_a, kx, g), strided(work_a, kx + 1, g))
-        slabs = [slab * coulomb_ref[slab_rows(kx + j, g), :] for j, slab in enumerate(slabs)]
-        store(work_b, kx, left_complex(left_backward, *slabs))
+        for k in range(0, PAIRS, 2):
+            chosen = (k, k + PAIRS, k + 1, k + 1 + PAIRS)
+            slabs = left_complex(left_forward, [spectrum[j * g : (j + 1) * g] for j in chosen])
+            store(work_a, start + k, slabs[::2])
+            store(work_a, start + k + half, slabs[1::2])
+
+    for kx in range(0, g, 4):
+        real, imag = left_packed(left_forward, *packed([strided(work_a, kx + j, g) for j in range(4)]))
+        factors = [coulomb_ref[slab_rows(kx + j, g), :] for j in range(4)]
+        low = lane_halves(factors[0].shape)
+        factor = beside(*[jnp.where(low, factors[j], factors[j + 1]) for j in (0, 2)])
+        store(work_b, kx, unpacked(*left_packed(left_backward, real * factor, imag * factor)))
 
     for start in range(0, half, last):
         lower, upper = [], []
-        for z in range(start, start + last):
-            a, b = left_complex(left_backward, strided(work_b, z, g), strided(work_b, z + half, g))
-            lower.append(a)
-            upper.append(b)
+        for y in range(start, start + last, 2):
+            slabs = left_complex(left_backward, [strided(work_b, j, g) for j in (y, y + half, y + 1, y + 1 + half)])
+            lower += slabs[::2]
+            upper += slabs[1::2]
         out = right(jnp.concatenate(lower + upper, 0), last_backward)
         emit(start, *regrouped(out[: last * g], out[last * g :]))
 
@@ -285,10 +311,10 @@
     potentials(g, phi_ref, first_ref, second_ref, tables, work_a, work_b, emit)
 
 
-def far_kernel(g, weights, phi_ref, first_ref, second_ref, before_ref, hot_ref, last_hot_ref, stick_out_ref, *refs):
+def far_kernel(g, weights, phi_ref, first_ref, second_ref, before_ref, hot_ref, last_hot_ref, stick_out_ref, real_forward_ref, *refs):
     tables, out_refs = refs[:5], refs[5:-3]
     work_a, work_b, picked_ref = refs[-3:]
-    forward = tables[2][...].astype(BF16)
+    forward, real_forward = tables[2][...].astype(BF16), real_forward_ref[...].astype(BF16)
     half = g // 2
 
     def emit(start, first, second):
@@ -296,7 +322,7 @@
         total = before_ref[rows, :] + weights[0] * (first * first_ref[rows, :])
         total = total + weights[1] * (second * second_ref[rows, :])
         for k in range(0, half, 2):
-            cos, sin = left(forward, beside(total[k * g : (k + 1) * g], total[(k + 1) * g : (k + 2) * g]))
+            cos, sin = left(real_forward, beside(total[k * g : (k + 1) * g], total[(k + 1) * g : (k + 2) * g]))
             for j, (real, imag) in enumerate(zip(halves(cos), halves(sin))):
                 lower, upper = regrouped(real, imag)
                 store(work_a, start + k + j, [lower])
@@ -307,8 +333,8 @@
     step = g // 3
     for first in range(0, g, step):
         slabs = []
-        for kx in range(first, first + step, 2):
-            slabs += left_complex(forward, strided(work_a, kx, g), strided(work_a, kx + 1, g))
+        for kx in range(first, first + step, 4):
+            slabs += left_complex(forward, [strided(work_a, kx + j, g) for j in range(4)])
         spectrum = beside(*split(jnp.concatenate(slabs, 0)))
         start = 0
         for ref in (hot_ref, last_hot_ref):
@@ -384,7 +410,7 @@
         space=pltpu.HBM,
         grant=SEND_GRANT,
     )
-    shapes = [(2 * g + 8, slots), (LANES, 6 * g), (2 * g, 3 * g), (2 * g, 4 * g)]
+    shapes = [(2 * g + 8, slots), (LANES, 6 * g), (4 * g, 4 * g), (2 * g, 4 * g)]
     staged, *first_tables = call(
         functools.partial(early_kernel, g),
         [jax.ShapeDtypeStruct(shape, kind) for shape, kind in zip(shapes, (F32, BF16, BF16, BF16))],
@@ -460,6 +486,7 @@
         total,
         *hot,
         t["stick_out"],
+        t["real_forward"],
         *pot_tables,
     )
     result = [result[order.index(d)] for d in range(owners)]

time: 55.3 us -> 58.1 us (1.051)
  Pallas kernels: 20.7 us -> 23.3 us
    pallas_call x13, Pallas kernels: 20.7 us -> 23.3 us  [call(): pl.pallas_call(kernel, out_shape=out_shapes, in_specs=[pl.BlockSpec(memor...]
    unnamed x16 -> x18, local copies, waits for them, and re-layouts: 1.88 us -> 1.94 us
  transfers between devices with their start and end apart: 18 -> 18, of which waited for: 5 -> 5; matrix products, arithmetic and copies ran while one was open for 0% -> 0% of each run, Pallas kernels for 21% -> 23%
where the time goes in v23:
time: 58.1 us; the launch traced here: 57.8 us
  starting transfers between devices  26.4 us (45%)
  Pallas kernels  23.3 us (40%)
  waiting for transfers between devices  5.97 us (10%)
  local copies, waits for them, and re-layouts  1.94 us (3%)
    pallas_call x13, Pallas kernels, call(): pl.pallas_call(kernel, out_shape=out_shapes, in_specs=[pl.BlockSpec(memor...  23.3 us
    ppermute x14, starting transfers between devices, exchanged(): moved[d] = lax.ppermute(block, 'stick', [(i, i ^ d) for i in range(owners)])  22.6 us
    ppermute x14, waiting for transfers between devices, exchanged(): moved[d] = lax.ppermute(block, 'stick', [(i, i ^ d) for i in range(owners)])  5.96 us
    ppermute x2, starting transfers between devices, shifted(): lax.ppermute(x, 'band', [(i, (i - distance) % groups) for i in range(grou...  3.11 us
    unnamed x18, local copies, waits for them, and re-layouts  1.94 us
  transfers between devices with their start and end apart: 18, of which 5 were waited for; matrix products, arithmetic and copies ran while one was open for 0% of the time, Pallas kernels for 23%

profile of v23, /device:TPU:0, one launch (start us, length us, event | category | flops | bytes accessed | tf_op | source)
XLA Modules:
  0.0 57.8 jit_solution(3475662545369193783)
XLA Ops:
  0.0 1.8 %shard_map.100 = (f32[104,128]{1,0:T(8,128)}, f32[104,128]{1,0:T(8,128)}, f32[104,128]{1,0:T(8,128)}, f32[104,128]{1,0:T(8,128)}, f32[104,128]{1,0:T(8,128)}, /*...) custom-call(f32[8,96,128]{2,1,0:T(8,128)} %sticks_ref.1, s32[1,128]{1,0:T(1,128)} %bitcast.1), custom_call_target="tpu_custom_call" | custom-call | flops 1 | bytes 1 | tf_op jit(solution)/shard_map/pallas_call | solution.py:357
  1.8 4.1 %collective-permute-start = (f32[104,128]{1,0:T(8,128)}, f32[104,128]{1,0:T(8,128)S(1)}, u32[]{:S(2)}, u32[]{:S(2)}) collective-permute-start(f32[104,128]{1,0:T(8,128)} %get-tuple-element.39), channel_id=1, source_target_pairs={{0,16},{4,20},{8,24},{12,28},{16,0},{20,4},{24,8},{28,12},{1,17},{... | collective-permute-start | bytes 159752 | tf_op jit(solution)/shard_map/ppermute | solution.py:378
  5.9 1.5 %collective-permute-start.1 = (f32[104,128]{1,0:T(8,128)}, f32[104,128]{1,0:T(8,128)S(1)}, u32[]{:S(2)}, u32[]{:S(2)}) collective-permute-start(f32[104,128]{1,0:T(8,128)} %get-tuple-element.40), channel_id=1, source_target_pairs={{0,4},{4,0},{8,12},{12,8},{16,20},{20,16},{24,28},{28,24},{1,5},{5... | collective-permute-start | bytes 159752 | tf_op jit(solution)/shard_map/ppermute | solution.py:378
  7.4 1.8 %collective-permute-start.3 = (f32[104,128]{1,0:T(8,128)}, f32[104,128]{1,0:T(8,128)S(1)}, u32[]{:S(2)}, u32[]{:S(2)}) collective-permute-start(f32[104,128]{1,0:T(8,128)} %get-tuple-element.42), channel_id=1, source_target_pairs={{0,8},{4,12},{8,0},{12,4},{16,24},{20,28},{24,16},{28,20},{1,9},{5... | collective-permute-start | bytes 159752 | tf_op jit(solution)/shard_map/ppermute | solution.py:378
  9.3 2.5 %collective-permute-start.4 = (f32[104,128]{1,0:T(8,128)}, f32[104,128]{1,0:T(8,128)S(1)}, u32[]{:S(2)}, u32[]{:S(2)}) collective-permute-start(f32[104,128]{1,0:T(8,128)} %get-tuple-element.43), channel_id=1, source_target_pairs={{0,24},{4,28},{8,16},{12,20},{16,8},{20,12},{24,0},{28,4},{1,25},{... | collective-permute-start | bytes 159752 | tf_op jit(solution)/shard_map/ppermute | solution.py:378
  11.8 1.1 %copy-done.5 = f32[416,288]{1,0:T(8,128)S(1)} copy-done((f32[416,288]{1,0:T(8,128)S(1)}, f32[416,288]{1,0:T(8,128)}, u32[]{:S(2)}) %copy-start.5) | copy-done | bytes 479256
  13.7 2.4 %collective-permute-start.5 = (f32[104,128]{1,0:T(8,128)}, f32[104,128]{1,0:T(8,128)S(1)}, u32[]{:S(2)}, u32[]{:S(2)}) collective-permute-start(f32[104,128]{1,0:T(8,128)} %get-tuple-element.48), channel_id=1, source_target_pairs={{0,28},{4,24},{8,20},{12,16},{16,12},{20,8},{24,4},{28,0},{1,29},{... | collective-permute-start | bytes 159752 | tf_op jit(solution)/shard_map/ppermute | solution.py:378
  16.1 1.6 %collective-permute-start.7 = (f32[576,128]{1,0:T(8,128)S(1)}, f32[576,128]{1,0:T(8,128)S(1)}, u32[]{:S(2)}, u32[]{:S(2)}) collective-permute-start(f32[576,128]{1,0:T(8,128)S(1)} %get-tuple-element.44.blocks_ref), channel_id=1, source_target_pairs={{0,2},{1,3},{2,0},{3,1},{4,6},{5,7},{6,4},{7,5},{8,10},{9,11},{10,... | collective-permute-start | bytes 884744 | tf_op jit(solution)/shard_map/ppermute | solution.py:394
  17.7 1.3 %shard_map.103.grid_ref = f32[2304,128]{1,0:T(8,128)S(1)} custom-call(f32[576,128]{1,0:T(8,128)S(1)} %get-tuple-element.44.blocks_ref, f32[8,768]{1,0:T(8,128)S(1)} %get-tuple-element.45.columns_ref, bf16[128,288]{1,0:T(8,128)(2,1)S(1)} %get-tuple-element.46.stick_in_ref), custom_call_target="tpu_custom_call" | custom-call | flops 5000000000 | bytes 5000000000 | tf_op jit(solution)/shard_map/pallas_call | solution.py:357
  19.0 0.9 %shard_map.104.hot_ref = bf16[768,2304]{1,0:T(8,128)(2,1)S(1)} custom-call(f32[8,768]{1,0:T(8,128)S(1)} %get-tuple-element.45.columns_ref), custom_call_target="tpu_custom_call" | custom-call | flops 1 | bytes 1 | tf_op jit(solution)/shard_map/pallas_call | solution.py:357
  20.0 0.8 %collective-permute-done.5.refs_0_ = f32[104,128]{1,0:T(8,128)S(1)} collective-permute-done((f32[104,128]{1,0:T(8,128)}, f32[104,128]{1,0:T(8,128)S(1)}, u32[]{:S(2)}, u32[]{:S(2)}) %collective-permute-start.5) | collective-permute-done | bytes 53280 | tf_op jit(solution)/shard_map/ppermute | solution.py:378
  21.4 1.6 %collective-permute-start.8 = (f32[192,128]{1,0:T(8,128)S(1)}, f32[192,128]{1,0:T(8,128)S(1)}, u32[]{:S(2)}, u32[]{:S(2)}) collective-permute-start(f32[192,128]{1,0:T(8,128)S(1)} %get-tuple-element.54.blocks_ref), channel_id=1, source_target_pairs={{0,2},{1,3},{2,0},{3,1},{4,6},{5,7},{6,4},{7,5},{8,10},{9,11},{10,... | collective-permute-start | bytes 294920 | tf_op jit(solution)/shard_map/ppermute | solution.py:394
  22.9 2.3 %shard_map.106.phi_ref = f32[1152,128]{1,0:T(8,128)S(1)} custom-call(f32[2304,128]{1,0:T(8,128)S(1)} %shard_map.103.grid_ref, f32[192,128]{1,0:T(8,128)S(1)} %get-tuple-element.54.blocks_ref, f32[8,256]{1,0:T(8,128)S(1)} %get-tuple-element.55.columns_ref, bf16[128,288]{1,0:T(8,128)(2,1)S(1)} %get-tuple-element.46.stick_in_ref, ...), custom_call_target="tpu_custom_call" | custom-call | flops 1 | bytes 1 | tf_op jit(solution)/shard_map/pallas_call | solution.py:357
  25.3 1.3 %shard_map.107.grid_ref = f32[2304,128]{1,0:T(8,128)S(1)} custom-call(f32[576,128]{1,0:T(8,128)S(1)} %collective-permute-done.7.blocks_ref, f32[8,768]{1,0:T(8,128)S(1)} %get-tuple-element.45.columns_ref, bf16[128,288]{1,0:T(8,128)(2,1)S(1)} %get-tuple-element.46.stick_in_ref), custom_call_target="tpu_custom_call" | custom-call | flops 1 | bytes 1 | tf_op jit(solution)/shard_map/pallas_call | solution.py:357
  26.7 2.3 %shard_map.108.first_ref = f32[1152,128]{1,0:T(8,128)S(1)} custom-call(f32[2304,128]{1,0:T(8,128)S(1)} %shard_map.107.grid_ref, f32[192,128]{1,0:T(8,128)S(1)} %collective-permute-done.8.blocks_ref, f32[8,256]{1,0:T(8,128)S(1)} %get-tuple-element.55.columns_ref, bf16[128,288]{1,0:T(8,128)(2,1)S(1)} %get-tuple-element.46.stick_in_ref, ...), custom_call_target="tpu_custom_call" | custom-call | flops 1 | bytes 1 | tf_op jit(solution)/shard_map/pallas_call | solution.py:357
  30.0 4.5 %shard_map.109.before_ref = f32[1152,128]{1,0:T(8,128)S(1)} custom-call(f32[1152,128]{1,0:T(8,128)S(1)} %shard_map.106.phi_ref, f32[1152,128]{1,0:T(8,128)S(1)} %collective-permute-done.10.other_ref, f32[256,256]{1,0:T(8,128)S(1)} %copy-done.2, f32[256,256]{1,0:T(8,128)S(1)} %copy-done.1, f32[192,192]{1,0:T(8,128)S(1)} %copy-done.4, ...), custom_call_target="tpu_custom_call" | custom-call | flops 1 | bytes 1 | tf_op jit(solution)/shard_map/pallas_call | solution.py:357
  34.6 7.6 %shard_map.111 = (f32[96,128]{1,0:T(8,128)S(1)}, f32[96,128]{1,0:T(8,128)S(1)}, f32[96,128]{1,0:T(8,128)S(1)}, f32[96,128]{1,0:T(8,128)S(1)}, f32[96,128]{1,0:T(...) custom-call(f32[1152,128]{1,0:T(8,128)S(1)} %shard_map.106.phi_ref, ...), custom_call_target="tpu_custom_call" | custom-call | flops 1 | bytes 1 | tf_op jit(solution)/shard_map/pallas_call | solution.py:357
  42.2 1.3 %collective-permute-start.11 = (f32[96,128]{1,0:T(8,128)S(1)}, f32[96,128]{1,0:T(8,128)S(1)}, u32[]{:S(2)}, u32[]{:S(2)}) collective-permute-start(f32[96,128]{1,0:T(8,128)S(1)} %get-tuple-element.58), channel_id=1, source_target_pairs={{0,16},{4,20},{8,24},{12,28},{16,0},{20,4},{24,8},{28,12},{1,17},{... | collective-permute-start | bytes 147464 | tf_op jit(solution)/shard_map/ppermute | solution.py:378
  43.5 1.5 %collective-permute-start.12 = (f32[96,128]{1,0:T(8,128)S(1)}, f32[96,128]{1,0:T(8,128)S(1)}, u32[]{:S(2)}, u32[]{:S(2)}) collective-permute-start(f32[96,128]{1,0:T(8,128)S(1)} %get-tuple-element.59), channel_id=1, source_target_pairs={{0,4},{4,0},{8,12},{12,8},{16,20},{20,16},{24,28},{28,24},{1,5},{5... | collective-permute-start | bytes 147464 | tf_op jit(solution)/shard_map/ppermute | solution.py:378
  45.0 1.6 %collective-permute-start.13 = (f32[96,128]{1,0:T(8,128)S(1)}, f32[96,128]{1,0:T(8,128)S(1)}, u32[]{:S(2)}, u32[]{:S(2)}) collective-permute-start(f32[96,128]{1,0:T(8,128)S(1)} %get-tuple-element.60), channel_id=1, source_target_pairs={{0,20},{4,16},{8,28},{12,24},{16,4},{20,0},{24,12},{28,8},{1,21},{... | collective-permute-start | bytes 147464 | tf_op jit(solution)/shard_map/ppermute | solution.py:378
  46.9 2.5 %collective-permute-start.15 = (f32[96,128]{1,0:T(8,128)S(1)}, f32[96,128]{1,0:T(8,128)S(1)}, u32[]{:S(2)}, u32[]{:S(2)}) collective-permute-start(f32[96,128]{1,0:T(8,128)S(1)} %get-tuple-element.62), channel_id=1, source_target_pairs={{0,24},{4,28},{8,16},{12,20},{16,8},{20,12},{24,0},{28,4},{1,25},{... | collective-permute-start | bytes 147464 | tf_op jit(solution)/shard_map/ppermute | solution.py:378
  50.2 2.4 %collective-permute-start.17 = (f32[96,128]{1,0:T(8,128)S(1)}, f32[96,128]{1,0:T(8,128)S(1)}, u32[]{:S(2)}, u32[]{:S(2)}) collective-permute-start(f32[96,128]{1,0:T(8,128)S(1)} %get-tuple-element.66), channel_id=1, source_target_pairs={{0,28},{4,24},{8,20},{12,16},{16,12},{20,8},{24,4},{28,0},{1,29},{... | collective-permute-start | bytes 147464 | tf_op jit(solution)/shard_map/ppermute | solution.py:378
  53.3 1.6 %collective-permute-done.16.refs_6_ = f32[96,128]{1,0:T(8,128)S(1)} collective-permute-done((f32[96,128]{1,0:T(8,128)S(1)}, f32[96,128]{1,0:T(8,128)S(1)}, u32[]{:S(2)}, u32[]{:S(2)}) %collective-permute-start.16) | collective-permute-done | bytes 49184 | tf_op jit(solution)/shard_map/ppermute | solution.py:378
  54.9 2.2 %collective-permute-done.17.refs_7_ = f32[96,128]{1,0:T(8,128)S(1)} collective-permute-done((f32[96,128]{1,0:T(8,128)S(1)}, f32[96,128]{1,0:T(8,128)S(1)}, u32[]{:S(2)}, u32[]{:S(2)}) %collective-permute-start.17) | collective-permute-done | bytes 49184 | tf_op jit(solution)/shard_map/ppermute | solution.py:378
  (43 shorter events, 5.1 us)
Async XLA Ops:
  1.8 11.9 %collective-permute-start = (f32[104,128]{1,0:T(8,128)}, f32[104,128]{1,0:T(8,128)S(1)}, u32[]{:S(2)}, u32[]{:S(2)}) collective-permute-start(f32[104,128]{1,0:T(8,128)} %get-tuple-element.39), channel_id=1, source_target_pairs={{0,16},{4,20},{8,24},{12,28},{16,0},{20,4},{24,8},{28,12},{1,17},{... | collective-permute-start | bytes 159752 | tf_op jit(solution)/shard_map/ppermute | solution.py:378
  5.9 10.2 %collective-permute-start.1 = (f32[104,128]{1,0:T(8,128)}, f32[104,128]{1,0:T(8,128)S(1)}, u32[]{:S(2)}, u32[]{:S(2)}) collective-permute-start(f32[104,128]{1,0:T(8,128)} %get-tuple-element.40), channel_id=1, source_target_pairs={{0,4},{4,0},{8,12},{12,8},{16,20},{20,16},{24,28},{28,24},{1,5},{5... | collective-permute-start | bytes 159752 | tf_op jit(solution)/shard_map/ppermute | solution.py:378
  7.4 8.6 %collective-permute-start.2 = (f32[104,128]{1,0:T(8,128)}, f32[104,128]{1,0:T(8,128)S(1)}, u32[]{:S(2)}, u32[]{:S(2)}) collective-permute-start(f32[104,128]{1,0:T(8,128)} %get-tuple-element.41), channel_id=1, source_target_pairs={{0,20},{4,16},{8,28},{12,24},{16,4},{20,0},{24,12},{28,8},{1,21},{... | collective-permute-start | bytes 159752 | tf_op jit(solution)/shard_map/ppermute | solution.py:378
  7.4 8.6 %collective-permute-start.3 = (f32[104,128]{1,0:T(8,128)}, f32[104,128]{1,0:T(8,128)S(1)}, u32[]{:S(2)}, u32[]{:S(2)}) collective-permute-start(f32[104,128]{1,0:T(8,128)} %get-tuple-element.42), channel_id=1, source_target_pairs={{0,8},{4,12},{8,0},{12,4},{16,24},{20,28},{24,16},{28,20},{1,9},{5... | collective-permute-start | bytes 159752 | tf_op jit(solution)/shard_map/ppermute | solution.py:378
  9.3 6.8 %collective-permute-start.4 = (f32[104,128]{1,0:T(8,128)}, f32[104,128]{1,0:T(8,128)S(1)}, u32[]{:S(2)}, u32[]{:S(2)}) collective-permute-start(f32[104,128]{1,0:T(8,128)} %get-tuple-element.43), channel_id=1, source_target_pairs={{0,24},{4,28},{8,16},{12,20},{16,8},{20,12},{24,0},{28,4},{1,25},{... | collective-permute-start | bytes 159752 | tf_op jit(solution)/shard_map/ppermute | solution.py:378
  13.7 7.1 %collective-permute-start.5 = (f32[104,128]{1,0:T(8,128)}, f32[104,128]{1,0:T(8,128)S(1)}, u32[]{:S(2)}, u32[]{:S(2)}) collective-permute-start(f32[104,128]{1,0:T(8,128)} %get-tuple-element.48), channel_id=1, source_target_pairs={{0,28},{4,24},{8,20},{12,16},{16,12},{20,8},{24,4},{28,0},{1,29},{... | collective-permute-start | bytes 159752 | tf_op jit(solution)/shard_map/ppermute | solution.py:378
  16.1 5.3 %collective-permute-start.6 = (f32[104,128]{1,0:T(8,128)}, f32[104,128]{1,0:T(8,128)S(1)}, u32[]{:S(2)}, u32[]{:S(2)}) collective-permute-start(f32[104,128]{1,0:T(8,128)} %get-tuple-element.53), channel_id=1, source_target_pairs={{0,12},{4,8},{8,4},{12,0},{16,28},{20,24},{24,20},{28,16},{1,13},{... | collective-permute-start | bytes 159752 | tf_op jit(solution)/shard_map/ppermute | solution.py:378
  16.1 9.2 %collective-permute-start.7 = (f32[576,128]{1,0:T(8,128)S(1)}, f32[576,128]{1,0:T(8,128)S(1)}, u32[]{:S(2)}, u32[]{:S(2)}) collective-permute-start(f32[576,128]{1,0:T(8,128)S(1)} %get-tuple-element.44.blocks_ref), channel_id=1, source_target_pairs={{0,2},{1,3},{2,0},{3,1},{4,6},{5,7},{6,4},{7,5},{8,10},{9,11},{10,... | collective-permute-start | bytes 884744 | tf_op jit(solution)/shard_map/ppermute | solution.py:394
  21.4 5.3 %collective-permute-start.8 = (f32[192,128]{1,0:T(8,128)S(1)}, f32[192,128]{1,0:T(8,128)S(1)}, u32[]{:S(2)}, u32[]{:S(2)}) collective-permute-start(f32[192,128]{1,0:T(8,128)S(1)} %get-tuple-element.54.blocks_ref), channel_id=1, source_target_pairs={{0,2},{1,3},{2,0},{3,1},{4,6},{5,7},{6,4},{7,5},{8,10},{9,11},{10,... | collective-permute-start | bytes 294920 | tf_op jit(solution)/shard_map/ppermute | solution.py:394
  25.2 4.7 %collective-permute-start.10 = (f32[1152,128]{1,0:T(8,128)S(1)}, f32[1152,128]{1,0:T(8,128)S(1)}, u32[]{:S(2)}, u32[]{:S(2)}) collective-permute-start(f32[1152,128]{1,0:T(8,128)S(1)} %shard_map.106.phi_ref), channel_id=1, source_target_pairs={{0,1},{1,0},{2,3},{3,2},{4,5},{5,4},{6,7},{7,6},{8,9},{9,8},{10,11... | collective-permute-start | bytes 1769480 | tf_op jit(solution)/shard_map/ppermute | solution.py:397
  26.6 3.3 %copy-start = (f32[2304,128]{1,0:T(8,128)S(1)}, f32[2304,128]{1,0:T(8,128)}, u32[]{:S(2)}) copy-start(f32[2304,128]{1,0:T(8,128)} %constant.23.clone.refs_4_) | copy-start | bytes 3538948
  26.7 3.3 %copy-start.1 = (f32[256,256]{1,0:T(8,128)S(1)}, f32[256,256]{1,0:T(8,128)}, u32[]{:S(2)}) copy-start(f32[256,256]{1,0:T(8,128)} %constant.17.clone.refs_1_) | copy-start | bytes 786436
  26.7 3.3 %copy-start.2 = (f32[256,256]{1,0:T(8,128)S(1)}, f32[256,256]{1,0:T(8,128)}, u32[]{:S(2)}) copy-start(f32[256,256]{1,0:T(8,128)} %constant.16.clone.refs_0_) | copy-start | bytes 786436
  26.7 3.3 %copy-start.3 = (f32[192,192]{1,0:T(8,128)S(1)}, f32[192,192]{1,0:T(8,128)}, u32[]{:S(2)}) copy-start(f32[192,192]{1,0:T(8,128)} %constant.20.clone.refs_3_) | copy-start | bytes 442372
  29.0 5.5 %collective-permute-start.9 = (f32[1152,128]{1,0:T(8,128)S(1)}, f32[1152,128]{1,0:T(8,128)S(1)}, u32[]{:S(2)}, u32[]{:S(2)}) collective-permute-start(f32[1152,128]{1,0:T(8,128)S(1)} %shard_map.108.first_ref), channel_id=1, source_target_pairs={{0,1},{1,0},{2,3},{3,2},{4,5},{5,4},{6,7},{7,6},{8,9},{9,8},{10,11... | collective-permute-start | bytes 1769480 | tf_op jit(solution)/shard_map/ppermute | solution.py:397
  29.9 4.6 %copy-start.6 = (f32[96,384]{1,0:T(8,128)S(1)}, f32[96,384]{1,0:T(8,128)}, u32[]{:S(2)}) copy-start(f32[96,384]{1,0:T(8,128)} %constant.22.clone.stick_out_ref) | copy-start | bytes 442372
  29.9 4.6 %copy-start.7 = (f32[96,144]{1,0:T(8,128)S(1)}, f32[96,144]{1,0:T(8,128)}, u32[]{:S(2)}) copy-start(f32[96,144]{1,0:T(8,128)} %constant.18.clone.real_forward_ref) | copy-start | bytes 165892
  42.2 7.2 %collective-permute-start.11 = (f32[96,128]{1,0:T(8,128)S(1)}, f32[96,128]{1,0:T(8,128)S(1)}, u32[]{:S(2)}, u32[]{:S(2)}) collective-permute-start(f32[96,128]{1,0:T(8,128)S(1)} %get-tuple-element.58), channel_id=1, source_target_pairs={{0,16},{4,20},{8,24},{12,28},{16,0},{20,4},{24,8},{28,12},{1,17},{... | collective-permute-start | bytes 147464 | tf_op jit(solution)/shard_map/ppermute | solution.py:378
  43.5 6.7 %collective-permute-start.12 = (f32[96,128]{1,0:T(8,128)S(1)}, f32[96,128]{1,0:T(8,128)S(1)}, u32[]{:S(2)}, u32[]{:S(2)}) collective-permute-start(f32[96,128]{1,0:T(8,128)S(1)} %get-tuple-element.59), channel_id=1, source_target_pairs={{0,4},{4,0},{8,12},{12,8},{16,20},{20,16},{24,28},{28,24},{1,5},{5... | collective-permute-start | bytes 147464 | tf_op jit(solution)/shard_map/ppermute | solution.py:378
  45.0 7.5 %collective-permute-start.13 = (f32[96,128]{1,0:T(8,128)S(1)}, f32[96,128]{1,0:T(8,128)S(1)}, u32[]{:S(2)}, u32[]{:S(2)}) collective-permute-start(f32[96,128]{1,0:T(8,128)S(1)} %get-tuple-element.60), channel_id=1, source_target_pairs={{0,20},{4,16},{8,28},{12,24},{16,4},{20,0},{24,12},{28,8},{1,21},{... | collective-permute-start | bytes 147464 | tf_op jit(solution)/shard_map/ppermute | solution.py:378
  46.7 5.9 %collective-permute-start.14 = (f32[96,128]{1,0:T(8,128)S(1)}, f32[96,128]{1,0:T(8,128)S(1)}, u32[]{:S(2)}, u32[]{:S(2)}) collective-permute-start(f32[96,128]{1,0:T(8,128)S(1)} %get-tuple-element.61), channel_id=1, source_target_pairs={{0,8},{4,12},{8,0},{12,4},{16,24},{20,28},{24,16},{28,20},{1,9},{5... | collective-permute-start | bytes 147464 | tf_op jit(solution)/shard_map/ppermute | solution.py:378
  46.9 6.4 %collective-permute-start.15 = (f32[96,128]{1,0:T(8,128)S(1)}, f32[96,128]{1,0:T(8,128)S(1)}, u32[]{:S(2)}, u32[]{:S(2)}) collective-permute-start(f32[96,128]{1,0:T(8,128)S(1)} %get-tuple-element.62), channel_id=1, source_target_pairs={{0,24},{4,28},{8,16},{12,20},{16,8},{20,12},{24,0},{28,4},{1,25},{... | collective-permute-start | bytes 147464 | tf_op jit(solution)/shard_map/ppermute | solution.py:378
  49.4 5.5 %collective-permute-start.16 = (f32[96,128]{1,0:T(8,128)S(1)}, f32[96,128]{1,0:T(8,128)S(1)}, u32[]{:S(2)}, u32[]{:S(2)}) collective-permute-start(f32[96,128]{1,0:T(8,128)S(1)} %get-tuple-element.64), channel_id=1, source_target_pairs={{0,12},{4,8},{8,4},{12,0},{16,28},{20,24},{24,20},{28,16},{1,13},{... | collective-permute-start | bytes 147464 | tf_op jit(solution)/shard_map/ppermute | solution.py:378
  50.2 6.9 %collective-permute-start.17 = (f32[96,128]{1,0:T(8,128)S(1)}, f32[96,128]{1,0:T(8,128)S(1)}, u32[]{:S(2)}, u32[]{:S(2)}) collective-permute-start(f32[96,128]{1,0:T(8,128)S(1)} %get-tuple-element.66), channel_id=1, source_target_pairs={{0,28},{4,24},{8,20},{12,16},{16,12},{20,8},{24,4},{28,0},{1,29},{... | collective-permute-start | bytes 147464 | tf_op jit(solution)/shard_map/ppermute | solution.py:378
  (3 other events, 5.2 us)

commit v24 on v22

--- a/solution.py
+++ b/solution.py
@@ -320,10 +320,8 @@
 
     stick_out = stick_out_ref[...].astype(BF16)
     for k in range(0, len(out_refs), 2):
-        high, low = split(picked_ref[k * LANES : (k + 2) * LANES, :])
-        lined = jnp.concatenate([high, low, high], 1)
-        out = lax.dot_general(stick_out, lined, (((1,), (1,)), ((), ())), preferred_element_type=F32)
-        out_refs[k][...], out_refs[k + 1][...] = halves(out)
+        lined = beside(*[picked_ref[j * LANES : (j + 1) * LANES, :].T for j in (k, k + 1)])
+        out_refs[k][...], out_refs[k + 1][...] = halves(dot(stick_out, stacked(lined)))
 
 
 def call(kernel, out_shapes, scratch, flops, *operands, space=pltpu.VMEM, out_space=pltpu.VMEM, grant=40):
@@ -464,7 +462,7 @@
     )
     result = [result[order.index(d)] for d in range(owners)]
     result = exchanged(result, mixed, {d: (half,) for d in before})
-    out_order = [0] + mixed
+    out_order = order
     return call(
         functools.partial(place_kernel, out_order),
         jax.ShapeDtypeStruct(sticks.shape, F32),

time: 55.3 us -> 55.4 us (level)
  transfers between devices with their start and end apart: 18 -> 18, of which waited for: 5 -> 5; matrix products, arithmetic and copies ran while one was open for 0% -> 0% of each run, Pallas kernels for 21% -> 20%
where the time goes in v24:
time: 55.4 us; the launch traced here: 55.2 us
  starting transfers between devices  26 us (47%)
  Pallas kernels  20.6 us (37%)
  waiting for transfers between devices  6.41 us (12%)
  local copies, waits for them, and re-layouts  1.88 us (3%)
    ppermute x14, starting transfers between devices, exchanged(): moved[d] = lax.ppermute(block, 'stick', [(i, i ^ d) for i in range(owners)])  22.2 us
    pallas_call x13, Pallas kernels, call(): pl.pallas_call(kernel, out_shape=out_shapes, in_specs=[pl.BlockSpec(memor...  20.6 us
    ppermute x14, waiting for transfers between devices, exchanged(): moved[d] = lax.ppermute(block, 'stick', [(i, i ^ d) for i in range(owners)])  6.4 us
    ppermute x2, starting transfers between devices, shifted(): lax.ppermute(x, 'band', [(i, (i - distance) % groups) for i in range(grou...  3.11 us
    unnamed x16, local copies, waits for them, and re-layouts  1.88 us
  transfers between devices with their start and end apart: 18, of which 5 were waited for; matrix products, arithmetic and copies ran while one was open for 0% of the time, Pallas kernels for 20%

profile of v24, /device:TPU:0, one launch (start us, length us, event | category | flops | bytes accessed | tf_op | source)
XLA Modules:
  0.0 55.2 jit_solution(14335799440818731309)
XLA Ops:
  0.0 1.8 %shard_map.91 = (f32[104,128]{1,0:T(8,128)}, f32[104,128]{1,0:T(8,128)}, f32[104,128]{1,0:T(8,128)}, f32[104,128]{1,0:T(8,128)}, f32[104,128]{1,0:T(8,128)}, /*i...) custom-call(f32[8,96,128]{2,1,0:T(8,128)} %sticks_ref.1, s32[1,128]{1,0:T(1,128)} %bitcast.1), custom_call_target="tpu_custom_call" | custom-call | flops 1 | bytes 1 | tf_op jit(solution)/shard_map/pallas_call | solution.py:329
  1.8 4.1 %collective-permute-start = (f32[104,128]{1,0:T(8,128)}, f32[104,128]{1,0:T(8,128)S(1)}, u32[]{:S(2)}, u32[]{:S(2)}) collective-permute-start(f32[104,128]{1,0:T(8,128)} %get-tuple-element.39), channel_id=1, source_target_pairs={{0,16},{4,20},{8,24},{12,28},{16,0},{20,4},{24,8},{28,12},{1,17},{... | collective-permute-start | bytes 159752 | tf_op jit(solution)/shard_map/ppermute | solution.py:350
  5.9 1.5 %collective-permute-start.1 = (f32[104,128]{1,0:T(8,128)}, f32[104,128]{1,0:T(8,128)S(1)}, u32[]{:S(2)}, u32[]{:S(2)}) collective-permute-start(f32[104,128]{1,0:T(8,128)} %get-tuple-element.40), channel_id=1, source_target_pairs={{0,4},{4,0},{8,12},{12,8},{16,20},{20,16},{24,28},{28,24},{1,5},{5... | collective-permute-start | bytes 159752 | tf_op jit(solution)/shard_map/ppermute | solution.py:350
  7.5 1.8 %collective-permute-start.3 = (f32[104,128]{1,0:T(8,128)}, f32[104,128]{1,0:T(8,128)S(1)}, u32[]{:S(2)}, u32[]{:S(2)}) collective-permute-start(f32[104,128]{1,0:T(8,128)} %get-tuple-element.42), channel_id=1, source_target_pairs={{0,8},{4,12},{8,0},{12,4},{16,24},{20,28},{24,16},{28,20},{1,9},{5... | collective-permute-start | bytes 159752 | tf_op jit(solution)/shard_map/ppermute | solution.py:350
  9.3 2.5 %collective-permute-start.4 = (f32[104,128]{1,0:T(8,128)}, f32[104,128]{1,0:T(8,128)S(1)}, u32[]{:S(2)}, u32[]{:S(2)}) collective-permute-start(f32[104,128]{1,0:T(8,128)} %get-tuple-element.43), channel_id=1, source_target_pairs={{0,24},{4,28},{8,16},{12,20},{16,8},{20,12},{24,0},{28,4},{1,25},{... | collective-permute-start | bytes 159752 | tf_op jit(solution)/shard_map/ppermute | solution.py:350
  11.8 1.0 %copy-done.3 = f32[320,288]{1,0:T(8,128)S(1)} copy-done((f32[320,288]{1,0:T(8,128)S(1)}, f32[320,288]{1,0:T(8,128)}, u32[]{:S(2)}) %copy-start.3) | copy-done | bytes 368664
  13.6 2.4 %collective-permute-start.5 = (f32[104,128]{1,0:T(8,128)}, f32[104,128]{1,0:T(8,128)S(1)}, u32[]{:S(2)}, u32[]{:S(2)}) collective-permute-start(f32[104,128]{1,0:T(8,128)} %get-tuple-element.48), channel_id=1, source_target_pairs={{0,28},{4,24},{8,20},{12,16},{16,12},{20,8},{24,4},{28,0},{1,29},{... | collective-permute-start | bytes 159752 | tf_op jit(solution)/shard_map/ppermute | solution.py:350
  16.1 1.6 %collective-permute-start.7 = (f32[576,128]{1,0:T(8,128)S(1)}, f32[576,128]{1,0:T(8,128)S(1)}, u32[]{:S(2)}, u32[]{:S(2)}) collective-permute-start(f32[576,128]{1,0:T(8,128)S(1)} %get-tuple-element.44.blocks_ref), channel_id=1, source_target_pairs={{0,2},{1,3},{2,0},{3,1},{4,6},{5,7},{6,4},{7,5},{8,10},{9,11},{10,... | collective-permute-start | bytes 884744 | tf_op jit(solution)/shard_map/ppermute | solution.py:366
  17.6 1.3 %shard_map.94.grid_ref = f32[2304,128]{1,0:T(8,128)S(1)} custom-call(f32[576,128]{1,0:T(8,128)S(1)} %get-tuple-element.44.blocks_ref, f32[8,768]{1,0:T(8,128)S(1)} %get-tuple-element.45.columns_ref, bf16[128,288]{1,0:T(8,128)(2,1)S(1)} %get-tuple-element.46.stick_in_ref), custom_call_target="tpu_custom_call" | custom-call | flops 5000000000 | bytes 5000000000 | tf_op jit(solution)/shard_map/pallas_call | solution.py:329
  19.0 0.9 %shard_map.95.hot_ref = bf16[768,2304]{1,0:T(8,128)(2,1)S(1)} custom-call(f32[8,768]{1,0:T(8,128)S(1)} %get-tuple-element.45.columns_ref), custom_call_target="tpu_custom_call" | custom-call | flops 1 | bytes 1 | tf_op jit(solution)/shard_map/pallas_call | solution.py:329
  19.9 0.8 %collective-permute-done.5.refs_0_ = f32[104,128]{1,0:T(8,128)S(1)} collective-permute-done((f32[104,128]{1,0:T(8,128)}, f32[104,128]{1,0:T(8,128)S(1)}, u32[]{:S(2)}, u32[]{:S(2)}) %collective-permute-start.5) | collective-permute-done | bytes 53280 | tf_op jit(solution)/shard_map/ppermute | solution.py:350
  21.3 1.6 %collective-permute-start.8 = (f32[192,128]{1,0:T(8,128)S(1)}, f32[192,128]{1,0:T(8,128)S(1)}, u32[]{:S(2)}, u32[]{:S(2)}) collective-permute-start(f32[192,128]{1,0:T(8,128)S(1)} %get-tuple-element.54.blocks_ref), channel_id=1, source_target_pairs={{0,2},{1,3},{2,0},{3,1},{4,6},{5,7},{6,4},{7,5},{8,10},{9,11},{10,... | collective-permute-start | bytes 294920 | tf_op jit(solution)/shard_map/ppermute | solution.py:366
  22.9 1.8 %shard_map.97.phi_ref = f32[1152,128]{1,0:T(8,128)S(1)} custom-call(f32[2304,128]{1,0:T(8,128)S(1)} %shard_map.94.grid_ref, f32[192,128]{1,0:T(8,128)S(1)} %get-tuple-element.54.blocks_ref, f32[8,256]{1,0:T(8,128)S(1)} %get-tuple-element.55.columns_ref, bf16[128,288]{1,0:T(8,128)(2,1)S(1)} %get-tuple-element.46.stick_in_ref, ...), custom_call_target="tpu_custom_call" | custom-call | flops 1 | bytes 1 | tf_op jit(solution)/shard_map/pallas_call | solution.py:329
  24.8 1.3 %shard_map.98.grid_ref = f32[2304,128]{1,0:T(8,128)S(1)} custom-call(f32[576,128]{1,0:T(8,128)S(1)} %collective-permute-done.7.blocks_ref, f32[8,768]{1,0:T(8,128)S(1)} %get-tuple-element.45.columns_ref, bf16[128,288]{1,0:T(8,128)(2,1)S(1)} %get-tuple-element.46.stick_in_ref), custom_call_target="tpu_custom_call" | custom-call | flops 1 | bytes 1 | tf_op jit(solution)/shard_map/pallas_call | solution.py:329
  26.2 1.8 %shard_map.99.first_ref = f32[1152,128]{1,0:T(8,128)S(1)} custom-call(f32[2304,128]{1,0:T(8,128)S(1)} %shard_map.98.grid_ref, f32[192,128]{1,0:T(8,128)S(1)} %collective-permute-done.8.blocks_ref, f32[8,256]{1,0:T(8,128)S(1)} %get-tuple-element.55.columns_ref, bf16[128,288]{1,0:T(8,128)(2,1)S(1)} %get-tuple-element.46.stick_in_ref, ...), custom_call_target="tpu_custom_call" | custom-call | flops 1 | bytes 1 | tf_op jit(solution)/shard_map/pallas_call | solution.py:329
  29.1 3.6 %shard_map.100.before_ref = f32[1152,128]{1,0:T(8,128)S(1)} custom-call(f32[1152,128]{1,0:T(8,128)S(1)} %shard_map.97.phi_ref, f32[1152,128]{1,0:T(8,128)S(1)} %collective-permute-done.10.other_ref, f32[256,256]{1,0:T(8,128)S(1)} %copy-done.2, f32[256,256]{1,0:T(8,128)S(1)} %copy-done.1, f32[96,144]{1,0:T(8,128)S(1)} %copy-done.5, f32[96,144]{1,0:T(8,128)S(1)} %copy-done.4, ...), custom_call_target="tpu_custom_call" | custom-call | flops 1 | bytes 1 | tf_op jit(solution)/shard_map/pallas_call | solution.py:329
  32.7 6.7 %shard_map.102 = (f32[96,128]{1,0:T(8,128)S(1)}, f32[96,128]{1,0:T(8,128)S(1)}, f32[96,128]{1,0:T(8,128)S(1)}, f32[96,128]{1,0:T(8,128)S(1)}, f32[96,128]{1,0:T(...) custom-call(f32[1152,128]{1,0:T(8,128)S(1)} %shard_map.97.phi_ref, ...), custom_call_target="tpu_custom_call" | custom-call | flops 1 | bytes 1 | tf_op jit(solution)/shard_map/pallas_call | solution.py:329
  39.5 1.7 %collective-permute-start.11 = (f32[96,128]{1,0:T(8,128)S(1)}, f32[96,128]{1,0:T(8,128)S(1)}, u32[]{:S(2)}, u32[]{:S(2)}) collective-permute-start(f32[96,128]{1,0:T(8,128)S(1)} %get-tuple-element.58), channel_id=1, source_target_pairs={{0,16},{4,20},{8,24},{12,28},{16,0},{20,4},{24,8},{28,12},{1,17},{... | collective-permute-start | bytes 147464 | tf_op jit(solution)/shard_map/ppermute | solution.py:350
  41.2 1.5 %collective-permute-start.12 = (f32[96,128]{1,0:T(8,128)S(1)}, f32[96,128]{1,0:T(8,128)S(1)}, u32[]{:S(2)}, u32[]{:S(2)}) collective-permute-start(f32[96,128]{1,0:T(8,128)S(1)} %get-tuple-element.59), channel_id=1, source_target_pairs={{0,4},{4,0},{8,12},{12,8},{16,20},{20,16},{24,28},{28,24},{1,5},{5... | collective-permute-start | bytes 147464 | tf_op jit(solution)/shard_map/ppermute | solution.py:350
  42.7 1.2 %collective-permute-start.13 = (f32[96,128]{1,0:T(8,128)S(1)}, f32[96,128]{1,0:T(8,128)S(1)}, u32[]{:S(2)}, u32[]{:S(2)}) collective-permute-start(f32[96,128]{1,0:T(8,128)S(1)} %get-tuple-element.60), channel_id=1, source_target_pairs={{0,20},{4,16},{8,28},{12,24},{16,4},{20,0},{24,12},{28,8},{1,21},{... | collective-permute-start | bytes 147464 | tf_op jit(solution)/shard_map/ppermute | solution.py:350
  44.6 2.5 %collective-permute-start.15 = (f32[96,128]{1,0:T(8,128)S(1)}, f32[96,128]{1,0:T(8,128)S(1)}, u32[]{:S(2)}, u32[]{:S(2)}) collective-permute-start(f32[96,128]{1,0:T(8,128)S(1)} %get-tuple-element.62), channel_id=1, source_target_pairs={{0,24},{4,28},{8,16},{12,20},{16,8},{20,12},{24,0},{28,4},{1,25},{... | collective-permute-start | bytes 147464 | tf_op jit(solution)/shard_map/ppermute | solution.py:350
  47.1 2.3 %collective-permute-start.16 = (f32[96,128]{1,0:T(8,128)S(1)}, f32[96,128]{1,0:T(8,128)S(1)}, u32[]{:S(2)}, u32[]{:S(2)}) collective-permute-start(f32[96,128]{1,0:T(8,128)S(1)} %get-tuple-element.64), channel_id=1, source_target_pairs={{0,28},{4,24},{8,20},{12,16},{16,12},{20,8},{24,4},{28,0},{1,29},{... | collective-permute-start | bytes 147464 | tf_op jit(solution)/shard_map/ppermute | solution.py:350
  49.4 1.2 %collective-permute-done.15.refs_5_ = f32[96,128]{1,0:T(8,128)S(1)} collective-permute-done((f32[96,128]{1,0:T(8,128)S(1)}, f32[96,128]{1,0:T(8,128)S(1)}, u32[]{:S(2)}, u32[]{:S(2)}) %collective-permute-start.15) | collective-permute-done | bytes 49184 | tf_op jit(solution)/shard_map/ppermute | solution.py:350
  50.6 3.3 %collective-permute-done.16.refs_6_ = f32[96,128]{1,0:T(8,128)S(1)} collective-permute-done((f32[96,128]{1,0:T(8,128)S(1)}, f32[96,128]{1,0:T(8,128)S(1)}, u32[]{:S(2)}, u32[]{:S(2)}) %collective-permute-start.16) | collective-permute-done | bytes 49184 | tf_op jit(solution)/shard_map/ppermute | solution.py:350
  (41 shorter events, 4.5 us)
Async XLA Ops:
  1.8 11.8 %collective-permute-start = (f32[104,128]{1,0:T(8,128)}, f32[104,128]{1,0:T(8,128)S(1)}, u32[]{:S(2)}, u32[]{:S(2)}) collective-permute-start(f32[104,128]{1,0:T(8,128)} %get-tuple-element.39), channel_id=1, source_target_pairs={{0,16},{4,20},{8,24},{12,28},{16,0},{20,4},{24,8},{28,12},{1,17},{... | collective-permute-start | bytes 159752 | tf_op jit(solution)/shard_map/ppermute | solution.py:350
  5.9 10.1 %collective-permute-start.1 = (f32[104,128]{1,0:T(8,128)}, f32[104,128]{1,0:T(8,128)S(1)}, u32[]{:S(2)}, u32[]{:S(2)}) collective-permute-start(f32[104,128]{1,0:T(8,128)} %get-tuple-element.40), channel_id=1, source_target_pairs={{0,4},{4,0},{8,12},{12,8},{16,20},{20,16},{24,28},{28,24},{1,5},{5... | collective-permute-start | bytes 159752 | tf_op jit(solution)/shard_map/ppermute | solution.py:350
  7.4 8.6 %collective-permute-start.2 = (f32[104,128]{1,0:T(8,128)}, f32[104,128]{1,0:T(8,128)S(1)}, u32[]{:S(2)}, u32[]{:S(2)}) collective-permute-start(f32[104,128]{1,0:T(8,128)} %get-tuple-element.41), channel_id=1, source_target_pairs={{0,20},{4,16},{8,28},{12,24},{16,4},{20,0},{24,12},{28,8},{1,21},{... | collective-permute-start | bytes 159752 | tf_op jit(solution)/shard_map/ppermute | solution.py:350
  7.5 8.6 %collective-permute-start.3 = (f32[104,128]{1,0:T(8,128)}, f32[104,128]{1,0:T(8,128)S(1)}, u32[]{:S(2)}, u32[]{:S(2)}) collective-permute-start(f32[104,128]{1,0:T(8,128)} %get-tuple-element.42), channel_id=1, source_target_pairs={{0,8},{4,12},{8,0},{12,4},{16,24},{20,28},{24,16},{28,20},{1,9},{5... | collective-permute-start | bytes 159752 | tf_op jit(solution)/shard_map/ppermute | solution.py:350
  9.3 6.8 %collective-permute-start.4 = (f32[104,128]{1,0:T(8,128)}, f32[104,128]{1,0:T(8,128)S(1)}, u32[]{:S(2)}, u32[]{:S(2)}) collective-permute-start(f32[104,128]{1,0:T(8,128)} %get-tuple-element.43), channel_id=1, source_target_pairs={{0,24},{4,28},{8,16},{12,20},{16,8},{20,12},{24,0},{28,4},{1,25},{... | collective-permute-start | bytes 159752 | tf_op jit(solution)/shard_map/ppermute | solution.py:350
  13.6 7.1 %collective-permute-start.5 = (f32[104,128]{1,0:T(8,128)}, f32[104,128]{1,0:T(8,128)S(1)}, u32[]{:S(2)}, u32[]{:S(2)}) collective-permute-start(f32[104,128]{1,0:T(8,128)} %get-tuple-element.48), channel_id=1, source_target_pairs={{0,28},{4,24},{8,20},{12,16},{16,12},{20,8},{24,4},{28,0},{1,29},{... | collective-permute-start | bytes 159752 | tf_op jit(solution)/shard_map/ppermute | solution.py:350
  16.0 5.3 %collective-permute-start.6 = (f32[104,128]{1,0:T(8,128)}, f32[104,128]{1,0:T(8,128)S(1)}, u32[]{:S(2)}, u32[]{:S(2)}) collective-permute-start(f32[104,128]{1,0:T(8,128)} %get-tuple-element.53), channel_id=1, source_target_pairs={{0,12},{4,8},{8,4},{12,0},{16,28},{20,24},{24,20},{28,16},{1,13},{... | collective-permute-start | bytes 159752 | tf_op jit(solution)/shard_map/ppermute | solution.py:350
  16.1 8.7 %collective-permute-start.7 = (f32[576,128]{1,0:T(8,128)S(1)}, f32[576,128]{1,0:T(8,128)S(1)}, u32[]{:S(2)}, u32[]{:S(2)}) collective-permute-start(f32[576,128]{1,0:T(8,128)S(1)} %get-tuple-element.44.blocks_ref), channel_id=1, source_target_pairs={{0,2},{1,3},{2,0},{3,1},{4,6},{5,7},{6,4},{7,5},{8,10},{9,11},{10,... | collective-permute-start | bytes 884744 | tf_op jit(solution)/shard_map/ppermute | solution.py:366
  21.3 4.9 %collective-permute-start.8 = (f32[192,128]{1,0:T(8,128)S(1)}, f32[192,128]{1,0:T(8,128)S(1)}, u32[]{:S(2)}, u32[]{:S(2)}) collective-permute-start(f32[192,128]{1,0:T(8,128)S(1)} %get-tuple-element.54.blocks_ref), channel_id=1, source_target_pairs={{0,2},{1,3},{2,0},{3,1},{4,6},{5,7},{6,4},{7,5},{8,10},{9,11},{10,... | collective-permute-start | bytes 294920 | tf_op jit(solution)/shard_map/ppermute | solution.py:366
  24.7 4.3 %collective-permute-start.10 = (f32[1152,128]{1,0:T(8,128)S(1)}, f32[1152,128]{1,0:T(8,128)S(1)}, u32[]{:S(2)}, u32[]{:S(2)}) collective-permute-start(f32[1152,128]{1,0:T(8,128)S(1)} %shard_map.97.phi_ref), channel_id=1, source_target_pairs={{0,1},{1,0},{2,3},{3,2},{4,5},{5,4},{6,7},{7,6},{8,9},{9,8},{10,11... | collective-permute-start | bytes 1769480 | tf_op jit(solution)/shard_map/ppermute | solution.py:369
  26.2 2.9 %copy-start = (f32[2304,128]{1,0:T(8,128)S(1)}, f32[2304,128]{1,0:T(8,128)}, u32[]{:S(2)}) copy-start(f32[2304,128]{1,0:T(8,128)} %constant.20.clone.refs_4_) | copy-start | bytes 3538948
  26.2 2.9 %copy-start.1 = (f32[256,256]{1,0:T(8,128)S(1)}, f32[256,256]{1,0:T(8,128)}, u32[]{:S(2)}) copy-start(f32[256,256]{1,0:T(8,128)} %constant.15.clone.refs_1_) | copy-start | bytes 786436
  26.2 2.8 %copy-start.2 = (f32[256,256]{1,0:T(8,128)S(1)}, f32[256,256]{1,0:T(8,128)}, u32[]{:S(2)}) copy-start(f32[256,256]{1,0:T(8,128)} %constant.14.clone.refs_0_) | copy-start | bytes 786436
  26.2 2.8 %copy-start.4 = (f32[96,144]{1,0:T(8,128)S(1)}, f32[96,144]{1,0:T(8,128)}, u32[]{:S(2)}) copy-start(f32[96,144]{1,0:T(8,128)} %constant.17.clone.refs_3_) | copy-start | bytes 165892
  26.2 2.8 %copy-start.5 = (f32[96,144]{1,0:T(8,128)S(1)}, f32[96,144]{1,0:T(8,128)}, u32[]{:S(2)}) copy-start(f32[96,144]{1,0:T(8,128)} %constant.16.clone.refs_2_) | copy-start | bytes 165892
  28.1 4.6 %collective-permute-start.9 = (f32[1152,128]{1,0:T(8,128)S(1)}, f32[1152,128]{1,0:T(8,128)S(1)}, u32[]{:S(2)}, u32[]{:S(2)}) collective-permute-start(f32[1152,128]{1,0:T(8,128)S(1)} %shard_map.99.first_ref), channel_id=1, source_target_pairs={{0,1},{1,0},{2,3},{3,2},{4,5},{5,4},{6,7},{7,6},{8,9},{9,8},{10,11... | collective-permute-start | bytes 1769480 | tf_op jit(solution)/shard_map/ppermute | solution.py:369
  29.0 3.7 %copy-start.6 = (f32[96,384]{1,0:T(8,128)S(1)}, f32[96,384]{1,0:T(8,128)}, u32[]{:S(2)}) copy-start(f32[96,384]{1,0:T(8,128)} %constant.19.clone.stick_out_ref) | copy-start | bytes 442372
  39.5 7.6 %collective-permute-start.11 = (f32[96,128]{1,0:T(8,128)S(1)}, f32[96,128]{1,0:T(8,128)S(1)}, u32[]{:S(2)}, u32[]{:S(2)}) collective-permute-start(f32[96,128]{1,0:T(8,128)S(1)} %get-tuple-element.58), channel_id=1, source_target_pairs={{0,16},{4,20},{8,24},{12,28},{16,0},{20,4},{24,8},{28,12},{1,17},{... | collective-permute-start | bytes 147464 | tf_op jit(solution)/shard_map/ppermute | solution.py:350
  41.2 8.2 %collective-permute-start.12 = (f32[96,128]{1,0:T(8,128)S(1)}, f32[96,128]{1,0:T(8,128)S(1)}, u32[]{:S(2)}, u32[]{:S(2)}) collective-permute-start(f32[96,128]{1,0:T(8,128)S(1)} %get-tuple-element.59), channel_id=1, source_target_pairs={{0,4},{4,0},{8,12},{12,8},{16,20},{20,16},{24,28},{28,24},{1,5},{5... | collective-permute-start | bytes 147464 | tf_op jit(solution)/shard_map/ppermute | solution.py:350
  42.7 6.7 %collective-permute-start.13 = (f32[96,128]{1,0:T(8,128)S(1)}, f32[96,128]{1,0:T(8,128)S(1)}, u32[]{:S(2)}, u32[]{:S(2)}) collective-permute-start(f32[96,128]{1,0:T(8,128)S(1)} %get-tuple-element.60), channel_id=1, source_target_pairs={{0,20},{4,16},{8,28},{12,24},{16,4},{20,0},{24,12},{28,8},{1,21},{... | collective-permute-start | bytes 147464 | tf_op jit(solution)/shard_map/ppermute | solution.py:350
  43.9 5.5 %collective-permute-start.14 = (f32[96,128]{1,0:T(8,128)S(1)}, f32[96,128]{1,0:T(8,128)S(1)}, u32[]{:S(2)}, u32[]{:S(2)}) collective-permute-start(f32[96,128]{1,0:T(8,128)S(1)} %get-tuple-element.61), channel_id=1, source_target_pairs={{0,8},{4,12},{8,0},{12,4},{16,24},{20,28},{24,16},{28,20},{1,9},{5... | collective-permute-start | bytes 147464 | tf_op jit(solution)/shard_map/ppermute | solution.py:350
  44.6 6.0 %collective-permute-start.15 = (f32[96,128]{1,0:T(8,128)S(1)}, f32[96,128]{1,0:T(8,128)S(1)}, u32[]{:S(2)}, u32[]{:S(2)}) collective-permute-start(f32[96,128]{1,0:T(8,128)S(1)} %get-tuple-element.62), channel_id=1, source_target_pairs={{0,24},{4,28},{8,16},{12,20},{16,8},{20,12},{24,0},{28,4},{1,25},{... | collective-permute-start | bytes 147464 | tf_op jit(solution)/shard_map/ppermute | solution.py:350
  47.1 6.8 %collective-permute-start.16 = (f32[96,128]{1,0:T(8,128)S(1)}, f32[96,128]{1,0:T(8,128)S(1)}, u32[]{:S(2)}, u32[]{:S(2)}) collective-permute-start(f32[96,128]{1,0:T(8,128)S(1)} %get-tuple-element.64), channel_id=1, source_target_pairs={{0,28},{4,24},{8,20},{12,16},{16,12},{20,8},{24,4},{28,0},{1,29},{... | collective-permute-start | bytes 147464 | tf_op jit(solution)/shard_map/ppermute | solution.py:350
  49.4 5.0 %collective-permute-start.17 = (f32[96,128]{1,0:T(8,128)S(1)}, f32[96,128]{1,0:T(8,128)S(1)}, u32[]{:S(2)}, u32[]{:S(2)}) collective-permute-start(f32[96,128]{1,0:T(8,128)S(1)} %get-tuple-element.66), channel_id=1, source_target_pairs={{0,12},{4,8},{8,4},{12,0},{16,28},{20,24},{24,20},{28,16},{1,13},{... | collective-permute-start | bytes 147464 | tf_op jit(solution)/shard_map/ppermute | solution.py:350
  (2 other events, 1.8 us)
